TPU v7x, 32 devices: a whole 2x2x4 slice. The times are simulated.
32 devices in a mesh: dp: 32 (over z, y, x, core), mp: 1.
Axes of the slice: x: 2, y: 2, z: 4, core: 2. Of those that a mesh axis runs over, the one named last changes fastest.
Arguments:
- tokens: bfloat16 [4096, 4096], P('dp')
- key_cot: bfloat16 [4096, 1024], P('dp', 'mp'), may hold values from -6 to 6
- routes: int32 [4096, 1], P('dp'), may hold values from 0 to 31; in each aligned block of 128 rows (0 to 127, 128 to 255, ...) at most 8 rows name the same one
- counts: int32 [32, 4], P('dp'), may hold values from 1 to 64, 128 in all within a row
- widths: int32 [4], replicated, may hold values from 2 to 8, as said below
- key_weight: bfloat16 [4096, 1024], P('dp', 'mp')
Outputs:
- row_grads: bfloat16 [8192, 4096], P('dp', 'mp')
- key_grad: float32 [4096, 1024], P('dp', 'mp')
Inputs may be any that keep to these rules, and one draw needn't show every extreme that they name: `routes`: within the rows of one index of dp no destination is named more than 8 times, a bound that some block reaches. Each index of dp has 4 counts that sum to 128. widths[0] = 8 (the full net), widths[1] = 8 // 4 (the smallest), the other two lie strictly between.
All inputs are finite; a program needn't handle non-finite values.
Results may differ from a plain program's by a relative error of at most 0.0058.
Values may be sent and summed in bfloat16 or wider, within the bound.
No kernel may reach another device: no remote copies, remote signals or barrier semaphores. Data moves between devices by JAX's collectives and lax.ppermute only.
A program may use at most 64 MiB of HBM per device.

v0:
```python
import math

import jax
import jax.numpy as jnp
from jax import lax
from jax.sharding import PartitionSpec as P

HEAD_DIM = 128
NSUB = 4


epsilon = 1e-06


def per_device(tokens, key_cot, routes, counts, widths, key_weight):
    row_count = tokens.shape[0]
    width_model = tokens.shape[1]
    local_cols = key_cot.shape[1]
    local_heads = local_cols // HEAD_DIM
    dp_size = lax.axis_size("dp")
    per_peer = 2 * row_count // dp_size
    receive = dp_size * per_peer
    destination = routes[:, 0]
    one_hot = (destination[:, None] == jnp.arange(dp_size, dtype=jnp.int32)[None, :]).astype(
        jnp.int32
    )
    earlier = jnp.sum(jnp.cumsum(one_hot, axis=0) * one_hot, axis=1) - 1
    send_slot = destination * per_peer + earlier
    bounds = jnp.cumsum(counts[0])
    positions = jnp.arange(row_count, dtype=jnp.int32)
    subnet = jnp.sum((positions[:, None] >= bounds[None, : NSUB - 1]).astype(jnp.int32), axis=1)
    send_subnet = (
        jnp.full((receive,), -1, jnp.int32).at[send_slot].set(subnet).reshape(dp_size, per_peer)
    )
    send_cot = jnp.zeros((receive, local_cols), jnp.bfloat16).at[send_slot].set(key_cot)
    send_cot = send_cot.reshape(dp_size, per_peer, local_cols)
    send_tokens = jnp.zeros((receive, width_model), jnp.bfloat16).at[send_slot].set(tokens)
    send_tokens = send_tokens.reshape(dp_size, per_peer, width_model)
    got_tokens, got_cot, got_subnet = (
        lax.all_to_all(send_tokens, "dp", split_axis=0, concat_axis=0, tiled=True),
        lax.all_to_all(send_cot, "dp", split_axis=0, concat_axis=0, tiled=True),
        lax.all_to_all(send_subnet, "dp", split_axis=0, concat_axis=0, tiled=True),
    )
    hidden = got_tokens.reshape(receive, width_model)
    got_cot = got_cot.reshape(receive, local_cols)
    got_subnet = got_subnet.reshape(receive)
    full_weight = lax.all_gather(key_weight, "dp", axis=0, tiled=True)
    key_proj = jnp.dot(hidden, full_weight, preferred_element_type=jnp.float32)
    per_head = key_proj.reshape(receive, local_heads, HEAD_DIM)
    head_scale = jnp.sqrt(jnp.mean(per_head * per_head, axis=2, keepdims=True) + epsilon)
    outputs = per_head / head_scale
    subnet_match = got_subnet[:, None] == jnp.arange(NSUB, dtype=jnp.int32)[None, :]
    row_width = jnp.sum(jnp.where(subnet_match, widths[None, :], 0), axis=1)
    head_index = lax.axis_index("mp") * local_heads + jnp.arange(local_heads, dtype=jnp.int32)
    head_mask = (head_index[None, :] < row_width[:, None]).astype(jnp.float32)
    upstream = (
        got_cot.astype(jnp.float32).reshape(receive, local_heads, HEAD_DIM) * head_mask[:, :, None]
    )
    key_delta = (
        upstream - outputs * jnp.mean(upstream * outputs, axis=2, keepdims=True)
    ) / head_scale
    delta_low = key_delta.reshape(receive, local_cols).astype(jnp.bfloat16)
    part_delta = lax.dot_general(
        delta_low, full_weight, (((1,), (1,)), ((), ())), preferred_element_type=jnp.float32
    )
    rounded = lax.optimization_barrier(part_delta.astype(jnp.bfloat16)).astype(jnp.float32)
    feature_delta = lax.psum_scatter(
        rounded.astype(jnp.bfloat16), "mp", scatter_dimension=1, tiled=True
    )
    weight_sum = lax.psum_scatter(
        lax.dot_general(
            hidden, delta_low, (((0,), (0,)), ((), ())), preferred_element_type=jnp.float32
        ),
        "dp",
        scatter_dimension=0,
        tiled=True,
    )
    key_grad = weight_sum / math.sqrt(row_count * dp_size)
    return (feature_delta, key_grad)


def solution(mesh):
    return jax.shard_map(
        per_device,
        mesh=mesh,
        in_specs=(P("dp", None), P("dp", "mp"), P("dp", None), P("dp", None), P(), P("dp", "mp")),
        out_specs=(P("dp", "mp"), P("dp", "mp")),
        check_vma=False,
    )
```

profile of v0, /device:TPU:0, one launch (start us, length us, event | category | flops | bytes accessed | tf_op | source)
XLA Modules:
  0.0 339.2 jit_solution(6529744526404740789)
XLA Ops:
  7.2 0.0 all-gather.2.cloned.1.call-start
  7.2 0.7 all-gather.2.cloned.1.call-update
  7.9 0.8 reduce-window.4
  8.7 0.7 fusion.8
  9.5 0.2 reduce_window_sum.18
  9.6 0.1 convert_reduce_fusion
  9.7 0.8 select_reduce_fusion
  10.6 0.7 fusion.10
  11.2 1.0 scatter_custom_fusion.1
  12.2 0.7 all_to_all.13
  12.9 7.3 %all-to-all-start.1 = ((s32[32,1,8]{2,1,0:T(1,128)}), s32[32,1,8]{2,1,0:T(1,128)S(1)}, u32[]{:S(2)}, u32[]{:S(2)}) async-start(s32[32,1,8]{2,1,0:T(1,128)} %bitcast.6), calls=%async_computation.1 | async-start | bytes 32768 | tf_op jit(solution)/shard_map/all_to_all | solution.py:42
  20.2 2.4 scatter_custom_fusion
  22.6 4.7 %all-to-all-done.1 = s32[32,1,8]{2,1,0:T(1,128)S(1)} async-done(((s32[32,1,8]{2,1,0:T(1,128)}), s32[32,1,8]{2,1,0:T(1,128)S(1)}, u32[]{:S(2)}, u32[]{:S(2)}) %all-to-all-start.1) | async-done | bytes 1056 | tf_op jit(solution)/shard_map/all_to_all | solution.py:42
  27.3 2.6 all-to-all-start
  29.9 4.3 %scatter_custom_fusion.2 = bf16[256,4096]{1,0:T(8,128)(2,1)} fusion(s32[128]{0:T(128)S(1)} %fusion.10, bf16[128,4096]{1,0:T(8,128)(2,1)} %param.6, bf16[]{:T(256)} %constant.12.clone.1), kind=kCustom, calls=%fused_computation.12 | custom fusion | bytes 2097664 | tf_op jit(solution)/shard_map/scatter | solution.py:37
  34.2 13.6 %all-to-all-done = bf16[32,8,1024]{2,1,0:T(8,128)(2,1)S(1)} async-done(((bf16[32,8,1024]{2,1,0:T(8,128)(2,1)}), bf16[32,8,1024]{2,1,0:T(8,128)(2,1)S(1)}, u32[]{:S(2)}, u32[]{:S(2)}) %all-to-all-start) | async-done | bytes 524320 | tf_op jit(solution)/shard_map/all_to_all | solution.py:41
  47.8 0.0 copy-start.2
  47.8 4.4 %all-to-all-start.2 = ((bf16[32,8,4096]{2,1,0:T(8,128)(2,1)}), bf16[32,8,4096]{2,1,0:T(8,128)(2,1)S(1)}, u32[]{:S(2)}, u32[]{:S(2)}) async-start(bf16[32,8,4096]{2,1,0:T(8,128)(2,1)} %bitcast.38), calls=%async_computation.2 | async-start | bytes 4194304 | tf_op jit(solution)/shard_map/all_to_all | solution.py:40
  52.2 0.2 reduce-scatter.2.cloned.1.call-start
  52.4 0.5 broadcast.76
  52.9 0.7 reduce.3
  53.6 0.1 eq.34
  53.7 0.0 copy-done.2
  53.7 0.1 select_reduce_fusion.1
  53.8 0.1 convert_bitcast_fusion
  53.9 1.2 copy.17
  55.1 1.6 copy.15
  56.7 66.3 %all-gather.2.cloned.1.call-done = bf16[4096,1024]{1,0:T(8,128)(2,1)} async-done(((bf16[128,1024]{1,0:T(8,128)(2,1)}), bf16[4096,1024]{1,0:T(8,128)(2,1)}) %all-gather.2.cloned.1.call-update) | async-done | bytes 8388624 | tf_op jit(solution)/shard_map/all_gather | solution.py:47
  123.0 11.3 %copy.16 = bf16[1024,4096]{1,0:T(8,128)(2,1)} copy(bf16[1024,4096]{0,1:T(8,128)(2,1)} %bitcast.36) | data formatting | bytes 16777216 | tf_op jit(solution)/shard_map/dot_general | solution.py:48
  134.2 0.0 all-to-all-done.2
  134.2 5.8 %multiply_reduce_fusion.1 = (f32[256,8]{0,1:T(8,128)S(1)}, f32[256,8,128]{0,2,1:T(8,128)S(1)}) fusion(bf16[8,128,4096]{2,1,0:T(8,128)(2,1)} %bitcast.37, bf16[32,8,4096]{2,1,0:T(8,128)(2,1)S(1)} %all-to-all-done.2), kind=kOutput, calls=%fused_computation.11 | convolution fusion | flops 2148005888 | bytes 11542528 | tf_op jit(solution)/shard_map/dot_general | solution.py:48
  140.0 0.2 multiply_reduce_fusion
  140.2 0.2 divide_convert_fusion
  140.4 0.0 copy-start
  140.4 0.8 copy-done
  141.2 8.1 %fusion.2 = f32[4096,1024]{1,0:T(8,128)} fusion(bf16[256,1024]{0,1:T(8,128)(2,1)S(1)} %bitcast.40, bf16[32,8,4096]{2,1,0:T(8,128)(2,1)S(1)} %all-to-all-done.2), kind=kOutput, calls=%fused_computation.6 | convolution fusion | flops 2147483648 | bytes 19398656 | tf_op jit(solution)/shard_map/dot_general | solution.py:71
  149.3 0.0 copy-start.1
  149.3 0.0 reduce-scatter.2.cloned.1.call-update
  149.4 1.0 copy-done.1
  150.4 7.1 %convolution_convert_fusion = bf16[256,4096]{1,0:T(8,128)(2,1)} fusion(bf16[256,1024]{0,1:T(8,128)(2,1)S(1)} %bitcast.41, bf16[4096,1024]{1,0:T(8,128)(2,1)} %all-gather.2.cloned.1.call-done), kind=kOutput, calls=%fused_computation.3 | convolution fusion | flops 2148532224 | bytes 11010048 | tf_op jit(solution)/shard_map/dot_general | solution.py:63
  157.5 173.0 %reduce-scatter.2.cloned.1.call-done = f32[128,1024]{1,0:T(8,128)} async-done(((f32[4096,1024]{1,0:T(8,128)}), f32[128,1024]{1,0:T(8,128)}) %reduce-scatter.2.cloned.1.call-update) | async-done | bytes 524304 | tf_op jit(solution)/shard_map/reduce_scatter | solution.py:70
  330.5 1.9 broadcast_multiply_fusion
  (4 shorter events, 0.0 us)
Async XLA Ops:
  7.2 115.8 %all-gather.2.cloned.1.call-start = ((), (), s32[]{:S(2)}) async-start(), calls=%async_computation.4 | async-start | bytes 8650752 | tf_op jit(solution)/shard_map/all_gather | solution.py:47
  12.9 14.4 %all-to-all-start.1 = ((s32[32,1,8]{2,1,0:T(1,128)}), s32[32,1,8]{2,1,0:T(1,128)S(1)}, u32[]{:S(2)}, u32[]{:S(2)}) async-start(s32[32,1,8]{2,1,0:T(1,128)} %bitcast.6), calls=%async_computation.1 | async-start | bytes 32768 | tf_op jit(solution)/shard_map/all_to_all | solution.py:42
  27.3 20.5 %all-to-all-start = ((bf16[32,8,1024]{2,1,0:T(8,128)(2,1)}), bf16[32,8,1024]{2,1,0:T(8,128)(2,1)S(1)}, u32[]{:S(2)}, u32[]{:S(2)}) async-start(bf16[32,8,1024]{2,1,0:T(8,128)(2,1)} %bitcast.3), calls=%async_computation | async-start | bytes 1048576 | tf_op jit(solution)/shard_map/all_to_all | solution.py:41
  47.8 5.9 %copy-start.2 = (s32[4]{0:T(128)S(1)}, s32[4]{0:T(128)}, u32[]{:S(2)}) copy-start(s32[4]{0:T(128)} %param.10) | copy-start | bytes 52
  47.8 86.4 %all-to-all-start.2 = ((bf16[32,8,4096]{2,1,0:T(8,128)(2,1)}), bf16[32,8,4096]{2,1,0:T(8,128)(2,1)S(1)}, u32[]{:S(2)}, u32[]{:S(2)}) async-start(bf16[32,8,4096]{2,1,0:T(8,128)(2,1)} %bitcast.38), calls=%async_computation.2 | async-start | bytes 4194304 | tf_op jit(solution)/shard_map/all_to_all | solution.py:40
  52.2 278.3 %reduce-scatter.2.cloned.1.call-start = ((), (), s32[]{:S(2)}) async-start(), calls=%async_computation.5 | async-start | bytes 17301504 | tf_op jit(solution)/shard_map/reduce_scatter | solution.py:70
  140.4 0.8 copy-start
  149.3 1.0 copy-start.1
Sparse Core Ops, SparseCore 0:
  10.9 112.0 all-gather.1
  149.5 180.9 reduce-scatter.1
where the time goes:
time: 341 us; the launch traced here: 339 us
  waiting for transfers between devices  258 us (76%)
  local copies, waits for them, and re-layouts  24.8 us (7%)
  matrix products  21 us (6%)
  starting transfers between devices  14.6 us (4%)
  between operations  14.2 us (4%)
  other arithmetic  6.48 us (2%)
    reduce_scatter x1, waiting for transfers between devices, per_device(): lax.psum_scatter(lax.dot_general(hidden, delta_low, (((0,), (0,)), ((), (...  173 us
    all_gather x1, waiting for transfers between devices, per_device(): full_weight = lax.all_gather(key_weight, 'dp', axis=0, tiled=True)  66.3 us
    all_to_all x1, waiting for transfers between devices, per_device(): lax.all_to_all(send_cot, 'dp', split_axis=0, concat_axis=0, tiled=True)  13.6 us
    dot_general x1, local copies, waits for them, and re-layouts, per_device(): key_proj = jnp.dot(hidden, full_weight, preferred_element_type=jnp.float32)  11.3 us
    dot_general x1, matrix products, per_device(): lax.dot_general(hidden, delta_low, (((0,), (0,)), ((), ())), preferred_el...  8.12 us
    all_to_all x1, starting transfers between devices, per_device(): lax.all_to_all(send_subnet, 'dp', split_axis=0, concat_axis=0, tiled=True)  7.3 us
    dot_general x1, matrix products, per_device(): lax.dot_general(delta_low, full_weight, (((1,), (1,)), ((), ())), preferr...  7.12 us
  transfers between devices with their start and end apart: 5, of which 4 were waited for; matrix products, arithmetic and copies ran while one was open for 10% of the time, Pallas kernels for 0%

commit v1 on v0

--- a/solution.py
+++ b/solution.py
@@ -1,18 +1,20 @@
+import functools
 import math
 
 import jax
 import jax.numpy as jnp
 from jax import lax
+from jax.experimental import pallas as pl
+from jax.experimental.pallas import tpu as pltpu
 from jax.sharding import PartitionSpec as P
 
 HEAD_DIM = 128
 NSUB = 4
-
-
+VMEM_LIMIT = 48 * 1024 * 1024
 epsilon = 1e-06
 
 
-def per_device(tokens, key_cot, routes, counts, widths, key_weight):
+def per_device_general(tokens, key_cot, routes, counts, widths, key_weight):
     row_count = tokens.shape[0]
     width_model = tokens.shape[1]
     local_cols = key_cot.shape[1]
@@ -79,9 +81,249 @@
     return (feature_delta, key_grad)
 
 
+CORE, X, Y = 1, 2, 4
+
+
+def swap(value, mask):
+    size = lax.axis_size("dp")
+    return lax.ppermute(value, "dp", [(i, i ^ mask) for i in range(size)])
+
+
+def gather_chips(piece):
+    size = lax.axis_size("dp")
+    half = piece.shape[0] // 2
+    column = {0: piece}
+    bits = []
+    bit = 8
+    while bit < size:
+        bits.append(bit)
+        bit *= 2
+    for bit in reversed(bits):
+        for mask in list(column):
+            column[mask | bit] = swap(column[mask], bit)
+    out = []
+    for mask, own in column.items():
+        by_x, by_y = swap(own, X), swap(own, Y)
+        out += [
+            (mask, 0, own),
+            (mask | X, 0, by_x),
+            (mask | Y, 0, by_y),
+            (mask | X | Y, 0, swap(by_y[:half], X)),
+            (mask | X | Y, half, swap(by_x[half:], Y)),
+        ]
+    return out
+
+
+def dot(a, b, dims):
+    return lax.dot_general(a, b, (dims, ((), ())), preferred_element_type=jnp.float32)
+
+
+def delta_kernel(places, me_ref, own_ref, mate_ref, own_cot_ref, mate_cot_ref, *refs):
+    pieces = refs[: len(places)]
+    delta_ref, weight_ref, acc = refs[len(places) :]
+    me = me_ref[0]
+    core = me & 1
+    rows = own_ref.shape[0]
+    chip_rows = 2 * pieces[0].shape[0] // 2
+    for n, (mask, first, _) in enumerate(places):
+        piece = pieces[n][...]
+        depth = piece.shape[0]
+        at = pl.multiple_of(((me ^ mask) >> 1) * chip_rows + first, 128)
+        weight_ref[pl.ds(at, depth), :] = piece
+        for side, ref in enumerate((own_ref, mate_ref)):
+            part = dot(ref[:, pl.ds(at, depth)], piece, ((1,), (0,)))
+            if n == 0:
+                acc[side] = part
+            else:
+                acc[side] += part
+    for side, cot_ref in enumerate((own_cot_ref, mate_cot_ref)):
+        at = pl.multiple_of((core ^ side) * rows, rows)
+        for head in range(own_cot_ref.shape[1] // HEAD_DIM):
+            cols = slice(head * HEAD_DIM, (head + 1) * HEAD_DIM)
+            proj = acc[side, :, cols]
+            scale = jnp.sqrt(jnp.mean(proj * proj, axis=1, keepdims=True) + epsilon)
+            normed = proj / scale
+            upstream = cot_ref[:, cols].astype(jnp.float32)
+            delta = (upstream - normed * jnp.mean(upstream * normed, axis=1, keepdims=True)) / scale
+            delta_ref[pl.ds(at, rows), cols] = delta.astype(jnp.bfloat16)
+
+
+def select_kernel(places, per_peer, me_ref, target_ref, *refs):
+    pieces, sel_ref = refs[: len(places)], refs[len(places)]
+    me = me_ref[0]
+    receive = sel_ref.shape[0] // 2
+    sel_ref[...] = jnp.zeros_like(sel_ref)
+    rows = target_ref.shape[2]
+    for n, (mask, first, _) in enumerate(places):
+        chip = (me ^ mask) >> 1
+        depth = pieces[n].shape[0]
+        for block in range(first // rows, (first + depth) // rows):
+            index = chip * 2 + block
+            want = target_ref[index]
+            delta = pieces[n][block * rows - first : (block + 1) * rows - first, :]
+            for side in range(2):
+                slots = lax.broadcasted_iota(jnp.int32, (2 * per_peer, rows), 0)
+                slots = slots + ((me & -2) + side) * receive + chip * 2 * per_peer
+                hot = (slots == want).astype(jnp.bfloat16)
+                at = pl.multiple_of(side * receive + chip * 2 * per_peer, 2 * per_peer)
+                sel_ref[pl.ds(at, 2 * per_peer), :] += dot(hot, delta, ((1,), (0,))).astype(
+                    jnp.bfloat16
+                )
+
+
+def weight_grad_kernel(places, norm, me_ref, own_ref, mate_ref, *refs):
+    pieces, grad_ref = refs[: len(places)], refs[len(places)]
+    me = me_ref[0]
+    core = me & 1
+    rows = own_ref.shape[1]
+    total = None
+    for n, (mask, first, _) in enumerate(places):
+        chip = (me ^ mask) >> 1
+        depth = pieces[n].shape[0]
+        for block in range(first // rows, (first + depth) // rows):
+            delta = pieces[n][block * rows - first : (block + 1) * rows - first, :]
+            hidden = jnp.where(core == block, own_ref[chip], mate_ref[chip])
+            part = dot(hidden, delta, ((0,), (0,)))
+            if n == 0 and block == 0:
+                grad_ref[...] = part
+            else:
+                grad_ref[...] += part
+    grad_ref[...] = grad_ref[...] / norm
+
+
+def row_grad_kernel(sel_a_ref, sel_b_ref, weight_a_ref, weight_b_ref, out_ref):
+    total = dot(sel_a_ref[...], weight_a_ref[...], ((1,), (1,)))
+    total += dot(sel_b_ref[...], weight_b_ref[...], ((1,), (1,)))
+    out_ref[...] = total.astype(jnp.bfloat16)
+
+
+def whole(count):
+    return [pl.BlockSpec(memory_space=pltpu.VMEM)] * count
+
+
+SCALAR = pl.BlockSpec(memory_space=pltpu.SMEM)
+PARAMS = pltpu.CompilerParams(vmem_limit_bytes=VMEM_LIMIT)
+
+
+def per_device_paired(tokens, key_cot, routes, counts, widths, key_weight):
+    rows, width_model = tokens.shape
+    cols = key_cot.shape[1]
+    half_cols = cols // 2
+    size = lax.axis_size("dp")
+    chips = size // 2
+    per_peer = 2 * rows // size
+    receive = size * per_peer
+    me = lax.axis_index("dp")
+    core = me % 2
+    me_scalar = me.astype(jnp.int32).reshape(1)
+
+    def mine(value):
+        return lax.dynamic_slice_in_dim(value, core * half_cols, half_cols, 1)
+
+    def theirs(value):
+        return lax.dynamic_slice_in_dim(value, (1 - core) * half_cols, half_cols, 1)
+
+    own_weight, mate_weight = mine(key_weight), swap(theirs(key_weight), CORE)
+    piece = jnp.where(
+        core == 0,
+        jnp.concatenate([own_weight, mate_weight], axis=0),
+        jnp.concatenate([mate_weight, own_weight], axis=0),
+    )
+    weights = gather_chips(piece)
+
+    mate_tokens = swap(tokens, CORE)
+    groups = [[c + 2 * i for i in range(chips)] for c in range(2)]
+    by_chip = tokens.reshape(rows, chips, width_model // chips).transpose(1, 0, 2)
+    own_features = lax.all_to_all(
+        by_chip, "dp", split_axis=0, concat_axis=0, axis_index_groups=groups, tiled=True
+    )
+    mate_features = swap(own_features, CORE)
+
+    bounds = jnp.cumsum(counts[0])
+    positions = jnp.arange(rows, dtype=jnp.int32)
+    subnet = jnp.sum((positions[:, None] >= bounds[None, : NSUB - 1]).astype(jnp.int32), axis=1)
+    subnet_match = subnet[:, None] == jnp.arange(NSUB, dtype=jnp.int32)[None, :]
+    row_width = jnp.sum(jnp.where(subnet_match, widths[None, :], 0), axis=1)
+    head_of_col = jnp.arange(cols, dtype=jnp.int32) // HEAD_DIM
+    upstream = jnp.where(
+        head_of_col[None, :] < row_width[:, None], key_cot, jnp.zeros_like(key_cot)
+    )
+    own_cot, mate_cot = mine(upstream), swap(theirs(upstream), CORE)
+
+    destination = routes[:, 0]
+    same = (destination[:, None] == destination[None, :]) & (
+        positions[:, None] < positions[None, :]
+    )
+    earlier = jnp.sum(same.astype(jnp.int32), axis=0)
+    target = destination * receive + me * per_peer + earlier
+    targets = lax.all_gather(target.reshape(1, 1, rows), "dp", axis=0, tiled=True)
+
+    places = [(mask, first, None) for mask, first, _ in weights]
+    arrays = [array for _, _, array in weights]
+    delta, weight_half = pl.pallas_call(
+        functools.partial(delta_kernel, places),
+        out_shape=(
+            jax.ShapeDtypeStruct((2 * rows, half_cols), jnp.bfloat16),
+            jax.ShapeDtypeStruct((width_model, half_cols), jnp.bfloat16),
+        ),
+        in_specs=[SCALAR] + whole(4 + len(arrays)),
+        out_specs=tuple(whole(2)),
+        scratch_shapes=[pltpu.VMEM((2, rows, half_cols), jnp.float32)],
+        compiler_params=PARAMS,
+        name="delta",
+    )(me_scalar, tokens, mate_tokens, own_cot, mate_cot, *arrays)
+
+    mate_half = swap(weight_half, CORE)
+    deltas = gather_chips(delta)
+    arrays = [array for _, _, array in deltas]
+    selected = pl.pallas_call(
+        functools.partial(select_kernel, places, per_peer),
+        out_shape=jax.ShapeDtypeStruct((2 * receive, half_cols), jnp.bfloat16),
+        in_specs=[SCALAR] + whole(1 + len(arrays)),
+        out_specs=whole(1)[0],
+        compiler_params=PARAMS,
+        name="select",
+    )(me_scalar, targets, *arrays)
+    own_selected = lax.dynamic_slice_in_dim(selected, core * receive, receive, 0)
+    mate_selected = swap(
+        lax.dynamic_slice_in_dim(selected, (1 - core) * receive, receive, 0), CORE
+    )
+    chip_grad = pl.pallas_call(
+        functools.partial(weight_grad_kernel, places, math.sqrt(rows * size)),
+        out_shape=jax.ShapeDtypeStruct((2 * rows, half_cols), jnp.float32),
+        in_specs=[SCALAR] + whole(2 + len(arrays)),
+        out_specs=whole(1)[0],
+        compiler_params=PARAMS,
+        name="weight_grad",
+    )(me_scalar, own_features, mate_features, *arrays)
+    shard = width_model // size
+    own_grad = lax.dynamic_slice_in_dim(chip_grad, core * shard, shard, 0)
+    mate_grad = swap(lax.dynamic_slice_in_dim(chip_grad, (1 - core) * shard, shard, 0), CORE)
+    key_grad = jnp.where(
+        core == 0,
+        jnp.concatenate([own_grad, mate_grad], axis=1),
+        jnp.concatenate([mate_grad, own_grad], axis=1),
+    )
+
+    tile = 1024
+    row_grads = pl.pallas_call(
+        row_grad_kernel,
+        out_shape=jax.ShapeDtypeStruct((receive, width_model), jnp.bfloat16),
+        grid=(width_model // tile,),
+        in_specs=[pl.BlockSpec((receive, half_cols), lambda i: (0, 0))] * 2
+        + [pl.BlockSpec((tile, half_cols), lambda i: (i, 0))] * 2,
+        out_specs=pl.BlockSpec((receive, tile), lambda i: (0, i)),
+        compiler_params=PARAMS,
+        name="row_grad",
+    )(own_selected, mate_selected, weight_half, mate_half)
+    return (row_grads, key_grad)
+
+
 def solution(mesh):
+    size, split = mesh.shape["dp"], mesh.shape["mp"]
+    paired = split == 1 and size == 32
     return jax.shard_map(
-        per_device,
+        per_device_paired if paired else per_device_general,
         mesh=mesh,
         in_specs=(P("dp", None), P("dp", "mp"), P("dp", None), P("dp", None), P(), P("dp", "mp")),
         out_specs=(P("dp", "mp"), P("dp", "mp")),

time: 341 us -> 199 us (0.58)
  waiting for transfers between devices: 258 us -> 67.6 us
  starting transfers between devices: 14.6 us -> 62.7 us
  blocking collectives: 0 us -> 37.4 us
  matrix products: 21 us -> 0 us
  Pallas kernels: 0 us -> 17.4 us
  local copies, waits for them, and re-layouts: 24.8 us -> 8.74 us
  between operations: 14.2 us -> 0.95 us
    reduce_scatter x1 -> x0, waiting for transfers between devices: 173 us -> none  [per_device(): lax.psum_scatter(lax.dot_general(hidden, delta_low, (((0,), (0,)), ((), (...]
    ppermute x0 -> x45, waiting for transfers between devices: none -> 67.6 us  [swap(): return lax.ppermute(value, 'dp', [(i, i ^ mask) for i in range(size)])]
    all_gather x1 -> x0, waiting for transfers between devices: 66.3 us -> none  [per_device(): full_weight = lax.all_gather(key_weight, 'dp', axis=0, tiled=True)]
    ppermute x0 -> x45, starting transfers between devices: none -> 56.3 us  [swap(): return lax.ppermute(value, 'dp', [(i, i ^ mask) for i in range(size)])]
    all_gather x0 -> x1, blocking collectives: none -> 37.4 us  [per_device_paired(): lax.all_gather(target.reshape(1, 1, rows), 'dp', axis=0, tiled=True)]
    dot_general x3 -> x0, matrix products: 21 us -> none  [the longest x1 8.12 us: per_device(): lax.dot_general(hidden, delta_low, (((0,), (0,)), ((), ())), preferred_el...]
    all_to_all x3 -> x1, waiting for transfers between devices: 18.3 us -> 0.01 us  [per_device_paired(): lax.all_to_all(by_chip, 'dp', split_axis=0, concat_axis=0, axis_index_gro...]
    pallas_call x0 -> x4, Pallas kernels: none -> 17.4 us  [the longest x1 5.78 us: per_device_paired(): pl.pallas_call(row_grad_kernel, out_shape=jax.ShapeDtypeStruct((receive,...]
  transfers between devices with their start and end apart: 5 -> 46, of which waited for: 4 -> 20; matrix products, arithmetic and copies ran while one was open for 10% -> 4% of each run, Pallas kernels for 0% -> 3%
where the time goes in v1:
time: 199 us; the launch traced here: 198 us
  waiting for transfers between devices  67.6 us (34%)
  starting transfers between devices  62.7 us (32%)
  blocking collectives  37.4 us (19%)
  Pallas kernels  17.4 us (9%)
  local copies, waits for them, and re-layouts  8.74 us (4%)
  other arithmetic  3.73 us (2%)
    ppermute x45, waiting for transfers between devices, swap(): return lax.ppermute(value, 'dp', [(i, i ^ mask) for i in range(size)])  67.6 us
    ppermute x45, starting transfers between devices, swap(): return lax.ppermute(value, 'dp', [(i, i ^ mask) for i in range(size)])  56.3 us
    all_gather x1, blocking collectives, per_device_paired(): lax.all_gather(target.reshape(1, 1, rows), 'dp', axis=0, tiled=True)  37.4 us
    all_to_all x1, starting transfers between devices, per_device_paired(): lax.all_to_all(by_chip, 'dp', split_axis=0, concat_axis=0, axis_index_gro...  6.32 us
    pallas_call x1, Pallas kernels, per_device_paired(): pl.pallas_call(row_grad_kernel, out_shape=jax.ShapeDtypeStruct((receive,...  5.78 us
    pallas_call x1, Pallas kernels, per_device_paired(): pl.pallas_call(functools.partial(delta_kernel, places), out_shape=(jax.Sh...  5.13 us
    unnamed x17, local copies, waits for them, and re-layouts  4.15 us
    pallas_call x1, Pallas kernels, per_device_paired(): pl.pallas_call(functools.partial(weight_grad_kernel, places, math.sqrt(ro...  4.02 us
  transfers between devices with their start and end apart: 46, of which 20 were waited for; matrix products, arithmetic and copies ran while one was open for 4% of the time, Pallas kernels for 3%

profile of v1, /device:TPU:0, one launch (start us, length us, event | category | flops | bytes accessed | tf_op | source)
XLA Modules:
  0.0 198.5 jit_solution(17020998123286697624)
XLA Ops:
  4.1 4.1 %collective-permute-start.7 = (bf16[256,512]{1,0:T(8,128)(2,1)S(1)}, bf16[256,512]{1,0:T(8,128)(2,1)S(1)}, u32[]{:S(2)}, u32[]{:S(2)}) collective-permute-start(bf16[256,512]{1,0:T(8,128)(2,1)S(1)} %maximum_select_fusion.1.refs_0_), channel_id=1, source_target_pairs={{0,16},{1,17},{2,18},{3,19},{4,20},{5,21},{6,22},{7,23},{8,24},{9,... | collective-permute-start | bytes 786440 | tf_op jit(solution)/shard_map/ppermute | solution.py:89
  8.1 1.6 collective-permute-start.12
  9.7 1.5 collective-permute-start.4
  12.4 1.3 collective-permute-done.1.mate_cot_ref
  13.8 1.5 collective-permute-start.3
  15.3 5.2 %collective-permute-done.7.refs_5_ = bf16[256,512]{1,0:T(8,128)(2,1)S(1)} collective-permute-done((bf16[256,512]{1,0:T(8,128)(2,1)S(1)}, bf16[256,512]{1,0:T(8,128)(2,1)S(1)}, u32[]{:S(2)}, u32[]{:S(2)}) %collective-permute-start.7) | collective-permute-done | bytes 262176 | tf_op jit(solution)/shard_map/ppermute | solution.py:89
  21.0 1.5 collective-permute-start.9
  22.6 1.5 collective-permute-start.8
  24.6 3.6 %collective-permute-done.17.refs_15_ = bf16[256,512]{1,0:T(8,128)(2,1)S(1)} collective-permute-done((bf16[256,512]{1,0:T(8,128)(2,1)S(1)}, bf16[256,512]{1,0:T(8,128)(2,1)S(1)}, u32[]{:S(2)}, u32[]{:S(2)}) %collective-permute-start.17) | collective-permute-done | bytes 262176 | tf_op jit(solution)/shard_map/ppermute | solution.py:89
  28.1 1.2 collective-permute-start.13
  30.2 1.5 collective-permute-start.19
  31.8 1.5 collective-permute-start.18
  33.3 2.5 %collective-permute-done.14.refs_12_ = bf16[256,512]{1,0:T(8,128)(2,1)S(1)} collective-permute-done((bf16[256,512]{1,0:T(8,128)(2,1)S(1)}, bf16[256,512]{1,0:T(8,128)(2,1)S(1)}, u32[]{:S(2)}, u32[]{:S(2)}) %collective-permute-start.14) | collective-permute-done | bytes 262176 | tf_op jit(solution)/shard_map/ppermute | solution.py:89
  35.9 1.5 collective-permute-start.5
  37.4 1.5 collective-permute-start.6
  38.9 2.6 %collective-permute-done.19.refs_17_ = bf16[256,512]{1,0:T(8,128)(2,1)S(1)} collective-permute-done((bf16[256,512]{1,0:T(8,128)(2,1)S(1)}, bf16[256,512]{1,0:T(8,128)(2,1)S(1)}, u32[]{:S(2)}, u32[]{:S(2)}) %collective-permute-start.19) | collective-permute-done | bytes 262176 | tf_op jit(solution)/shard_map/ppermute | solution.py:89
  41.5 1.5 collective-permute-start.10
  43.0 1.5 collective-permute-start.11
  44.6 1.2 collective-permute-done.5.refs_3_
  45.8 1.5 collective-permute-start.15
  48.6 1.5 collective-permute-start.20
  53.6 1.5 collective-permute-done.21.refs_19_
  56.0 5.1 %delta.1 = (bf16[256,512]{1,0:T(8,128)(2,1)S(1)}, bf16[4096,512]{1,0:T(8,128)(2,1)}) custom-call(s32[1]{0:T(128)} %bitcast.me_ref, bf16[128,4096]{1,0:T(8,128)(2,1)S(1)} %copy-done.1, bf16[128,4096]{1,0:T(8,128)(2,1)} %copy-done.6, bf16[128,512]{1,0:T(8,128)(2,1)S(1)} %get-tuple-element.13.own_cot_ref, ...), custom_call_target="tpu_custom_call" | custom-call | tf_op jit(solution)/shard_map/delta/pallas_call | solution.py:263
  61.8 1.3 copy.13
  63.1 6.3 %all-to-all-start = ((bf16[16,128,256]{2,1,0:T(8,128)(2,1)}), bf16[16,128,256]{2,1,0:T(8,128)(2,1)S(1)}, u32[]{:S(2)}, u32[]{:S(2)}) async-start(bf16[16,128,256]{2,1,0:T(8,128)(2,1)} %bitcast.7), calls=%async_computation | async-start | bytes 2097152 | tf_op jit(solution)/shard_map/all_to_all | solution.py:237
  69.4 2.8 %collective-permute-start.26 = (bf16[256,512]{1,0:T(8,128)(2,1)S(1)}, bf16[256,512]{1,0:T(8,128)(2,1)S(1)}, u32[]{:S(2)}, u32[]{:S(2)}) collective-permute-start(bf16[256,512]{1,0:T(8,128)(2,1)S(1)} %get-tuple-element.4.refs_0_), channel_id=1, source_target_pairs={{0,16},{1,17},{2,18},{3,19},{4,20},{5,21},{6,22},{7,23},{8,24},{9,... | collective-permute-start | bytes 786440 | tf_op jit(solution)/shard_map/ppermute | solution.py:89
  72.3 1.5 collective-permute-start.23
  73.7 1.5 collective-permute-start.22
  75.2 1.5 collective-permute-start.31
  76.7 30.4 %collective-permute-done.26.refs_5_ = bf16[256,512]{1,0:T(8,128)(2,1)S(1)} collective-permute-done((bf16[256,512]{1,0:T(8,128)(2,1)S(1)}, bf16[256,512]{1,0:T(8,128)(2,1)S(1)}, u32[]{:S(2)}, u32[]{:S(2)}) %collective-permute-start.26) | collective-permute-done | bytes 262176 | tf_op jit(solution)/shard_map/ppermute | solution.py:89
  107.2 1.5 collective-permute-start.24
  108.7 1.7 collective-permute-start.25
  110.4 2.7 %collective-permute-done.24.refs_3_ = bf16[128,512]{1,0:T(8,128)(2,1)S(1)} collective-permute-done((bf16[128,512]{1,0:T(8,128)(2,1)S(1)}, bf16[128,512]{1,0:T(8,128)(2,1)S(1)}, u32[]{:S(2)}, u32[]{:S(2)}) %collective-permute-start.24) | collective-permute-done | bytes 131104 | tf_op jit(solution)/shard_map/ppermute | solution.py:89
  113.1 1.9 collective-permute-start.28
  117.6 4.7 %collective-permute-done.28.refs_7_ = bf16[256,512]{1,0:T(8,128)(2,1)S(1)} collective-permute-done((bf16[256,512]{1,0:T(8,128)(2,1)S(1)}, bf16[256,512]{1,0:T(8,128)(2,1)S(1)}, u32[]{:S(2)}, u32[]{:S(2)}) %collective-permute-start.28) | collective-permute-done | bytes 262176 | tf_op jit(solution)/shard_map/ppermute | solution.py:89
  122.3 1.5 collective-permute-start.32
  123.8 1.7 collective-permute-start.38
  125.4 2.5 %collective-permute-done.33.refs_12_ = bf16[256,512]{1,0:T(8,128)(2,1)S(1)} collective-permute-done((bf16[256,512]{1,0:T(8,128)(2,1)}, bf16[256,512]{1,0:T(8,128)(2,1)S(1)}, u32[]{:S(2)}, u32[]{:S(2)}) %collective-permute-start.33) | collective-permute-done | bytes 262176 | tf_op jit(solution)/shard_map/ppermute | solution.py:89
  127.9 1.5 collective-permute-start.37
  132.6 1.7 collective-permute-start.30
  134.3 2.0 %collective-permute-done.37.refs_16_ = bf16[256,512]{1,0:T(8,128)(2,1)S(1)} collective-permute-done((bf16[256,512]{1,0:T(8,128)(2,1)}, bf16[256,512]{1,0:T(8,128)(2,1)S(1)}, u32[]{:S(2)}, u32[]{:S(2)}) %collective-permute-start.37) | collective-permute-done | bytes 262176 | tf_op jit(solution)/shard_map/ppermute | solution.py:89
  136.4 1.4 collective-permute-start.34
  139.0 2.2 %collective-permute-start.35 = (bf16[128,512]{1,0:T(8,128)(2,1)S(1)}, bf16[128,512]{1,0:T(8,128)(2,1)S(1)}, u32[]{:S(2)}, u32[]{:S(2)}) collective-permute-start(bf16[128,512]{1,0:T(8,128)(2,1)S(1)} %slice.82), channel_id=1, source_target_pairs={{0,4},{1,5},{2,6},{3,7},{4,0},{5,1},{6,2},{7,3},{8,12},{9,13},{10,... | collective-permute-start | bytes 393224 | tf_op jit(solution)/shard_map/ppermute | solution.py:89
  142.4 2.0 collective-permute-start.40
  144.4 37.4 %all_gather.3.target_ref = s32[32,1,128]{2,1,0:T(1,128)S(1)} all-gather(s32[1,1,128]{2,1,0:T(1,128)S(1)} %bitcast_add_fusion), channel_id=1, replica_groups=mesh['dp'=32,'mp'=1] {'dp'}, dimensions={0}, use_global_device_ids=true | all-gather | bytes 16896 | tf_op jit(solution)/shard_map/all_gather | solution.py:259
  183.7 2.4 %select.11 = bf16[512,512]{1,0:T(8,128)(2,1)S(1)} custom-call(s32[1]{0:T(128)} %bitcast.me_ref, s32[32,1,128]{2,1,0:T(1,128)S(1)} %all_gather.3.target_ref, bf16[256,512]{1,0:T(8,128)(2,1)S(1)} %get-tuple-element.4.refs_0_, bf16[256,512]{1,0:T(8,128)(2,1)S(1)} %collective-permute-done.22.refs_1_, bf16[256,512]{1,0:T(8,128)(2,1)S(1)} %collective-permute-done.23.refs_2_, ...), custom_call_target="tpu_custom_call" | custom-call | tf_op jit(solution)/shard_map/select/pallas_call | solution.py:279
  186.1 4.0 %weight_grad.1 = f32[256,512]{1,0:T(8,128)S(1)} custom-call(s32[1]{0:T(128)} %bitcast.me_ref, bf16[16,128,256]{2,1,0:T(8,128)(2,1)S(1)} %all-to-all-done.own_ref, bf16[16,128,256]{2,1,0:T(8,128)(2,1)} %collective-permute-done.43.mate_ref, bf16[256,512]{1,0:T(8,128)(2,1)S(1)} %get-tuple-element.4.refs_0_, ...), custom_call_target="tpu_custom_call" | custom-call | tf_op jit(solution)/shard_map/weight_grad/pallas_call | solution.py:291
  192.7 5.8 %row_grad.1 = bf16[256,4096]{1,0:T(8,128)(2,1)} custom-call(bf16[256,512]{1,0:T(8,128)(2,1)S(1)} %get-tuple-element.9.sel_a_ref, bf16[256,512]{1,0:T(8,128)(2,1)S(1)} %collective-permute-done.41.sel_b_ref, bf16[4096,512]{1,0:T(8,128)(2,1)S(1)} %copy-done, bf16[4096,512]{1,0:T(8,128)(2,1)} %collective-permute-done.42.weight_b_ref), custom_call_target="tpu_custom_call" | custom-call | tf_op jit(solution)/shard_map/row_grad/pallas_call | solution.py:309
  (97 shorter events, 25.8 us)
Async XLA Ops:
  0.6 55.4 %copy-start.1 = (bf16[128,4096]{1,0:T(8,128)(2,1)S(1)}, bf16[128,4096]{1,0:T(8,128)(2,1)}, u32[]{:S(2)}) copy-start(bf16[128,4096]{1,0:T(8,128)(2,1)} %own_ref.1) | copy-start | bytes 3145732
  1.7 2.3 %collective-permute-start.2 = (bf16[128,512]{1,0:T(8,128)(2,1)S(1)}, bf16[128,512]{1,0:T(8,128)(2,1)S(1)}, u32[]{:S(2)}, u32[]{:S(2)}) collective-permute-start(bf16[128,512]{1,0:T(8,128)(2,1)S(1)} %get-tuple-element.11), channel_id=1, source_target_pairs={{0,1},{1,0},{2,3},{3,2},{4,5},{5,4},{6,7},{7,6},{8,9},{9,8},{10,11... | collective-permute-start | bytes 393224 | tf_op jit(solution)/shard_map/ppermute | solution.py:89
  2.3 52.8 %collective-permute-start = (bf16[128,4096]{1,0:T(8,128)(2,1)}, bf16[128,4096]{1,0:T(8,128)(2,1)S(1)}, u32[]{:S(2)}, u32[]{:S(2)}) collective-permute-start(bf16[128,4096]{1,0:T(8,128)(2,1)} %own_ref.1), channel_id=1, source_target_pairs={{0,1},{1,0},{2,3},{3,2},{4,5},{5,4},{6,7},{7,6},{8,9},{9,8},{10,11... | collective-permute-start | bytes 3145736 | tf_op jit(solution)/shard_map/ppermute | solution.py:89
  4.1 16.4 %collective-permute-start.7 = (bf16[256,512]{1,0:T(8,128)(2,1)S(1)}, bf16[256,512]{1,0:T(8,128)(2,1)S(1)}, u32[]{:S(2)}, u32[]{:S(2)}) collective-permute-start(bf16[256,512]{1,0:T(8,128)(2,1)S(1)} %maximum_select_fusion.1.refs_0_), channel_id=1, source_target_pairs={{0,16},{1,17},{2,18},{3,19},{4,20},{5,21},{6,22},{7,23},{8,24},{9,... | collective-permute-start | bytes 786440 | tf_op jit(solution)/shard_map/ppermute | solution.py:89
  8.1 12.9 %collective-permute-start.12 = (bf16[256,512]{1,0:T(8,128)(2,1)S(1)}, bf16[256,512]{1,0:T(8,128)(2,1)S(1)}, u32[]{:S(2)}, u32[]{:S(2)}) collective-permute-start(bf16[256,512]{1,0:T(8,128)(2,1)S(1)} %maximum_select_fusion.1.refs_0_), channel_id=1, source_target_pairs={{0,8},{1,9},{2,10},{3,11},{4,12},{5,13},{6,14},{7,15},{8,0},{9,1},... | collective-permute-start | bytes 786440 | tf_op jit(solution)/shard_map/ppermute | solution.py:89
  9.7 12.8 %collective-permute-start.4 = (bf16[256,512]{1,0:T(8,128)(2,1)S(1)}, bf16[256,512]{1,0:T(8,128)(2,1)S(1)}, u32[]{:S(2)}, u32[]{:S(2)}) collective-permute-start(bf16[256,512]{1,0:T(8,128)(2,1)S(1)} %maximum_select_fusion.1.refs_0_), channel_id=1, source_target_pairs={{0,4},{1,5},{2,6},{3,7},{4,0},{5,1},{6,2},{7,3},{8,12},{9,13},{10,... | collective-permute-start | bytes 786440 | tf_op jit(solution)/shard_map/ppermute | solution.py:89
  12.4 1.4 collective-permute-start.1
  13.8 10.3 %collective-permute-start.3 = (bf16[256,512]{1,0:T(8,128)(2,1)S(1)}, bf16[256,512]{1,0:T(8,128)(2,1)S(1)}, u32[]{:S(2)}, u32[]{:S(2)}) collective-permute-start(bf16[256,512]{1,0:T(8,128)(2,1)S(1)} %maximum_select_fusion.1.refs_0_), channel_id=1, source_target_pairs={{0,2},{1,3},{2,0},{3,1},{4,6},{5,7},{6,4},{7,5},{8,10},{9,11},{10,... | collective-permute-start | bytes 786440 | tf_op jit(solution)/shard_map/ppermute | solution.py:89
  20.4 7.7 %collective-permute-start.17 = (bf16[256,512]{1,0:T(8,128)(2,1)S(1)}, bf16[256,512]{1,0:T(8,128)(2,1)S(1)}, u32[]{:S(2)}, u32[]{:S(2)}) collective-permute-start(bf16[256,512]{1,0:T(8,128)(2,1)S(1)} %collective-permute-done.7.refs_5_), channel_id=1, source_target_pairs={{0,8},{1,9},{2,10},{3,11},{4,12},{5,13},{6,14},{7,15},{8,0},{9,1},... | collective-permute-start | bytes 786440 | tf_op jit(solution)/shard_map/ppermute | solution.py:89
  21.0 9.2 %collective-permute-start.9 = (bf16[256,512]{1,0:T(8,128)(2,1)S(1)}, bf16[256,512]{1,0:T(8,128)(2,1)S(1)}, u32[]{:S(2)}, u32[]{:S(2)}) collective-permute-start(bf16[256,512]{1,0:T(8,128)(2,1)S(1)} %collective-permute-done.7.refs_5_), channel_id=1, source_target_pairs={{0,4},{1,5},{2,6},{3,7},{4,0},{5,1},{6,2},{7,3},{8,12},{9,13},{10,... | collective-permute-start | bytes 786440 | tf_op jit(solution)/shard_map/ppermute | solution.py:89
  22.6 9.2 %collective-permute-start.8 = (bf16[256,512]{1,0:T(8,128)(2,1)S(1)}, bf16[256,512]{1,0:T(8,128)(2,1)S(1)}, u32[]{:S(2)}, u32[]{:S(2)}) collective-permute-start(bf16[256,512]{1,0:T(8,128)(2,1)S(1)} %collective-permute-done.7.refs_5_), channel_id=1, source_target_pairs={{0,2},{1,3},{2,0},{3,1},{4,6},{5,7},{6,4},{7,5},{8,10},{9,11},{10,... | collective-permute-start | bytes 786440 | tf_op jit(solution)/shard_map/ppermute | solution.py:89
  24.1 11.8 %collective-permute-start.14 = (bf16[256,512]{1,0:T(8,128)(2,1)S(1)}, bf16[256,512]{1,0:T(8,128)(2,1)S(1)}, u32[]{:S(2)}, u32[]{:S(2)}) collective-permute-start(bf16[256,512]{1,0:T(8,128)(2,1)S(1)} %collective-permute-done.12.refs_10_), channel_id=1, source_target_pairs={{0,4},{1,5},{2,6},{3,7},{4,0},{5,1},{6,2},{7,3},{8,12},{9,13},{10,... | collective-permute-start | bytes 786440 | tf_op jit(solution)/shard_map/ppermute | solution.py:89
  28.1 9.2 %collective-permute-start.13 = (bf16[256,512]{1,0:T(8,128)(2,1)S(1)}, bf16[256,512]{1,0:T(8,128)(2,1)S(1)}, u32[]{:S(2)}, u32[]{:S(2)}) collective-permute-start(bf16[256,512]{1,0:T(8,128)(2,1)S(1)} %collective-permute-done.12.refs_10_), channel_id=1, source_target_pairs={{0,2},{1,3},{2,0},{3,1},{4,6},{5,7},{6,4},{7,5},{8,10},{9,11},{10,... | collective-permute-start | bytes 786440 | tf_op jit(solution)/shard_map/ppermute | solution.py:89
  30.2 11.2 %collective-permute-start.19 = (bf16[256,512]{1,0:T(8,128)(2,1)S(1)}, bf16[256,512]{1,0:T(8,128)(2,1)S(1)}, u32[]{:S(2)}, u32[]{:S(2)}) collective-permute-start(bf16[256,512]{1,0:T(8,128)(2,1)S(1)} %collective-permute-done.17.refs_15_), channel_id=1, source_target_pairs={{0,4},{1,5},{2,6},{3,7},{4,0},{5,1},{6,2},{7,3},{8,12},{9,13},{10,... | collective-permute-start | bytes 786440 | tf_op jit(solution)/shard_map/ppermute | solution.py:89
  31.8 11.2 %collective-permute-start.18 = (bf16[256,512]{1,0:T(8,128)(2,1)S(1)}, bf16[256,512]{1,0:T(8,128)(2,1)S(1)}, u32[]{:S(2)}, u32[]{:S(2)}) collective-permute-start(bf16[256,512]{1,0:T(8,128)(2,1)S(1)} %collective-permute-done.17.refs_15_), channel_id=1, source_target_pairs={{0,2},{1,3},{2,0},{3,1},{4,6},{5,7},{6,4},{7,5},{8,10},{9,11},{10,... | collective-permute-start | bytes 786440 | tf_op jit(solution)/shard_map/ppermute | solution.py:89
  35.9 9.9 %collective-permute-start.5 = (bf16[128,512]{1,0:T(8,128)(2,1)S(1)}, bf16[128,512]{1,0:T(8,128)(2,1)S(1)}, u32[]{:S(2)}, u32[]{:S(2)}) collective-permute-start(bf16[128,512]{1,0:T(8,128)(2,1)S(1)} %slice.69), channel_id=1, source_target_pairs={{0,2},{1,3},{2,0},{3,1},{4,6},{5,7},{6,4},{7,5},{8,10},{9,11},{10,... | collective-permute-start | bytes 393224 | tf_op jit(solution)/shard_map/ppermute | solution.py:89
  37.4 9.9 %collective-permute-start.6 = (bf16[128,512]{1,0:T(8,128)(2,1)S(1)}, bf16[128,512]{1,0:T(8,128)(2,1)S(1)}, u32[]{:S(2)}, u32[]{:S(2)}) collective-permute-start(bf16[128,512]{1,0:T(8,128)(2,1)S(1)} %slice.70), channel_id=1, source_target_pairs={{0,4},{1,5},{2,6},{3,7},{4,0},{5,1},{6,2},{7,3},{8,12},{9,13},{10,... | collective-permute-start | bytes 393224 | tf_op jit(solution)/shard_map/ppermute | solution.py:89
  41.5 7.1 %collective-permute-start.10 = (bf16[128,512]{1,0:T(8,128)(2,1)S(1)}, bf16[128,512]{1,0:T(8,128)(2,1)S(1)}, u32[]{:S(2)}, u32[]{:S(2)}) collective-permute-start(bf16[128,512]{1,0:T(8,128)(2,1)S(1)} %slice.71), channel_id=1, source_target_pairs={{0,2},{1,3},{2,0},{3,1},{4,6},{5,7},{6,4},{7,5},{8,10},{9,11},{10,... | collective-permute-start | bytes 393224 | tf_op jit(solution)/shard_map/ppermute | solution.py:89
  43.0 7.1 %collective-permute-start.11 = (bf16[128,512]{1,0:T(8,128)(2,1)S(1)}, bf16[128,512]{1,0:T(8,128)(2,1)S(1)}, u32[]{:S(2)}, u32[]{:S(2)}) collective-permute-start(bf16[128,512]{1,0:T(8,128)(2,1)S(1)} %slice.72), channel_id=1, source_target_pairs={{0,4},{1,5},{2,6},{3,7},{4,0},{5,1},{6,2},{7,3},{8,12},{9,13},{10,... | collective-permute-start | bytes 393224 | tf_op jit(solution)/shard_map/ppermute | solution.py:89
  45.8 5.5 %collective-permute-start.15 = (bf16[128,512]{1,0:T(8,128)(2,1)S(1)}, bf16[128,512]{1,0:T(8,128)(2,1)S(1)}, u32[]{:S(2)}, u32[]{:S(2)}) collective-permute-start(bf16[128,512]{1,0:T(8,128)(2,1)S(1)} %slice.73), channel_id=1, source_target_pairs={{0,2},{1,3},{2,0},{3,1},{4,6},{5,7},{6,4},{7,5},{8,10},{9,11},{10,... | collective-permute-start | bytes 393224 | tf_op jit(solution)/shard_map/ppermute | solution.py:89
  47.3 5.1 %collective-permute-start.16 = (bf16[128,512]{1,0:T(8,128)(2,1)S(1)}, bf16[128,512]{1,0:T(8,128)(2,1)S(1)}, u32[]{:S(2)}, u32[]{:S(2)}) collective-permute-start(bf16[128,512]{1,0:T(8,128)(2,1)S(1)} %slice.74), channel_id=1, source_target_pairs={{0,4},{1,5},{2,6},{3,7},{4,0},{5,1},{6,2},{7,3},{8,12},{9,13},{10,... | collective-permute-start | bytes 393224 | tf_op jit(solution)/shard_map/ppermute | solution.py:89
  48.6 5.0 %collective-permute-start.20 = (bf16[128,512]{1,0:T(8,128)(2,1)S(1)}, bf16[128,512]{1,0:T(8,128)(2,1)S(1)}, u32[]{:S(2)}, u32[]{:S(2)}) collective-permute-start(bf16[128,512]{1,0:T(8,128)(2,1)S(1)} %slice.75), channel_id=1, source_target_pairs={{0,2},{1,3},{2,0},{3,1},{4,6},{5,7},{6,4},{7,5},{8,10},{9,11},{10,... | collective-permute-start | bytes 393224 | tf_op jit(solution)/shard_map/ppermute | solution.py:89
  50.1 5.0 %collective-permute-start.21 = (bf16[128,512]{1,0:T(8,128)(2,1)S(1)}, bf16[128,512]{1,0:T(8,128)(2,1)S(1)}, u32[]{:S(2)}, u32[]{:S(2)}) collective-permute-start(bf16[128,512]{1,0:T(8,128)(2,1)S(1)} %slice.76), channel_id=1, source_target_pairs={{0,4},{1,5},{2,6},{3,7},{4,0},{5,1},{6,2},{7,3},{8,12},{9,13},{10,... | collective-permute-start | bytes 393224 | tf_op jit(solution)/shard_map/ppermute | solution.py:89
  61.1 76.6 %copy-start.7 = (s32[128,1]{0,1:T(1,128)S(1)}, s32[128,1]{0,1:T(1,128)}, u32[]{:S(2)}) copy-start(s32[128,1]{0,1:T(1,128)} %param.8) | copy-start | bytes 1540
  61.1 131.5 %collective-permute-start.42 = (bf16[4096,512]{1,0:T(8,128)(2,1)}, bf16[4096,512]{1,0:T(8,128)(2,1)}, u32[]{:S(2)}, u32[]{:S(2)}) collective-permute-start(bf16[4096,512]{1,0:T(8,128)(2,1)} %get-tuple-element.5.weight_a_ref), channel_id=1, source_target_pairs={{0,1},{1,0},{2,3},{3,2},{4,5},{5,4},{6,7},{7,6},{8,9},{9,8},{10,11... | collective-permute-start | bytes 12582920 | tf_op jit(solution)/shard_map/ppermute | solution.py:89
  63.1 43.9 %all-to-all-start = ((bf16[16,128,256]{2,1,0:T(8,128)(2,1)}), bf16[16,128,256]{2,1,0:T(8,128)(2,1)S(1)}, u32[]{:S(2)}, u32[]{:S(2)}) async-start(bf16[16,128,256]{2,1,0:T(8,128)(2,1)} %bitcast.7), calls=%async_computation | async-start | bytes 2097152 | tf_op jit(solution)/shard_map/all_to_all | solution.py:237
  69.4 37.6 %collective-permute-start.26 = (bf16[256,512]{1,0:T(8,128)(2,1)S(1)}, bf16[256,512]{1,0:T(8,128)(2,1)S(1)}, u32[]{:S(2)}, u32[]{:S(2)}) collective-permute-start(bf16[256,512]{1,0:T(8,128)(2,1)S(1)} %get-tuple-element.4.refs_0_), channel_id=1, source_target_pairs={{0,16},{1,17},{2,18},{3,19},{4,20},{5,21},{6,22},{7,23},{8,24},{9,... | collective-permute-start | bytes 786440 | tf_op jit(solution)/shard_map/ppermute | solution.py:89
  72.3 34.8 %collective-permute-start.23 = (bf16[256,512]{1,0:T(8,128)(2,1)S(1)}, bf16[256,512]{1,0:T(8,128)(2,1)S(1)}, u32[]{:S(2)}, u32[]{:S(2)}) collective-permute-start(bf16[256,512]{1,0:T(8,128)(2,1)S(1)} %get-tuple-element.4.refs_0_), channel_id=1, source_target_pairs={{0,4},{1,5},{2,6},{3,7},{4,0},{5,1},{6,2},{7,3},{8,12},{9,13},{10,... | collective-permute-start | bytes 786440 | tf_op jit(solution)/shard_map/ppermute | solution.py:89
  73.7 33.4 %collective-permute-start.22 = (bf16[256,512]{1,0:T(8,128)(2,1)S(1)}, bf16[256,512]{1,0:T(8,128)(2,1)S(1)}, u32[]{:S(2)}, u32[]{:S(2)}) collective-permute-start(bf16[256,512]{1,0:T(8,128)(2,1)S(1)} %get-tuple-element.4.refs_0_), channel_id=1, source_target_pairs={{0,2},{1,3},{2,0},{3,1},{4,6},{5,7},{6,4},{7,5},{8,10},{9,11},{10,... | collective-permute-start | bytes 786440 | tf_op jit(solution)/shard_map/ppermute | solution.py:89
  75.2 33.5 %collective-permute-start.31 = (bf16[256,512]{1,0:T(8,128)(2,1)S(1)}, bf16[256,512]{1,0:T(8,128)(2,1)}, u32[]{:S(2)}, u32[]{:S(2)}) collective-permute-start(bf16[256,512]{1,0:T(8,128)(2,1)S(1)} %get-tuple-element.4.refs_0_), channel_id=1, source_target_pairs={{0,8},{1,9},{2,10},{3,11},{4,12},{5,13},{6,14},{7,15},{8,0},{9,1},... | collective-permute-start | bytes 786440 | tf_op jit(solution)/shard_map/ppermute | solution.py:89
  107.0 9.9 %collective-permute-start.36 = (bf16[256,512]{1,0:T(8,128)(2,1)S(1)}, bf16[256,512]{1,0:T(8,128)(2,1)}, u32[]{:S(2)}, u32[]{:S(2)}) collective-permute-start(bf16[256,512]{1,0:T(8,128)(2,1)S(1)} %collective-permute-done.26.refs_5_), channel_id=1, source_target_pairs={{0,8},{1,9},{2,10},{3,11},{4,12},{5,13},{6,14},{7,15},{8,0},{9,1},... | collective-permute-start | bytes 786440 | tf_op jit(solution)/shard_map/ppermute | solution.py:89
  107.0 79.1 %collective-permute-start.43 = (bf16[16,128,256]{2,1,0:T(8,128)(2,1)S(1)}, bf16[16,128,256]{2,1,0:T(8,128)(2,1)}, u32[]{:S(2)}, u32[]{:S(2)}) collective-permute-start(bf16[16,128,256]{2,1,0:T(8,128)(2,1)S(1)} %all-to-all-done.own_ref), channel_id=1, source_target_pairs={{0,1},{1,0},{2,3},{3,2},{4,5},{5,4},{6,7},{7,6},{8,9},{9,8},{10,11... | collective-permute-start | bytes 3145736 | tf_op jit(solution)/shard_map/ppermute | solution.py:89
  107.2 6.0 %collective-permute-start.24 = (bf16[128,512]{1,0:T(8,128)(2,1)S(1)}, bf16[128,512]{1,0:T(8,128)(2,1)S(1)}, u32[]{:S(2)}, u32[]{:S(2)}) collective-permute-start(bf16[128,512]{1,0:T(8,128)(2,1)S(1)} %slice.77), channel_id=1, source_target_pairs={{0,2},{1,3},{2,0},{3,1},{4,6},{5,7},{6,4},{7,5},{8,10},{9,11},{10,... | collective-permute-start | bytes 393224 | tf_op jit(solution)/shard_map/ppermute | solution.py:89
  108.7 6.4 %collective-permute-start.25 = (bf16[128,512]{1,0:T(8,128)(2,1)S(1)}, bf16[128,512]{1,0:T(8,128)(2,1)S(1)}, u32[]{:S(2)}, u32[]{:S(2)}) collective-permute-start(bf16[128,512]{1,0:T(8,128)(2,1)S(1)} %slice.78), channel_id=1, source_target_pairs={{0,4},{1,5},{2,6},{3,7},{4,0},{5,1},{6,2},{7,3},{8,12},{9,13},{10,... | collective-permute-start | bytes 393224 | tf_op jit(solution)/shard_map/ppermute | solution.py:89
  113.1 9.2 %collective-permute-start.28 = (bf16[256,512]{1,0:T(8,128)(2,1)S(1)}, bf16[256,512]{1,0:T(8,128)(2,1)S(1)}, u32[]{:S(2)}, u32[]{:S(2)}) collective-permute-start(bf16[256,512]{1,0:T(8,128)(2,1)S(1)} %collective-permute-done.26.refs_5_), channel_id=1, source_target_pairs={{0,4},{1,5},{2,6},{3,7},{4,0},{5,1},{6,2},{7,3},{8,12},{9,13},{10,... | collective-permute-start | bytes 786440 | tf_op jit(solution)/shard_map/ppermute | solution.py:89
  115.7 8.1 %collective-permute-start.27 = (bf16[256,512]{1,0:T(8,128)(2,1)S(1)}, bf16[256,512]{1,0:T(8,128)(2,1)S(1)}, u32[]{:S(2)}, u32[]{:S(2)}) collective-permute-start(bf16[256,512]{1,0:T(8,128)(2,1)S(1)} %collective-permute-done.26.refs_5_), channel_id=1, source_target_pairs={{0,2},{1,3},{2,0},{3,1},{4,6},{5,7},{6,4},{7,5},{8,10},{9,11},{10,... | collective-permute-start | bytes 786440 | tf_op jit(solution)/shard_map/ppermute | solution.py:89
  116.9 11.0 %collective-permute-start.33 = (bf16[256,512]{1,0:T(8,128)(2,1)}, bf16[256,512]{1,0:T(8,128)(2,1)S(1)}, u32[]{:S(2)}, u32[]{:S(2)}) collective-permute-start(bf16[256,512]{1,0:T(8,128)(2,1)} %collective-permute-done.31.refs_10_), channel_id=1, source_target_pairs={{0,4},{1,5},{2,6},{3,7},{4,0},{5,1},{6,2},{7,3},{8,12},{9,13},{10,... | collective-permute-start | bytes 786440 | tf_op jit(solution)/shard_map/ppermute | solution.py:89
  122.3 9.1 %collective-permute-start.32 = (bf16[256,512]{1,0:T(8,128)(2,1)}, bf16[256,512]{1,0:T(8,128)(2,1)S(1)}, u32[]{:S(2)}, u32[]{:S(2)}) collective-permute-start(bf16[256,512]{1,0:T(8,128)(2,1)} %collective-permute-done.31.refs_10_), channel_id=1, source_target_pairs={{0,2},{1,3},{2,0},{3,1},{4,6},{5,7},{6,4},{7,5},{8,10},{9,11},{10,... | collective-permute-start | bytes 786440 | tf_op jit(solution)/shard_map/ppermute | solution.py:89
  123.8 8.8 %collective-permute-start.38 = (bf16[256,512]{1,0:T(8,128)(2,1)}, bf16[256,512]{1,0:T(8,128)(2,1)S(1)}, u32[]{:S(2)}, u32[]{:S(2)}) collective-permute-start(bf16[256,512]{1,0:T(8,128)(2,1)} %collective-permute-done.36.refs_15_), channel_id=1, source_target_pairs={{0,4},{1,5},{2,6},{3,7},{4,0},{5,1},{6,2},{7,3},{8,12},{9,13},{10,... | collective-permute-start | bytes 786440 | tf_op jit(solution)/shard_map/ppermute | solution.py:89
  127.9 8.5 %collective-permute-start.37 = (bf16[256,512]{1,0:T(8,128)(2,1)}, bf16[256,512]{1,0:T(8,128)(2,1)S(1)}, u32[]{:S(2)}, u32[]{:S(2)}) collective-permute-start(bf16[256,512]{1,0:T(8,128)(2,1)} %collective-permute-done.36.refs_15_), channel_id=1, source_target_pairs={{0,2},{1,3},{2,0},{3,1},{4,6},{5,7},{6,4},{7,5},{8,10},{9,11},{10,... | collective-permute-start | bytes 786440 | tf_op jit(solution)/shard_map/ppermute | solution.py:89
  131.4 7.7 %collective-permute-start.29 = (bf16[128,512]{1,0:T(8,128)(2,1)}, bf16[128,512]{1,0:T(8,128)(2,1)}, u32[]{:S(2)}, u32[]{:S(2)}) collective-permute-start(bf16[128,512]{1,0:T(8,128)(2,1)} %slice.79), channel_id=1, source_target_pairs={{0,2},{1,3},{2,0},{3,1},{4,6},{5,7},{6,4},{7,5},{8,10},{9,11},{10,... | collective-permute-start | bytes 393224 | tf_op jit(solution)/shard_map/ppermute | solution.py:89
  132.6 8.6 %collective-permute-start.30 = (bf16[128,512]{1,0:T(8,128)(2,1)}, bf16[128,512]{1,0:T(8,128)(2,1)}, u32[]{:S(2)}, u32[]{:S(2)}) collective-permute-start(bf16[128,512]{1,0:T(8,128)(2,1)} %slice.80), channel_id=1, source_target_pairs={{0,4},{1,5},{2,6},{3,7},{4,0},{5,1},{6,2},{7,3},{8,12},{9,13},{10,... | collective-permute-start | bytes 393224 | tf_op jit(solution)/shard_map/ppermute | solution.py:89
  136.4 6.0 %collective-permute-start.34 = (bf16[128,512]{1,0:T(8,128)(2,1)}, bf16[128,512]{1,0:T(8,128)(2,1)}, u32[]{:S(2)}, u32[]{:S(2)}) collective-permute-start(bf16[128,512]{1,0:T(8,128)(2,1)} %slice.81), channel_id=1, source_target_pairs={{0,2},{1,3},{2,0},{3,1},{4,6},{5,7},{6,4},{7,5},{8,10},{9,11},{10,... | collective-permute-start | bytes 393224 | tf_op jit(solution)/shard_map/ppermute | solution.py:89
  139.0 42.8 %collective-permute-start.35 = (bf16[128,512]{1,0:T(8,128)(2,1)S(1)}, bf16[128,512]{1,0:T(8,128)(2,1)S(1)}, u32[]{:S(2)}, u32[]{:S(2)}) collective-permute-start(bf16[128,512]{1,0:T(8,128)(2,1)S(1)} %slice.82), channel_id=1, source_target_pairs={{0,4},{1,5},{2,6},{3,7},{4,0},{5,1},{6,2},{7,3},{8,12},{9,13},{10,... | collective-permute-start | bytes 393224 | tf_op jit(solution)/shard_map/ppermute | solution.py:89
  141.2 40.6 %collective-permute-start.39 = (bf16[128,512]{1,0:T(8,128)(2,1)S(1)}, bf16[128,512]{1,0:T(8,128)(2,1)S(1)}, u32[]{:S(2)}, u32[]{:S(2)}) collective-permute-start(bf16[128,512]{1,0:T(8,128)(2,1)S(1)} %slice.83), channel_id=1, source_target_pairs={{0,2},{1,3},{2,0},{3,1},{4,6},{5,7},{6,4},{7,5},{8,10},{9,11},{10,... | collective-permute-start | bytes 393224 | tf_op jit(solution)/shard_map/ppermute | solution.py:89
  142.4 39.4 %collective-permute-start.40 = (bf16[128,512]{1,0:T(8,128)(2,1)S(1)}, bf16[128,512]{1,0:T(8,128)(2,1)S(1)}, u32[]{:S(2)}, u32[]{:S(2)}) collective-permute-start(bf16[128,512]{1,0:T(8,128)(2,1)S(1)} %slice.84), channel_id=1, source_target_pairs={{0,4},{1,5},{2,6},{3,7},{4,0},{5,1},{6,2},{7,3},{8,12},{9,13},{10,... | collective-permute-start | bytes 393224 | tf_op jit(solution)/shard_map/ppermute | solution.py:89
  190.2 1.6 collective-permute-start.44
  190.6 2.0 %collective-permute-start.41 = (bf16[256,512]{1,0:T(8,128)(2,1)S(1)}, bf16[256,512]{1,0:T(8,128)(2,1)S(1)}, u32[]{:S(2)}, u32[]{:S(2)}) collective-permute-start(bf16[256,512]{1,0:T(8,128)(2,1)S(1)} %get-tuple-element.8), channel_id=1, source_target_pairs={{0,1},{1,0},{2,3},{3,2},{4,5},{5,4},{6,7},{7,6},{8,9},{9,8},{10,11... | collective-permute-start | bytes 786440 | tf_op jit(solution)/shard_map/ppermute | solution.py:89
  (6 other events, 26.8 us)

commit v2 on v1

--- a/solution.py
+++ b/solution.py
@@ -118,14 +118,16 @@
     return lax.dot_general(a, b, (dims, ((), ())), preferred_element_type=jnp.float32)
 
 
-def delta_kernel(places, me_ref, own_ref, mate_ref, own_cot_ref, mate_cot_ref, *refs):
+def delta_kernel(
+    places, me_ref, own_slot_ref, mate_slot_ref, own_ref, mate_ref, own_cot_ref, mate_cot_ref, *refs
+):
     pieces = refs[: len(places)]
-    delta_ref, weight_ref, acc = refs[len(places) :]
+    delta_ref, send_ref, weight_ref, acc = refs[len(places) :]
     me = me_ref[0]
     core = me & 1
     rows = own_ref.shape[0]
-    chip_rows = 2 * pieces[0].shape[0] // 2
-    for n, (mask, first, _) in enumerate(places):
+    chip_rows = pieces[0].shape[0]
+    for n, (mask, first) in enumerate(places):
         piece = pieces[n][...]
         depth = piece.shape[0]
         at = pl.multiple_of(((me ^ mask) >> 1) * chip_rows + first, 128)
@@ -146,58 +148,54 @@
             upstream = cot_ref[:, cols].astype(jnp.float32)
             delta = (upstream - normed * jnp.mean(upstream * normed, axis=1, keepdims=True)) / scale
             delta_ref[pl.ds(at, rows), cols] = delta.astype(jnp.bfloat16)
-
-
-def select_kernel(places, per_peer, me_ref, target_ref, *refs):
-    pieces, sel_ref = refs[: len(places)], refs[len(places)]
-    me = me_ref[0]
-    receive = sel_ref.shape[0] // 2
-    sel_ref[...] = jnp.zeros_like(sel_ref)
-    rows = target_ref.shape[2]
-    for n, (mask, first, _) in enumerate(places):
-        chip = (me ^ mask) >> 1
-        depth = pieces[n].shape[0]
-        for block in range(first // rows, (first + depth) // rows):
-            index = chip * 2 + block
-            want = target_ref[index]
-            delta = pieces[n][block * rows - first : (block + 1) * rows - first, :]
-            for side in range(2):
-                slots = lax.broadcasted_iota(jnp.int32, (2 * per_peer, rows), 0)
-                slots = slots + ((me & -2) + side) * receive + chip * 2 * per_peer
-                hot = (slots == want).astype(jnp.bfloat16)
-                at = pl.multiple_of(side * receive + chip * 2 * per_peer, 2 * per_peer)
-                sel_ref[pl.ds(at, 2 * per_peer), :] += dot(hot, delta, ((1,), (0,))).astype(
-                    jnp.bfloat16
-                )
-
-
-def weight_grad_kernel(places, norm, me_ref, own_ref, mate_ref, *refs):
-    pieces, grad_ref = refs[: len(places)], refs[len(places)]
+    slots = lax.broadcasted_iota(jnp.int32, (send_ref.shape[0], rows), 0)
+    sent = None
+    for side, slot_ref in enumerate((own_slot_ref, mate_slot_ref)):
+        at = pl.multiple_of((core ^ side) * rows, rows)
+        hot = (slots == slot_ref[...]).astype(jnp.bfloat16)
+        part = dot(hot, delta_ref[pl.ds(at, rows), :], ((1,), (0,)))
+        sent = part if sent is None else sent + part
+    send_ref[...] = sent.astype(jnp.bfloat16)
+
+
+def weight_grad_kernel(masks, me_ref, own_ref, mate_ref, *refs):
+    pieces, part_ref, acc = refs[: len(masks)], refs[len(masks)], refs[len(masks) + 1]
     me = me_ref[0]
     core = me & 1
     rows = own_ref.shape[1]
-    total = None
-    for n, (mask, first, _) in enumerate(places):
-        chip = (me ^ mask) >> 1
-        depth = pieces[n].shape[0]
-        for block in range(first // rows, (first + depth) // rows):
-            delta = pieces[n][block * rows - first : (block + 1) * rows - first, :]
-            hidden = jnp.where(core == block, own_ref[chip], mate_ref[chip])
-            part = dot(hidden, delta, ((0,), (0,)))
-            if n == 0 and block == 0:
-                grad_ref[...] = part
+    for n, mask in enumerate(masks):
+        level = (me ^ mask) >> 3
+        for side, ref in enumerate((own_ref, mate_ref)):
+            at = pl.multiple_of((core ^ side) * rows, rows)
+            part = dot(ref[level], pieces[n][pl.ds(at, rows), :], ((0,), (0,)))
+            if n == 0 and side == 0:
+                acc[...] = part
             else:
-                grad_ref[...] += part
-    grad_ref[...] = grad_ref[...] / norm
-
-
-def row_grad_kernel(sel_a_ref, sel_b_ref, weight_a_ref, weight_b_ref, out_ref):
-    total = dot(sel_a_ref[...], weight_a_ref[...], ((1,), (1,)))
-    total += dot(sel_b_ref[...], weight_b_ref[...], ((1,), (1,)))
+                acc[...] += part
+    part_ref[...] = acc[...].astype(jnp.bfloat16)
+
+
+def sum_kernel(norm, parts_ref, grad_ref):
+    half = parts_ref.shape[3]
+    for side in range(2):
+        total = parts_ref[0, side].astype(jnp.float32)
+        for chip in range(1, parts_ref.shape[0]):
+            total += parts_ref[chip, side].astype(jnp.float32)
+        grad_ref[:, side * half : (side + 1) * half] = total / norm
+
+
+def row_grad_kernel(me_ref, got_ref, own_weight_ref, mate_weight_ref, out_ref):
+    core = me_ref[0] & 1
+    receive = out_ref.shape[0]
+    half = got_ref.shape[3]
+    low, high = got_ref[:, 0].reshape(receive, half), got_ref[:, 1].reshape(receive, half)
+    own, mate = jnp.where(core == 0, low, high), jnp.where(core == 0, high, low)
+    total = dot(own, own_weight_ref[...], ((1,), (1,)))
+    total += dot(mate, mate_weight_ref[...], ((1,), (1,)))
     out_ref[...] = total.astype(jnp.bfloat16)
 
 
-def whole(count):
+def vmem(count):
     return [pl.BlockSpec(memory_space=pltpu.VMEM)] * count
 
 
@@ -211,6 +209,8 @@
     half_cols = cols // 2
     size = lax.axis_size("dp")
     chips = size // 2
+    plane = 8
+    levels = size // plane
     per_peer = 2 * rows // size
     receive = size * per_peer
     me = lax.axis_index("dp")
@@ -230,12 +230,14 @@
         jnp.concatenate([mate_weight, own_weight], axis=0),
     )
     weights = gather_chips(piece)
+    places = [(mask, first) for mask, first, _ in weights]
+    arrays = [array for _, _, array in weights]
 
     mate_tokens = swap(tokens, CORE)
-    groups = [[c + 2 * i for i in range(chips)] for c in range(2)]
-    by_chip = tokens.reshape(rows, chips, width_model // chips).transpose(1, 0, 2)
+    columns = [[p + plane * z for z in range(levels)] for p in range(plane)]
+    by_level = tokens.reshape(rows, levels, width_model // levels).transpose(1, 0, 2)
     own_features = lax.all_to_all(
-        by_chip, "dp", split_axis=0, concat_axis=0, axis_index_groups=groups, tiled=True
+        by_level, "dp", split_axis=0, concat_axis=0, axis_index_groups=columns, tiled=True
     )
     mate_features = swap(own_features, CORE)
 
@@ -255,67 +257,72 @@
         positions[:, None] < positions[None, :]
     )
     earlier = jnp.sum(same.astype(jnp.int32), axis=0)
-    target = destination * receive + me * per_peer + earlier
-    targets = lax.all_gather(target.reshape(1, 1, rows), "dp", axis=0, tiled=True)
-
-    places = [(mask, first, None) for mask, first, _ in weights]
-    arrays = [array for _, _, array in weights]
-    delta, weight_half = pl.pallas_call(
+    own_slot = ((destination * 2 + core) * per_peer + earlier).reshape(1, rows)
+    mate_slot = swap(own_slot, CORE)
+
+    delta, send, weight_half = pl.pallas_call(
         functools.partial(delta_kernel, places),
         out_shape=(
             jax.ShapeDtypeStruct((2 * rows, half_cols), jnp.bfloat16),
+            jax.ShapeDtypeStruct((2 * receive, half_cols), jnp.bfloat16),
             jax.ShapeDtypeStruct((width_model, half_cols), jnp.bfloat16),
         ),
-        in_specs=[SCALAR] + whole(4 + len(arrays)),
-        out_specs=tuple(whole(2)),
+        in_specs=[SCALAR] + vmem(6 + len(arrays)),
+        out_specs=tuple(vmem(3)),
         scratch_shapes=[pltpu.VMEM((2, rows, half_cols), jnp.float32)],
         compiler_params=PARAMS,
         name="delta",
-    )(me_scalar, tokens, mate_tokens, own_cot, mate_cot, *arrays)
-
-    mate_half = swap(weight_half, CORE)
-    deltas = gather_chips(delta)
-    arrays = [array for _, _, array in deltas]
-    selected = pl.pallas_call(
-        functools.partial(select_kernel, places, per_peer),
-        out_shape=jax.ShapeDtypeStruct((2 * receive, half_cols), jnp.bfloat16),
-        in_specs=[SCALAR] + whole(1 + len(arrays)),
-        out_specs=whole(1)[0],
-        compiler_params=PARAMS,
-        name="select",
-    )(me_scalar, targets, *arrays)
-    own_selected = lax.dynamic_slice_in_dim(selected, core * receive, receive, 0)
-    mate_selected = swap(
-        lax.dynamic_slice_in_dim(selected, (1 - core) * receive, receive, 0), CORE
-    )
-    chip_grad = pl.pallas_call(
-        functools.partial(weight_grad_kernel, places, math.sqrt(rows * size)),
-        out_shape=jax.ShapeDtypeStruct((2 * rows, half_cols), jnp.float32),
-        in_specs=[SCALAR] + whole(2 + len(arrays)),
-        out_specs=whole(1)[0],
+    )(me_scalar, own_slot, mate_slot, tokens, mate_tokens, own_cot, mate_cot, *arrays)
+
+    masks = [plane * z for z in range(levels)]
+    deltas = [delta if mask == 0 else swap(delta, mask) for mask in masks]
+    part = pl.pallas_call(
+        functools.partial(weight_grad_kernel, masks),
+        out_shape=jax.ShapeDtypeStruct((width_model // levels, half_cols), jnp.bfloat16),
+        in_specs=[SCALAR] + vmem(2 + len(deltas)),
+        out_specs=vmem(1)[0],
+        scratch_shapes=[pltpu.VMEM((width_model // levels, half_cols), jnp.float32)],
         compiler_params=PARAMS,
         name="weight_grad",
-    )(me_scalar, own_features, mate_features, *arrays)
+    )(me_scalar, own_features, mate_features, *deltas)
     shard = width_model // size
-    own_grad = lax.dynamic_slice_in_dim(chip_grad, core * shard, shard, 0)
-    mate_grad = swap(lax.dynamic_slice_in_dim(chip_grad, (1 - core) * shard, shard, 0), CORE)
-    key_grad = jnp.where(
-        core == 0,
-        jnp.concatenate([own_grad, mate_grad], axis=1),
-        jnp.concatenate([mate_grad, own_grad], axis=1),
-    )
-
+    planes = [[z * plane + p for p in range(plane)] for z in range(levels)]
+    parts = lax.all_to_all(
+        part.reshape(plane, shard, half_cols),
+        "dp",
+        split_axis=0,
+        concat_axis=0,
+        axis_index_groups=planes,
+        tiled=True,
+    )
+    key_grad = pl.pallas_call(
+        functools.partial(sum_kernel, math.sqrt(rows * size)),
+        out_shape=jax.ShapeDtypeStruct((shard, cols), jnp.float32),
+        in_specs=vmem(1),
+        out_specs=vmem(1)[0],
+        compiler_params=PARAMS,
+        name="sum",
+    )(parts.reshape(plane // 2, 2, shard, half_cols))
+
+    mate_half = swap(weight_half, CORE)
+    got = lax.all_to_all(
+        send.reshape(size, 2 * per_peer, half_cols), "dp", split_axis=0, concat_axis=0, tiled=True
+    )
     tile = 1024
     row_grads = pl.pallas_call(
         row_grad_kernel,
         out_shape=jax.ShapeDtypeStruct((receive, width_model), jnp.bfloat16),
         grid=(width_model // tile,),
-        in_specs=[pl.BlockSpec((receive, half_cols), lambda i: (0, 0))] * 2
-        + [pl.BlockSpec((tile, half_cols), lambda i: (i, 0))] * 2,
+        in_specs=[
+            SCALAR,
+            pl.BlockSpec((chips, 2, 2 * per_peer, half_cols), lambda i: (0, 0, 0, 0)),
+            pl.BlockSpec((tile, half_cols), lambda i: (i, 0)),
+            pl.BlockSpec((tile, half_cols), lambda i: (i, 0)),
+        ],
         out_specs=pl.BlockSpec((receive, tile), lambda i: (0, i)),
         compiler_params=PARAMS,
         name="row_grad",
-    )(own_selected, mate_selected, weight_half, mate_half)
+    )(me_scalar, got.reshape(chips, 2, 2 * per_peer, half_cols), weight_half, mate_half)
     return (row_grads, key_grad)
 
 

time: 199 us -> 143 us (0.72)
  starting transfers between devices: 62.7 us -> 38.8 us
  blocking collectives: 37.4 us -> 17.8 us
  waiting for transfers between devices: 67.6 us -> 55.7 us
  Pallas kernels: 17.4 us -> 14.3 us
  local copies, waits for them, and re-layouts: 8.74 us -> 11.1 us
    all_gather x1 -> x0, blocking collectives: 37.4 us -> none  [per_device_paired(): lax.all_gather(target.reshape(1, 1, rows), 'dp', axis=0, tiled=True)]
    ppermute x45 -> x28, starting transfers between devices: 56.3 us -> 26.5 us  [swap(): return lax.ppermute(value, 'dp', [(i, i ^ mask) for i in range(size)])]
    ppermute x45 -> x28, waiting for transfers between devices: 67.6 us -> 41 us  [swap(): return lax.ppermute(value, 'dp', [(i, i ^ mask) for i in range(size)])]
    all_to_all x0 -> x1, blocking collectives: none -> 17.8 us  [per_device_paired(): lax.all_to_all(part.reshape(plane, shard, half_cols), 'dp', split_axis=0,...]
    all_to_all x1 -> x2, waiting for transfers between devices: 0.01 us -> 14.6 us  [the longest x1 14.6 us: per_device_paired(): lax.all_to_all(send.reshape(size, 2 * per_peer, half_cols), 'dp', split_a...]
    all_to_all x1 -> x2, starting transfers between devices: 6.32 us -> 12.3 us  [the longest x1 6.55 us: per_device_paired(): lax.all_to_all(send.reshape(size, 2 * per_peer, half_cols), 'dp', split_a...]
    unnamed x17 -> x15, local copies, waits for them, and re-layouts: 4.15 us -> 8.66 us
    pallas_call x2, Pallas kernels: 6.45 us -> 3.28 us  [the longest x1 2.35 us: per_device_paired(): pl.pallas_call(functools.partial(weight_grad_kernel, masks), out_shape=ja...]
  transfers between devices with their start and end apart: 46 -> 30, of which waited for: 20 -> 15; matrix products, arithmetic and copies ran while one was open for 4% -> 5% of each run, Pallas kernels for 3% -> 6%
where the time goes in v2:
time: 143 us
  waiting for transfers between devices  55.7 us (39%)
  starting transfers between devices  38.8 us (27%)
  blocking collectives  17.8 us (12%)
  Pallas kernels  14.3 us (10%)
  local copies, waits for them, and re-layouts  11.1 us (8%)
  other arithmetic  4.28 us (3%)
    ppermute x28, waiting for transfers between devices, swap(): return lax.ppermute(value, 'dp', [(i, i ^ mask) for i in range(size)])  41 us
    ppermute x28, starting transfers between devices, swap(): return lax.ppermute(value, 'dp', [(i, i ^ mask) for i in range(size)])  26.5 us
    all_to_all x1, blocking collectives, per_device_paired(): lax.all_to_all(part.reshape(plane, shard, half_cols), 'dp', split_axis=0,...  17.8 us
    all_to_all x1, waiting for transfers between devices, per_device_paired(): lax.all_to_all(send.reshape(size, 2 * per_peer, half_cols), 'dp', split_a...  14.6 us
    unnamed x15, local copies, waits for them, and re-layouts  8.66 us
    all_to_all x1, starting transfers between devices, per_device_paired(): lax.all_to_all(send.reshape(size, 2 * per_peer, half_cols), 'dp', split_a...  6.55 us
    pallas_call x1, Pallas kernels, per_device_paired(): pl.pallas_call(row_grad_kernel, out_shape=jax.ShapeDtypeStruct((receive,...  5.77 us
    all_to_all x1, starting transfers between devices, per_device_paired(): lax.all_to_all(by_level, 'dp', split_axis=0, concat_axis=0, axis_index_gr...  5.71 us
  transfers between devices with their start and end apart: 30, of which 15 were waited for; matrix products, arithmetic and copies ran while one was open for 5% of the time, Pallas kernels for 6%

profile of v2, /device:TPU:0, one launch (start us, length us, event | category | flops | bytes accessed | tf_op | source)
XLA Modules:
  0.0 142.7 jit_solution(8940250826378995988)
XLA Ops:
  0.6 0.8 convert_reduce_fusion
  1.5 0.7 bitcast_add_fusion.own_slot_ref
  2.6 1.0 constant_dynamic-slice_fusion
  4.2 0.8 reduce-window.4
  5.1 0.7 select_reduce_fusion
  5.9 2.6 %collective-permute-start.4 = (bf16[256,512]{1,0:T(8,128)(2,1)S(1)}, bf16[256,512]{1,0:T(8,128)(2,1)S(1)}, u32[]{:S(2)}, u32[]{:S(2)}) collective-permute-start(bf16[256,512]{1,0:T(8,128)(2,1)S(1)} %maximum_select_fusion.refs_0_), channel_id=1, source_target_pairs={{0,2},{1,3},{2,0},{3,1},{4,6},{5,7},{6,4},{7,5},{8,10},{9,11},{10,... | collective-permute-start | bytes 786440 | tf_op jit(solution)/shard_map/ppermute | solution.py:89
  8.5 1.5 %collective-permute-start.5 = (bf16[256,512]{1,0:T(8,128)(2,1)S(1)}, bf16[256,512]{1,0:T(8,128)(2,1)S(1)}, u32[]{:S(2)}, u32[]{:S(2)}) collective-permute-start(bf16[256,512]{1,0:T(8,128)(2,1)S(1)} %maximum_select_fusion.refs_0_), channel_id=1, source_target_pairs={{0,4},{1,5},{2,6},{3,7},{4,0},{5,1},{6,2},{7,3},{8,12},{9,13},{10,... | collective-permute-start | bytes 786440 | tf_op jit(solution)/shard_map/ppermute | solution.py:89
  10.0 2.6 %collective-permute-start.8 = (bf16[256,512]{1,0:T(8,128)(2,1)S(1)}, bf16[256,512]{1,0:T(8,128)(2,1)S(1)}, u32[]{:S(2)}, u32[]{:S(2)}) collective-permute-start(bf16[256,512]{1,0:T(8,128)(2,1)S(1)} %maximum_select_fusion.refs_0_), channel_id=1, source_target_pairs={{0,16},{1,17},{2,18},{3,19},{4,20},{5,21},{6,22},{7,23},{8,24},{9,... | collective-permute-start | bytes 786440 | tf_op jit(solution)/shard_map/ppermute | solution.py:89
  12.6 1.1 compare_select_fusion
  13.8 1.3 collective-permute-done.2.mate_cot_ref
  15.1 0.6 copy-done.5
  15.8 1.6 %collective-permute-start.13 = (bf16[256,512]{1,0:T(8,128)(2,1)S(1)}, bf16[256,512]{1,0:T(8,128)(2,1)}, u32[]{:S(2)}, u32[]{:S(2)}) collective-permute-start(bf16[256,512]{1,0:T(8,128)(2,1)S(1)} %maximum_select_fusion.refs_0_), channel_id=1, source_target_pairs={{0,8},{1,9},{2,10},{3,11},{4,12},{5,13},{6,14},{7,15},{8,0},{9,1},... | collective-permute-start | bytes 786440 | tf_op jit(solution)/shard_map/ppermute | solution.py:89
  17.3 7.4 %collective-permute-done.8.refs_5_ = bf16[256,512]{1,0:T(8,128)(2,1)S(1)} collective-permute-done((bf16[256,512]{1,0:T(8,128)(2,1)S(1)}, bf16[256,512]{1,0:T(8,128)(2,1)S(1)}, u32[]{:S(2)}, u32[]{:S(2)}) %collective-permute-start.8) | collective-permute-done | bytes 262176 | tf_op jit(solution)/shard_map/ppermute | solution.py:89
  26.4 0.7 copy-done.1
  27.1 2.3 %collective-permute-done.13.refs_10_ = bf16[256,512]{1,0:T(8,128)(2,1)} collective-permute-done((bf16[256,512]{1,0:T(8,128)(2,1)S(1)}, bf16[256,512]{1,0:T(8,128)(2,1)}, u32[]{:S(2)}, u32[]{:S(2)}) %collective-permute-start.13) | collective-permute-done | bytes 262176 | tf_op jit(solution)/shard_map/ppermute | solution.py:89
  30.0 3.0 %collective-permute-done.9.refs_6_ = bf16[256,512]{1,0:T(8,128)(2,1)S(1)} collective-permute-done((bf16[256,512]{1,0:T(8,128)(2,1)S(1)}, bf16[256,512]{1,0:T(8,128)(2,1)S(1)}, u32[]{:S(2)}, u32[]{:S(2)}) %collective-permute-start.9) | collective-permute-done | bytes 262176 | tf_op jit(solution)/shard_map/ppermute | solution.py:89
  33.5 0.9 collective-permute-done.18.refs_15_
  34.9 0.7 collective-permute-start.20
  35.5 1.6 %copy.10 = bf16[128,4096]{0,1:T(8,128)(2,1)S(1)} copy(bf16[128,4096]{1,0:T(8,128)(2,1)} %own_ref.1) | data formatting | bytes 2097152 | tf_op args[0]
  37.2 1.3 copy.11
  38.5 5.7 %all-to-all-start.1 = ((bf16[4,128,1024]{2,1,0:T(8,128)(2,1)}), bf16[4,128,1024]{2,1,0:T(8,128)(2,1)S(1)}, u32[]{:S(2)}, u32[]{:S(2)}) async-start(bf16[4,128,1024]{2,1,0:T(8,128)(2,1)} %bitcast.18), calls=%async_computation.1 | async-start | bytes 2097152 | tf_op jit(solution)/shard_map/all_to_all | solution.py:239
  44.3 1.6 %collective-permute-start.6 = (bf16[128,512]{1,0:T(8,128)(2,1)S(1)}, bf16[128,512]{1,0:T(8,128)(2,1)S(1)}, u32[]{:S(2)}, u32[]{:S(2)}) collective-permute-start(bf16[128,512]{1,0:T(8,128)(2,1)S(1)} %slice.37), channel_id=1, source_target_pairs={{0,2},{1,3},{2,0},{3,1},{4,6},{5,7},{6,4},{7,5},{8,10},{9,11},{10,... | collective-permute-start | bytes 393224 | tf_op jit(solution)/shard_map/ppermute | solution.py:89
  45.8 0.6 collective-permute-start.7
  47.0 1.4 collective-permute-start.12
  48.5 2.2 %collective-permute-done.6.refs_3_ = bf16[128,512]{1,0:T(8,128)(2,1)S(1)} collective-permute-done((bf16[128,512]{1,0:T(8,128)(2,1)S(1)}, bf16[128,512]{1,0:T(8,128)(2,1)S(1)}, u32[]{:S(2)}, u32[]{:S(2)}) %collective-permute-start.6) | collective-permute-done | bytes 131104 | tf_op jit(solution)/shard_map/ppermute | solution.py:89
  50.7 1.4 collective-permute-start.16
  52.2 0.6 collective-permute-start.17
  53.4 1.5 %collective-permute-start.21 = (bf16[128,512]{1,0:T(8,128)(2,1)S(1)}, bf16[128,512]{1,0:T(8,128)(2,1)S(1)}, u32[]{:S(2)}, u32[]{:S(2)}) collective-permute-start(bf16[128,512]{1,0:T(8,128)(2,1)S(1)} %slice.43), channel_id=1, source_target_pairs={{0,2},{1,3},{2,0},{3,1},{4,6},{5,7},{6,4},{7,5},{8,10},{9,11},{10,... | collective-permute-start | bytes 393224 | tf_op jit(solution)/shard_map/ppermute | solution.py:89
  54.9 0.7 collective-permute-start.22
  55.7 1.5 %collective-permute-done.17.refs_14_ = bf16[128,512]{1,0:T(8,128)(2,1)S(1)} collective-permute-done((bf16[128,512]{1,0:T(8,128)(2,1)S(1)}, bf16[128,512]{1,0:T(8,128)(2,1)S(1)}, u32[]{:S(2)}, u32[]{:S(2)}) %collective-permute-start.17) | collective-permute-done | bytes 131104 | tf_op jit(solution)/shard_map/ppermute | solution.py:89
  57.2 1.2 collective-permute-done.21.refs_18_
  58.4 1.5 %collective-permute-done.22.refs_19_ = bf16[128,512]{1,0:T(8,128)(2,1)S(1)} collective-permute-done((bf16[128,512]{1,0:T(8,128)(2,1)S(1)}, bf16[128,512]{1,0:T(8,128)(2,1)S(1)}, u32[]{:S(2)}, u32[]{:S(2)}) %collective-permute-start.22) | collective-permute-done | bytes 131104 | tf_op jit(solution)/shard_map/ppermute | solution.py:89
  59.9 0.9 copy-done.2
  60.8 0.9 copy-done.6
  61.7 5.2 %delta.1 = (bf16[256,512]{1,0:T(8,128)(2,1)S(1)}, bf16[512,512]{1,0:T(8,128)(2,1)}, bf16[4096,512]{1,0:T(8,128)(2,1)}) custom-call(s32[1]{0:T(128)} %bitcast.me_ref, s32[1,128]{1,0:T(1,128)S(1)} %bitcast_add_fusion.own_slot_ref, s32[1,128]{1,0:T(1,128)S(1)} %collective-permute-done.mate_slot_ref, bf16[128,4096]{1,0:T(8,128)(2,1)} %own_ref.1, ...), custom_call_target="tpu_custom_call" | custom-call | tf_op jit(solution)/shard_map/delta/pallas_call | solution.py:263
  67.0 0.7 copy-done.3
  68.2 1.8 %collective-permute-start.25 = (bf16[256,512]{1,0:T(8,128)(2,1)}, bf16[256,512]{1,0:T(8,128)(2,1)S(1)}, u32[]{:S(2)}, u32[]{:S(2)}) collective-permute-start(bf16[256,512]{1,0:T(8,128)(2,1)} %copy-done.3), channel_id=1, source_target_pairs={{0,8},{1,9},{2,10},{3,11},{4,12},{5,13},{6,14},{7,15},{8,0},{9,1},... | collective-permute-start | bytes 786440 | tf_op jit(solution)/shard_map/ppermute | solution.py:89
  70.0 2.6 %collective-permute-start.26 = (bf16[256,512]{1,0:T(8,128)(2,1)}, bf16[256,512]{1,0:T(8,128)(2,1)S(1)}, u32[]{:S(2)}, u32[]{:S(2)}) collective-permute-start(bf16[256,512]{1,0:T(8,128)(2,1)} %copy-done.3), channel_id=1, source_target_pairs={{0,16},{1,17},{2,18},{3,19},{4,20},{5,21},{6,22},{7,23},{8,24},{9,... | collective-permute-start | bytes 786440 | tf_op jit(solution)/shard_map/ppermute | solution.py:89
  72.7 9.0 %collective-permute-done.25.refs_1_ = bf16[256,512]{1,0:T(8,128)(2,1)S(1)} collective-permute-done((bf16[256,512]{1,0:T(8,128)(2,1)}, bf16[256,512]{1,0:T(8,128)(2,1)S(1)}, u32[]{:S(2)}, u32[]{:S(2)}) %collective-permute-start.25) | collective-permute-done | bytes 262176 | tf_op jit(solution)/shard_map/ppermute | solution.py:89
  81.7 9.8 %collective-permute-done.26.refs_2_ = bf16[256,512]{1,0:T(8,128)(2,1)S(1)} collective-permute-done((bf16[256,512]{1,0:T(8,128)(2,1)}, bf16[256,512]{1,0:T(8,128)(2,1)S(1)}, u32[]{:S(2)}, u32[]{:S(2)}) %collective-permute-start.26) | collective-permute-done | bytes 262176 | tf_op jit(solution)/shard_map/ppermute | solution.py:89
  91.5 0.9 copy-done.4
  92.5 2.3 %weight_grad.1 = bf16[1024,512]{1,0:T(8,128)(2,1)S(1)} custom-call(s32[1]{0:T(128)} %bitcast.me_ref, bf16[4,128,1024]{2,1,0:T(8,128)(2,1)S(1)} %all-to-all-done.1.own_ref, bf16[4,128,1024]{2,1,0:T(8,128)(2,1)S(1)} %collective-permute-done.24.mate_ref, bf16[256,512]{1,0:T(8,128)(2,1)S(1)} %copy-done.4, bf16[256,512]{1,0:T(8,128)(2,1)S(1)} %collective-permute-done.25.refs_1_, ...), custom_call_target="tpu_custom_call" | custom-call | tf_op jit(solution)/shard_map/weight_grad/pallas_call | solution.py:279
  94.8 17.8 %all_to_all.15 = bf16[8,128,512]{2,1,0:T(8,128)(2,1)S(1)} all-to-all(bf16[8,128,512]{2,1,0:T(8,128)(2,1)S(1)} %bitcast.15), channel_id=1, replica_groups={{0,1,2,3,4,5,6,7},{8,9,10,11,12,13,14,15},{16,17,18,19,20,21,22,23},{24..., dimensions={0} | all-to-all | bytes 2097152 | tf_op jit(solution)/shard_map/all_to_all | solution.py:290
  112.6 6.6 %all-to-all-start = ((bf16[32,16,512]{2,1,0:T(8,128)(2,1)}), bf16[32,16,512]{2,1,0:T(8,128)(2,1)S(1)}, u32[]{:S(2)}, u32[]{:S(2)}) async-start(bf16[32,16,512]{2,1,0:T(8,128)(2,1)} %bitcast.6), calls=%async_computation | async-start | bytes 1048576 | tf_op jit(solution)/shard_map/all_to_all | solution.py:308
  119.2 0.9 sum.1
  120.1 14.6 %all-to-all-done = bf16[32,16,512]{2,1,0:T(8,128)(2,1)S(1)} async-done(((bf16[32,16,512]{2,1,0:T(8,128)(2,1)}), bf16[32,16,512]{2,1,0:T(8,128)(2,1)S(1)}, u32[]{:S(2)}, u32[]{:S(2)}) %all-to-all-start) | async-done | bytes 524320 | tf_op jit(solution)/shard_map/all_to_all | solution.py:308
  134.7 2.2 %copy-done = bf16[4096,512]{1,0:T(8,128)(2,1)S(1)} copy-done((bf16[4096,512]{1,0:T(8,128)(2,1)S(1)}, bf16[4096,512]{1,0:T(8,128)(2,1)}, u32[]{:S(2)}) %copy-start) | copy-done | bytes 4194328
  136.9 5.8 %row_grad.1 = bf16[256,4096]{1,0:T(8,128)(2,1)} custom-call(s32[1]{0:T(128)} %bitcast.me_ref, bf16[16,2,16,512]{3,2,1,0:T(8,128)(2,1)S(1)} %bitcast.17, bf16[4096,512]{1,0:T(8,128)(2,1)S(1)} %copy-done, bf16[4096,512]{1,0:T(8,128)(2,1)} %collective-permute-done.23.mate_weight_ref), custom_call_target="tpu_custom_call" | custom-call | tf_op jit(solution)/shard_map/row_grad/pallas_call | solution.py:312
  (52 shorter events, 6.5 us)
Async XLA Ops:
  2.1 11.5 %collective-permute-start = (s32[1,128]{1,0:T(1,128)S(1)}, s32[1,128]{1,0:T(1,128)S(1)}, u32[]{:S(2)}, u32[]{:S(2)}) collective-permute-start(s32[1,128]{1,0:T(1,128)S(1)} %bitcast_add_fusion.own_slot_ref), channel_id=1, source_target_pairs={{0,1},{1,0},{2,3},{3,2},{4,5},{5,4},{6,7},{7,6},{8,9},{9,8},{10,11... | collective-permute-start | bytes 1544 | tf_op jit(solution)/shard_map/ppermute | solution.py:89
  2.6 54.6 %collective-permute-start.1 = (bf16[128,4096]{1,0:T(8,128)(2,1)}, bf16[128,4096]{1,0:T(8,128)(2,1)}, u32[]{:S(2)}, u32[]{:S(2)}) collective-permute-start(bf16[128,4096]{1,0:T(8,128)(2,1)} %own_ref.1), channel_id=1, source_target_pairs={{0,1},{1,0},{2,3},{3,2},{4,5},{5,4},{6,7},{7,6},{8,9},{9,8},{10,11... | collective-permute-start | bytes 3145736 | tf_op jit(solution)/shard_map/ppermute | solution.py:89
  3.6 2.2 %collective-permute-start.3 = (bf16[128,512]{1,0:T(8,128)(2,1)S(1)}, bf16[128,512]{1,0:T(8,128)(2,1)S(1)}, u32[]{:S(2)}, u32[]{:S(2)}) collective-permute-start(bf16[128,512]{1,0:T(8,128)(2,1)S(1)} %get-tuple-element.9), channel_id=1, source_target_pairs={{0,1},{1,0},{2,3},{3,2},{4,5},{5,4},{6,7},{7,6},{8,9},{9,8},{10,11... | collective-permute-start | bytes 393224 | tf_op jit(solution)/shard_map/ppermute | solution.py:89
  5.9 19.4 %collective-permute-start.4 = (bf16[256,512]{1,0:T(8,128)(2,1)S(1)}, bf16[256,512]{1,0:T(8,128)(2,1)S(1)}, u32[]{:S(2)}, u32[]{:S(2)}) collective-permute-start(bf16[256,512]{1,0:T(8,128)(2,1)S(1)} %maximum_select_fusion.refs_0_), channel_id=1, source_target_pairs={{0,2},{1,3},{2,0},{3,1},{4,6},{5,7},{6,4},{7,5},{8,10},{9,11},{10,... | collective-permute-start | bytes 786440 | tf_op jit(solution)/shard_map/ppermute | solution.py:89
  8.5 17.4 %collective-permute-start.5 = (bf16[256,512]{1,0:T(8,128)(2,1)S(1)}, bf16[256,512]{1,0:T(8,128)(2,1)S(1)}, u32[]{:S(2)}, u32[]{:S(2)}) collective-permute-start(bf16[256,512]{1,0:T(8,128)(2,1)S(1)} %maximum_select_fusion.refs_0_), channel_id=1, source_target_pairs={{0,4},{1,5},{2,6},{3,7},{4,0},{5,1},{6,2},{7,3},{8,12},{9,13},{10,... | collective-permute-start | bytes 786440 | tf_op jit(solution)/shard_map/ppermute | solution.py:89
  10.0 14.8 %collective-permute-start.8 = (bf16[256,512]{1,0:T(8,128)(2,1)S(1)}, bf16[256,512]{1,0:T(8,128)(2,1)S(1)}, u32[]{:S(2)}, u32[]{:S(2)}) collective-permute-start(bf16[256,512]{1,0:T(8,128)(2,1)S(1)} %maximum_select_fusion.refs_0_), channel_id=1, source_target_pairs={{0,16},{1,17},{2,18},{3,19},{4,20},{5,21},{6,22},{7,23},{8,24},{9,... | collective-permute-start | bytes 786440 | tf_op jit(solution)/shard_map/ppermute | solution.py:89
  13.7 1.4 collective-permute-start.2
  15.1 0.7 copy-start.5
  15.8 13.7 %collective-permute-start.13 = (bf16[256,512]{1,0:T(8,128)(2,1)S(1)}, bf16[256,512]{1,0:T(8,128)(2,1)}, u32[]{:S(2)}, u32[]{:S(2)}) collective-permute-start(bf16[256,512]{1,0:T(8,128)(2,1)S(1)} %maximum_select_fusion.refs_0_), channel_id=1, source_target_pairs={{0,8},{1,9},{2,10},{3,11},{4,12},{5,13},{6,14},{7,15},{8,0},{9,1},... | collective-permute-start | bytes 786440 | tf_op jit(solution)/shard_map/ppermute | solution.py:89
  24.7 8.2 %collective-permute-start.9 = (bf16[256,512]{1,0:T(8,128)(2,1)S(1)}, bf16[256,512]{1,0:T(8,128)(2,1)S(1)}, u32[]{:S(2)}, u32[]{:S(2)}) collective-permute-start(bf16[256,512]{1,0:T(8,128)(2,1)S(1)} %collective-permute-done.8.refs_5_), channel_id=1, source_target_pairs={{0,2},{1,3},{2,0},{3,1},{4,6},{5,7},{6,4},{7,5},{8,10},{9,11},{10,... | collective-permute-start | bytes 786440 | tf_op jit(solution)/shard_map/ppermute | solution.py:89
  25.3 9.1 %collective-permute-start.18 = (bf16[256,512]{1,0:T(8,128)(2,1)S(1)}, bf16[256,512]{1,0:T(8,128)(2,1)}, u32[]{:S(2)}, u32[]{:S(2)}) collective-permute-start(bf16[256,512]{1,0:T(8,128)(2,1)S(1)} %collective-permute-done.8.refs_5_), channel_id=1, source_target_pairs={{0,8},{1,9},{2,10},{3,11},{4,12},{5,13},{6,14},{7,15},{8,0},{9,1},... | collective-permute-start | bytes 786440 | tf_op jit(solution)/shard_map/ppermute | solution.py:89
  25.9 9.0 %collective-permute-start.10 = (bf16[256,512]{1,0:T(8,128)(2,1)S(1)}, bf16[256,512]{1,0:T(8,128)(2,1)S(1)}, u32[]{:S(2)}, u32[]{:S(2)}) collective-permute-start(bf16[256,512]{1,0:T(8,128)(2,1)S(1)} %collective-permute-done.8.refs_5_), channel_id=1, source_target_pairs={{0,4},{1,5},{2,6},{3,7},{4,0},{5,1},{6,2},{7,3},{8,12},{9,13},{10,... | collective-permute-start | bytes 786440 | tf_op jit(solution)/shard_map/ppermute | solution.py:89
  26.4 0.7 copy-start.1
  29.4 14.8 %collective-permute-start.14 = (bf16[256,512]{1,0:T(8,128)(2,1)}, bf16[256,512]{1,0:T(8,128)(2,1)S(1)}, u32[]{:S(2)}, u32[]{:S(2)}) collective-permute-start(bf16[256,512]{1,0:T(8,128)(2,1)} %collective-permute-done.13.refs_10_), channel_id=1, source_target_pairs={{0,2},{1,3},{2,0},{3,1},{4,6},{5,7},{6,4},{7,5},{8,10},{9,11},{10,... | collective-permute-start | bytes 786440 | tf_op jit(solution)/shard_map/ppermute | solution.py:89
  33.0 12.8 %collective-permute-start.15 = (bf16[256,512]{1,0:T(8,128)(2,1)}, bf16[256,512]{1,0:T(8,128)(2,1)S(1)}, u32[]{:S(2)}, u32[]{:S(2)}) collective-permute-start(bf16[256,512]{1,0:T(8,128)(2,1)} %collective-permute-done.13.refs_10_), channel_id=1, source_target_pairs={{0,4},{1,5},{2,6},{3,7},{4,0},{5,1},{6,2},{7,3},{8,12},{9,13},{10,... | collective-permute-start | bytes 786440 | tf_op jit(solution)/shard_map/ppermute | solution.py:89
  34.3 12.1 %collective-permute-start.19 = (bf16[256,512]{1,0:T(8,128)(2,1)}, bf16[256,512]{1,0:T(8,128)(2,1)S(1)}, u32[]{:S(2)}, u32[]{:S(2)}) collective-permute-start(bf16[256,512]{1,0:T(8,128)(2,1)} %collective-permute-done.18.refs_15_), channel_id=1, source_target_pairs={{0,2},{1,3},{2,0},{3,1},{4,6},{5,7},{6,4},{7,5},{8,10},{9,11},{10,... | collective-permute-start | bytes 786440 | tf_op jit(solution)/shard_map/ppermute | solution.py:89
  34.9 12.1 %collective-permute-start.20 = (bf16[256,512]{1,0:T(8,128)(2,1)}, bf16[256,512]{1,0:T(8,128)(2,1)S(1)}, u32[]{:S(2)}, u32[]{:S(2)}) collective-permute-start(bf16[256,512]{1,0:T(8,128)(2,1)} %collective-permute-done.18.refs_15_), channel_id=1, source_target_pairs={{0,4},{1,5},{2,6},{3,7},{4,0},{5,1},{6,2},{7,3},{8,12},{9,13},{10,... | collective-permute-start | bytes 786440 | tf_op jit(solution)/shard_map/ppermute | solution.py:89
  38.5 29.2 %all-to-all-start.1 = ((bf16[4,128,1024]{2,1,0:T(8,128)(2,1)}), bf16[4,128,1024]{2,1,0:T(8,128)(2,1)S(1)}, u32[]{:S(2)}, u32[]{:S(2)}) async-start(bf16[4,128,1024]{2,1,0:T(8,128)(2,1)} %bitcast.18), calls=%async_computation.1 | async-start | bytes 2097152 | tf_op jit(solution)/shard_map/all_to_all | solution.py:239
  44.3 6.4 %collective-permute-start.6 = (bf16[128,512]{1,0:T(8,128)(2,1)S(1)}, bf16[128,512]{1,0:T(8,128)(2,1)S(1)}, u32[]{:S(2)}, u32[]{:S(2)}) collective-permute-start(bf16[128,512]{1,0:T(8,128)(2,1)S(1)} %slice.37), channel_id=1, source_target_pairs={{0,2},{1,3},{2,0},{3,1},{4,6},{5,7},{6,4},{7,5},{8,10},{9,11},{10,... | collective-permute-start | bytes 393224 | tf_op jit(solution)/shard_map/ppermute | solution.py:89
  45.8 6.4 %collective-permute-start.7 = (bf16[128,512]{1,0:T(8,128)(2,1)S(1)}, bf16[128,512]{1,0:T(8,128)(2,1)S(1)}, u32[]{:S(2)}, u32[]{:S(2)}) collective-permute-start(bf16[128,512]{1,0:T(8,128)(2,1)S(1)} %slice.38), channel_id=1, source_target_pairs={{0,4},{1,5},{2,6},{3,7},{4,0},{5,1},{6,2},{7,3},{8,12},{9,13},{10,... | collective-permute-start | bytes 393224 | tf_op jit(solution)/shard_map/ppermute | solution.py:89
  46.5 7.0 %collective-permute-start.11 = (bf16[128,512]{1,0:T(8,128)(2,1)S(1)}, bf16[128,512]{1,0:T(8,128)(2,1)S(1)}, u32[]{:S(2)}, u32[]{:S(2)}) collective-permute-start(bf16[128,512]{1,0:T(8,128)(2,1)S(1)} %slice.39), channel_id=1, source_target_pairs={{0,2},{1,3},{2,0},{3,1},{4,6},{5,7},{6,4},{7,5},{8,10},{9,11},{10,... | collective-permute-start | bytes 393224 | tf_op jit(solution)/shard_map/ppermute | solution.py:89
  47.0 7.9 %collective-permute-start.12 = (bf16[128,512]{1,0:T(8,128)(2,1)S(1)}, bf16[128,512]{1,0:T(8,128)(2,1)S(1)}, u32[]{:S(2)}, u32[]{:S(2)}) collective-permute-start(bf16[128,512]{1,0:T(8,128)(2,1)S(1)} %slice.40), channel_id=1, source_target_pairs={{0,4},{1,5},{2,6},{3,7},{4,0},{5,1},{6,2},{7,3},{8,12},{9,13},{10,... | collective-permute-start | bytes 393224 | tf_op jit(solution)/shard_map/ppermute | solution.py:89
  50.7 5.0 %collective-permute-start.16 = (bf16[128,512]{1,0:T(8,128)(2,1)S(1)}, bf16[128,512]{1,0:T(8,128)(2,1)S(1)}, u32[]{:S(2)}, u32[]{:S(2)}) collective-permute-start(bf16[128,512]{1,0:T(8,128)(2,1)S(1)} %slice.41), channel_id=1, source_target_pairs={{0,2},{1,3},{2,0},{3,1},{4,6},{5,7},{6,4},{7,5},{8,10},{9,11},{10,... | collective-permute-start | bytes 393224 | tf_op jit(solution)/shard_map/ppermute | solution.py:89
  52.2 5.0 %collective-permute-start.17 = (bf16[128,512]{1,0:T(8,128)(2,1)S(1)}, bf16[128,512]{1,0:T(8,128)(2,1)S(1)}, u32[]{:S(2)}, u32[]{:S(2)}) collective-permute-start(bf16[128,512]{1,0:T(8,128)(2,1)S(1)} %slice.42), channel_id=1, source_target_pairs={{0,4},{1,5},{2,6},{3,7},{4,0},{5,1},{6,2},{7,3},{8,12},{9,13},{10,... | collective-permute-start | bytes 393224 | tf_op jit(solution)/shard_map/ppermute | solution.py:89
  53.4 5.0 %collective-permute-start.21 = (bf16[128,512]{1,0:T(8,128)(2,1)S(1)}, bf16[128,512]{1,0:T(8,128)(2,1)S(1)}, u32[]{:S(2)}, u32[]{:S(2)}) collective-permute-start(bf16[128,512]{1,0:T(8,128)(2,1)S(1)} %slice.43), channel_id=1, source_target_pairs={{0,2},{1,3},{2,0},{3,1},{4,6},{5,7},{6,4},{7,5},{8,10},{9,11},{10,... | collective-permute-start | bytes 393224 | tf_op jit(solution)/shard_map/ppermute | solution.py:89
  54.9 5.0 %collective-permute-start.22 = (bf16[128,512]{1,0:T(8,128)(2,1)S(1)}, bf16[128,512]{1,0:T(8,128)(2,1)S(1)}, u32[]{:S(2)}, u32[]{:S(2)}) collective-permute-start(bf16[128,512]{1,0:T(8,128)(2,1)S(1)} %slice.44), channel_id=1, source_target_pairs={{0,4},{1,5},{2,6},{3,7},{4,0},{5,1},{6,2},{7,3},{8,12},{9,13},{10,... | collective-permute-start | bytes 393224 | tf_op jit(solution)/shard_map/ppermute | solution.py:89
  59.9 1.0 copy-start.2
  60.8 0.9 copy-start.6
  67.0 0.7 copy-start.3
  67.7 67.1 %collective-permute-start.23 = (bf16[4096,512]{1,0:T(8,128)(2,1)}, bf16[4096,512]{1,0:T(8,128)(2,1)}, u32[]{:S(2)}, u32[]{:S(2)}) collective-permute-start(bf16[4096,512]{1,0:T(8,128)(2,1)} %get-tuple-element.6.own_weight_ref), channel_id=1, source_target_pairs={{0,1},{1,0},{2,3},{3,2},{4,5},{5,4},{6,7},{7,6},{8,9},{9,8},{10,11... | collective-permute-start | bytes 12582920 | tf_op jit(solution)/shard_map/ppermute | solution.py:89
  67.7 23.9 %collective-permute-start.24 = (bf16[4,128,1024]{2,1,0:T(8,128)(2,1)S(1)}, bf16[4,128,1024]{2,1,0:T(8,128)(2,1)S(1)}, u32[]{:S(2)}, u32[]{:S(2)}) collective-permute-start(bf16[4,128,1024]{2,1,0:T(8,128)(2,1)S(1)} %all-to-all-done.1.own_ref), channel_id=1, source_target_pairs={{0,1},{1,0},{2,3},{3,2},{4,5},{5,4},{6,7},{7,6},{8,9},{9,8},{10,11... | collective-permute-start | bytes 3145736 | tf_op jit(solution)/shard_map/ppermute | solution.py:89
  68.2 13.5 %collective-permute-start.25 = (bf16[256,512]{1,0:T(8,128)(2,1)}, bf16[256,512]{1,0:T(8,128)(2,1)S(1)}, u32[]{:S(2)}, u32[]{:S(2)}) collective-permute-start(bf16[256,512]{1,0:T(8,128)(2,1)} %copy-done.3), channel_id=1, source_target_pairs={{0,8},{1,9},{2,10},{3,11},{4,12},{5,13},{6,14},{7,15},{8,0},{9,1},... | collective-permute-start | bytes 786440 | tf_op jit(solution)/shard_map/ppermute | solution.py:89
  70.0 21.5 %collective-permute-start.26 = (bf16[256,512]{1,0:T(8,128)(2,1)}, bf16[256,512]{1,0:T(8,128)(2,1)S(1)}, u32[]{:S(2)}, u32[]{:S(2)}) collective-permute-start(bf16[256,512]{1,0:T(8,128)(2,1)} %copy-done.3), channel_id=1, source_target_pairs={{0,16},{1,17},{2,18},{3,19},{4,20},{5,21},{6,22},{7,23},{8,24},{9,... | collective-permute-start | bytes 786440 | tf_op jit(solution)/shard_map/ppermute | solution.py:89
  72.6 18.9 %collective-permute-start.27 = (bf16[256,512]{1,0:T(8,128)(2,1)}, bf16[256,512]{1,0:T(8,128)(2,1)S(1)}, u32[]{:S(2)}, u32[]{:S(2)}) collective-permute-start(bf16[256,512]{1,0:T(8,128)(2,1)} %copy-done.3), channel_id=1, source_target_pairs={{0,24},{1,25},{2,26},{3,27},{4,28},{5,29},{6,30},{7,31},{8,16},{9,... | collective-permute-start | bytes 786440 | tf_op jit(solution)/shard_map/ppermute | solution.py:89
  91.5 1.0 copy-start.4
  112.6 22.1 %all-to-all-start = ((bf16[32,16,512]{2,1,0:T(8,128)(2,1)}), bf16[32,16,512]{2,1,0:T(8,128)(2,1)S(1)}, u32[]{:S(2)}, u32[]{:S(2)}) async-start(bf16[32,16,512]{2,1,0:T(8,128)(2,1)} %bitcast.6), calls=%async_computation | async-start | bytes 1048576 | tf_op jit(solution)/shard_map/all_to_all | solution.py:308
  134.7 2.2 %copy-start = (bf16[4096,512]{1,0:T(8,128)(2,1)S(1)}, bf16[4096,512]{1,0:T(8,128)(2,1)}, u32[]{:S(2)}) copy-start(bf16[4096,512]{1,0:T(8,128)(2,1)} %get-tuple-element.6.own_weight_ref) | copy-start | bytes 12582916

commit v3 on v2

--- a/solution.py
+++ b/solution.py
@@ -82,6 +82,7 @@
 
 
 CORE, X, Y = 1, 2, 4
+PLANE = 8
 
 
 def swap(value, mask):
@@ -89,55 +90,88 @@
     return lax.ppermute(value, "dp", [(i, i ^ mask) for i in range(size)])
 
 
-def gather_chips(piece):
+def after(value, *others):
+    return lax.optimization_barrier((value, *others))[0]
+
+
+def gather_column(piece):
     size = lax.axis_size("dp")
-    half = piece.shape[0] // 2
     column = {0: piece}
+    bit = PLANE
     bits = []
-    bit = 8
     while bit < size:
         bits.append(bit)
         bit *= 2
     for bit in reversed(bits):
         for mask in list(column):
             column[mask | bit] = swap(column[mask], bit)
-    out = []
-    for mask, own in column.items():
-        by_x, by_y = swap(own, X), swap(own, Y)
-        out += [
-            (mask, 0, own),
-            (mask | X, 0, by_x),
-            (mask | Y, 0, by_y),
-            (mask | X | Y, 0, swap(by_y[:half], X)),
-            (mask | X | Y, half, swap(by_x[half:], Y)),
-        ]
-    return out
+    return column
+
+
+def gather_planes(column, masks):
+    arrays, places = [], []
+    depth = column[masks[0]].shape[0]
+    half = depth // 2
+    to_x, to_y = [], []
+    for mask in masks:
+        by_x, by_y = swap(column[mask], X), swap(column[mask], Y)
+        for bits, array in ((0, column[mask]), (X, by_x), (Y, by_y)):
+            places.append((mask | bits, 0, len(arrays), 0, depth))
+            arrays.append(array)
+        to_x.append(by_y[:half])
+        to_y.append(by_x[half:])
+    for first, bits, halves in ((0, X, to_x), (half, Y, to_y)):
+        for n, mask in enumerate(masks):
+            places.append((mask | X | Y, first, len(arrays), n * half, half))
+        arrays.append(swap(jnp.concatenate(halves, axis=0), bits))
+    return arrays, places
 
 
 def dot(a, b, dims):
     return lax.dot_general(a, b, (dims, ((), ())), preferred_element_type=jnp.float32)
 
 
+def add_products(places, me, own_ref, mate_ref, pieces, weight_ref, acc, fresh):
+    masks = sorted({mask for mask, *_ in places})
+    chip_rows = weight_ref.shape[0] // len(masks)
+    for mask, first, array, begin, depth in places:
+        piece = pieces[array][begin : begin + depth, :]
+        at = pl.multiple_of(((me ^ mask) >> 1) * chip_rows + first, 128)
+        kept = masks.index(mask) * chip_rows + first
+        weight_ref[kept : kept + depth, :] = piece
+        for side, ref in enumerate((own_ref, mate_ref)):
+            part = dot(ref[:, pl.ds(at, depth)], piece, ((1,), (0,)))
+            if fresh:
+                acc[side] = part
+            else:
+                acc[side] += part
+        fresh = False
+
+
+def project_kernel(places, count, me_ref, own_ref, mate_ref, *refs):
+    weight_ref, acc_ref = refs[count:]
+    add_products(places, me_ref[0], own_ref, mate_ref, refs[:count], weight_ref, acc_ref, True)
+
+
 def delta_kernel(
-    places, me_ref, own_slot_ref, mate_slot_ref, own_ref, mate_ref, own_cot_ref, mate_cot_ref, *refs
+    places,
+    count,
+    me_ref,
+    own_slot_ref,
+    mate_slot_ref,
+    own_ref,
+    mate_ref,
+    own_cot_ref,
+    mate_cot_ref,
+    begun_ref,
+    *refs,
 ):
-    pieces = refs[: len(places)]
-    delta_ref, send_ref, weight_ref, acc = refs[len(places) :]
+    delta_ref, send_ref, weight_ref, acc = refs[count:]
     me = me_ref[0]
     core = me & 1
     rows = own_ref.shape[0]
-    chip_rows = pieces[0].shape[0]
-    for n, (mask, first) in enumerate(places):
-        piece = pieces[n][...]
-        depth = piece.shape[0]
-        at = pl.multiple_of(((me ^ mask) >> 1) * chip_rows + first, 128)
-        weight_ref[pl.ds(at, depth), :] = piece
-        for side, ref in enumerate((own_ref, mate_ref)):
-            part = dot(ref[:, pl.ds(at, depth)], piece, ((1,), (0,)))
-            if n == 0:
-                acc[side] = part
-            else:
-                acc[side] += part
+    acc[...] = begun_ref[...]
+    add_products(places, me, own_ref, mate_ref, refs[:count], weight_ref, acc, False)
     for side, cot_ref in enumerate((own_cot_ref, mate_cot_ref)):
         at = pl.multiple_of((core ^ side) * rows, rows)
         for head in range(own_cot_ref.shape[1] // HEAD_DIM):
@@ -158,16 +192,19 @@
     send_ref[...] = sent.astype(jnp.bfloat16)
 
 
-def weight_grad_kernel(masks, me_ref, own_ref, mate_ref, *refs):
-    pieces, part_ref, acc = refs[: len(masks)], refs[len(masks)], refs[len(masks) + 1]
+def weight_grad_kernel(count, me_ref, own_ref, mate_ref, *refs):
+    own, mate, deltas = refs[: count - 1], refs[count - 1 : 2 * count - 2], refs[2 * count - 2 : -2]
+    part_ref, acc = refs[-2:]
     me = me_ref[0]
     core = me & 1
-    rows = own_ref.shape[1]
-    for n, mask in enumerate(masks):
-        level = (me ^ mask) >> 3
-        for side, ref in enumerate((own_ref, mate_ref)):
+    rows = own_ref.shape[0]
+    wide = part_ref.shape[0]
+    here = pl.ds(pl.multiple_of((me // PLANE) * wide, wide), wide)
+    for n in range(count):
+        for side, (whole, parts) in enumerate(((own_ref, own), (mate_ref, mate))):
             at = pl.multiple_of((core ^ side) * rows, rows)
-            part = dot(ref[level], pieces[n][pl.ds(at, rows), :], ((0,), (0,)))
+            hidden = whole[:, here] if n == 0 else parts[n - 1][...]
+            part = dot(hidden, deltas[n][pl.ds(at, rows), :], ((0,), (0,)))
             if n == 0 and side == 0:
                 acc[...] = part
             else:
@@ -184,15 +221,20 @@
         grad_ref[:, side * half : (side + 1) * half] = total / norm
 
 
-def row_grad_kernel(me_ref, got_ref, own_weight_ref, mate_weight_ref, out_ref):
-    core = me_ref[0] & 1
+def row_grad_kernel(first_masks, me_ref, got_ref, *refs):
+    out_ref = refs[-1]
+    me = me_ref[0]
     receive = out_ref.shape[0]
     half = got_ref.shape[3]
+    depth = refs[0].shape[0]
     low, high = got_ref[:, 0].reshape(receive, half), got_ref[:, 1].reshape(receive, half)
-    own, mate = jnp.where(core == 0, low, high), jnp.where(core == 0, high, low)
-    total = dot(own, own_weight_ref[...], ((1,), (1,)))
-    total += dot(mate, mate_weight_ref[...], ((1,), (1,)))
-    out_ref[...] = total.astype(jnp.bfloat16)
+    own = jnp.where(me & 1 == 0, low, high)
+    mate = jnp.where(me & 1 == 0, high, low)
+    for n, first in enumerate(first_masks):
+        total = dot(own, refs[2 * n][...], ((1,), (1,)))
+        total += dot(mate, refs[2 * n + 1][...], ((1,), (1,)))
+        chip = (me ^ (first + 2 * pl.program_id(0))) >> 1
+        out_ref[:, pl.ds(pl.multiple_of(chip * depth, depth), depth)] = total.astype(jnp.bfloat16)
 
 
 def vmem(count):
@@ -201,6 +243,10 @@
 
 SCALAR = pl.BlockSpec(memory_space=pltpu.SMEM)
 PARAMS = pltpu.CompilerParams(vmem_limit_bytes=VMEM_LIMIT)
+
+
+def cost(products, moved):
+    return pl.CostEstimate(flops=2 * products, bytes_accessed=moved, transcendentals=0)
 
 
 def per_device_paired(tokens, key_cot, routes, counts, widths, key_weight):
@@ -209,10 +255,10 @@
     half_cols = cols // 2
     size = lax.axis_size("dp")
     chips = size // 2
-    plane = 8
-    levels = size // plane
+    levels = size // PLANE
     per_peer = 2 * rows // size
     receive = size * per_peer
+    wide = width_model // levels
     me = lax.axis_index("dp")
     core = me % 2
     me_scalar = me.astype(jnp.int32).reshape(1)
@@ -229,18 +275,22 @@
         jnp.concatenate([own_weight, mate_weight], axis=0),
         jnp.concatenate([mate_weight, own_weight], axis=0),
     )
-    weights = gather_chips(piece)
-    places = [(mask, first) for mask, first, _ in weights]
-    arrays = [array for _, _, array in weights]
+    column = gather_column(piece)
+    masks = sorted(column)
+    parts_of = [masks[: levels // 2], masks[levels // 2 :]]
+    sets = [gather_planes(column, part) for part in parts_of]
 
     mate_tokens = swap(tokens, CORE)
-    columns = [[p + plane * z for z in range(levels)] for p in range(plane)]
-    by_level = tokens.reshape(rows, levels, width_model // levels).transpose(1, 0, 2)
-    own_features = lax.all_to_all(
-        by_level, "dp", split_axis=0, concat_axis=0, axis_index_groups=columns, tiled=True
-    )
-    mate_features = swap(own_features, CORE)
-
+    late_tokens = after(tokens, column[masks[-1]])
+    own_features = []
+    for mask in masks[1:]:
+        there = lax.shift_right_logical(me ^ mask, 3)
+        own_features.append(
+            swap(lax.dynamic_slice_in_dim(late_tokens, there * wide, wide, 1), mask)
+        )
+    mate_features = [swap(value, CORE) for value in own_features]
+
+    key_cot, routes, counts = lax.optimization_barrier((key_cot, routes, counts, column[PLANE]))[:3]
     bounds = jnp.cumsum(counts[0])
     positions = jnp.arange(rows, dtype=jnp.int32)
     subnet = jnp.sum((positions[:, None] >= bounds[None, : NSUB - 1]).astype(jnp.int32), axis=1)
@@ -260,35 +310,60 @@
     own_slot = ((destination * 2 + core) * per_peer + earlier).reshape(1, rows)
     mate_slot = swap(own_slot, CORE)
 
-    delta, send, weight_half = pl.pallas_call(
-        functools.partial(delta_kernel, places),
+    kept = jax.ShapeDtypeStruct((width_model // 2, half_cols), jnp.bfloat16)
+    sums = jax.ShapeDtypeStruct((2, rows, half_cols), jnp.float32)
+    arrays, places = sets[0]
+    first_weight, begun = pl.pallas_call(
+        functools.partial(project_kernel, places, len(arrays)),
+        out_shape=(kept, sums),
+        in_specs=[SCALAR] + vmem(2 + len(arrays)),
+        out_specs=tuple(vmem(2)),
+        compiler_params=PARAMS,
+        cost_estimate=cost(2 * rows * width_model // 2 * half_cols, 6 << 20),
+        name="project",
+    )(me_scalar, tokens, mate_tokens, *arrays)
+    arrays, places = sets[1]
+    delta, send, last_weight = pl.pallas_call(
+        functools.partial(delta_kernel, places, len(arrays)),
         out_shape=(
             jax.ShapeDtypeStruct((2 * rows, half_cols), jnp.bfloat16),
             jax.ShapeDtypeStruct((2 * receive, half_cols), jnp.bfloat16),
-            jax.ShapeDtypeStruct((width_model, half_cols), jnp.bfloat16),
+            kept,
         ),
-        in_specs=[SCALAR] + vmem(6 + len(arrays)),
+        in_specs=[SCALAR] + vmem(7 + len(arrays)),
         out_specs=tuple(vmem(3)),
-        scratch_shapes=[pltpu.VMEM((2, rows, half_cols), jnp.float32)],
+        scratch_shapes=[pltpu.VMEM(sums.shape, sums.dtype)],
         compiler_params=PARAMS,
+        cost_estimate=cost(2 * rows * width_model // 2 * half_cols, 6 << 20),
         name="delta",
-    )(me_scalar, own_slot, mate_slot, tokens, mate_tokens, own_cot, mate_cot, *arrays)
-
-    masks = [plane * z for z in range(levels)]
-    deltas = [delta if mask == 0 else swap(delta, mask) for mask in masks]
+    )(me_scalar, own_slot, mate_slot, tokens, mate_tokens, own_cot, mate_cot, begun, *arrays)
+
+    deltas = gather_column(delta)
     part = pl.pallas_call(
-        functools.partial(weight_grad_kernel, masks),
-        out_shape=jax.ShapeDtypeStruct((width_model // levels, half_cols), jnp.bfloat16),
-        in_specs=[SCALAR] + vmem(2 + len(deltas)),
+        functools.partial(weight_grad_kernel, levels),
+        out_shape=jax.ShapeDtypeStruct((wide, half_cols), jnp.bfloat16),
+        in_specs=[SCALAR] + vmem(2 + 2 * (levels - 1) + levels),
         out_specs=vmem(1)[0],
-        scratch_shapes=[pltpu.VMEM((width_model // levels, half_cols), jnp.float32)],
+        scratch_shapes=[pltpu.VMEM((wide, half_cols), jnp.float32)],
         compiler_params=PARAMS,
+        cost_estimate=cost(2 * rows * levels * wide * half_cols, 4 << 20),
         name="weight_grad",
-    )(me_scalar, own_features, mate_features, *deltas)
+    )(
+        me_scalar,
+        tokens,
+        mate_tokens,
+        *own_features,
+        *mate_features,
+        *[deltas[mask] for mask in masks],
+    )
+    got = lax.all_to_all(
+        send.reshape(size, 2 * per_peer, half_cols), "dp", split_axis=0, concat_axis=0, tiled=True
+    )
+    part = after(part, got)
     shard = width_model // size
-    planes = [[z * plane + p for p in range(plane)] for z in range(levels)]
+    planes = [[z * PLANE + p for p in range(PLANE)] for z in range(levels)]
     parts = lax.all_to_all(
-        part.reshape(plane, shard, half_cols),
+        part.reshape(PLANE, shard, half_cols),
         "dp",
         split_axis=0,
         concat_axis=0,
@@ -301,28 +376,26 @@
         in_specs=vmem(1),
         out_specs=vmem(1)[0],
         compiler_params=PARAMS,
+        cost_estimate=cost(PLANE * shard * half_cols, 2 << 20),
         name="sum",
-    )(parts.reshape(plane // 2, 2, shard, half_cols))
-
-    mate_half = swap(weight_half, CORE)
-    got = lax.all_to_all(
-        send.reshape(size, 2 * per_peer, half_cols), "dp", split_axis=0, concat_axis=0, tiled=True
-    )
-    tile = 1024
+    )(parts.reshape(PLANE // 2, 2, shard, half_cols))
+
+    depth = width_model // chips
+    kept_weights = [first_weight, swap(first_weight, CORE), last_weight, swap(last_weight, CORE)]
     row_grads = pl.pallas_call(
-        row_grad_kernel,
+        functools.partial(row_grad_kernel, [part[0] for part in parts_of]),
         out_shape=jax.ShapeDtypeStruct((receive, width_model), jnp.bfloat16),
-        grid=(width_model // tile,),
+        grid=(chips // 2,),
         in_specs=[
             SCALAR,
             pl.BlockSpec((chips, 2, 2 * per_peer, half_cols), lambda i: (0, 0, 0, 0)),
-            pl.BlockSpec((tile, half_cols), lambda i: (i, 0)),
-            pl.BlockSpec((tile, half_cols), lambda i: (i, 0)),
-        ],
-        out_specs=pl.BlockSpec((receive, tile), lambda i: (0, i)),
+        ]
+        + [pl.BlockSpec((depth, half_cols), lambda i: (i, 0))] * len(kept_weights),
+        out_specs=pl.BlockSpec((receive, width_model), lambda i: (0, 0)),
         compiler_params=PARAMS,
+        cost_estimate=cost(receive * width_model * cols, 12 << 20),
         name="row_grad",
-    )(me_scalar, got.reshape(chips, 2, 2 * per_peer, half_cols), weight_half, mate_half)
+    )(me_scalar, got.reshape(chips, 2, 2 * per_peer, half_cols), *kept_weights)
     return (row_grads, key_grad)
 
 

time: 143 us -> 155 us (1.084)
  waiting for transfers between devices: 55.7 us -> 82.3 us
  local copies, waits for them, and re-layouts: 11.1 us -> 1.17 us
  starting transfers between devices: 38.8 us -> 31.8 us
  Pallas kernels: 14.3 us -> 16.5 us
    ppermute x28 -> x30, waiting for transfers between devices: 41 us -> 82.3 us  [swap(): return lax.ppermute(value, 'dp', [(i, i ^ mask) for i in range(size)])]
    all_to_all x1, waiting for transfers between devices: 14.6 us -> 0.01 us  [per_device_paired(): lax.all_to_all(send.reshape(size, 2 * per_peer, half_cols), 'dp', split_a...]
    unnamed x15 -> x6, local copies, waits for them, and re-layouts: 8.66 us -> 0.01 us
    all_to_all x1 -> x0, starting transfers between devices: 5.71 us -> none  [per_device_paired(): lax.all_to_all(by_level, 'dp', split_axis=0, concat_axis=0, axis_index_gr...]
    all_to_all x1, starting transfers between devices: 6.55 us -> 4.02 us  [per_device_paired(): lax.all_to_all(send.reshape(size, 2 * per_peer, half_cols), 'dp', split_a...]
    pallas_call x3 -> x4, Pallas kernels: 13.4 us -> 15.6 us  [the longest x1 8.73 us: per_device_paired(): pl.pallas_call(functools.partial(row_grad_kernel, [part[0] for part in pa...]
    ppermute x28 -> x30, starting transfers between devices: 26.5 us -> 27.8 us  [swap(): return lax.ppermute(value, 'dp', [(i, i ^ mask) for i in range(size)])]
  transfers between devices with their start and end apart: 30 -> 31, of which waited for: 15 -> 14; matrix products, arithmetic and copies ran while one was open for 5% -> 2% of each run, Pallas kernels for 6% -> 5%
where the time goes in v3:
time: 155 us
  waiting for transfers between devices  82.3 us (53%)
  starting transfers between devices  31.8 us (21%)
  blocking collectives  19.1 us (12%)
  Pallas kernels  16.5 us (11%)
  other arithmetic  2.96 us (2%)
    ppermute x30, waiting for transfers between devices, swap(): return lax.ppermute(value, 'dp', [(i, i ^ mask) for i in range(size)])  82.3 us
    ppermute x30, starting transfers between devices, swap(): return lax.ppermute(value, 'dp', [(i, i ^ mask) for i in range(size)])  27.8 us
    all_to_all x1, blocking collectives, per_device_paired(): lax.all_to_all(part.reshape(PLANE, shard, half_cols), 'dp', split_axis=0,...  19.1 us
    pallas_call x1, Pallas kernels, per_device_paired(): pl.pallas_call(functools.partial(row_grad_kernel, [part[0] for part in pa...  8.73 us
    all_to_all x1, starting transfers between devices, per_device_paired(): lax.all_to_all(send.reshape(size, 2 * per_peer, half_cols), 'dp', split_a...  4.02 us
  transfers between devices with their start and end apart: 31, of which 14 were waited for; matrix products, arithmetic and copies ran while one was open for 2% of the time, Pallas kernels for 5%

profile of v3, /device:TPU:0, one launch (start us, length us, event | category | flops | bytes accessed | tf_op | source)
XLA Modules:
  0.0 154.8 jit_solution(13792793617468636052)
XLA Ops:
  0.7 1.0 constant_dynamic-slice_fusion.6
  1.7 0.5 collective-permute-start
  2.2 1.0 collective-permute-done
  3.2 3.0 %collective-permute-start.1 = (bf16[256,512]{1,0:T(8,128)(2,1)S(1)}, bf16[256,512]{1,0:T(8,128)(2,1)S(1)}, u32[]{:S(2)}, u32[]{:S(2)}) collective-permute-start(bf16[256,512]{1,0:T(8,128)(2,1)S(1)} %maximum_select_fusion.refs_0_), channel_id=1, source_target_pairs={{0,8},{1,9},{2,10},{3,11},{4,12},{5,13},{6,14},{7,15},{8,0},{9,1},... | collective-permute-start | bytes 786440 | tf_op jit(solution)/shard_map/ppermute | solution.py:90
  6.2 2.6 %collective-permute-start.11 = (bf16[256,512]{1,0:T(8,128)(2,1)S(1)}, bf16[256,512]{1,0:T(8,128)(2,1)S(1)}, u32[]{:S(2)}, u32[]{:S(2)}) collective-permute-start(bf16[256,512]{1,0:T(8,128)(2,1)S(1)} %maximum_select_fusion.refs_0_), channel_id=1, source_target_pairs={{0,16},{1,17},{2,18},{3,19},{4,20},{5,21},{6,22},{7,23},{8,24},{9,... | collective-permute-start | bytes 786440 | tf_op jit(solution)/shard_map/ppermute | solution.py:90
  8.8 1.5 collective-permute-start.6
  10.3 1.5 collective-permute-start.5
  11.8 5.9 %collective-permute-done.1.refs_3_ = bf16[256,512]{1,0:T(8,128)(2,1)S(1)} collective-permute-done((bf16[256,512]{1,0:T(8,128)(2,1)S(1)}, bf16[256,512]{1,0:T(8,128)(2,1)S(1)}, u32[]{:S(2)}, u32[]{:S(2)}) %collective-permute-start.1) | collective-permute-done | bytes 262176 | tf_op jit(solution)/shard_map/ppermute | solution.py:90
  17.7 0.8 reduce-window.4
  18.5 0.1 convert_reduce_fusion.1
  18.6 0.7 select_reduce_fusion
  19.4 1.7 %collective-permute-start.8 = (bf16[256,512]{1,0:T(8,128)(2,1)S(1)}, bf16[256,512]{1,0:T(8,128)(2,1)S(1)}, u32[]{:S(2)}, u32[]{:S(2)}) collective-permute-start(bf16[256,512]{1,0:T(8,128)(2,1)S(1)} %collective-permute-done.1.refs_3_), channel_id=1, source_target_pairs={{0,4},{1,5},{2,6},{3,7},{4,0},{5,1},{6,2},{7,3},{8,12},{9,13},{10,... | collective-permute-start | bytes 786440 | tf_op jit(solution)/shard_map/ppermute | solution.py:90
  21.0 0.5 collective-permute-done.11.refs_0_
  21.5 1.5 collective-permute-start.7
  23.0 1.1 compare_select_fusion
  24.1 1.6 %collective-permute-start.13 = (bf16[256,512]{1,0:T(8,128)(2,1)S(1)}, bf16[256,512]{1,0:T(8,128)(2,1)S(1)}, u32[]{:S(2)}, u32[]{:S(2)}) collective-permute-start(bf16[256,512]{1,0:T(8,128)(2,1)S(1)} %collective-permute-done.11.refs_0_), channel_id=1, source_target_pairs={{0,4},{1,5},{2,6},{3,7},{4,0},{5,1},{6,2},{7,3},{8,12},{9,13},{10,... | collective-permute-start | bytes 786440 | tf_op jit(solution)/shard_map/ppermute | solution.py:90
  25.7 5.0 %collective-permute-done.14.refs_3_ = bf16[256,512]{1,0:T(8,128)(2,1)S(1)} collective-permute-done((bf16[256,512]{1,0:T(8,128)(2,1)S(1)}, bf16[256,512]{1,0:T(8,128)(2,1)S(1)}, u32[]{:S(2)}, u32[]{:S(2)}) %collective-permute-start.14) | collective-permute-done | bytes 262176 | tf_op jit(solution)/shard_map/ppermute | solution.py:90
  30.7 0.5 collective-permute-start.12
  31.2 1.5 collective-permute-start.16
  32.7 0.1 convert_reduce_fusion
  32.9 1.6 %collective-permute-start.15 = (bf16[256,512]{1,0:T(8,128)(2,1)S(1)}, bf16[256,512]{1,0:T(8,128)(2,1)S(1)}, u32[]{:S(2)}, u32[]{:S(2)}) collective-permute-start(bf16[256,512]{1,0:T(8,128)(2,1)S(1)} %collective-permute-done.14.refs_3_), channel_id=1, source_target_pairs={{0,2},{1,3},{2,0},{3,1},{4,6},{5,7},{6,4},{7,5},{8,10},{9,11},{10,... | collective-permute-start | bytes 786440 | tf_op jit(solution)/shard_map/ppermute | solution.py:90
  34.5 0.6 collective-permute-start.9
  35.1 4.8 %collective-permute-done.12.refs_1_ = bf16[256,512]{1,0:T(8,128)(2,1)S(1)} collective-permute-done((bf16[256,512]{1,0:T(8,128)(2,1)S(1)}, bf16[256,512]{1,0:T(8,128)(2,1)S(1)}, u32[]{:S(2)}, u32[]{:S(2)}) %collective-permute-start.12) | collective-permute-done | bytes 262176 | tf_op jit(solution)/shard_map/ppermute | solution.py:90
  39.9 1.6 %collective-permute-start.10 = (bf16[256,512]{1,0:T(8,128)(2,1)S(1)}, bf16[256,512]{1,0:T(8,128)(2,1)S(1)}, u32[]{:S(2)}, u32[]{:S(2)}) collective-permute-start(bf16[256,512]{1,0:T(8,128)(2,1)S(1)} %pad_maximum_fusion.1), channel_id=1, source_target_pairs={{0,4},{1,5},{2,6},{3,7},{4,0},{5,1},{6,2},{7,3},{8,12},{9,13},{10,... | collective-permute-start | bytes 786440 | tf_op jit(solution)/shard_map/ppermute | solution.py:90
  41.6 4.0 %collective-permute-done.15.refs_4_ = bf16[256,512]{1,0:T(8,128)(2,1)S(1)} collective-permute-done((bf16[256,512]{1,0:T(8,128)(2,1)S(1)}, bf16[256,512]{1,0:T(8,128)(2,1)S(1)}, u32[]{:S(2)}, u32[]{:S(2)}) %collective-permute-start.15) | collective-permute-done | bytes 262176 | tf_op jit(solution)/shard_map/ppermute | solution.py:90
  45.5 0.5 collective-permute-start.17
  46.1 5.0 %collective-permute-done.9.refs_6_ = bf16[256,512]{1,0:T(8,128)(2,1)S(1)} collective-permute-done((bf16[256,512]{1,0:T(8,128)(2,1)S(1)}, bf16[256,512]{1,0:T(8,128)(2,1)S(1)}, u32[]{:S(2)}, u32[]{:S(2)}) %collective-permute-start.9) | collective-permute-done | bytes 262176 | tf_op jit(solution)/shard_map/ppermute | solution.py:90
  51.1 1.5 collective-permute-start.18
  52.7 2.0 %project.1 = (bf16[2048,512]{1,0:T(8,128)(2,1)}, f32[2,128,512]{2,1,0:T(8,128)S(1)}) custom-call(s32[1]{0:T(128)} %bitcast.me_ref, bf16[128,4096]{1,0:T(8,128)(2,1)S(1)} %copy-done, bf16[128,4096]{1,0:T(8,128)(2,1)S(1)} %collective-permute-done.3.mate_ref, bf16[256,512]{1,0:T(8,128)(2,1)S(1)} %maximum_select_fusion.refs_0_, ...), custom_call_target="tpu_custom_call" | custom-call | flops 536870912 | bytes 6291456 | tf_op jit(solution)/shard_map/project/pallas_call | solution.py:316
  54.7 0.5 collective-permute-start.19
  55.2 2.3 %collective-permute-done.18.refs_7_ = bf16[256,512]{1,0:T(8,128)(2,1)S(1)} collective-permute-done((bf16[256,512]{1,0:T(8,128)(2,1)S(1)}, bf16[256,512]{1,0:T(8,128)(2,1)S(1)}, u32[]{:S(2)}, u32[]{:S(2)}) %collective-permute-start.18) | collective-permute-done | bytes 262176 | tf_op jit(solution)/shard_map/ppermute | solution.py:90
  57.5 2.5 %delta.1 = (bf16[256,512]{1,0:T(8,128)(2,1)S(1)}, bf16[512,512]{1,0:T(8,128)(2,1)}, bf16[2048,512]{1,0:T(8,128)(2,1)}) custom-call(s32[1]{0:T(128)} %bitcast.me_ref, s32[1,128]{1,0:T(1,128)S(1)} %bitcast_add_fusion.own_slot_ref, s32[1,128]{1,0:T(1,128)S(1)} %collective-permute-done.2.mate_slot_ref, bf16[128,4096]{1,0:T(8,128)(2,1)S(1)} %copy-done, ...), custom_call_target="tpu_custom_call" | custom-call | flops 536870912 | bytes 6291456 | tf_op jit(solution)/shard_map/delta/pallas_call | solution.py:326
  60.1 4.0 %all-to-all-start = ((bf16[32,16,512]{2,1,0:T(8,128)(2,1)}), bf16[32,16,512]{2,1,0:T(8,128)(2,1)}, u32[]{:S(2)}, u32[]{:S(2)}) async-start(bf16[32,16,512]{2,1,0:T(8,128)(2,1)} %bitcast.6), calls=%async_computation | async-start | bytes 1048576 | tf_op jit(solution)/shard_map/all_to_all | solution.py:359
  64.1 0.1 constant_dynamic-slice_fusion
  64.2 3.6 %collective-permute-start.23 = (bf16[128,1024]{1,0:T(8,128)(2,1)S(1)}, bf16[128,1024]{1,0:T(8,128)(2,1)S(1)}, u32[]{:S(2)}, u32[]{:S(2)}) collective-permute-start(bf16[128,1024]{1,0:T(8,128)(2,1)S(1)} %get-tuple-element.22), channel_id=1, source_target_pairs={{0,24},{1,25},{2,26},{3,27},{4,28},{5,29},{6,30},{7,31},{8,16},{9,... | collective-permute-start | bytes 786440 | tf_op jit(solution)/shard_map/ppermute | solution.py:90
  67.8 0.8 collective-permute-start.21
  68.6 14.6 %collective-permute-done.23.refs_2_ = bf16[128,1024]{1,0:T(8,128)(2,1)S(1)} collective-permute-done((bf16[128,1024]{1,0:T(8,128)(2,1)S(1)}, bf16[128,1024]{1,0:T(8,128)(2,1)S(1)}, u32[]{:S(2)}, u32[]{:S(2)}) %collective-permute-start.23) | collective-permute-done | bytes 262176 | tf_op jit(solution)/shard_map/ppermute | solution.py:90
  83.2 18.2 %collective-permute-done.22.refs_1_ = bf16[128,1024]{1,0:T(8,128)(2,1)S(1)} collective-permute-done((bf16[128,1024]{1,0:T(8,128)(2,1)S(1)}, bf16[128,1024]{1,0:T(8,128)(2,1)S(1)}, u32[]{:S(2)}, u32[]{:S(2)}) %collective-permute-start.22) | collective-permute-done | bytes 262176 | tf_op jit(solution)/shard_map/ppermute | solution.py:90
  101.5 0.6 collective-permute-start.24
  102.0 0.9 collective-permute-done.25.refs_4_
  103.0 0.6 collective-permute-start.27
  103.5 11.9 %collective-permute-done.28.refs_8_ = bf16[256,512]{1,0:T(8,128)(2,1)S(1)} collective-permute-done((bf16[256,512]{1,0:T(8,128)(2,1)S(1)}, bf16[256,512]{1,0:T(8,128)(2,1)S(1)}, u32[]{:S(2)}, u32[]{:S(2)}) %collective-permute-start.28) | collective-permute-done | bytes 262176 | tf_op jit(solution)/shard_map/ppermute | solution.py:90
  115.4 1.5 collective-permute-done.27.refs_7_
  116.9 6.7 %collective-permute-done.29.refs_9_ = bf16[256,512]{1,0:T(8,128)(2,1)S(1)} collective-permute-done((bf16[256,512]{1,0:T(8,128)(2,1)S(1)}, bf16[256,512]{1,0:T(8,128)(2,1)S(1)}, u32[]{:S(2)}, u32[]{:S(2)}) %collective-permute-start.29) | collective-permute-done | bytes 262176 | tf_op jit(solution)/shard_map/ppermute | solution.py:90
  123.6 2.3 %weight_grad.1 = bf16[1024,512]{1,0:T(8,128)(2,1)S(1)} custom-call(s32[1]{0:T(128)} %bitcast.me_ref, bf16[128,4096]{1,0:T(8,128)(2,1)S(1)} %copy-done, bf16[128,4096]{1,0:T(8,128)(2,1)S(1)} %collective-permute-done.3.mate_ref, bf16[128,1024]{1,0:T(8,128)(2,1)S(1)} %collective-permute-done.21.refs_0_, bf16[128,1024]{1,0:T(8,128)(2,1)S(1)} %collective-permute-done.22.refs_1_, ...), custom_call_target="tpu_custom_call" | custom-call | flops 1073741824 | bytes 4194304 | tf_op jit(solution)/shard_map/weight_grad/pallas_call | solution.py:342
  126.0 19.1 %all_to_all.10 = bf16[8,128,512]{2,1,0:T(8,128)(2,1)S(1)} all-to-all(bf16[8,128,512]{2,1,0:T(8,128)(2,1)S(1)} %bitcast.14), channel_id=1, replica_groups={{0,1,2,3,4,5,6,7},{8,9,10,11,12,13,14,15},{16,17,18,19,20,21,22,23},{24..., dimensions={0} | all-to-all | bytes 2097152 | tf_op jit(solution)/shard_map/all_to_all | solution.py:365
  145.1 0.9 sum.1
  146.1 8.7 %row_grad.1 = bf16[256,4096]{1,0:T(8,128)(2,1)} custom-call(s32[1]{0:T(128)} %bitcast.me_ref, bf16[16,2,16,512]{3,2,1,0:T(8,128)(2,1)} %bitcast.7.got_ref, bf16[2048,512]{1,0:T(8,128)(2,1)S(1)} %copy-done.1, bf16[2048,512]{1,0:T(8,128)(2,1)} %collective-permute-done.19.refs_1_, bf16[2048,512]{1,0:T(8,128)(2,1)} %get-tuple-element.18.refs_2_, ...), custom_call_target="tpu_custom_call" | custom-call | flops 2147483648 | bytes 12582912 | tf_op jit(solution)/shard_map/row_grad/pallas_call | solution.py:385
  (50 shorter events, 0.3 us)
Async XLA Ops:
  0.6 32.1 %copy-start.2 = (s32[128,1]{0,1:T(1,128)S(1)}, s32[128,1]{0,1:T(1,128)}, u32[]{:S(2)}) copy-start(s32[128,1]{0,1:T(1,128)} %param.8) | copy-start | bytes 1540
  1.7 1.5 collective-permute-start
  3.2 14.5 %collective-permute-start.1 = (bf16[256,512]{1,0:T(8,128)(2,1)S(1)}, bf16[256,512]{1,0:T(8,128)(2,1)S(1)}, u32[]{:S(2)}, u32[]{:S(2)}) collective-permute-start(bf16[256,512]{1,0:T(8,128)(2,1)S(1)} %maximum_select_fusion.refs_0_), channel_id=1, source_target_pairs={{0,8},{1,9},{2,10},{3,11},{4,12},{5,13},{6,14},{7,15},{8,0},{9,1},... | collective-permute-start | bytes 786440 | tf_op jit(solution)/shard_map/ppermute | solution.py:90
  6.2 46.5 %collective-permute-start.3 = (bf16[128,4096]{1,0:T(8,128)(2,1)}, bf16[128,4096]{1,0:T(8,128)(2,1)S(1)}, u32[]{:S(2)}, u32[]{:S(2)}) collective-permute-start(bf16[128,4096]{1,0:T(8,128)(2,1)} %own_ref.5), channel_id=1, source_target_pairs={{0,1},{1,0},{2,3},{3,2},{4,5},{5,4},{6,7},{7,6},{8,9},{9,8},{10,11... | collective-permute-start | bytes 3145736 | tf_op jit(solution)/shard_map/ppermute | solution.py:90
  6.2 15.3 %collective-permute-start.11 = (bf16[256,512]{1,0:T(8,128)(2,1)S(1)}, bf16[256,512]{1,0:T(8,128)(2,1)S(1)}, u32[]{:S(2)}, u32[]{:S(2)}) collective-permute-start(bf16[256,512]{1,0:T(8,128)(2,1)S(1)} %maximum_select_fusion.refs_0_), channel_id=1, source_target_pairs={{0,16},{1,17},{2,18},{3,19},{4,20},{5,21},{6,22},{7,23},{8,24},{9,... | collective-permute-start | bytes 786440 | tf_op jit(solution)/shard_map/ppermute | solution.py:90
  8.8 14.2 %collective-permute-start.6 = (bf16[256,512]{1,0:T(8,128)(2,1)S(1)}, bf16[256,512]{1,0:T(8,128)(2,1)S(1)}, u32[]{:S(2)}, u32[]{:S(2)}) collective-permute-start(bf16[256,512]{1,0:T(8,128)(2,1)S(1)} %maximum_select_fusion.refs_0_), channel_id=1, source_target_pairs={{0,4},{1,5},{2,6},{3,7},{4,0},{5,1},{6,2},{7,3},{8,12},{9,13},{10,... | collective-permute-start | bytes 786440 | tf_op jit(solution)/shard_map/ppermute | solution.py:90
  10.3 13.8 %collective-permute-start.5 = (bf16[256,512]{1,0:T(8,128)(2,1)S(1)}, bf16[256,512]{1,0:T(8,128)(2,1)S(1)}, u32[]{:S(2)}, u32[]{:S(2)}) collective-permute-start(bf16[256,512]{1,0:T(8,128)(2,1)S(1)} %maximum_select_fusion.refs_0_), channel_id=1, source_target_pairs={{0,2},{1,3},{2,0},{3,1},{4,6},{5,7},{6,4},{7,5},{8,10},{9,11},{10,... | collective-permute-start | bytes 786440 | tf_op jit(solution)/shard_map/ppermute | solution.py:90
  19.4 11.8 %collective-permute-start.8 = (bf16[256,512]{1,0:T(8,128)(2,1)S(1)}, bf16[256,512]{1,0:T(8,128)(2,1)S(1)}, u32[]{:S(2)}, u32[]{:S(2)}) collective-permute-start(bf16[256,512]{1,0:T(8,128)(2,1)S(1)} %collective-permute-done.1.refs_3_), channel_id=1, source_target_pairs={{0,4},{1,5},{2,6},{3,7},{4,0},{5,1},{6,2},{7,3},{8,12},{9,13},{10,... | collective-permute-start | bytes 786440 | tf_op jit(solution)/shard_map/ppermute | solution.py:90
  21.5 11.4 %collective-permute-start.7 = (bf16[256,512]{1,0:T(8,128)(2,1)S(1)}, bf16[256,512]{1,0:T(8,128)(2,1)S(1)}, u32[]{:S(2)}, u32[]{:S(2)}) collective-permute-start(bf16[256,512]{1,0:T(8,128)(2,1)S(1)} %collective-permute-done.1.refs_3_), channel_id=1, source_target_pairs={{0,2},{1,3},{2,0},{3,1},{4,6},{5,7},{6,4},{7,5},{8,10},{9,11},{10,... | collective-permute-start | bytes 786440 | tf_op jit(solution)/shard_map/ppermute | solution.py:90
  23.0 7.7 %collective-permute-start.14 = (bf16[256,512]{1,0:T(8,128)(2,1)S(1)}, bf16[256,512]{1,0:T(8,128)(2,1)S(1)}, u32[]{:S(2)}, u32[]{:S(2)}) collective-permute-start(bf16[256,512]{1,0:T(8,128)(2,1)S(1)} %collective-permute-done.11.refs_0_), channel_id=1, source_target_pairs={{0,8},{1,9},{2,10},{3,11},{4,12},{5,13},{6,14},{7,15},{8,0},{9,1},... | collective-permute-start | bytes 786440 | tf_op jit(solution)/shard_map/ppermute | solution.py:90
  24.1 10.4 %collective-permute-start.13 = (bf16[256,512]{1,0:T(8,128)(2,1)S(1)}, bf16[256,512]{1,0:T(8,128)(2,1)S(1)}, u32[]{:S(2)}, u32[]{:S(2)}) collective-permute-start(bf16[256,512]{1,0:T(8,128)(2,1)S(1)} %collective-permute-done.11.refs_0_), channel_id=1, source_target_pairs={{0,4},{1,5},{2,6},{3,7},{4,0},{5,1},{6,2},{7,3},{8,12},{9,13},{10,... | collective-permute-start | bytes 786440 | tf_op jit(solution)/shard_map/ppermute | solution.py:90
  30.7 9.2 %collective-permute-start.12 = (bf16[256,512]{1,0:T(8,128)(2,1)S(1)}, bf16[256,512]{1,0:T(8,128)(2,1)S(1)}, u32[]{:S(2)}, u32[]{:S(2)}) collective-permute-start(bf16[256,512]{1,0:T(8,128)(2,1)S(1)} %collective-permute-done.11.refs_0_), channel_id=1, source_target_pairs={{0,2},{1,3},{2,0},{3,1},{4,6},{5,7},{6,4},{7,5},{8,10},{9,11},{10,... | collective-permute-start | bytes 786440 | tf_op jit(solution)/shard_map/ppermute | solution.py:90
  31.2 8.7 %collective-permute-start.16 = (bf16[256,512]{1,0:T(8,128)(2,1)S(1)}, bf16[256,512]{1,0:T(8,128)(2,1)S(1)}, u32[]{:S(2)}, u32[]{:S(2)}) collective-permute-start(bf16[256,512]{1,0:T(8,128)(2,1)S(1)} %collective-permute-done.14.refs_3_), channel_id=1, source_target_pairs={{0,4},{1,5},{2,6},{3,7},{4,0},{5,1},{6,2},{7,3},{8,12},{9,13},{10,... | collective-permute-start | bytes 786440 | tf_op jit(solution)/shard_map/ppermute | solution.py:90
  32.8 19.9 %copy-start = (bf16[128,4096]{1,0:T(8,128)(2,1)S(1)}, bf16[128,4096]{1,0:T(8,128)(2,1)}, u32[]{:S(2)}) copy-start(bf16[128,4096]{1,0:T(8,128)(2,1)} %own_ref.5) | copy-start | bytes 3145732
  32.9 12.6 %collective-permute-start.15 = (bf16[256,512]{1,0:T(8,128)(2,1)S(1)}, bf16[256,512]{1,0:T(8,128)(2,1)S(1)}, u32[]{:S(2)}, u32[]{:S(2)}) collective-permute-start(bf16[256,512]{1,0:T(8,128)(2,1)S(1)} %collective-permute-done.14.refs_3_), channel_id=1, source_target_pairs={{0,2},{1,3},{2,0},{3,1},{4,6},{5,7},{6,4},{7,5},{8,10},{9,11},{10,... | collective-permute-start | bytes 786440 | tf_op jit(solution)/shard_map/ppermute | solution.py:90
  34.5 16.6 %collective-permute-start.9 = (bf16[256,512]{1,0:T(8,128)(2,1)S(1)}, bf16[256,512]{1,0:T(8,128)(2,1)S(1)}, u32[]{:S(2)}, u32[]{:S(2)}) collective-permute-start(bf16[256,512]{1,0:T(8,128)(2,1)S(1)} %pad_maximum_fusion), channel_id=1, source_target_pairs={{0,2},{1,3},{2,0},{3,1},{4,6},{5,7},{6,4},{7,5},{8,10},{9,11},{10,... | collective-permute-start | bytes 786440 | tf_op jit(solution)/shard_map/ppermute | solution.py:90
  39.9 15.3 %collective-permute-start.4 = (bf16[128,512]{1,0:T(8,128)(2,1)S(1)}, bf16[128,512]{1,0:T(8,128)(2,1)S(1)}, u32[]{:S(2)}, u32[]{:S(2)}) collective-permute-start(bf16[128,512]{1,0:T(8,128)(2,1)S(1)} %get-tuple-element.25), channel_id=1, source_target_pairs={{0,1},{1,0},{2,3},{3,2},{4,5},{5,4},{6,7},{7,6},{8,9},{9,8},{10,11... | collective-permute-start | bytes 393224 | tf_op jit(solution)/shard_map/ppermute | solution.py:90
  39.9 12.7 %collective-permute-start.10 = (bf16[256,512]{1,0:T(8,128)(2,1)S(1)}, bf16[256,512]{1,0:T(8,128)(2,1)S(1)}, u32[]{:S(2)}, u32[]{:S(2)}) collective-permute-start(bf16[256,512]{1,0:T(8,128)(2,1)S(1)} %pad_maximum_fusion.1), channel_id=1, source_target_pairs={{0,4},{1,5},{2,6},{3,7},{4,0},{5,1},{6,2},{7,3},{8,12},{9,13},{10,... | collective-permute-start | bytes 786440 | tf_op jit(solution)/shard_map/ppermute | solution.py:90
  45.5 9.6 %collective-permute-start.17 = (bf16[256,512]{1,0:T(8,128)(2,1)S(1)}, bf16[256,512]{1,0:T(8,128)(2,1)S(1)}, u32[]{:S(2)}, u32[]{:S(2)}) collective-permute-start(bf16[256,512]{1,0:T(8,128)(2,1)S(1)} %pad_maximum_fusion.2), channel_id=1, source_target_pairs={{0,2},{1,3},{2,0},{3,1},{4,6},{5,7},{6,4},{7,5},{8,10},{9,11},{10,... | collective-permute-start | bytes 786440 | tf_op jit(solution)/shard_map/ppermute | solution.py:90
  51.1 6.4 %collective-permute-start.18 = (bf16[256,512]{1,0:T(8,128)(2,1)S(1)}, bf16[256,512]{1,0:T(8,128)(2,1)S(1)}, u32[]{:S(2)}, u32[]{:S(2)}) collective-permute-start(bf16[256,512]{1,0:T(8,128)(2,1)S(1)} %pad_maximum_fusion.3), channel_id=1, source_target_pairs={{0,4},{1,5},{2,6},{3,7},{4,0},{5,1},{6,2},{7,3},{8,12},{9,13},{10,... | collective-permute-start | bytes 786440 | tf_op jit(solution)/shard_map/ppermute | solution.py:90
  52.7 2.5 %collective-permute-start.2 = (s32[1,128]{1,0:T(1,128)S(1)}, s32[1,128]{1,0:T(1,128)S(1)}, u32[]{:S(2)}, u32[]{:S(2)}) collective-permute-start(s32[1,128]{1,0:T(1,128)S(1)} %bitcast_add_fusion.own_slot_ref), channel_id=1, source_target_pairs={{0,1},{1,0},{2,3},{3,2},{4,5},{5,4},{6,7},{7,6},{8,9},{9,8},{10,11... | collective-permute-start | bytes 1544 | tf_op jit(solution)/shard_map/ppermute | solution.py:90
  54.7 91.4 %collective-permute-start.19 = (bf16[2048,512]{1,0:T(8,128)(2,1)}, bf16[2048,512]{1,0:T(8,128)(2,1)}, u32[]{:S(2)}, u32[]{:S(2)}) collective-permute-start(bf16[2048,512]{1,0:T(8,128)(2,1)} %get-tuple-element.17.refs_0_), channel_id=1, source_target_pairs={{0,1},{1,0},{2,3},{3,2},{4,5},{5,4},{6,7},{7,6},{8,9},{9,8},{10,11... | collective-permute-start | bytes 6291464 | tf_op jit(solution)/shard_map/ppermute | solution.py:90
  60.1 86.0 %collective-permute-start.20 = (bf16[2048,512]{1,0:T(8,128)(2,1)}, bf16[2048,512]{1,0:T(8,128)(2,1)}, u32[]{:S(2)}, u32[]{:S(2)}) collective-permute-start(bf16[2048,512]{1,0:T(8,128)(2,1)} %get-tuple-element.18.refs_2_), channel_id=1, source_target_pairs={{0,1},{1,0},{2,3},{3,2},{4,5},{5,4},{6,7},{7,6},{8,9},{9,8},{10,11... | collective-permute-start | bytes 6291464 | tf_op jit(solution)/shard_map/ppermute | solution.py:90
  60.1 66.0 %all-to-all-start = ((bf16[32,16,512]{2,1,0:T(8,128)(2,1)}), bf16[32,16,512]{2,1,0:T(8,128)(2,1)}, u32[]{:S(2)}, u32[]{:S(2)}) async-start(bf16[32,16,512]{2,1,0:T(8,128)(2,1)} %bitcast.6), calls=%async_computation | async-start | bytes 1048576 | tf_op jit(solution)/shard_map/all_to_all | solution.py:359
  64.2 19.0 %collective-permute-start.23 = (bf16[128,1024]{1,0:T(8,128)(2,1)S(1)}, bf16[128,1024]{1,0:T(8,128)(2,1)S(1)}, u32[]{:S(2)}, u32[]{:S(2)}) collective-permute-start(bf16[128,1024]{1,0:T(8,128)(2,1)S(1)} %get-tuple-element.22), channel_id=1, source_target_pairs={{0,24},{1,25},{2,26},{3,27},{4,28},{5,29},{6,30},{7,31},{8,16},{9,... | collective-permute-start | bytes 786440 | tf_op jit(solution)/shard_map/ppermute | solution.py:90
  67.8 33.7 %collective-permute-start.22 = (bf16[128,1024]{1,0:T(8,128)(2,1)S(1)}, bf16[128,1024]{1,0:T(8,128)(2,1)S(1)}, u32[]{:S(2)}, u32[]{:S(2)}) collective-permute-start(bf16[128,1024]{1,0:T(8,128)(2,1)S(1)} %get-tuple-element.23), channel_id=1, source_target_pairs={{0,16},{1,17},{2,18},{3,19},{4,20},{5,21},{6,22},{7,23},{8,24},{9,... | collective-permute-start | bytes 786440 | tf_op jit(solution)/shard_map/ppermute | solution.py:90
  67.8 33.7 %collective-permute-start.21 = (bf16[128,1024]{1,0:T(8,128)(2,1)S(1)}, bf16[128,1024]{1,0:T(8,128)(2,1)S(1)}, u32[]{:S(2)}, u32[]{:S(2)}) collective-permute-start(bf16[128,1024]{1,0:T(8,128)(2,1)S(1)} %get-tuple-element.24), channel_id=1, source_target_pairs={{0,8},{1,9},{2,10},{3,11},{4,12},{5,13},{6,14},{7,15},{8,0},{9,1},... | collective-permute-start | bytes 786440 | tf_op jit(solution)/shard_map/ppermute | solution.py:90
  83.2 18.3 %collective-permute-start.26 = (bf16[128,1024]{1,0:T(8,128)(2,1)S(1)}, bf16[128,1024]{1,0:T(8,128)(2,1)S(1)}, u32[]{:S(2)}, u32[]{:S(2)}) collective-permute-start(bf16[128,1024]{1,0:T(8,128)(2,1)S(1)} %collective-permute-done.23.refs_2_), channel_id=1, source_target_pairs={{0,1},{1,0},{2,3},{3,2},{4,5},{5,4},{6,7},{7,6},{8,9},{9,8},{10,11... | collective-permute-start | bytes 786440 | tf_op jit(solution)/shard_map/ppermute | solution.py:90
  101.4 1.5 collective-permute-start.25
  101.4 14.0 %collective-permute-start.28 = (bf16[256,512]{1,0:T(8,128)(2,1)S(1)}, bf16[256,512]{1,0:T(8,128)(2,1)S(1)}, u32[]{:S(2)}, u32[]{:S(2)}) collective-permute-start(bf16[256,512]{1,0:T(8,128)(2,1)S(1)} %get-tuple-element.20.refs_6_), channel_id=1, source_target_pairs={{0,16},{1,17},{2,18},{3,19},{4,20},{5,21},{6,22},{7,23},{8,24},{9,... | collective-permute-start | bytes 786440 | tf_op jit(solution)/shard_map/ppermute | solution.py:90
  101.5 14.0 %collective-permute-start.24 = (bf16[128,1024]{1,0:T(8,128)(2,1)S(1)}, bf16[128,1024]{1,0:T(8,128)(2,1)S(1)}, u32[]{:S(2)}, u32[]{:S(2)}) collective-permute-start(bf16[128,1024]{1,0:T(8,128)(2,1)S(1)} %collective-permute-done.21.refs_0_), channel_id=1, source_target_pairs={{0,1},{1,0},{2,3},{3,2},{4,5},{5,4},{6,7},{7,6},{8,9},{9,8},{10,11... | collective-permute-start | bytes 786440 | tf_op jit(solution)/shard_map/ppermute | solution.py:90
  103.0 13.9 %collective-permute-start.27 = (bf16[256,512]{1,0:T(8,128)(2,1)S(1)}, bf16[256,512]{1,0:T(8,128)(2,1)S(1)}, u32[]{:S(2)}, u32[]{:S(2)}) collective-permute-start(bf16[256,512]{1,0:T(8,128)(2,1)S(1)} %get-tuple-element.20.refs_6_), channel_id=1, source_target_pairs={{0,8},{1,9},{2,10},{3,11},{4,12},{5,13},{6,14},{7,15},{8,0},{9,1},... | collective-permute-start | bytes 786440 | tf_op jit(solution)/shard_map/ppermute | solution.py:90
  115.4 8.2 %collective-permute-start.29 = (bf16[256,512]{1,0:T(8,128)(2,1)S(1)}, bf16[256,512]{1,0:T(8,128)(2,1)S(1)}, u32[]{:S(2)}, u32[]{:S(2)}) collective-permute-start(bf16[256,512]{1,0:T(8,128)(2,1)S(1)} %collective-permute-done.28.refs_8_), channel_id=1, source_target_pairs={{0,8},{1,9},{2,10},{3,11},{4,12},{5,13},{6,14},{7,15},{8,0},{9,1},... | collective-permute-start | bytes 786440 | tf_op jit(solution)/shard_map/ppermute | solution.py:90
  126.0 20.1 %copy-start.1 = (bf16[2048,512]{1,0:T(8,128)(2,1)S(1)}, bf16[2048,512]{1,0:T(8,128)(2,1)}, u32[]{:S(2)}) copy-start(bf16[2048,512]{1,0:T(8,128)(2,1)} %get-tuple-element.17.refs_0_) | copy-start | bytes 6291460

commit v4 on v3

--- a/solution.py
+++ b/solution.py
@@ -110,20 +110,19 @@
 
 def gather_planes(column, masks):
     arrays, places = [], []
-    depth = column[masks[0]].shape[0]
-    half = depth // 2
-    to_x, to_y = [], []
+
+    def add(mask, first, array):
+        places.append((mask, first, len(arrays), 0, array.shape[0]))
+        arrays.append(array)
+
+    half = column[masks[0]].shape[0] // 2
     for mask in masks:
         by_x, by_y = swap(column[mask], X), swap(column[mask], Y)
-        for bits, array in ((0, column[mask]), (X, by_x), (Y, by_y)):
-            places.append((mask | bits, 0, len(arrays), 0, depth))
-            arrays.append(array)
-        to_x.append(by_y[:half])
-        to_y.append(by_x[half:])
-    for first, bits, halves in ((0, X, to_x), (half, Y, to_y)):
-        for n, mask in enumerate(masks):
-            places.append((mask | X | Y, first, len(arrays), n * half, half))
-        arrays.append(swap(jnp.concatenate(halves, axis=0), bits))
+        add(mask, 0, column[mask])
+        add(mask | X, 0, by_x)
+        add(mask | Y, 0, by_y)
+        add(mask | X | Y, 0, swap(by_y[:half], X))
+        add(mask | X | Y, half, swap(by_x[half:], Y))
     return arrays, places
 
 
@@ -157,8 +156,6 @@
     places,
     count,
     me_ref,
-    own_slot_ref,
-    mate_slot_ref,
     own_ref,
     mate_ref,
     own_cot_ref,
@@ -166,7 +163,7 @@
     begun_ref,
     *refs,
 ):
-    delta_ref, send_ref, weight_ref, acc = refs[count:]
+    delta_ref, weight_ref, acc = refs[count:]
     me = me_ref[0]
     core = me & 1
     rows = own_ref.shape[0]
@@ -182,14 +179,21 @@
             upstream = cot_ref[:, cols].astype(jnp.float32)
             delta = (upstream - normed * jnp.mean(upstream * normed, axis=1, keepdims=True)) / scale
             delta_ref[pl.ds(at, rows), cols] = delta.astype(jnp.bfloat16)
-    slots = lax.broadcasted_iota(jnp.int32, (send_ref.shape[0], rows), 0)
-    sent = None
-    for side, slot_ref in enumerate((own_slot_ref, mate_slot_ref)):
-        at = pl.multiple_of((core ^ side) * rows, rows)
-        hot = (slots == slot_ref[...]).astype(jnp.bfloat16)
-        part = dot(hot, delta_ref[pl.ds(at, rows), :], ((1,), (0,)))
-        sent = part if sent is None else sent + part
-    send_ref[...] = sent.astype(jnp.bfloat16)
+
+
+def select_kernel(count, me_ref, code_ref, *refs):
+    sent_ref = refs[count]
+    slot_count, half_cols = sent_ref.shape
+    rows = code_ref.shape[1]
+    level = lax.shift_right_logical(me_ref[0], 3)
+    slots = lax.broadcasted_iota(jnp.int32, (slot_count, rows), 0) + level * slot_count
+    total = None
+    for n in range(count):
+        for side in range(2):
+            hot = (slots == code_ref[2 * n + side : 2 * n + side + 1, :]).astype(jnp.bfloat16)
+            part = dot(hot, refs[n][side * rows : (side + 1) * rows, :], ((1,), (0,)))
+            total = part if total is None else total + part
+    sent_ref[...] = total.astype(jnp.bfloat16)
 
 
 def weight_grad_kernel(count, me_ref, own_ref, mate_ref, *refs):
@@ -222,14 +226,23 @@
 
 
 def row_grad_kernel(first_masks, me_ref, got_ref, *refs):
-    out_ref = refs[-1]
+    out_ref, rows_ref = refs[-2:]
     me = me_ref[0]
-    receive = out_ref.shape[0]
-    half = got_ref.shape[3]
+    chips, _, count, _ = got_ref.shape
     depth = refs[0].shape[0]
-    low, high = got_ref[:, 0].reshape(receive, half), got_ref[:, 1].reshape(receive, half)
-    own = jnp.where(me & 1 == 0, low, high)
-    mate = jnp.where(me & 1 == 0, high, low)
+    block = 16
+
+    @pl.when(pl.program_id(0) == 0)
+    def _():
+        for level in range(count // block):
+            for chip in range(chips):
+                at = (level * chips + chip) * block
+                for side in range(2):
+                    rows_ref[side, at : at + block, :] = got_ref[
+                        chip, side, level * block : (level + 1) * block, :
+                    ]
+
+    own, mate = rows_ref[me & 1], rows_ref[1 - (me & 1)]
     for n, first in enumerate(first_masks):
         total = dot(own, refs[2 * n][...], ((1,), (1,)))
         total += dot(mate, refs[2 * n + 1][...], ((1,), (1,)))
@@ -281,13 +294,13 @@
     sets = [gather_planes(column, part) for part in parts_of]
 
     mate_tokens = swap(tokens, CORE)
-    late_tokens = after(tokens, column[masks[-1]])
+    far_tokens = after(tokens, sets[0][0][3], sets[0][0][4])
+    near_tokens = after(tokens, column[masks[-1]])
     own_features = []
     for mask in masks[1:]:
         there = lax.shift_right_logical(me ^ mask, 3)
-        own_features.append(
-            swap(lax.dynamic_slice_in_dim(late_tokens, there * wide, wide, 1), mask)
-        )
+        source = near_tokens if mask == PLANE else far_tokens
+        own_features.append(swap(lax.dynamic_slice_in_dim(source, there * wide, wide, 1), mask))
     mate_features = [swap(value, CORE) for value in own_features]
 
     key_cot, routes, counts = lax.optimization_barrier((key_cot, routes, counts, column[PLANE]))[:3]
@@ -307,8 +320,18 @@
         positions[:, None] < positions[None, :]
     )
     earlier = jnp.sum(same.astype(jnp.int32), axis=0)
-    own_slot = ((destination * 2 + core) * per_peer + earlier).reshape(1, rows)
-    mate_slot = swap(own_slot, CORE)
+    source = 2 * lax.shift_right_logical(me, 3) + core
+    code = ((destination * 2 * levels + source) * per_peer + earlier).reshape(1, rows)
+    mate_code = swap(code, CORE)
+    codes = jnp.where(
+        core == 0,
+        jnp.concatenate([code, mate_code], axis=0),
+        jnp.concatenate([mate_code, code], axis=0),
+    )
+    order = [0]
+    for bit in reversed([PLANE << n for n in range(levels.bit_length() - 1)]):
+        codes = jnp.concatenate([codes, swap(codes, bit)], axis=0)
+        order += [mask | bit for mask in order]
 
     kept = jax.ShapeDtypeStruct((width_model // 2, half_cols), jnp.bfloat16)
     sums = jax.ShapeDtypeStruct((2, rows, half_cols), jnp.float32)
@@ -323,22 +346,43 @@
         name="project",
     )(me_scalar, tokens, mate_tokens, *arrays)
     arrays, places = sets[1]
-    delta, send, last_weight = pl.pallas_call(
+    begun = after(begun, codes, *own_features)
+    delta, last_weight = pl.pallas_call(
         functools.partial(delta_kernel, places, len(arrays)),
-        out_shape=(
-            jax.ShapeDtypeStruct((2 * rows, half_cols), jnp.bfloat16),
-            jax.ShapeDtypeStruct((2 * receive, half_cols), jnp.bfloat16),
-            kept,
-        ),
-        in_specs=[SCALAR] + vmem(7 + len(arrays)),
-        out_specs=tuple(vmem(3)),
+        out_shape=(jax.ShapeDtypeStruct((2 * rows, half_cols), jnp.bfloat16), kept),
+        in_specs=[SCALAR] + vmem(5 + len(arrays)),
+        out_specs=tuple(vmem(2)),
         scratch_shapes=[pltpu.VMEM(sums.shape, sums.dtype)],
         compiler_params=PARAMS,
         cost_estimate=cost(2 * rows * width_model // 2 * half_cols, 6 << 20),
         name="delta",
-    )(me_scalar, own_slot, mate_slot, tokens, mate_tokens, own_cot, mate_cot, begun, *arrays)
+    )(me_scalar, tokens, mate_tokens, own_cot, mate_cot, begun, *arrays)
 
     deltas = gather_column(delta)
+    selected = pl.pallas_call(
+        functools.partial(select_kernel, levels),
+        out_shape=jax.ShapeDtypeStruct((PLANE * 2 * levels * per_peer, half_cols), jnp.bfloat16),
+        in_specs=[SCALAR] + vmem(1 + levels),
+        out_specs=vmem(1)[0],
+        compiler_params=PARAMS,
+        cost_estimate=cost(receive * 2 * levels * 2 * rows * half_cols, 2 << 20),
+        name="select",
+    )(me_scalar, codes, *[deltas[mask] for mask in order])
+    planes = [[z * PLANE + p for p in range(PLANE)] for z in range(levels)]
+
+    def to_plane(value):
+        return lax.all_to_all(
+            value.reshape(PLANE, -1, half_cols),
+            "dp",
+            split_axis=0,
+            concat_axis=0,
+            axis_index_groups=planes,
+            tiled=True,
+        )
+
+    got = to_plane(selected)
+
+    ready = after(deltas[0], selected)
     part = pl.pallas_call(
         functools.partial(weight_grad_kernel, levels),
         out_shape=jax.ShapeDtypeStruct((wide, half_cols), jnp.bfloat16),
@@ -354,31 +398,10 @@
         mate_tokens,
         *own_features,
         *mate_features,
-        *[deltas[mask] for mask in masks],
-    )
-    got = lax.all_to_all(
-        send.reshape(size, 2 * per_peer, half_cols), "dp", split_axis=0, concat_axis=0, tiled=True
-    )
-    part = after(part, got)
+        *[ready if mask == 0 else deltas[mask] for mask in masks],
+    )
     shard = width_model // size
-    planes = [[z * PLANE + p for p in range(PLANE)] for z in range(levels)]
-    parts = lax.all_to_all(
-        part.reshape(PLANE, shard, half_cols),
-        "dp",
-        split_axis=0,
-        concat_axis=0,
-        axis_index_groups=planes,
-        tiled=True,
-    )
-    key_grad = pl.pallas_call(
-        functools.partial(sum_kernel, math.sqrt(rows * size)),
-        out_shape=jax.ShapeDtypeStruct((shard, cols), jnp.float32),
-        in_specs=vmem(1),
-        out_specs=vmem(1)[0],
-        compiler_params=PARAMS,
-        cost_estimate=cost(PLANE * shard * half_cols, 2 << 20),
-        name="sum",
-    )(parts.reshape(PLANE // 2, 2, shard, half_cols))
+    parts = to_plane(part)
 
     depth = width_model // chips
     kept_weights = [first_weight, swap(first_weight, CORE), last_weight, swap(last_weight, CORE)]
@@ -388,14 +411,26 @@
         grid=(chips // 2,),
         in_specs=[
             SCALAR,
-            pl.BlockSpec((chips, 2, 2 * per_peer, half_cols), lambda i: (0, 0, 0, 0)),
+            pl.BlockSpec((PLANE // 2, 2, 2 * levels * per_peer, half_cols), lambda i: (0, 0, 0, 0)),
         ]
         + [pl.BlockSpec((depth, half_cols), lambda i: (i, 0))] * len(kept_weights),
         out_specs=pl.BlockSpec((receive, width_model), lambda i: (0, 0)),
+        scratch_shapes=[pltpu.VMEM((2, receive, half_cols), jnp.bfloat16)],
         compiler_params=PARAMS,
         cost_estimate=cost(receive * width_model * cols, 12 << 20),
         name="row_grad",
-    )(me_scalar, got.reshape(chips, 2, 2 * per_peer, half_cols), *kept_weights)
+    )(me_scalar, got.reshape(PLANE // 2, 2, 2 * levels * per_peer, half_cols), *kept_weights)
+
+    parts = after(parts, row_grads)
+    key_grad = pl.pallas_call(
+        functools.partial(sum_kernel, math.sqrt(rows * size)),
+        out_shape=jax.ShapeDtypeStruct((shard, cols), jnp.float32),
+        in_specs=vmem(1),
+        out_specs=vmem(1)[0],
+        compiler_params=PARAMS,
+        cost_estimate=cost(PLANE * shard * half_cols, 2 << 20),
+        name="sum",
+    )(parts.reshape(PLANE // 2, 2, shard, half_cols))
     return (row_grads, key_grad)
 
 

time: 155 us -> 142 us (0.916)
  waiting for transfers between devices: 82.3 us -> 48.6 us
  starting transfers between devices: 31.8 us -> 57.6 us
  blocking collectives: 19.1 us -> 0 us
  local copies, waits for them, and re-layouts: 1.17 us -> 8.81 us
  Pallas kernels: 16.5 us -> 20.5 us
  other arithmetic: 2.96 us -> 4.57 us
    ppermute x30 -> x36, waiting for transfers between devices: 82.3 us -> 41.8 us  [swap(): return lax.ppermute(value, 'dp', [(i, i ^ mask) for i in range(size)])]
    ppermute x30 -> x36, starting transfers between devices: 27.8 us -> 50.3 us  [swap(): return lax.ppermute(value, 'dp', [(i, i ^ mask) for i in range(size)])]
    all_to_all x1 -> x0, blocking collectives: 19.1 us -> none  [per_device_paired(): lax.all_to_all(part.reshape(PLANE, shard, half_cols), 'dp', split_axis=0,...]
    all_to_all x1 -> x2, waiting for transfers between devices: 0.01 us -> 6.77 us  [to_plane(): lax.all_to_all(value.reshape(PLANE, -1, half_cols), 'dp', split_axis=0, c...]
    unnamed x6 -> x32, local copies, waits for them, and re-layouts: 0.01 us -> 4.56 us
    all_to_all x1 -> x2, starting transfers between devices: 4.02 us -> 7.38 us  [to_plane(): lax.all_to_all(value.reshape(PLANE, -1, half_cols), 'dp', split_axis=0, c...]
    pallas_call x0 -> x1, Pallas kernels: none -> 2.02 us  [per_device_paired(): pl.pallas_call(functools.partial(select_kernel, levels), out_shape=jax.Sh...]
  transfers between devices with their start and end apart: 31 -> 38, of which waited for: 14 -> 17; matrix products, arithmetic and copies ran while one was open for 2% -> 5% of each run, Pallas kernels for 5% -> 12%
where the time goes in v4:
time: 142 us; the launch traced here: 141 us
  starting transfers between devices  57.6 us (41%)
  waiting for transfers between devices  48.6 us (34%)
  Pallas kernels  20.5 us (14%)
  local copies, waits for them, and re-layouts  8.81 us (6%)
  other arithmetic  4.57 us (3%)
    ppermute x36, starting transfers between devices, swap(): return lax.ppermute(value, 'dp', [(i, i ^ mask) for i in range(size)])  50.3 us
    ppermute x36, waiting for transfers between devices, swap(): return lax.ppermute(value, 'dp', [(i, i ^ mask) for i in range(size)])  41.8 us
    pallas_call x1, Pallas kernels, per_device_paired(): pl.pallas_call(functools.partial(row_grad_kernel, [part[0] for part in pa...  8.8 us
    all_to_all x2, starting transfers between devices, to_plane(): lax.all_to_all(value.reshape(PLANE, -1, half_cols), 'dp', split_axis=0, c...  7.38 us
    all_to_all x2, waiting for transfers between devices, to_plane(): lax.all_to_all(value.reshape(PLANE, -1, half_cols), 'dp', split_axis=0, c...  6.77 us
    unnamed x32, local copies, waits for them, and re-layouts  4.56 us
    pallas_call x1, Pallas kernels, per_device_paired(): pl.pallas_call(functools.partial(weight_grad_kernel, levels), out_shape=j...  3.33 us
    pallas_call x1, Pallas kernels, per_device_paired(): pl.pallas_call(functools.partial(project_kernel, places, len(arrays)), ou...  2.87 us
  transfers between devices with their start and end apart: 38, of which 17 were waited for; matrix products, arithmetic and copies ran while one was open for 5% of the time, Pallas kernels for 12%

profile of v4, /device:TPU:0, one launch (start us, length us, event | category | flops | bytes accessed | tf_op | source)
XLA Modules:
  0.0 141.0 jit_solution(14811798604818893592)
XLA Ops:
  0.7 1.1 constant_dynamic-slice_fusion.6
  2.3 1.0 collective-permute-done
  3.3 3.0 %collective-permute-start.1 = (bf16[256,512]{1,0:T(8,128)(2,1)S(1)}, bf16[256,512]{1,0:T(8,128)(2,1)S(1)}, u32[]{:S(2)}, u32[]{:S(2)}) collective-permute-start(bf16[256,512]{1,0:T(8,128)(2,1)S(1)} %maximum_select_fusion.refs_0_), channel_id=1, source_target_pairs={{0,8},{1,9},{2,10},{3,11},{4,12},{5,13},{6,14},{7,15},{8,0},{9,1},... | collective-permute-start | bytes 786440 | tf_op jit(solution)/shard_map/ppermute | solution.py:90
  6.3 1.5 %collective-permute-start.8 = (bf16[256,512]{1,0:T(8,128)(2,1)S(1)}, bf16[256,512]{1,0:T(8,128)(2,1)S(1)}, u32[]{:S(2)}, u32[]{:S(2)}) collective-permute-start(bf16[256,512]{1,0:T(8,128)(2,1)S(1)} %maximum_select_fusion.refs_0_), channel_id=1, source_target_pairs={{0,4},{1,5},{2,6},{3,7},{4,0},{5,1},{6,2},{7,3},{8,12},{9,13},{10,... | collective-permute-start | bytes 786440 | tf_op jit(solution)/shard_map/ppermute | solution.py:90
  7.8 1.5 %collective-permute-start.7 = (bf16[256,512]{1,0:T(8,128)(2,1)S(1)}, bf16[256,512]{1,0:T(8,128)(2,1)S(1)}, u32[]{:S(2)}, u32[]{:S(2)}) collective-permute-start(bf16[256,512]{1,0:T(8,128)(2,1)S(1)} %maximum_select_fusion.refs_0_), channel_id=1, source_target_pairs={{0,2},{1,3},{2,0},{3,1},{4,6},{5,7},{6,4},{7,5},{8,10},{9,11},{10,... | collective-permute-start | bytes 786440 | tf_op jit(solution)/shard_map/ppermute | solution.py:90
  9.3 3.6 %collective-permute-done.1.refs_5_ = bf16[256,512]{1,0:T(8,128)(2,1)S(1)} collective-permute-done((bf16[256,512]{1,0:T(8,128)(2,1)S(1)}, bf16[256,512]{1,0:T(8,128)(2,1)S(1)}, u32[]{:S(2)}, u32[]{:S(2)}) %collective-permute-start.1) | collective-permute-done | bytes 262176 | tf_op jit(solution)/shard_map/ppermute | solution.py:90
  12.9 0.8 convert_reduce_fusion
  14.4 2.8 %collective-permute-start.15 = (bf16[256,512]{1,0:T(8,128)(2,1)S(1)}, bf16[256,512]{1,0:T(8,128)(2,1)S(1)}, u32[]{:S(2)}, u32[]{:S(2)}) collective-permute-start(bf16[256,512]{1,0:T(8,128)(2,1)S(1)} %maximum_select_fusion.refs_0_), channel_id=1, source_target_pairs={{0,16},{1,17},{2,18},{3,19},{4,20},{5,21},{6,22},{7,23},{8,24},{9,... | collective-permute-start | bytes 786440 | tf_op jit(solution)/shard_map/ppermute | solution.py:90
  17.2 1.1 collective-permute-start.3
  19.0 1.5 %collective-permute-start.9 = (bf16[128,512]{1,0:T(8,128)(2,1)}, bf16[128,512]{1,0:T(8,128)(2,1)S(1)}, u32[]{:S(2)}, u32[]{:S(2)}) collective-permute-start(bf16[128,512]{1,0:T(8,128)(2,1)} %slice.37), channel_id=1, source_target_pairs={{0,2},{1,3},{2,0},{3,1},{4,6},{5,7},{6,4},{7,5},{8,10},{9,11},{10,... | collective-permute-start | bytes 393224 | tf_op jit(solution)/shard_map/ppermute | solution.py:90
  21.1 1.5 %collective-permute-start.10 = (bf16[128,512]{1,0:T(8,128)(2,1)}, bf16[128,512]{1,0:T(8,128)(2,1)}, u32[]{:S(2)}, u32[]{:S(2)}) collective-permute-start(bf16[128,512]{1,0:T(8,128)(2,1)} %slice.38), channel_id=1, source_target_pairs={{0,4},{1,5},{2,6},{3,7},{4,0},{5,1},{6,2},{7,3},{8,12},{9,13},{10,... | collective-permute-start | bytes 393224 | tf_op jit(solution)/shard_map/ppermute | solution.py:90
  22.7 7.2 %collective-permute-done.3 = s32[2,128]{1,0:T(2,128)S(1)} collective-permute-done((s32[2,128]{1,0:T(2,128)S(1)}, s32[2,128]{1,0:T(2,128)S(1)}, u32[]{:S(2)}, u32[]{:S(2)}) %collective-permute-start.3) | collective-permute-done | bytes 1056 | tf_op jit(solution)/shard_map/ppermute | solution.py:90
  30.6 1.4 reduce-window.4
  32.0 1.5 %collective-permute-start.21 = (bf16[256,512]{1,0:T(8,128)(2,1)S(1)}, bf16[256,512]{1,0:T(8,128)(2,1)S(1)}, u32[]{:S(2)}, u32[]{:S(2)}) collective-permute-start(bf16[256,512]{1,0:T(8,128)(2,1)S(1)} %collective-permute-done.15.refs_0_), channel_id=1, source_target_pairs={{0,4},{1,5},{2,6},{3,7},{4,0},{5,1},{6,2},{7,3},{8,12},{9,13},{10,... | collective-permute-start | bytes 786440 | tf_op jit(solution)/shard_map/ppermute | solution.py:90
  33.5 1.3 collective-permute-start.16
  34.9 0.9 collective-permute-start.12
  35.8 1.5 %collective-permute-start.11 = (bf16[256,512]{1,0:T(8,128)(2,1)S(1)}, bf16[256,512]{1,0:T(8,128)(2,1)S(1)}, u32[]{:S(2)}, u32[]{:S(2)}) collective-permute-start(bf16[256,512]{1,0:T(8,128)(2,1)S(1)} %collective-permute-done.1.refs_5_), channel_id=1, source_target_pairs={{0,2},{1,3},{2,0},{3,1},{4,6},{5,7},{6,4},{7,5},{8,10},{9,11},{10,... | collective-permute-start | bytes 786440 | tf_op jit(solution)/shard_map/ppermute | solution.py:90
  38.0 1.1 constant_dynamic-slice_fusion
  39.0 2.2 %collective-permute-done.21.refs_2_ = bf16[256,512]{1,0:T(8,128)(2,1)S(1)} collective-permute-done((bf16[256,512]{1,0:T(8,128)(2,1)S(1)}, bf16[256,512]{1,0:T(8,128)(2,1)S(1)}, u32[]{:S(2)}, u32[]{:S(2)}) %collective-permute-start.21) | collective-permute-done | bytes 262176 | tf_op jit(solution)/shard_map/ppermute | solution.py:90
  41.2 1.5 %collective-permute-start.20 = (bf16[256,512]{1,0:T(8,128)(2,1)S(1)}, bf16[256,512]{1,0:T(8,128)(2,1)S(1)}, u32[]{:S(2)}, u32[]{:S(2)}) collective-permute-start(bf16[256,512]{1,0:T(8,128)(2,1)S(1)} %collective-permute-done.15.refs_0_), channel_id=1, source_target_pairs={{0,2},{1,3},{2,0},{3,1},{4,6},{5,7},{6,4},{7,5},{8,10},{9,11},{10,... | collective-permute-start | bytes 786440 | tf_op jit(solution)/shard_map/ppermute | solution.py:90
  42.7 2.8 %collective-permute-start.19 = (bf16[128,1024]{1,0:T(8,128)(2,1)S(1)}, bf16[128,1024]{1,0:T(8,128)(2,1)S(1)}, u32[]{:S(2)}, u32[]{:S(2)}) collective-permute-start(bf16[128,1024]{1,0:T(8,128)(2,1)S(1)} %get-tuple-element.26), channel_id=1, source_target_pairs={{0,24},{1,25},{2,26},{3,27},{4,28},{5,29},{6,30},{7,31},{8,16},{9,... | collective-permute-start | bytes 786440 | tf_op jit(solution)/shard_map/ppermute | solution.py:90
  45.6 1.5 %collective-permute-start.25 = (bf16[256,512]{1,0:T(8,128)(2,1)S(1)}, bf16[256,512]{1,0:T(8,128)(2,1)S(1)}, u32[]{:S(2)}, u32[]{:S(2)}) collective-permute-start(bf16[256,512]{1,0:T(8,128)(2,1)S(1)} %collective-permute-done.16.refs_5_), channel_id=1, source_target_pairs={{0,4},{1,5},{2,6},{3,7},{4,0},{5,1},{6,2},{7,3},{8,12},{9,13},{10,... | collective-permute-start | bytes 786440 | tf_op jit(solution)/shard_map/ppermute | solution.py:90
  47.1 1.5 %collective-permute-start.24 = (bf16[256,512]{1,0:T(8,128)(2,1)S(1)}, bf16[256,512]{1,0:T(8,128)(2,1)S(1)}, u32[]{:S(2)}, u32[]{:S(2)}) collective-permute-start(bf16[256,512]{1,0:T(8,128)(2,1)S(1)} %collective-permute-done.16.refs_5_), channel_id=1, source_target_pairs={{0,2},{1,3},{2,0},{3,1},{4,6},{5,7},{6,4},{7,5},{8,10},{9,11},{10,... | collective-permute-start | bytes 786440 | tf_op jit(solution)/shard_map/ppermute | solution.py:90
  49.5 3.4 %collective-permute-start.18 = (bf16[128,1024]{1,0:T(8,128)(2,1)S(1)}, bf16[128,1024]{1,0:T(8,128)(2,1)S(1)}, u32[]{:S(2)}, u32[]{:S(2)}) collective-permute-start(bf16[128,1024]{1,0:T(8,128)(2,1)S(1)} %get-tuple-element.27), channel_id=1, source_target_pairs={{0,16},{1,17},{2,18},{3,19},{4,20},{5,21},{6,22},{7,23},{8,24},{9,... | collective-permute-start | bytes 786440 | tf_op jit(solution)/shard_map/ppermute | solution.py:90
  52.9 9.3 %collective-permute-start.17 = (bf16[128,1024]{1,0:T(8,128)(2,1)S(1)}, bf16[128,1024]{1,0:T(8,128)(2,1)S(1)}, u32[]{:S(2)}, u32[]{:S(2)}) collective-permute-start(bf16[128,1024]{1,0:T(8,128)(2,1)S(1)} %constant_dynamic-slice_fusion.2), channel_id=1, source_target_pairs={{0,8},{1,9},{2,10},{3,11},{4,12},{5,13},{6,14},{7,15},{8,0},{9,1},... | collective-permute-start | bytes 786440 | tf_op jit(solution)/shard_map/ppermute | solution.py:90
  63.1 1.3 collective-permute-start.14
  64.6 2.2 %collective-permute-done.18.refs_1_ = bf16[128,1024]{1,0:T(8,128)(2,1)S(1)} collective-permute-done((bf16[128,1024]{1,0:T(8,128)(2,1)S(1)}, bf16[128,1024]{1,0:T(8,128)(2,1)S(1)}, u32[]{:S(2)}, u32[]{:S(2)}) %collective-permute-start.18) | collective-permute-done | bytes 262176 | tf_op jit(solution)/shard_map/ppermute | solution.py:90
  67.2 0.9 collective-permute-start.22
  68.1 1.2 collective-permute-start.23
  69.3 3.0 %collective-permute-done.17.refs_0_ = bf16[128,1024]{1,0:T(8,128)(2,1)S(1)} collective-permute-done((bf16[128,1024]{1,0:T(8,128)(2,1)S(1)}, bf16[128,1024]{1,0:T(8,128)(2,1)S(1)}, u32[]{:S(2)}, u32[]{:S(2)}) %collective-permute-start.17) | collective-permute-done | bytes 262176 | tf_op jit(solution)/shard_map/ppermute | solution.py:90
  72.3 1.2 collective-permute-start.26
  73.5 0.9 collective-permute-start.27
  75.1 2.9 %project.1 = (bf16[2048,512]{1,0:T(8,128)(2,1)}, f32[2,128,512]{2,1,0:T(8,128)S(1)}) custom-call(s32[1]{0:T(128)} %bitcast.me_ref, bf16[128,4096]{1,0:T(8,128)(2,1)S(1)} %copy-done, bf16[128,4096]{1,0:T(8,128)(2,1)S(1)} %collective-permute-done.5.mate_ref, bf16[256,512]{1,0:T(8,128)(2,1)S(1)} %maximum_select_fusion.refs_0_, ...), custom_call_target="tpu_custom_call" | custom-call | flops 536870912 | bytes 6291456 | tf_op jit(solution)/shard_map/project/pallas_call | solution.py:339
  78.7 2.5 %delta.1 = (bf16[256,512]{1,0:T(8,128)(2,1)S(1)}, bf16[2048,512]{1,0:T(8,128)(2,1)}) custom-call(s32[1]{0:T(128)} %bitcast.me_ref, bf16[128,4096]{1,0:T(8,128)(2,1)S(1)} %copy-done, bf16[128,4096]{1,0:T(8,128)(2,1)S(1)} %collective-permute-done.5.mate_ref, bf16[128,512]{1,0:T(8,128)(2,1)S(1)} %get-tuple-element.29.own_cot_ref, ...), custom_call_target="tpu_custom_call" | custom-call | flops 536870912 | bytes 6291456 | tf_op jit(solution)/shard_map/delta/pallas_call | solution.py:350
  82.5 2.5 %collective-permute-start.29 = (bf16[256,512]{1,0:T(8,128)(2,1)S(1)}, bf16[256,512]{1,0:T(8,128)(2,1)S(1)}, u32[]{:S(2)}, u32[]{:S(2)}) collective-permute-start(bf16[256,512]{1,0:T(8,128)(2,1)S(1)} %get-tuple-element.24.refs_0_.refs_6_), channel_id=1, source_target_pairs={{0,8},{1,9},{2,10},{3,11},{4,12},{5,13},{6,14},{7,15},{8,0},{9,1},... | collective-permute-start | bytes 786440 | tf_op jit(solution)/shard_map/ppermute | solution.py:90
  85.0 11.7 %collective-permute-done.28.refs_1_.refs_8_ = bf16[256,512]{1,0:T(8,128)(2,1)S(1)} collective-permute-done((bf16[256,512]{1,0:T(8,128)(2,1)S(1)}, bf16[256,512]{1,0:T(8,128)(2,1)S(1)}, u32[]{:S(2)}, u32[]{:S(2)}) %collective-permute-start.28) | collective-permute-done | bytes 262176 | tf_op jit(solution)/shard_map/ppermute | solution.py:90
  96.8 8.0 %collective-permute-done.30.refs_3_.refs_9_ = bf16[256,512]{1,0:T(8,128)(2,1)S(1)} collective-permute-done((bf16[256,512]{1,0:T(8,128)(2,1)S(1)}, bf16[256,512]{1,0:T(8,128)(2,1)S(1)}, u32[]{:S(2)}, u32[]{:S(2)}) %collective-permute-start.30) | collective-permute-done | bytes 262176 | tf_op jit(solution)/shard_map/ppermute | solution.py:90
  104.8 2.0 %select.11 = bf16[512,512]{1,0:T(8,128)(2,1)} custom-call(s32[1]{0:T(128)} %bitcast.me_ref, s32[8,128]{1,0:T(8,128)S(1)} %pad_add_fusion.code_ref, bf16[256,512]{1,0:T(8,128)(2,1)S(1)} %get-tuple-element.24.refs_0_.refs_6_, bf16[256,512]{1,0:T(8,128)(2,1)S(1)} %collective-permute-done.28.refs_1_.refs_8_, ...), custom_call_target="tpu_custom_call" | custom-call | flops 536870912 | bytes 2097152 | tf_op jit(solution)/shard_map/select/pallas_call | solution.py:362
  107.6 3.5 %all-to-all-start = ((bf16[8,64,512]{2,1,0:T(8,128)(2,1)}), bf16[8,64,512]{2,1,0:T(8,128)(2,1)S(1)}, u32[]{:S(2)}, u32[]{:S(2)}) async-start(bf16[8,64,512]{2,1,0:T(8,128)(2,1)} %bitcast.6), calls=%async_computation | async-start | bytes 1048576 | tf_op jit(solution)/shard_map/all_to_all | solution.py:374
  113.5 0.9 copy-done.8
  114.4 0.9 copy-done.10
  115.4 0.9 copy-done.12
  116.3 0.9 copy-done.14
  117.3 3.3 %weight_grad.1 = bf16[1024,512]{1,0:T(8,128)(2,1)} custom-call(s32[1]{0:T(128)} %bitcast.me_ref, bf16[128,4096]{1,0:T(8,128)(2,1)S(1)} %copy-done, bf16[128,4096]{1,0:T(8,128)(2,1)S(1)} %collective-permute-done.5.mate_ref, bf16[128,1024]{1,0:T(8,128)(2,1)S(1)} %copy-done.6, bf16[128,1024]{1,0:T(8,128)(2,1)S(1)} %copy-done.4, ...), custom_call_target="tpu_custom_call" | custom-call | flops 1073741824 | bytes 4194304 | tf_op jit(solution)/shard_map/weight_grad/pallas_call | solution.py:386
  120.8 3.9 %all-to-all-start.1 = ((bf16[8,128,512]{2,1,0:T(8,128)(2,1)}), bf16[8,128,512]{2,1,0:T(8,128)(2,1)S(1)}, u32[]{:S(2)}, u32[]{:S(2)}) async-start(bf16[8,128,512]{2,1,0:T(8,128)(2,1)} %bitcast.8), calls=%async_computation.1 | async-start | bytes 2097152 | tf_op jit(solution)/shard_map/all_to_all | solution.py:374
  124.7 8.8 %row_grad.1 = bf16[256,4096]{1,0:T(8,128)(2,1)} custom-call(s32[1]{0:T(128)} %bitcast.me_ref, bf16[4,2,64,512]{3,2,1,0:T(8,128)(2,1)S(1)} %bitcast.14, bf16[2048,512]{1,0:T(8,128)(2,1)} %get-tuple-element.22.refs_0_, bf16[2048,512]{1,0:T(8,128)(2,1)} %collective-permute-done.31.refs_1_, bf16[2048,512]{1,0:T(8,128)(2,1)} %get-tuple-element.23.refs_2_, ...), custom_call_target="tpu_custom_call" | custom-call | flops 2147483648 | bytes 12582912 | tf_op jit(solution)/shard_map/row_grad/pallas_call | solution.py:408
  133.5 6.6 %all-to-all-done.1 = bf16[8,128,512]{2,1,0:T(8,128)(2,1)S(1)} async-done(((bf16[8,128,512]{2,1,0:T(8,128)(2,1)}), bf16[8,128,512]{2,1,0:T(8,128)(2,1)S(1)}, u32[]{:S(2)}, u32[]{:S(2)}) %all-to-all-start.1) | async-done | bytes 1048608 | tf_op jit(solution)/shard_map/all_to_all | solution.py:374
  140.1 0.9 sum.1
  (90 shorter events, 12.4 us)
Async XLA Ops:
  0.6 48.8 %copy-start = (bf16[128,4096]{1,0:T(8,128)(2,1)S(1)}, bf16[128,4096]{1,0:T(8,128)(2,1)}, u32[]{:S(2)}) copy-start(bf16[128,4096]{1,0:T(8,128)(2,1)} %own_ref.5) | copy-start | bytes 3145732
  1.7 1.5 %collective-permute-start = (bf16[128,512]{1,0:T(8,128)(2,1)S(1)}, bf16[128,512]{1,0:T(8,128)(2,1)S(1)}, u32[]{:S(2)}, u32[]{:S(2)}) collective-permute-start(bf16[128,512]{1,0:T(8,128)(2,1)S(1)} %get-tuple-element.31), channel_id=1, source_target_pairs={{0,1},{1,0},{2,3},{3,2},{4,5},{5,4},{6,7},{7,6},{8,9},{9,8},{10,11... | collective-permute-start | bytes 393224 | tf_op jit(solution)/shard_map/ppermute | solution.py:90
  3.3 9.6 %collective-permute-start.1 = (bf16[256,512]{1,0:T(8,128)(2,1)S(1)}, bf16[256,512]{1,0:T(8,128)(2,1)S(1)}, u32[]{:S(2)}, u32[]{:S(2)}) collective-permute-start(bf16[256,512]{1,0:T(8,128)(2,1)S(1)} %maximum_select_fusion.refs_0_), channel_id=1, source_target_pairs={{0,8},{1,9},{2,10},{3,11},{4,12},{5,13},{6,14},{7,15},{8,0},{9,1},... | collective-permute-start | bytes 786440 | tf_op jit(solution)/shard_map/ppermute | solution.py:90
  6.3 12.0 %collective-permute-start.8 = (bf16[256,512]{1,0:T(8,128)(2,1)S(1)}, bf16[256,512]{1,0:T(8,128)(2,1)S(1)}, u32[]{:S(2)}, u32[]{:S(2)}) collective-permute-start(bf16[256,512]{1,0:T(8,128)(2,1)S(1)} %maximum_select_fusion.refs_0_), channel_id=1, source_target_pairs={{0,4},{1,5},{2,6},{3,7},{4,0},{5,1},{6,2},{7,3},{8,12},{9,13},{10,... | collective-permute-start | bytes 786440 | tf_op jit(solution)/shard_map/ppermute | solution.py:90
  7.8 12.6 %collective-permute-start.7 = (bf16[256,512]{1,0:T(8,128)(2,1)S(1)}, bf16[256,512]{1,0:T(8,128)(2,1)S(1)}, u32[]{:S(2)}, u32[]{:S(2)}) collective-permute-start(bf16[256,512]{1,0:T(8,128)(2,1)S(1)} %maximum_select_fusion.refs_0_), channel_id=1, source_target_pairs={{0,2},{1,3},{2,0},{3,1},{4,6},{5,7},{6,4},{7,5},{8,10},{9,11},{10,... | collective-permute-start | bytes 786440 | tf_op jit(solution)/shard_map/ppermute | solution.py:90
  14.4 2.8 %collective-permute-start.2 = (s32[1,128]{1,0:T(1,128)S(1)}, s32[1,128]{1,0:T(1,128)S(1)}, u32[]{:S(2)}, u32[]{:S(2)}) collective-permute-start(s32[1,128]{1,0:T(1,128)S(1)} %bitcast_add_fusion), channel_id=1, source_target_pairs={{0,1},{1,0},{2,3},{3,2},{4,5},{5,4},{6,7},{7,6},{8,9},{9,8},{10,11... | collective-permute-start | bytes 1544 | tf_op jit(solution)/shard_map/ppermute | solution.py:90
  14.4 17.6 %collective-permute-start.15 = (bf16[256,512]{1,0:T(8,128)(2,1)S(1)}, bf16[256,512]{1,0:T(8,128)(2,1)S(1)}, u32[]{:S(2)}, u32[]{:S(2)}) collective-permute-start(bf16[256,512]{1,0:T(8,128)(2,1)S(1)} %maximum_select_fusion.refs_0_), channel_id=1, source_target_pairs={{0,16},{1,17},{2,18},{3,19},{4,20},{5,21},{6,22},{7,23},{8,24},{9,... | collective-permute-start | bytes 786440 | tf_op jit(solution)/shard_map/ppermute | solution.py:90
  17.2 12.7 %collective-permute-start.3 = (s32[2,128]{1,0:T(2,128)S(1)}, s32[2,128]{1,0:T(2,128)S(1)}, u32[]{:S(2)}, u32[]{:S(2)}) collective-permute-start(s32[2,128]{1,0:T(2,128)S(1)} %add_select_fusion.1), channel_id=1, source_target_pairs={{0,16},{1,17},{2,18},{3,19},{4,20},{5,21},{6,22},{7,23},{8,24},{9,... | collective-permute-start | bytes 3080 | tf_op jit(solution)/shard_map/ppermute | solution.py:90
  18.3 55.2 %collective-permute-start.5 = (bf16[128,4096]{1,0:T(8,128)(2,1)}, bf16[128,4096]{1,0:T(8,128)(2,1)S(1)}, u32[]{:S(2)}, u32[]{:S(2)}) collective-permute-start(bf16[128,4096]{1,0:T(8,128)(2,1)} %own_ref.5), channel_id=1, source_target_pairs={{0,1},{1,0},{2,3},{3,2},{4,5},{5,4},{6,7},{7,6},{8,9},{9,8},{10,11... | collective-permute-start | bytes 3145736 | tf_op jit(solution)/shard_map/ppermute | solution.py:90
  19.0 15.9 %collective-permute-start.9 = (bf16[128,512]{1,0:T(8,128)(2,1)}, bf16[128,512]{1,0:T(8,128)(2,1)S(1)}, u32[]{:S(2)}, u32[]{:S(2)}) collective-permute-start(bf16[128,512]{1,0:T(8,128)(2,1)} %slice.37), channel_id=1, source_target_pairs={{0,2},{1,3},{2,0},{3,1},{4,6},{5,7},{6,4},{7,5},{8,10},{9,11},{10,... | collective-permute-start | bytes 393224 | tf_op jit(solution)/shard_map/ppermute | solution.py:90
  21.1 14.7 %collective-permute-start.10 = (bf16[128,512]{1,0:T(8,128)(2,1)}, bf16[128,512]{1,0:T(8,128)(2,1)}, u32[]{:S(2)}, u32[]{:S(2)}) collective-permute-start(bf16[128,512]{1,0:T(8,128)(2,1)} %slice.38), channel_id=1, source_target_pairs={{0,4},{1,5},{2,6},{3,7},{4,0},{5,1},{6,2},{7,3},{8,12},{9,13},{10,... | collective-permute-start | bytes 393224 | tf_op jit(solution)/shard_map/ppermute | solution.py:90
  29.9 3.7 %collective-permute-start.4 = (s32[4,128]{1,0:T(4,128)S(1)}, s32[4,128]{1,0:T(4,128)}, u32[]{:S(2)}, u32[]{:S(2)}) collective-permute-start(s32[4,128]{1,0:T(4,128)S(1)} %pad_add_fusion.1), channel_id=1, source_target_pairs={{0,8},{1,9},{2,10},{3,11},{4,12},{5,13},{6,14},{7,15},{8,0},{9,1},... | collective-permute-start | bytes 6152 | tf_op jit(solution)/shard_map/ppermute | solution.py:90
  32.0 32.4 %copy-start.15 = (bf16[128,1024]{1,0:T(8,128)(2,1)S(1)}, bf16[128,1024]{1,0:T(8,128)(2,1)}, u32[]{:S(2)}) copy-start(bf16[128,1024]{1,0:T(8,128)(2,1)} %param.7) | copy-start | bytes 786436
  32.0 9.2 %collective-permute-start.21 = (bf16[256,512]{1,0:T(8,128)(2,1)S(1)}, bf16[256,512]{1,0:T(8,128)(2,1)S(1)}, u32[]{:S(2)}, u32[]{:S(2)}) collective-permute-start(bf16[256,512]{1,0:T(8,128)(2,1)S(1)} %collective-permute-done.15.refs_0_), channel_id=1, source_target_pairs={{0,4},{1,5},{2,6},{3,7},{4,0},{5,1},{6,2},{7,3},{8,12},{9,13},{10,... | collective-permute-start | bytes 786440 | tf_op jit(solution)/shard_map/ppermute | solution.py:90
  33.5 9.1 %collective-permute-start.16 = (bf16[256,512]{1,0:T(8,128)(2,1)S(1)}, bf16[256,512]{1,0:T(8,128)(2,1)S(1)}, u32[]{:S(2)}, u32[]{:S(2)}) collective-permute-start(bf16[256,512]{1,0:T(8,128)(2,1)S(1)} %collective-permute-done.15.refs_0_), channel_id=1, source_target_pairs={{0,8},{1,9},{2,10},{3,11},{4,12},{5,13},{6,14},{7,15},{8,0},{9,1},... | collective-permute-start | bytes 786440 | tf_op jit(solution)/shard_map/ppermute | solution.py:90
  34.9 10.7 %collective-permute-start.12 = (bf16[256,512]{1,0:T(8,128)(2,1)S(1)}, bf16[256,512]{1,0:T(8,128)(2,1)S(1)}, u32[]{:S(2)}, u32[]{:S(2)}) collective-permute-start(bf16[256,512]{1,0:T(8,128)(2,1)S(1)} %collective-permute-done.1.refs_5_), channel_id=1, source_target_pairs={{0,4},{1,5},{2,6},{3,7},{4,0},{5,1},{6,2},{7,3},{8,12},{9,13},{10,... | collective-permute-start | bytes 786440 | tf_op jit(solution)/shard_map/ppermute | solution.py:90
  35.8 11.3 %collective-permute-start.11 = (bf16[256,512]{1,0:T(8,128)(2,1)S(1)}, bf16[256,512]{1,0:T(8,128)(2,1)S(1)}, u32[]{:S(2)}, u32[]{:S(2)}) collective-permute-start(bf16[256,512]{1,0:T(8,128)(2,1)S(1)} %collective-permute-done.1.refs_5_), channel_id=1, source_target_pairs={{0,2},{1,3},{2,0},{3,1},{4,6},{5,7},{6,4},{7,5},{8,10},{9,11},{10,... | collective-permute-start | bytes 786440 | tf_op jit(solution)/shard_map/ppermute | solution.py:90
  41.2 8.3 %collective-permute-start.20 = (bf16[256,512]{1,0:T(8,128)(2,1)S(1)}, bf16[256,512]{1,0:T(8,128)(2,1)S(1)}, u32[]{:S(2)}, u32[]{:S(2)}) collective-permute-start(bf16[256,512]{1,0:T(8,128)(2,1)S(1)} %collective-permute-done.15.refs_0_), channel_id=1, source_target_pairs={{0,2},{1,3},{2,0},{3,1},{4,6},{5,7},{6,4},{7,5},{8,10},{9,11},{10,... | collective-permute-start | bytes 786440 | tf_op jit(solution)/shard_map/ppermute | solution.py:90
  42.7 10.2 %collective-permute-start.19 = (bf16[128,1024]{1,0:T(8,128)(2,1)S(1)}, bf16[128,1024]{1,0:T(8,128)(2,1)S(1)}, u32[]{:S(2)}, u32[]{:S(2)}) collective-permute-start(bf16[128,1024]{1,0:T(8,128)(2,1)S(1)} %get-tuple-element.26), channel_id=1, source_target_pairs={{0,24},{1,25},{2,26},{3,27},{4,28},{5,29},{6,30},{7,31},{8,16},{9,... | collective-permute-start | bytes 786440 | tf_op jit(solution)/shard_map/ppermute | solution.py:90
  45.6 16.7 %collective-permute-start.25 = (bf16[256,512]{1,0:T(8,128)(2,1)S(1)}, bf16[256,512]{1,0:T(8,128)(2,1)S(1)}, u32[]{:S(2)}, u32[]{:S(2)}) collective-permute-start(bf16[256,512]{1,0:T(8,128)(2,1)S(1)} %collective-permute-done.16.refs_5_), channel_id=1, source_target_pairs={{0,4},{1,5},{2,6},{3,7},{4,0},{5,1},{6,2},{7,3},{8,12},{9,13},{10,... | collective-permute-start | bytes 786440 | tf_op jit(solution)/shard_map/ppermute | solution.py:90
  47.1 16.0 %collective-permute-start.24 = (bf16[256,512]{1,0:T(8,128)(2,1)S(1)}, bf16[256,512]{1,0:T(8,128)(2,1)S(1)}, u32[]{:S(2)}, u32[]{:S(2)}) collective-permute-start(bf16[256,512]{1,0:T(8,128)(2,1)S(1)} %collective-permute-done.16.refs_5_), channel_id=1, source_target_pairs={{0,2},{1,3},{2,0},{3,1},{4,6},{5,7},{6,4},{7,5},{8,10},{9,11},{10,... | collective-permute-start | bytes 786440 | tf_op jit(solution)/shard_map/ppermute | solution.py:90
  49.5 17.3 %collective-permute-start.18 = (bf16[128,1024]{1,0:T(8,128)(2,1)S(1)}, bf16[128,1024]{1,0:T(8,128)(2,1)S(1)}, u32[]{:S(2)}, u32[]{:S(2)}) collective-permute-start(bf16[128,1024]{1,0:T(8,128)(2,1)S(1)} %get-tuple-element.27), channel_id=1, source_target_pairs={{0,16},{1,17},{2,18},{3,19},{4,20},{5,21},{6,22},{7,23},{8,24},{9,... | collective-permute-start | bytes 786440 | tf_op jit(solution)/shard_map/ppermute | solution.py:90
  52.9 11.4 %copy-start.1 = (bf16[128,1024]{1,0:T(8,128)(2,1)}, bf16[128,1024]{1,0:T(8,128)(2,1)S(1)}, u32[]{:S(2)}) copy-start(bf16[128,1024]{1,0:T(8,128)(2,1)S(1)} %collective-permute-done.19.refs_2_) | copy-start | bytes 786436
  52.9 19.4 %collective-permute-start.17 = (bf16[128,1024]{1,0:T(8,128)(2,1)S(1)}, bf16[128,1024]{1,0:T(8,128)(2,1)S(1)}, u32[]{:S(2)}, u32[]{:S(2)}) collective-permute-start(bf16[128,1024]{1,0:T(8,128)(2,1)S(1)} %constant_dynamic-slice_fusion.2), channel_id=1, source_target_pairs={{0,8},{1,9},{2,10},{3,11},{4,12},{5,13},{6,14},{7,15},{8,0},{9,1},... | collective-permute-start | bytes 786440 | tf_op jit(solution)/shard_map/ppermute | solution.py:90
  62.3 5.0 %collective-permute-start.13 = (bf16[128,512]{1,0:T(8,128)(2,1)S(1)}, bf16[128,512]{1,0:T(8,128)(2,1)S(1)}, u32[]{:S(2)}, u32[]{:S(2)}) collective-permute-start(bf16[128,512]{1,0:T(8,128)(2,1)S(1)} %slice.39), channel_id=1, source_target_pairs={{0,2},{1,3},{2,0},{3,1},{4,6},{5,7},{6,4},{7,5},{8,10},{9,11},{10,... | collective-permute-start | bytes 393224 | tf_op jit(solution)/shard_map/ppermute | solution.py:90
  63.1 5.1 %collective-permute-start.14 = (bf16[128,512]{1,0:T(8,128)(2,1)S(1)}, bf16[128,512]{1,0:T(8,128)(2,1)S(1)}, u32[]{:S(2)}, u32[]{:S(2)}) collective-permute-start(bf16[128,512]{1,0:T(8,128)(2,1)S(1)} %slice.40), channel_id=1, source_target_pairs={{0,4},{1,5},{2,6},{3,7},{4,0},{5,1},{6,2},{7,3},{8,12},{9,13},{10,... | collective-permute-start | bytes 393224 | tf_op jit(solution)/shard_map/ppermute | solution.py:90
  66.8 11.1 %copy-start.3 = (bf16[128,1024]{1,0:T(8,128)(2,1)}, bf16[128,1024]{1,0:T(8,128)(2,1)S(1)}, u32[]{:S(2)}) copy-start(bf16[128,1024]{1,0:T(8,128)(2,1)S(1)} %collective-permute-done.18.refs_1_) | copy-start | bytes 786436
  66.8 11.1 %collective-permute-start.6 = (bf16[128,512]{1,0:T(8,128)(2,1)S(1)}, bf16[128,512]{1,0:T(8,128)(2,1)S(1)}, u32[]{:S(2)}, u32[]{:S(2)}) collective-permute-start(bf16[128,512]{1,0:T(8,128)(2,1)S(1)} %get-tuple-element.28), channel_id=1, source_target_pairs={{0,1},{1,0},{2,3},{3,2},{4,5},{5,4},{6,7},{7,6},{8,9},{9,8},{10,11... | collective-permute-start | bytes 393224 | tf_op jit(solution)/shard_map/ppermute | solution.py:90
  67.2 10.7 %collective-permute-start.22 = (bf16[128,512]{1,0:T(8,128)(2,1)S(1)}, bf16[128,512]{1,0:T(8,128)(2,1)S(1)}, u32[]{:S(2)}, u32[]{:S(2)}) collective-permute-start(bf16[128,512]{1,0:T(8,128)(2,1)S(1)} %slice.41), channel_id=1, source_target_pairs={{0,2},{1,3},{2,0},{3,1},{4,6},{5,7},{6,4},{7,5},{8,10},{9,11},{10,... | collective-permute-start | bytes 393224 | tf_op jit(solution)/shard_map/ppermute | solution.py:90
  68.1 9.9 %collective-permute-start.23 = (bf16[128,512]{1,0:T(8,128)(2,1)S(1)}, bf16[128,512]{1,0:T(8,128)(2,1)S(1)}, u32[]{:S(2)}, u32[]{:S(2)}) collective-permute-start(bf16[128,512]{1,0:T(8,128)(2,1)S(1)} %slice.42), channel_id=1, source_target_pairs={{0,4},{1,5},{2,6},{3,7},{4,0},{5,1},{6,2},{7,3},{8,12},{9,13},{10,... | collective-permute-start | bytes 393224 | tf_op jit(solution)/shard_map/ppermute | solution.py:90
  72.3 5.6 %copy-start.5 = (bf16[128,1024]{1,0:T(8,128)(2,1)}, bf16[128,1024]{1,0:T(8,128)(2,1)S(1)}, u32[]{:S(2)}) copy-start(bf16[128,1024]{1,0:T(8,128)(2,1)S(1)} %collective-permute-done.17.refs_0_) | copy-start | bytes 786436
  72.3 5.6 %collective-permute-start.26 = (bf16[128,512]{1,0:T(8,128)(2,1)S(1)}, bf16[128,512]{1,0:T(8,128)(2,1)S(1)}, u32[]{:S(2)}, u32[]{:S(2)}) collective-permute-start(bf16[128,512]{1,0:T(8,128)(2,1)S(1)} %slice.43), channel_id=1, source_target_pairs={{0,2},{1,3},{2,0},{3,1},{4,6},{5,7},{6,4},{7,5},{8,10},{9,11},{10,... | collective-permute-start | bytes 393224 | tf_op jit(solution)/shard_map/ppermute | solution.py:90
  73.5 5.2 %collective-permute-start.27 = (bf16[128,512]{1,0:T(8,128)(2,1)S(1)}, bf16[128,512]{1,0:T(8,128)(2,1)S(1)}, u32[]{:S(2)}, u32[]{:S(2)}) collective-permute-start(bf16[128,512]{1,0:T(8,128)(2,1)S(1)} %slice.44), channel_id=1, source_target_pairs={{0,4},{1,5},{2,6},{3,7},{4,0},{5,1},{6,2},{7,3},{8,12},{9,13},{10,... | collective-permute-start | bytes 393224 | tf_op jit(solution)/shard_map/ppermute | solution.py:90
  81.2 29.9 %copy-start.2 = (bf16[128,1024]{1,0:T(8,128)(2,1)S(1)}, bf16[128,1024]{1,0:T(8,128)(2,1)}, u32[]{:S(2)}) copy-start(bf16[128,1024]{1,0:T(8,128)(2,1)} %copy-done.1) | copy-start | bytes 786436
  81.3 30.3 %copy-start.4 = (bf16[128,1024]{1,0:T(8,128)(2,1)S(1)}, bf16[128,1024]{1,0:T(8,128)(2,1)}, u32[]{:S(2)}) copy-start(bf16[128,1024]{1,0:T(8,128)(2,1)} %copy-done.3) | copy-start | bytes 786436
  81.3 30.4 %copy-start.6 = (bf16[128,1024]{1,0:T(8,128)(2,1)S(1)}, bf16[128,1024]{1,0:T(8,128)(2,1)}, u32[]{:S(2)}) copy-start(bf16[128,1024]{1,0:T(8,128)(2,1)} %copy-done.5) | copy-start | bytes 786436
  81.3 43.4 %collective-permute-start.32 = (bf16[2048,512]{1,0:T(8,128)(2,1)}, bf16[2048,512]{1,0:T(8,128)(2,1)}, u32[]{:S(2)}, u32[]{:S(2)}) collective-permute-start(bf16[2048,512]{1,0:T(8,128)(2,1)} %get-tuple-element.23.refs_2_), channel_id=1, source_target_pairs={{0,1},{1,0},{2,3},{3,2},{4,5},{5,4},{6,7},{7,6},{8,9},{9,8},{10,11... | collective-permute-start | bytes 6291464 | tf_op jit(solution)/shard_map/ppermute | solution.py:90
  81.3 43.4 %collective-permute-start.31 = (bf16[2048,512]{1,0:T(8,128)(2,1)}, bf16[2048,512]{1,0:T(8,128)(2,1)}, u32[]{:S(2)}, u32[]{:S(2)}) collective-permute-start(bf16[2048,512]{1,0:T(8,128)(2,1)} %get-tuple-element.22.refs_0_), channel_id=1, source_target_pairs={{0,1},{1,0},{2,3},{3,2},{4,5},{5,4},{6,7},{7,6},{8,9},{9,8},{10,11... | collective-permute-start | bytes 6291464 | tf_op jit(solution)/shard_map/ppermute | solution.py:90
  81.8 14.9 %collective-permute-start.28 = (bf16[256,512]{1,0:T(8,128)(2,1)S(1)}, bf16[256,512]{1,0:T(8,128)(2,1)S(1)}, u32[]{:S(2)}, u32[]{:S(2)}) collective-permute-start(bf16[256,512]{1,0:T(8,128)(2,1)S(1)} %get-tuple-element.24.refs_0_.refs_6_), channel_id=1, source_target_pairs={{0,16},{1,17},{2,18},{3,19},{4,20},{5,21},{6,22},{7,23},{8,24},{9,... | collective-permute-start | bytes 786440 | tf_op jit(solution)/shard_map/ppermute | solution.py:90
  82.5 14.3 %collective-permute-start.29 = (bf16[256,512]{1,0:T(8,128)(2,1)S(1)}, bf16[256,512]{1,0:T(8,128)(2,1)S(1)}, u32[]{:S(2)}, u32[]{:S(2)}) collective-permute-start(bf16[256,512]{1,0:T(8,128)(2,1)S(1)} %get-tuple-element.24.refs_0_.refs_6_), channel_id=1, source_target_pairs={{0,8},{1,9},{2,10},{3,11},{4,12},{5,13},{6,14},{7,15},{8,0},{9,1},... | collective-permute-start | bytes 786440 | tf_op jit(solution)/shard_map/ppermute | solution.py:90
  96.7 10.2 %copy-start.9 = (bf16[256,512]{1,0:T(8,128)(2,1)}, bf16[256,512]{1,0:T(8,128)(2,1)S(1)}, u32[]{:S(2)}) copy-start(bf16[256,512]{1,0:T(8,128)(2,1)S(1)} %collective-permute-done.28.refs_1_.refs_8_) | copy-start | bytes 786436
  96.7 8.2 %collective-permute-start.30 = (bf16[256,512]{1,0:T(8,128)(2,1)S(1)}, bf16[256,512]{1,0:T(8,128)(2,1)S(1)}, u32[]{:S(2)}, u32[]{:S(2)}) collective-permute-start(bf16[256,512]{1,0:T(8,128)(2,1)S(1)} %collective-permute-done.28.refs_1_.refs_8_), channel_id=1, source_target_pairs={{0,8},{1,9},{2,10},{3,11},{4,12},{5,13},{6,14},{7,15},{8,0},{9,1},... | collective-permute-start | bytes 786440 | tf_op jit(solution)/shard_map/ppermute | solution.py:90
  96.8 10.1 %copy-start.11 = (bf16[256,512]{1,0:T(8,128)(2,1)}, bf16[256,512]{1,0:T(8,128)(2,1)S(1)}, u32[]{:S(2)}) copy-start(bf16[256,512]{1,0:T(8,128)(2,1)S(1)} %collective-permute-done.29.refs_2_.refs_7_) | copy-start | bytes 786436
  107.6 13.2 %all-to-all-start = ((bf16[8,64,512]{2,1,0:T(8,128)(2,1)}), bf16[8,64,512]{2,1,0:T(8,128)(2,1)S(1)}, u32[]{:S(2)}, u32[]{:S(2)}) async-start(bf16[8,64,512]{2,1,0:T(8,128)(2,1)} %bitcast.6), calls=%async_computation | async-start | bytes 1048576 | tf_op jit(solution)/shard_map/all_to_all | solution.py:374
  111.1 1.6 %collective-permute-start.35 = (bf16[128,1024]{1,0:T(8,128)(2,1)S(1)}, bf16[128,1024]{1,0:T(8,128)(2,1)S(1)}, u32[]{:S(2)}, u32[]{:S(2)}) collective-permute-start(bf16[128,1024]{1,0:T(8,128)(2,1)S(1)} %copy-done.2), channel_id=1, source_target_pairs={{0,1},{1,0},{2,3},{3,2},{4,5},{5,4},{6,7},{7,6},{8,9},{9,8},{10,11... | collective-permute-start | bytes 786440 | tf_op jit(solution)/shard_map/ppermute | solution.py:90
  111.5 1.6 %collective-permute-start.34 = (bf16[128,1024]{1,0:T(8,128)(2,1)S(1)}, bf16[128,1024]{1,0:T(8,128)(2,1)S(1)}, u32[]{:S(2)}, u32[]{:S(2)}) collective-permute-start(bf16[128,1024]{1,0:T(8,128)(2,1)S(1)} %copy-done.4), channel_id=1, source_target_pairs={{0,1},{1,0},{2,3},{3,2},{4,5},{5,4},{6,7},{7,6},{8,9},{9,8},{10,11... | collective-permute-start | bytes 786440 | tf_op jit(solution)/shard_map/ppermute | solution.py:90
  111.7 1.8 %collective-permute-start.33 = (bf16[128,1024]{1,0:T(8,128)(2,1)S(1)}, bf16[128,1024]{1,0:T(8,128)(2,1)S(1)}, u32[]{:S(2)}, u32[]{:S(2)}) collective-permute-start(bf16[128,1024]{1,0:T(8,128)(2,1)S(1)} %copy-done.6), channel_id=1, source_target_pairs={{0,1},{1,0},{2,3},{3,2},{4,5},{5,4},{6,7},{7,6},{8,9},{9,8},{10,11... | collective-permute-start | bytes 786440 | tf_op jit(solution)/shard_map/ppermute | solution.py:90
  120.8 19.3 %all-to-all-start.1 = ((bf16[8,128,512]{2,1,0:T(8,128)(2,1)}), bf16[8,128,512]{2,1,0:T(8,128)(2,1)S(1)}, u32[]{:S(2)}, u32[]{:S(2)}) async-start(bf16[8,128,512]{2,1,0:T(8,128)(2,1)} %bitcast.8), calls=%async_computation.1 | async-start | bytes 2097152 | tf_op jit(solution)/shard_map/all_to_all | solution.py:374
  (6 other events, 6.6 us)

commit v5 on v4

--- a/solution.py
+++ b/solution.py
@@ -108,22 +108,18 @@
     return column
 
 
-def gather_planes(column, masks):
-    arrays, places = [], []
-
-    def add(mask, first, array):
-        places.append((mask, first, len(arrays), 0, array.shape[0]))
-        arrays.append(array)
-
-    half = column[masks[0]].shape[0] // 2
-    for mask in masks:
-        by_x, by_y = swap(column[mask], X), swap(column[mask], Y)
-        add(mask, 0, column[mask])
-        add(mask | X, 0, by_x)
-        add(mask | Y, 0, by_y)
-        add(mask | X | Y, 0, swap(by_y[:half], X))
-        add(mask | X | Y, half, swap(by_x[half:], Y))
-    return arrays, places
+class Places:
+    def __init__(self):
+        self.arrays, self.places = [], []
+
+    def add(self, mask, first, array):
+        self.places.append((mask, first, len(self.arrays), 0, array.shape[0]))
+        self.arrays.append(array)
+
+
+def diagonal(by_x, by_y):
+    half = by_x.shape[0] // 2
+    return swap(by_y[:half], X), swap(by_x[half:], Y)
 
 
 def dot(a, b, dims):
@@ -197,18 +193,15 @@
 
 
 def weight_grad_kernel(count, me_ref, own_ref, mate_ref, *refs):
-    own, mate, deltas = refs[: count - 1], refs[count - 1 : 2 * count - 2], refs[2 * count - 2 : -2]
-    part_ref, acc = refs[-2:]
+    part_ref, acc = refs[count:]
     me = me_ref[0]
     core = me & 1
-    rows = own_ref.shape[0]
-    wide = part_ref.shape[0]
-    here = pl.ds(pl.multiple_of((me // PLANE) * wide, wide), wide)
+    rows = own_ref.shape[1]
     for n in range(count):
-        for side, (whole, parts) in enumerate(((own_ref, own), (mate_ref, mate))):
+        level = lax.shift_right_logical(me, 3) ^ n
+        for side, ref in enumerate((own_ref, mate_ref)):
             at = pl.multiple_of((core ^ side) * rows, rows)
-            hidden = whole[:, here] if n == 0 else parts[n - 1][...]
-            part = dot(hidden, deltas[n][pl.ds(at, rows), :], ((0,), (0,)))
+            part = dot(ref[level], refs[n][pl.ds(at, rows), :], ((0,), (0,)))
             if n == 0 and side == 0:
                 acc[...] = part
             else:
@@ -282,28 +275,61 @@
     def theirs(value):
         return lax.dynamic_slice_in_dim(value, (1 - core) * half_cols, half_cols, 1)
 
-    own_weight, mate_weight = mine(key_weight), swap(theirs(key_weight), CORE)
+    mate_shard = swap(key_weight, CORE)
     piece = jnp.where(
         core == 0,
-        jnp.concatenate([own_weight, mate_weight], axis=0),
-        jnp.concatenate([mate_weight, own_weight], axis=0),
-    )
-    column = gather_column(piece)
+        jnp.concatenate([key_weight[:, :half_cols], mate_shard[:, :half_cols]], axis=0),
+        jnp.concatenate([mate_shard[:, half_cols:], key_weight[:, half_cols:]], axis=0),
+    )
+    bits = [PLANE << n for n in range(levels.bit_length() - 1)]
+    column = {0: piece}
+    for bit in bits:
+        column[bit] = swap(piece, bit)
+    by_x, by_y = swap(piece, X), swap(piece, Y)
+    across = diagonal(by_x, by_y)
+    planes_of = {0: (by_x, by_y, *across)}
+    arrived = lax.optimization_barrier([column[bit] for bit in bits])
+    column.update(zip(bits, arrived))
+    waits = {bits[0]: (by_x, by_y), bits[-1]: across}
+    for mask in [PLANE * n for n in range(1, levels)]:
+        if mask not in column:
+            low = mask & -mask
+            column[mask] = swap(column[mask ^ low], low)
+    order = bits + [PLANE * n for n in range(1, levels) if PLANE * n not in bits]
+    for n, mask in enumerate(order):
+        before = waits[mask] if mask in waits else planes_of[order[n - 2]][:2]
+        own = after(column[mask], *before)
+        by_x, by_y = swap(own, X), swap(own, Y)
+        planes_of[mask] = (by_x, by_y, *diagonal(by_x, by_y))
     masks = sorted(column)
     parts_of = [masks[: levels // 2], masks[levels // 2 :]]
-    sets = [gather_planes(column, part) for part in parts_of]
-
-    mate_tokens = swap(tokens, CORE)
-    far_tokens = after(tokens, sets[0][0][3], sets[0][0][4])
-    near_tokens = after(tokens, column[masks[-1]])
-    own_features = []
-    for mask in masks[1:]:
-        there = lax.shift_right_logical(me ^ mask, 3)
-        source = near_tokens if mask == PLANE else far_tokens
-        own_features.append(swap(lax.dynamic_slice_in_dim(source, there * wide, wide, 1), mask))
-    mate_features = [swap(value, CORE) for value in own_features]
-
-    key_cot, routes, counts = lax.optimization_barrier((key_cot, routes, counts, column[PLANE]))[:3]
+    sets = []
+    for part in parts_of:
+        found = Places()
+        for mask in part:
+            by_x, by_y, first, last = planes_of[mask]
+            found.add(mask, 0, column[mask])
+            found.add(mask | X, 0, by_x)
+            found.add(mask | Y, 0, by_y)
+            found.add(mask | X | Y, 0, first)
+            found.add(mask | X | Y, first.shape[0], last)
+        sets.append((found.arrays, found.places))
+
+    mate_tokens = swap(after(tokens, *arrived), CORE)
+    columns = [[p + PLANE * z for z in range(levels)] for p in range(PLANE)]
+    late_tokens = after(tokens, *arrived)
+    own_features = lax.all_to_all(
+        jnp.stack([late_tokens[:, z * wide : (z + 1) * wide] for z in range(levels)]),
+        "dp",
+        split_axis=0,
+        concat_axis=0,
+        axis_index_groups=columns,
+        tiled=True,
+    )
+    mate_features = swap(own_features, CORE)
+
+    key_cot, counts = lax.optimization_barrier((key_cot, counts, *planes_of[bits[-1]][:2]))[:2]
+    routes = after(routes, *planes_of[bits[0]][:2])
     bounds = jnp.cumsum(counts[0])
     positions = jnp.arange(rows, dtype=jnp.int32)
     subnet = jnp.sum((positions[:, None] >= bounds[None, : NSUB - 1]).astype(jnp.int32), axis=1)
@@ -329,7 +355,7 @@
         jnp.concatenate([mate_code, code], axis=0),
     )
     order = [0]
-    for bit in reversed([PLANE << n for n in range(levels.bit_length() - 1)]):
+    for bit in reversed(bits):
         codes = jnp.concatenate([codes, swap(codes, bit)], axis=0)
         order += [mask | bit for mask in order]
 
@@ -346,7 +372,7 @@
         name="project",
     )(me_scalar, tokens, mate_tokens, *arrays)
     arrays, places = sets[1]
-    begun = after(begun, codes, *own_features)
+    begun = after(begun, codes, own_features, mate_features)
     delta, last_weight = pl.pallas_call(
         functools.partial(delta_kernel, places, len(arrays)),
         out_shape=(jax.ShapeDtypeStruct((2 * rows, half_cols), jnp.bfloat16), kept),
@@ -386,7 +412,7 @@
     part = pl.pallas_call(
         functools.partial(weight_grad_kernel, levels),
         out_shape=jax.ShapeDtypeStruct((wide, half_cols), jnp.bfloat16),
-        in_specs=[SCALAR] + vmem(2 + 2 * (levels - 1) + levels),
+        in_specs=[SCALAR] + vmem(2 + levels),
         out_specs=vmem(1)[0],
         scratch_shapes=[pltpu.VMEM((wide, half_cols), jnp.float32)],
         compiler_params=PARAMS,
@@ -394,10 +420,8 @@
         name="weight_grad",
     )(
         me_scalar,
-        tokens,
-        mate_tokens,
-        *own_features,
-        *mate_features,
+        own_features,
+        mate_features,
         *[ready if mask == 0 else deltas[mask] for mask in masks],
     )
     shard = width_model // size

time: 142 us -> 144 us (1.014)
  starting transfers between devices: 57.6 us -> 45.3 us
  waiting for transfers between devices: 48.6 us -> 57 us
  local copies, waits for them, and re-layouts: 8.81 us -> 13.1 us
  Pallas kernels: 20.5 us -> 22.7 us
    ppermute x36 -> x31, starting transfers between devices: 50.3 us -> 33.8 us  [swap(): return lax.ppermute(value, 'dp', [(i, i ^ mask) for i in range(size)])]
    slice x8 -> x10, local copies, waits for them, and re-layouts: 1.39 us -> 7.82 us  [the longest x8 6.81 us: diagonal(): return (swap(by_y[:half], X), swap(by_x[half:], Y))]
    all_to_all x0 -> x1, starting transfers between devices: none -> 4.41 us  [per_device_paired(): lax.all_to_all(jnp.stack([late_tokens[:, z * wide:(z + 1) * wide] for z i...]
    all_to_all x0 -> x1, waiting for transfers between devices: none -> 3.02 us  [per_device_paired(): lax.all_to_all(jnp.stack([late_tokens[:, z * wide:(z + 1) * wide] for z i...]
    ppermute x36 -> x31, waiting for transfers between devices: 41.8 us -> 44.5 us  [swap(): return lax.ppermute(value, 'dp', [(i, i ^ mask) for i in range(size)])]
    all_to_all x2, waiting for transfers between devices: 6.77 us -> 9.44 us  [to_plane(): lax.all_to_all(value.reshape(PLANE, -1, half_cols), 'dp', split_axis=0, c...]
    dynamic_slice x3 -> x0, local copies, waits for them, and re-layouts: 2.16 us -> none  [the longest x2 1.09 us: per_device_paired(): lax.dynamic_slice_in_dim(source, there * wide, wide, 1)]
    unnamed x32 -> x34, local copies, waits for them, and re-layouts: 4.56 us -> 4.53 us
  transfers between devices with their start and end apart: 38 -> 34, of which waited for: 17 -> 18; matrix products, arithmetic and copies ran while one was open for 5% -> 8% of each run, Pallas kernels for 12% -> 15%
where the time goes in v5:
time: 144 us
  waiting for transfers between devices  57 us (40%)
  starting transfers between devices  45.3 us (31%)
  Pallas kernels  22.7 us (16%)
  local copies, waits for them, and re-layouts  13.1 us (9%)
  other arithmetic  4.53 us (3%)
    ppermute x31, waiting for transfers between devices, swap(): return lax.ppermute(value, 'dp', [(i, i ^ mask) for i in range(size)])  44.5 us
    ppermute x31, starting transfers between devices, swap(): return lax.ppermute(value, 'dp', [(i, i ^ mask) for i in range(size)])  33.8 us
    all_to_all x2, waiting for transfers between devices, to_plane(): lax.all_to_all(value.reshape(PLANE, -1, half_cols), 'dp', split_axis=0, c...  9.44 us
    pallas_call x1, Pallas kernels, per_device_paired(): pl.pallas_call(functools.partial(row_grad_kernel, [part[0] for part in pa...  8.4 us
    all_to_all x2, starting transfers between devices, to_plane(): lax.all_to_all(value.reshape(PLANE, -1, half_cols), 'dp', split_axis=0, c...  7.05 us
    slice x8, local copies, waits for them, and re-layouts, diagonal(): return (swap(by_y[:half], X), swap(by_x[half:], Y))  6.81 us
    pallas_call x1, Pallas kernels, per_device_paired(): pl.pallas_call(functools.partial(weight_grad_kernel, levels), out_shape=j...  4.61 us
    unnamed x34, local copies, waits for them, and re-layouts  4.53 us
  transfers between devices with their start and end apart: 34, of which 18 were waited for; matrix products, arithmetic and copies ran while one was open for 8% of the time, Pallas kernels for 15%

profile of v5, /device:TPU:0, one launch (start us, length us, event | category | flops | bytes accessed | tf_op | source)
XLA Modules:
  0.0 143.6 jit_solution(6140946071016828505)
XLA Ops:
  1.2 1.0 fusion.5
  2.6 4.0 %collective-permute-start.2 = (bf16[256,512]{1,0:T(8,128)(2,1)S(1)}, bf16[256,512]{1,0:T(8,128)(2,1)S(1)}, u32[]{:S(2)}, u32[]{:S(2)}) collective-permute-start(bf16[256,512]{1,0:T(8,128)(2,1)S(1)} %maximum_select_fusion.refs_0_), channel_id=1, source_target_pairs={{0,16},{1,17},{2,18},{3,19},{4,20},{5,21},{6,22},{7,23},{8,24},{9,... | collective-permute-start | bytes 786440 | tf_op jit(solution)/shard_map/ppermute | solution.py:90
  6.6 1.6 %collective-permute-start.1 = (bf16[256,512]{1,0:T(8,128)(2,1)S(1)}, bf16[256,512]{1,0:T(8,128)(2,1)}, u32[]{:S(2)}, u32[]{:S(2)}) collective-permute-start(bf16[256,512]{1,0:T(8,128)(2,1)S(1)} %maximum_select_fusion.refs_0_), channel_id=1, source_target_pairs={{0,8},{1,9},{2,10},{3,11},{4,12},{5,13},{6,14},{7,15},{8,0},{9,1},... | collective-permute-start | bytes 786440 | tf_op jit(solution)/shard_map/ppermute | solution.py:90
  8.2 10.8 %collective-permute-done.2.refs_0_ = bf16[256,512]{1,0:T(8,128)(2,1)S(1)} collective-permute-done((bf16[256,512]{1,0:T(8,128)(2,1)S(1)}, bf16[256,512]{1,0:T(8,128)(2,1)S(1)}, u32[]{:S(2)}, u32[]{:S(2)}) %collective-permute-start.2) | collective-permute-done | bytes 262176 | tf_op jit(solution)/shard_map/ppermute | solution.py:90
  19.4 1.1 pad_maximum_fusion
  20.5 4.4 %all-to-all-start = ((bf16[4,128,1024]{2,1,0:T(8,128)(2,1)}), bf16[4,128,1024]{2,1,0:T(8,128)(2,1)S(1)}, u32[]{:S(2)}, u32[]{:S(2)}) async-start(bf16[4,128,1024]{2,1,0:T(8,128)(2,1)} %pad_maximum_fusion), calls=%async_computation | async-start | bytes 2097152 | tf_op jit(solution)/shard_map/all_to_all | solution.py:321
  24.9 1.5 %collective-permute-start.4 = (bf16[256,512]{1,0:T(8,128)(2,1)S(1)}, bf16[256,512]{1,0:T(8,128)(2,1)S(1)}, u32[]{:S(2)}, u32[]{:S(2)}) collective-permute-start(bf16[256,512]{1,0:T(8,128)(2,1)S(1)} %maximum_select_fusion.refs_0_), channel_id=1, source_target_pairs={{0,4},{1,5},{2,6},{3,7},{4,0},{5,1},{6,2},{7,3},{8,12},{9,13},{10,... | collective-permute-start | bytes 786440 | tf_op jit(solution)/shard_map/ppermute | solution.py:90
  26.4 1.5 %collective-permute-start.3 = (bf16[256,512]{1,0:T(8,128)(2,1)S(1)}, bf16[256,512]{1,0:T(8,128)(2,1)S(1)}, u32[]{:S(2)}, u32[]{:S(2)}) collective-permute-start(bf16[256,512]{1,0:T(8,128)(2,1)S(1)} %maximum_select_fusion.refs_0_), channel_id=1, source_target_pairs={{0,2},{1,3},{2,0},{3,1},{4,6},{5,7},{6,4},{7,5},{8,10},{9,11},{10,... | collective-permute-start | bytes 786440 | tf_op jit(solution)/shard_map/ppermute | solution.py:90
  27.9 5.0 %collective-permute-done.4.refs_2_ = bf16[256,512]{1,0:T(8,128)(2,1)S(1)} collective-permute-done((bf16[256,512]{1,0:T(8,128)(2,1)S(1)}, bf16[256,512]{1,0:T(8,128)(2,1)S(1)}, u32[]{:S(2)}, u32[]{:S(2)}) %collective-permute-start.4) | collective-permute-done | bytes 262176 | tf_op jit(solution)/shard_map/ppermute | solution.py:90
  32.9 1.2 collective-permute-done.3.refs_1_
  34.6 1.5 %collective-permute-start.5 = (bf16[256,512]{1,0:T(8,128)(2,1)}, bf16[256,512]{1,0:T(8,128)(2,1)S(1)}, u32[]{:S(2)}, u32[]{:S(2)}) collective-permute-start(bf16[256,512]{1,0:T(8,128)(2,1)} %collective-permute-done.1.refs_5_), channel_id=1, source_target_pairs={{0,2},{1,3},{2,0},{3,1},{4,6},{5,7},{6,4},{7,5},{8,10},{9,11},{10,... | collective-permute-start | bytes 786440 | tf_op jit(solution)/shard_map/ppermute | solution.py:90
  36.1 1.7 %collective-permute-start.21 = (bf16[256,512]{1,0:T(8,128)(2,1)}, bf16[256,512]{1,0:T(8,128)(2,1)}, u32[]{:S(2)}, u32[]{:S(2)}) collective-permute-start(bf16[256,512]{1,0:T(8,128)(2,1)} %copy-done.10), channel_id=1, source_target_pairs={{0,8},{1,9},{2,10},{3,11},{4,12},{5,13},{6,14},{7,15},{8,0},{9,1},... | collective-permute-start | bytes 786440 | tf_op jit(solution)/shard_map/ppermute | solution.py:90
  38.5 1.6 %collective-permute-start.12 = (bf16[128,512]{1,0:T(8,128)(2,1)S(1)}, bf16[128,512]{1,0:T(8,128)(2,1)S(1)}, u32[]{:S(2)}, u32[]{:S(2)}) collective-permute-start(bf16[128,512]{1,0:T(8,128)(2,1)S(1)} %slice.72), channel_id=1, source_target_pairs={{0,4},{1,5},{2,6},{3,7},{4,0},{5,1},{6,2},{7,3},{8,12},{9,13},{10,... | collective-permute-start | bytes 393224 | tf_op jit(solution)/shard_map/ppermute | solution.py:90
  40.1 2.4 %collective-permute-done.6.refs_7_ = bf16[256,512]{1,0:T(8,128)(2,1)S(1)} collective-permute-done((bf16[256,512]{1,0:T(8,128)(2,1)}, bf16[256,512]{1,0:T(8,128)(2,1)S(1)}, u32[]{:S(2)}, u32[]{:S(2)}) %collective-permute-start.6) | collective-permute-done | bytes 262176 | tf_op jit(solution)/shard_map/ppermute | solution.py:90
  45.0 1.4 collective-permute-start.14
  46.3 1.5 %collective-permute-start.13 = (bf16[256,512]{1,0:T(8,128)(2,1)}, bf16[256,512]{1,0:T(8,128)(2,1)}, u32[]{:S(2)}, u32[]{:S(2)}) collective-permute-start(bf16[256,512]{1,0:T(8,128)(2,1)} %copy-done.10), channel_id=1, source_target_pairs={{0,2},{1,3},{2,0},{3,1},{4,6},{5,7},{6,4},{7,5},{8,10},{9,11},{10,... | collective-permute-start | bytes 786440 | tf_op jit(solution)/shard_map/ppermute | solution.py:90
  47.8 3.0 %all-to-all-done.own_ref = bf16[4,128,1024]{2,1,0:T(8,128)(2,1)S(1)} async-done(((bf16[4,128,1024]{2,1,0:T(8,128)(2,1)}), bf16[4,128,1024]{2,1,0:T(8,128)(2,1)S(1)}, u32[]{:S(2)}, u32[]{:S(2)}) %all-to-all-start) | async-done | bytes 1048608 | tf_op jit(solution)/shard_map/all_to_all | solution.py:321
  50.9 1.6 %collective-permute-start.8 = (s32[2,128]{1,0:T(2,128)S(1)}, s32[2,128]{1,0:T(2,128)S(1)}, u32[]{:S(2)}, u32[]{:S(2)}) collective-permute-start(s32[2,128]{1,0:T(2,128)S(1)} %add_select_fusion.1), channel_id=1, source_target_pairs={{0,16},{1,17},{2,18},{3,19},{4,20},{5,21},{6,22},{7,23},{8,24},{9,... | collective-permute-start | bytes 3080 | tf_op jit(solution)/shard_map/ppermute | solution.py:90
  52.5 1.6 %slice.73 = bf16[128,512]{1,0:T(8,128)(2,1)} slice(bf16[256,512]{1,0:T(8,128)(2,1)} %copy-done.6), slice={[0:128], [0:512]} | slice | bytes 262144 | tf_op jit(solution)/shard_map/slice | solution.py:122
  54.1 1.6 %slice.74 = bf16[128,512]{1,0:T(8,128)(2,1)} slice(bf16[256,512]{1,0:T(8,128)(2,1)} %copy-done.8), slice={[128:256], [0:512]} | slice | bytes 262144 | tf_op jit(solution)/shard_map/slice | solution.py:122
  55.6 1.5 %collective-permute-start.23 = (bf16[256,512]{1,0:T(8,128)(2,1)}, bf16[256,512]{1,0:T(8,128)(2,1)}, u32[]{:S(2)}, u32[]{:S(2)}) collective-permute-start(bf16[256,512]{1,0:T(8,128)(2,1)} %collective-permute-done.21.refs_5_), channel_id=1, source_target_pairs={{0,4},{1,5},{2,6},{3,7},{4,0},{5,1},{6,2},{7,3},{8,12},{9,13},{10,... | collective-permute-start | bytes 786440 | tf_op jit(solution)/shard_map/ppermute | solution.py:90
  57.2 1.6 %collective-permute-start.22 = (bf16[256,512]{1,0:T(8,128)(2,1)}, bf16[256,512]{1,0:T(8,128)(2,1)}, u32[]{:S(2)}, u32[]{:S(2)}) collective-permute-start(bf16[256,512]{1,0:T(8,128)(2,1)} %collective-permute-done.21.refs_5_), channel_id=1, source_target_pairs={{0,2},{1,3},{2,0},{3,1},{4,6},{5,7},{6,4},{7,5},{8,10},{9,11},{10,... | collective-permute-start | bytes 786440 | tf_op jit(solution)/shard_map/ppermute | solution.py:90
  59.3 1.3 reduce-window.4
  62.1 1.1 collective-permute-done.23.refs_7_
  63.3 1.5 %collective-permute-start.17 = (bf16[128,512]{1,0:T(8,128)(2,1)}, bf16[128,512]{1,0:T(8,128)(2,1)S(1)}, u32[]{:S(2)}, u32[]{:S(2)}) collective-permute-start(bf16[128,512]{1,0:T(8,128)(2,1)} %slice.74), channel_id=1, source_target_pairs={{0,4},{1,5},{2,6},{3,7},{4,0},{5,1},{6,2},{7,3},{8,12},{9,13},{10,... | collective-permute-start | bytes 393224 | tf_op jit(solution)/shard_map/ppermute | solution.py:90
  64.8 1.1 compare_select_fusion
  66.0 1.5 %collective-permute-start.9 = (s32[4,128]{1,0:T(4,128)S(1)}, s32[4,128]{1,0:T(4,128)S(1)}, u32[]{:S(2)}, u32[]{:S(2)}) collective-permute-start(s32[4,128]{1,0:T(4,128)S(1)} %pad_add_fusion.1), channel_id=1, source_target_pairs={{0,8},{1,9},{2,10},{3,11},{4,12},{5,13},{6,14},{7,15},{8,0},{9,1},... | collective-permute-start | bytes 6152 | tf_op jit(solution)/shard_map/ppermute | solution.py:90
  68.4 0.9 slice.76
  70.3 0.9 slice.78
  71.2 1.6 %collective-permute-start.19 = (bf16[128,512]{1,0:T(8,128)(2,1)S(1)}, bf16[128,512]{1,0:T(8,128)(2,1)S(1)}, u32[]{:S(2)}, u32[]{:S(2)}) collective-permute-start(bf16[128,512]{1,0:T(8,128)(2,1)S(1)} %slice.75), channel_id=1, source_target_pairs={{0,2},{1,3},{2,0},{3,1},{4,6},{5,7},{6,4},{7,5},{8,10},{9,11},{10,... | collective-permute-start | bytes 393224 | tf_op jit(solution)/shard_map/ppermute | solution.py:90
  73.9 1.5 %collective-permute-start.25 = (bf16[128,512]{1,0:T(8,128)(2,1)S(1)}, bf16[128,512]{1,0:T(8,128)(2,1)S(1)}, u32[]{:S(2)}, u32[]{:S(2)}) collective-permute-start(bf16[128,512]{1,0:T(8,128)(2,1)S(1)} %slice.78), channel_id=1, source_target_pairs={{0,4},{1,5},{2,6},{3,7},{4,0},{5,1},{6,2},{7,3},{8,12},{9,13},{10,... | collective-permute-start | bytes 393224 | tf_op jit(solution)/shard_map/ppermute | solution.py:90
  75.5 3.0 %project.1 = (bf16[2048,512]{1,0:T(8,128)(2,1)}, f32[2,128,512]{2,1,0:T(8,128)S(1)}) custom-call(s32[1]{0:T(128)} %bitcast.me_ref, bf16[128,4096]{1,0:T(8,128)(2,1)S(1)} %copy-done, bf16[128,4096]{1,0:T(8,128)(2,1)S(1)} %collective-permute-done.10.mate_ref, bf16[256,512]{1,0:T(8,128)(2,1)S(1)} %maximum_select_fusion.refs_0_, bf16[256,512]{1,0:T(8,128)(2,1)S(1)} %copy-done.5, ...), custom_call_target="tpu_custom_call" | custom-call | flops 536870912 | bytes 6291456 | tf_op jit(solution)/shard_map/project/pallas_call | solution.py:365
  79.2 1.3 collective-permute-done.25.refs_9_
  80.6 3.8 %delta.1 = (bf16[256,512]{1,0:T(8,128)(2,1)S(1)}, bf16[2048,512]{1,0:T(8,128)(2,1)}) custom-call(s32[1]{0:T(128)} %bitcast.me_ref, bf16[128,4096]{1,0:T(8,128)(2,1)S(1)} %copy-done, bf16[128,4096]{1,0:T(8,128)(2,1)S(1)} %collective-permute-done.10.mate_ref, bf16[128,512]{1,0:T(8,128)(2,1)S(1)} %get-tuple-element.39.own_cot_ref, ...), custom_call_target="tpu_custom_call" | custom-call | flops 536870912 | bytes 6291456 | tf_op jit(solution)/shard_map/delta/pallas_call | solution.py:376
  84.4 0.9 collective-permute-start.26
  85.3 2.0 %collective-permute-start.27 = (bf16[256,512]{1,0:T(8,128)(2,1)S(1)}, bf16[256,512]{1,0:T(8,128)(2,1)S(1)}, u32[]{:S(2)}, u32[]{:S(2)}) collective-permute-start(bf16[256,512]{1,0:T(8,128)(2,1)S(1)} %get-tuple-element.32.refs_0_), channel_id=1, source_target_pairs={{0,8},{1,9},{2,10},{3,11},{4,12},{5,13},{6,14},{7,15},{8,0},{9,1},... | collective-permute-start | bytes 786440 | tf_op jit(solution)/shard_map/ppermute | solution.py:90
  87.3 12.3 %collective-permute-done.26.refs_1_.refs_2_ = bf16[256,512]{1,0:T(8,128)(2,1)S(1)} collective-permute-done((bf16[256,512]{1,0:T(8,128)(2,1)S(1)}, bf16[256,512]{1,0:T(8,128)(2,1)S(1)}, u32[]{:S(2)}, u32[]{:S(2)}) %collective-permute-start.26) | collective-permute-done | bytes 262176 | tf_op jit(solution)/shard_map/ppermute | solution.py:90
  99.6 8.2 %collective-permute-done.28.refs_3_ = bf16[256,512]{1,0:T(8,128)(2,1)S(1)} collective-permute-done((bf16[256,512]{1,0:T(8,128)(2,1)S(1)}, bf16[256,512]{1,0:T(8,128)(2,1)S(1)}, u32[]{:S(2)}, u32[]{:S(2)}) %collective-permute-start.28) | collective-permute-done | bytes 262176 | tf_op jit(solution)/shard_map/ppermute | solution.py:90
  107.8 2.0 %select.11 = bf16[512,512]{1,0:T(8,128)(2,1)} custom-call(s32[1]{0:T(128)} %bitcast.me_ref, s32[8,128]{1,0:T(8,128)S(1)} %pad_add_fusion.code_ref, bf16[256,512]{1,0:T(8,128)(2,1)S(1)} %get-tuple-element.32.refs_0_, bf16[256,512]{1,0:T(8,128)(2,1)S(1)} %collective-permute-done.26.refs_1_.refs_2_, ...), custom_call_target="tpu_custom_call" | custom-call | flops 536870912 | bytes 2097152 | tf_op jit(solution)/shard_map/select/pallas_call | solution.py:388
  110.6 3.5 %all-to-all-start.1 = ((bf16[8,64,512]{2,1,0:T(8,128)(2,1)}), bf16[8,64,512]{2,1,0:T(8,128)(2,1)S(1)}, u32[]{:S(2)}, u32[]{:S(2)}) async-start(bf16[8,64,512]{2,1,0:T(8,128)(2,1)} %bitcast.10), calls=%async_computation.1 | async-start | bytes 1048576 | tf_op jit(solution)/shard_map/all_to_all | solution.py:400
  114.1 0.9 copy-done.13
  115.0 4.6 %weight_grad.1 = bf16[1024,512]{1,0:T(8,128)(2,1)} custom-call(s32[1]{0:T(128)} %bitcast.me_ref, bf16[4,128,1024]{2,1,0:T(8,128)(2,1)S(1)} %all-to-all-done.own_ref, bf16[4,128,1024]{2,1,0:T(8,128)(2,1)} %collective-permute-done.18.mate_ref, bf16[256,512]{1,0:T(8,128)(2,1)S(1)} %copy-done.13, bf16[256,512]{1,0:T(8,128)(2,1)S(1)} %collective-permute-done.27.refs_2_.refs_1_, ...), custom_call_target="tpu_custom_call" | custom-call | flops 1073741824 | bytes 4194304 | tf_op jit(solution)/shard_map/weight_grad/pallas_call | solution.py:412
  119.6 4.1 %all-to-all-done.1 = bf16[8,64,512]{2,1,0:T(8,128)(2,1)S(1)} async-done(((bf16[8,64,512]{2,1,0:T(8,128)(2,1)}), bf16[8,64,512]{2,1,0:T(8,128)(2,1)S(1)}, u32[]{:S(2)}, u32[]{:S(2)}) %all-to-all-start.1) | async-done | bytes 524320 | tf_op jit(solution)/shard_map/all_to_all | solution.py:400
  123.7 3.6 %all-to-all-start.2 = ((bf16[8,128,512]{2,1,0:T(8,128)(2,1)}), bf16[8,128,512]{2,1,0:T(8,128)(2,1)S(1)}, u32[]{:S(2)}, u32[]{:S(2)}) async-start(bf16[8,128,512]{2,1,0:T(8,128)(2,1)} %bitcast.12), calls=%async_computation.2 | async-start | bytes 2097152 | tf_op jit(solution)/shard_map/all_to_all | solution.py:400
  127.3 1.6 %copy-done.1 = bf16[2048,512]{1,0:T(8,128)(2,1)S(1)} copy-done((bf16[2048,512]{1,0:T(8,128)(2,1)S(1)}, bf16[2048,512]{1,0:T(8,128)(2,1)}, u32[]{:S(2)}) %copy-start.1) | copy-done | bytes 2097176
  128.9 8.4 %row_grad.1 = bf16[256,4096]{1,0:T(8,128)(2,1)} custom-call(s32[1]{0:T(128)} %bitcast.me_ref, bf16[4,2,64,512]{3,2,1,0:T(8,128)(2,1)S(1)} %bitcast.22, bf16[2048,512]{1,0:T(8,128)(2,1)S(1)} %copy-done.1, bf16[2048,512]{1,0:T(8,128)(2,1)} %collective-permute-done.29.refs_1_, bf16[2048,512]{1,0:T(8,128)(2,1)} %get-tuple-element.31.refs_2_, ...), custom_call_target="tpu_custom_call" | custom-call | flops 2147483648 | bytes 12582912 | tf_op jit(solution)/shard_map/row_grad/pallas_call | solution.py:432
  137.3 5.3 %all-to-all-done.2 = bf16[8,128,512]{2,1,0:T(8,128)(2,1)S(1)} async-done(((bf16[8,128,512]{2,1,0:T(8,128)(2,1)}), bf16[8,128,512]{2,1,0:T(8,128)(2,1)S(1)}, u32[]{:S(2)}, u32[]{:S(2)}) %all-to-all-start.2) | async-done | bytes 1048608 | tf_op jit(solution)/shard_map/all_to_all | solution.py:400
  142.6 0.9 sum.1
  (85 shorter events, 11.6 us)
Async XLA Ops:
  0.6 18.6 %copy-start = (bf16[128,4096]{1,0:T(8,128)(2,1)S(1)}, bf16[128,4096]{1,0:T(8,128)(2,1)}, u32[]{:S(2)}) copy-start(bf16[128,4096]{1,0:T(8,128)(2,1)} %own_ref.3) | copy-start | bytes 3145732
  0.6 1.9 %collective-permute-start = (bf16[128,1024]{1,0:T(8,128)(2,1)}, bf16[128,1024]{1,0:T(8,128)(2,1)S(1)}, u32[]{:S(2)}, u32[]{:S(2)}) collective-permute-start(bf16[128,1024]{1,0:T(8,128)(2,1)} %param.11), channel_id=1, source_target_pairs={{0,1},{1,0},{2,3},{3,2},{4,5},{5,4},{6,7},{7,6},{8,9},{9,8},{10,11... | collective-permute-start | bytes 786440 | tf_op jit(solution)/shard_map/ppermute | solution.py:90
  2.6 16.4 %collective-permute-start.2 = (bf16[256,512]{1,0:T(8,128)(2,1)S(1)}, bf16[256,512]{1,0:T(8,128)(2,1)S(1)}, u32[]{:S(2)}, u32[]{:S(2)}) collective-permute-start(bf16[256,512]{1,0:T(8,128)(2,1)S(1)} %maximum_select_fusion.refs_0_), channel_id=1, source_target_pairs={{0,16},{1,17},{2,18},{3,19},{4,20},{5,21},{6,22},{7,23},{8,24},{9,... | collective-permute-start | bytes 786440 | tf_op jit(solution)/shard_map/ppermute | solution.py:90
  6.6 12.6 %collective-permute-start.1 = (bf16[256,512]{1,0:T(8,128)(2,1)S(1)}, bf16[256,512]{1,0:T(8,128)(2,1)}, u32[]{:S(2)}, u32[]{:S(2)}) collective-permute-start(bf16[256,512]{1,0:T(8,128)(2,1)S(1)} %maximum_select_fusion.refs_0_), channel_id=1, source_target_pairs={{0,8},{1,9},{2,10},{3,11},{4,12},{5,13},{6,14},{7,15},{8,0},{9,1},... | collective-permute-start | bytes 786440 | tf_op jit(solution)/shard_map/ppermute | solution.py:90
  19.0 1.5 %copy-start.10 = (bf16[256,512]{1,0:T(8,128)(2,1)}, bf16[256,512]{1,0:T(8,128)(2,1)S(1)}, u32[]{:S(2)}) copy-start(bf16[256,512]{1,0:T(8,128)(2,1)S(1)} %collective-permute-done.2.refs_0_) | copy-start | bytes 786436
  19.4 23.5 %copy-start.16 = (s32[128,1]{0,1:T(1,128)S(1)}, s32[128,1]{0,1:T(1,128)}, u32[]{:S(2)}) copy-start(s32[128,1]{0,1:T(1,128)} %param.8) | copy-start | bytes 1540
  20.5 30.3 %all-to-all-start = ((bf16[4,128,1024]{2,1,0:T(8,128)(2,1)}), bf16[4,128,1024]{2,1,0:T(8,128)(2,1)S(1)}, u32[]{:S(2)}, u32[]{:S(2)}) async-start(bf16[4,128,1024]{2,1,0:T(8,128)(2,1)} %pad_maximum_fusion), calls=%async_computation | async-start | bytes 2097152 | tf_op jit(solution)/shard_map/all_to_all | solution.py:321
  24.9 8.0 %collective-permute-start.4 = (bf16[256,512]{1,0:T(8,128)(2,1)S(1)}, bf16[256,512]{1,0:T(8,128)(2,1)S(1)}, u32[]{:S(2)}, u32[]{:S(2)}) collective-permute-start(bf16[256,512]{1,0:T(8,128)(2,1)S(1)} %maximum_select_fusion.refs_0_), channel_id=1, source_target_pairs={{0,4},{1,5},{2,6},{3,7},{4,0},{5,1},{6,2},{7,3},{8,12},{9,13},{10,... | collective-permute-start | bytes 786440 | tf_op jit(solution)/shard_map/ppermute | solution.py:90
  26.4 7.7 %collective-permute-start.3 = (bf16[256,512]{1,0:T(8,128)(2,1)S(1)}, bf16[256,512]{1,0:T(8,128)(2,1)S(1)}, u32[]{:S(2)}, u32[]{:S(2)}) collective-permute-start(bf16[256,512]{1,0:T(8,128)(2,1)S(1)} %maximum_select_fusion.refs_0_), channel_id=1, source_target_pairs={{0,2},{1,3},{2,0},{3,1},{4,6},{5,7},{6,4},{7,5},{8,10},{9,11},{10,... | collective-permute-start | bytes 786440 | tf_op jit(solution)/shard_map/ppermute | solution.py:90
  32.9 10.1 %copy-start.2 = (bf16[256,512]{1,0:T(8,128)(2,1)}, bf16[256,512]{1,0:T(8,128)(2,1)S(1)}, u32[]{:S(2)}) copy-start(bf16[256,512]{1,0:T(8,128)(2,1)S(1)} %collective-permute-done.4.refs_2_) | copy-start | bytes 786436
  34.1 8.9 %copy-start.4 = (bf16[256,512]{1,0:T(8,128)(2,1)}, bf16[256,512]{1,0:T(8,128)(2,1)S(1)}, u32[]{:S(2)}) copy-start(bf16[256,512]{1,0:T(8,128)(2,1)S(1)} %collective-permute-done.3.refs_1_) | copy-start | bytes 786436
  34.1 8.4 %collective-permute-start.6 = (bf16[256,512]{1,0:T(8,128)(2,1)}, bf16[256,512]{1,0:T(8,128)(2,1)S(1)}, u32[]{:S(2)}, u32[]{:S(2)}) collective-permute-start(bf16[256,512]{1,0:T(8,128)(2,1)} %collective-permute-done.1.refs_5_), channel_id=1, source_target_pairs={{0,4},{1,5},{2,6},{3,7},{4,0},{5,1},{6,2},{7,3},{8,12},{9,13},{10,... | collective-permute-start | bytes 786440 | tf_op jit(solution)/shard_map/ppermute | solution.py:90
  34.6 8.3 %collective-permute-start.5 = (bf16[256,512]{1,0:T(8,128)(2,1)}, bf16[256,512]{1,0:T(8,128)(2,1)S(1)}, u32[]{:S(2)}, u32[]{:S(2)}) collective-permute-start(bf16[256,512]{1,0:T(8,128)(2,1)} %collective-permute-done.1.refs_5_), channel_id=1, source_target_pairs={{0,2},{1,3},{2,0},{3,1},{4,6},{5,7},{6,4},{7,5},{8,10},{9,11},{10,... | collective-permute-start | bytes 786440 | tf_op jit(solution)/shard_map/ppermute | solution.py:90
  36.1 14.7 %collective-permute-start.21 = (bf16[256,512]{1,0:T(8,128)(2,1)}, bf16[256,512]{1,0:T(8,128)(2,1)}, u32[]{:S(2)}, u32[]{:S(2)}) collective-permute-start(bf16[256,512]{1,0:T(8,128)(2,1)} %copy-done.10), channel_id=1, source_target_pairs={{0,8},{1,9},{2,10},{3,11},{4,12},{5,13},{6,14},{7,15},{8,0},{9,1},... | collective-permute-start | bytes 786440 | tf_op jit(solution)/shard_map/ppermute | solution.py:90
  37.9 6.4 %collective-permute-start.11 = (bf16[128,512]{1,0:T(8,128)(2,1)S(1)}, bf16[128,512]{1,0:T(8,128)(2,1)S(1)}, u32[]{:S(2)}, u32[]{:S(2)}) collective-permute-start(bf16[128,512]{1,0:T(8,128)(2,1)S(1)} %slice.71), channel_id=1, source_target_pairs={{0,2},{1,3},{2,0},{3,1},{4,6},{5,7},{6,4},{7,5},{8,10},{9,11},{10,... | collective-permute-start | bytes 393224 | tf_op jit(solution)/shard_map/ppermute | solution.py:90
  38.5 5.8 %collective-permute-start.12 = (bf16[128,512]{1,0:T(8,128)(2,1)S(1)}, bf16[128,512]{1,0:T(8,128)(2,1)S(1)}, u32[]{:S(2)}, u32[]{:S(2)}) collective-permute-start(bf16[128,512]{1,0:T(8,128)(2,1)S(1)} %slice.72), channel_id=1, source_target_pairs={{0,4},{1,5},{2,6},{3,7},{4,0},{5,1},{6,2},{7,3},{8,12},{9,13},{10,... | collective-permute-start | bytes 393224 | tf_op jit(solution)/shard_map/ppermute | solution.py:90
  42.5 0.7 copy-start.6
  43.6 4.2 %collective-permute-start.7 = (s32[1,128]{1,0:T(1,128)S(1)}, s32[1,128]{1,0:T(1,128)S(1)}, u32[]{:S(2)}, u32[]{:S(2)}) collective-permute-start(s32[1,128]{1,0:T(1,128)S(1)} %bitcast_add_fusion), channel_id=1, source_target_pairs={{0,1},{1,0},{2,3},{3,2},{4,5},{5,4},{6,7},{7,6},{8,9},{9,8},{10,11... | collective-permute-start | bytes 1544 | tf_op jit(solution)/shard_map/ppermute | solution.py:90
  43.6 29.7 %collective-permute-start.10 = (bf16[128,4096]{1,0:T(8,128)(2,1)S(1)}, bf16[128,4096]{1,0:T(8,128)(2,1)S(1)}, u32[]{:S(2)}, u32[]{:S(2)}) collective-permute-start(bf16[128,4096]{1,0:T(8,128)(2,1)S(1)} %copy-done), channel_id=1, source_target_pairs={{0,1},{1,0},{2,3},{3,2},{4,5},{5,4},{6,7},{7,6},{8,9},{9,8},{10,11... | collective-permute-start | bytes 3145736 | tf_op jit(solution)/shard_map/ppermute | solution.py:90
  45.0 12.2 %collective-permute-start.14 = (bf16[256,512]{1,0:T(8,128)(2,1)}, bf16[256,512]{1,0:T(8,128)(2,1)}, u32[]{:S(2)}, u32[]{:S(2)}) collective-permute-start(bf16[256,512]{1,0:T(8,128)(2,1)} %copy-done.10), channel_id=1, source_target_pairs={{0,4},{1,5},{2,6},{3,7},{4,0},{5,1},{6,2},{7,3},{8,12},{9,13},{10,... | collective-permute-start | bytes 786440 | tf_op jit(solution)/shard_map/ppermute | solution.py:90
  46.3 12.4 %collective-permute-start.13 = (bf16[256,512]{1,0:T(8,128)(2,1)}, bf16[256,512]{1,0:T(8,128)(2,1)}, u32[]{:S(2)}, u32[]{:S(2)}) collective-permute-start(bf16[256,512]{1,0:T(8,128)(2,1)} %copy-done.10), channel_id=1, source_target_pairs={{0,2},{1,3},{2,0},{3,1},{4,6},{5,7},{6,4},{7,5},{8,10},{9,11},{10,... | collective-permute-start | bytes 786440 | tf_op jit(solution)/shard_map/ppermute | solution.py:90
  50.8 23.1 %collective-permute-start.18 = (bf16[4,128,1024]{2,1,0:T(8,128)(2,1)S(1)}, bf16[4,128,1024]{2,1,0:T(8,128)(2,1)}, u32[]{:S(2)}, u32[]{:S(2)}) collective-permute-start(bf16[4,128,1024]{2,1,0:T(8,128)(2,1)S(1)} %all-to-all-done.own_ref), channel_id=1, source_target_pairs={{0,1},{1,0},{2,3},{3,2},{4,5},{5,4},{6,7},{7,6},{8,9},{9,8},{10,11... | collective-permute-start | bytes 3145736 | tf_op jit(solution)/shard_map/ppermute | solution.py:90
  50.9 4.8 %collective-permute-start.8 = (s32[2,128]{1,0:T(2,128)S(1)}, s32[2,128]{1,0:T(2,128)S(1)}, u32[]{:S(2)}, u32[]{:S(2)}) collective-permute-start(s32[2,128]{1,0:T(2,128)S(1)} %add_select_fusion.1), channel_id=1, source_target_pairs={{0,16},{1,17},{2,18},{3,19},{4,20},{5,21},{6,22},{7,23},{8,24},{9,... | collective-permute-start | bytes 3080 | tf_op jit(solution)/shard_map/ppermute | solution.py:90
  55.6 7.6 %collective-permute-start.23 = (bf16[256,512]{1,0:T(8,128)(2,1)}, bf16[256,512]{1,0:T(8,128)(2,1)}, u32[]{:S(2)}, u32[]{:S(2)}) collective-permute-start(bf16[256,512]{1,0:T(8,128)(2,1)} %collective-permute-done.21.refs_5_), channel_id=1, source_target_pairs={{0,4},{1,5},{2,6},{3,7},{4,0},{5,1},{6,2},{7,3},{8,12},{9,13},{10,... | collective-permute-start | bytes 786440 | tf_op jit(solution)/shard_map/ppermute | solution.py:90
  57.2 8.8 %collective-permute-start.22 = (bf16[256,512]{1,0:T(8,128)(2,1)}, bf16[256,512]{1,0:T(8,128)(2,1)}, u32[]{:S(2)}, u32[]{:S(2)}) collective-permute-start(bf16[256,512]{1,0:T(8,128)(2,1)} %collective-permute-done.21.refs_5_), channel_id=1, source_target_pairs={{0,2},{1,3},{2,0},{3,1},{4,6},{5,7},{6,4},{7,5},{8,10},{9,11},{10,... | collective-permute-start | bytes 786440 | tf_op jit(solution)/shard_map/ppermute | solution.py:90
  58.7 14.1 %collective-permute-start.16 = (bf16[128,512]{1,0:T(8,128)(2,1)}, bf16[128,512]{1,0:T(8,128)(2,1)}, u32[]{:S(2)}, u32[]{:S(2)}) collective-permute-start(bf16[128,512]{1,0:T(8,128)(2,1)} %slice.73), channel_id=1, source_target_pairs={{0,2},{1,3},{2,0},{3,1},{4,6},{5,7},{6,4},{7,5},{8,10},{9,11},{10,... | collective-permute-start | bytes 393224 | tf_op jit(solution)/shard_map/ppermute | solution.py:90
  60.6 14.8 %copy-start.3 = (bf16[256,512]{1,0:T(8,128)(2,1)S(1)}, bf16[256,512]{1,0:T(8,128)(2,1)}, u32[]{:S(2)}) copy-start(bf16[256,512]{1,0:T(8,128)(2,1)} %copy-done.2) | copy-start | bytes 786436
  60.6 14.8 %copy-start.5 = (bf16[256,512]{1,0:T(8,128)(2,1)S(1)}, bf16[256,512]{1,0:T(8,128)(2,1)}, u32[]{:S(2)}) copy-start(bf16[256,512]{1,0:T(8,128)(2,1)} %copy-done.4) | copy-start | bytes 786436
  60.6 14.9 %copy-start.7 = (bf16[256,512]{1,0:T(8,128)(2,1)S(1)}, bf16[256,512]{1,0:T(8,128)(2,1)}, u32[]{:S(2)}) copy-start(bf16[256,512]{1,0:T(8,128)(2,1)} %copy-done.6) | copy-start | bytes 786436
  60.6 14.9 %copy-start.9 = (bf16[256,512]{1,0:T(8,128)(2,1)S(1)}, bf16[256,512]{1,0:T(8,128)(2,1)}, u32[]{:S(2)}) copy-start(bf16[256,512]{1,0:T(8,128)(2,1)} %copy-done.8) | copy-start | bytes 786436
  60.6 14.9 %copy-start.15 = (bf16[128,512]{1,0:T(8,128)(2,1)S(1)}, bf16[128,512]{1,0:T(8,128)(2,1)}, u32[]{:S(2)}) copy-start(bf16[128,512]{1,0:T(8,128)(2,1)} %copy-done.14) | copy-start | bytes 393220
  63.3 10.0 %collective-permute-start.17 = (bf16[128,512]{1,0:T(8,128)(2,1)}, bf16[128,512]{1,0:T(8,128)(2,1)S(1)}, u32[]{:S(2)}, u32[]{:S(2)}) collective-permute-start(bf16[128,512]{1,0:T(8,128)(2,1)} %slice.74), channel_id=1, source_target_pairs={{0,4},{1,5},{2,6},{3,7},{4,0},{5,1},{6,2},{7,3},{8,12},{9,13},{10,... | collective-permute-start | bytes 393224 | tf_op jit(solution)/shard_map/ppermute | solution.py:90
  66.0 5.2 %collective-permute-start.9 = (s32[4,128]{1,0:T(4,128)S(1)}, s32[4,128]{1,0:T(4,128)S(1)}, u32[]{:S(2)}, u32[]{:S(2)}) collective-permute-start(s32[4,128]{1,0:T(4,128)S(1)} %pad_add_fusion.1), channel_id=1, source_target_pairs={{0,8},{1,9},{2,10},{3,11},{4,12},{5,13},{6,14},{7,15},{8,0},{9,1},... | collective-permute-start | bytes 6152 | tf_op jit(solution)/shard_map/ppermute | solution.py:90
  71.2 7.2 %collective-permute-start.19 = (bf16[128,512]{1,0:T(8,128)(2,1)S(1)}, bf16[128,512]{1,0:T(8,128)(2,1)S(1)}, u32[]{:S(2)}, u32[]{:S(2)}) collective-permute-start(bf16[128,512]{1,0:T(8,128)(2,1)S(1)} %slice.75), channel_id=1, source_target_pairs={{0,2},{1,3},{2,0},{3,1},{4,6},{5,7},{6,4},{7,5},{8,10},{9,11},{10,... | collective-permute-start | bytes 393224 | tf_op jit(solution)/shard_map/ppermute | solution.py:90
  72.8 6.1 %collective-permute-start.20 = (bf16[128,512]{1,0:T(8,128)(2,1)S(1)}, bf16[128,512]{1,0:T(8,128)(2,1)S(1)}, u32[]{:S(2)}, u32[]{:S(2)}) collective-permute-start(bf16[128,512]{1,0:T(8,128)(2,1)S(1)} %slice.76), channel_id=1, source_target_pairs={{0,4},{1,5},{2,6},{3,7},{4,0},{5,1},{6,2},{7,3},{8,12},{9,13},{10,... | collective-permute-start | bytes 393224 | tf_op jit(solution)/shard_map/ppermute | solution.py:90
  73.3 5.5 %collective-permute-start.15 = (bf16[128,512]{1,0:T(8,128)(2,1)S(1)}, bf16[128,512]{1,0:T(8,128)(2,1)S(1)}, u32[]{:S(2)}, u32[]{:S(2)}) collective-permute-start(bf16[128,512]{1,0:T(8,128)(2,1)S(1)} %get-tuple-element.38), channel_id=1, source_target_pairs={{0,1},{1,0},{2,3},{3,2},{4,5},{5,4},{6,7},{7,6},{8,9},{9,8},{10,11... | collective-permute-start | bytes 393224 | tf_op jit(solution)/shard_map/ppermute | solution.py:90
  73.3 5.9 %collective-permute-start.24 = (bf16[128,512]{1,0:T(8,128)(2,1)S(1)}, bf16[128,512]{1,0:T(8,128)(2,1)S(1)}, u32[]{:S(2)}, u32[]{:S(2)}) collective-permute-start(bf16[128,512]{1,0:T(8,128)(2,1)S(1)} %slice.77), channel_id=1, source_target_pairs={{0,2},{1,3},{2,0},{3,1},{4,6},{5,7},{6,4},{7,5},{8,10},{9,11},{10,... | collective-permute-start | bytes 393224 | tf_op jit(solution)/shard_map/ppermute | solution.py:90
  73.9 6.7 %collective-permute-start.25 = (bf16[128,512]{1,0:T(8,128)(2,1)S(1)}, bf16[128,512]{1,0:T(8,128)(2,1)S(1)}, u32[]{:S(2)}, u32[]{:S(2)}) collective-permute-start(bf16[128,512]{1,0:T(8,128)(2,1)S(1)} %slice.78), channel_id=1, source_target_pairs={{0,4},{1,5},{2,6},{3,7},{4,0},{5,1},{6,2},{7,3},{8,12},{9,13},{10,... | collective-permute-start | bytes 393224 | tf_op jit(solution)/shard_map/ppermute | solution.py:90
  75.5 5.1 %copy-start.11 = (bf16[256,512]{1,0:T(8,128)(2,1)S(1)}, bf16[256,512]{1,0:T(8,128)(2,1)}, u32[]{:S(2)}) copy-start(bf16[256,512]{1,0:T(8,128)(2,1)} %copy-done.10) | copy-start | bytes 786436
  78.5 48.8 %collective-permute-start.29 = (bf16[2048,512]{1,0:T(8,128)(2,1)}, bf16[2048,512]{1,0:T(8,128)(2,1)}, u32[]{:S(2)}, u32[]{:S(2)}) collective-permute-start(bf16[2048,512]{1,0:T(8,128)(2,1)} %get-tuple-element.30.refs_0_), channel_id=1, source_target_pairs={{0,1},{1,0},{2,3},{3,2},{4,5},{5,4},{6,7},{7,6},{8,9},{9,8},{10,11... | collective-permute-start | bytes 6291464 | tf_op jit(solution)/shard_map/ppermute | solution.py:90
  84.3 43.0 %collective-permute-start.30 = (bf16[2048,512]{1,0:T(8,128)(2,1)}, bf16[2048,512]{1,0:T(8,128)(2,1)}, u32[]{:S(2)}, u32[]{:S(2)}) collective-permute-start(bf16[2048,512]{1,0:T(8,128)(2,1)} %get-tuple-element.31.refs_2_), channel_id=1, source_target_pairs={{0,1},{1,0},{2,3},{3,2},{4,5},{5,4},{6,7},{7,6},{8,9},{9,8},{10,11... | collective-permute-start | bytes 6291464 | tf_op jit(solution)/shard_map/ppermute | solution.py:90
  84.4 15.2 %collective-permute-start.26 = (bf16[256,512]{1,0:T(8,128)(2,1)S(1)}, bf16[256,512]{1,0:T(8,128)(2,1)S(1)}, u32[]{:S(2)}, u32[]{:S(2)}) collective-permute-start(bf16[256,512]{1,0:T(8,128)(2,1)S(1)} %get-tuple-element.32.refs_0_), channel_id=1, source_target_pairs={{0,16},{1,17},{2,18},{3,19},{4,20},{5,21},{6,22},{7,23},{8,24},{9,... | collective-permute-start | bytes 786440 | tf_op jit(solution)/shard_map/ppermute | solution.py:90
  85.3 14.3 %collective-permute-start.27 = (bf16[256,512]{1,0:T(8,128)(2,1)S(1)}, bf16[256,512]{1,0:T(8,128)(2,1)S(1)}, u32[]{:S(2)}, u32[]{:S(2)}) collective-permute-start(bf16[256,512]{1,0:T(8,128)(2,1)S(1)} %get-tuple-element.32.refs_0_), channel_id=1, source_target_pairs={{0,8},{1,9},{2,10},{3,11},{4,12},{5,13},{6,14},{7,15},{8,0},{9,1},... | collective-permute-start | bytes 786440 | tf_op jit(solution)/shard_map/ppermute | solution.py:90
  99.6 8.2 %collective-permute-start.28 = (bf16[256,512]{1,0:T(8,128)(2,1)S(1)}, bf16[256,512]{1,0:T(8,128)(2,1)S(1)}, u32[]{:S(2)}, u32[]{:S(2)}) collective-permute-start(bf16[256,512]{1,0:T(8,128)(2,1)S(1)} %collective-permute-done.26.refs_1_.refs_2_), channel_id=1, source_target_pairs={{0,8},{1,9},{2,10},{3,11},{4,12},{5,13},{6,14},{7,15},{8,0},{9,1},... | collective-permute-start | bytes 786440 | tf_op jit(solution)/shard_map/ppermute | solution.py:90
  110.6 13.2 %all-to-all-start.1 = ((bf16[8,64,512]{2,1,0:T(8,128)(2,1)}), bf16[8,64,512]{2,1,0:T(8,128)(2,1)S(1)}, u32[]{:S(2)}, u32[]{:S(2)}) async-start(bf16[8,64,512]{2,1,0:T(8,128)(2,1)} %bitcast.10), calls=%async_computation.1 | async-start | bytes 1048576 | tf_op jit(solution)/shard_map/all_to_all | solution.py:400
  114.1 1.0 copy-start.13
  123.7 18.9 %all-to-all-start.2 = ((bf16[8,128,512]{2,1,0:T(8,128)(2,1)}), bf16[8,128,512]{2,1,0:T(8,128)(2,1)S(1)}, u32[]{:S(2)}, u32[]{:S(2)}) async-start(bf16[8,128,512]{2,1,0:T(8,128)(2,1)} %bitcast.12), calls=%async_computation.2 | async-start | bytes 2097152 | tf_op jit(solution)/shard_map/all_to_all | solution.py:400
  127.3 1.6 %copy-start.1 = (bf16[2048,512]{1,0:T(8,128)(2,1)S(1)}, bf16[2048,512]{1,0:T(8,128)(2,1)}, u32[]{:S(2)}) copy-start(bf16[2048,512]{1,0:T(8,128)(2,1)} %get-tuple-element.30.refs_0_) | copy-start | bytes 6291460
  (3 other events, 2.1 us)

commit v6 on v5

v6 whole, which is shorter than its diff:
```python
import functools
import math

import jax
import jax.numpy as jnp
from jax import lax
from jax.experimental import pallas as pl
from jax.experimental.pallas import tpu as pltpu
from jax.sharding import PartitionSpec as P

HEAD_DIM = 128
NSUB = 4
VMEM_LIMIT = 48 * 1024 * 1024
epsilon = 1e-06


def per_device_general(tokens, key_cot, routes, counts, widths, key_weight):
    row_count = tokens.shape[0]
    width_model = tokens.shape[1]
    local_cols = key_cot.shape[1]
    local_heads = local_cols // HEAD_DIM
    dp_size = lax.axis_size("dp")
    per_peer = 2 * row_count // dp_size
    receive = dp_size * per_peer
    destination = routes[:, 0]
    one_hot = (destination[:, None] == jnp.arange(dp_size, dtype=jnp.int32)[None, :]).astype(
        jnp.int32
    )
    earlier = jnp.sum(jnp.cumsum(one_hot, axis=0) * one_hot, axis=1) - 1
    send_slot = destination * per_peer + earlier
    bounds = jnp.cumsum(counts[0])
    positions = jnp.arange(row_count, dtype=jnp.int32)
    subnet = jnp.sum((positions[:, None] >= bounds[None, : NSUB - 1]).astype(jnp.int32), axis=1)
    send_subnet = (
        jnp.full((receive,), -1, jnp.int32).at[send_slot].set(subnet).reshape(dp_size, per_peer)
    )
    send_cot = jnp.zeros((receive, local_cols), jnp.bfloat16).at[send_slot].set(key_cot)
    send_cot = send_cot.reshape(dp_size, per_peer, local_cols)
    send_tokens = jnp.zeros((receive, width_model), jnp.bfloat16).at[send_slot].set(tokens)
    send_tokens = send_tokens.reshape(dp_size, per_peer, width_model)
    got_tokens, got_cot, got_subnet = (
        lax.all_to_all(send_tokens, "dp", split_axis=0, concat_axis=0, tiled=True),
        lax.all_to_all(send_cot, "dp", split_axis=0, concat_axis=0, tiled=True),
        lax.all_to_all(send_subnet, "dp", split_axis=0, concat_axis=0, tiled=True),
    )
    hidden = got_tokens.reshape(receive, width_model)
    got_cot = got_cot.reshape(receive, local_cols)
    got_subnet = got_subnet.reshape(receive)
    full_weight = lax.all_gather(key_weight, "dp", axis=0, tiled=True)
    key_proj = jnp.dot(hidden, full_weight, preferred_element_type=jnp.float32)
    per_head = key_proj.reshape(receive, local_heads, HEAD_DIM)
    head_scale = jnp.sqrt(jnp.mean(per_head * per_head, axis=2, keepdims=True) + epsilon)
    outputs = per_head / head_scale
    subnet_match = got_subnet[:, None] == jnp.arange(NSUB, dtype=jnp.int32)[None, :]
    row_width = jnp.sum(jnp.where(subnet_match, widths[None, :], 0), axis=1)
    head_index = lax.axis_index("mp") * local_heads + jnp.arange(local_heads, dtype=jnp.int32)
    head_mask = (head_index[None, :] < row_width[:, None]).astype(jnp.float32)
    upstream = (
        got_cot.astype(jnp.float32).reshape(receive, local_heads, HEAD_DIM) * head_mask[:, :, None]
    )
    key_delta = (
        upstream - outputs * jnp.mean(upstream * outputs, axis=2, keepdims=True)
    ) / head_scale
    delta_low = key_delta.reshape(receive, local_cols).astype(jnp.bfloat16)
    part_delta = lax.dot_general(
        delta_low, full_weight, (((1,), (1,)), ((), ())), preferred_element_type=jnp.float32
    )
    rounded = lax.optimization_barrier(part_delta.astype(jnp.bfloat16)).astype(jnp.float32)
    feature_delta = lax.psum_scatter(
        rounded.astype(jnp.bfloat16), "mp", scatter_dimension=1, tiled=True
    )
    weight_sum = lax.psum_scatter(
        lax.dot_general(
            hidden, delta_low, (((0,), (0,)), ((), ())), preferred_element_type=jnp.float32
        ),
        "dp",
        scatter_dimension=0,
        tiled=True,
    )
    key_grad = weight_sum / math.sqrt(row_count * dp_size)
    return (feature_delta, key_grad)


CORE, X, Y = 1, 2, 4
PLANE = 8


def swap(value, mask):
    size = lax.axis_size("dp")
    return lax.ppermute(value, "dp", [(i, i ^ mask) for i in range(size)])


def after(value, *others):
    return lax.optimization_barrier((value, *others))[0]


def dot(a, b, dims):
    return lax.dot_general(a, b, (dims, ((), ())), preferred_element_type=jnp.float32)


def add_products(chips_ref, begin, own_ref, mate_ref, pieces, weight_ref, acc, fresh):
    for n, piece_ref in enumerate(pieces):
        piece = piece_ref[...]
        depth = piece.shape[0]
        at = pl.multiple_of(chips_ref[begin + n] * depth, depth)
        weight_ref[n * depth : (n + 1) * depth, :] = piece
        for side, ref in enumerate((own_ref, mate_ref)):
            part = dot(ref[:, pl.ds(at, depth)], piece, ((1,), (0,)))
            if fresh and n == 0:
                acc[side] = part
            else:
                acc[side] += part


def project_kernel(count, chips_ref, own_ref, mate_ref, *refs):
    weight_ref, acc_ref = refs[count:]
    add_products(chips_ref, 0, own_ref, mate_ref, refs[:count], weight_ref, acc_ref, True)


def delta_kernel(
    count,
    begin,
    chips_ref,
    me_ref,
    own_ref,
    mate_ref,
    own_cot_ref,
    mate_cot_ref,
    begun_ref,
    *refs,
):
    delta_ref, weight_ref, acc = refs[count:]
    core = me_ref[0] & 1
    rows = own_ref.shape[0]
    acc[...] = begun_ref[...]
    add_products(chips_ref, begin, own_ref, mate_ref, refs[:count], weight_ref, acc, False)
    for side, cot_ref in enumerate((own_cot_ref, mate_cot_ref)):
        at = pl.multiple_of((core ^ side) * rows, rows)
        for head in range(own_cot_ref.shape[1] // HEAD_DIM):
            cols = slice(head * HEAD_DIM, (head + 1) * HEAD_DIM)
            proj = acc[side, :, cols]
            scale = jnp.sqrt(jnp.mean(proj * proj, axis=1, keepdims=True) + epsilon)
            normed = proj / scale
            upstream = cot_ref[:, cols].astype(jnp.float32)
            delta = (upstream - normed * jnp.mean(upstream * normed, axis=1, keepdims=True)) / scale
            delta_ref[pl.ds(at, rows), cols] = delta.astype(jnp.bfloat16)


def select_kernel(levels, me_ref, code_ref, *refs):
    deltas, sent_ref = refs[:-1], refs[-1]
    slot_count = sent_ref.shape[0]
    rows = code_ref.shape[1]
    plane = lax.shift_right_logical(me_ref[0], 3)
    per_chip = slot_count // (PLANE * len(deltas))
    iota = lax.broadcasted_iota(jnp.int32, (slot_count, rows), 0)
    destination, slot = iota // (per_chip * len(deltas)), iota % (per_chip * len(deltas))
    total = None
    for n, level in enumerate(levels):
        for side in range(2):
            want = (plane * PLANE + destination) * per_chip + slot - n * per_chip
            inside = (slot >= n * per_chip) & (slot < (n + 1) * per_chip)
            code = code_ref[2 * level + side : 2 * level + side + 1, :]
            hot = (inside & (want == code)).astype(jnp.bfloat16)
            part = dot(hot, deltas[n][side * rows : (side + 1) * rows, :], ((1,), (0,)))
            total = part if total is None else total + part
    sent_ref[...] = total.astype(jnp.bfloat16)


def weight_grad_kernel(begin, me_ref, own_ref, mate_ref, *refs):
    if begin:
        begun_ref, *deltas, part_ref, acc = refs
        acc[...] = begun_ref[...]
    else:
        *deltas, acc = refs
    core = me_ref[0] & 1
    rows = own_ref.shape[1]
    for n, delta_ref in enumerate(deltas):
        level = lax.shift_right_logical(me_ref[0], 3) ^ (begin + n)
        for side, ref in enumerate((own_ref, mate_ref)):
            at = pl.multiple_of((core ^ side) * rows, rows)
            part = dot(ref[level], delta_ref[pl.ds(at, rows), :], ((0,), (0,)))
            if begin + n + side == 0:
                acc[...] = part
            else:
                acc[...] += part
    if begin:
        part_ref[...] = acc[...].astype(jnp.bfloat16)


def sum_kernel(norm, parts_ref, grad_ref):
    half = parts_ref.shape[3]
    for side in range(2):
        total = parts_ref[0, side].astype(jnp.float32)
        for chip in range(1, parts_ref.shape[0]):
            total += parts_ref[chip, side].astype(jnp.float32)
        grad_ref[:, side * half : (side + 1) * half] = total / norm


def row_grad_kernel(me_ref, chips_ref, near_ref, far_ref, *refs):
    out_ref, rows_ref = refs[-2:]
    me = me_ref[0]
    step = pl.program_id(0)
    chips, _, count, _ = near_ref.shape
    depth = refs[0].shape[0]
    block = far_ref.shape[2]
    level = lax.shift_right_logical(me, 3)

    @pl.when(step == 0)
    def _():
        for n in range(count // block + 1):
            for chip in range(chips):
                at = pl.multiple_of(((level ^ n) * chips + chip) * block, block)
                for side in range(2):
                    if n < count // block:
                        rows = near_ref[chip, side, n * block : (n + 1) * block, :]
                    else:
                        rows = far_ref[chip, side]
                    rows_ref[side, pl.ds(at, block), :] = rows

    own, mate = rows_ref[me & 1], rows_ref[1 - (me & 1)]
    for n in range(2):
        total = dot(own, refs[2 * n][...], ((1,), (1,)))
        total += dot(mate, refs[2 * n + 1][...], ((1,), (1,)))
        at = chips_ref[n * pl.num_programs(0) + step] * depth
        out_ref[:, pl.ds(pl.multiple_of(at, depth), depth)] = total.astype(jnp.bfloat16)


def vmem(count):
    return [pl.BlockSpec(memory_space=pltpu.VMEM)] * count


SCALAR = pl.BlockSpec(memory_space=pltpu.SMEM)
PARAMS = pltpu.CompilerParams(vmem_limit_bytes=VMEM_LIMIT)


def cost(products, moved):
    return pl.CostEstimate(flops=2 * products, bytes_accessed=moved, transcendentals=0)


def per_device_paired(tokens, key_cot, routes, counts, widths, key_weight):
    rows, width_model = tokens.shape
    cols = key_cot.shape[1]
    half_cols = cols // 2
    size = lax.axis_size("dp")
    chips = size // 2
    levels = size // PLANE
    per_peer = 2 * rows // size
    receive = size * per_peer
    wide = width_model // levels
    me = lax.axis_index("dp")
    core = me % 2
    me_scalar = me.astype(jnp.int32).reshape(1)

    def mine(value):
        return lax.dynamic_slice_in_dim(value, core * half_cols, half_cols, 1)

    def theirs(value):
        return lax.dynamic_slice_in_dim(value, (1 - core) * half_cols, half_cols, 1)

    mate_shard = swap(key_weight, CORE)
    piece = jnp.where(
        core == 0,
        jnp.concatenate([key_weight[:, :half_cols], mate_shard[:, :half_cols]], axis=0),
        jnp.concatenate([mate_shard[:, half_cols:], key_weight[:, half_cols:]], axis=0),
    )
    near, far, both = PLANE, 2 * PLANE, 3 * PLANE
    z_far, z_near = swap(piece, far), swap(piece, near)
    x_own, y_own = swap(piece, X), swap(piece, Y)
    d_own = swap(y_own, X)
    z_far, z_near = lax.optimization_barrier((z_far, z_near, x_own, y_own))[:2]
    z_both = swap(z_far, near)
    x_near, y_near = swap(z_near, X), swap(z_near, Y)
    z_far = after(z_far, d_own)
    x_far, y_far = swap(z_far, X), swap(z_far, Y)
    z_both_late = after(z_both, x_near, y_near)
    x_both, y_both = swap(z_both_late, X), swap(z_both_late, Y)
    d_far = swap(x_far, Y)
    d_near = swap(after(y_near, x_both), X)
    first_pieces = {
        0: piece,
        X: x_own,
        Y: y_own,
        near: z_near,
        near | X: x_near,
        near | Y: y_near,
        far: z_far,
        far | X: x_far,
    }

    mate_tokens = swap(after(tokens, z_near), CORE)
    columns = [[p + PLANE * z for z in range(levels)] for p in range(PLANE)]
    late_tokens = after(tokens, z_both)
    own_features = lax.all_to_all(
        jnp.stack([late_tokens[:, z * wide : (z + 1) * wide] for z in range(levels)]),
        "dp",
        split_axis=0,
        concat_axis=0,
        axis_index_groups=columns,
        tiled=True,
    )
    mate_features = swap(own_features, CORE)

    key_cot, counts = lax.optimization_barrier((key_cot, counts, x_far, y_far))[:2]
    routes = after(routes, x_near, y_near)
    bounds = jnp.cumsum(counts[0])
    positions = jnp.arange(rows, dtype=jnp.int32)
    subnet = jnp.sum((positions[:, None] >= bounds[None, : NSUB - 1]).astype(jnp.int32), axis=1)
    subnet_match = subnet[:, None] == jnp.arange(NSUB, dtype=jnp.int32)[None, :]
    row_width = jnp.sum(jnp.where(subnet_match, widths[None, :], 0), axis=1)
    head_of_col = jnp.arange(cols, dtype=jnp.int32) // HEAD_DIM
    upstream = jnp.where(
        head_of_col[None, :] < row_width[:, None], key_cot, jnp.zeros_like(key_cot)
    )
    own_cot, mate_cot = mine(upstream), swap(theirs(upstream), CORE)

    destination = routes[:, 0]
    same = (destination[:, None] == destination[None, :]) & (
        positions[:, None] < positions[None, :]
    )
    earlier = jnp.sum(same.astype(jnp.int32), axis=0)
    code = ((destination * 2 + core) * per_peer + earlier).reshape(1, rows)
    mate_code = swap(code, CORE)
    codes = jnp.where(
        core == 0,
        jnp.concatenate([code, mate_code], axis=0),
        jnp.concatenate([mate_code, code], axis=0),
    )
    for bit in (near, far):
        codes = jnp.concatenate([codes, swap(codes, bit)], axis=0)

    kept = jax.ShapeDtypeStruct((width_model // 2, half_cols), jnp.bfloat16)
    sums = jax.ShapeDtypeStruct((2, rows, half_cols), jnp.float32)
    first_weight, begun = pl.pallas_call(
        functools.partial(project_kernel, len(first_pieces)),
        out_shape=(kept, sums),
        in_specs=[SCALAR] + vmem(2 + len(first_pieces)),
        out_specs=tuple(vmem(2)),
        compiler_params=PARAMS,
        cost_estimate=cost(2 * rows * width_model // 2 * half_cols, 6 << 20),
        name="project",
    )(
        jnp.stack([lax.shift_right_logical(me ^ mask, 1) for mask in first_pieces]),
        tokens,
        mate_tokens,
        *first_pieces.values(),
    )
    d_both = swap(after(x_both, begun), Y)
    last_pieces = {
        far | Y: y_far,
        X | Y: d_own,
        both: z_both,
        both | X: x_both,
        both | Y: y_both,
        near | X | Y: d_near,
        far | X | Y: d_far,
        both | X | Y: d_both,
    }
    order = jnp.stack(
        [lax.shift_right_logical(me ^ mask, 1) for mask in (*first_pieces, *last_pieces)]
    )
    begun = after(begun, codes, own_features, mate_features)
    delta, last_weight = pl.pallas_call(
        functools.partial(delta_kernel, len(last_pieces), len(first_pieces)),
        out_shape=(jax.ShapeDtypeStruct((2 * rows, half_cols), jnp.bfloat16), kept),
        in_specs=[SCALAR] * 2 + vmem(5 + len(last_pieces)),
        out_specs=tuple(vmem(2)),
        scratch_shapes=[pltpu.VMEM(sums.shape, sums.dtype)],
        compiler_params=PARAMS,
        cost_estimate=cost(2 * rows * width_model // 2 * half_cols, 6 << 20),
        name="delta",
    )(
        order,
        me_scalar,
        tokens,
        mate_tokens,
        own_cot,
        mate_cot,
        begun,
        *last_pieces.values(),
    )

    delta_far, delta_near = swap(delta, far), swap(delta, near)
    delta_both = swap(delta_far, near)
    planes = [[z * PLANE + p for p in range(PLANE)] for z in range(levels)]

    def to_plane(value):
        return lax.all_to_all(
            value.reshape(PLANE, -1, half_cols),
            "dp",
            split_axis=0,
            concat_axis=0,
            axis_index_groups=planes,
            tiled=True,
        )

    def select(codes, levels, deltas, name):
        return pl.pallas_call(
            functools.partial(select_kernel, levels),
            out_shape=jax.ShapeDtypeStruct(
                (PLANE * 2 * per_peer * len(deltas), half_cols), jnp.bfloat16
            ),
            in_specs=[SCALAR] + vmem(1 + len(deltas)),
            out_specs=vmem(1)[0],
            compiler_params=PARAMS,
            cost_estimate=cost(receive * len(deltas) * 2 * rows * half_cols, 2 << 20),
            name=name,
        )(me_scalar, codes, *deltas)

    near_deltas = [delta, delta_near, delta_far]
    selected = select(codes, (0, 1, 2), near_deltas, "select_near")
    got_near = to_plane(selected)

    ready = after(delta, selected)
    terms = jax.ShapeDtypeStruct((wide, half_cols), jnp.float32)
    begun_terms = pl.pallas_call(
        functools.partial(weight_grad_kernel, 0),
        out_shape=terms,
        in_specs=[SCALAR] + vmem(5),
        out_specs=vmem(1)[0],
        compiler_params=PARAMS,
        cost_estimate=cost(6 * rows * wide * half_cols, 4 << 20),
        name="weight_grad_near",
    )(me_scalar, own_features, mate_features, ready, delta_near, delta_far)
    delta_both = after(delta_both, begun_terms)
    part = pl.pallas_call(
        functools.partial(weight_grad_kernel, 3),
        out_shape=jax.ShapeDtypeStruct(terms.shape, jnp.bfloat16),
        in_specs=[SCALAR] + vmem(4),
        out_specs=vmem(1)[0],
        scratch_shapes=[pltpu.VMEM(terms.shape, terms.dtype)],
        compiler_params=PARAMS,
        cost_estimate=cost(2 * rows * wide * half_cols, 4 << 20),
        name="weight_grad",
    )(me_scalar, own_features, mate_features, begun_terms, delta_both)
    parts = to_plane(part)
    got_both = to_plane(select(after(codes, part), (3,), [delta_both], "select_far"))
    shard = width_model // size

    depth = width_model // chips
    kept_weights = [first_weight, swap(first_weight, CORE), last_weight, swap(last_weight, CORE)]
    row_grads = pl.pallas_call(
        row_grad_kernel,
        out_shape=jax.ShapeDtypeStruct((receive, width_model), jnp.bfloat16),
        grid=(chips // 2,),
        in_specs=[SCALAR] * 2
        + [
            pl.BlockSpec((PLANE // 2, 2, 2 * per_peer * n, half_cols), lambda i: (0, 0, 0, 0))
            for n in (levels - 1, 1)
        ]
        + [pl.BlockSpec((depth, half_cols), lambda i: (i, 0))] * len(kept_weights),
        out_specs=pl.BlockSpec((receive, width_model), lambda i: (0, 0)),
        scratch_shapes=[pltpu.VMEM((2, receive, half_cols), jnp.bfloat16)],
        compiler_params=PARAMS,
        cost_estimate=cost(receive * width_model * cols, 12 << 20),
        name="row_grad",
    )(
        me_scalar,
        order,
        got_near.reshape(PLANE // 2, 2, -1, half_cols),
        got_both.reshape(PLANE // 2, 2, -1, half_cols),
        *kept_weights,
    )

    parts = after(parts, row_grads)
    key_grad = pl.pallas_call(
        functools.partial(sum_kernel, math.sqrt(rows * size)),
        out_shape=jax.ShapeDtypeStruct((shard, cols), jnp.float32),
        in_specs=vmem(1),
        out_specs=vmem(1)[0],
        compiler_params=PARAMS,
        cost_estimate=cost(PLANE * shard * half_cols, 2 << 20),
        name="sum",
    )(parts.reshape(PLANE // 2, 2, shard, half_cols))
    return (row_grads, key_grad)


def solution(mesh):
    size, split = mesh.shape["dp"], mesh.shape["mp"]
    paired = split == 1 and size == 32
    return jax.shard_map(
        per_device_paired if paired else per_device_general,
        mesh=mesh,
        in_specs=(P("dp", None), P("dp", "mp"), P("dp", None), P("dp", None), P(), P("dp", "mp")),
        out_specs=(P("dp", "mp"), P("dp", "mp")),
        check_vma=False,
    )
```

time: 144 us -> 147 us (1.021)
  blocking collectives: 0 us -> 9.2 us
  starting transfers between devices: 45.3 us -> 39.3 us
  other arithmetic: 4.53 us -> 2.45 us
  waiting for transfers between devices: 57 us -> 58.7 us
    all_to_all x0 -> x1, blocking collectives: none -> 9.2 us  [to_plane(): lax.all_to_all(value.reshape(PLANE, -1, half_cols), 'dp', split_axis=0, c...]
    ppermute x31 -> x27, waiting for transfers between devices: 44.5 us -> 52.1 us  [swap(): return lax.ppermute(value, 'dp', [(i, i ^ mask) for i in range(size)])]
    slice x8 -> x0, local copies, waits for them, and re-layouts: 6.81 us -> none  [diagonal(): return (swap(by_y[:half], X), swap(by_x[half:], Y))]
    ppermute x31 -> x27, starting transfers between devices: 33.8 us -> 28.5 us  [swap(): return lax.ppermute(value, 'dp', [(i, i ^ mask) for i in range(size)])]
    unnamed x34 -> x40, local copies, waits for them, and re-layouts: 4.53 us -> 9.8 us
    all_to_all x2, waiting for transfers between devices: 9.44 us -> 5.27 us  [to_plane(): lax.all_to_all(value.reshape(PLANE, -1, half_cols), 'dp', split_axis=0, c...]
    all_to_all x1, waiting for transfers between devices: 3.02 us -> 1.38 us  [per_device_paired(): lax.all_to_all(jnp.stack([late_tokens[:, z * wide:(z + 1) * wide] for z i...]
    pallas_call x5 -> x7, Pallas kernels: 21.8 us -> 22.5 us  [the longest x1 8.45 us: per_device_paired(): pl.pallas_call(row_grad_kernel, out_shape=jax.ShapeDtypeStruct((receive,...]
  transfers between devices with their start and end apart: 34 -> 30, of which waited for: 18 -> 18; matrix products, arithmetic and copies ran while one was open for 8% -> 2% of each run, Pallas kernels for 15% -> 15%
where the time goes in v6:
time: 147 us; the launch traced here: 146 us
  waiting for transfers between devices  58.7 us (40%)
  starting transfers between devices  39.3 us (27%)
  Pallas kernels  23.4 us (16%)
  local copies, waits for them, and re-layouts  11.7 us (8%)
  blocking collectives  9.2 us (6%)
  other arithmetic  2.45 us (2%)
    ppermute x27, waiting for transfers between devices, swap(): return lax.ppermute(value, 'dp', [(i, i ^ mask) for i in range(size)])  52.1 us
    ppermute x27, starting transfers between devices, swap(): return lax.ppermute(value, 'dp', [(i, i ^ mask) for i in range(size)])  28.5 us
    unnamed x40, local copies, waits for them, and re-layouts  9.8 us
    all_to_all x1, blocking collectives, to_plane(): lax.all_to_all(value.reshape(PLANE, -1, half_cols), 'dp', split_axis=0, c...  9.2 us
    pallas_call x1, Pallas kernels, per_device_paired(): pl.pallas_call(row_grad_kernel, out_shape=jax.ShapeDtypeStruct((receive,...  8.45 us
    all_to_all x2, starting transfers between devices, to_plane(): lax.all_to_all(value.reshape(PLANE, -1, half_cols), 'dp', split_axis=0, c...  7.01 us
    all_to_all x2, waiting for transfers between devices, to_plane(): lax.all_to_all(value.reshape(PLANE, -1, half_cols), 'dp', split_axis=0, c...  5.27 us
    all_to_all x1, starting transfers between devices, per_device_paired(): lax.all_to_all(jnp.stack([late_tokens[:, z * wide:(z + 1) * wide] for z i...  3.83 us
  transfers between devices with their start and end apart: 30, of which 18 were waited for; matrix products, arithmetic and copies ran while one was open for 2% of the time, Pallas kernels for 15%

profile of v6, /device:TPU:0, one launch (start us, length us, event | category | flops | bytes accessed | tf_op | source)
XLA Modules:
  0.0 145.7 jit_solution(3594604244077464574)
XLA Ops:
  1.2 1.0 fusion.5
  2.6 3.0 %collective-permute-start.4 = (bf16[256,512]{1,0:T(8,128)(2,1)S(1)}, bf16[256,512]{1,0:T(8,128)(2,1)S(1)}, u32[]{:S(2)}, u32[]{:S(2)}) collective-permute-start(bf16[256,512]{1,0:T(8,128)(2,1)S(1)} %maximum_select_fusion.refs_0_), channel_id=1, source_target_pairs={{0,4},{1,5},{2,6},{3,7},{4,0},{5,1},{6,2},{7,3},{8,12},{9,13},{10,... | collective-permute-start | bytes 786440 | tf_op jit(solution)/shard_map/ppermute | solution.py:90
  5.6 1.5 %collective-permute-start.3 = (bf16[256,512]{1,0:T(8,128)(2,1)S(1)}, bf16[256,512]{1,0:T(8,128)(2,1)S(1)}, u32[]{:S(2)}, u32[]{:S(2)}) collective-permute-start(bf16[256,512]{1,0:T(8,128)(2,1)S(1)} %maximum_select_fusion.refs_0_), channel_id=1, source_target_pairs={{0,2},{1,3},{2,0},{3,1},{4,6},{5,7},{6,4},{7,5},{8,10},{9,11},{10,... | collective-permute-start | bytes 786440 | tf_op jit(solution)/shard_map/ppermute | solution.py:90
  7.1 1.6 %collective-permute-start.2 = (bf16[256,512]{1,0:T(8,128)(2,1)S(1)}, bf16[256,512]{1,0:T(8,128)(2,1)}, u32[]{:S(2)}, u32[]{:S(2)}) collective-permute-start(bf16[256,512]{1,0:T(8,128)(2,1)S(1)} %maximum_select_fusion.refs_0_), channel_id=1, source_target_pairs={{0,8},{1,9},{2,10},{3,11},{4,12},{5,13},{6,14},{7,15},{8,0},{9,1},... | collective-permute-start | bytes 786440 | tf_op jit(solution)/shard_map/ppermute | solution.py:90
  8.6 2.6 %collective-permute-start.1 = (bf16[256,512]{1,0:T(8,128)(2,1)S(1)}, bf16[256,512]{1,0:T(8,128)(2,1)S(1)}, u32[]{:S(2)}, u32[]{:S(2)}) collective-permute-start(bf16[256,512]{1,0:T(8,128)(2,1)S(1)} %maximum_select_fusion.refs_0_), channel_id=1, source_target_pairs={{0,16},{1,17},{2,18},{3,19},{4,20},{5,21},{6,22},{7,23},{8,24},{9,... | collective-permute-start | bytes 786440 | tf_op jit(solution)/shard_map/ppermute | solution.py:90
  11.2 0.9 collective-permute-done.4.refs_2_
  12.2 1.5 %collective-permute-done.3.refs_1_ = bf16[256,512]{1,0:T(8,128)(2,1)S(1)} collective-permute-done((bf16[256,512]{1,0:T(8,128)(2,1)S(1)}, bf16[256,512]{1,0:T(8,128)(2,1)S(1)}, u32[]{:S(2)}, u32[]{:S(2)}) %collective-permute-start.3) | collective-permute-done | bytes 262176 | tf_op jit(solution)/shard_map/ppermute | solution.py:90
  13.6 6.8 %collective-permute-done.2.refs_3_ = bf16[256,512]{1,0:T(8,128)(2,1)} collective-permute-done((bf16[256,512]{1,0:T(8,128)(2,1)S(1)}, bf16[256,512]{1,0:T(8,128)(2,1)}, u32[]{:S(2)}, u32[]{:S(2)}) %collective-permute-start.2) | collective-permute-done | bytes 262176 | tf_op jit(solution)/shard_map/ppermute | solution.py:90
  20.5 2.3 %collective-permute-done.1.refs_6_ = bf16[256,512]{1,0:T(8,128)(2,1)S(1)} collective-permute-done((bf16[256,512]{1,0:T(8,128)(2,1)S(1)}, bf16[256,512]{1,0:T(8,128)(2,1)S(1)}, u32[]{:S(2)}, u32[]{:S(2)}) %collective-permute-start.1) | collective-permute-done | bytes 262176 | tf_op jit(solution)/shard_map/ppermute | solution.py:90
  23.2 5.9 %collective-permute-done.15.refs_2_ = bf16[256,512]{1,0:T(8,128)(2,1)S(1)} collective-permute-done((bf16[256,512]{1,0:T(8,128)(2,1)S(1)}, bf16[256,512]{1,0:T(8,128)(2,1)S(1)}, u32[]{:S(2)}, u32[]{:S(2)}) %collective-permute-start.15) | collective-permute-done | bytes 262176 | tf_op jit(solution)/shard_map/ppermute | solution.py:90
  29.2 1.1 pad_maximum_fusion
  30.3 3.8 %all-to-all-start = ((bf16[4,128,1024]{2,1,0:T(8,128)(2,1)}), bf16[4,128,1024]{2,1,0:T(8,128)(2,1)S(1)}, u32[]{:S(2)}, u32[]{:S(2)}) async-start(bf16[4,128,1024]{2,1,0:T(8,128)(2,1)} %pad_maximum_fusion), calls=%async_computation | async-start | bytes 2097152 | tf_op jit(solution)/shard_map/all_to_all | solution.py:293
  35.2 1.5 %collective-permute-start.11 = (bf16[256,512]{1,0:T(8,128)(2,1)}, bf16[256,512]{1,0:T(8,128)(2,1)S(1)}, u32[]{:S(2)}, u32[]{:S(2)}) collective-permute-start(bf16[256,512]{1,0:T(8,128)(2,1)} %copy-done.4), channel_id=1, source_target_pairs={{0,2},{1,3},{2,0},{3,1},{4,6},{5,7},{6,4},{7,5},{8,10},{9,11},{10,... | collective-permute-start | bytes 786440 | tf_op jit(solution)/shard_map/ppermute | solution.py:90
  36.7 4.2 %collective-permute-done.6.refs_5_ = bf16[256,512]{1,0:T(8,128)(2,1)} collective-permute-done((bf16[256,512]{1,0:T(8,128)(2,1)}, bf16[256,512]{1,0:T(8,128)(2,1)}, u32[]{:S(2)}, u32[]{:S(2)}) %collective-permute-start.6) | collective-permute-done | bytes 262176 | tf_op jit(solution)/shard_map/ppermute | solution.py:90
  40.9 3.2 %collective-permute-done.5.refs_4_ = bf16[256,512]{1,0:T(8,128)(2,1)} collective-permute-done((bf16[256,512]{1,0:T(8,128)(2,1)}, bf16[256,512]{1,0:T(8,128)(2,1)}, u32[]{:S(2)}, u32[]{:S(2)}) %collective-permute-start.5) | collective-permute-done | bytes 262176 | tf_op jit(solution)/shard_map/ppermute | solution.py:90
  44.3 2.6 %collective-permute-done.11.refs_1_ = bf16[256,512]{1,0:T(8,128)(2,1)S(1)} collective-permute-done((bf16[256,512]{1,0:T(8,128)(2,1)}, bf16[256,512]{1,0:T(8,128)(2,1)S(1)}, u32[]{:S(2)}, u32[]{:S(2)}) %collective-permute-start.11) | collective-permute-done | bytes 262176 | tf_op jit(solution)/shard_map/ppermute | solution.py:90
  47.6 1.5 %collective-permute-start.13 = (bf16[256,512]{1,0:T(8,128)(2,1)}, bf16[256,512]{1,0:T(8,128)(2,1)}, u32[]{:S(2)}, u32[]{:S(2)}) collective-permute-start(bf16[256,512]{1,0:T(8,128)(2,1)} %copy-done.8), channel_id=1, source_target_pairs={{0,4},{1,5},{2,6},{3,7},{4,0},{5,1},{6,2},{7,3},{8,12},{9,13},{10,... | collective-permute-start | bytes 786440 | tf_op jit(solution)/shard_map/ppermute | solution.py:90
  49.7 1.5 %collective-permute-start.17 = (bf16[256,512]{1,0:T(8,128)(2,1)}, bf16[256,512]{1,0:T(8,128)(2,1)}, u32[]{:S(2)}, u32[]{:S(2)}) collective-permute-start(bf16[256,512]{1,0:T(8,128)(2,1)} %copy-done.10), channel_id=1, source_target_pairs={{0,2},{1,3},{2,0},{3,1},{4,6},{5,7},{6,4},{7,5},{8,10},{9,11},{10,... | collective-permute-start | bytes 786440 | tf_op jit(solution)/shard_map/ppermute | solution.py:90
  51.2 2.1 %collective-permute-start.8 = (s32[2,128]{1,0:T(2,128)S(1)}, s32[2,128]{1,0:T(2,128)S(1)}, u32[]{:S(2)}, u32[]{:S(2)}) collective-permute-start(s32[2,128]{1,0:T(2,128)S(1)} %add_select_fusion.1), channel_id=1, source_target_pairs={{0,8},{1,9},{2,10},{3,11},{4,12},{5,13},{6,14},{7,15},{8,0},{9,1},... | collective-permute-start | bytes 3080 | tf_op jit(solution)/shard_map/ppermute | solution.py:90
  53.3 1.6 %collective-permute-done.8 = s32[2,128]{1,0:T(2,128)S(1)} collective-permute-done((s32[2,128]{1,0:T(2,128)S(1)}, s32[2,128]{1,0:T(2,128)S(1)}, u32[]{:S(2)}, u32[]{:S(2)}) %collective-permute-start.8) | collective-permute-done | bytes 1056 | tf_op jit(solution)/shard_map/ppermute | solution.py:90
  54.9 1.4 all-to-all-done.own_ref
  56.9 1.2 collective-permute-done.12.refs_7_
  58.1 2.9 %collective-permute-start.9 = (s32[4,128]{1,0:T(4,128)S(1)}, s32[4,128]{1,0:T(4,128)}, u32[]{:S(2)}, u32[]{:S(2)}) collective-permute-start(s32[4,128]{1,0:T(4,128)S(1)} %pad_add_fusion.1), channel_id=1, source_target_pairs={{0,16},{1,17},{2,18},{3,19},{4,20},{5,21},{6,22},{7,23},{8,24},{9,... | collective-permute-start | bytes 6152 | tf_op jit(solution)/shard_map/ppermute | solution.py:90
  61.2 1.0 collective-permute-start.19
  62.9 0.9 copy-done.5
  63.9 0.9 copy-done.7
  64.8 0.9 copy-done.9
  65.8 3.1 %project.1 = (bf16[2048,512]{1,0:T(8,128)(2,1)}, f32[2,128,512]{2,1,0:T(8,128)S(1)}) custom-call(s32[8]{0:T(128)S(1)} %stack.94.chips_ref, bf16[128,4096]{1,0:T(8,128)(2,1)S(1)} %copy-done, bf16[128,4096]{1,0:T(8,128)(2,1)S(1)} %collective-permute-done.10.mate_ref, bf16[256,512]{1,0:T(8,128)(2,1)S(1)} %maximum_select_fusion.refs_0_, ...), custom_call_target="tpu_custom_call" | custom-call | flops 536870912 | bytes 6291456 | tf_op jit(solution)/shard_map/project/pallas_call | solution.py:333
  68.8 1.5 %collective-permute-start.21 = (bf16[256,512]{1,0:T(8,128)(2,1)}, bf16[256,512]{1,0:T(8,128)(2,1)S(1)}, u32[]{:S(2)}, u32[]{:S(2)}) collective-permute-start(bf16[256,512]{1,0:T(8,128)(2,1)} %collective-permute-done.17.refs_3_), channel_id=1, source_target_pairs={{0,4},{1,5},{2,6},{3,7},{4,0},{5,1},{6,2},{7,3},{8,12},{9,13},{10,... | collective-permute-start | bytes 786440 | tf_op jit(solution)/shard_map/ppermute | solution.py:90
  72.8 3.7 %collective-permute-done.21.refs_7_ = bf16[256,512]{1,0:T(8,128)(2,1)S(1)} collective-permute-done((bf16[256,512]{1,0:T(8,128)(2,1)}, bf16[256,512]{1,0:T(8,128)(2,1)S(1)}, u32[]{:S(2)}, u32[]{:S(2)}) %collective-permute-start.21) | collective-permute-done | bytes 262176 | tf_op jit(solution)/shard_map/ppermute | solution.py:90
  77.3 1.0 copy-done.3
  78.3 0.9 copy-done.11
  79.3 0.9 copy-done.13
  80.2 0.9 copy-done.15
  81.1 3.2 %delta.1 = (bf16[256,512]{1,0:T(8,128)(2,1)S(1)}, bf16[2048,512]{1,0:T(8,128)(2,1)}) custom-call(s32[16]{0:T(128)S(1)} %stack.93.chips_ref, s32[1]{0:T(128)} %bitcast.me_ref, bf16[128,4096]{1,0:T(8,128)(2,1)S(1)} %copy-done, bf16[128,4096]{1,0:T(8,128)(2,1)S(1)} %collective-permute-done.10.mate_ref, bf16[128,512]{1,0:T(8,128)(2,1)S(1)} %get-tuple-element.47.own_cot_ref, ...), custom_call_target="tpu_custom_call" | custom-call | flops 536870912 | bytes 6291456 | tf_op jit(solution)/shard_map/delta/pallas_call | solution.py:362
  84.4 1.5 %collective-permute-start.23 = (bf16[256,512]{1,0:T(8,128)(2,1)S(1)}, bf16[256,512]{1,0:T(8,128)(2,1)S(1)}, u32[]{:S(2)}, u32[]{:S(2)}) collective-permute-start(bf16[256,512]{1,0:T(8,128)(2,1)S(1)} %get-tuple-element.36.refs_0_), channel_id=1, source_target_pairs={{0,16},{1,17},{2,18},{3,19},{4,20},{5,21},{6,22},{7,23},{8,24},{9,... | collective-permute-start | bytes 786440 | tf_op jit(solution)/shard_map/ppermute | solution.py:90
  85.8 1.5 %collective-permute-start.22 = (bf16[256,512]{1,0:T(8,128)(2,1)S(1)}, bf16[256,512]{1,0:T(8,128)(2,1)S(1)}, u32[]{:S(2)}, u32[]{:S(2)}) collective-permute-start(bf16[256,512]{1,0:T(8,128)(2,1)S(1)} %get-tuple-element.36.refs_0_), channel_id=1, source_target_pairs={{0,8},{1,9},{2,10},{3,11},{4,12},{5,13},{6,14},{7,15},{8,0},{9,1},... | collective-permute-start | bytes 786440 | tf_op jit(solution)/shard_map/ppermute | solution.py:90
  87.3 12.4 %collective-permute-done.23.refs_2_ = bf16[256,512]{1,0:T(8,128)(2,1)S(1)} collective-permute-done((bf16[256,512]{1,0:T(8,128)(2,1)S(1)}, bf16[256,512]{1,0:T(8,128)(2,1)S(1)}, u32[]{:S(2)}, u32[]{:S(2)}) %collective-permute-start.23) | collective-permute-done | bytes 262176 | tf_op jit(solution)/shard_map/ppermute | solution.py:90
  99.8 1.5 %select_near.1 = bf16[384,512]{1,0:T(8,128)(2,1)} custom-call(s32[1]{0:T(128)} %bitcast.me_ref, s32[8,128]{1,0:T(8,128)S(1)} %pad_add_fusion.code_ref, bf16[256,512]{1,0:T(8,128)(2,1)S(1)} %get-tuple-element.36.refs_0_, bf16[256,512]{1,0:T(8,128)(2,1)S(1)} %collective-permute-done.22.refs_1_, bf16[256,512]{1,0:T(8,128)(2,1)S(1)} %collective-permute-done.23.refs_2_), custom_call_target="tpu_custom_call" | custom-call | flops 201326592 | bytes 2097152 | tf_op jit(solution)/shard_map/select_near/pallas_call | solution.py:397
  101.3 3.5 %all-to-all-start.1 = ((bf16[8,48,512]{2,1,0:T(8,128)(2,1)}), bf16[8,48,512]{2,1,0:T(8,128)(2,1)S(1)}, u32[]{:S(2)}, u32[]{:S(2)}) async-start(bf16[8,48,512]{2,1,0:T(8,128)(2,1)} %bitcast.26), calls=%async_computation.1 | async-start | bytes 786432 | tf_op jit(solution)/shard_map/all_to_all | solution.py:387
  105.4 3.0 %weight_grad_near.1.refs_0_ = f32[1024,512]{1,0:T(8,128)S(1)} custom-call(s32[1]{0:T(128)} %bitcast.me_ref, bf16[4,128,1024]{2,1,0:T(8,128)(2,1)S(1)} %all-to-all-done.own_ref, bf16[4,128,1024]{2,1,0:T(8,128)(2,1)} %collective-permute-done.16.mate_ref, bf16[256,512]{1,0:T(8,128)(2,1)S(1)} %get-tuple-element.36.refs_0_, ...), custom_call_target="tpu_custom_call" | custom-call | flops 805306368 | bytes 4194304 | tf_op jit(solution)/shard_map/weight_grad_near/pallas_call | solution.py:415
  108.4 5.0 %collective-permute-done.24.refs_1_.refs_0_ = bf16[256,512]{1,0:T(8,128)(2,1)S(1)} collective-permute-done((bf16[256,512]{1,0:T(8,128)(2,1)S(1)}, bf16[256,512]{1,0:T(8,128)(2,1)S(1)}, u32[]{:S(2)}, u32[]{:S(2)}) %collective-permute-start.24) | collective-permute-done | bytes 262176 | tf_op jit(solution)/shard_map/ppermute | solution.py:90
  113.4 3.0 %weight_grad.1 = bf16[1024,512]{1,0:T(8,128)(2,1)} custom-call(s32[1]{0:T(128)} %bitcast.me_ref, bf16[4,128,1024]{2,1,0:T(8,128)(2,1)S(1)} %all-to-all-done.own_ref, bf16[4,128,1024]{2,1,0:T(8,128)(2,1)} %collective-permute-done.16.mate_ref, f32[1024,512]{1,0:T(8,128)S(1)} %weight_grad_near.1.refs_0_, ...), custom_call_target="tpu_custom_call" | custom-call | flops 268435456 | bytes 4194304 | tf_op jit(solution)/shard_map/weight_grad/pallas_call | solution.py:425
  116.6 9.2 %all_to_all.20 = bf16[8,16,512]{2,1,0:T(8,128)(2,1)S(1)} all-to-all(bf16[8,16,512]{2,1,0:T(8,128)(2,1)S(1)} %bitcast.42), channel_id=1, replica_groups={{0,1,2,3,4,5,6,7},{8,9,10,11,12,13,14,15},{16,17,18,19,20,21,22,23},{24..., dimensions={0} | all-to-all | bytes 262144 | tf_op jit(solution)/shard_map/all_to_all | solution.py:387
  125.8 3.6 %all-to-all-start.3 = ((bf16[8,128,512]{2,1,0:T(8,128)(2,1)}), bf16[8,128,512]{2,1,0:T(8,128)(2,1)S(1)}, u32[]{:S(2)}, u32[]{:S(2)}) async-start(bf16[8,128,512]{2,1,0:T(8,128)(2,1)} %bitcast.30), calls=%async_computation.3 | async-start | bytes 2097152 | tf_op jit(solution)/shard_map/all_to_all | solution.py:387
  129.4 1.6 %copy-done.1 = bf16[2048,512]{1,0:T(8,128)(2,1)S(1)} copy-done((bf16[2048,512]{1,0:T(8,128)(2,1)S(1)}, bf16[2048,512]{1,0:T(8,128)(2,1)}, u32[]{:S(2)}) %copy-start.1) | copy-done | bytes 2097176
  131.0 8.5 %row_grad.1 = bf16[256,4096]{1,0:T(8,128)(2,1)} custom-call(s32[1]{0:T(128)} %bitcast.me_ref, s32[16]{0:T(128)S(1)} %stack.93.chips_ref, bf16[4,2,48,512]{3,2,1,0:T(8,128)(2,1)S(1)} %bitcast.40, bf16[4,2,16,512]{3,2,1,0:T(8,128)(2,1)S(1)} %bitcast.41, bf16[2048,512]{1,0:T(8,128)(2,1)S(1)} %copy-done.1, bf16[2048,512]{1,0:T(8,128)(2,1)} %collective-permute-done.25.refs_1_, ...), custom_call_target="tpu_custom_call" | custom-call | flops 2147483648 | bytes 12582912 | tf_op jit(solution)/shard_map/row_grad/pallas_call | solution.py:441
  139.5 5.3 %all-to-all-done.3 = bf16[8,128,512]{2,1,0:T(8,128)(2,1)S(1)} async-done(((bf16[8,128,512]{2,1,0:T(8,128)(2,1)}), bf16[8,128,512]{2,1,0:T(8,128)(2,1)S(1)}, u32[]{:S(2)}, u32[]{:S(2)}) %all-to-all-start.3) | async-done | bytes 1048608 | tf_op jit(solution)/shard_map/all_to_all | solution.py:387
  (80 shorter events, 10.7 us)
Async XLA Ops:
  0.6 28.5 %copy-start = (bf16[128,4096]{1,0:T(8,128)(2,1)S(1)}, bf16[128,4096]{1,0:T(8,128)(2,1)}, u32[]{:S(2)}) copy-start(bf16[128,4096]{1,0:T(8,128)(2,1)} %own_ref.3) | copy-start | bytes 3145732
  0.6 1.9 %collective-permute-start = (bf16[128,1024]{1,0:T(8,128)(2,1)}, bf16[128,1024]{1,0:T(8,128)(2,1)S(1)}, u32[]{:S(2)}, u32[]{:S(2)}) collective-permute-start(bf16[128,1024]{1,0:T(8,128)(2,1)} %param.11), channel_id=1, source_target_pairs={{0,1},{1,0},{2,3},{3,2},{4,5},{5,4},{6,7},{7,6},{8,9},{9,8},{10,11... | collective-permute-start | bytes 786440 | tf_op jit(solution)/shard_map/ppermute | solution.py:90
  2.6 9.6 %collective-permute-start.4 = (bf16[256,512]{1,0:T(8,128)(2,1)S(1)}, bf16[256,512]{1,0:T(8,128)(2,1)S(1)}, u32[]{:S(2)}, u32[]{:S(2)}) collective-permute-start(bf16[256,512]{1,0:T(8,128)(2,1)S(1)} %maximum_select_fusion.refs_0_), channel_id=1, source_target_pairs={{0,4},{1,5},{2,6},{3,7},{4,0},{5,1},{6,2},{7,3},{8,12},{9,13},{10,... | collective-permute-start | bytes 786440 | tf_op jit(solution)/shard_map/ppermute | solution.py:90
  5.6 8.1 %collective-permute-start.3 = (bf16[256,512]{1,0:T(8,128)(2,1)S(1)}, bf16[256,512]{1,0:T(8,128)(2,1)S(1)}, u32[]{:S(2)}, u32[]{:S(2)}) collective-permute-start(bf16[256,512]{1,0:T(8,128)(2,1)S(1)} %maximum_select_fusion.refs_0_), channel_id=1, source_target_pairs={{0,2},{1,3},{2,0},{3,1},{4,6},{5,7},{6,4},{7,5},{8,10},{9,11},{10,... | collective-permute-start | bytes 786440 | tf_op jit(solution)/shard_map/ppermute | solution.py:90
  7.1 13.4 %collective-permute-start.2 = (bf16[256,512]{1,0:T(8,128)(2,1)S(1)}, bf16[256,512]{1,0:T(8,128)(2,1)}, u32[]{:S(2)}, u32[]{:S(2)}) collective-permute-start(bf16[256,512]{1,0:T(8,128)(2,1)S(1)} %maximum_select_fusion.refs_0_), channel_id=1, source_target_pairs={{0,8},{1,9},{2,10},{3,11},{4,12},{5,13},{6,14},{7,15},{8,0},{9,1},... | collective-permute-start | bytes 786440 | tf_op jit(solution)/shard_map/ppermute | solution.py:90
  8.6 14.1 %collective-permute-start.1 = (bf16[256,512]{1,0:T(8,128)(2,1)S(1)}, bf16[256,512]{1,0:T(8,128)(2,1)S(1)}, u32[]{:S(2)}, u32[]{:S(2)}) collective-permute-start(bf16[256,512]{1,0:T(8,128)(2,1)S(1)} %maximum_select_fusion.refs_0_), channel_id=1, source_target_pairs={{0,16},{1,17},{2,18},{3,19},{4,20},{5,21},{6,22},{7,23},{8,24},{9,... | collective-permute-start | bytes 786440 | tf_op jit(solution)/shard_map/ppermute | solution.py:90
  12.2 18.2 %copy-start.4 = (bf16[256,512]{1,0:T(8,128)(2,1)}, bf16[256,512]{1,0:T(8,128)(2,1)S(1)}, u32[]{:S(2)}) copy-start(bf16[256,512]{1,0:T(8,128)(2,1)S(1)} %collective-permute-done.4.refs_2_) | copy-start | bytes 786436
  13.6 16.7 %copy-start.6 = (bf16[256,512]{1,0:T(8,128)(2,1)}, bf16[256,512]{1,0:T(8,128)(2,1)S(1)}, u32[]{:S(2)}) copy-start(bf16[256,512]{1,0:T(8,128)(2,1)S(1)} %collective-permute-done.3.refs_1_) | copy-start | bytes 786436
  22.7 7.6 %copy-start.8 = (bf16[256,512]{1,0:T(8,128)(2,1)}, bf16[256,512]{1,0:T(8,128)(2,1)S(1)}, u32[]{:S(2)}) copy-start(bf16[256,512]{1,0:T(8,128)(2,1)S(1)} %collective-permute-done.1.refs_6_) | copy-start | bytes 786436
  22.7 6.4 %collective-permute-start.15 = (bf16[256,512]{1,0:T(8,128)(2,1)S(1)}, bf16[256,512]{1,0:T(8,128)(2,1)S(1)}, u32[]{:S(2)}, u32[]{:S(2)}) collective-permute-start(bf16[256,512]{1,0:T(8,128)(2,1)S(1)} %collective-permute-done.1.refs_6_), channel_id=1, source_target_pairs={{0,8},{1,9},{2,10},{3,11},{4,12},{5,13},{6,14},{7,15},{8,0},{9,1},... | collective-permute-start | bytes 786440 | tf_op jit(solution)/shard_map/ppermute | solution.py:90
  29.1 1.2 copy-start.10
  29.2 14.9 %copy-start.17 = (s32[128,1]{0,1:T(1,128)S(1)}, s32[128,1]{0,1:T(1,128)}, u32[]{:S(2)}) copy-start(s32[128,1]{0,1:T(1,128)} %param.8) | copy-start | bytes 1540
  29.2 31.8 %copy-start.18 = (s32[1,4]{1,0:T(1,128)S(1)}, s32[1,4]{1,0:T(1,128)}, u32[]{:S(2)}) copy-start(s32[1,4]{1,0:T(1,128)} %param.9) | copy-start | bytes 52
  29.2 33.0 %copy-start.19 = (s32[4]{0:T(128)S(1)}, s32[4]{0:T(128)}, u32[]{:S(2)}) copy-start(s32[4]{0:T(128)} %param.10) | copy-start | bytes 52
  30.3 25.9 %all-to-all-start = ((bf16[4,128,1024]{2,1,0:T(8,128)(2,1)}), bf16[4,128,1024]{2,1,0:T(8,128)(2,1)S(1)}, u32[]{:S(2)}, u32[]{:S(2)}) async-start(bf16[4,128,1024]{2,1,0:T(8,128)(2,1)} %pad_maximum_fusion), calls=%async_computation | async-start | bytes 2097152 | tf_op jit(solution)/shard_map/all_to_all | solution.py:293
  34.2 6.7 %collective-permute-start.6 = (bf16[256,512]{1,0:T(8,128)(2,1)}, bf16[256,512]{1,0:T(8,128)(2,1)}, u32[]{:S(2)}, u32[]{:S(2)}) collective-permute-start(bf16[256,512]{1,0:T(8,128)(2,1)} %collective-permute-done.2.refs_3_), channel_id=1, source_target_pairs={{0,4},{1,5},{2,6},{3,7},{4,0},{5,1},{6,2},{7,3},{8,12},{9,13},{10,... | collective-permute-start | bytes 786440 | tf_op jit(solution)/shard_map/ppermute | solution.py:90
  34.7 9.4 %collective-permute-start.5 = (bf16[256,512]{1,0:T(8,128)(2,1)}, bf16[256,512]{1,0:T(8,128)(2,1)}, u32[]{:S(2)}, u32[]{:S(2)}) collective-permute-start(bf16[256,512]{1,0:T(8,128)(2,1)} %collective-permute-done.2.refs_3_), channel_id=1, source_target_pairs={{0,2},{1,3},{2,0},{3,1},{4,6},{5,7},{6,4},{7,5},{8,10},{9,11},{10,... | collective-permute-start | bytes 786440 | tf_op jit(solution)/shard_map/ppermute | solution.py:90
  35.2 27.1 %collective-permute-start.10 = (bf16[128,4096]{1,0:T(8,128)(2,1)S(1)}, bf16[128,4096]{1,0:T(8,128)(2,1)S(1)}, u32[]{:S(2)}, u32[]{:S(2)}) collective-permute-start(bf16[128,4096]{1,0:T(8,128)(2,1)S(1)} %copy-done), channel_id=1, source_target_pairs={{0,1},{1,0},{2,3},{3,2},{4,5},{5,4},{6,7},{7,6},{8,9},{9,8},{10,11... | collective-permute-start | bytes 3145736 | tf_op jit(solution)/shard_map/ppermute | solution.py:90
  35.2 11.7 %collective-permute-start.11 = (bf16[256,512]{1,0:T(8,128)(2,1)}, bf16[256,512]{1,0:T(8,128)(2,1)S(1)}, u32[]{:S(2)}, u32[]{:S(2)}) collective-permute-start(bf16[256,512]{1,0:T(8,128)(2,1)} %copy-done.4), channel_id=1, source_target_pairs={{0,2},{1,3},{2,0},{3,1},{4,6},{5,7},{6,4},{7,5},{8,10},{9,11},{10,... | collective-permute-start | bytes 786440 | tf_op jit(solution)/shard_map/ppermute | solution.py:90
  44.2 6.9 %collective-permute-start.7 = (s32[1,128]{1,0:T(1,128)S(1)}, s32[1,128]{1,0:T(1,128)S(1)}, u32[]{:S(2)}, u32[]{:S(2)}) collective-permute-start(s32[1,128]{1,0:T(1,128)S(1)} %bitcast_add_fusion), channel_id=1, source_target_pairs={{0,1},{1,0},{2,3},{3,2},{4,5},{5,4},{6,7},{7,6},{8,9},{9,8},{10,11... | collective-permute-start | bytes 1544 | tf_op jit(solution)/shard_map/ppermute | solution.py:90
  47.6 8.7 %collective-permute-start.13 = (bf16[256,512]{1,0:T(8,128)(2,1)}, bf16[256,512]{1,0:T(8,128)(2,1)}, u32[]{:S(2)}, u32[]{:S(2)}) collective-permute-start(bf16[256,512]{1,0:T(8,128)(2,1)} %copy-done.8), channel_id=1, source_target_pairs={{0,4},{1,5},{2,6},{3,7},{4,0},{5,1},{6,2},{7,3},{8,12},{9,13},{10,... | collective-permute-start | bytes 786440 | tf_op jit(solution)/shard_map/ppermute | solution.py:90
  49.1 9.0 %collective-permute-start.12 = (bf16[256,512]{1,0:T(8,128)(2,1)}, bf16[256,512]{1,0:T(8,128)(2,1)}, u32[]{:S(2)}, u32[]{:S(2)}) collective-permute-start(bf16[256,512]{1,0:T(8,128)(2,1)} %copy-done.8), channel_id=1, source_target_pairs={{0,2},{1,3},{2,0},{3,1},{4,6},{5,7},{6,4},{7,5},{8,10},{9,11},{10,... | collective-permute-start | bytes 786440 | tf_op jit(solution)/shard_map/ppermute | solution.py:90
  49.7 11.5 %collective-permute-start.17 = (bf16[256,512]{1,0:T(8,128)(2,1)}, bf16[256,512]{1,0:T(8,128)(2,1)}, u32[]{:S(2)}, u32[]{:S(2)}) collective-permute-start(bf16[256,512]{1,0:T(8,128)(2,1)} %copy-done.10), channel_id=1, source_target_pairs={{0,2},{1,3},{2,0},{3,1},{4,6},{5,7},{6,4},{7,5},{8,10},{9,11},{10,... | collective-permute-start | bytes 786440 | tf_op jit(solution)/shard_map/ppermute | solution.py:90
  51.2 3.7 %collective-permute-start.8 = (s32[2,128]{1,0:T(2,128)S(1)}, s32[2,128]{1,0:T(2,128)S(1)}, u32[]{:S(2)}, u32[]{:S(2)}) collective-permute-start(s32[2,128]{1,0:T(2,128)S(1)} %add_select_fusion.1), channel_id=1, source_target_pairs={{0,8},{1,9},{2,10},{3,11},{4,12},{5,13},{6,14},{7,15},{8,0},{9,1},... | collective-permute-start | bytes 3080 | tf_op jit(solution)/shard_map/ppermute | solution.py:90
  56.3 14.9 %collective-permute-start.16 = (bf16[4,128,1024]{2,1,0:T(8,128)(2,1)S(1)}, bf16[4,128,1024]{2,1,0:T(8,128)(2,1)}, u32[]{:S(2)}, u32[]{:S(2)}) collective-permute-start(bf16[4,128,1024]{2,1,0:T(8,128)(2,1)S(1)} %all-to-all-done.own_ref), channel_id=1, source_target_pairs={{0,1},{1,0},{2,3},{3,2},{4,5},{5,4},{6,7},{7,6},{8,9},{9,8},{10,11... | collective-permute-start | bytes 3145736 | tf_op jit(solution)/shard_map/ppermute | solution.py:90
  56.3 15.6 %collective-permute-start.18 = (bf16[256,512]{1,0:T(8,128)(2,1)}, bf16[256,512]{1,0:T(8,128)(2,1)}, u32[]{:S(2)}, u32[]{:S(2)}) collective-permute-start(bf16[256,512]{1,0:T(8,128)(2,1)} %copy-done.10), channel_id=1, source_target_pairs={{0,4},{1,5},{2,6},{3,7},{4,0},{5,1},{6,2},{7,3},{8,12},{9,13},{10,... | collective-permute-start | bytes 786440 | tf_op jit(solution)/shard_map/ppermute | solution.py:90
  58.1 10.7 %collective-permute-start.9 = (s32[4,128]{1,0:T(4,128)S(1)}, s32[4,128]{1,0:T(4,128)}, u32[]{:S(2)}, u32[]{:S(2)}) collective-permute-start(s32[4,128]{1,0:T(4,128)S(1)} %pad_add_fusion.1), channel_id=1, source_target_pairs={{0,16},{1,17},{2,18},{3,19},{4,20},{5,21},{6,22},{7,23},{8,24},{9,... | collective-permute-start | bytes 6152 | tf_op jit(solution)/shard_map/ppermute | solution.py:90
  61.2 11.7 %collective-permute-start.19 = (bf16[256,512]{1,0:T(8,128)(2,1)}, bf16[256,512]{1,0:T(8,128)(2,1)}, u32[]{:S(2)}, u32[]{:S(2)}) collective-permute-start(bf16[256,512]{1,0:T(8,128)(2,1)} %collective-permute-done.6.refs_5_), channel_id=1, source_target_pairs={{0,2},{1,3},{2,0},{3,1},{4,6},{5,7},{6,4},{7,5},{8,10},{9,11},{10,... | collective-permute-start | bytes 786440 | tf_op jit(solution)/shard_map/ppermute | solution.py:90
  62.3 10.5 %collective-permute-start.20 = (bf16[256,512]{1,0:T(8,128)(2,1)}, bf16[256,512]{1,0:T(8,128)(2,1)}, u32[]{:S(2)}, u32[]{:S(2)}) collective-permute-start(bf16[256,512]{1,0:T(8,128)(2,1)} %collective-permute-done.12.refs_7_), channel_id=1, source_target_pairs={{0,4},{1,5},{2,6},{3,7},{4,0},{5,1},{6,2},{7,3},{8,12},{9,13},{10,... | collective-permute-start | bytes 786440 | tf_op jit(solution)/shard_map/ppermute | solution.py:90
  62.9 0.9 copy-start.5
  63.9 0.9 copy-start.7
  64.8 0.9 copy-start.9
  65.8 4.6 %copy-start.16 = (bf16[128,1024]{1,0:T(8,128)(2,1)S(1)}, bf16[128,1024]{1,0:T(8,128)(2,1)}, u32[]{:S(2)}) copy-start(bf16[128,1024]{1,0:T(8,128)(2,1)} %param.7) | copy-start | bytes 786436
  68.8 2.3 %copy-start.2 = (f32[2,128,512]{2,1,0:T(8,128)}, f32[2,128,512]{2,1,0:T(8,128)S(1)}, u32[]{:S(2)}) copy-start(f32[2,128,512]{2,1,0:T(8,128)S(1)} %get-tuple-element.31.begun_ref) | copy-start | bytes 1572868
  68.8 7.7 %collective-permute-start.21 = (bf16[256,512]{1,0:T(8,128)(2,1)}, bf16[256,512]{1,0:T(8,128)(2,1)S(1)}, u32[]{:S(2)}, u32[]{:S(2)}) collective-permute-start(bf16[256,512]{1,0:T(8,128)(2,1)} %collective-permute-done.17.refs_3_), channel_id=1, source_target_pairs={{0,4},{1,5},{2,6},{3,7},{4,0},{5,1},{6,2},{7,3},{8,12},{9,13},{10,... | collective-permute-start | bytes 786440 | tf_op jit(solution)/shard_map/ppermute | solution.py:90
  71.2 1.7 %collective-permute-start.14 = (bf16[128,512]{1,0:T(8,128)(2,1)}, bf16[128,512]{1,0:T(8,128)(2,1)}, u32[]{:S(2)}, u32[]{:S(2)}) collective-permute-start(bf16[128,512]{1,0:T(8,128)(2,1)} %get-tuple-element.46), channel_id=1, source_target_pairs={{0,1},{1,0},{2,3},{3,2},{4,5},{5,4},{6,7},{7,6},{8,9},{9,8},{10,11... | collective-permute-start | bytes 393224 | tf_op jit(solution)/shard_map/ppermute | solution.py:90
  72.0 57.4 %collective-permute-start.25 = (bf16[2048,512]{1,0:T(8,128)(2,1)}, bf16[2048,512]{1,0:T(8,128)(2,1)}, u32[]{:S(2)}, u32[]{:S(2)}) collective-permute-start(bf16[2048,512]{1,0:T(8,128)(2,1)} %get-tuple-element.39.refs_0_), channel_id=1, source_target_pairs={{0,1},{1,0},{2,3},{3,2},{4,5},{5,4},{6,7},{7,6},{8,9},{9,8},{10,11... | collective-permute-start | bytes 6291464 | tf_op jit(solution)/shard_map/ppermute | solution.py:90
  77.3 1.0 copy-start.3
  78.3 0.9 copy-start.11
  79.2 0.9 copy-start.13
  80.2 0.9 copy-start.15
  84.4 45.0 %collective-permute-start.26 = (bf16[2048,512]{1,0:T(8,128)(2,1)}, bf16[2048,512]{1,0:T(8,128)(2,1)}, u32[]{:S(2)}, u32[]{:S(2)}) collective-permute-start(bf16[2048,512]{1,0:T(8,128)(2,1)} %get-tuple-element.40.refs_2_), channel_id=1, source_target_pairs={{0,1},{1,0},{2,3},{3,2},{4,5},{5,4},{6,7},{7,6},{8,9},{9,8},{10,11... | collective-permute-start | bytes 6291464 | tf_op jit(solution)/shard_map/ppermute | solution.py:90
  84.4 15.3 %collective-permute-start.23 = (bf16[256,512]{1,0:T(8,128)(2,1)S(1)}, bf16[256,512]{1,0:T(8,128)(2,1)S(1)}, u32[]{:S(2)}, u32[]{:S(2)}) collective-permute-start(bf16[256,512]{1,0:T(8,128)(2,1)S(1)} %get-tuple-element.36.refs_0_), channel_id=1, source_target_pairs={{0,16},{1,17},{2,18},{3,19},{4,20},{5,21},{6,22},{7,23},{8,24},{9,... | collective-permute-start | bytes 786440 | tf_op jit(solution)/shard_map/ppermute | solution.py:90
  85.8 13.9 %collective-permute-start.22 = (bf16[256,512]{1,0:T(8,128)(2,1)S(1)}, bf16[256,512]{1,0:T(8,128)(2,1)S(1)}, u32[]{:S(2)}, u32[]{:S(2)}) collective-permute-start(bf16[256,512]{1,0:T(8,128)(2,1)S(1)} %get-tuple-element.36.refs_0_), channel_id=1, source_target_pairs={{0,8},{1,9},{2,10},{3,11},{4,12},{5,13},{6,14},{7,15},{8,0},{9,1},... | collective-permute-start | bytes 786440 | tf_op jit(solution)/shard_map/ppermute | solution.py:90
  101.3 15.3 %all-to-all-start.1 = ((bf16[8,48,512]{2,1,0:T(8,128)(2,1)}), bf16[8,48,512]{2,1,0:T(8,128)(2,1)S(1)}, u32[]{:S(2)}, u32[]{:S(2)}) async-start(bf16[8,48,512]{2,1,0:T(8,128)(2,1)} %bitcast.26), calls=%async_computation.1 | async-start | bytes 786432 | tf_op jit(solution)/shard_map/all_to_all | solution.py:387
  104.8 8.6 %collective-permute-start.24 = (bf16[256,512]{1,0:T(8,128)(2,1)S(1)}, bf16[256,512]{1,0:T(8,128)(2,1)S(1)}, u32[]{:S(2)}, u32[]{:S(2)}) collective-permute-start(bf16[256,512]{1,0:T(8,128)(2,1)S(1)} %collective-permute-done.23.refs_2_), channel_id=1, source_target_pairs={{0,8},{1,9},{2,10},{3,11},{4,12},{5,13},{6,14},{7,15},{8,0},{9,1},... | collective-permute-start | bytes 786440 | tf_op jit(solution)/shard_map/ppermute | solution.py:90
  125.8 18.9 %all-to-all-start.3 = ((bf16[8,128,512]{2,1,0:T(8,128)(2,1)}), bf16[8,128,512]{2,1,0:T(8,128)(2,1)S(1)}, u32[]{:S(2)}, u32[]{:S(2)}) async-start(bf16[8,128,512]{2,1,0:T(8,128)(2,1)} %bitcast.30), calls=%async_computation.3 | async-start | bytes 2097152 | tf_op jit(solution)/shard_map/all_to_all | solution.py:387
  129.4 1.6 %copy-start.1 = (bf16[2048,512]{1,0:T(8,128)(2,1)S(1)}, bf16[2048,512]{1,0:T(8,128)(2,1)}, u32[]{:S(2)}) copy-start(bf16[2048,512]{1,0:T(8,128)(2,1)} %get-tuple-element.39.refs_0_) | copy-start | bytes 6291460
  (2 other events, 1.4 us)

commit v7 on v6

v7 whole, which is shorter than its diff:
```python
import functools
import math

import jax
import jax.numpy as jnp
from jax import lax
from jax.experimental import pallas as pl
from jax.experimental.pallas import tpu as pltpu
from jax.sharding import PartitionSpec as P

HEAD_DIM = 128
NSUB = 4
VMEM_LIMIT = 48 * 1024 * 1024
epsilon = 1e-06


def per_device_general(tokens, key_cot, routes, counts, widths, key_weight):
    row_count = tokens.shape[0]
    width_model = tokens.shape[1]
    local_cols = key_cot.shape[1]
    local_heads = local_cols // HEAD_DIM
    dp_size = lax.axis_size("dp")
    per_peer = 2 * row_count // dp_size
    receive = dp_size * per_peer
    destination = routes[:, 0]
    one_hot = (destination[:, None] == jnp.arange(dp_size, dtype=jnp.int32)[None, :]).astype(
        jnp.int32
    )
    earlier = jnp.sum(jnp.cumsum(one_hot, axis=0) * one_hot, axis=1) - 1
    send_slot = destination * per_peer + earlier
    bounds = jnp.cumsum(counts[0])
    positions = jnp.arange(row_count, dtype=jnp.int32)
    subnet = jnp.sum((positions[:, None] >= bounds[None, : NSUB - 1]).astype(jnp.int32), axis=1)
    send_subnet = (
        jnp.full((receive,), -1, jnp.int32).at[send_slot].set(subnet).reshape(dp_size, per_peer)
    )
    send_cot = jnp.zeros((receive, local_cols), jnp.bfloat16).at[send_slot].set(key_cot)
    send_cot = send_cot.reshape(dp_size, per_peer, local_cols)
    send_tokens = jnp.zeros((receive, width_model), jnp.bfloat16).at[send_slot].set(tokens)
    send_tokens = send_tokens.reshape(dp_size, per_peer, width_model)
    got_tokens, got_cot, got_subnet = (
        lax.all_to_all(send_tokens, "dp", split_axis=0, concat_axis=0, tiled=True),
        lax.all_to_all(send_cot, "dp", split_axis=0, concat_axis=0, tiled=True),
        lax.all_to_all(send_subnet, "dp", split_axis=0, concat_axis=0, tiled=True),
    )
    hidden = got_tokens.reshape(receive, width_model)
    got_cot = got_cot.reshape(receive, local_cols)
    got_subnet = got_subnet.reshape(receive)
    full_weight = lax.all_gather(key_weight, "dp", axis=0, tiled=True)
    key_proj = jnp.dot(hidden, full_weight, preferred_element_type=jnp.float32)
    per_head = key_proj.reshape(receive, local_heads, HEAD_DIM)
    head_scale = jnp.sqrt(jnp.mean(per_head * per_head, axis=2, keepdims=True) + epsilon)
    outputs = per_head / head_scale
    subnet_match = got_subnet[:, None] == jnp.arange(NSUB, dtype=jnp.int32)[None, :]
    row_width = jnp.sum(jnp.where(subnet_match, widths[None, :], 0), axis=1)
    head_index = lax.axis_index("mp") * local_heads + jnp.arange(local_heads, dtype=jnp.int32)
    head_mask = (head_index[None, :] < row_width[:, None]).astype(jnp.float32)
    upstream = (
        got_cot.astype(jnp.float32).reshape(receive, local_heads, HEAD_DIM) * head_mask[:, :, None]
    )
    key_delta = (
        upstream - outputs * jnp.mean(upstream * outputs, axis=2, keepdims=True)
    ) / head_scale
    delta_low = key_delta.reshape(receive, local_cols).astype(jnp.bfloat16)
    part_delta = lax.dot_general(
        delta_low, full_weight, (((1,), (1,)), ((), ())), preferred_element_type=jnp.float32
    )
    rounded = lax.optimization_barrier(part_delta.astype(jnp.bfloat16)).astype(jnp.float32)
    feature_delta = lax.psum_scatter(
        rounded.astype(jnp.bfloat16), "mp", scatter_dimension=1, tiled=True
    )
    weight_sum = lax.psum_scatter(
        lax.dot_general(
            hidden, delta_low, (((0,), (0,)), ((), ())), preferred_element_type=jnp.float32
        ),
        "dp",
        scatter_dimension=0,
        tiled=True,
    )
    key_grad = weight_sum / math.sqrt(row_count * dp_size)
    return (feature_delta, key_grad)


CORE, X, Y = 1, 2, 4
PLANE = 8


def swap(value, mask):
    size = lax.axis_size("dp")
    return lax.ppermute(value, "dp", [(i, i ^ mask) for i in range(size)])


def after(value, *others):
    return lax.optimization_barrier((value, *others))[0]


def dot(a, b, dims):
    return lax.dot_general(a, b, (dims, ((), ())), preferred_element_type=jnp.float32)


def fetch(pairs, sems):
    copies = [
        pltpu.make_async_copy(source, target, sems.at[n])
        for n, (source, target) in enumerate(pairs)
    ]
    for copy in copies:
        copy.start()
    return copies


def add_products(chips_ref, begin, token_refs, pieces, weight_ref, acc, held, weights, sems, fresh):
    depth = pieces[0].shape[0]

    def rows_of(ref, n):
        return ref.at[n * depth : (n + 1) * depth, :]

    pairs = [(ref, held.at[side]) for side, ref in enumerate(token_refs)]
    pairs += [(ref, rows_of(weights, n)) for n, ref in enumerate(pieces)]
    copies = fetch(pairs, sems)
    for copy in copies[:2]:
        copy.wait()
    kept = []
    for n in range(len(pieces)):
        copies[2 + n].wait()
        out = pltpu.make_async_copy(
            rows_of(weights, n), rows_of(weight_ref, n), sems.at[2 + len(pieces) + n]
        )
        out.start()
        kept.append(out)
        piece = weights[n * depth : (n + 1) * depth, :]
        at = pl.multiple_of(chips_ref[begin + n] * depth, depth)
        for side in range(2):
            part = dot(held[side, :, pl.ds(at, depth)], piece, ((1,), (0,)))
            if fresh and n == 0:
                acc[side] = part
            else:
                acc[side] += part
    return kept


def project_kernel(count, chips_ref, own_ref, mate_ref, *refs):
    pieces = refs[:count]
    weight_ref, acc_ref, held, weights, sems = refs[count:]
    kept = add_products(
        chips_ref, 0, (own_ref, mate_ref), pieces, weight_ref, acc_ref, held, weights, sems, True
    )
    for copy in kept:
        copy.wait()


def delta_kernel(
    count,
    begin,
    chips_ref,
    me_ref,
    own_ref,
    mate_ref,
    own_cot_ref,
    mate_cot_ref,
    begun_ref,
    *refs,
):
    pieces = refs[:count]
    delta_ref, weight_ref, acc, held, weights, sems = refs[count:]
    core = me_ref[0] & 1
    rows = own_ref.shape[0]
    acc[...] = begun_ref[...]
    kept = add_products(
        chips_ref, begin, (own_ref, mate_ref), pieces, weight_ref, acc, held, weights, sems, False
    )
    for side, cot_ref in enumerate((own_cot_ref, mate_cot_ref)):
        at = pl.multiple_of((core ^ side) * rows, rows)
        for head in range(own_cot_ref.shape[1] // HEAD_DIM):
            cols = slice(head * HEAD_DIM, (head + 1) * HEAD_DIM)
            proj = acc[side, :, cols]
            scale = jnp.sqrt(jnp.mean(proj * proj, axis=1, keepdims=True) + epsilon)
            normed = proj / scale
            upstream = cot_ref[:, cols].astype(jnp.float32)
            delta = (upstream - normed * jnp.mean(upstream * normed, axis=1, keepdims=True)) / scale
            delta_ref[pl.ds(at, rows), cols] = delta.astype(jnp.bfloat16)
    for copy in kept:
        copy.wait()


def selected_rows(plane, code_ref, levels, deltas, slot_count):
    rows = code_ref.shape[1]
    per_chip = slot_count // (PLANE * len(levels))
    iota = lax.broadcasted_iota(jnp.int32, (slot_count, rows), 0)
    destination, slot = iota // (per_chip * len(levels)), iota % (per_chip * len(levels))
    total = None
    for n, level in enumerate(levels):
        for side in range(2):
            want = (plane * PLANE + destination) * per_chip + slot - n * per_chip
            inside = (slot >= n * per_chip) & (slot < (n + 1) * per_chip)
            code = code_ref[2 * level + side : 2 * level + side + 1, :]
            hot = (inside & (want == code)).astype(jnp.bfloat16)
            part = dot(hot, deltas[n][side * rows : (side + 1) * rows, :], ((1,), (0,)))
            total = part if total is None else total + part
    return total.astype(jnp.bfloat16)


def select_kernel(levels, me_ref, code_ref, *refs):
    *deltas, sent_ref, held, sems = refs
    for copy in fetch([(ref, held.at[n]) for n, ref in enumerate(deltas)], sems):
        copy.wait()
    plane = lax.shift_right_logical(me_ref[0], 3)
    values = [held[n] for n in range(len(deltas))]
    sent_ref[...] = selected_rows(plane, code_ref, levels, values, sent_ref.shape[0])


def weight_grad_kernel(me_ref, code_ref, own_ref, mate_ref, *refs):
    *deltas, part_ref, hidden, held, acc, sems = refs
    plane = lax.shift_right_logical(me_ref[0], 3)
    core = me_ref[0] & 1
    rows = own_ref.shape[1]
    count = len(deltas)
    pairs = []
    for n, ref in enumerate(deltas):
        pairs += [
            (own_ref.at[plane ^ n], hidden.at[n, 0]),
            (mate_ref.at[plane ^ n], hidden.at[n, 1]),
            (ref, held.at[n]),
        ]
    copies = fetch(pairs, sems)
    for n in range(count):
        for copy in copies[3 * n : 3 * n + 3]:
            copy.wait()
        for side in range(2):
            at = pl.multiple_of((core ^ side) * rows, rows)
            part = dot(hidden[n, side], held[n, pl.ds(at, rows), :], ((0,), (0,)))
            if n + side == 0:
                acc[...] = part
            else:
                acc[...] += part
    blocks, depth, _ = part_ref.shape
    shard = acc.shape[0] // blocks
    extra = depth - shard
    far = selected_rows(plane, code_ref, (count - 1,), [held[count - 1]], blocks * extra)
    for block in range(blocks):
        part_ref[block, :shard, :] = acc[block * shard : (block + 1) * shard, :].astype(
            jnp.bfloat16
        )
        part_ref[block, shard:, :] = far[block * extra : (block + 1) * extra, :]


def sum_kernel(norm, parts_ref, grad_ref):
    shard, cols = grad_ref.shape
    half = cols // 2
    for side in range(2):
        total = parts_ref[0, side, :shard, :].astype(jnp.float32)
        for chip in range(1, parts_ref.shape[0]):
            total += parts_ref[chip, side, :shard, :].astype(jnp.float32)
        grad_ref[:, side * half : (side + 1) * half] = total / norm


def add_columns(core, step, chips_ref, rows_ref, weights, out_ref):
    own, mate = rows_ref[core], rows_ref[1 - core]
    depth = weights[0].shape[0]
    for n in range(2):
        total = dot(own, weights[2 * n][...], ((1,), (1,)))
        total += dot(mate, weights[2 * n + 1][...], ((1,), (1,)))
        at = chips_ref[n * pl.num_programs(0) + step] * depth
        out_ref[:, pl.ds(pl.multiple_of(at, depth), depth)] = total.astype(jnp.bfloat16)


def row_grad_kernel(chips_ref, me_ref, got_ref, *refs):
    *weights, out_ref, rows_ref = refs
    step = pl.program_id(0)
    chips, _, count, _ = got_ref.shape
    block = rows_ref.shape[1] // (chips * 4)
    level = lax.shift_right_logical(me_ref[0], 3)

    @pl.when(step == 0)
    def _():
        for n in range(4):
            for chip in range(chips):
                at = pl.multiple_of(((level ^ n) * chips + chip) * block, block)
                for side in range(2):
                    if n < count // block:
                        rows = got_ref[chip, side, n * block : (n + 1) * block, :]
                    else:
                        rows = jnp.zeros((block, got_ref.shape[3]), jnp.bfloat16)
                    rows_ref[side, pl.ds(at, block), :] = rows

    add_columns(me_ref[0] & 1, step, chips_ref, rows_ref, weights, out_ref)


def far_row_grad_kernel(chips_ref, me_ref, before_ref, got_ref, *refs):
    *weights, out_ref, rows_ref = refs
    step = pl.program_id(0)
    chips, _, count, _ = got_ref.shape
    block = rows_ref.shape[1] // chips

    @pl.when(step == 0)
    def _():
        for chip in range(chips):
            for side in range(2):
                rows_ref[side, chip * block : (chip + 1) * block, :] = got_ref[
                    chip, side, count - block :, :
                ]

    add_columns(me_ref[0] & 1, step, chips_ref, rows_ref, weights, out_ref)


def column_codes(destination, core, per_peer):
    positions = jnp.arange(destination.shape[0], dtype=jnp.int32)
    same = (destination[:, None] == destination[None, :]) & (
        positions[:, None] < positions[None, :]
    )
    earlier = jnp.sum(same.astype(jnp.int32), axis=0)
    code = ((destination * 2 + core) * per_peer + earlier).reshape(1, -1)
    mate_code = swap(code, CORE)
    codes = jnp.where(
        core == 0,
        jnp.concatenate([code, mate_code], axis=0),
        jnp.concatenate([mate_code, code], axis=0),
    )
    for bit in (PLANE, 2 * PLANE):
        codes = jnp.concatenate([codes, swap(codes, bit)], axis=0)
    return codes


def vmem(count):
    return [pl.BlockSpec(memory_space=pltpu.VMEM)] * count


def anywhere(count):
    return [pl.BlockSpec(memory_space=pl.ANY)] * count


SCALAR = pl.BlockSpec(memory_space=pltpu.SMEM)
PARAMS = pltpu.CompilerParams(vmem_limit_bytes=VMEM_LIMIT)


COST = pl.CostEstimate(flops=1024, bytes_accessed=1024, transcendentals=0)


def per_device_paired(tokens, key_cot, routes, counts, widths, key_weight):
    rows, width_model = tokens.shape
    cols = key_cot.shape[1]
    half_cols = cols // 2
    size = lax.axis_size("dp")
    chips = size // 2
    levels = size // PLANE
    per_peer = 2 * rows // size
    receive = size * per_peer
    wide = width_model // levels
    me = lax.axis_index("dp")
    core = me % 2
    me_scalar = me.astype(jnp.int32).reshape(1)

    def mine(value):
        return lax.dynamic_slice_in_dim(value, core * half_cols, half_cols, 1)

    def theirs(value):
        return lax.dynamic_slice_in_dim(value, (1 - core) * half_cols, half_cols, 1)

    mate_shard = swap(key_weight, CORE)
    piece = jnp.where(
        core == 0,
        jnp.concatenate([key_weight[:, :half_cols], mate_shard[:, :half_cols]], axis=0),
        jnp.concatenate([mate_shard[:, half_cols:], key_weight[:, half_cols:]], axis=0),
    )
    near, far, both = PLANE, 2 * PLANE, 3 * PLANE
    z_far, z_near = swap(piece, far), swap(piece, near)
    x_own, y_own = swap(piece, X), swap(piece, Y)
    z_far, z_near, y_own, *_ = lax.optimization_barrier((z_far, z_near, y_own, x_own))
    z_both = swap(z_far, near)
    x_near, y_near = swap(z_near, X), swap(z_near, Y)
    x_far, y_far = swap(z_far, X), swap(z_far, Y)
    codes = column_codes(routes[:, 0], core, per_peer)
    z_both_late = after(z_both, x_near, y_near, codes)
    x_both, y_both = swap(z_both_late, X), swap(z_both_late, Y)
    d_far = swap(after(x_far, y_far), Y)
    d_own = swap(after(y_own, x_far), X)
    d_near = swap(after(y_near, x_both, d_own), X)
    first_pieces = {
        0: piece,
        X: x_own,
        Y: y_own,
        near: z_near,
        near | X: x_near,
        near | Y: y_near,
        far: z_far,
        far | X: x_far,
    }

    mate_tokens = swap(after(tokens, z_near), CORE)
    columns = [[p + PLANE * z for z in range(levels)] for p in range(PLANE)]
    late_tokens = after(tokens, z_both, x_near, y_near)
    own_features = lax.all_to_all(
        jnp.stack([late_tokens[:, z * wide : (z + 1) * wide] for z in range(levels)]),
        "dp",
        split_axis=0,
        concat_axis=0,
        axis_index_groups=columns,
        tiled=True,
    )
    mate_features = swap(own_features, CORE)

    key_cot, counts = lax.optimization_barrier((key_cot, counts, x_far, y_far))[:2]
    bounds = jnp.cumsum(counts[0])
    positions = jnp.arange(rows, dtype=jnp.int32)
    subnet = jnp.sum((positions[:, None] >= bounds[None, : NSUB - 1]).astype(jnp.int32), axis=1)
    subnet_match = subnet[:, None] == jnp.arange(NSUB, dtype=jnp.int32)[None, :]
    row_width = jnp.sum(jnp.where(subnet_match, widths[None, :], 0), axis=1)
    head_of_col = jnp.arange(cols, dtype=jnp.int32) // HEAD_DIM
    upstream = jnp.where(
        head_of_col[None, :] < row_width[:, None], key_cot, jnp.zeros_like(key_cot)
    )
    own_cot, mate_cot = mine(upstream), swap(theirs(upstream), CORE)

    kept = jax.ShapeDtypeStruct((width_model // 2, half_cols), jnp.bfloat16)
    sums = jax.ShapeDtypeStruct((2, rows, half_cols), jnp.float32)
    room = [
        pltpu.VMEM((2, rows, width_model), jnp.bfloat16),
        pltpu.VMEM((width_model // 2, half_cols), jnp.bfloat16),
        pltpu.SemaphoreType.DMA((2 + chips,)),
    ]
    first_weight, begun = pl.pallas_call(
        functools.partial(project_kernel, len(first_pieces)),
        out_shape=(kept, sums),
        in_specs=[SCALAR] + anywhere(2 + len(first_pieces)),
        out_specs=(anywhere(1)[0], vmem(1)[0]),
        scratch_shapes=room,
        compiler_params=PARAMS,
        cost_estimate=COST,
        name="project",
    )(
        jnp.stack([lax.shift_right_logical(me ^ mask, 1) for mask in first_pieces]),
        tokens,
        mate_tokens,
        *first_pieces.values(),
    )
    d_both = swap(after(x_both, begun, d_far, y_both), Y)
    last_pieces = {
        far | Y: y_far,
        X | Y: d_own,
        both: z_both,
        both | X: x_both,
        both | Y: y_both,
        far | X | Y: d_far,
        near | X | Y: d_near,
        both | X | Y: d_both,
    }
    order = jnp.stack(
        [lax.shift_right_logical(me ^ mask, 1) for mask in (*first_pieces, *last_pieces)]
    )
    begun = after(begun, own_features)
    delta, last_weight = pl.pallas_call(
        functools.partial(delta_kernel, len(last_pieces), len(first_pieces)),
        out_shape=(jax.ShapeDtypeStruct((2 * rows, half_cols), jnp.bfloat16), kept),
        in_specs=[SCALAR] * 2 + anywhere(2) + vmem(3) + anywhere(len(last_pieces)),
        out_specs=(vmem(1)[0], anywhere(1)[0]),
        scratch_shapes=[pltpu.VMEM(sums.shape, sums.dtype)] + room,
        compiler_params=PARAMS,
        cost_estimate=COST,
        name="delta",
    )(
        order,
        me_scalar,
        tokens,
        mate_tokens,
        own_cot,
        mate_cot,
        begun,
        *last_pieces.values(),
    )

    delta_far, delta_near = swap(delta, far), swap(delta, near)
    delta_both = swap(delta_far, near)
    planes = [[z * PLANE + p for p in range(PLANE)] for z in range(levels)]

    def to_plane(value):
        got = lax.all_to_all(
            value, "dp", split_axis=0, concat_axis=0, axis_index_groups=planes, tiled=True
        )
        return got.reshape(PLANE // 2, 2, *value.shape[1:])

    per_chip = 2 * per_peer
    near_deltas = [delta, delta_near, delta_far]
    piece_room = (2 * rows, half_cols)
    selected = pl.pallas_call(
        functools.partial(select_kernel, (0, 1, 2)),
        out_shape=jax.ShapeDtypeStruct((PLANE * 3 * per_chip, half_cols), jnp.bfloat16),
        in_specs=[SCALAR] + vmem(1) + anywhere(3),
        out_specs=vmem(1)[0],
        scratch_shapes=[
            pltpu.VMEM((3, *piece_room), jnp.bfloat16),
            pltpu.SemaphoreType.DMA((3,)),
        ],
        compiler_params=PARAMS,
        cost_estimate=COST,
        name="select",
    )(me_scalar, codes, *near_deltas)
    got_near = to_plane(selected.reshape(PLANE, 3 * per_chip, half_cols))

    shard = width_model // size
    terms = pl.pallas_call(
        weight_grad_kernel,
        out_shape=jax.ShapeDtypeStruct((PLANE, shard + per_chip, half_cols), jnp.bfloat16),
        in_specs=[SCALAR] + vmem(1) + anywhere(2 + levels),
        out_specs=vmem(1)[0],
        scratch_shapes=[
            pltpu.VMEM((levels, 2, rows, wide), jnp.bfloat16),
            pltpu.VMEM((levels, *piece_room), jnp.bfloat16),
            pltpu.VMEM((wide, half_cols), jnp.float32),
            pltpu.SemaphoreType.DMA((3 * levels,)),
        ],
        compiler_params=PARAMS,
        cost_estimate=COST,
        name="weight_grad",
    )(me_scalar, codes, own_features, mate_features, *near_deltas, delta_both)
    got = to_plane(terms)

    depth = width_model // chips
    kept_weights = [first_weight, swap(first_weight, CORE), last_weight, swap(last_weight, CORE)]
    weight_specs = [pl.BlockSpec((depth, half_cols), lambda i, *_: (i, 0))] * len(kept_weights)
    row_shape = jax.ShapeDtypeStruct((receive, width_model), jnp.bfloat16)
    row_grads = pl.pallas_call(
        row_grad_kernel,
        out_shape=row_shape,
        grid_spec=pltpu.PrefetchScalarGridSpec(
            num_scalar_prefetch=2,
            grid=(chips // 2,),
            in_specs=[pl.BlockSpec(got_near.shape, lambda i, *_: (0, 0, 0, 0))] + weight_specs,
            out_specs=pl.BlockSpec((receive, width_model), lambda i, *_: (0, 0)),
            scratch_shapes=[pltpu.VMEM((2, receive, half_cols), jnp.bfloat16)],
        ),
        compiler_params=PARAMS,
        cost_estimate=COST,
        name="row_grad",
    )(order, me_scalar, got_near, *kept_weights)
    count = receive // levels
    row_grads = pl.pallas_call(
        far_row_grad_kernel,
        out_shape=row_shape,
        grid_spec=pltpu.PrefetchScalarGridSpec(
            num_scalar_prefetch=2,
            grid=(chips // 2,),
            in_specs=anywhere(1)
            + [pl.BlockSpec(got.shape, lambda i, *_: (0, 0, 0, 0))]
            + weight_specs,
            out_specs=pl.BlockSpec(
                (count, width_model),
                lambda i, order, me: (lax.shift_right_logical(me[0], 3) ^ (levels - 1), 0),
            ),
            scratch_shapes=[pltpu.VMEM((2, count, half_cols), jnp.bfloat16)],
        ),
        input_output_aliases={2: 0},
        compiler_params=PARAMS,
        cost_estimate=COST,
        name="far_row_grad",
    )(order, me_scalar, row_grads, got, *kept_weights)

    key_grad = pl.pallas_call(
        functools.partial(sum_kernel, math.sqrt(rows * size)),
        out_shape=jax.ShapeDtypeStruct((shard, cols), jnp.float32),
        in_specs=vmem(1),
        out_specs=vmem(1)[0],
        compiler_params=PARAMS,
        cost_estimate=COST,
        name="sum",
    )(got)
    return (row_grads, key_grad)


def solution(mesh):
    size, split = mesh.shape["dp"], mesh.shape["mp"]
    paired = split == 1 and size == 32
    return jax.shard_map(
        per_device_paired if paired else per_device_general,
        mesh=mesh,
        in_specs=(P("dp", None), P("dp", "mp"), P("dp", None), P("dp", None), P(), P("dp", "mp")),
        out_specs=(P("dp", "mp"), P("dp", "mp")),
        check_vma=False,
    )
```

time: 147 us -> 161 us (1.095)
  waiting for transfers between devices: 58.7 us -> 69.3 us
  blocking collectives: 9.2 us -> 0 us
  Pallas kernels: 23.4 us -> 29.2 us
  local copies, waits for them, and re-layouts: 11.7 us -> 15.4 us
  starting transfers between devices: 39.3 us -> 42.9 us
    ppermute x27, waiting for transfers between devices: 52.1 us -> 62.5 us  [swap(): return lax.ppermute(value, 'dp', [(i, i ^ mask) for i in range(size)])]
    all_to_all x1 -> x0, blocking collectives: 9.2 us -> none  [to_plane(): lax.all_to_all(value.reshape(PLANE, -1, half_cols), 'dp', split_axis=0, c...]
    pallas_call x5 -> x4, Pallas kernels: 16.2 us -> 21.7 us  [the longest x1 8.95 us: per_device_paired(): pl.pallas_call(row_grad_kernel, out_shape=row_shape, grid_spec=pltpu.Pref...]
    unnamed x40 -> x50, local copies, waits for them, and re-layouts: 9.8 us -> 13.5 us
    all_to_all x1, starting transfers between devices: 3.83 us -> 5.45 us  [per_device_paired(): lax.all_to_all(jnp.stack([late_tokens[:, z * wide:(z + 1) * wide] for z i...]
  transfers between devices with their start and end apart: 30 -> 30, of which waited for: 18 -> 17; matrix products, arithmetic and copies ran while one was open for 2% -> 3% of each run, Pallas kernels for 15% -> 13%
where the time goes in v7:
time: 161 us; the launch traced here: 160 us
  waiting for transfers between devices  69.3 us (43%)
  starting transfers between devices  42.9 us (27%)
  Pallas kernels  29.2 us (18%)
  local copies, waits for them, and re-layouts  15.4 us (10%)
  other arithmetic  2.51 us (2%)
    ppermute x27, waiting for transfers between devices, swap(): return lax.ppermute(value, 'dp', [(i, i ^ mask) for i in range(size)])  62.5 us
    ppermute x27, starting transfers between devices, swap(): return lax.ppermute(value, 'dp', [(i, i ^ mask) for i in range(size)])  30 us
    unnamed x50, local copies, waits for them, and re-layouts  13.5 us
    pallas_call x1, Pallas kernels, per_device_paired(): pl.pallas_call(row_grad_kernel, out_shape=row_shape, grid_spec=pltpu.Pref...  8.95 us
    pallas_call x1, Pallas kernels, per_device_paired(): pl.pallas_call(far_row_grad_kernel, out_shape=row_shape, grid_spec=pltpu....  8.18 us
    all_to_all x2, starting transfers between devices, to_plane(): lax.all_to_all(value, 'dp', split_axis=0, concat_axis=0, axis_index_group...  7.47 us
    all_to_all x2, waiting for transfers between devices, to_plane(): lax.all_to_all(value, 'dp', split_axis=0, concat_axis=0, axis_index_group...  6.84 us
    all_to_all x1, starting transfers between devices, per_device_paired(): lax.all_to_all(jnp.stack([late_tokens[:, z * wide:(z + 1) * wide] for z i...  5.45 us
  transfers between devices with their start and end apart: 30, of which 17 were waited for; matrix products, arithmetic and copies ran while one was open for 3% of the time, Pallas kernels for 13%

profile of v7, /device:TPU:0, one launch (start us, length us, event | category | flops | bytes accessed | tf_op | source)
XLA Modules:
  0.0 160.2 jit_solution(4280574977922545897)
XLA Ops:
  1.2 1.0 fusion.5
  2.6 4.0 %collective-permute-start.4 = (bf16[256,512]{1,0:T(8,128)(2,1)S(1)}, bf16[256,512]{1,0:T(8,128)(2,1)S(1)}, u32[]{:S(2)}, u32[]{:S(2)}) collective-permute-start(bf16[256,512]{1,0:T(8,128)(2,1)S(1)} %maximum_select_fusion.refs_0_), channel_id=1, source_target_pairs={{0,16},{1,17},{2,18},{3,19},{4,20},{5,21},{6,22},{7,23},{8,24},{9,... | collective-permute-start | bytes 786440 | tf_op jit(solution)/shard_map/ppermute | solution.py:90
  6.7 1.6 collective-permute-start.5
  8.2 1.5 collective-permute-start.6
  9.7 1.5 collective-permute-start.7
  11.2 7.7 %collective-permute-done.4.refs_6_ = bf16[256,512]{1,0:T(8,128)(2,1)S(1)} collective-permute-done((bf16[256,512]{1,0:T(8,128)(2,1)S(1)}, bf16[256,512]{1,0:T(8,128)(2,1)S(1)}, u32[]{:S(2)}, u32[]{:S(2)}) %collective-permute-start.4) | collective-permute-done | bytes 262176 | tf_op jit(solution)/shard_map/ppermute | solution.py:90
  19.9 1.5 collective-permute-start.12
  21.5 1.5 collective-permute-start.13
  23.0 1.4 collective-permute-start.14
  25.3 2.2 %collective-permute-done.12.refs_4_ = bf16[256,512]{1,0:T(8,128)(2,1)S(1)} collective-permute-done((bf16[256,512]{1,0:T(8,128)(2,1)S(1)}, bf16[256,512]{1,0:T(8,128)(2,1)S(1)}, u32[]{:S(2)}, u32[]{:S(2)}) %collective-permute-start.12) | collective-permute-done | bytes 262176 | tf_op jit(solution)/shard_map/ppermute | solution.py:90
  28.5 1.3 collective-permute-done.14.refs_2_
  30.0 1.1 pad_maximum_fusion
  31.1 5.4 %all-to-all-start = ((bf16[4,128,1024]{2,1,0:T(8,128)(2,1)}), bf16[4,128,1024]{2,1,0:T(8,128)(2,1)S(1)}, u32[]{:S(2)}, u32[]{:S(2)}) async-start(bf16[4,128,1024]{2,1,0:T(8,128)(2,1)} %pad_maximum_fusion), calls=%async_computation | async-start | bytes 2097152 | tf_op jit(solution)/shard_map/all_to_all | solution.py:391
  36.6 1.1 collective-permute-done
  37.8 2.0 %collective-permute-start.1 = (s32[2,128]{1,0:T(2,128)S(1)}, s32[2,128]{1,0:T(2,128)S(1)}, u32[]{:S(2)}, u32[]{:S(2)}) collective-permute-start(s32[2,128]{1,0:T(2,128)S(1)} %add_select_fusion.1), channel_id=1, source_target_pairs={{0,8},{1,9},{2,10},{3,11},{4,12},{5,13},{6,14},{7,15},{8,0},{9,1},... | collective-permute-start | bytes 3080 | tf_op jit(solution)/shard_map/ppermute | solution.py:90
  41.0 11.5 %collective-permute-done.1 = s32[2,128]{1,0:T(2,128)S(1)} collective-permute-done((s32[2,128]{1,0:T(2,128)S(1)}, s32[2,128]{1,0:T(2,128)S(1)}, u32[]{:S(2)}, u32[]{:S(2)}) %collective-permute-start.1) | collective-permute-done | bytes 1056 | tf_op jit(solution)/shard_map/ppermute | solution.py:90
  52.5 4.5 %collective-permute-start.2 = (s32[4,128]{1,0:T(4,128)S(1)}, s32[4,128]{1,0:T(4,128)S(1)}, u32[]{:S(2)}, u32[]{:S(2)}) collective-permute-start(s32[4,128]{1,0:T(4,128)S(1)} %pad_add_fusion.1), channel_id=1, source_target_pairs={{0,16},{1,17},{2,18},{3,19},{4,20},{5,21},{6,22},{7,23},{8,24},{9,... | collective-permute-start | bytes 6152 | tf_op jit(solution)/shard_map/ppermute | solution.py:90
  57.0 4.1 %collective-permute-done.2 = s32[4,128]{1,0:T(4,128)S(1)} collective-permute-done((s32[4,128]{1,0:T(4,128)S(1)}, s32[4,128]{1,0:T(4,128)S(1)}, u32[]{:S(2)}, u32[]{:S(2)}) %collective-permute-start.2) | collective-permute-done | bytes 2080 | tf_op jit(solution)/shard_map/ppermute | solution.py:90
  61.7 1.4 collective-permute-start.17
  63.7 1.5 collective-permute-start.15
  65.6 5.1 %collective-permute-done.16.refs_3_ = bf16[256,512]{1,0:T(8,128)(2,1)} collective-permute-done((bf16[256,512]{1,0:T(8,128)(2,1)}, bf16[256,512]{1,0:T(8,128)(2,1)}, u32[]{:S(2)}, u32[]{:S(2)}) %collective-permute-start.16) | collective-permute-done | bytes 262176 | tf_op jit(solution)/shard_map/ppermute | solution.py:90
  70.7 3.6 %collective-permute-done.15.refs_1_ = bf16[256,512]{1,0:T(8,128)(2,1)} collective-permute-done((bf16[256,512]{1,0:T(8,128)(2,1)}, bf16[256,512]{1,0:T(8,128)(2,1)}, u32[]{:S(2)}, u32[]{:S(2)}) %collective-permute-start.15) | collective-permute-done | bytes 262176 | tf_op jit(solution)/shard_map/ppermute | solution.py:90
  74.9 1.0 copy-done.8
  75.9 0.9 copy-done.10
  76.8 0.9 copy-done.12
  77.8 0.9 copy-done.14
  78.7 0.9 copy-done.16
  79.7 0.9 copy-done.18
  80.6 2.8 %project.1 = (bf16[2048,512]{1,0:T(8,128)(2,1)}, f32[2,128,512]{2,1,0:T(8,128)S(1)}) custom-call(s32[8]{0:T(128)S(1)} %stack.94.chips_ref, bf16[128,4096]{1,0:T(8,128)(2,1)S(1)} %copy-done, bf16[128,4096]{1,0:T(8,128)(2,1)S(1)} %collective-permute-done.8.mate_ref, bf16[256,512]{1,0:T(8,128)(2,1)S(1)} %maximum_select_fusion.refs_0_, ...), custom_call_target="tpu_custom_call" | custom-call | flops 1024 | bytes 1024 | tf_op jit(solution)/shard_map/project/pallas_call | solution.py:420
  84.2 1.4 collective-permute-start.20
  87.1 1.0 collective-permute-done.11.mate_cot_ref
  88.1 2.7 %collective-permute-done.20.refs_7_ = bf16[256,512]{1,0:T(8,128)(2,1)S(1)} collective-permute-done((bf16[256,512]{1,0:T(8,128)(2,1)}, bf16[256,512]{1,0:T(8,128)(2,1)S(1)}, u32[]{:S(2)}, u32[]{:S(2)}) %collective-permute-start.20) | collective-permute-done | bytes 262176 | tf_op jit(solution)/shard_map/ppermute | solution.py:90
  91.5 1.0 copy-done.6
  92.5 0.9 copy-done.20
  93.5 3.8 %delta.1 = (bf16[256,512]{1,0:T(8,128)(2,1)S(1)}, bf16[2048,512]{1,0:T(8,128)(2,1)}) custom-call(s32[16]{0:T(128)S(1)} %stack.93.chips_ref, s32[1]{0:T(128)} %bitcast.16.me_ref, bf16[128,4096]{1,0:T(8,128)(2,1)S(1)} %copy-done, bf16[128,4096]{1,0:T(8,128)(2,1)S(1)} %collective-permute-done.8.mate_ref, bf16[128,512]{1,0:T(8,128)(2,1)S(1)} %get-tuple-element.41.own_cot_ref, ...), custom_call_target="tpu_custom_call" | custom-call | flops 1024 | bytes 1024 | tf_op jit(solution)/shard_map/delta/pallas_call | solution.py:450
  98.8 11.7 %collective-permute-done.22.refs_2_ = bf16[256,512]{1,0:T(8,128)(2,1)S(1)} collective-permute-done((bf16[256,512]{1,0:T(8,128)(2,1)S(1)}, bf16[256,512]{1,0:T(8,128)(2,1)S(1)}, u32[]{:S(2)}, u32[]{:S(2)}) %collective-permute-start.22) | collective-permute-done | bytes 262176 | tf_op jit(solution)/shard_map/ppermute | solution.py:90
  110.5 1.3 collective-permute-done.21.refs_1_
  111.8 1.6 %select.11 = bf16[384,512]{1,0:T(8,128)(2,1)} custom-call(s32[1]{0:T(128)} %bitcast.16.me_ref, s32[8,128]{1,0:T(8,128)S(1)} %pad_add_fusion.code_ref, bf16[256,512]{1,0:T(8,128)(2,1)S(1)} %get-tuple-element.33.refs_0_, bf16[256,512]{1,0:T(8,128)(2,1)S(1)} %collective-permute-done.21.refs_1_, bf16[256,512]{1,0:T(8,128)(2,1)S(1)} %collective-permute-done.22.refs_2_), custom_call_target="tpu_custom_call" | custom-call | flops 1024 | bytes 1024 | tf_op jit(solution)/shard_map/select/pallas_call | solution.py:483
  113.4 3.5 %all-to-all-start.1 = ((bf16[8,48,512]{2,1,0:T(8,128)(2,1)}), bf16[8,48,512]{2,1,0:T(8,128)(2,1)S(1)}, u32[]{:S(2)}, u32[]{:S(2)}) async-start(bf16[8,48,512]{2,1,0:T(8,128)(2,1)} %bitcast.26), calls=%async_computation.1 | async-start | bytes 786432 | tf_op jit(solution)/shard_map/all_to_all | solution.py:475
  117.2 8.2 %collective-permute-done.26.refs_3_ = bf16[256,512]{1,0:T(8,128)(2,1)S(1)} collective-permute-done((bf16[256,512]{1,0:T(8,128)(2,1)S(1)}, bf16[256,512]{1,0:T(8,128)(2,1)S(1)}, u32[]{:S(2)}, u32[]{:S(2)}) %collective-permute-start.26) | collective-permute-done | bytes 262176 | tf_op jit(solution)/shard_map/ppermute | solution.py:90
  125.5 3.0 %weight_grad.1 = bf16[8,144,512]{2,1,0:T(8,128)(2,1)S(1)} custom-call(s32[1]{0:T(128)} %bitcast.16.me_ref, s32[8,128]{1,0:T(8,128)S(1)} %pad_add_fusion.code_ref, bf16[4,128,1024]{2,1,0:T(8,128)(2,1)S(1)} %all-to-all-done.own_ref, bf16[4,128,1024]{2,1,0:T(8,128)(2,1)S(1)} %collective-permute-done.25.mate_ref, ...), custom_call_target="tpu_custom_call" | custom-call | flops 1024 | bytes 1024 | tf_op jit(solution)/shard_map/weight_grad/pallas_call | solution.py:499
  128.5 1.0 copy-done.2
  130.3 4.0 %all-to-all-start.2 = ((bf16[8,144,512]{2,1,0:T(8,128)(2,1)}), bf16[8,144,512]{2,1,0:T(8,128)(2,1)S(1)}, u32[]{:S(2)}, u32[]{:S(2)}) async-start(bf16[8,144,512]{2,1,0:T(8,128)(2,1)} %copy-done.2), calls=%async_computation.2 | async-start | bytes 2359296 | tf_op jit(solution)/shard_map/all_to_all | solution.py:475
  134.3 1.0 copy-done.4
  135.3 8.9 %row_grad.1.before_ref = bf16[256,4096]{1,0:T(8,128)(2,1)} custom-call(s32[16]{0:T(128)S(1)} %stack.93.chips_ref, s32[1]{0:T(128)} %bitcast.16.me_ref, bf16[4,2,48,512]{3,2,1,0:T(8,128)(2,1)S(1)} %bitcast.38, bf16[2048,512]{1,0:T(8,128)(2,1)S(1)} %copy-done.1, bf16[2048,512]{1,0:T(8,128)(2,1)} %collective-permute-done.23.refs_1_, ...), custom_call_target="tpu_custom_call" | custom-call | flops 1024 | bytes 1024 | tf_op jit(solution)/shard_map/row_grad/pallas_call | solution.py:520
  144.2 6.8 %all-to-all-done.2 = bf16[8,144,512]{2,1,0:T(8,128)(2,1)S(1)} async-done(((bf16[8,144,512]{2,1,0:T(8,128)(2,1)}), bf16[8,144,512]{2,1,0:T(8,128)(2,1)S(1)}, u32[]{:S(2)}, u32[]{:S(2)}) %all-to-all-start.2) | async-done | bytes 1179680 | tf_op jit(solution)/shard_map/all_to_all | solution.py:475
  151.1 0.9 sum.1
  152.0 8.2 %far_row_grad.1 = bf16[256,4096]{1,0:T(8,128)(2,1)} custom-call(s32[16]{0:T(128)S(1)} %stack.93.chips_ref, s32[1]{0:T(128)} %bitcast.16.me_ref, bf16[256,4096]{1,0:T(8,128)(2,1)} %row_grad.1.before_ref, bf16[4,2,144,512]{3,2,1,0:T(8,128)(2,1)S(1)} %bitcast.37, bf16[2048,512]{1,0:T(8,128)(2,1)S(1)} %copy-done.1, ...), custom_call_target="tpu_custom_call", output_to_operand_aliasing={{}: (2, {})} | custom-call | flops 1024 | bytes 1024 | tf_op jit(solution)/shard_map/far_row_grad/pallas_call | solution.py:535
  (88 shorter events, 13.0 us)
Async XLA Ops:
  0.6 29.2 %copy-start = (bf16[128,4096]{1,0:T(8,128)(2,1)S(1)}, bf16[128,4096]{1,0:T(8,128)(2,1)}, u32[]{:S(2)}) copy-start(bf16[128,4096]{1,0:T(8,128)(2,1)} %own_ref.3) | copy-start | bytes 3145732
  0.6 1.9 %collective-permute-start.3 = (bf16[128,1024]{1,0:T(8,128)(2,1)}, bf16[128,1024]{1,0:T(8,128)(2,1)S(1)}, u32[]{:S(2)}, u32[]{:S(2)}) collective-permute-start(bf16[128,1024]{1,0:T(8,128)(2,1)} %param.11), channel_id=1, source_target_pairs={{0,1},{1,0},{2,3},{3,2},{4,5},{5,4},{6,7},{7,6},{8,9},{9,8},{10,11... | collective-permute-start | bytes 786440 | tf_op jit(solution)/shard_map/ppermute | solution.py:90
  2.6 16.4 %collective-permute-start.4 = (bf16[256,512]{1,0:T(8,128)(2,1)S(1)}, bf16[256,512]{1,0:T(8,128)(2,1)S(1)}, u32[]{:S(2)}, u32[]{:S(2)}) collective-permute-start(bf16[256,512]{1,0:T(8,128)(2,1)S(1)} %maximum_select_fusion.refs_0_), channel_id=1, source_target_pairs={{0,16},{1,17},{2,18},{3,19},{4,20},{5,21},{6,22},{7,23},{8,24},{9,... | collective-permute-start | bytes 786440 | tf_op jit(solution)/shard_map/ppermute | solution.py:90
  6.7 12.5 %collective-permute-start.5 = (bf16[256,512]{1,0:T(8,128)(2,1)S(1)}, bf16[256,512]{1,0:T(8,128)(2,1)S(1)}, u32[]{:S(2)}, u32[]{:S(2)}) collective-permute-start(bf16[256,512]{1,0:T(8,128)(2,1)S(1)} %maximum_select_fusion.refs_0_), channel_id=1, source_target_pairs={{0,8},{1,9},{2,10},{3,11},{4,12},{5,13},{6,14},{7,15},{8,0},{9,1},... | collective-permute-start | bytes 786440 | tf_op jit(solution)/shard_map/ppermute | solution.py:90
  8.2 11.0 %collective-permute-start.6 = (bf16[256,512]{1,0:T(8,128)(2,1)S(1)}, bf16[256,512]{1,0:T(8,128)(2,1)S(1)}, u32[]{:S(2)}, u32[]{:S(2)}) collective-permute-start(bf16[256,512]{1,0:T(8,128)(2,1)S(1)} %maximum_select_fusion.refs_0_), channel_id=1, source_target_pairs={{0,4},{1,5},{2,6},{3,7},{4,0},{5,1},{6,2},{7,3},{8,12},{9,13},{10,... | collective-permute-start | bytes 786440 | tf_op jit(solution)/shard_map/ppermute | solution.py:90
  9.7 9.4 %collective-permute-start.7 = (bf16[256,512]{1,0:T(8,128)(2,1)S(1)}, bf16[256,512]{1,0:T(8,128)(2,1)S(1)}, u32[]{:S(2)}, u32[]{:S(2)}) collective-permute-start(bf16[256,512]{1,0:T(8,128)(2,1)S(1)} %maximum_select_fusion.refs_0_), channel_id=1, source_target_pairs={{0,2},{1,3},{2,0},{3,1},{4,6},{5,7},{6,4},{7,5},{8,10},{9,11},{10,... | collective-permute-start | bytes 786440 | tf_op jit(solution)/shard_map/ppermute | solution.py:90
  19.0 12.1 %copy-start.9 = (bf16[256,512]{1,0:T(8,128)(2,1)}, bf16[256,512]{1,0:T(8,128)(2,1)S(1)}, u32[]{:S(2)}) copy-start(bf16[256,512]{1,0:T(8,128)(2,1)S(1)} %collective-permute-done.4.refs_6_) | copy-start | bytes 786436
  19.2 11.9 %copy-start.11 = (bf16[256,512]{1,0:T(8,128)(2,1)}, bf16[256,512]{1,0:T(8,128)(2,1)S(1)}, u32[]{:S(2)}) copy-start(bf16[256,512]{1,0:T(8,128)(2,1)S(1)} %collective-permute-done.5.refs_3_) | copy-start | bytes 786436
  19.2 11.9 %copy-start.13 = (bf16[256,512]{1,0:T(8,128)(2,1)}, bf16[256,512]{1,0:T(8,128)(2,1)S(1)}, u32[]{:S(2)}) copy-start(bf16[256,512]{1,0:T(8,128)(2,1)S(1)} %collective-permute-done.6.refs_2_) | copy-start | bytes 786436
  19.9 7.6 %collective-permute-start.12 = (bf16[256,512]{1,0:T(8,128)(2,1)S(1)}, bf16[256,512]{1,0:T(8,128)(2,1)S(1)}, u32[]{:S(2)}, u32[]{:S(2)}) collective-permute-start(bf16[256,512]{1,0:T(8,128)(2,1)S(1)} %collective-permute-done.5.refs_3_), channel_id=1, source_target_pairs={{0,2},{1,3},{2,0},{3,1},{4,6},{5,7},{6,4},{7,5},{8,10},{9,11},{10,... | collective-permute-start | bytes 786440 | tf_op jit(solution)/shard_map/ppermute | solution.py:90
  21.5 7.0 %collective-permute-start.13 = (bf16[256,512]{1,0:T(8,128)(2,1)S(1)}, bf16[256,512]{1,0:T(8,128)(2,1)S(1)}, u32[]{:S(2)}, u32[]{:S(2)}) collective-permute-start(bf16[256,512]{1,0:T(8,128)(2,1)S(1)} %collective-permute-done.5.refs_3_), channel_id=1, source_target_pairs={{0,4},{1,5},{2,6},{3,7},{4,0},{5,1},{6,2},{7,3},{8,12},{9,13},{10,... | collective-permute-start | bytes 786440 | tf_op jit(solution)/shard_map/ppermute | solution.py:90
  23.0 6.9 %collective-permute-start.14 = (bf16[256,512]{1,0:T(8,128)(2,1)S(1)}, bf16[256,512]{1,0:T(8,128)(2,1)}, u32[]{:S(2)}, u32[]{:S(2)}) collective-permute-start(bf16[256,512]{1,0:T(8,128)(2,1)S(1)} %collective-permute-done.4.refs_6_), channel_id=1, source_target_pairs={{0,8},{1,9},{2,10},{3,11},{4,12},{5,13},{6,14},{7,15},{8,0},{9,1},... | collective-permute-start | bytes 786440 | tf_op jit(solution)/shard_map/ppermute | solution.py:90
  25.3 49.6 %collective-permute-start.8 = (bf16[128,4096]{1,0:T(8,128)(2,1)}, bf16[128,4096]{1,0:T(8,128)(2,1)S(1)}, u32[]{:S(2)}, u32[]{:S(2)}) collective-permute-start(bf16[128,4096]{1,0:T(8,128)(2,1)} %own_ref.3), channel_id=1, source_target_pairs={{0,1},{1,0},{2,3},{3,2},{4,5},{5,4},{6,7},{7,6},{8,9},{9,8},{10,11... | collective-permute-start | bytes 3145736 | tf_op jit(solution)/shard_map/ppermute | solution.py:90
  28.5 2.6 %copy-start.7 = (bf16[256,512]{1,0:T(8,128)(2,1)}, bf16[256,512]{1,0:T(8,128)(2,1)S(1)}, u32[]{:S(2)}) copy-start(bf16[256,512]{1,0:T(8,128)(2,1)S(1)} %collective-permute-done.13.refs_5_) | copy-start | bytes 786436
  29.9 6.6 %copy-start.22 = (s32[128,1]{0,1:T(1,128)S(1)}, s32[128,1]{0,1:T(1,128)}, u32[]{:S(2)}) copy-start(s32[128,1]{0,1:T(1,128)} %param.8) | copy-start | bytes 1540
  30.0 35.3 %copy-start.23 = (s32[1,4]{1,0:T(1,128)S(1)}, s32[1,4]{1,0:T(1,128)}, u32[]{:S(2)}) copy-start(s32[1,4]{1,0:T(1,128)} %param.9) | copy-start | bytes 52
  30.0 35.5 %copy-start.24 = (s32[4]{0:T(128)S(1)}, s32[4]{0:T(128)}, u32[]{:S(2)}) copy-start(s32[4]{0:T(128)} %param.10) | copy-start | bytes 52
  31.1 56.0 %all-to-all-start = ((bf16[4,128,1024]{2,1,0:T(8,128)(2,1)}), bf16[4,128,1024]{2,1,0:T(8,128)(2,1)S(1)}, u32[]{:S(2)}, u32[]{:S(2)}) async-start(bf16[4,128,1024]{2,1,0:T(8,128)(2,1)} %pad_maximum_fusion), calls=%async_computation | async-start | bytes 2097152 | tf_op jit(solution)/shard_map/all_to_all | solution.py:391
  36.6 1.2 collective-permute-start
  37.8 14.7 %collective-permute-start.1 = (s32[2,128]{1,0:T(2,128)S(1)}, s32[2,128]{1,0:T(2,128)S(1)}, u32[]{:S(2)}, u32[]{:S(2)}) collective-permute-start(s32[2,128]{1,0:T(2,128)S(1)} %add_select_fusion.1), channel_id=1, source_target_pairs={{0,8},{1,9},{2,10},{3,11},{4,12},{5,13},{6,14},{7,15},{8,0},{9,1},... | collective-permute-start | bytes 3080 | tf_op jit(solution)/shard_map/ppermute | solution.py:90
  39.8 23.3 %collective-permute-start.9 = (bf16[256,512]{1,0:T(8,128)(2,1)}, bf16[256,512]{1,0:T(8,128)(2,1)}, u32[]{:S(2)}, u32[]{:S(2)}) collective-permute-start(bf16[256,512]{1,0:T(8,128)(2,1)} %copy-done.9), channel_id=1, source_target_pairs={{0,2},{1,3},{2,0},{3,1},{4,6},{5,7},{6,4},{7,5},{8,10},{9,11},{10,... | collective-permute-start | bytes 786440 | tf_op jit(solution)/shard_map/ppermute | solution.py:90
  40.3 22.8 %collective-permute-start.10 = (bf16[256,512]{1,0:T(8,128)(2,1)}, bf16[256,512]{1,0:T(8,128)(2,1)}, u32[]{:S(2)}, u32[]{:S(2)}) collective-permute-start(bf16[256,512]{1,0:T(8,128)(2,1)} %copy-done.9), channel_id=1, source_target_pairs={{0,4},{1,5},{2,6},{3,7},{4,0},{5,1},{6,2},{7,3},{8,12},{9,13},{10,... | collective-permute-start | bytes 786440 | tf_op jit(solution)/shard_map/ppermute | solution.py:90
  52.5 8.6 %collective-permute-start.2 = (s32[4,128]{1,0:T(4,128)S(1)}, s32[4,128]{1,0:T(4,128)S(1)}, u32[]{:S(2)}, u32[]{:S(2)}) collective-permute-start(s32[4,128]{1,0:T(4,128)S(1)} %pad_add_fusion.1), channel_id=1, source_target_pairs={{0,16},{1,17},{2,18},{3,19},{4,20},{5,21},{6,22},{7,23},{8,24},{9,... | collective-permute-start | bytes 6152 | tf_op jit(solution)/shard_map/ppermute | solution.py:90
  61.1 9.6 %collective-permute-start.16 = (bf16[256,512]{1,0:T(8,128)(2,1)}, bf16[256,512]{1,0:T(8,128)(2,1)}, u32[]{:S(2)}, u32[]{:S(2)}) collective-permute-start(bf16[256,512]{1,0:T(8,128)(2,1)} %collective-permute-done.14.refs_2_), channel_id=1, source_target_pairs={{0,2},{1,3},{2,0},{3,1},{4,6},{5,7},{6,4},{7,5},{8,10},{9,11},{10,... | collective-permute-start | bytes 786440 | tf_op jit(solution)/shard_map/ppermute | solution.py:90
  61.7 22.5 %collective-permute-start.17 = (bf16[256,512]{1,0:T(8,128)(2,1)}, bf16[256,512]{1,0:T(8,128)(2,1)}, u32[]{:S(2)}, u32[]{:S(2)}) collective-permute-start(bf16[256,512]{1,0:T(8,128)(2,1)} %collective-permute-done.14.refs_2_), channel_id=1, source_target_pairs={{0,4},{1,5},{2,6},{3,7},{4,0},{5,1},{6,2},{7,3},{8,12},{9,13},{10,... | collective-permute-start | bytes 786440 | tf_op jit(solution)/shard_map/ppermute | solution.py:90
  63.1 21.1 %collective-permute-start.18 = (bf16[256,512]{1,0:T(8,128)(2,1)}, bf16[256,512]{1,0:T(8,128)(2,1)}, u32[]{:S(2)}, u32[]{:S(2)}) collective-permute-start(bf16[256,512]{1,0:T(8,128)(2,1)} %collective-permute-done.9.refs_7_), channel_id=1, source_target_pairs={{0,4},{1,5},{2,6},{3,7},{4,0},{5,1},{6,2},{7,3},{8,12},{9,13},{10,... | collective-permute-start | bytes 786440 | tf_op jit(solution)/shard_map/ppermute | solution.py:90
  63.7 10.6 %collective-permute-start.15 = (bf16[256,512]{1,0:T(8,128)(2,1)}, bf16[256,512]{1,0:T(8,128)(2,1)}, u32[]{:S(2)}, u32[]{:S(2)}) collective-permute-start(bf16[256,512]{1,0:T(8,128)(2,1)} %copy-done.13), channel_id=1, source_target_pairs={{0,2},{1,3},{2,0},{3,1},{4,6},{5,7},{6,4},{7,5},{8,10},{9,11},{10,... | collective-permute-start | bytes 786440 | tf_op jit(solution)/shard_map/ppermute | solution.py:90
  74.3 13.7 %collective-permute-start.19 = (bf16[256,512]{1,0:T(8,128)(2,1)}, bf16[256,512]{1,0:T(8,128)(2,1)}, u32[]{:S(2)}, u32[]{:S(2)}) collective-permute-start(bf16[256,512]{1,0:T(8,128)(2,1)} %copy-done.7), channel_id=1, source_target_pairs={{0,2},{1,3},{2,0},{3,1},{4,6},{5,7},{6,4},{7,5},{8,10},{9,11},{10,... | collective-permute-start | bytes 786440 | tf_op jit(solution)/shard_map/ppermute | solution.py:90
  74.9 1.0 copy-start.8
  75.9 0.9 copy-start.10
  76.8 0.9 copy-start.12
  77.8 0.9 copy-start.14
  78.7 0.9 copy-start.16
  80.6 5.0 %copy-start.21 = (bf16[128,1024]{1,0:T(8,128)(2,1)S(1)}, bf16[128,1024]{1,0:T(8,128)(2,1)}, u32[]{:S(2)}) copy-start(bf16[128,1024]{1,0:T(8,128)(2,1)} %param.7) | copy-start | bytes 786436
  84.2 6.6 %collective-permute-start.20 = (bf16[256,512]{1,0:T(8,128)(2,1)}, bf16[256,512]{1,0:T(8,128)(2,1)S(1)}, u32[]{:S(2)}, u32[]{:S(2)}) collective-permute-start(bf16[256,512]{1,0:T(8,128)(2,1)} %collective-permute-done.16.refs_3_), channel_id=1, source_target_pairs={{0,4},{1,5},{2,6},{3,7},{4,0},{5,1},{6,2},{7,3},{8,12},{9,13},{10,... | collective-permute-start | bytes 786440 | tf_op jit(solution)/shard_map/ppermute | solution.py:90
  86.4 1.7 %collective-permute-start.11 = (bf16[128,512]{1,0:T(8,128)(2,1)}, bf16[128,512]{1,0:T(8,128)(2,1)}, u32[]{:S(2)}, u32[]{:S(2)}) collective-permute-start(bf16[128,512]{1,0:T(8,128)(2,1)} %get-tuple-element.40), channel_id=1, source_target_pairs={{0,1},{1,0},{2,3},{3,2},{4,5},{5,4},{6,7},{7,6},{8,9},{9,8},{10,11... | collective-permute-start | bytes 393224 | tf_op jit(solution)/shard_map/ppermute | solution.py:90
  86.5 47.8 %collective-permute-start.23 = (bf16[2048,512]{1,0:T(8,128)(2,1)}, bf16[2048,512]{1,0:T(8,128)(2,1)}, u32[]{:S(2)}, u32[]{:S(2)}) collective-permute-start(bf16[2048,512]{1,0:T(8,128)(2,1)} %get-tuple-element.34.refs_0_), channel_id=1, source_target_pairs={{0,1},{1,0},{2,3},{3,2},{4,5},{5,4},{6,7},{7,6},{8,9},{9,8},{10,11... | collective-permute-start | bytes 6291464 | tf_op jit(solution)/shard_map/ppermute | solution.py:90
  91.5 1.0 copy-start.6
  97.3 37.0 %collective-permute-start.24 = (bf16[2048,512]{1,0:T(8,128)(2,1)}, bf16[2048,512]{1,0:T(8,128)(2,1)}, u32[]{:S(2)}, u32[]{:S(2)}) collective-permute-start(bf16[2048,512]{1,0:T(8,128)(2,1)} %get-tuple-element.35.refs_2_), channel_id=1, source_target_pairs={{0,1},{1,0},{2,3},{3,2},{4,5},{5,4},{6,7},{7,6},{8,9},{9,8},{10,11... | collective-permute-start | bytes 6291464 | tf_op jit(solution)/shard_map/ppermute | solution.py:90
  97.3 28.1 %collective-permute-start.25 = (bf16[4,128,1024]{2,1,0:T(8,128)(2,1)S(1)}, bf16[4,128,1024]{2,1,0:T(8,128)(2,1)S(1)}, u32[]{:S(2)}, u32[]{:S(2)}) collective-permute-start(bf16[4,128,1024]{2,1,0:T(8,128)(2,1)S(1)} %all-to-all-done.own_ref), channel_id=1, source_target_pairs={{0,1},{1,0},{2,3},{3,2},{4,5},{5,4},{6,7},{7,6},{8,9},{9,8},{10,11... | collective-permute-start | bytes 3145736 | tf_op jit(solution)/shard_map/ppermute | solution.py:90
  97.8 12.6 %collective-permute-start.22 = (bf16[256,512]{1,0:T(8,128)(2,1)S(1)}, bf16[256,512]{1,0:T(8,128)(2,1)S(1)}, u32[]{:S(2)}, u32[]{:S(2)}) collective-permute-start(bf16[256,512]{1,0:T(8,128)(2,1)S(1)} %get-tuple-element.33.refs_0_), channel_id=1, source_target_pairs={{0,16},{1,17},{2,18},{3,19},{4,20},{5,21},{6,22},{7,23},{8,24},{9,... | collective-permute-start | bytes 786440 | tf_op jit(solution)/shard_map/ppermute | solution.py:90
  97.8 13.9 %collective-permute-start.21 = (bf16[256,512]{1,0:T(8,128)(2,1)S(1)}, bf16[256,512]{1,0:T(8,128)(2,1)S(1)}, u32[]{:S(2)}, u32[]{:S(2)}) collective-permute-start(bf16[256,512]{1,0:T(8,128)(2,1)S(1)} %get-tuple-element.33.refs_0_), channel_id=1, source_target_pairs={{0,8},{1,9},{2,10},{3,11},{4,12},{5,13},{6,14},{7,15},{8,0},{9,1},... | collective-permute-start | bytes 786440 | tf_op jit(solution)/shard_map/ppermute | solution.py:90
  113.4 16.1 %all-to-all-start.1 = ((bf16[8,48,512]{2,1,0:T(8,128)(2,1)}), bf16[8,48,512]{2,1,0:T(8,128)(2,1)S(1)}, u32[]{:S(2)}, u32[]{:S(2)}) async-start(bf16[8,48,512]{2,1,0:T(8,128)(2,1)} %bitcast.26), calls=%async_computation.1 | async-start | bytes 786432 | tf_op jit(solution)/shard_map/all_to_all | solution.py:475
  116.9 8.6 %collective-permute-start.26 = (bf16[256,512]{1,0:T(8,128)(2,1)S(1)}, bf16[256,512]{1,0:T(8,128)(2,1)S(1)}, u32[]{:S(2)}, u32[]{:S(2)}) collective-permute-start(bf16[256,512]{1,0:T(8,128)(2,1)S(1)} %collective-permute-done.22.refs_2_), channel_id=1, source_target_pairs={{0,8},{1,9},{2,10},{3,11},{4,12},{5,13},{6,14},{7,15},{8,0},{9,1},... | collective-permute-start | bytes 786440 | tf_op jit(solution)/shard_map/ppermute | solution.py:90
  128.5 1.0 copy-start.2
  129.5 4.8 %copy-start.1 = (bf16[2048,512]{1,0:T(8,128)(2,1)S(1)}, bf16[2048,512]{1,0:T(8,128)(2,1)}, u32[]{:S(2)}) copy-start(bf16[2048,512]{1,0:T(8,128)(2,1)} %get-tuple-element.34.refs_0_) | copy-start | bytes 6291460
  130.3 20.8 %all-to-all-start.2 = ((bf16[8,144,512]{2,1,0:T(8,128)(2,1)}), bf16[8,144,512]{2,1,0:T(8,128)(2,1)S(1)}, u32[]{:S(2)}, u32[]{:S(2)}) async-start(bf16[8,144,512]{2,1,0:T(8,128)(2,1)} %copy-done.2), calls=%async_computation.2 | async-start | bytes 2359296 | tf_op jit(solution)/shard_map/all_to_all | solution.py:475
  134.3 1.0 copy-start.4
  (7 other events, 5.6 us)

commit v8 on v7

--- a/solution.py
+++ b/solution.py
@@ -10,7 +10,8 @@
 
 HEAD_DIM = 128
 NSUB = 4
-VMEM_LIMIT = 48 * 1024 * 1024
+VMEM_LIMIT = 20 * 1024 * 1024
+CODE_ROWS = 16
 epsilon = 1e-06
 
 
@@ -98,58 +99,29 @@
     return lax.dot_general(a, b, (dims, ((), ())), preferred_element_type=jnp.float32)
 
 
-def fetch(pairs, sems):
-    copies = [
-        pltpu.make_async_copy(source, target, sems.at[n])
-        for n, (source, target) in enumerate(pairs)
-    ]
-    for copy in copies:
-        copy.start()
-    return copies
-
-
-def add_products(chips_ref, begin, token_refs, pieces, weight_ref, acc, held, weights, sems, fresh):
-    depth = pieces[0].shape[0]
-
-    def rows_of(ref, n):
-        return ref.at[n * depth : (n + 1) * depth, :]
-
-    pairs = [(ref, held.at[side]) for side, ref in enumerate(token_refs)]
-    pairs += [(ref, rows_of(weights, n)) for n, ref in enumerate(pieces)]
-    copies = fetch(pairs, sems)
-    for copy in copies[:2]:
-        copy.wait()
-    kept = []
-    for n in range(len(pieces)):
-        copies[2 + n].wait()
-        out = pltpu.make_async_copy(
-            rows_of(weights, n), rows_of(weight_ref, n), sems.at[2 + len(pieces) + n]
-        )
-        out.start()
-        kept.append(out)
-        piece = weights[n * depth : (n + 1) * depth, :]
-        at = pl.multiple_of(chips_ref[begin + n] * depth, depth)
-        for side in range(2):
-            part = dot(held[side, :, pl.ds(at, depth)], piece, ((1,), (0,)))
-            if fresh and n == 0:
+def add_products(places, chips_ref, begin, token_refs, pieces, weight_ref, acc, fresh):
+    chip_rows = max(piece.shape[0] for piece in pieces)
+    for (chip, first), piece_ref in zip(places, pieces):
+        piece = piece_ref[...]
+        depth = piece.shape[0]
+        weight_ref[chip * chip_rows + first : chip * chip_rows + first + depth, :] = piece
+        at = pl.multiple_of(chips_ref[begin + chip] * chip_rows + first, 128)
+        for side, ref in enumerate(token_refs):
+            part = dot(ref[:, pl.ds(at, depth)], piece, ((1,), (0,)))
+            if fresh:
                 acc[side] = part
             else:
                 acc[side] += part
-    return kept
-
-
-def project_kernel(count, chips_ref, own_ref, mate_ref, *refs):
-    pieces = refs[:count]
-    weight_ref, acc_ref, held, weights, sems = refs[count:]
-    kept = add_products(
-        chips_ref, 0, (own_ref, mate_ref), pieces, weight_ref, acc_ref, held, weights, sems, True
-    )
-    for copy in kept:
-        copy.wait()
+        fresh = False
+
+
+def project_kernel(places, chips_ref, own_ref, mate_ref, *refs):
+    *pieces, weight_ref, acc_ref = refs
+    add_products(places, chips_ref, 0, (own_ref, mate_ref), pieces, weight_ref, acc_ref, True)
 
 
 def delta_kernel(
-    count,
+    places,
     begin,
     chips_ref,
     me_ref,
@@ -160,14 +132,12 @@
     begun_ref,
     *refs,
 ):
-    pieces = refs[:count]
-    delta_ref, weight_ref, acc, held, weights, sems = refs[count:]
+    *pieces, delta_ref, weight_ref, acc = refs
     core = me_ref[0] & 1
     rows = own_ref.shape[0]
     acc[...] = begun_ref[...]
-    kept = add_products(
-        chips_ref, begin, (own_ref, mate_ref), pieces, weight_ref, acc, held, weights, sems, False
-    )
+    add_products(places, chips_ref, begin, (own_ref, mate_ref), pieces, weight_ref, acc, False)
+    delta_ref[2 * rows :, :] = jnp.zeros_like(delta_ref[2 * rows :, :])
     for side, cot_ref in enumerate((own_cot_ref, mate_cot_ref)):
         at = pl.multiple_of((core ^ side) * rows, rows)
         for head in range(own_cot_ref.shape[1] // HEAD_DIM):
@@ -175,59 +145,43 @@
             proj = acc[side, :, cols]
             scale = jnp.sqrt(jnp.mean(proj * proj, axis=1, keepdims=True) + epsilon)
             normed = proj / scale
-            upstream = cot_ref[:, cols].astype(jnp.float32)
+            upstream = cot_ref[:rows, cols].astype(jnp.float32)
             delta = (upstream - normed * jnp.mean(upstream * normed, axis=1, keepdims=True)) / scale
             delta_ref[pl.ds(at, rows), cols] = delta.astype(jnp.bfloat16)
-    for copy in kept:
-        copy.wait()
-
-
-def selected_rows(plane, code_ref, levels, deltas, slot_count):
-    rows = code_ref.shape[1]
-    per_chip = slot_count // (PLANE * len(levels))
-    iota = lax.broadcasted_iota(jnp.int32, (slot_count, rows), 0)
-    destination, slot = iota // (per_chip * len(levels)), iota % (per_chip * len(levels))
+        delta_ref[2 * rows :, pl.ds(at, rows)] = cot_ref[rows:, :rows]
+
+
+def selected_rows(plane, deltas, slot_count):
+    rows = (deltas[0].shape[0] - CODE_ROWS) // 2
+    per_chip = slot_count // (PLANE * len(deltas))
+    iota = lax.broadcasted_iota(jnp.int32, (slot_count, 2 * rows), 0)
+    destination, slot = iota // (per_chip * len(deltas)), iota % (per_chip * len(deltas))
+    destination = destination + plane * PLANE
     total = None
-    for n, level in enumerate(levels):
-        for side in range(2):
-            want = (plane * PLANE + destination) * per_chip + slot - n * per_chip
-            inside = (slot >= n * per_chip) & (slot < (n + 1) * per_chip)
-            code = code_ref[2 * level + side : 2 * level + side + 1, :]
-            hot = (inside & (want == code)).astype(jnp.bfloat16)
-            part = dot(hot, deltas[n][side * rows : (side + 1) * rows, :], ((1,), (0,)))
-            total = part if total is None else total + part
+    for n, delta in enumerate(deltas):
+        code = delta[2 * rows :, : 2 * rows].astype(jnp.float32).astype(jnp.int32)
+        hot = (destination == code[0:1, :]) & (slot == code[1:2, :] + n * per_chip)
+        part = dot(hot.astype(jnp.bfloat16), delta[: 2 * rows, :], ((1,), (0,)))
+        total = part if total is None else total + part
     return total.astype(jnp.bfloat16)
 
 
-def select_kernel(levels, me_ref, code_ref, *refs):
-    *deltas, sent_ref, held, sems = refs
-    for copy in fetch([(ref, held.at[n]) for n, ref in enumerate(deltas)], sems):
-        copy.wait()
+def select_kernel(me_ref, *refs):
+    *deltas, sent_ref = refs
     plane = lax.shift_right_logical(me_ref[0], 3)
-    values = [held[n] for n in range(len(deltas))]
-    sent_ref[...] = selected_rows(plane, code_ref, levels, values, sent_ref.shape[0])
-
-
-def weight_grad_kernel(me_ref, code_ref, own_ref, mate_ref, *refs):
-    *deltas, part_ref, hidden, held, acc, sems = refs
+    values = [ref[...] for ref in deltas]
+    sent_ref[...] = selected_rows(plane, values, sent_ref.shape[0])
+
+
+def weight_grad_kernel(me_ref, own_ref, mate_ref, *refs):
+    *deltas, part_ref, acc = refs
     plane = lax.shift_right_logical(me_ref[0], 3)
     core = me_ref[0] & 1
     rows = own_ref.shape[1]
-    count = len(deltas)
-    pairs = []
-    for n, ref in enumerate(deltas):
-        pairs += [
-            (own_ref.at[plane ^ n], hidden.at[n, 0]),
-            (mate_ref.at[plane ^ n], hidden.at[n, 1]),
-            (ref, held.at[n]),
-        ]
-    copies = fetch(pairs, sems)
-    for n in range(count):
-        for copy in copies[3 * n : 3 * n + 3]:
-            copy.wait()
-        for side in range(2):
+    for n, delta_ref in enumerate(deltas):
+        for side, ref in enumerate((own_ref, mate_ref)):
             at = pl.multiple_of((core ^ side) * rows, rows)
-            part = dot(hidden[n, side], held[n, pl.ds(at, rows), :], ((0,), (0,)))
+            part = dot(ref[plane ^ n], delta_ref[pl.ds(at, rows), :], ((0,), (0,)))
             if n + side == 0:
                 acc[...] = part
             else:
@@ -235,7 +189,7 @@
     blocks, depth, _ = part_ref.shape
     shard = acc.shape[0] // blocks
     extra = depth - shard
-    far = selected_rows(plane, code_ref, (count - 1,), [held[count - 1]], blocks * extra)
+    far = selected_rows(plane, [deltas[-1][...]], blocks * extra)
     for block in range(blocks):
         part_ref[block, :shard, :] = acc[block * shard : (block + 1) * shard, :].astype(
             jnp.bfloat16
@@ -302,22 +256,14 @@
     add_columns(me_ref[0] & 1, step, chips_ref, rows_ref, weights, out_ref)
 
 
-def column_codes(destination, core, per_peer):
+def code_rows(destination, core, per_peer, width):
     positions = jnp.arange(destination.shape[0], dtype=jnp.int32)
     same = (destination[:, None] == destination[None, :]) & (
         positions[:, None] < positions[None, :]
     )
     earlier = jnp.sum(same.astype(jnp.int32), axis=0)
-    code = ((destination * 2 + core) * per_peer + earlier).reshape(1, -1)
-    mate_code = swap(code, CORE)
-    codes = jnp.where(
-        core == 0,
-        jnp.concatenate([code, mate_code], axis=0),
-        jnp.concatenate([mate_code, code], axis=0),
-    )
-    for bit in (PLANE, 2 * PLANE):
-        codes = jnp.concatenate([codes, swap(codes, bit)], axis=0)
-    return codes
+    codes = jnp.stack([destination, core * per_peer + earlier]).astype(jnp.bfloat16)
+    return jnp.pad(codes, ((0, CODE_ROWS - 2), (0, width - destination.shape[0])))
 
 
 def vmem(count):
@@ -362,34 +308,26 @@
         jnp.concatenate([mate_shard[:, half_cols:], key_weight[:, half_cols:]], axis=0),
     )
     near, far, both = PLANE, 2 * PLANE, 3 * PLANE
-    z_far, z_near = swap(piece, far), swap(piece, near)
-    x_own, y_own = swap(piece, X), swap(piece, Y)
-    z_far, z_near, y_own, *_ = lax.optimization_barrier((z_far, z_near, y_own, x_own))
-    z_both = swap(z_far, near)
-    x_near, y_near = swap(z_near, X), swap(z_near, Y)
-    x_far, y_far = swap(z_far, X), swap(z_far, Y)
-    codes = column_codes(routes[:, 0], core, per_peer)
-    z_both_late = after(z_both, x_near, y_near, codes)
-    x_both, y_both = swap(z_both_late, X), swap(z_both_late, Y)
-    d_far = swap(after(x_far, y_far), Y)
-    d_own = swap(after(y_own, x_far), X)
-    d_near = swap(after(y_near, x_both, d_own), X)
-    first_pieces = {
-        0: piece,
-        X: x_own,
-        Y: y_own,
-        near: z_near,
-        near | X: x_near,
-        near | Y: y_near,
-        far: z_far,
-        far | X: x_far,
-    }
-
-    mate_tokens = swap(after(tokens, z_near), CORE)
+    column = {0: piece, far: swap(piece, far), near: swap(piece, near)}
+    column[both] = swap(column[far], near)
+    half = piece.shape[0] // 2
+    sets, masks = [], []
+    for part in ((0, near), (far, both)):
+        pieces, places = [], []
+        for mask in part:
+            own = column[mask]
+            by_x, by_y = swap(own, X), swap(own, Y)
+            chip = len(masks) % (chips // 2)
+            masks += [mask, mask | X, mask | Y, mask | X | Y]
+            pieces += [own, by_x, by_y, swap(by_y[:half], X), swap(by_x[half:], Y)]
+            places += [(chip, 0), (chip + 1, 0), (chip + 2, 0), (chip + 3, 0), (chip + 3, half)]
+        sets.append((pieces, places))
+    order = jnp.stack([lax.shift_right_logical(me ^ mask, 1) for mask in masks])
+
+    mate_tokens = swap(after(tokens, column[near]), CORE)
     columns = [[p + PLANE * z for z in range(levels)] for p in range(PLANE)]
-    late_tokens = after(tokens, z_both, x_near, y_near)
     own_features = lax.all_to_all(
-        jnp.stack([late_tokens[:, z * wide : (z + 1) * wide] for z in range(levels)]),
+        jnp.stack([tokens[:, z * wide : (z + 1) * wide] for z in range(levels)]),
         "dp",
         split_axis=0,
         concat_axis=0,
@@ -398,7 +336,7 @@
     )
     mate_features = swap(own_features, CORE)
 
-    key_cot, counts = lax.optimization_barrier((key_cot, counts, x_far, y_far))[:2]
+    key_cot, counts, routes = lax.optimization_barrier((key_cot, counts, routes, column[near]))[:3]
     bounds = jnp.cumsum(counts[0])
     positions = jnp.arange(rows, dtype=jnp.int32)
     subnet = jnp.sum((positions[:, None] >= bounds[None, : NSUB - 1]).astype(jnp.int32), axis=1)
@@ -408,64 +346,32 @@
     upstream = jnp.where(
         head_of_col[None, :] < row_width[:, None], key_cot, jnp.zeros_like(key_cot)
     )
-    own_cot, mate_cot = mine(upstream), swap(theirs(upstream), CORE)
+    codes = code_rows(routes[:, 0], core, per_peer, half_cols)
+    own_cot = jnp.concatenate([mine(upstream), codes], axis=0)
+    mate_cot = swap(jnp.concatenate([theirs(upstream), codes], axis=0), CORE)
 
     kept = jax.ShapeDtypeStruct((width_model // 2, half_cols), jnp.bfloat16)
     sums = jax.ShapeDtypeStruct((2, rows, half_cols), jnp.float32)
-    room = [
-        pltpu.VMEM((2, rows, width_model), jnp.bfloat16),
-        pltpu.VMEM((width_model // 2, half_cols), jnp.bfloat16),
-        pltpu.SemaphoreType.DMA((2 + chips,)),
-    ]
+    (pieces, places), (last_pieces, last_places) = sets
     first_weight, begun = pl.pallas_call(
-        functools.partial(project_kernel, len(first_pieces)),
+        functools.partial(project_kernel, places),
         out_shape=(kept, sums),
-        in_specs=[SCALAR] + anywhere(2 + len(first_pieces)),
-        out_specs=(anywhere(1)[0], vmem(1)[0]),
-        scratch_shapes=room,
+        in_specs=[SCALAR] + vmem(2 + len(pieces)),
+        out_specs=tuple(vmem(2)),
         compiler_params=PARAMS,
         cost_estimate=COST,
         name="project",
-    )(
-        jnp.stack([lax.shift_right_logical(me ^ mask, 1) for mask in first_pieces]),
-        tokens,
-        mate_tokens,
-        *first_pieces.values(),
-    )
-    d_both = swap(after(x_both, begun, d_far, y_both), Y)
-    last_pieces = {
-        far | Y: y_far,
-        X | Y: d_own,
-        both: z_both,
-        both | X: x_both,
-        both | Y: y_both,
-        far | X | Y: d_far,
-        near | X | Y: d_near,
-        both | X | Y: d_both,
-    }
-    order = jnp.stack(
-        [lax.shift_right_logical(me ^ mask, 1) for mask in (*first_pieces, *last_pieces)]
-    )
-    begun = after(begun, own_features)
+    )(order, tokens, mate_tokens, *pieces)
     delta, last_weight = pl.pallas_call(
-        functools.partial(delta_kernel, len(last_pieces), len(first_pieces)),
-        out_shape=(jax.ShapeDtypeStruct((2 * rows, half_cols), jnp.bfloat16), kept),
-        in_specs=[SCALAR] * 2 + anywhere(2) + vmem(3) + anywhere(len(last_pieces)),
-        out_specs=(vmem(1)[0], anywhere(1)[0]),
-        scratch_shapes=[pltpu.VMEM(sums.shape, sums.dtype)] + room,
+        functools.partial(delta_kernel, last_places, chips // 2),
+        out_shape=(jax.ShapeDtypeStruct((2 * rows + CODE_ROWS, half_cols), jnp.bfloat16), kept),
+        in_specs=[SCALAR] * 2 + vmem(5 + len(last_pieces)),
+        out_specs=tuple(vmem(2)),
+        scratch_shapes=[pltpu.VMEM(sums.shape, sums.dtype)],
         compiler_params=PARAMS,
         cost_estimate=COST,
         name="delta",
-    )(
-        order,
-        me_scalar,
-        tokens,
-        mate_tokens,
-        own_cot,
-        mate_cot,
-        begun,
-        *last_pieces.values(),
-    )
+    )(order, me_scalar, tokens, mate_tokens, own_cot, mate_cot, begun, *last_pieces)
 
     delta_far, delta_near = swap(delta, far), swap(delta, near)
     delta_both = swap(delta_far, near)
@@ -479,38 +385,28 @@
 
     per_chip = 2 * per_peer
     near_deltas = [delta, delta_near, delta_far]
-    piece_room = (2 * rows, half_cols)
     selected = pl.pallas_call(
-        functools.partial(select_kernel, (0, 1, 2)),
+        select_kernel,
         out_shape=jax.ShapeDtypeStruct((PLANE * 3 * per_chip, half_cols), jnp.bfloat16),
-        in_specs=[SCALAR] + vmem(1) + anywhere(3),
+        in_specs=[SCALAR] + vmem(3),
         out_specs=vmem(1)[0],
-        scratch_shapes=[
-            pltpu.VMEM((3, *piece_room), jnp.bfloat16),
-            pltpu.SemaphoreType.DMA((3,)),
-        ],
         compiler_params=PARAMS,
         cost_estimate=COST,
         name="select",
-    )(me_scalar, codes, *near_deltas)
+    )(me_scalar, *near_deltas)
     got_near = to_plane(selected.reshape(PLANE, 3 * per_chip, half_cols))
 
     shard = width_model // size
     terms = pl.pallas_call(
         weight_grad_kernel,
         out_shape=jax.ShapeDtypeStruct((PLANE, shard + per_chip, half_cols), jnp.bfloat16),
-        in_specs=[SCALAR] + vmem(1) + anywhere(2 + levels),
+        in_specs=[SCALAR] + vmem(2 + levels),
         out_specs=vmem(1)[0],
-        scratch_shapes=[
-            pltpu.VMEM((levels, 2, rows, wide), jnp.bfloat16),
-            pltpu.VMEM((levels, *piece_room), jnp.bfloat16),
-            pltpu.VMEM((wide, half_cols), jnp.float32),
-            pltpu.SemaphoreType.DMA((3 * levels,)),
-        ],
+        scratch_shapes=[pltpu.VMEM((wide, half_cols), jnp.float32)],
         compiler_params=PARAMS,
         cost_estimate=COST,
         name="weight_grad",
-    )(me_scalar, codes, own_features, mate_features, *near_deltas, delta_both)
+    )(me_scalar, own_features, mate_features, *near_deltas, delta_both)
     got = to_plane(terms)
 
     depth = width_model // chips

time: 161 us -> 161 us (level)
  starting transfers between devices: 42.9 us -> 36.3 us
  local copies, waits for them, and re-layouts: 15.4 us -> 19.7 us
  waiting for transfers between devices: 69.3 us -> 72.2 us
    ppermute x27 -> x28, starting transfers between devices: 30 us -> 24.6 us  [swap(): return lax.ppermute(value, 'dp', [(i, i ^ mask) for i in range(size)])]
    ppermute x27 -> x28, waiting for transfers between devices: 62.5 us -> 65.3 us  [swap(): return lax.ppermute(value, 'dp', [(i, i ^ mask) for i in range(size)])]
    slice x0 -> x8, local copies, waits for them, and re-layouts: none -> 2.75 us  [per_device_paired(): pieces += [own, by_x, by_y, swap(by_y[:half], X), swap(by_x[half:], Y)]]
    unnamed x50 -> x80, local copies, waits for them, and re-layouts: 13.5 us -> 15.8 us
    pallas_call x3, Pallas kernels: 8.14 us -> 6.42 us  [the longest x1 3.21 us: per_device_paired(): pl.pallas_call(functools.partial(delta_kernel, last_places, chips // 2),...]
  transfers between devices with their start and end apart: 30 -> 31, of which waited for: 17 -> 10; matrix products, arithmetic and copies ran while one was open for 3% -> 4% of each run, Pallas kernels for 13% -> 12%
where the time goes in v8:
time: 161 us; the launch traced here: 160 us
  waiting for transfers between devices  72.2 us (45%)
  starting transfers between devices  36.3 us (23%)
  Pallas kernels  28.4 us (18%)
  local copies, waits for them, and re-layouts  19.7 us (12%)
  other arithmetic  2.58 us (2%)
    ppermute x28, waiting for transfers between devices, swap(): return lax.ppermute(value, 'dp', [(i, i ^ mask) for i in range(size)])  65.3 us
    ppermute x28, starting transfers between devices, swap(): return lax.ppermute(value, 'dp', [(i, i ^ mask) for i in range(size)])  24.6 us
    unnamed x80, local copies, waits for them, and re-layouts  15.8 us
    pallas_call x1, Pallas kernels, per_device_paired(): pl.pallas_call(row_grad_kernel, out_shape=row_shape, grid_spec=pltpu.Pref...  8.95 us
    pallas_call x1, Pallas kernels, per_device_paired(): pl.pallas_call(far_row_grad_kernel, out_shape=row_shape, grid_spec=pltpu....  8.19 us
    all_to_all x2, starting transfers between devices, to_plane(): lax.all_to_all(value, 'dp', split_axis=0, concat_axis=0, axis_index_group...  7.33 us
    all_to_all x2, waiting for transfers between devices, to_plane(): lax.all_to_all(value, 'dp', split_axis=0, concat_axis=0, axis_index_group...  6.84 us
    all_to_all x1, starting transfers between devices, per_device_paired(): lax.all_to_all(jnp.stack([tokens[:, z * wide:(z + 1) * wide] for z in ran...  4.37 us
  transfers between devices with their start and end apart: 31, of which 10 were waited for; matrix products, arithmetic and copies ran while one was open for 4% of the time, Pallas kernels for 12%

profile of v8, /device:TPU:0, one launch (start us, length us, event | category | flops | bytes accessed | tf_op | source)
XLA Modules:
  0.0 160.3 jit_solution(8459140631938332796)
XLA Ops:
  1.2 1.0 fusion.11
  2.6 3.0 %collective-permute-start.1 = (bf16[256,512]{1,0:T(8,128)(2,1)S(1)}, bf16[256,512]{1,0:T(8,128)(2,1)}, u32[]{:S(2)}, u32[]{:S(2)}) collective-permute-start(bf16[256,512]{1,0:T(8,128)(2,1)S(1)} %maximum_select_fusion.refs_0_), channel_id=1, source_target_pairs={{0,8},{1,9},{2,10},{3,11},{4,12},{5,13},{6,14},{7,15},{8,0},{9,1},... | collective-permute-start | bytes 786440 | tf_op jit(solution)/shard_map/ppermute | solution.py:91
  5.6 1.5 collective-permute-start.5
  7.3 1.2 pad_maximum_fusion
  8.5 4.4 %all-to-all-start.1 = ((bf16[4,128,1024]{2,1,0:T(8,128)(2,1)}), bf16[4,128,1024]{2,1,0:T(8,128)(2,1)}, u32[]{:S(2)}, u32[]{:S(2)}) async-start(bf16[4,128,1024]{2,1,0:T(8,128)(2,1)} %pad_maximum_fusion), calls=%async_computation.1 | async-start | bytes 2097152 | tf_op jit(solution)/shard_map/all_to_all | solution.py:329
  12.9 1.6 collective-permute-start.4
  14.4 2.8 %collective-permute-start.12 = (bf16[256,512]{1,0:T(8,128)(2,1)S(1)}, bf16[256,512]{1,0:T(8,128)(2,1)}, u32[]{:S(2)}, u32[]{:S(2)}) collective-permute-start(bf16[256,512]{1,0:T(8,128)(2,1)S(1)} %maximum_select_fusion.refs_0_), channel_id=1, source_target_pairs={{0,16},{1,17},{2,18},{3,19},{4,20},{5,21},{6,22},{7,23},{8,24},{9,... | collective-permute-start | bytes 786440 | tf_op jit(solution)/shard_map/ppermute | solution.py:91
  18.9 31.0 %collective-permute-done.12.refs_0_ = bf16[256,512]{1,0:T(8,128)(2,1)} collective-permute-done((bf16[256,512]{1,0:T(8,128)(2,1)S(1)}, bf16[256,512]{1,0:T(8,128)(2,1)}, u32[]{:S(2)}, u32[]{:S(2)}) %collective-permute-start.12) | collective-permute-done | bytes 262176 | tf_op jit(solution)/shard_map/ppermute | solution.py:91
  49.9 1.6 collective-permute-start.8
  53.3 4.1 %collective-permute-done.17.refs_5_ = bf16[256,512]{1,0:T(8,128)(2,1)S(1)} collective-permute-done((bf16[256,512]{1,0:T(8,128)(2,1)}, bf16[256,512]{1,0:T(8,128)(2,1)S(1)}, u32[]{:S(2)}, u32[]{:S(2)}) %collective-permute-start.17) | collective-permute-done | bytes 262176 | tf_op jit(solution)/shard_map/ppermute | solution.py:91
  57.9 1.6 collective-permute-done.8.refs_6_
  59.4 1.5 collective-permute-start.18
  61.6 3.4 %collective-permute-done.13.refs_1_ = bf16[256,512]{1,0:T(8,128)(2,1)S(1)} collective-permute-done((bf16[256,512]{1,0:T(8,128)(2,1)}, bf16[256,512]{1,0:T(8,128)(2,1)S(1)}, u32[]{:S(2)}, u32[]{:S(2)}) %collective-permute-start.13) | collective-permute-done | bytes 262176 | tf_op jit(solution)/shard_map/ppermute | solution.py:91
  65.1 1.5 collective-permute-start.10
  67.1 0.7 pad_maximum_fusion.1
  67.9 2.2 %collective-permute-done.18.refs_6_ = bf16[256,512]{1,0:T(8,128)(2,1)S(1)} collective-permute-done((bf16[256,512]{1,0:T(8,128)(2,1)S(1)}, bf16[256,512]{1,0:T(8,128)(2,1)S(1)}, u32[]{:S(2)}, u32[]{:S(2)}) %collective-permute-start.18) | collective-permute-done | bytes 262176 | tf_op jit(solution)/shard_map/ppermute | solution.py:91
  70.1 0.7 slice.75
  70.8 0.7 slice.76
  73.5 1.5 collective-permute-start.15
  75.0 0.7 copy-done.29
  76.1 0.7 copy-done.31
  77.4 1.0 copy-done.2
  78.4 1.5 collective-permute-start.21
  80.0 1.2 copy-done.3
  81.2 0.9 copy-done.8
  82.2 0.9 copy-done.10
  83.1 0.9 copy-done.16
  84.1 0.9 copy-done.22
  85.0 0.9 copy-done.26
  85.9 0.9 copy-done.28
  86.8 0.9 copy-done.30
  87.7 0.9 copy-done.32
  88.7 2.0 %project.1 = (bf16[2048,512]{1,0:T(8,128)(2,1)S(1)}, f32[2,128,512]{2,1,0:T(8,128)S(1)}) custom-call(s32[16]{0:T(128)S(1)} %stack.87.chips_ref, bf16[128,4096]{1,0:T(8,128)(2,1)S(1)} %copy-done, bf16[128,4096]{1,0:T(8,128)(2,1)S(1)} %copy-done.3, bf16[256,512]{1,0:T(8,128)(2,1)S(1)} %maximum_select_fusion.refs_0_, bf16[256,512]{1,0:T(8,128)(2,1)S(1)} %copy-done.10, ...), custom_call_target="tpu_custom_call" | custom-call | flops 1024 | bytes 1024 | tf_op jit(solution)/shard_map/project/pallas_call | solution.py:356
  91.4 3.2 %delta.1 = (bf16[272,512]{1,0:T(8,128)(2,1)S(1)}, bf16[2048,512]{1,0:T(8,128)(2,1)}) custom-call(s32[16]{0:T(128)S(1)} %copy-done.34, s32[1]{0:T(128)} %bitcast.16.me_ref, bf16[128,4096]{1,0:T(8,128)(2,1)S(1)} %copy-done, bf16[128,4096]{1,0:T(8,128)(2,1)S(1)} %copy-done.3, bf16[144,512]{1,0:T(8,128)(2,1)S(1)} %copy-done.6, ...), custom_call_target="tpu_custom_call" | custom-call | flops 1024 | bytes 1024 | tf_op jit(solution)/shard_map/delta/pallas_call | solution.py:365
  95.2 1.3 collective-permute-start.23
  97.0 14.1 %collective-permute-done.23.refs_2_ = bf16[272,512]{1,0:T(8,128)(2,1)S(1)} collective-permute-done((bf16[272,512]{1,0:T(8,128)(2,1)S(1)}, bf16[272,512]{1,0:T(8,128)(2,1)S(1)}, u32[]{:S(2)}, u32[]{:S(2)}) %collective-permute-start.23) | collective-permute-done | bytes 278560 | tf_op jit(solution)/shard_map/ppermute | solution.py:91
  111.1 1.2 select.28
  112.3 3.5 %all-to-all-start = ((bf16[8,48,512]{2,1,0:T(8,128)(2,1)}), bf16[8,48,512]{2,1,0:T(8,128)(2,1)S(1)}, u32[]{:S(2)}, u32[]{:S(2)}) async-start(bf16[8,48,512]{2,1,0:T(8,128)(2,1)} %bitcast.22), calls=%async_computation | async-start | bytes 786432 | tf_op jit(solution)/shard_map/all_to_all | solution.py:381
  116.3 8.4 %collective-permute-done.27.refs_3_ = bf16[272,512]{1,0:T(8,128)(2,1)S(1)} collective-permute-done((bf16[272,512]{1,0:T(8,128)(2,1)S(1)}, bf16[272,512]{1,0:T(8,128)(2,1)S(1)}, u32[]{:S(2)}, u32[]{:S(2)}) %collective-permute-start.27) | collective-permute-done | bytes 278560 | tf_op jit(solution)/shard_map/ppermute | solution.py:91
  124.8 3.9 %weight_grad.1 = bf16[8,144,512]{2,1,0:T(8,128)(2,1)S(1)} custom-call(s32[1]{0:T(128)} %bitcast.16.me_ref, bf16[4,128,1024]{2,1,0:T(8,128)(2,1)} %all-to-all-done.1.own_ref, bf16[4,128,1024]{2,1,0:T(8,128)(2,1)} %collective-permute-done.26.mate_ref, bf16[272,512]{1,0:T(8,128)(2,1)S(1)} %get-tuple-element.15.refs_0_, ...), custom_call_target="tpu_custom_call" | custom-call | flops 1024 | bytes 1024 | tf_op jit(solution)/shard_map/weight_grad/pallas_call | solution.py:400
  128.7 1.0 copy-done.1
  129.8 0.7 copy-done.4
  130.5 3.9 %all-to-all-start.2 = ((bf16[8,144,512]{2,1,0:T(8,128)(2,1)}), bf16[8,144,512]{2,1,0:T(8,128)(2,1)S(1)}, u32[]{:S(2)}, u32[]{:S(2)}) async-start(bf16[8,144,512]{2,1,0:T(8,128)(2,1)} %copy-done.1), calls=%async_computation.2 | async-start | bytes 2359296 | tf_op jit(solution)/shard_map/all_to_all | solution.py:381
  134.4 1.0 copy-done.5
  135.4 9.0 %row_grad.1.before_ref = bf16[256,4096]{1,0:T(8,128)(2,1)} custom-call(s32[16]{0:T(128)S(1)} %copy-done.35, s32[1]{0:T(128)} %bitcast.16.me_ref, bf16[4,2,48,512]{3,2,1,0:T(8,128)(2,1)S(1)} %bitcast.38, bf16[2048,512]{1,0:T(8,128)(2,1)S(1)} %get-tuple-element.16.refs_0_, bf16[2048,512]{1,0:T(8,128)(2,1)} %collective-permute-done.24.refs_1_, ...), custom_call_target="tpu_custom_call" | custom-call | flops 1024 | bytes 1024 | tf_op jit(solution)/shard_map/row_grad/pallas_call | solution.py:416
  144.4 6.8 %all-to-all-done.2 = bf16[8,144,512]{2,1,0:T(8,128)(2,1)S(1)} async-done(((bf16[8,144,512]{2,1,0:T(8,128)(2,1)}), bf16[8,144,512]{2,1,0:T(8,128)(2,1)S(1)}, u32[]{:S(2)}, u32[]{:S(2)}) %all-to-all-start.2) | async-done | bytes 1179680 | tf_op jit(solution)/shard_map/all_to_all | solution.py:381
  151.2 0.9 sum.1
  152.1 8.2 %far_row_grad.1 = bf16[256,4096]{1,0:T(8,128)(2,1)} custom-call(s32[16]{0:T(128)S(1)} %copy-done.35, s32[1]{0:T(128)} %bitcast.16.me_ref, bf16[256,4096]{1,0:T(8,128)(2,1)} %row_grad.1.before_ref, bf16[4,2,144,512]{3,2,1,0:T(8,128)(2,1)S(1)} %bitcast.37, bf16[2048,512]{1,0:T(8,128)(2,1)S(1)} %get-tuple-element.16.refs_0_, ...), custom_call_target="tpu_custom_call", output_to_operand_aliasing={{}: (2, {})} | custom-call | flops 1024 | bytes 1024 | tf_op jit(solution)/shard_map/far_row_grad/pallas_call | solution.py:431
  (127 shorter events, 11.7 us)
Async XLA Ops:
  0.6 6.5 %copy-start = (bf16[128,4096]{1,0:T(8,128)(2,1)S(1)}, bf16[128,4096]{1,0:T(8,128)(2,1)}, u32[]{:S(2)}) copy-start(bf16[128,4096]{1,0:T(8,128)(2,1)} %own_ref.3) | copy-start | bytes 3145732
  0.6 1.9 %collective-permute-start = (bf16[128,1024]{1,0:T(8,128)(2,1)}, bf16[128,1024]{1,0:T(8,128)(2,1)S(1)}, u32[]{:S(2)}, u32[]{:S(2)}) collective-permute-start(bf16[128,1024]{1,0:T(8,128)(2,1)} %param.11), channel_id=1, source_target_pairs={{0,1},{1,0},{2,3},{3,2},{4,5},{5,4},{6,7},{7,6},{8,9},{9,8},{10,11... | collective-permute-start | bytes 786440 | tf_op jit(solution)/shard_map/ppermute | solution.py:91
  2.6 14.6 %collective-permute-start.1 = (bf16[256,512]{1,0:T(8,128)(2,1)S(1)}, bf16[256,512]{1,0:T(8,128)(2,1)}, u32[]{:S(2)}, u32[]{:S(2)}) collective-permute-start(bf16[256,512]{1,0:T(8,128)(2,1)S(1)} %maximum_select_fusion.refs_0_), channel_id=1, source_target_pairs={{0,8},{1,9},{2,10},{3,11},{4,12},{5,13},{6,14},{7,15},{8,0},{9,1},... | collective-permute-start | bytes 786440 | tf_op jit(solution)/shard_map/ppermute | solution.py:91
  5.6 11.6 %collective-permute-start.5 = (bf16[256,512]{1,0:T(8,128)(2,1)S(1)}, bf16[256,512]{1,0:T(8,128)(2,1)S(1)}, u32[]{:S(2)}, u32[]{:S(2)}) collective-permute-start(bf16[256,512]{1,0:T(8,128)(2,1)S(1)} %maximum_select_fusion.refs_0_), channel_id=1, source_target_pairs={{0,4},{1,5},{2,6},{3,7},{4,0},{5,1},{6,2},{7,3},{8,12},{9,13},{10,... | collective-permute-start | bytes 786440 | tf_op jit(solution)/shard_map/ppermute | solution.py:91
  7.2 10.6 %copy-start.37 = (s32[1,4]{1,0:T(1,128)S(1)}, s32[1,4]{1,0:T(1,128)}, u32[]{:S(2)}) copy-start(s32[1,4]{1,0:T(1,128)} %param.9) | copy-start | bytes 52
  7.3 10.9 %copy-start.38 = (s32[4]{0:T(128)S(1)}, s32[4]{0:T(128)}, u32[]{:S(2)}) copy-start(s32[4]{0:T(128)} %param.10) | copy-start | bytes 52
  7.3 42.6 %copy-start.39 = (s32[128,1]{0,1:T(1,128)S(1)}, s32[128,1]{0,1:T(1,128)}, u32[]{:S(2)}) copy-start(s32[128,1]{0,1:T(1,128)} %param.8) | copy-start | bytes 1540
  8.5 9.8 %copy-start.36 = (bf16[128,1024]{1,0:T(8,128)(2,1)S(1)}, bf16[128,1024]{1,0:T(8,128)(2,1)}, u32[]{:S(2)}) copy-start(bf16[128,1024]{1,0:T(8,128)(2,1)} %param.7) | copy-start | bytes 786436
  8.5 86.7 %all-to-all-start.1 = ((bf16[4,128,1024]{2,1,0:T(8,128)(2,1)}), bf16[4,128,1024]{2,1,0:T(8,128)(2,1)}, u32[]{:S(2)}, u32[]{:S(2)}) async-start(bf16[4,128,1024]{2,1,0:T(8,128)(2,1)} %pad_maximum_fusion), calls=%async_computation.1 | async-start | bytes 2097152 | tf_op jit(solution)/shard_map/all_to_all | solution.py:329
  12.9 37.0 %collective-permute-start.4 = (bf16[256,512]{1,0:T(8,128)(2,1)S(1)}, bf16[256,512]{1,0:T(8,128)(2,1)S(1)}, u32[]{:S(2)}, u32[]{:S(2)}) collective-permute-start(bf16[256,512]{1,0:T(8,128)(2,1)S(1)} %maximum_select_fusion.refs_0_), channel_id=1, source_target_pairs={{0,2},{1,3},{2,0},{3,1},{4,6},{5,7},{6,4},{7,5},{8,10},{9,11},{10,... | collective-permute-start | bytes 786440 | tf_op jit(solution)/shard_map/ppermute | solution.py:91
  14.4 35.5 %collective-permute-start.12 = (bf16[256,512]{1,0:T(8,128)(2,1)S(1)}, bf16[256,512]{1,0:T(8,128)(2,1)}, u32[]{:S(2)}, u32[]{:S(2)}) collective-permute-start(bf16[256,512]{1,0:T(8,128)(2,1)S(1)} %maximum_select_fusion.refs_0_), channel_id=1, source_target_pairs={{0,16},{1,17},{2,18},{3,19},{4,20},{5,21},{6,22},{7,23},{8,24},{9,... | collective-permute-start | bytes 786440 | tf_op jit(solution)/shard_map/ppermute | solution.py:91
  17.2 60.2 %collective-permute-start.2 = (bf16[128,4096]{1,0:T(8,128)(2,1)S(1)}, bf16[128,4096]{1,0:T(8,128)(2,1)S(1)}, u32[]{:S(2)}, u32[]{:S(2)}) collective-permute-start(bf16[128,4096]{1,0:T(8,128)(2,1)S(1)} %copy-done), channel_id=1, source_target_pairs={{0,1},{1,0},{2,3},{3,2},{4,5},{5,4},{6,7},{7,6},{8,9},{9,8},{10,11... | collective-permute-start | bytes 3145736 | tf_op jit(solution)/shard_map/ppermute | solution.py:91
  17.2 62.7 %copy-start.7 = (bf16[256,512]{1,0:T(8,128)(2,1)}, bf16[256,512]{1,0:T(8,128)(2,1)S(1)}, u32[]{:S(2)}) copy-start(bf16[256,512]{1,0:T(8,128)(2,1)S(1)} %collective-permute-done.5.refs_2_) | copy-start | bytes 786436
  17.3 34.3 %collective-permute-start.6 = (bf16[128,512]{1,0:T(8,128)(2,1)S(1)}, bf16[128,512]{1,0:T(8,128)(2,1)S(1)}, u32[]{:S(2)}, u32[]{:S(2)}) collective-permute-start(bf16[128,512]{1,0:T(8,128)(2,1)S(1)} %slice.71), channel_id=1, source_target_pairs={{0,2},{1,3},{2,0},{3,1},{4,6},{5,7},{6,4},{7,5},{8,10},{9,11},{10,... | collective-permute-start | bytes 393224 | tf_op jit(solution)/shard_map/ppermute | solution.py:91
  18.3 34.4 %collective-permute-start.9 = (bf16[256,512]{1,0:T(8,128)(2,1)}, bf16[256,512]{1,0:T(8,128)(2,1)S(1)}, u32[]{:S(2)}, u32[]{:S(2)}) collective-permute-start(bf16[256,512]{1,0:T(8,128)(2,1)} %collective-permute-done.1.refs_5_), channel_id=1, source_target_pairs={{0,4},{1,5},{2,6},{3,7},{4,0},{5,1},{6,2},{7,3},{8,12},{9,13},{10,... | collective-permute-start | bytes 786440 | tf_op jit(solution)/shard_map/ppermute | solution.py:91
  49.9 7.5 %collective-permute-start.17 = (bf16[256,512]{1,0:T(8,128)(2,1)}, bf16[256,512]{1,0:T(8,128)(2,1)S(1)}, u32[]{:S(2)}, u32[]{:S(2)}) collective-permute-start(bf16[256,512]{1,0:T(8,128)(2,1)} %collective-permute-done.12.refs_0_), channel_id=1, source_target_pairs={{0,8},{1,9},{2,10},{3,11},{4,12},{5,13},{6,14},{7,15},{8,0},{9,1},... | collective-permute-start | bytes 786440 | tf_op jit(solution)/shard_map/ppermute | solution.py:91
  49.9 30.0 %copy-start.9 = (bf16[256,512]{1,0:T(8,128)(2,1)}, bf16[256,512]{1,0:T(8,128)(2,1)S(1)}, u32[]{:S(2)}) copy-start(bf16[256,512]{1,0:T(8,128)(2,1)S(1)} %collective-permute-done.4.refs_1_) | copy-start | bytes 786436
  49.9 9.5 %collective-permute-start.8 = (bf16[256,512]{1,0:T(8,128)(2,1)}, bf16[256,512]{1,0:T(8,128)(2,1)S(1)}, u32[]{:S(2)}, u32[]{:S(2)}) collective-permute-start(bf16[256,512]{1,0:T(8,128)(2,1)} %collective-permute-done.1.refs_5_), channel_id=1, source_target_pairs={{0,2},{1,3},{2,0},{3,1},{4,6},{5,7},{6,4},{7,5},{8,10},{9,11},{10,... | collective-permute-start | bytes 786440 | tf_op jit(solution)/shard_map/ppermute | solution.py:91
  52.2 8.8 %collective-permute-start.14 = (bf16[256,512]{1,0:T(8,128)(2,1)}, bf16[256,512]{1,0:T(8,128)(2,1)S(1)}, u32[]{:S(2)}, u32[]{:S(2)}) collective-permute-start(bf16[256,512]{1,0:T(8,128)(2,1)} %collective-permute-done.12.refs_0_), channel_id=1, source_target_pairs={{0,4},{1,5},{2,6},{3,7},{4,0},{5,1},{6,2},{7,3},{8,12},{9,13},{10,... | collective-permute-start | bytes 786440 | tf_op jit(solution)/shard_map/ppermute | solution.py:91
  52.7 12.3 %copy-start.15 = (bf16[256,512]{1,0:T(8,128)(2,1)}, bf16[256,512]{1,0:T(8,128)(2,1)S(1)}, u32[]{:S(2)}) copy-start(bf16[256,512]{1,0:T(8,128)(2,1)S(1)} %collective-permute-done.9.refs_7_) | copy-start | bytes 786436
  52.7 12.3 %collective-permute-start.13 = (bf16[256,512]{1,0:T(8,128)(2,1)}, bf16[256,512]{1,0:T(8,128)(2,1)S(1)}, u32[]{:S(2)}, u32[]{:S(2)}) collective-permute-start(bf16[256,512]{1,0:T(8,128)(2,1)} %collective-permute-done.12.refs_0_), channel_id=1, source_target_pairs={{0,2},{1,3},{2,0},{3,1},{4,6},{5,7},{6,4},{7,5},{8,10},{9,11},{10,... | collective-permute-start | bytes 786440 | tf_op jit(solution)/shard_map/ppermute | solution.py:91
  57.4 20.0 %copy-start.23 = (bf16[256,512]{1,0:T(8,128)(2,1)}, bf16[256,512]{1,0:T(8,128)(2,1)S(1)}, u32[]{:S(2)}) copy-start(bf16[256,512]{1,0:T(8,128)(2,1)S(1)} %collective-permute-done.17.refs_5_) | copy-start | bytes 786436
  57.4 9.2 %collective-permute-start.19 = (bf16[256,512]{1,0:T(8,128)(2,1)S(1)}, bf16[256,512]{1,0:T(8,128)(2,1)S(1)}, u32[]{:S(2)}, u32[]{:S(2)}) collective-permute-start(bf16[256,512]{1,0:T(8,128)(2,1)S(1)} %collective-permute-done.17.refs_5_), channel_id=1, source_target_pairs={{0,4},{1,5},{2,6},{3,7},{4,0},{5,1},{6,2},{7,3},{8,12},{9,13},{10,... | collective-permute-start | bytes 786440 | tf_op jit(solution)/shard_map/ppermute | solution.py:91
  59.4 7.2 %copy-start.21 = (bf16[256,512]{1,0:T(8,128)(2,1)}, bf16[256,512]{1,0:T(8,128)(2,1)S(1)}, u32[]{:S(2)}) copy-start(bf16[256,512]{1,0:T(8,128)(2,1)S(1)} %collective-permute-done.8.refs_6_) | copy-start | bytes 786436
  59.4 10.7 %collective-permute-start.18 = (bf16[256,512]{1,0:T(8,128)(2,1)S(1)}, bf16[256,512]{1,0:T(8,128)(2,1)S(1)}, u32[]{:S(2)}, u32[]{:S(2)}) collective-permute-start(bf16[256,512]{1,0:T(8,128)(2,1)S(1)} %collective-permute-done.17.refs_5_), channel_id=1, source_target_pairs={{0,2},{1,3},{2,0},{3,1},{4,6},{5,7},{6,4},{7,5},{8,10},{9,11},{10,... | collective-permute-start | bytes 786440 | tf_op jit(solution)/shard_map/ppermute | solution.py:91
  61.0 18.8 %copy-start.11 = (bf16[256,512]{1,0:T(8,128)(2,1)}, bf16[256,512]{1,0:T(8,128)(2,1)S(1)}, u32[]{:S(2)}) copy-start(bf16[256,512]{1,0:T(8,128)(2,1)S(1)} %collective-permute-done.14.refs_2_) | copy-start | bytes 786436
  61.1 11.8 %collective-permute-start.7 = (bf16[128,512]{1,0:T(8,128)(2,1)S(1)}, bf16[128,512]{1,0:T(8,128)(2,1)S(1)}, u32[]{:S(2)}, u32[]{:S(2)}) collective-permute-start(bf16[128,512]{1,0:T(8,128)(2,1)S(1)} %slice.72), channel_id=1, source_target_pairs={{0,4},{1,5},{2,6},{3,7},{4,0},{5,1},{6,2},{7,3},{8,12},{9,13},{10,... | collective-permute-start | bytes 393224 | tf_op jit(solution)/shard_map/ppermute | solution.py:91
  65.1 14.8 %copy-start.13 = (bf16[256,512]{1,0:T(8,128)(2,1)}, bf16[256,512]{1,0:T(8,128)(2,1)S(1)}, u32[]{:S(2)}) copy-start(bf16[256,512]{1,0:T(8,128)(2,1)S(1)} %collective-permute-done.13.refs_1_) | copy-start | bytes 786436
  65.1 9.9 %collective-permute-start.10 = (bf16[128,512]{1,0:T(8,128)(2,1)S(1)}, bf16[128,512]{1,0:T(8,128)(2,1)S(1)}, u32[]{:S(2)}, u32[]{:S(2)}) collective-permute-start(bf16[128,512]{1,0:T(8,128)(2,1)S(1)} %slice.73), channel_id=1, source_target_pairs={{0,2},{1,3},{2,0},{3,1},{4,6},{5,7},{6,4},{7,5},{8,10},{9,11},{10,... | collective-permute-start | bytes 393224 | tf_op jit(solution)/shard_map/ppermute | solution.py:91
  66.6 10.8 %copy-start.17 = (bf16[256,512]{1,0:T(8,128)(2,1)}, bf16[256,512]{1,0:T(8,128)(2,1)S(1)}, u32[]{:S(2)}) copy-start(bf16[256,512]{1,0:T(8,128)(2,1)S(1)} %collective-permute-done.19.refs_7_) | copy-start | bytes 786436
  66.6 9.5 %collective-permute-start.11 = (bf16[128,512]{1,0:T(8,128)(2,1)S(1)}, bf16[128,512]{1,0:T(8,128)(2,1)S(1)}, u32[]{:S(2)}, u32[]{:S(2)}) collective-permute-start(bf16[128,512]{1,0:T(8,128)(2,1)S(1)} %slice.74), channel_id=1, source_target_pairs={{0,4},{1,5},{2,6},{3,7},{4,0},{5,1},{6,2},{7,3},{8,12},{9,13},{10,... | collective-permute-start | bytes 393224 | tf_op jit(solution)/shard_map/ppermute | solution.py:91
  70.1 7.3 %copy-start.19 = (bf16[256,512]{1,0:T(8,128)(2,1)}, bf16[256,512]{1,0:T(8,128)(2,1)S(1)}, u32[]{:S(2)}) copy-start(bf16[256,512]{1,0:T(8,128)(2,1)S(1)} %collective-permute-done.18.refs_6_) | copy-start | bytes 786436
  70.1 20.6 %collective-permute-start.3 = (bf16[144,512]{1,0:T(8,128)(2,1)}, bf16[144,512]{1,0:T(8,128)(2,1)}, u32[]{:S(2)}, u32[]{:S(2)}) collective-permute-start(bf16[144,512]{1,0:T(8,128)(2,1)} %get-tuple-element.28), channel_id=1, source_target_pairs={{0,1},{1,0},{2,3},{3,2},{4,5},{5,4},{6,7},{7,6},{8,9},{9,8},{10,11... | collective-permute-start | bytes 442376 | tf_op jit(solution)/shard_map/ppermute | solution.py:91
  73.5 17.2 %collective-permute-start.15 = (bf16[128,512]{1,0:T(8,128)(2,1)}, bf16[128,512]{1,0:T(8,128)(2,1)}, u32[]{:S(2)}, u32[]{:S(2)}) collective-permute-start(bf16[128,512]{1,0:T(8,128)(2,1)} %slice.75), channel_id=1, source_target_pairs={{0,2},{1,3},{2,0},{3,1},{4,6},{5,7},{6,4},{7,5},{8,10},{9,11},{10,... | collective-permute-start | bytes 393224 | tf_op jit(solution)/shard_map/ppermute | solution.py:91
  75.6 15.1 %collective-permute-start.16 = (bf16[128,512]{1,0:T(8,128)(2,1)}, bf16[128,512]{1,0:T(8,128)(2,1)}, u32[]{:S(2)}, u32[]{:S(2)}) collective-permute-start(bf16[128,512]{1,0:T(8,128)(2,1)} %slice.76), channel_id=1, source_target_pairs={{0,4},{1,5},{2,6},{3,7},{4,0},{5,1},{6,2},{7,3},{8,12},{9,13},{10,... | collective-permute-start | bytes 393224 | tf_op jit(solution)/shard_map/ppermute | solution.py:91
  76.8 13.9 %collective-permute-start.20 = (bf16[128,512]{1,0:T(8,128)(2,1)}, bf16[128,512]{1,0:T(8,128)(2,1)}, u32[]{:S(2)}, u32[]{:S(2)}) collective-permute-start(bf16[128,512]{1,0:T(8,128)(2,1)} %slice.77), channel_id=1, source_target_pairs={{0,2},{1,3},{2,0},{3,1},{4,6},{5,7},{6,4},{7,5},{8,10},{9,11},{10,... | collective-permute-start | bytes 393224 | tf_op jit(solution)/shard_map/ppermute | solution.py:91
  78.4 12.4 %collective-permute-start.21 = (bf16[128,512]{1,0:T(8,128)(2,1)}, bf16[128,512]{1,0:T(8,128)(2,1)S(1)}, u32[]{:S(2)}, u32[]{:S(2)}) collective-permute-start(bf16[128,512]{1,0:T(8,128)(2,1)} %slice.78), channel_id=1, source_target_pairs={{0,4},{1,5},{2,6},{3,7},{4,0},{5,1},{6,2},{7,3},{8,12},{9,13},{10,... | collective-permute-start | bytes 393224 | tf_op jit(solution)/shard_map/ppermute | solution.py:91
  88.6 2.1 %copy-start.18 = (bf16[256,512]{1,0:T(8,128)(2,1)S(1)}, bf16[256,512]{1,0:T(8,128)(2,1)}, u32[]{:S(2)}) copy-start(bf16[256,512]{1,0:T(8,128)(2,1)} %copy-done.17) | copy-start | bytes 786436
  88.7 2.1 %copy-start.20 = (bf16[256,512]{1,0:T(8,128)(2,1)S(1)}, bf16[256,512]{1,0:T(8,128)(2,1)}, u32[]{:S(2)}) copy-start(bf16[256,512]{1,0:T(8,128)(2,1)} %copy-done.19) | copy-start | bytes 786436
  94.7 39.7 %collective-permute-start.25 = (bf16[2048,512]{1,0:T(8,128)(2,1)}, bf16[2048,512]{1,0:T(8,128)(2,1)}, u32[]{:S(2)}, u32[]{:S(2)}) collective-permute-start(bf16[2048,512]{1,0:T(8,128)(2,1)} %get-tuple-element.17.refs_2_), channel_id=1, source_target_pairs={{0,1},{1,0},{2,3},{3,2},{4,5},{5,4},{6,7},{7,6},{8,9},{9,8},{10,11... | collective-permute-start | bytes 6291464 | tf_op jit(solution)/shard_map/ppermute | solution.py:91
  94.7 39.7 %collective-permute-start.24 = (bf16[2048,512]{1,0:T(8,128)(2,1)S(1)}, bf16[2048,512]{1,0:T(8,128)(2,1)}, u32[]{:S(2)}, u32[]{:S(2)}) collective-permute-start(bf16[2048,512]{1,0:T(8,128)(2,1)S(1)} %get-tuple-element.16.refs_0_), channel_id=1, source_target_pairs={{0,1},{1,0},{2,3},{3,2},{4,5},{5,4},{6,7},{7,6},{8,9},{9,8},{10,11... | collective-permute-start | bytes 6291464 | tf_op jit(solution)/shard_map/ppermute | solution.py:91
  95.2 29.6 %collective-permute-start.26 = (bf16[4,128,1024]{2,1,0:T(8,128)(2,1)}, bf16[4,128,1024]{2,1,0:T(8,128)(2,1)}, u32[]{:S(2)}, u32[]{:S(2)}) collective-permute-start(bf16[4,128,1024]{2,1,0:T(8,128)(2,1)} %all-to-all-done.1.own_ref), channel_id=1, source_target_pairs={{0,1},{1,0},{2,3},{3,2},{4,5},{5,4},{6,7},{7,6},{8,9},{9,8},{10,11... | collective-permute-start | bytes 3145736 | tf_op jit(solution)/shard_map/ppermute | solution.py:91
  95.2 15.9 %collective-permute-start.23 = (bf16[272,512]{1,0:T(8,128)(2,1)S(1)}, bf16[272,512]{1,0:T(8,128)(2,1)S(1)}, u32[]{:S(2)}, u32[]{:S(2)}) collective-permute-start(bf16[272,512]{1,0:T(8,128)(2,1)S(1)} %get-tuple-element.15.refs_0_), channel_id=1, source_target_pairs={{0,16},{1,17},{2,18},{3,19},{4,20},{5,21},{6,22},{7,23},{8,24},{9,... | collective-permute-start | bytes 835592 | tf_op jit(solution)/shard_map/ppermute | solution.py:91
  96.5 14.6 %collective-permute-start.22 = (bf16[272,512]{1,0:T(8,128)(2,1)S(1)}, bf16[272,512]{1,0:T(8,128)(2,1)S(1)}, u32[]{:S(2)}, u32[]{:S(2)}) collective-permute-start(bf16[272,512]{1,0:T(8,128)(2,1)S(1)} %get-tuple-element.15.refs_0_), channel_id=1, source_target_pairs={{0,8},{1,9},{2,10},{3,11},{4,12},{5,13},{6,14},{7,15},{8,0},{9,1},... | collective-permute-start | bytes 835592 | tf_op jit(solution)/shard_map/ppermute | solution.py:91
  112.3 17.4 %all-to-all-start = ((bf16[8,48,512]{2,1,0:T(8,128)(2,1)}), bf16[8,48,512]{2,1,0:T(8,128)(2,1)S(1)}, u32[]{:S(2)}, u32[]{:S(2)}) async-start(bf16[8,48,512]{2,1,0:T(8,128)(2,1)} %bitcast.22), calls=%async_computation | async-start | bytes 786432 | tf_op jit(solution)/shard_map/all_to_all | solution.py:381
  115.8 9.0 %collective-permute-start.27 = (bf16[272,512]{1,0:T(8,128)(2,1)S(1)}, bf16[272,512]{1,0:T(8,128)(2,1)S(1)}, u32[]{:S(2)}, u32[]{:S(2)}) collective-permute-start(bf16[272,512]{1,0:T(8,128)(2,1)S(1)} %collective-permute-done.23.refs_2_), channel_id=1, source_target_pairs={{0,8},{1,9},{2,10},{3,11},{4,12},{5,13},{6,14},{7,15},{8,0},{9,1},... | collective-permute-start | bytes 835592 | tf_op jit(solution)/shard_map/ppermute | solution.py:91
  129.8 4.6 %copy-start.35 = (s32[16]{0:T(128)S(1)}, s32[16]{0:T(128)}, u32[]{:S(2)}) copy-start(s32[16]{0:T(128)} %copy-done.33) | copy-start | bytes 196
  130.5 20.7 %all-to-all-start.2 = ((bf16[8,144,512]{2,1,0:T(8,128)(2,1)}), bf16[8,144,512]{2,1,0:T(8,128)(2,1)S(1)}, u32[]{:S(2)}, u32[]{:S(2)}) async-start(bf16[8,144,512]{2,1,0:T(8,128)(2,1)} %copy-done.1), calls=%async_computation.2 | async-start | bytes 2359296 | tf_op jit(solution)/shard_map/all_to_all | solution.py:381
  (23 other events, 26.2 us)

commit v9 on v8

--- a/solution.py
+++ b/solution.py
@@ -10,7 +10,7 @@
 
 HEAD_DIM = 128
 NSUB = 4
-VMEM_LIMIT = 20 * 1024 * 1024
+VMEM_LIMIT = 48 * 1024 * 1024
 CODE_ROWS = 16
 epsilon = 1e-06
 
@@ -99,56 +99,74 @@
     return lax.dot_general(a, b, (dims, ((), ())), preferred_element_type=jnp.float32)
 
 
-def add_products(places, chips_ref, begin, token_refs, pieces, weight_ref, acc, fresh):
+def fetch(pairs, sems):
+    copies = [
+        pltpu.make_async_copy(source, target, sems.at[n])
+        for n, (source, target) in enumerate(pairs)
+    ]
+    for copy in copies:
+        copy.start()
+    return copies
+
+
+def project_kernel(places, begin, last, chips_ref, me_ref, own_ref, mate_ref, *refs):
+    count = len(places)
+    refs = list(refs)
+    cots = [refs.pop(0) for _ in range(2)] if last else []
+    begun = refs.pop(0) if begin else None
+    pieces, refs = refs[:count], refs[count:]
+    weight_ref, out_ref, held, weights, sems = refs[:5]
+    acc = refs[5] if last else out_ref
+    rows = own_ref.shape[0]
     chip_rows = max(piece.shape[0] for piece in pieces)
-    for (chip, first), piece_ref in zip(places, pieces):
-        piece = piece_ref[...]
+
+    def at_place(ref, n):
+        chip, first = places[n]
+        first += chip * chip_rows
+        return ref.at[first : first + pieces[n].shape[0], :]
+
+    pairs = [(own_ref, held.at[0]), (mate_ref, held.at[1])]
+    pairs += [(piece, at_place(weights, n)) for n, piece in enumerate(pieces)]
+    copies = fetch(pairs, sems)
+    if begin:
+        acc[...] = begun[...]
+    for copy in copies[:2]:
+        copy.wait()
+    kept = []
+    for n, (chip, first) in enumerate(places):
+        copies[2 + n].wait()
+        out = pltpu.make_async_copy(
+            at_place(weights, n), at_place(weight_ref, n), sems.at[2 + count + n]
+        )
+        out.start()
+        kept.append(out)
+        piece = at_place(weights, n)[...]
         depth = piece.shape[0]
-        weight_ref[chip * chip_rows + first : chip * chip_rows + first + depth, :] = piece
         at = pl.multiple_of(chips_ref[begin + chip] * chip_rows + first, 128)
-        for side, ref in enumerate(token_refs):
-            part = dot(ref[:, pl.ds(at, depth)], piece, ((1,), (0,)))
-            if fresh:
+        for side in range(2):
+            part = dot(held[side, :, pl.ds(at, depth)], piece, ((1,), (0,)))
+            if begin + n == 0:
                 acc[side] = part
             else:
                 acc[side] += part
-        fresh = False
-
-
-def project_kernel(places, chips_ref, own_ref, mate_ref, *refs):
-    *pieces, weight_ref, acc_ref = refs
-    add_products(places, chips_ref, 0, (own_ref, mate_ref), pieces, weight_ref, acc_ref, True)
-
-
-def delta_kernel(
-    places,
-    begin,
-    chips_ref,
-    me_ref,
-    own_ref,
-    mate_ref,
-    own_cot_ref,
-    mate_cot_ref,
-    begun_ref,
-    *refs,
-):
-    *pieces, delta_ref, weight_ref, acc = refs
-    core = me_ref[0] & 1
-    rows = own_ref.shape[0]
-    acc[...] = begun_ref[...]
-    add_products(places, chips_ref, begin, (own_ref, mate_ref), pieces, weight_ref, acc, False)
-    delta_ref[2 * rows :, :] = jnp.zeros_like(delta_ref[2 * rows :, :])
-    for side, cot_ref in enumerate((own_cot_ref, mate_cot_ref)):
-        at = pl.multiple_of((core ^ side) * rows, rows)
-        for head in range(own_cot_ref.shape[1] // HEAD_DIM):
-            cols = slice(head * HEAD_DIM, (head + 1) * HEAD_DIM)
-            proj = acc[side, :, cols]
-            scale = jnp.sqrt(jnp.mean(proj * proj, axis=1, keepdims=True) + epsilon)
-            normed = proj / scale
-            upstream = cot_ref[:rows, cols].astype(jnp.float32)
-            delta = (upstream - normed * jnp.mean(upstream * normed, axis=1, keepdims=True)) / scale
-            delta_ref[pl.ds(at, rows), cols] = delta.astype(jnp.bfloat16)
-        delta_ref[2 * rows :, pl.ds(at, rows)] = cot_ref[rows:, :rows]
+    if last:
+        core = me_ref[0] & 1
+        delta_ref = out_ref
+        delta_ref[2 * rows :, :] = jnp.zeros_like(delta_ref[2 * rows :, :])
+        for side, cot_ref in enumerate(cots):
+            at = pl.multiple_of((core ^ side) * rows, rows)
+            for head in range(cot_ref.shape[1] // HEAD_DIM):
+                cols = slice(head * HEAD_DIM, (head + 1) * HEAD_DIM)
+                proj = acc[side, :, cols]
+                scale = jnp.sqrt(jnp.mean(proj * proj, axis=1, keepdims=True) + epsilon)
+                normed = proj / scale
+                upstream = cot_ref[:rows, cols].astype(jnp.float32)
+                inner = jnp.mean(upstream * normed, axis=1, keepdims=True)
+                delta = (upstream - normed * inner) / scale
+                delta_ref[pl.ds(at, rows), cols] = delta.astype(jnp.bfloat16)
+            delta_ref[2 * rows :, pl.ds(at, rows)] = cot_ref[rows:, :rows]
+    for copy in kept:
+        copy.wait()
 
 
 def selected_rows(plane, deltas, slot_count):
@@ -167,21 +185,34 @@
 
 
 def select_kernel(me_ref, *refs):
-    *deltas, sent_ref = refs
+    *deltas, sent_ref, held, sems = refs
+    for copy in fetch([(ref, held.at[n]) for n, ref in enumerate(deltas)], sems):
+        copy.wait()
     plane = lax.shift_right_logical(me_ref[0], 3)
-    values = [ref[...] for ref in deltas]
+    values = [held[n] for n in range(len(deltas))]
     sent_ref[...] = selected_rows(plane, values, sent_ref.shape[0])
 
 
 def weight_grad_kernel(me_ref, own_ref, mate_ref, *refs):
-    *deltas, part_ref, acc = refs
+    *deltas, part_ref, hidden, held, acc, made, sems = refs
     plane = lax.shift_right_logical(me_ref[0], 3)
     core = me_ref[0] & 1
     rows = own_ref.shape[1]
-    for n, delta_ref in enumerate(deltas):
-        for side, ref in enumerate((own_ref, mate_ref)):
+    count = len(deltas)
+    pairs = []
+    for n, ref in enumerate(deltas):
+        pairs += [
+            (own_ref.at[plane ^ n], hidden.at[n, 0]),
+            (mate_ref.at[plane ^ n], hidden.at[n, 1]),
+            (ref, held.at[n]),
+        ]
+    copies = fetch(pairs, sems)
+    for n in range(count):
+        for copy in copies[3 * n : 3 * n + 3]:
+            copy.wait()
+        for side in range(2):
             at = pl.multiple_of((core ^ side) * rows, rows)
-            part = dot(ref[plane ^ n], delta_ref[pl.ds(at, rows), :], ((0,), (0,)))
+            part = dot(hidden[n, side], held[n, pl.ds(at, rows), :], ((0,), (0,)))
             if n + side == 0:
                 acc[...] = part
             else:
@@ -189,12 +220,16 @@
     blocks, depth, _ = part_ref.shape
     shard = acc.shape[0] // blocks
     extra = depth - shard
-    far = selected_rows(plane, [deltas[-1][...]], blocks * extra)
+    far = selected_rows(plane, [held[count - 1]], blocks * extra)
+    sent = []
     for block in range(blocks):
-        part_ref[block, :shard, :] = acc[block * shard : (block + 1) * shard, :].astype(
-            jnp.bfloat16
-        )
-        part_ref[block, shard:, :] = far[block * extra : (block + 1) * extra, :]
+        made[block, :shard, :] = acc[block * shard : (block + 1) * shard, :].astype(jnp.bfloat16)
+        made[block, shard:, :] = far[block * extra : (block + 1) * extra, :]
+        copy = pltpu.make_async_copy(made.at[block], part_ref.at[block], sems.at[3 * count + block])
+        copy.start()
+        sent.append(copy)
+    for copy in sent:
+        copy.wait()
 
 
 def sum_kernel(norm, parts_ref, grad_ref):
@@ -210,50 +245,60 @@
 def add_columns(core, step, chips_ref, rows_ref, weights, out_ref):
     own, mate = rows_ref[core], rows_ref[1 - core]
     depth = weights[0].shape[0]
-    for n in range(2):
-        total = dot(own, weights[2 * n][...], ((1,), (1,)))
-        total += dot(mate, weights[2 * n + 1][...], ((1,), (1,)))
+    for n in range(len(weights) // 2):
+        total = dot(weights[2 * n][...], own, ((1,), (0,)))
+        total += dot(weights[2 * n + 1][...], mate, ((1,), (0,)))
         at = chips_ref[n * pl.num_programs(0) + step] * depth
-        out_ref[:, pl.ds(pl.multiple_of(at, depth), depth)] = total.astype(jnp.bfloat16)
+        out_ref[:, pl.ds(pl.multiple_of(at, depth), depth)] = total.T.astype(jnp.bfloat16)
 
 
 def row_grad_kernel(chips_ref, me_ref, got_ref, *refs):
-    *weights, out_ref, rows_ref = refs
+    *weights, out_ref, rows_ref, held = refs
     step = pl.program_id(0)
-    chips, _, count, _ = got_ref.shape
-    block = rows_ref.shape[1] // (chips * 4)
+    chips, _, count, half = got_ref.shape
+    block = held.shape[0] // (chips * 4)
     level = lax.shift_right_logical(me_ref[0], 3)
 
     @pl.when(step == 0)
     def _():
-        for n in range(4):
-            for chip in range(chips):
-                at = pl.multiple_of(((level ^ n) * chips + chip) * block, block)
-                for side in range(2):
+        for side in range(2):
+            for n in range(4):
+                for chip in range(chips):
+                    at = pl.multiple_of(((level ^ n) * chips + chip) * block, block)
                     if n < count // block:
                         rows = got_ref[chip, side, n * block : (n + 1) * block, :]
                     else:
-                        rows = jnp.zeros((block, got_ref.shape[3]), jnp.bfloat16)
-                    rows_ref[side, pl.ds(at, block), :] = rows
+                        rows = jnp.zeros((block, half), jnp.bfloat16)
+                    held[pl.ds(at, block), :] = rows.astype(jnp.float32)
+            rows_ref[side] = held[...].T.astype(jnp.bfloat16)
 
     add_columns(me_ref[0] & 1, step, chips_ref, rows_ref, weights, out_ref)
 
 
 def far_row_grad_kernel(chips_ref, me_ref, before_ref, got_ref, *refs):
-    *weights, out_ref, rows_ref = refs
+    *weights, out_ref, rows_ref, held = refs
     step = pl.program_id(0)
     chips, _, count, _ = got_ref.shape
-    block = rows_ref.shape[1] // chips
+    block = out_ref.shape[0] // chips
 
     @pl.when(step == 0)
     def _():
-        for chip in range(chips):
-            for side in range(2):
-                rows_ref[side, chip * block : (chip + 1) * block, :] = got_ref[
-                    chip, side, count - block :, :
-                ]
-
-    add_columns(me_ref[0] & 1, step, chips_ref, rows_ref, weights, out_ref)
+        held[...] = jnp.zeros_like(held)
+        for side in range(2):
+            for chip in range(chips):
+                rows = got_ref[chip, side, count - block :, :]
+                held[chip * block : (chip + 1) * block, :] = rows.astype(jnp.float32)
+            rows_ref[side] = held[...].T.astype(jnp.bfloat16)
+
+    own, mate = rows_ref[me_ref[0] & 1], rows_ref[1 - (me_ref[0] & 1)]
+    depth = weights[0].shape[0]
+    for n in range(len(weights) // 2):
+        total = dot(weights[2 * n][...], own, ((1,), (0,)))
+        total += dot(weights[2 * n + 1][...], mate, ((1,), (0,)))
+        at = chips_ref[n * pl.num_programs(0) + step] * depth
+        out_ref[:, pl.ds(pl.multiple_of(at, depth), depth)] = total.T[: chips * block].astype(
+            jnp.bfloat16
+        )
 
 
 def code_rows(destination, core, per_peer, width):
@@ -270,8 +315,8 @@
     return [pl.BlockSpec(memory_space=pltpu.VMEM)] * count
 
 
-def anywhere(count):
-    return [pl.BlockSpec(memory_space=pl.ANY)] * count
+def hbm(count):
+    return [pl.BlockSpec(memory_space=pltpu.HBM)] * count
 
 
 SCALAR = pl.BlockSpec(memory_space=pltpu.SMEM)
@@ -279,6 +324,7 @@
 
 
 COST = pl.CostEstimate(flops=1024, bytes_accessed=1024, transcendentals=0)
+TRANSFER_COST = pl.CostEstimate(flops=1024, bytes_accessed=28 << 20, transcendentals=0)
 
 
 def per_device_paired(tokens, key_cot, routes, counts, widths, key_weight):
@@ -312,22 +358,22 @@
     column[both] = swap(column[far], near)
     half = piece.shape[0] // 2
     sets, masks = [], []
-    for part in ((0, near), (far, both)):
-        pieces, places = [], []
-        for mask in part:
-            own = column[mask]
-            by_x, by_y = swap(own, X), swap(own, Y)
-            chip = len(masks) % (chips // 2)
-            masks += [mask, mask | X, mask | Y, mask | X | Y]
-            pieces += [own, by_x, by_y, swap(by_y[:half], X), swap(by_x[half:], Y)]
-            places += [(chip, 0), (chip + 1, 0), (chip + 2, 0), (chip + 3, 0), (chip + 3, half)]
-        sets.append((pieces, places))
+    for n, (mask, own) in enumerate(sorted(column.items())):
+        by_x, by_y = swap(own, X), swap(own, Y)
+        if mask == both:
+            across = [swap(by_y[:half], X), swap(by_x[half:], Y)]
+        else:
+            across = [swap(by_x, Y) if mask == near else swap(by_y, X)]
+        places = [(0, 0), (1, 0), (2, 0), (3, 0), (3, half)]
+        sets.append(([own, by_x, by_y, *across], places[: 3 + len(across)]))
+        masks += [mask, mask | X, mask | Y, mask | X | Y]
     order = jnp.stack([lax.shift_right_logical(me ^ mask, 1) for mask in masks])
 
     mate_tokens = swap(after(tokens, column[near]), CORE)
+    late_tokens = after(tokens, column[both])
     columns = [[p + PLANE * z for z in range(levels)] for p in range(PLANE)]
     own_features = lax.all_to_all(
-        jnp.stack([tokens[:, z * wide : (z + 1) * wide] for z in range(levels)]),
+        jnp.stack([late_tokens[:, z * wide : (z + 1) * wide] for z in range(levels)]),
         "dp",
         split_axis=0,
         concat_axis=0,
@@ -350,28 +396,34 @@
     own_cot = jnp.concatenate([mine(upstream), codes], axis=0)
     mate_cot = swap(jnp.concatenate([theirs(upstream), codes], axis=0), CORE)
 
-    kept = jax.ShapeDtypeStruct((width_model // 2, half_cols), jnp.bfloat16)
+    kept = jax.ShapeDtypeStruct((width_model // levels, half_cols), jnp.bfloat16)
     sums = jax.ShapeDtypeStruct((2, rows, half_cols), jnp.float32)
-    (pieces, places), (last_pieces, last_places) = sets
-    first_weight, begun = pl.pallas_call(
-        functools.partial(project_kernel, places),
-        out_shape=(kept, sums),
-        in_specs=[SCALAR] + vmem(2 + len(pieces)),
-        out_specs=tuple(vmem(2)),
-        compiler_params=PARAMS,
-        cost_estimate=COST,
-        name="project",
-    )(order, tokens, mate_tokens, *pieces)
-    delta, last_weight = pl.pallas_call(
-        functools.partial(delta_kernel, last_places, chips // 2),
-        out_shape=(jax.ShapeDtypeStruct((2 * rows + CODE_ROWS, half_cols), jnp.bfloat16), kept),
-        in_specs=[SCALAR] * 2 + vmem(5 + len(last_pieces)),
-        out_specs=tuple(vmem(2)),
-        scratch_shapes=[pltpu.VMEM(sums.shape, sums.dtype)],
-        compiler_params=PARAMS,
-        cost_estimate=COST,
-        name="delta",
-    )(order, me_scalar, tokens, mate_tokens, own_cot, mate_cot, begun, *last_pieces)
+    deltas = jax.ShapeDtypeStruct((2 * rows + CODE_ROWS, half_cols), jnp.bfloat16)
+    kept_weights, begun = [], []
+    for n, (pieces, places) in enumerate(sets):
+        last = n == levels - 1
+        extra = [own_cot, mate_cot] if last else []
+        weight, result = pl.pallas_call(
+            functools.partial(project_kernel, places, n * len(sets), last),
+            out_shape=(kept, deltas if last else sums),
+            in_specs=[SCALAR] * 2
+            + hbm(2)
+            + vmem(len(extra) + len(begun))
+            + hbm(len(pieces)),
+            out_specs=(hbm(1)[0], vmem(1)[0]),
+            scratch_shapes=[
+                pltpu.VMEM((2, rows, width_model), jnp.bfloat16),
+                pltpu.VMEM(kept.shape, jnp.bfloat16),
+                pltpu.SemaphoreType.DMA((2 + 2 * len(pieces),)),
+            ]
+            + ([pltpu.VMEM(sums.shape, sums.dtype)] if last else []),
+            compiler_params=PARAMS,
+            cost_estimate=COST if last else TRANSFER_COST,
+            name="delta" if last else f"project_{n}",
+        )(order, me_scalar, tokens, mate_tokens, *extra, *begun, *pieces)
+        kept_weights += [weight, swap(weight, CORE)]
+        begun = [result]
+    delta = begun[0]
 
     delta_far, delta_near = swap(delta, far), swap(delta, near)
     delta_both = swap(delta_far, near)
@@ -388,8 +440,12 @@
     selected = pl.pallas_call(
         select_kernel,
         out_shape=jax.ShapeDtypeStruct((PLANE * 3 * per_chip, half_cols), jnp.bfloat16),
-        in_specs=[SCALAR] + vmem(3),
+        in_specs=[SCALAR] + hbm(3),
         out_specs=vmem(1)[0],
+        scratch_shapes=[
+            pltpu.VMEM((3, *delta.shape), jnp.bfloat16),
+            pltpu.SemaphoreType.DMA((3,)),
+        ],
         compiler_params=PARAMS,
         cost_estimate=COST,
         name="select",
@@ -400,9 +456,15 @@
     terms = pl.pallas_call(
         weight_grad_kernel,
         out_shape=jax.ShapeDtypeStruct((PLANE, shard + per_chip, half_cols), jnp.bfloat16),
-        in_specs=[SCALAR] + vmem(2 + levels),
-        out_specs=vmem(1)[0],
-        scratch_shapes=[pltpu.VMEM((wide, half_cols), jnp.float32)],
+        in_specs=[SCALAR] + hbm(2 + levels),
+        out_specs=hbm(1)[0],
+        scratch_shapes=[
+            pltpu.VMEM((levels, 2, rows, wide), jnp.bfloat16),
+            pltpu.VMEM((levels, *delta.shape), jnp.bfloat16),
+            pltpu.VMEM((wide, half_cols), jnp.float32),
+            pltpu.VMEM((PLANE, shard + per_chip, half_cols), jnp.bfloat16),
+            pltpu.SemaphoreType.DMA((3 * levels + PLANE,)),
+        ],
         compiler_params=PARAMS,
         cost_estimate=COST,
         name="weight_grad",
@@ -410,7 +472,6 @@
     got = to_plane(terms)
 
     depth = width_model // chips
-    kept_weights = [first_weight, swap(first_weight, CORE), last_weight, swap(last_weight, CORE)]
     weight_specs = [pl.BlockSpec((depth, half_cols), lambda i, *_: (i, 0))] * len(kept_weights)
     row_shape = jax.ShapeDtypeStruct((receive, width_model), jnp.bfloat16)
     row_grads = pl.pallas_call(
@@ -418,10 +479,13 @@
         out_shape=row_shape,
         grid_spec=pltpu.PrefetchScalarGridSpec(
             num_scalar_prefetch=2,
-            grid=(chips // 2,),
+            grid=(chips // levels,),
             in_specs=[pl.BlockSpec(got_near.shape, lambda i, *_: (0, 0, 0, 0))] + weight_specs,
             out_specs=pl.BlockSpec((receive, width_model), lambda i, *_: (0, 0)),
-            scratch_shapes=[pltpu.VMEM((2, receive, half_cols), jnp.bfloat16)],
+            scratch_shapes=[
+                pltpu.VMEM((2, half_cols, receive), jnp.bfloat16),
+                pltpu.VMEM((receive, half_cols), jnp.float32),
+            ],
         ),
         compiler_params=PARAMS,
         cost_estimate=COST,
@@ -433,15 +497,18 @@
         out_shape=row_shape,
         grid_spec=pltpu.PrefetchScalarGridSpec(
             num_scalar_prefetch=2,
-            grid=(chips // 2,),
-            in_specs=anywhere(1)
+            grid=(chips // levels,),
+            in_specs=hbm(1)
             + [pl.BlockSpec(got.shape, lambda i, *_: (0, 0, 0, 0))]
             + weight_specs,
             out_specs=pl.BlockSpec(
                 (count, width_model),
                 lambda i, order, me: (lax.shift_right_logical(me[0], 3) ^ (levels - 1), 0),
             ),
-            scratch_shapes=[pltpu.VMEM((2, count, half_cols), jnp.bfloat16)],
+            scratch_shapes=[
+                pltpu.VMEM((2, half_cols, 128), jnp.bfloat16),
+                pltpu.VMEM((128, half_cols), jnp.float32),
+            ],
         ),
         input_output_aliases={2: 0},
         compiler_params=PARAMS,

time: 161 us -> 175 us (1.087)
  starting transfers between devices: 36.3 us -> 42.7 us
  Pallas kernels: 28.4 us -> 31.2 us
    ppermute x28 -> x27, starting transfers between devices: 24.6 us -> 30 us  [swap(): return lax.ppermute(value, 'dp', [(i, i ^ mask) for i in range(size)])]
    pallas_call x2 -> x4, Pallas kernels: 5.18 us -> 9.73 us  [per_device_paired(): pl.pallas_call(functools.partial(project_kernel, places, n * len(sets), l...]
    ppermute x28 -> x27, waiting for transfers between devices: 65.3 us -> 67.7 us  [swap(): return lax.ppermute(value, 'dp', [(i, i ^ mask) for i in range(size)])]
    unnamed x80 -> x68, local copies, waits for them, and re-layouts: 15.8 us -> 15.5 us
  transfers between devices with their start and end apart: 31 -> 30, of which waited for: 10 -> 12; matrix products, arithmetic and copies ran while one was open for 4% -> 5% of each run, Pallas kernels for 12% -> 13%
where the time goes in v9:
time: 175 us; the launch traced here: 174 us
  waiting for transfers between devices  73.8 us (42%)
  starting transfers between devices  42.7 us (24%)
  Pallas kernels  31.2 us (18%)
  local copies, waits for them, and re-layouts  21.3 us (12%)
  other arithmetic  4.16 us (2%)
    ppermute x27, waiting for transfers between devices, swap(): return lax.ppermute(value, 'dp', [(i, i ^ mask) for i in range(size)])  67.7 us
    ppermute x27, starting transfers between devices, swap(): return lax.ppermute(value, 'dp', [(i, i ^ mask) for i in range(size)])  30 us
    unnamed x68, local copies, waits for them, and re-layouts  15.5 us
    pallas_call x4, Pallas kernels, per_device_paired(): pl.pallas_call(functools.partial(project_kernel, places, n * len(sets), l...  9.73 us
    all_to_all x2, starting transfers between devices, to_plane(): lax.all_to_all(value, 'dp', split_axis=0, concat_axis=0, axis_index_group...  7.45 us
    pallas_call x1, Pallas kernels, per_device_paired(): pl.pallas_call(row_grad_kernel, out_shape=row_shape, grid_spec=pltpu.Pref...  7.26 us
    pallas_call x1, Pallas kernels, per_device_paired(): pl.pallas_call(far_row_grad_kernel, out_shape=row_shape, grid_spec=pltpu....  7.07 us
    all_to_all x2, waiting for transfers between devices, to_plane(): lax.all_to_all(value, 'dp', split_axis=0, concat_axis=0, axis_index_group...  6.06 us
  transfers between devices with their start and end apart: 30, of which 12 were waited for; matrix products, arithmetic and copies ran while one was open for 5% of the time, Pallas kernels for 13%

profile of v9, /device:TPU:0, one launch (start us, length us, event | category | flops | bytes accessed | tf_op | source)
XLA Modules:
  0.0 174.1 jit_solution(4432185327207170471)
XLA Ops:
  1.2 1.0 fusion.11
  2.6 4.0 %collective-permute-start.10 = (bf16[256,512]{1,0:T(8,128)(2,1)S(1)}, bf16[256,512]{1,0:T(8,128)(2,1)S(1)}, u32[]{:S(2)}, u32[]{:S(2)}) collective-permute-start(bf16[256,512]{1,0:T(8,128)(2,1)S(1)} %maximum_select_fusion.refs_0_), channel_id=1, source_target_pairs={{0,16},{1,17},{2,18},{3,19},{4,20},{5,21},{6,22},{7,23},{8,24},{9,... | collective-permute-start | bytes 786440 | tf_op jit(solution)/shard_map/ppermute | solution.py:91
  6.6 12.2 %collective-permute-done.10.refs_1_ = bf16[256,512]{1,0:T(8,128)(2,1)S(1)} collective-permute-done((bf16[256,512]{1,0:T(8,128)(2,1)S(1)}, bf16[256,512]{1,0:T(8,128)(2,1)S(1)}, u32[]{:S(2)}, u32[]{:S(2)}) %collective-permute-start.10) | collective-permute-done | bytes 262176 | tf_op jit(solution)/shard_map/ppermute | solution.py:91
  19.6 7.1 %collective-permute-done.14.refs_3_ = bf16[256,512]{1,0:T(8,128)(2,1)S(1)} collective-permute-done((bf16[256,512]{1,0:T(8,128)(2,1)S(1)}, bf16[256,512]{1,0:T(8,128)(2,1)S(1)}, u32[]{:S(2)}, u32[]{:S(2)}) %collective-permute-start.14) | collective-permute-done | bytes 262176 | tf_op jit(solution)/shard_map/ppermute | solution.py:91
  26.8 1.1 pad_maximum_fusion
  28.0 5.2 %all-to-all-start.1 = ((bf16[4,128,1024]{2,1,0:T(8,128)(2,1)}), bf16[4,128,1024]{2,1,0:T(8,128)(2,1)S(1)}, u32[]{:S(2)}, u32[]{:S(2)}) async-start(bf16[4,128,1024]{2,1,0:T(8,128)(2,1)} %pad_maximum_fusion), calls=%async_computation.1 | async-start | bytes 2097152 | tf_op jit(solution)/shard_map/all_to_all | solution.py:375
  33.2 2.0 %collective-permute-start.1 = (bf16[256,512]{1,0:T(8,128)(2,1)S(1)}, bf16[256,512]{1,0:T(8,128)(2,1)}, u32[]{:S(2)}, u32[]{:S(2)}) collective-permute-start(bf16[256,512]{1,0:T(8,128)(2,1)S(1)} %maximum_select_fusion.refs_0_), channel_id=1, source_target_pairs={{0,8},{1,9},{2,10},{3,11},{4,12},{5,13},{6,14},{7,15},{8,0},{9,1},... | collective-permute-start | bytes 786440 | tf_op jit(solution)/shard_map/ppermute | solution.py:91
  35.2 1.5 collective-permute-start.5
  36.7 1.5 collective-permute-start.4
  38.2 17.0 %collective-permute-done.1.refs_1_ = bf16[256,512]{1,0:T(8,128)(2,1)} collective-permute-done((bf16[256,512]{1,0:T(8,128)(2,1)S(1)}, bf16[256,512]{1,0:T(8,128)(2,1)}, u32[]{:S(2)}, u32[]{:S(2)}) %collective-permute-start.1) | collective-permute-done | bytes 262176 | tf_op jit(solution)/shard_map/ppermute | solution.py:91
  55.4 1.5 collective-permute-start.6
  57.1 1.8 %compare_select_fusion = bf16[128,1024]{1,0:T(8,128)(2,1)} fusion(bf16[128,1024]{1,0:T(8,128)(2,1)} %param.7, s32[1024]{0:T(1024)S(1)} %add_select_fusion, s32[128]{0:T(128)S(1)} %select_reduce_fusion), kind=kLoop, calls=%fused_computation.1 | loop fusion | flops 262144 | bytes 528896 | tf_op jit(solution)/shard_map/jit(_where)/select_n | solution.py:392
  59.4 1.5 collective-permute-start.8
  61.5 3.2 %collective-permute-done.6.refs_3_ = bf16[256,512]{1,0:T(8,128)(2,1)S(1)} collective-permute-done((bf16[256,512]{1,0:T(8,128)(2,1)}, bf16[256,512]{1,0:T(8,128)(2,1)S(1)}, u32[]{:S(2)}, u32[]{:S(2)}) %collective-permute-start.6) | collective-permute-done | bytes 262176 | tf_op jit(solution)/shard_map/ppermute | solution.py:91
  65.4 1.5 collective-permute-start.11
  67.0 3.4 %collective-permute-done.7.refs_2_ = bf16[256,512]{1,0:T(8,128)(2,1)} collective-permute-done((bf16[256,512]{1,0:T(8,128)(2,1)}, bf16[256,512]{1,0:T(8,128)(2,1)}, u32[]{:S(2)}, u32[]{:S(2)}) %collective-permute-start.7) | collective-permute-done | bytes 262176 | tf_op jit(solution)/shard_map/ppermute | solution.py:91
  70.4 1.5 collective-permute-start.16
  72.6 1.5 collective-permute-start.15
  74.1 1.5 collective-permute-start.9
  76.7 1.0 constant_dynamic-slice_fusion.1
  77.7 2.3 %collective-permute-done.16.refs_5_ = bf16[256,512]{1,0:T(8,128)(2,1)} collective-permute-done((bf16[256,512]{1,0:T(8,128)(2,1)}, bf16[256,512]{1,0:T(8,128)(2,1)}, u32[]{:S(2)}, u32[]{:S(2)}) %collective-permute-start.16) | collective-permute-done | bytes 262176 | tf_op jit(solution)/shard_map/ppermute | solution.py:91
  80.0 1.5 collective-permute-start.13
  82.2 1.6 slice.47
  83.8 1.6 slice.48
  86.2 1.5 collective-permute-start.18
  89.8 2.3 %project_0.1 = (bf16[1024,512]{1,0:T(8,128)(2,1)S(1)}, f32[2,128,512]{2,1,0:T(8,128)S(1)}) custom-call(s32[16]{0:T(128)S(1)} %copy-done.28, s32[1]{0:T(128)} %bitcast.16.me_ref, bf16[128,4096]{1,0:T(8,128)(2,1)S(1)} %copy-done, bf16[128,4096]{1,0:T(8,128)(2,1)S(1)} %collective-permute-done.2.mate_ref, bf16[256,512]{1,0:T(8,128)(2,1)S(1)} %maximum_select_fusion.refs_0_, ...), custom_call_target="tpu_custom_call" | custom-call | flops 1024 | bytes 29360128 | tf_op jit(solution)/shard_map/project_0/pallas_call | solution.py:406
  92.1 1.0 copy-done.2
  93.1 2.4 %project_1.1 = (bf16[1024,512]{1,0:T(8,128)(2,1)S(1)}, f32[2,128,512]{2,1,0:T(8,128)S(1)}) custom-call(s32[16]{0:T(128)S(1)} %copy-done.29, s32[1]{0:T(128)} %bitcast.16.me_ref, bf16[128,4096]{1,0:T(8,128)(2,1)S(1)} %copy-done, bf16[128,4096]{1,0:T(8,128)(2,1)S(1)} %collective-permute-done.2.mate_ref, f32[2,128,512]{2,1,0:T(8,128)S(1)} %get-tuple-element.19.refs_0_, ...), custom_call_target="tpu_custom_call" | custom-call | flops 1024 | bytes 29360128 | tf_op jit(solution)/shard_map/project_1/pallas_call | solution.py:406
  95.5 1.0 copy-done.4
  96.5 2.0 %project_2.1 = (bf16[1024,512]{1,0:T(8,128)(2,1)S(1)}, f32[2,128,512]{2,1,0:T(8,128)S(1)}) custom-call(s32[16]{0:T(128)S(1)} %copy-done.29, s32[1]{0:T(128)} %bitcast.16.me_ref, bf16[128,4096]{1,0:T(8,128)(2,1)S(1)} %copy-done, bf16[128,4096]{1,0:T(8,128)(2,1)S(1)} %collective-permute-done.2.mate_ref, f32[2,128,512]{2,1,0:T(8,128)S(1)} %get-tuple-element.20.refs_0_, ...), custom_call_target="tpu_custom_call" | custom-call | flops 1024 | bytes 29360128 | tf_op jit(solution)/shard_map/project_2/pallas_call | solution.py:406
  98.6 1.0 copy-done.7
  101.1 3.0 %delta.1 = (bf16[1024,512]{1,0:T(8,128)(2,1)S(1)}, bf16[272,512]{1,0:T(8,128)(2,1)S(1)}) custom-call(s32[16]{0:T(128)S(1)} %copy-done.29, s32[1]{0:T(128)} %bitcast.16.me_ref, bf16[128,4096]{1,0:T(8,128)(2,1)S(1)} %copy-done, bf16[128,4096]{1,0:T(8,128)(2,1)S(1)} %collective-permute-done.2.mate_ref, bf16[144,512]{1,0:T(8,128)(2,1)S(1)} %copy-done.13, ...), custom_call_target="tpu_custom_call" | custom-call | flops 1024 | bytes 1024 | tf_op jit(solution)/shard_map/delta/pallas_call | solution.py:406
  104.2 1.1 copy-done.10
  105.2 4.7 %collective-permute-start.20 = (bf16[272,512]{1,0:T(8,128)(2,1)S(1)}, bf16[272,512]{1,0:T(8,128)(2,1)S(1)}, u32[]{:S(2)}, u32[]{:S(2)}) collective-permute-start(bf16[272,512]{1,0:T(8,128)(2,1)S(1)} %get-tuple-element.22.refs_0_), channel_id=1, source_target_pairs={{0,16},{1,17},{2,18},{3,19},{4,20},{5,21},{6,22},{7,23},{8,24},{9,... | collective-permute-start | bytes 835592 | tf_op jit(solution)/shard_map/ppermute | solution.py:91
  109.9 12.5 %collective-permute-done.20.refs_2_ = bf16[272,512]{1,0:T(8,128)(2,1)S(1)} collective-permute-done((bf16[272,512]{1,0:T(8,128)(2,1)S(1)}, bf16[272,512]{1,0:T(8,128)(2,1)S(1)}, u32[]{:S(2)}, u32[]{:S(2)}) %collective-permute-start.20) | collective-permute-done | bytes 278560 | tf_op jit(solution)/shard_map/ppermute | solution.py:91
  122.4 1.3 collective-permute-done.19.refs_1_
  123.7 1.4 select.28
  125.1 3.5 %all-to-all-start = ((bf16[8,48,512]{2,1,0:T(8,128)(2,1)}), bf16[8,48,512]{2,1,0:T(8,128)(2,1)S(1)}, u32[]{:S(2)}, u32[]{:S(2)}) async-start(bf16[8,48,512]{2,1,0:T(8,128)(2,1)} %bitcast.22), calls=%async_computation | async-start | bytes 786432 | tf_op jit(solution)/shard_map/all_to_all | solution.py:433
  129.7 7.9 %collective-permute-done.26.refs_3_ = bf16[272,512]{1,0:T(8,128)(2,1)S(1)} collective-permute-done((bf16[272,512]{1,0:T(8,128)(2,1)S(1)}, bf16[272,512]{1,0:T(8,128)(2,1)S(1)}, u32[]{:S(2)}, u32[]{:S(2)}) %collective-permute-start.26) | collective-permute-done | bytes 278560 | tf_op jit(solution)/shard_map/ppermute | solution.py:91
  137.6 4.8 %weight_grad.1 = bf16[8,144,512]{2,1,0:T(8,128)(2,1)} custom-call(s32[1]{0:T(128)} %bitcast.16.me_ref, bf16[4,128,1024]{2,1,0:T(8,128)(2,1)S(1)} %all-to-all-done.1.own_ref, bf16[4,128,1024]{2,1,0:T(8,128)(2,1)} %collective-permute-done.25.mate_ref, bf16[272,512]{1,0:T(8,128)(2,1)S(1)} %get-tuple-element.22.refs_0_, ...), custom_call_target="tpu_custom_call" | custom-call | flops 1024 | bytes 1024 | tf_op jit(solution)/shard_map/weight_grad/pallas_call | solution.py:456
  143.2 4.0 %all-to-all-start.2 = ((bf16[8,144,512]{2,1,0:T(8,128)(2,1)}), bf16[8,144,512]{2,1,0:T(8,128)(2,1)S(1)}, u32[]{:S(2)}, u32[]{:S(2)}) async-start(bf16[8,144,512]{2,1,0:T(8,128)(2,1)} %weight_grad.1), calls=%async_computation.2 | async-start | bytes 2359296 | tf_op jit(solution)/shard_map/all_to_all | solution.py:433
  147.2 1.2 copy-done.5
  148.4 1.2 copy-done.8
  149.7 1.0 copy-done.12
  150.7 7.3 %row_grad.1.before_ref = bf16[256,4096]{1,0:T(8,128)(2,1)} custom-call(s32[16]{0:T(128)S(1)} %copy-done.30, s32[1]{0:T(128)} %bitcast.16.me_ref, bf16[4,2,48,512]{3,2,1,0:T(8,128)(2,1)S(1)} %bitcast.38, bf16[1024,512]{1,0:T(8,128)(2,1)S(1)} %copy-done.3, bf16[1024,512]{1,0:T(8,128)(2,1)} %collective-permute-done.21.refs_1_, bf16[1024,512]{1,0:T(8,128)(2,1)S(1)} %copy-done.5, ...), custom_call_target="tpu_custom_call" | custom-call | flops 1024 | bytes 1024 | tf_op jit(solution)/shard_map/row_grad/pallas_call | solution.py:477
  157.9 6.1 %all-to-all-done.2 = bf16[8,144,512]{2,1,0:T(8,128)(2,1)S(1)} async-done(((bf16[8,144,512]{2,1,0:T(8,128)(2,1)}), bf16[8,144,512]{2,1,0:T(8,128)(2,1)S(1)}, u32[]{:S(2)}, u32[]{:S(2)}) %all-to-all-start.2) | async-done | bytes 1179680 | tf_op jit(solution)/shard_map/all_to_all | solution.py:433
  165.8 1.2 copy-done.9
  167.0 7.1 %far_row_grad.1 = bf16[256,4096]{1,0:T(8,128)(2,1)} custom-call(s32[16]{0:T(128)S(1)} %copy-done.30, s32[1]{0:T(128)} %bitcast.16.me_ref, bf16[256,4096]{1,0:T(8,128)(2,1)} %row_grad.1.before_ref, bf16[4,2,144,512]{3,2,1,0:T(8,128)(2,1)} %bitcast.37, bf16[1024,512]{1,0:T(8,128)(2,1)S(1)} %copy-done.3, ...), custom_call_target="tpu_custom_call", output_to_operand_aliasing={{}: (2, {})} | custom-call | flops 1024 | bytes 1024 | tf_op jit(solution)/shard_map/far_row_grad/pallas_call | solution.py:495
  (109 shorter events, 14.9 us)
Async XLA Ops:
  0.6 26.1 %copy-start = (bf16[128,4096]{1,0:T(8,128)(2,1)S(1)}, bf16[128,4096]{1,0:T(8,128)(2,1)}, u32[]{:S(2)}) copy-start(bf16[128,4096]{1,0:T(8,128)(2,1)} %own_ref.7) | copy-start | bytes 3145732
  0.6 1.9 %collective-permute-start = (bf16[128,1024]{1,0:T(8,128)(2,1)}, bf16[128,1024]{1,0:T(8,128)(2,1)S(1)}, u32[]{:S(2)}, u32[]{:S(2)}) collective-permute-start(bf16[128,1024]{1,0:T(8,128)(2,1)} %param.11), channel_id=1, source_target_pairs={{0,1},{1,0},{2,3},{3,2},{4,5},{5,4},{6,7},{7,6},{8,9},{9,8},{10,11... | collective-permute-start | bytes 786440 | tf_op jit(solution)/shard_map/ppermute | solution.py:91
  2.6 16.2 %collective-permute-start.10 = (bf16[256,512]{1,0:T(8,128)(2,1)S(1)}, bf16[256,512]{1,0:T(8,128)(2,1)S(1)}, u32[]{:S(2)}, u32[]{:S(2)}) collective-permute-start(bf16[256,512]{1,0:T(8,128)(2,1)S(1)} %maximum_select_fusion.refs_0_), channel_id=1, source_target_pairs={{0,16},{1,17},{2,18},{3,19},{4,20},{5,21},{6,22},{7,23},{8,24},{9,... | collective-permute-start | bytes 786440 | tf_op jit(solution)/shard_map/ppermute | solution.py:91
  18.9 9.1 %copy-start.18 = (bf16[256,512]{1,0:T(8,128)(2,1)}, bf16[256,512]{1,0:T(8,128)(2,1)S(1)}, u32[]{:S(2)}) copy-start(bf16[256,512]{1,0:T(8,128)(2,1)S(1)} %collective-permute-done.10.refs_1_) | copy-start | bytes 786436
  18.9 7.8 %collective-permute-start.14 = (bf16[256,512]{1,0:T(8,128)(2,1)S(1)}, bf16[256,512]{1,0:T(8,128)(2,1)S(1)}, u32[]{:S(2)}, u32[]{:S(2)}) collective-permute-start(bf16[256,512]{1,0:T(8,128)(2,1)S(1)} %collective-permute-done.10.refs_1_), channel_id=1, source_target_pairs={{0,8},{1,9},{2,10},{3,11},{4,12},{5,13},{6,14},{7,15},{8,0},{9,1},... | collective-permute-start | bytes 786440 | tf_op jit(solution)/shard_map/ppermute | solution.py:91
  26.7 1.2 copy-start.14
  26.8 28.4 %copy-start.31 = (s32[1,4]{1,0:T(1,128)S(1)}, s32[1,4]{1,0:T(1,128)}, u32[]{:S(2)}) copy-start(s32[1,4]{1,0:T(1,128)} %param.9) | copy-start | bytes 52
  26.8 30.1 %copy-start.32 = (s32[4]{0:T(128)S(1)}, s32[4]{0:T(128)}, u32[]{:S(2)}) copy-start(s32[4]{0:T(128)} %param.10) | copy-start | bytes 52
  26.8 34.1 %copy-start.33 = (s32[128,1]{0,1:T(1,128)S(1)}, s32[128,1]{0,1:T(1,128)}, u32[]{:S(2)}) copy-start(s32[128,1]{0,1:T(1,128)} %param.8) | copy-start | bytes 1540
  28.0 48.7 %all-to-all-start.1 = ((bf16[4,128,1024]{2,1,0:T(8,128)(2,1)}), bf16[4,128,1024]{2,1,0:T(8,128)(2,1)S(1)}, u32[]{:S(2)}, u32[]{:S(2)}) async-start(bf16[4,128,1024]{2,1,0:T(8,128)(2,1)} %pad_maximum_fusion), calls=%async_computation.1 | async-start | bytes 2097152 | tf_op jit(solution)/shard_map/all_to_all | solution.py:375
  33.2 22.0 %collective-permute-start.1 = (bf16[256,512]{1,0:T(8,128)(2,1)S(1)}, bf16[256,512]{1,0:T(8,128)(2,1)}, u32[]{:S(2)}, u32[]{:S(2)}) collective-permute-start(bf16[256,512]{1,0:T(8,128)(2,1)S(1)} %maximum_select_fusion.refs_0_), channel_id=1, source_target_pairs={{0,8},{1,9},{2,10},{3,11},{4,12},{5,13},{6,14},{7,15},{8,0},{9,1},... | collective-permute-start | bytes 786440 | tf_op jit(solution)/shard_map/ppermute | solution.py:91
  35.2 20.2 %collective-permute-start.5 = (bf16[256,512]{1,0:T(8,128)(2,1)S(1)}, bf16[256,512]{1,0:T(8,128)(2,1)}, u32[]{:S(2)}, u32[]{:S(2)}) collective-permute-start(bf16[256,512]{1,0:T(8,128)(2,1)S(1)} %maximum_select_fusion.refs_0_), channel_id=1, source_target_pairs={{0,4},{1,5},{2,6},{3,7},{4,0},{5,1},{6,2},{7,3},{8,12},{9,13},{10,... | collective-permute-start | bytes 786440 | tf_op jit(solution)/shard_map/ppermute | solution.py:91
  36.7 24.2 %collective-permute-start.4 = (bf16[256,512]{1,0:T(8,128)(2,1)S(1)}, bf16[256,512]{1,0:T(8,128)(2,1)}, u32[]{:S(2)}, u32[]{:S(2)}) collective-permute-start(bf16[256,512]{1,0:T(8,128)(2,1)S(1)} %maximum_select_fusion.refs_0_), channel_id=1, source_target_pairs={{0,2},{1,3},{2,0},{3,1},{4,6},{5,7},{6,4},{7,5},{8,10},{9,11},{10,... | collective-permute-start | bytes 786440 | tf_op jit(solution)/shard_map/ppermute | solution.py:91
  55.2 31.0 %collective-permute-start.2 = (bf16[128,4096]{1,0:T(8,128)(2,1)S(1)}, bf16[128,4096]{1,0:T(8,128)(2,1)S(1)}, u32[]{:S(2)}, u32[]{:S(2)}) collective-permute-start(bf16[128,4096]{1,0:T(8,128)(2,1)S(1)} %copy-done), channel_id=1, source_target_pairs={{0,1},{1,0},{2,3},{3,2},{4,5},{5,4},{6,7},{7,6},{8,9},{9,8},{10,11... | collective-permute-start | bytes 3145736 | tf_op jit(solution)/shard_map/ppermute | solution.py:91
  55.4 9.3 %collective-permute-start.6 = (bf16[256,512]{1,0:T(8,128)(2,1)}, bf16[256,512]{1,0:T(8,128)(2,1)S(1)}, u32[]{:S(2)}, u32[]{:S(2)}) collective-permute-start(bf16[256,512]{1,0:T(8,128)(2,1)} %collective-permute-done.5.refs_2_), channel_id=1, source_target_pairs={{0,2},{1,3},{2,0},{3,1},{4,6},{5,7},{6,4},{7,5},{8,10},{9,11},{10,... | collective-permute-start | bytes 786440 | tf_op jit(solution)/shard_map/ppermute | solution.py:91
  58.8 11.6 %collective-permute-start.7 = (bf16[256,512]{1,0:T(8,128)(2,1)}, bf16[256,512]{1,0:T(8,128)(2,1)}, u32[]{:S(2)}, u32[]{:S(2)}) collective-permute-start(bf16[256,512]{1,0:T(8,128)(2,1)} %collective-permute-done.1.refs_1_), channel_id=1, source_target_pairs={{0,2},{1,3},{2,0},{3,1},{4,6},{5,7},{6,4},{7,5},{8,10},{9,11},{10,... | collective-permute-start | bytes 786440 | tf_op jit(solution)/shard_map/ppermute | solution.py:91
  59.4 12.6 %collective-permute-start.8 = (bf16[256,512]{1,0:T(8,128)(2,1)}, bf16[256,512]{1,0:T(8,128)(2,1)S(1)}, u32[]{:S(2)}, u32[]{:S(2)}) collective-permute-start(bf16[256,512]{1,0:T(8,128)(2,1)} %collective-permute-done.1.refs_1_), channel_id=1, source_target_pairs={{0,4},{1,5},{2,6},{3,7},{4,0},{5,1},{6,2},{7,3},{8,12},{9,13},{10,... | collective-permute-start | bytes 786440 | tf_op jit(solution)/shard_map/ppermute | solution.py:91
  60.9 13.2 %collective-permute-start.12 = (bf16[256,512]{1,0:T(8,128)(2,1)}, bf16[256,512]{1,0:T(8,128)(2,1)S(1)}, u32[]{:S(2)}, u32[]{:S(2)}) collective-permute-start(bf16[256,512]{1,0:T(8,128)(2,1)} %copy-done.18), channel_id=1, source_target_pairs={{0,4},{1,5},{2,6},{3,7},{4,0},{5,1},{6,2},{7,3},{8,12},{9,13},{10,... | collective-permute-start | bytes 786440 | tf_op jit(solution)/shard_map/ppermute | solution.py:91
  65.4 10.5 %collective-permute-start.11 = (bf16[256,512]{1,0:T(8,128)(2,1)}, bf16[256,512]{1,0:T(8,128)(2,1)S(1)}, u32[]{:S(2)}, u32[]{:S(2)}) collective-permute-start(bf16[256,512]{1,0:T(8,128)(2,1)} %copy-done.18), channel_id=1, source_target_pairs={{0,2},{1,3},{2,0},{3,1},{4,6},{5,7},{6,4},{7,5},{8,10},{9,11},{10,... | collective-permute-start | bytes 786440 | tf_op jit(solution)/shard_map/ppermute | solution.py:91
  70.4 9.6 %collective-permute-start.16 = (bf16[256,512]{1,0:T(8,128)(2,1)}, bf16[256,512]{1,0:T(8,128)(2,1)}, u32[]{:S(2)}, u32[]{:S(2)}) collective-permute-start(bf16[256,512]{1,0:T(8,128)(2,1)} %copy-done.14), channel_id=1, source_target_pairs={{0,4},{1,5},{2,6},{3,7},{4,0},{5,1},{6,2},{7,3},{8,12},{9,13},{10,... | collective-permute-start | bytes 786440 | tf_op jit(solution)/shard_map/ppermute | solution.py:91
  72.6 9.6 %collective-permute-start.15 = (bf16[256,512]{1,0:T(8,128)(2,1)}, bf16[256,512]{1,0:T(8,128)(2,1)}, u32[]{:S(2)}, u32[]{:S(2)}) collective-permute-start(bf16[256,512]{1,0:T(8,128)(2,1)} %copy-done.14), channel_id=1, source_target_pairs={{0,2},{1,3},{2,0},{3,1},{4,6},{5,7},{6,4},{7,5},{8,10},{9,11},{10,... | collective-permute-start | bytes 786440 | tf_op jit(solution)/shard_map/ppermute | solution.py:91
  74.1 1.5 copy-start.20
  74.1 11.2 %collective-permute-start.9 = (bf16[256,512]{1,0:T(8,128)(2,1)}, bf16[256,512]{1,0:T(8,128)(2,1)}, u32[]{:S(2)}, u32[]{:S(2)}) collective-permute-start(bf16[256,512]{1,0:T(8,128)(2,1)} %collective-permute-done.7.refs_2_), channel_id=1, source_target_pairs={{0,4},{1,5},{2,6},{3,7},{4,0},{5,1},{6,2},{7,3},{8,12},{9,13},{10,... | collective-permute-start | bytes 786440 | tf_op jit(solution)/shard_map/ppermute | solution.py:91
  76.7 60.9 %collective-permute-start.25 = (bf16[4,128,1024]{2,1,0:T(8,128)(2,1)S(1)}, bf16[4,128,1024]{2,1,0:T(8,128)(2,1)}, u32[]{:S(2)}, u32[]{:S(2)}) collective-permute-start(bf16[4,128,1024]{2,1,0:T(8,128)(2,1)S(1)} %all-to-all-done.1.own_ref), channel_id=1, source_target_pairs={{0,1},{1,0},{2,3},{3,2},{4,5},{5,4},{6,7},{7,6},{8,9},{9,8},{10,11... | collective-permute-start | bytes 3145736 | tf_op jit(solution)/shard_map/ppermute | solution.py:91
  80.0 16.5 %collective-permute-start.13 = (bf16[256,512]{1,0:T(8,128)(2,1)}, bf16[256,512]{1,0:T(8,128)(2,1)}, u32[]{:S(2)}, u32[]{:S(2)}) collective-permute-start(bf16[256,512]{1,0:T(8,128)(2,1)} %copy-done.20), channel_id=1, source_target_pairs={{0,2},{1,3},{2,0},{3,1},{4,6},{5,7},{6,4},{7,5},{8,10},{9,11},{10,... | collective-permute-start | bytes 786440 | tf_op jit(solution)/shard_map/ppermute | solution.py:91
  82.2 17.3 %collective-permute-start.3 = (bf16[144,512]{1,0:T(8,128)(2,1)}, bf16[144,512]{1,0:T(8,128)(2,1)S(1)}, u32[]{:S(2)}, u32[]{:S(2)}) collective-permute-start(bf16[144,512]{1,0:T(8,128)(2,1)} %get-tuple-element.38), channel_id=1, source_target_pairs={{0,1},{1,0},{2,3},{3,2},{4,5},{5,4},{6,7},{7,6},{8,9},{9,8},{10,11... | collective-permute-start | bytes 442376 | tf_op jit(solution)/shard_map/ppermute | solution.py:91
  85.3 14.9 %collective-permute-start.17 = (bf16[128,512]{1,0:T(8,128)(2,1)}, bf16[128,512]{1,0:T(8,128)(2,1)}, u32[]{:S(2)}, u32[]{:S(2)}) collective-permute-start(bf16[128,512]{1,0:T(8,128)(2,1)} %slice.47), channel_id=1, source_target_pairs={{0,2},{1,3},{2,0},{3,1},{4,6},{5,7},{6,4},{7,5},{8,10},{9,11},{10,... | collective-permute-start | bytes 393224 | tf_op jit(solution)/shard_map/ppermute | solution.py:91
  86.2 14.0 %collective-permute-start.18 = (bf16[128,512]{1,0:T(8,128)(2,1)}, bf16[128,512]{1,0:T(8,128)(2,1)}, u32[]{:S(2)}, u32[]{:S(2)}) collective-permute-start(bf16[128,512]{1,0:T(8,128)(2,1)} %slice.48), channel_id=1, source_target_pairs={{0,4},{1,5},{2,6},{3,7},{4,0},{5,1},{6,2},{7,3},{8,12},{9,13},{10,... | collective-permute-start | bytes 393224 | tf_op jit(solution)/shard_map/ppermute | solution.py:91
  88.3 4.8 %copy-start.29 = (s32[16]{0:T(128)S(1)}, s32[16]{0:T(128)}, u32[]{:S(2)}) copy-start(s32[16]{0:T(128)} %stack.87.chips_ref) | copy-start | bytes 196
  89.8 3.3 %copy-start.23 = (bf16[256,512]{1,0:T(8,128)(2,1)S(1)}, bf16[256,512]{1,0:T(8,128)(2,1)}, u32[]{:S(2)}) copy-start(bf16[256,512]{1,0:T(8,128)(2,1)} %copy-done.22) | copy-start | bytes 786436
  93.1 3.4 %copy-start.19 = (bf16[256,512]{1,0:T(8,128)(2,1)S(1)}, bf16[256,512]{1,0:T(8,128)(2,1)}, u32[]{:S(2)}) copy-start(bf16[256,512]{1,0:T(8,128)(2,1)} %copy-done.18) | copy-start | bytes 786436
  93.1 3.4 %copy-start.21 = (bf16[256,512]{1,0:T(8,128)(2,1)S(1)}, bf16[256,512]{1,0:T(8,128)(2,1)}, u32[]{:S(2)}) copy-start(bf16[256,512]{1,0:T(8,128)(2,1)} %copy-done.20) | copy-start | bytes 786436
  93.1 3.4 %copy-start.25 = (bf16[256,512]{1,0:T(8,128)(2,1)S(1)}, bf16[256,512]{1,0:T(8,128)(2,1)}, u32[]{:S(2)}) copy-start(bf16[256,512]{1,0:T(8,128)(2,1)} %copy-done.24) | copy-start | bytes 786436
  96.5 3.7 %copy-start.13 = (bf16[144,512]{1,0:T(8,128)(2,1)S(1)}, bf16[144,512]{1,0:T(8,128)(2,1)}, u32[]{:S(2)}) copy-start(bf16[144,512]{1,0:T(8,128)(2,1)} %get-tuple-element.39.refs_0_) | copy-start | bytes 442372
  96.5 3.7 %copy-start.15 = (bf16[256,512]{1,0:T(8,128)(2,1)S(1)}, bf16[256,512]{1,0:T(8,128)(2,1)}, u32[]{:S(2)}) copy-start(bf16[256,512]{1,0:T(8,128)(2,1)} %copy-done.14) | copy-start | bytes 786436
  105.2 17.2 %collective-permute-start.20 = (bf16[272,512]{1,0:T(8,128)(2,1)S(1)}, bf16[272,512]{1,0:T(8,128)(2,1)S(1)}, u32[]{:S(2)}, u32[]{:S(2)}) collective-permute-start(bf16[272,512]{1,0:T(8,128)(2,1)S(1)} %get-tuple-element.22.refs_0_), channel_id=1, source_target_pairs={{0,16},{1,17},{2,18},{3,19},{4,20},{5,21},{6,22},{7,23},{8,24},{9,... | collective-permute-start | bytes 835592 | tf_op jit(solution)/shard_map/ppermute | solution.py:91
  109.9 13.8 %collective-permute-start.19 = (bf16[272,512]{1,0:T(8,128)(2,1)S(1)}, bf16[272,512]{1,0:T(8,128)(2,1)S(1)}, u32[]{:S(2)}, u32[]{:S(2)}) collective-permute-start(bf16[272,512]{1,0:T(8,128)(2,1)S(1)} %get-tuple-element.22.refs_0_), channel_id=1, source_target_pairs={{0,8},{1,9},{2,10},{3,11},{4,12},{5,13},{6,14},{7,15},{8,0},{9,1},... | collective-permute-start | bytes 835592 | tf_op jit(solution)/shard_map/ppermute | solution.py:91
  125.1 17.3 %all-to-all-start = ((bf16[8,48,512]{2,1,0:T(8,128)(2,1)}), bf16[8,48,512]{2,1,0:T(8,128)(2,1)S(1)}, u32[]{:S(2)}, u32[]{:S(2)}) async-start(bf16[8,48,512]{2,1,0:T(8,128)(2,1)} %bitcast.22), calls=%async_computation | async-start | bytes 786432 | tf_op jit(solution)/shard_map/all_to_all | solution.py:433
  128.6 9.0 %collective-permute-start.26 = (bf16[272,512]{1,0:T(8,128)(2,1)S(1)}, bf16[272,512]{1,0:T(8,128)(2,1)S(1)}, u32[]{:S(2)}, u32[]{:S(2)}) collective-permute-start(bf16[272,512]{1,0:T(8,128)(2,1)S(1)} %collective-permute-done.20.refs_2_), channel_id=1, source_target_pairs={{0,8},{1,9},{2,10},{3,11},{4,12},{5,13},{6,14},{7,15},{8,0},{9,1},... | collective-permute-start | bytes 835592 | tf_op jit(solution)/shard_map/ppermute | solution.py:91
  129.1 18.1 %collective-permute-start.24 = (bf16[1024,512]{1,0:T(8,128)(2,1)}, bf16[1024,512]{1,0:T(8,128)(2,1)}, u32[]{:S(2)}, u32[]{:S(2)}) collective-permute-start(bf16[1024,512]{1,0:T(8,128)(2,1)} %copy-done.10), channel_id=1, source_target_pairs={{0,1},{1,0},{2,3},{3,2},{4,5},{5,4},{6,7},{7,6},{8,9},{9,8},{10,11... | collective-permute-start | bytes 3145736 | tf_op jit(solution)/shard_map/ppermute | solution.py:91
  129.2 18.0 %collective-permute-start.23 = (bf16[1024,512]{1,0:T(8,128)(2,1)}, bf16[1024,512]{1,0:T(8,128)(2,1)}, u32[]{:S(2)}, u32[]{:S(2)}) collective-permute-start(bf16[1024,512]{1,0:T(8,128)(2,1)} %copy-done.7), channel_id=1, source_target_pairs={{0,1},{1,0},{2,3},{3,2},{4,5},{5,4},{6,7},{7,6},{8,9},{9,8},{10,11... | collective-permute-start | bytes 3145736 | tf_op jit(solution)/shard_map/ppermute | solution.py:91
  129.6 17.6 %collective-permute-start.22 = (bf16[1024,512]{1,0:T(8,128)(2,1)}, bf16[1024,512]{1,0:T(8,128)(2,1)}, u32[]{:S(2)}, u32[]{:S(2)}) collective-permute-start(bf16[1024,512]{1,0:T(8,128)(2,1)} %copy-done.4), channel_id=1, source_target_pairs={{0,1},{1,0},{2,3},{3,2},{4,5},{5,4},{6,7},{7,6},{8,9},{9,8},{10,11... | collective-permute-start | bytes 3145736 | tf_op jit(solution)/shard_map/ppermute | solution.py:91
  137.6 9.6 %collective-permute-start.21 = (bf16[1024,512]{1,0:T(8,128)(2,1)}, bf16[1024,512]{1,0:T(8,128)(2,1)}, u32[]{:S(2)}, u32[]{:S(2)}) collective-permute-start(bf16[1024,512]{1,0:T(8,128)(2,1)} %copy-done.2), channel_id=1, source_target_pairs={{0,1},{1,0},{2,3},{3,2},{4,5},{5,4},{6,7},{7,6},{8,9},{9,8},{10,11... | collective-permute-start | bytes 3145736 | tf_op jit(solution)/shard_map/ppermute | solution.py:91
  142.4 4.8 %copy-start.3 = (bf16[1024,512]{1,0:T(8,128)(2,1)S(1)}, bf16[1024,512]{1,0:T(8,128)(2,1)}, u32[]{:S(2)}) copy-start(bf16[1024,512]{1,0:T(8,128)(2,1)} %copy-done.2) | copy-start | bytes 3145732
  142.4 4.8 %copy-start.30 = (s32[16]{0:T(128)S(1)}, s32[16]{0:T(128)}, u32[]{:S(2)}) copy-start(s32[16]{0:T(128)} %stack.87.chips_ref) | copy-start | bytes 196
  143.2 20.8 %all-to-all-start.2 = ((bf16[8,144,512]{2,1,0:T(8,128)(2,1)}), bf16[8,144,512]{2,1,0:T(8,128)(2,1)S(1)}, u32[]{:S(2)}, u32[]{:S(2)}) async-start(bf16[8,144,512]{2,1,0:T(8,128)(2,1)} %weight_grad.1), calls=%async_computation.2 | async-start | bytes 2359296 | tf_op jit(solution)/shard_map/all_to_all | solution.py:433
  164.0 1.2 copy-start.1
  164.0 1.8 %copy-start.6 = (bf16[1024,512]{1,0:T(8,128)(2,1)S(1)}, bf16[1024,512]{1,0:T(8,128)(2,1)}, u32[]{:S(2)}) copy-start(bf16[1024,512]{1,0:T(8,128)(2,1)} %copy-done.4) | copy-start | bytes 3145732
  (16 other events, 14.6 us)

commit v10 on v8

--- a/solution.py
+++ b/solution.py
@@ -10,7 +10,7 @@
 
 HEAD_DIM = 128
 NSUB = 4
-VMEM_LIMIT = 20 * 1024 * 1024
+VMEM_LIMIT = 48 * 1024 * 1024
 CODE_ROWS = 16
 epsilon = 1e-06
 
@@ -99,44 +99,22 @@
     return lax.dot_general(a, b, (dims, ((), ())), preferred_element_type=jnp.float32)
 
 
-def add_products(places, chips_ref, begin, token_refs, pieces, weight_ref, acc, fresh):
-    chip_rows = max(piece.shape[0] for piece in pieces)
-    for (chip, first), piece_ref in zip(places, pieces):
+def delta_kernel(places, chips_ref, me_ref, own_ref, mate_ref, own_cot_ref, mate_cot_ref, *refs):
+    *pieces, delta_ref, weight_ref, acc = refs
+    core = me_ref[0] & 1
+    rows = own_ref.shape[0]
+    chip_rows = pieces[0].shape[0]
+    for n, ((chip, first), piece_ref) in enumerate(zip(places, pieces)):
         piece = piece_ref[...]
         depth = piece.shape[0]
         weight_ref[chip * chip_rows + first : chip * chip_rows + first + depth, :] = piece
-        at = pl.multiple_of(chips_ref[begin + chip] * chip_rows + first, 128)
-        for side, ref in enumerate(token_refs):
+        at = pl.multiple_of(chips_ref[chip] * chip_rows + first, 128)
+        for side, ref in enumerate((own_ref, mate_ref)):
             part = dot(ref[:, pl.ds(at, depth)], piece, ((1,), (0,)))
-            if fresh:
+            if n == 0:
                 acc[side] = part
             else:
                 acc[side] += part
-        fresh = False
-
-
-def project_kernel(places, chips_ref, own_ref, mate_ref, *refs):
-    *pieces, weight_ref, acc_ref = refs
-    add_products(places, chips_ref, 0, (own_ref, mate_ref), pieces, weight_ref, acc_ref, True)
-
-
-def delta_kernel(
-    places,
-    begin,
-    chips_ref,
-    me_ref,
-    own_ref,
-    mate_ref,
-    own_cot_ref,
-    mate_cot_ref,
-    begun_ref,
-    *refs,
-):
-    *pieces, delta_ref, weight_ref, acc = refs
-    core = me_ref[0] & 1
-    rows = own_ref.shape[0]
-    acc[...] = begun_ref[...]
-    add_products(places, chips_ref, begin, (own_ref, mate_ref), pieces, weight_ref, acc, False)
     delta_ref[2 * rows :, :] = jnp.zeros_like(delta_ref[2 * rows :, :])
     for side, cot_ref in enumerate((own_cot_ref, mate_cot_ref)):
         at = pl.multiple_of((core ^ side) * rows, rows)
@@ -186,74 +164,43 @@
                 acc[...] = part
             else:
                 acc[...] += part
-    blocks, depth, _ = part_ref.shape
-    shard = acc.shape[0] // blocks
-    extra = depth - shard
-    far = selected_rows(plane, [deltas[-1][...]], blocks * extra)
-    for block in range(blocks):
-        part_ref[block, :shard, :] = acc[block * shard : (block + 1) * shard, :].astype(
-            jnp.bfloat16
-        )
-        part_ref[block, shard:, :] = far[block * extra : (block + 1) * extra, :]
+    part_ref[...] = acc[...].astype(jnp.bfloat16)
 
 
 def sum_kernel(norm, parts_ref, grad_ref):
-    shard, cols = grad_ref.shape
-    half = cols // 2
+    half = parts_ref.shape[3]
     for side in range(2):
-        total = parts_ref[0, side, :shard, :].astype(jnp.float32)
+        total = parts_ref[0, side].astype(jnp.float32)
         for chip in range(1, parts_ref.shape[0]):
-            total += parts_ref[chip, side, :shard, :].astype(jnp.float32)
+            total += parts_ref[chip, side].astype(jnp.float32)
         grad_ref[:, side * half : (side + 1) * half] = total / norm
 
 
-def add_columns(core, step, chips_ref, rows_ref, weights, out_ref):
-    own, mate = rows_ref[core], rows_ref[1 - core]
-    depth = weights[0].shape[0]
-    for n in range(2):
-        total = dot(own, weights[2 * n][...], ((1,), (1,)))
-        total += dot(mate, weights[2 * n + 1][...], ((1,), (1,)))
-        at = chips_ref[n * pl.num_programs(0) + step] * depth
-        out_ref[:, pl.ds(pl.multiple_of(at, depth), depth)] = total.astype(jnp.bfloat16)
-
-
 def row_grad_kernel(chips_ref, me_ref, got_ref, *refs):
-    *weights, out_ref, rows_ref = refs
+    *weights, out_ref, rows_ref, held = refs
     step = pl.program_id(0)
-    chips, _, count, _ = got_ref.shape
-    block = rows_ref.shape[1] // (chips * 4)
+    chips, _, count, half = got_ref.shape
+    block = held.shape[0] // (chips * 4)
     level = lax.shift_right_logical(me_ref[0], 3)
 
     @pl.when(step == 0)
     def _():
-        for n in range(4):
-            for chip in range(chips):
-                at = pl.multiple_of(((level ^ n) * chips + chip) * block, block)
-                for side in range(2):
-                    if n < count // block:
-                        rows = got_ref[chip, side, n * block : (n + 1) * block, :]
-                    else:
-                        rows = jnp.zeros((block, got_ref.shape[3]), jnp.bfloat16)
-                    rows_ref[side, pl.ds(at, block), :] = rows
-
-    add_columns(me_ref[0] & 1, step, chips_ref, rows_ref, weights, out_ref)
-
-
-def far_row_grad_kernel(chips_ref, me_ref, before_ref, got_ref, *refs):
-    *weights, out_ref, rows_ref = refs
-    step = pl.program_id(0)
-    chips, _, count, _ = got_ref.shape
-    block = rows_ref.shape[1] // chips
-
-    @pl.when(step == 0)
-    def _():
-        for chip in range(chips):
-            for side in range(2):
-                rows_ref[side, chip * block : (chip + 1) * block, :] = got_ref[
-                    chip, side, count - block :, :
-                ]
-
-    add_columns(me_ref[0] & 1, step, chips_ref, rows_ref, weights, out_ref)
+        for side in range(2):
+            for n in range(count // block):
+                for chip in range(chips):
+                    at = pl.multiple_of(((level ^ n) * chips + chip) * block, block)
+                    rows = got_ref[chip, side, n * block : (n + 1) * block, :]
+                    held[pl.ds(at, block), :] = rows.astype(jnp.float32)
+            rows_ref[side] = held[...].T.astype(jnp.bfloat16)
+
+    core = me_ref[0] & 1
+    own, mate = rows_ref[core], rows_ref[1 - core]
+    depth = half // 2
+    for n in range(weights[0].shape[0] // depth):
+        total = dot(weights[0][n * depth : (n + 1) * depth, :], own, ((1,), (0,)))
+        total += dot(weights[1][n * depth : (n + 1) * depth, :], mate, ((1,), (0,)))
+        at = chips_ref[weights[0].shape[0] // depth * step + n] * depth
+        out_ref[:, pl.ds(pl.multiple_of(at, depth), depth)] = total.T.astype(jnp.bfloat16)
 
 
 def code_rows(destination, core, per_peer, width):
@@ -276,9 +223,6 @@
 
 SCALAR = pl.BlockSpec(memory_space=pltpu.SMEM)
 PARAMS = pltpu.CompilerParams(vmem_limit_bytes=VMEM_LIMIT)
-
-
-COST = pl.CostEstimate(flops=1024, bytes_accessed=1024, transcendentals=0)
 
 
 def per_device_paired(tokens, key_cot, routes, counts, widths, key_weight):
@@ -311,17 +255,12 @@
     column = {0: piece, far: swap(piece, far), near: swap(piece, near)}
     column[both] = swap(column[far], near)
     half = piece.shape[0] // 2
-    sets, masks = [], []
-    for part in ((0, near), (far, both)):
-        pieces, places = [], []
-        for mask in part:
-            own = column[mask]
-            by_x, by_y = swap(own, X), swap(own, Y)
-            chip = len(masks) % (chips // 2)
-            masks += [mask, mask | X, mask | Y, mask | X | Y]
-            pieces += [own, by_x, by_y, swap(by_y[:half], X), swap(by_x[half:], Y)]
-            places += [(chip, 0), (chip + 1, 0), (chip + 2, 0), (chip + 3, 0), (chip + 3, half)]
-        sets.append((pieces, places))
+    pieces, places, masks = [], [], []
+    for n, (mask, own) in enumerate(sorted(column.items())):
+        by_x, by_y = swap(own, X), swap(own, Y)
+        masks += [mask, mask | X, mask | Y, mask | X | Y]
+        pieces += [own, by_x, by_y, swap(by_y[:half], X), swap(by_x[half:], Y)]
+        places += [(4 * n, 0), (4 * n + 1, 0), (4 * n + 2, 0), (4 * n + 3, 0), (4 * n + 3, half)]
     order = jnp.stack([lax.shift_right_logical(me ^ mask, 1) for mask in masks])
 
     mate_tokens = swap(after(tokens, column[near]), CORE)
@@ -350,31 +289,18 @@
     own_cot = jnp.concatenate([mine(upstream), codes], axis=0)
     mate_cot = swap(jnp.concatenate([theirs(upstream), codes], axis=0), CORE)
 
-    kept = jax.ShapeDtypeStruct((width_model // 2, half_cols), jnp.bfloat16)
-    sums = jax.ShapeDtypeStruct((2, rows, half_cols), jnp.float32)
-    (pieces, places), (last_pieces, last_places) = sets
-    first_weight, begun = pl.pallas_call(
-        functools.partial(project_kernel, places),
-        out_shape=(kept, sums),
-        in_specs=[SCALAR] + vmem(2 + len(pieces)),
+    kept = jax.ShapeDtypeStruct((width_model, half_cols), jnp.bfloat16)
+    delta, own_half = pl.pallas_call(
+        functools.partial(delta_kernel, places),
+        out_shape=(jax.ShapeDtypeStruct((2 * rows + CODE_ROWS, half_cols), jnp.bfloat16), kept),
+        in_specs=[SCALAR] * 2 + vmem(4 + len(pieces)),
         out_specs=tuple(vmem(2)),
-        compiler_params=PARAMS,
-        cost_estimate=COST,
-        name="project",
-    )(order, tokens, mate_tokens, *pieces)
-    delta, last_weight = pl.pallas_call(
-        functools.partial(delta_kernel, last_places, chips // 2),
-        out_shape=(jax.ShapeDtypeStruct((2 * rows + CODE_ROWS, half_cols), jnp.bfloat16), kept),
-        in_specs=[SCALAR] * 2 + vmem(5 + len(last_pieces)),
-        out_specs=tuple(vmem(2)),
-        scratch_shapes=[pltpu.VMEM(sums.shape, sums.dtype)],
-        compiler_params=PARAMS,
-        cost_estimate=COST,
+        scratch_shapes=[pltpu.VMEM((2, rows, half_cols), jnp.float32)],
+        compiler_params=PARAMS,
         name="delta",
-    )(order, me_scalar, tokens, mate_tokens, own_cot, mate_cot, begun, *last_pieces)
-
-    delta_far, delta_near = swap(delta, far), swap(delta, near)
-    delta_both = swap(delta_far, near)
+    )(order, me_scalar, tokens, mate_tokens, own_cot, mate_cot, *pieces)
+
+    deltas = [delta, *(swap(delta, mask) for mask in (near, far, both))]
     planes = [[z * PLANE + p for p in range(PLANE)] for z in range(levels)]
 
     def to_plane(value):
@@ -383,71 +309,46 @@
         )
         return got.reshape(PLANE // 2, 2, *value.shape[1:])
 
-    per_chip = 2 * per_peer
-    near_deltas = [delta, delta_near, delta_far]
     selected = pl.pallas_call(
         select_kernel,
-        out_shape=jax.ShapeDtypeStruct((PLANE * 3 * per_chip, half_cols), jnp.bfloat16),
-        in_specs=[SCALAR] + vmem(3),
+        out_shape=jax.ShapeDtypeStruct((PLANE * 2 * levels * per_peer, half_cols), jnp.bfloat16),
+        in_specs=[SCALAR] + vmem(levels),
         out_specs=vmem(1)[0],
         compiler_params=PARAMS,
-        cost_estimate=COST,
         name="select",
-    )(me_scalar, *near_deltas)
-    got_near = to_plane(selected.reshape(PLANE, 3 * per_chip, half_cols))
+    )(me_scalar, *deltas)
+    got = to_plane(selected.reshape(PLANE, 2 * levels * per_peer, half_cols))
 
     shard = width_model // size
     terms = pl.pallas_call(
         weight_grad_kernel,
-        out_shape=jax.ShapeDtypeStruct((PLANE, shard + per_chip, half_cols), jnp.bfloat16),
+        out_shape=jax.ShapeDtypeStruct((wide, half_cols), jnp.bfloat16),
         in_specs=[SCALAR] + vmem(2 + levels),
         out_specs=vmem(1)[0],
         scratch_shapes=[pltpu.VMEM((wide, half_cols), jnp.float32)],
         compiler_params=PARAMS,
-        cost_estimate=COST,
         name="weight_grad",
-    )(me_scalar, own_features, mate_features, *near_deltas, delta_both)
-    got = to_plane(terms)
-
-    depth = width_model // chips
-    kept_weights = [first_weight, swap(first_weight, CORE), last_weight, swap(last_weight, CORE)]
-    weight_specs = [pl.BlockSpec((depth, half_cols), lambda i, *_: (i, 0))] * len(kept_weights)
-    row_shape = jax.ShapeDtypeStruct((receive, width_model), jnp.bfloat16)
+    )(me_scalar, own_features, mate_features, after(delta, selected), *deltas[1:])
+    parts = to_plane(terms.reshape(PLANE, shard, half_cols))
+
+    depth = width_model // 4
     row_grads = pl.pallas_call(
         row_grad_kernel,
-        out_shape=row_shape,
+        out_shape=jax.ShapeDtypeStruct((receive, width_model), jnp.bfloat16),
         grid_spec=pltpu.PrefetchScalarGridSpec(
             num_scalar_prefetch=2,
-            grid=(chips // 2,),
-            in_specs=[pl.BlockSpec(got_near.shape, lambda i, *_: (0, 0, 0, 0))] + weight_specs,
+            grid=(width_model // depth,),
+            in_specs=[pl.BlockSpec(got.shape, lambda i, *_: (0, 0, 0, 0))]
+            + [pl.BlockSpec((depth, half_cols), lambda i, *_: (i, 0))] * 2,
             out_specs=pl.BlockSpec((receive, width_model), lambda i, *_: (0, 0)),
-            scratch_shapes=[pltpu.VMEM((2, receive, half_cols), jnp.bfloat16)],
+            scratch_shapes=[
+                pltpu.VMEM((2, half_cols, receive), jnp.bfloat16),
+                pltpu.VMEM((receive, half_cols), jnp.float32),
+            ],
         ),
         compiler_params=PARAMS,
-        cost_estimate=COST,
         name="row_grad",
-    )(order, me_scalar, got_near, *kept_weights)
-    count = receive // levels
-    row_grads = pl.pallas_call(
-        far_row_grad_kernel,
-        out_shape=row_shape,
-        grid_spec=pltpu.PrefetchScalarGridSpec(
-            num_scalar_prefetch=2,
-            grid=(chips // 2,),
-            in_specs=anywhere(1)
-            + [pl.BlockSpec(got.shape, lambda i, *_: (0, 0, 0, 0))]
-            + weight_specs,
-            out_specs=pl.BlockSpec(
-                (count, width_model),
-                lambda i, order, me: (lax.shift_right_logical(me[0], 3) ^ (levels - 1), 0),
-            ),
-            scratch_shapes=[pltpu.VMEM((2, count, half_cols), jnp.bfloat16)],
-        ),
-        input_output_aliases={2: 0},
-        compiler_params=PARAMS,
-        cost_estimate=COST,
-        name="far_row_grad",
-    )(order, me_scalar, row_grads, got, *kept_weights)
+    )(order, me_scalar, got, own_half, swap(own_half, CORE))
 
     key_grad = pl.pallas_call(
         functools.partial(sum_kernel, math.sqrt(rows * size)),
@@ -455,9 +356,8 @@
         in_specs=vmem(1),
         out_specs=vmem(1)[0],
         compiler_params=PARAMS,
-        cost_estimate=COST,
         name="sum",
-    )(got)
+    )(after(parts, row_grads))
     return (row_grads, key_grad)
 
 

time: 161 us -> 169 us (1.050)
  the two profiles are of different devices: /device:TPU:0 before, /device:TPU:8 now
where the time goes in v10:
time: 169 us; the launch traced here: 168 us
  waiting for transfers between devices  59.8 us (35%)
  starting transfers between devices  34.9 us (21%)
  blocking collectives  30.7 us (18%)
  Pallas kernels  19.5 us (12%)
  local copies, waits for them, and re-layouts  18.1 us (11%)
  other arithmetic  4.46 us (3%)
    ppermute x27, waiting for transfers between devices, swap(): return lax.ppermute(value, 'dp', [(i, i ^ mask) for i in range(size)])  48.7 us
    all_to_all x1, blocking collectives, per_device_paired(): lax.all_to_all(jnp.stack([tokens[:, z * wide:(z + 1) * wide] for z in ran...  30.7 us
    ppermute x27, starting transfers between devices, swap(): return lax.ppermute(value, 'dp', [(i, i ^ mask) for i in range(size)])  27.8 us
    unnamed x40, local copies, waits for them, and re-layouts  13.5 us
    all_to_all x2, waiting for transfers between devices, to_plane(): lax.all_to_all(value, 'dp', split_axis=0, concat_axis=0, axis_index_group...  11.1 us
    pallas_call x1, Pallas kernels, per_device_paired(): pl.pallas_call(row_grad_kernel, out_shape=jax.ShapeDtypeStruct((receive,...  7.14 us
    all_to_all x2, starting transfers between devices, to_plane(): lax.all_to_all(value, 'dp', split_axis=0, concat_axis=0, axis_index_group...  7.05 us
    pallas_call x1, Pallas kernels, per_device_paired(): pl.pallas_call(functools.partial(delta_kernel, places), out_shape=(jax.Sh...  5.37 us
  transfers between devices with their start and end apart: 29, of which 14 were waited for; matrix products, arithmetic and copies ran while one was open for 5% of the time, Pallas kernels for 8%

profile of v10, /device:TPU:8, one launch (start us, length us, event | category | flops | bytes accessed | tf_op | source)
XLA Modules:
  0.0 168.3 jit_solution(12017338237721369527)
XLA Ops:
  0.7 1.1 fusion.11
  2.7 3.0 %collective-permute-start.12 = (bf16[256,512]{1,0:T(8,128)(2,1)S(1)}, bf16[256,512]{1,0:T(8,128)(2,1)}, u32[]{:S(2)}, u32[]{:S(2)}) collective-permute-start(bf16[256,512]{1,0:T(8,128)(2,1)S(1)} %maximum_select_fusion.refs_0_), channel_id=1, source_target_pairs={{0,16},{1,17},{2,18},{3,19},{4,20},{5,21},{6,22},{7,23},{8,24},{9,... | collective-permute-start | bytes 786440 | tf_op jit(solution)/shard_map/ppermute | solution.py:91
  5.7 1.5 collective-permute-start.5
  7.2 1.5 collective-permute-start.4
  8.7 5.6 %collective-permute-done.1.refs_5_ = bf16[256,512]{1,0:T(8,128)(2,1)} collective-permute-done((bf16[256,512]{1,0:T(8,128)(2,1)S(1)}, bf16[256,512]{1,0:T(8,128)(2,1)}, u32[]{:S(2)}, u32[]{:S(2)}) %collective-permute-start.1) | collective-permute-done | bytes 262176 | tf_op jit(solution)/shard_map/ppermute | solution.py:91
  14.3 0.8 reduce-window.4
  15.2 0.7 select_reduce_fusion
  15.9 1.1 compare_select_fusion
  17.7 1.7 %collective-permute-start.9 = (bf16[256,512]{1,0:T(8,128)(2,1)}, bf16[256,512]{1,0:T(8,128)(2,1)S(1)}, u32[]{:S(2)}, u32[]{:S(2)}) collective-permute-start(bf16[256,512]{1,0:T(8,128)(2,1)} %collective-permute-done.1.refs_5_), channel_id=1, source_target_pairs={{0,4},{1,5},{2,6},{3,7},{4,0},{5,1},{6,2},{7,3},{8,12},{9,13},{10,... | collective-permute-start | bytes 786440 | tf_op jit(solution)/shard_map/ppermute | solution.py:91
  19.4 1.5 collective-permute-start.8
  20.9 2.6 %collective-permute-start.17 = (bf16[256,512]{1,0:T(8,128)(2,1)}, bf16[256,512]{1,0:T(8,128)(2,1)S(1)}, u32[]{:S(2)}, u32[]{:S(2)}) collective-permute-start(bf16[256,512]{1,0:T(8,128)(2,1)} %collective-permute-done.12.refs_10_), channel_id=1, source_target_pairs={{0,8},{1,9},{2,10},{3,11},{4,12},{5,13},{6,14},{7,15},{8,0},{9,1},... | collective-permute-start | bytes 786440 | tf_op jit(solution)/shard_map/ppermute | solution.py:91
  23.5 0.8 convert_reduce_fusion
  24.9 5.9 %collective-permute-done.6.refs_3_ = bf16[128,512]{1,0:T(8,128)(2,1)S(1)} collective-permute-done((bf16[128,512]{1,0:T(8,128)(2,1)S(1)}, bf16[128,512]{1,0:T(8,128)(2,1)S(1)}, u32[]{:S(2)}, u32[]{:S(2)}) %collective-permute-start.6) | collective-permute-done | bytes 131104 | tf_op jit(solution)/shard_map/ppermute | solution.py:91
  31.2 1.7 collective-permute-start.13
  32.8 1.5 collective-permute-start.19
  35.0 5.3 %collective-permute-done.14.refs_12_ = bf16[256,512]{1,0:T(8,128)(2,1)S(1)} collective-permute-done((bf16[256,512]{1,0:T(8,128)(2,1)}, bf16[256,512]{1,0:T(8,128)(2,1)S(1)}, u32[]{:S(2)}, u32[]{:S(2)}) %collective-permute-start.14) | collective-permute-done | bytes 262176 | tf_op jit(solution)/shard_map/ppermute | solution.py:91
  40.6 1.7 collective-permute-start.7
  42.3 2.6 %collective-permute-done.19.refs_17_ = bf16[256,512]{1,0:T(8,128)(2,1)S(1)} collective-permute-done((bf16[256,512]{1,0:T(8,128)(2,1)S(1)}, bf16[256,512]{1,0:T(8,128)(2,1)S(1)}, u32[]{:S(2)}, u32[]{:S(2)}) %collective-permute-start.19) | collective-permute-done | bytes 262176 | tf_op jit(solution)/shard_map/ppermute | solution.py:91
  45.0 1.5 collective-permute-start.10
  51.6 1.4 collective-permute-start.16
  53.7 1.5 collective-permute-start.20
  56.3 0.7 stack.87.chips_ref
  57.9 1.1 collective-permute-done.20.refs_18_
  59.0 2.1 %collective-permute-done.21.refs_19_ = bf16[128,512]{1,0:T(8,128)(2,1)} collective-permute-done((bf16[128,512]{1,0:T(8,128)(2,1)}, bf16[128,512]{1,0:T(8,128)(2,1)}, u32[]{:S(2)}, u32[]{:S(2)}) %collective-permute-start.21) | collective-permute-done | bytes 131104 | tf_op jit(solution)/shard_map/ppermute | solution.py:91
  61.1 0.9 copy-done.3
  62.1 0.9 copy-done.5
  63.0 0.9 copy-done.7
  64.0 0.9 copy-done.9
  64.9 0.9 copy-done.11
  65.8 0.9 copy-done.13
  66.7 0.9 copy-done.15
  67.6 0.9 copy-done.17
  69.2 5.4 %delta.1 = (bf16[272,512]{1,0:T(8,128)(2,1)S(1)}, bf16[4096,512]{1,0:T(8,128)(2,1)}) custom-call(s32[16]{0:T(128)S(1)} %copy-done.18, s32[1]{0:T(128)} %bitcast.16.me_ref, bf16[128,4096]{1,0:T(8,128)(2,1)S(1)} %copy-done.1, bf16[128,4096]{1,0:T(8,128)(2,1)} %collective-permute-done.2.mate_ref, bf16[144,512]{1,0:T(8,128)(2,1)S(1)} %get-tuple-element.29.own_cot_ref, ...), custom_call_target="tpu_custom_call" | custom-call | tf_op jit(solution)/shard_map/delta/pallas_call | solution.py:293
  74.8 30.7 %all_to_all.15.own_ref = bf16[4,128,1024]{2,1,0:T(8,128)(2,1)S(1)} all-to-all(bf16[4,128,1024]{2,1,0:T(8,128)(2,1)S(1)} %pad_maximum_fusion), channel_id=1, replica_groups={{0,8,16,24},{1,9,17,25},{2,10,18,26},{3,11,19,27},{4,12,20,28},{5,13,21..., dimensions={0} | all-to-all | bytes 2097152 | tf_op jit(solution)/shard_map/all_to_all | solution.py:268
  105.5 1.8 %collective-permute-start.22 = (bf16[272,512]{1,0:T(8,128)(2,1)S(1)}, bf16[272,512]{1,0:T(8,128)(2,1)S(1)}, u32[]{:S(2)}, u32[]{:S(2)}) collective-permute-start(bf16[272,512]{1,0:T(8,128)(2,1)S(1)} %get-tuple-element.16.refs_0_), channel_id=1, source_target_pairs={{0,8},{1,9},{2,10},{3,11},{4,12},{5,13},{6,14},{7,15},{8,0},{9,1},... | collective-permute-start | bytes 835592 | tf_op jit(solution)/shard_map/ppermute | solution.py:91
  107.5 1.5 collective-permute-start.24
  109.0 9.8 %collective-permute-done.22.refs_1_ = bf16[272,512]{1,0:T(8,128)(2,1)S(1)} collective-permute-done((bf16[272,512]{1,0:T(8,128)(2,1)S(1)}, bf16[272,512]{1,0:T(8,128)(2,1)S(1)}, u32[]{:S(2)}, u32[]{:S(2)}) %collective-permute-start.22) | collective-permute-done | bytes 278560 | tf_op jit(solution)/shard_map/ppermute | solution.py:91
  118.7 7.8 %collective-permute-done.23.refs_2_ = bf16[272,512]{1,0:T(8,128)(2,1)S(1)} collective-permute-done((bf16[272,512]{1,0:T(8,128)(2,1)S(1)}, bf16[272,512]{1,0:T(8,128)(2,1)S(1)}, u32[]{:S(2)}, u32[]{:S(2)}) %collective-permute-start.23) | collective-permute-done | bytes 278560 | tf_op jit(solution)/shard_map/ppermute | solution.py:91
  126.5 7.3 %collective-permute-done.24.refs_3_ = bf16[272,512]{1,0:T(8,128)(2,1)S(1)} collective-permute-done((bf16[272,512]{1,0:T(8,128)(2,1)S(1)}, bf16[272,512]{1,0:T(8,128)(2,1)S(1)}, u32[]{:S(2)}, u32[]{:S(2)}) %collective-permute-start.24) | collective-permute-done | bytes 278560 | tf_op jit(solution)/shard_map/ppermute | solution.py:91
  133.8 1.5 select.28
  135.3 3.5 %all-to-all-start = ((bf16[8,64,512]{2,1,0:T(8,128)(2,1)}), bf16[8,64,512]{2,1,0:T(8,128)(2,1)S(1)}, u32[]{:S(2)}, u32[]{:S(2)}) async-start(bf16[8,64,512]{2,1,0:T(8,128)(2,1)} %bitcast.22), calls=%async_computation | async-start | bytes 1048576 | tf_op jit(solution)/shard_map/all_to_all | solution.py:307
  138.8 4.6 %weight_grad.1 = bf16[1024,512]{1,0:T(8,128)(2,1)} custom-call(s32[1]{0:T(128)} %bitcast.16.me_ref, bf16[4,128,1024]{2,1,0:T(8,128)(2,1)S(1)} %all_to_all.15.own_ref, bf16[4,128,1024]{2,1,0:T(8,128)(2,1)} %collective-permute-done.26.mate_ref, bf16[272,512]{1,0:T(8,128)(2,1)S(1)} %get-tuple-element.16.refs_0_, ...), custom_call_target="tpu_custom_call" | custom-call | tf_op jit(solution)/shard_map/weight_grad/pallas_call | solution.py:323
  143.4 5.1 %all-to-all-done = bf16[8,64,512]{2,1,0:T(8,128)(2,1)S(1)} async-done(((bf16[8,64,512]{2,1,0:T(8,128)(2,1)}), bf16[8,64,512]{2,1,0:T(8,128)(2,1)S(1)}, u32[]{:S(2)}, u32[]{:S(2)}) %all-to-all-start) | async-done | bytes 524320 | tf_op jit(solution)/shard_map/all_to_all | solution.py:307
  148.5 3.6 %all-to-all-start.2 = ((bf16[8,128,512]{2,1,0:T(8,128)(2,1)}), bf16[8,128,512]{2,1,0:T(8,128)(2,1)S(1)}, u32[]{:S(2)}, u32[]{:S(2)}) async-start(bf16[8,128,512]{2,1,0:T(8,128)(2,1)} %bitcast.28), calls=%async_computation.2 | async-start | bytes 2097152 | tf_op jit(solution)/shard_map/all_to_all | solution.py:307
  152.1 2.2 %copy-done = bf16[4096,512]{1,0:T(8,128)(2,1)S(1)} copy-done((bf16[4096,512]{1,0:T(8,128)(2,1)S(1)}, bf16[4096,512]{1,0:T(8,128)(2,1)}, u32[]{:S(2)}) %copy-start) | copy-done | bytes 4194328
  154.2 7.1 %row_grad.1 = bf16[256,4096]{1,0:T(8,128)(2,1)} custom-call(s32[16]{0:T(128)S(1)} %copy-done.19, s32[1]{0:T(128)} %bitcast.16.me_ref, bf16[4,2,64,512]{3,2,1,0:T(8,128)(2,1)S(1)} %bitcast.38, bf16[4096,512]{1,0:T(8,128)(2,1)S(1)} %copy-done, bf16[4096,512]{1,0:T(8,128)(2,1)} %collective-permute-done.25.refs_1_), custom_call_target="tpu_custom_call" | custom-call | tf_op jit(solution)/shard_map/row_grad/pallas_call | solution.py:335
  161.4 6.0 %all-to-all-done.2 = bf16[8,128,512]{2,1,0:T(8,128)(2,1)S(1)} async-done(((bf16[8,128,512]{2,1,0:T(8,128)(2,1)}), bf16[8,128,512]{2,1,0:T(8,128)(2,1)S(1)}, u32[]{:S(2)}, u32[]{:S(2)}) %all-to-all-start.2) | async-done | bytes 1048608 | tf_op jit(solution)/shard_map/all_to_all | solution.py:307
  167.4 0.9 sum.1
  (82 shorter events, 12.5 us)
Async XLA Ops:
  0.6 60.5 %copy-start.1 = (bf16[128,4096]{1,0:T(8,128)(2,1)S(1)}, bf16[128,4096]{1,0:T(8,128)(2,1)}, u32[]{:S(2)}) copy-start(bf16[128,4096]{1,0:T(8,128)(2,1)} %own_ref.1) | copy-start | bytes 3145732
  0.6 1.8 %collective-permute-start = (bf16[128,1024]{1,0:T(8,128)(2,1)}, bf16[128,1024]{1,0:T(8,128)(2,1)S(1)}, u32[]{:S(2)}, u32[]{:S(2)}) collective-permute-start(bf16[128,1024]{1,0:T(8,128)(2,1)} %param.11), channel_id=1, source_target_pairs={{0,1},{1,0},{2,3},{3,2},{4,5},{5,4},{6,7},{7,6},{8,9},{9,8},{10,11... | collective-permute-start | bytes 786440 | tf_op jit(solution)/shard_map/ppermute | solution.py:91
  2.5 11.7 %collective-permute-start.1 = (bf16[256,512]{1,0:T(8,128)(2,1)S(1)}, bf16[256,512]{1,0:T(8,128)(2,1)}, u32[]{:S(2)}, u32[]{:S(2)}) collective-permute-start(bf16[256,512]{1,0:T(8,128)(2,1)S(1)} %maximum_select_fusion.refs_0_), channel_id=1, source_target_pairs={{0,8},{1,9},{2,10},{3,11},{4,12},{5,13},{6,14},{7,15},{8,0},{9,1},... | collective-permute-start | bytes 786440 | tf_op jit(solution)/shard_map/ppermute | solution.py:91
  2.7 16.7 %collective-permute-start.12 = (bf16[256,512]{1,0:T(8,128)(2,1)S(1)}, bf16[256,512]{1,0:T(8,128)(2,1)}, u32[]{:S(2)}, u32[]{:S(2)}) collective-permute-start(bf16[256,512]{1,0:T(8,128)(2,1)S(1)} %maximum_select_fusion.refs_0_), channel_id=1, source_target_pairs={{0,16},{1,17},{2,18},{3,19},{4,20},{5,21},{6,22},{7,23},{8,24},{9,... | collective-permute-start | bytes 786440 | tf_op jit(solution)/shard_map/ppermute | solution.py:91
  5.7 15.2 %collective-permute-start.5 = (bf16[256,512]{1,0:T(8,128)(2,1)S(1)}, bf16[256,512]{1,0:T(8,128)(2,1)S(1)}, u32[]{:S(2)}, u32[]{:S(2)}) collective-permute-start(bf16[256,512]{1,0:T(8,128)(2,1)S(1)} %maximum_select_fusion.refs_0_), channel_id=1, source_target_pairs={{0,4},{1,5},{2,6},{3,7},{4,0},{5,1},{6,2},{7,3},{8,12},{9,13},{10,... | collective-permute-start | bytes 786440 | tf_op jit(solution)/shard_map/ppermute | solution.py:91
  7.2 17.1 %collective-permute-start.4 = (bf16[256,512]{1,0:T(8,128)(2,1)S(1)}, bf16[256,512]{1,0:T(8,128)(2,1)S(1)}, u32[]{:S(2)}, u32[]{:S(2)}) collective-permute-start(bf16[256,512]{1,0:T(8,128)(2,1)S(1)} %maximum_select_fusion.refs_0_), channel_id=1, source_target_pairs={{0,2},{1,3},{2,0},{3,1},{4,6},{5,7},{6,4},{7,5},{8,10},{9,11},{10,... | collective-permute-start | bytes 786440 | tf_op jit(solution)/shard_map/ppermute | solution.py:91
  15.2 45.9 %collective-permute-start.2 = (bf16[128,4096]{1,0:T(8,128)(2,1)}, bf16[128,4096]{1,0:T(8,128)(2,1)}, u32[]{:S(2)}, u32[]{:S(2)}) collective-permute-start(bf16[128,4096]{1,0:T(8,128)(2,1)} %own_ref.1), channel_id=1, source_target_pairs={{0,1},{1,0},{2,3},{3,2},{4,5},{5,4},{6,7},{7,6},{8,9},{9,8},{10,11... | collective-permute-start | bytes 3145736 | tf_op jit(solution)/shard_map/ppermute | solution.py:91
  17.7 15.2 %collective-permute-start.9 = (bf16[256,512]{1,0:T(8,128)(2,1)}, bf16[256,512]{1,0:T(8,128)(2,1)S(1)}, u32[]{:S(2)}, u32[]{:S(2)}) collective-permute-start(bf16[256,512]{1,0:T(8,128)(2,1)} %collective-permute-done.1.refs_5_), channel_id=1, source_target_pairs={{0,4},{1,5},{2,6},{3,7},{4,0},{5,1},{6,2},{7,3},{8,12},{9,13},{10,... | collective-permute-start | bytes 786440 | tf_op jit(solution)/shard_map/ppermute | solution.py:91
  19.4 15.0 %collective-permute-start.8 = (bf16[256,512]{1,0:T(8,128)(2,1)}, bf16[256,512]{1,0:T(8,128)(2,1)S(1)}, u32[]{:S(2)}, u32[]{:S(2)}) collective-permute-start(bf16[256,512]{1,0:T(8,128)(2,1)} %collective-permute-done.1.refs_5_), channel_id=1, source_target_pairs={{0,2},{1,3},{2,0},{3,1},{4,6},{5,7},{6,4},{7,5},{8,10},{9,11},{10,... | collective-permute-start | bytes 786440 | tf_op jit(solution)/shard_map/ppermute | solution.py:91
  20.9 10.3 %collective-permute-start.17 = (bf16[256,512]{1,0:T(8,128)(2,1)}, bf16[256,512]{1,0:T(8,128)(2,1)S(1)}, u32[]{:S(2)}, u32[]{:S(2)}) collective-permute-start(bf16[256,512]{1,0:T(8,128)(2,1)} %collective-permute-done.12.refs_10_), channel_id=1, source_target_pairs={{0,8},{1,9},{2,10},{3,11},{4,12},{5,13},{6,14},{7,15},{8,0},{9,1},... | collective-permute-start | bytes 786440 | tf_op jit(solution)/shard_map/ppermute | solution.py:91
  24.3 6.5 %collective-permute-start.6 = (bf16[128,512]{1,0:T(8,128)(2,1)S(1)}, bf16[128,512]{1,0:T(8,128)(2,1)S(1)}, u32[]{:S(2)}, u32[]{:S(2)}) collective-permute-start(bf16[128,512]{1,0:T(8,128)(2,1)S(1)} %slice.71), channel_id=1, source_target_pairs={{0,2},{1,3},{2,0},{3,1},{4,6},{5,7},{6,4},{7,5},{8,10},{9,11},{10,... | collective-permute-start | bytes 393224 | tf_op jit(solution)/shard_map/ppermute | solution.py:91
  30.8 9.5 %collective-permute-start.14 = (bf16[256,512]{1,0:T(8,128)(2,1)}, bf16[256,512]{1,0:T(8,128)(2,1)S(1)}, u32[]{:S(2)}, u32[]{:S(2)}) collective-permute-start(bf16[256,512]{1,0:T(8,128)(2,1)} %collective-permute-done.12.refs_10_), channel_id=1, source_target_pairs={{0,4},{1,5},{2,6},{3,7},{4,0},{5,1},{6,2},{7,3},{8,12},{9,13},{10,... | collective-permute-start | bytes 786440 | tf_op jit(solution)/shard_map/ppermute | solution.py:91
  31.2 18.5 %copy-start.6 = (bf16[256,512]{1,0:T(8,128)(2,1)}, bf16[256,512]{1,0:T(8,128)(2,1)S(1)}, u32[]{:S(2)}) copy-start(bf16[256,512]{1,0:T(8,128)(2,1)S(1)} %collective-permute-done.17.refs_15_) | copy-start | bytes 786436
  31.2 9.5 %collective-permute-start.13 = (bf16[256,512]{1,0:T(8,128)(2,1)}, bf16[256,512]{1,0:T(8,128)(2,1)S(1)}, u32[]{:S(2)}, u32[]{:S(2)}) collective-permute-start(bf16[256,512]{1,0:T(8,128)(2,1)} %collective-permute-done.12.refs_10_), channel_id=1, source_target_pairs={{0,2},{1,3},{2,0},{3,1},{4,6},{5,7},{6,4},{7,5},{8,10},{9,11},{10,... | collective-permute-start | bytes 786440 | tf_op jit(solution)/shard_map/ppermute | solution.py:91
  32.8 12.2 %collective-permute-start.19 = (bf16[256,512]{1,0:T(8,128)(2,1)S(1)}, bf16[256,512]{1,0:T(8,128)(2,1)S(1)}, u32[]{:S(2)}, u32[]{:S(2)}) collective-permute-start(bf16[256,512]{1,0:T(8,128)(2,1)S(1)} %collective-permute-done.17.refs_15_), channel_id=1, source_target_pairs={{0,4},{1,5},{2,6},{3,7},{4,0},{5,1},{6,2},{7,3},{8,12},{9,13},{10,... | collective-permute-start | bytes 786440 | tf_op jit(solution)/shard_map/ppermute | solution.py:91
  34.4 12.1 %collective-permute-start.18 = (bf16[256,512]{1,0:T(8,128)(2,1)S(1)}, bf16[256,512]{1,0:T(8,128)(2,1)S(1)}, u32[]{:S(2)}, u32[]{:S(2)}) collective-permute-start(bf16[256,512]{1,0:T(8,128)(2,1)S(1)} %collective-permute-done.17.refs_15_), channel_id=1, source_target_pairs={{0,2},{1,3},{2,0},{3,1},{4,6},{5,7},{6,4},{7,5},{8,10},{9,11},{10,... | collective-permute-start | bytes 786440 | tf_op jit(solution)/shard_map/ppermute | solution.py:91
  40.3 10.7 %collective-permute-start.3 = (bf16[144,512]{1,0:T(8,128)(2,1)S(1)}, bf16[144,512]{1,0:T(8,128)(2,1)S(1)}, u32[]{:S(2)}, u32[]{:S(2)}) collective-permute-start(bf16[144,512]{1,0:T(8,128)(2,1)S(1)} %get-tuple-element.28), channel_id=1, source_target_pairs={{0,1},{1,0},{2,3},{3,2},{4,5},{5,4},{6,7},{7,6},{8,9},{9,8},{10,11... | collective-permute-start | bytes 442376 | tf_op jit(solution)/shard_map/ppermute | solution.py:91
  40.6 9.1 %collective-permute-start.7 = (bf16[128,512]{1,0:T(8,128)(2,1)S(1)}, bf16[128,512]{1,0:T(8,128)(2,1)S(1)}, u32[]{:S(2)}, u32[]{:S(2)}) collective-permute-start(bf16[128,512]{1,0:T(8,128)(2,1)S(1)} %slice.72), channel_id=1, source_target_pairs={{0,4},{1,5},{2,6},{3,7},{4,0},{5,1},{6,2},{7,3},{8,12},{9,13},{10,... | collective-permute-start | bytes 393224 | tf_op jit(solution)/shard_map/ppermute | solution.py:91
  45.0 16.1 %copy-start.2 = (bf16[256,512]{1,0:T(8,128)(2,1)}, bf16[256,512]{1,0:T(8,128)(2,1)S(1)}, u32[]{:S(2)}) copy-start(bf16[256,512]{1,0:T(8,128)(2,1)S(1)} %collective-permute-done.19.refs_17_) | copy-start | bytes 786436
  45.0 8.1 %collective-permute-start.10 = (bf16[128,512]{1,0:T(8,128)(2,1)S(1)}, bf16[128,512]{1,0:T(8,128)(2,1)S(1)}, u32[]{:S(2)}, u32[]{:S(2)}) collective-permute-start(bf16[128,512]{1,0:T(8,128)(2,1)S(1)} %slice.73), channel_id=1, source_target_pairs={{0,2},{1,3},{2,0},{3,1},{4,6},{5,7},{6,4},{7,5},{8,10},{9,11},{10,... | collective-permute-start | bytes 393224 | tf_op jit(solution)/shard_map/ppermute | solution.py:91
  46.5 2.5 %copy-start.4 = (bf16[256,512]{1,0:T(8,128)(2,1)}, bf16[256,512]{1,0:T(8,128)(2,1)S(1)}, u32[]{:S(2)}) copy-start(bf16[256,512]{1,0:T(8,128)(2,1)S(1)} %collective-permute-done.18.refs_16_) | copy-start | bytes 786436
  46.5 8.7 %collective-permute-start.11 = (bf16[128,512]{1,0:T(8,128)(2,1)S(1)}, bf16[128,512]{1,0:T(8,128)(2,1)S(1)}, u32[]{:S(2)}, u32[]{:S(2)}) collective-permute-start(bf16[128,512]{1,0:T(8,128)(2,1)S(1)} %slice.74), channel_id=1, source_target_pairs={{0,4},{1,5},{2,6},{3,7},{4,0},{5,1},{6,2},{7,3},{8,12},{9,13},{10,... | collective-permute-start | bytes 393224 | tf_op jit(solution)/shard_map/ppermute | solution.py:91
  49.7 0.7 copy-start.10
  50.3 6.7 %collective-permute-start.15 = (bf16[128,512]{1,0:T(8,128)(2,1)}, bf16[128,512]{1,0:T(8,128)(2,1)S(1)}, u32[]{:S(2)}, u32[]{:S(2)}) collective-permute-start(bf16[128,512]{1,0:T(8,128)(2,1)} %slice.75), channel_id=1, source_target_pairs={{0,2},{1,3},{2,0},{3,1},{4,6},{5,7},{6,4},{7,5},{8,10},{9,11},{10,... | collective-permute-start | bytes 393224 | tf_op jit(solution)/shard_map/ppermute | solution.py:91
  50.9 0.7 copy-start.8
  51.6 6.3 %collective-permute-start.16 = (bf16[128,512]{1,0:T(8,128)(2,1)}, bf16[128,512]{1,0:T(8,128)(2,1)}, u32[]{:S(2)}, u32[]{:S(2)}) collective-permute-start(bf16[128,512]{1,0:T(8,128)(2,1)} %slice.76), channel_id=1, source_target_pairs={{0,4},{1,5},{2,6},{3,7},{4,0},{5,1},{6,2},{7,3},{8,12},{9,13},{10,... | collective-permute-start | bytes 393224 | tf_op jit(solution)/shard_map/ppermute | solution.py:91
  53.0 0.7 copy-start.12
  53.7 5.3 %collective-permute-start.20 = (bf16[128,512]{1,0:T(8,128)(2,1)}, bf16[128,512]{1,0:T(8,128)(2,1)}, u32[]{:S(2)}, u32[]{:S(2)}) collective-permute-start(bf16[128,512]{1,0:T(8,128)(2,1)} %slice.77), channel_id=1, source_target_pairs={{0,2},{1,3},{2,0},{3,1},{4,6},{5,7},{6,4},{7,5},{8,10},{9,11},{10,... | collective-permute-start | bytes 393224 | tf_op jit(solution)/shard_map/ppermute | solution.py:91
  55.8 5.3 %collective-permute-start.21 = (bf16[128,512]{1,0:T(8,128)(2,1)}, bf16[128,512]{1,0:T(8,128)(2,1)}, u32[]{:S(2)}, u32[]{:S(2)}) collective-permute-start(bf16[128,512]{1,0:T(8,128)(2,1)} %slice.78), channel_id=1, source_target_pairs={{0,4},{1,5},{2,6},{3,7},{4,0},{5,1},{6,2},{7,3},{8,12},{9,13},{10,... | collective-permute-start | bytes 393224 | tf_op jit(solution)/shard_map/ppermute | solution.py:91
  57.0 0.7 copy-start.16
  61.1 1.0 copy-start.3
  62.1 0.9 copy-start.5
  63.0 0.9 copy-start.7
  64.0 0.9 copy-start.9
  64.9 0.9 copy-start.11
  65.8 0.9 copy-start.13
  66.7 0.9 copy-start.15
  67.6 0.9 copy-start.17
  68.5 0.7 copy-start.18
  74.6 77.5 %collective-permute-start.25 = (bf16[4096,512]{1,0:T(8,128)(2,1)}, bf16[4096,512]{1,0:T(8,128)(2,1)}, u32[]{:S(2)}, u32[]{:S(2)}) collective-permute-start(bf16[4096,512]{1,0:T(8,128)(2,1)} %get-tuple-element.15.refs_0_), channel_id=1, source_target_pairs={{0,1},{1,0},{2,3},{3,2},{4,5},{5,4},{6,7},{7,6},{8,9},{9,8},{10,11... | collective-permute-start | bytes 12582920 | tf_op jit(solution)/shard_map/ppermute | solution.py:91
  105.5 33.3 %collective-permute-start.26 = (bf16[4,128,1024]{2,1,0:T(8,128)(2,1)S(1)}, bf16[4,128,1024]{2,1,0:T(8,128)(2,1)}, u32[]{:S(2)}, u32[]{:S(2)}) collective-permute-start(bf16[4,128,1024]{2,1,0:T(8,128)(2,1)S(1)} %all_to_all.15.own_ref), channel_id=1, source_target_pairs={{0,1},{1,0},{2,3},{3,2},{4,5},{5,4},{6,7},{7,6},{8,9},{9,8},{10,11... | collective-permute-start | bytes 3145736 | tf_op jit(solution)/shard_map/ppermute | solution.py:91
  105.5 46.5 %copy-start.19 = (s32[16]{0:T(128)S(1)}, s32[16]{0:T(128)}, u32[]{:S(2)}) copy-start(s32[16]{0:T(128)} %stack.87.chips_ref) | copy-start | bytes 196
  105.5 13.2 %collective-permute-start.22 = (bf16[272,512]{1,0:T(8,128)(2,1)S(1)}, bf16[272,512]{1,0:T(8,128)(2,1)S(1)}, u32[]{:S(2)}, u32[]{:S(2)}) collective-permute-start(bf16[272,512]{1,0:T(8,128)(2,1)S(1)} %get-tuple-element.16.refs_0_), channel_id=1, source_target_pairs={{0,8},{1,9},{2,10},{3,11},{4,12},{5,13},{6,14},{7,15},{8,0},{9,1},... | collective-permute-start | bytes 835592 | tf_op jit(solution)/shard_map/ppermute | solution.py:91
  107.3 19.2 %collective-permute-start.23 = (bf16[272,512]{1,0:T(8,128)(2,1)S(1)}, bf16[272,512]{1,0:T(8,128)(2,1)S(1)}, u32[]{:S(2)}, u32[]{:S(2)}) collective-permute-start(bf16[272,512]{1,0:T(8,128)(2,1)S(1)} %get-tuple-element.16.refs_0_), channel_id=1, source_target_pairs={{0,16},{1,17},{2,18},{3,19},{4,20},{5,21},{6,22},{7,23},{8,24},{9,... | collective-permute-start | bytes 835592 | tf_op jit(solution)/shard_map/ppermute | solution.py:91
  107.5 26.3 %collective-permute-start.24 = (bf16[272,512]{1,0:T(8,128)(2,1)S(1)}, bf16[272,512]{1,0:T(8,128)(2,1)S(1)}, u32[]{:S(2)}, u32[]{:S(2)}) collective-permute-start(bf16[272,512]{1,0:T(8,128)(2,1)S(1)} %get-tuple-element.16.refs_0_), channel_id=1, source_target_pairs={{0,24},{1,25},{2,26},{3,27},{4,28},{5,29},{6,30},{7,31},{8,16},{9,... | collective-permute-start | bytes 835592 | tf_op jit(solution)/shard_map/ppermute | solution.py:91
  135.3 13.2 %all-to-all-start = ((bf16[8,64,512]{2,1,0:T(8,128)(2,1)}), bf16[8,64,512]{2,1,0:T(8,128)(2,1)S(1)}, u32[]{:S(2)}, u32[]{:S(2)}) async-start(bf16[8,64,512]{2,1,0:T(8,128)(2,1)} %bitcast.22), calls=%async_computation | async-start | bytes 1048576 | tf_op jit(solution)/shard_map/all_to_all | solution.py:307
  148.5 18.9 %all-to-all-start.2 = ((bf16[8,128,512]{2,1,0:T(8,128)(2,1)}), bf16[8,128,512]{2,1,0:T(8,128)(2,1)S(1)}, u32[]{:S(2)}, u32[]{:S(2)}) async-start(bf16[8,128,512]{2,1,0:T(8,128)(2,1)} %bitcast.28), calls=%async_computation.2 | async-start | bytes 2097152 | tf_op jit(solution)/shard_map/all_to_all | solution.py:307
  152.0 2.2 %copy-start = (bf16[4096,512]{1,0:T(8,128)(2,1)S(1)}, bf16[4096,512]{1,0:T(8,128)(2,1)}, u32[]{:S(2)}) copy-start(bf16[4096,512]{1,0:T(8,128)(2,1)} %get-tuple-element.15.refs_0_) | copy-start | bytes 12582916
  (1 other events, 0.6 us)

commit v11 on v10

--- a/solution.py
+++ b/solution.py
@@ -10,7 +10,7 @@
 
 HEAD_DIM = 128
 NSUB = 4
-VMEM_LIMIT = 48 * 1024 * 1024
+VMEM_LIMIT = 60 * 1024 * 1024
 CODE_ROWS = 16
 epsilon = 1e-06
 
@@ -84,6 +84,7 @@
 
 CORE, X, Y = 1, 2, 4
 PLANE = 8
+PLANE_MASKS = (0, X, Y, X | Y)
 
 
 def swap(value, mask):
@@ -99,18 +100,43 @@
     return lax.dot_general(a, b, (dims, ((), ())), preferred_element_type=jnp.float32)
 
 
-def delta_kernel(places, chips_ref, me_ref, own_ref, mate_ref, own_cot_ref, mate_cot_ref, *refs):
-    *pieces, delta_ref, weight_ref, acc = refs
+def fetch(pairs, sems):
+    copies = [
+        pltpu.make_async_copy(source, target, sems.at[n])
+        for n, (source, target) in enumerate(pairs)
+    ]
+    for copy in copies:
+        copy.start()
+    return copies
+
+
+def delta_kernel(chips_ref, me_ref, own_cot_ref, mate_cot_ref, own_ref, mate_ref, *refs):
+    *pieces, delta_ref, weight_ref, held, weights, acc, sems = refs
     core = me_ref[0] & 1
     rows = own_ref.shape[0]
-    chip_rows = pieces[0].shape[0]
-    for n, ((chip, first), piece_ref) in enumerate(zip(places, pieces)):
-        piece = piece_ref[...]
-        depth = piece.shape[0]
-        weight_ref[chip * chip_rows + first : chip * chip_rows + first + depth, :] = piece
-        at = pl.multiple_of(chips_ref[chip] * chip_rows + first, 128)
-        for side, ref in enumerate((own_ref, mate_ref)):
-            part = dot(ref[:, pl.ds(at, depth)], piece, ((1,), (0,)))
+    depth = pieces[0].shape[0]
+    count = len(pieces)
+
+    def rows_of(ref, n):
+        return ref.at[n * depth : (n + 1) * depth, :]
+
+    pairs = [(own_ref, held.at[0]), (mate_ref, held.at[1])]
+    pairs += [(ref, rows_of(weights, n)) for n, ref in enumerate(pieces)]
+    copies = fetch(pairs, sems)
+    for copy in copies[:2]:
+        copy.wait()
+    kept = []
+    for n in range(count):
+        copies[2 + n].wait()
+        out = pltpu.make_async_copy(
+            rows_of(weights, n), rows_of(weight_ref, n), sems.at[2 + count + n]
+        )
+        out.start()
+        kept.append(out)
+        piece = rows_of(weights, n)[...]
+        at = pl.multiple_of(chips_ref[n] * depth, depth)
+        for side in range(2):
+            part = dot(held[side, :, pl.ds(at, depth)], piece, ((1,), (0,)))
             if n == 0:
                 acc[side] = part
             else:
@@ -127,39 +153,60 @@
             delta = (upstream - normed * jnp.mean(upstream * normed, axis=1, keepdims=True)) / scale
             delta_ref[pl.ds(at, rows), cols] = delta.astype(jnp.bfloat16)
         delta_ref[2 * rows :, pl.ds(at, rows)] = cot_ref[rows:, :rows]
-
-
-def selected_rows(plane, deltas, slot_count):
-    rows = (deltas[0].shape[0] - CODE_ROWS) // 2
-    per_chip = slot_count // (PLANE * len(deltas))
-    iota = lax.broadcasted_iota(jnp.int32, (slot_count, 2 * rows), 0)
-    destination, slot = iota // (per_chip * len(deltas)), iota % (per_chip * len(deltas))
-    destination = destination + plane * PLANE
-    total = None
-    for n, delta in enumerate(deltas):
-        code = delta[2 * rows :, : 2 * rows].astype(jnp.float32).astype(jnp.int32)
-        hot = (destination == code[0:1, :]) & (slot == code[1:2, :] + n * per_chip)
-        part = dot(hot.astype(jnp.bfloat16), delta[: 2 * rows, :], ((1,), (0,)))
-        total = part if total is None else total + part
-    return total.astype(jnp.bfloat16)
+    for copy in kept:
+        copy.wait()
 
 
 def select_kernel(me_ref, *refs):
-    *deltas, sent_ref = refs
-    plane = lax.shift_right_logical(me_ref[0], 3)
-    values = [ref[...] for ref in deltas]
-    sent_ref[...] = selected_rows(plane, values, sent_ref.shape[0])
+    deltas, sent, (held, sems) = refs[:4], refs[4:8], refs[8:]
+    copies = fetch([(ref, held.at[n]) for n, ref in enumerate(deltas)], sems)
+    for copy in copies:
+        copy.wait()
+    rows = (held.shape[1] - CODE_ROWS) // 2
+    per_core = sent[0].shape[0] // 2
+    per_chip = per_core // len(deltas)
+    iota = lax.broadcasted_iota(jnp.int32, (2 * per_core, 2 * rows), 0)
+    core = (iota >= per_core).astype(jnp.int32)
+    slot = iota - core * per_core
+    for out_ref, mask in zip(sent, PLANE_MASKS):
+        total = None
+        for n in range(len(deltas)):
+            code = held[n, 2 * rows :, : 2 * rows].astype(jnp.float32).astype(jnp.int32)
+            want = code[0:1, :] - ((me_ref[0] ^ mask) & -2)
+            hot = (core == want) & (slot == code[1:2, :] + n * per_chip)
+            part = dot(hot.astype(jnp.bfloat16), held[n, : 2 * rows, :], ((1,), (0,)))
+            total = part if total is None else total + part
+        out_ref[...] = total.astype(jnp.bfloat16)
+
+
+def share_kernel(me_ref, *refs):
+    got, (keep_ref, give_ref) = refs[:4], refs[4:]
+    count = keep_ref.shape[1]
+    core = me_ref[0] & 1
+    for n, ref in enumerate(got):
+        keep_ref[n] = ref[pl.ds(pl.multiple_of(core * count, count), count), :]
+        give_ref[n] = ref[pl.ds(pl.multiple_of((1 - core) * count, count), count), :]
 
 
 def weight_grad_kernel(me_ref, own_ref, mate_ref, *refs):
-    *deltas, part_ref, acc = refs
+    *deltas, part_ref, hidden, held, acc, sems = refs
     plane = lax.shift_right_logical(me_ref[0], 3)
     core = me_ref[0] & 1
     rows = own_ref.shape[1]
-    for n, delta_ref in enumerate(deltas):
-        for side, ref in enumerate((own_ref, mate_ref)):
+    pairs = []
+    for n, ref in enumerate(deltas):
+        pairs += [
+            (own_ref.at[plane ^ n], hidden.at[n, 0]),
+            (mate_ref.at[plane ^ n], hidden.at[n, 1]),
+            (ref, held.at[n]),
+        ]
+    copies = fetch(pairs, sems)
+    for n in range(len(deltas)):
+        for copy in copies[3 * n : 3 * n + 3]:
+            copy.wait()
+        for side in range(2):
             at = pl.multiple_of((core ^ side) * rows, rows)
-            part = dot(ref[plane ^ n], delta_ref[pl.ds(at, rows), :], ((0,), (0,)))
+            part = dot(hidden[n, side], held[n, pl.ds(at, rows), :], ((0,), (0,)))
             if n + side == 0:
                 acc[...] = part
             else:
@@ -176,30 +223,30 @@
         grad_ref[:, side * half : (side + 1) * half] = total / norm
 
 
-def row_grad_kernel(chips_ref, me_ref, got_ref, *refs):
-    *weights, out_ref, rows_ref, held = refs
+def row_grad_kernel(chips_ref, me_ref, own_got_ref, mate_got_ref, *refs):
+    own_weight_ref, mate_weight_ref, out_ref, rows_ref, held = refs
     step = pl.program_id(0)
-    chips, _, count, half = got_ref.shape
-    block = held.shape[0] // (chips * 4)
+    chips, count, half = own_got_ref.shape
+    block = count // 4
     level = lax.shift_right_logical(me_ref[0], 3)
 
     @pl.when(step == 0)
     def _():
-        for side in range(2):
-            for n in range(count // block):
-                for chip in range(chips):
-                    at = pl.multiple_of(((level ^ n) * chips + chip) * block, block)
-                    rows = got_ref[chip, side, n * block : (n + 1) * block, :]
+        for side, got_ref in enumerate((own_got_ref, mate_got_ref)):
+            for chip, mask in enumerate(PLANE_MASKS):
+                place = lax.shift_right_logical((me_ref[0] ^ mask) & 6, 1)
+                for n in range(4):
+                    at = pl.multiple_of(((level ^ n) * chips + place) * block, block)
+                    rows = got_ref[chip, n * block : (n + 1) * block, :]
                     held[pl.ds(at, block), :] = rows.astype(jnp.float32)
             rows_ref[side] = held[...].T.astype(jnp.bfloat16)
 
-    core = me_ref[0] & 1
-    own, mate = rows_ref[core], rows_ref[1 - core]
     depth = half // 2
-    for n in range(weights[0].shape[0] // depth):
-        total = dot(weights[0][n * depth : (n + 1) * depth, :], own, ((1,), (0,)))
-        total += dot(weights[1][n * depth : (n + 1) * depth, :], mate, ((1,), (0,)))
-        at = chips_ref[weights[0].shape[0] // depth * step + n] * depth
+    for n in range(own_weight_ref.shape[0] // depth):
+        part = slice(n * depth, (n + 1) * depth)
+        total = dot(own_weight_ref[part, :], rows_ref[0], ((1,), (0,)))
+        total += dot(mate_weight_ref[part, :], rows_ref[1], ((1,), (0,)))
+        at = chips_ref[own_weight_ref.shape[0] // depth * step + n] * depth
         out_ref[:, pl.ds(pl.multiple_of(at, depth), depth)] = total.T.astype(jnp.bfloat16)
 
 
@@ -211,6 +258,10 @@
     earlier = jnp.sum(same.astype(jnp.int32), axis=0)
     codes = jnp.stack([destination, core * per_peer + earlier]).astype(jnp.bfloat16)
     return jnp.pad(codes, ((0, CODE_ROWS - 2), (0, width - destination.shape[0])))
+
+
+def anywhere(count):
+    return [pl.BlockSpec(memory_space=pl.ANY)] * count
 
 
 def vmem(count):
@@ -252,30 +303,35 @@
         jnp.concatenate([mate_shard[:, half_cols:], key_weight[:, half_cols:]], axis=0),
     )
     near, far, both = PLANE, 2 * PLANE, 3 * PLANE
-    column = {0: piece, far: swap(piece, far), near: swap(piece, near)}
-    column[both] = swap(column[far], near)
-    half = piece.shape[0] // 2
-    pieces, places, masks = [], [], []
-    for n, (mask, own) in enumerate(sorted(column.items())):
-        by_x, by_y = swap(own, X), swap(own, Y)
-        masks += [mask, mask | X, mask | Y, mask | X | Y]
-        pieces += [own, by_x, by_y, swap(by_y[:half], X), swap(by_x[half:], Y)]
-        places += [(4 * n, 0), (4 * n + 1, 0), (4 * n + 2, 0), (4 * n + 3, 0), (4 * n + 3, half)]
-    order = jnp.stack([lax.shift_right_logical(me ^ mask, 1) for mask in masks])
-
-    mate_tokens = swap(after(tokens, column[near]), CORE)
-    columns = [[p + PLANE * z for z in range(levels)] for p in range(PLANE)]
-    own_features = lax.all_to_all(
-        jnp.stack([tokens[:, z * wide : (z + 1) * wide] for z in range(levels)]),
-        "dp",
-        split_axis=0,
-        concat_axis=0,
-        axis_index_groups=columns,
-        tiled=True,
-    )
-    mate_features = swap(own_features, CORE)
-
-    key_cot, counts, routes = lax.optimization_barrier((key_cot, counts, routes, column[near]))[:3]
+    have = {0: piece}
+
+    def after_round(**beside):
+        names, masks = list(beside), list(have)
+        values = lax.optimization_barrier([*beside.values(), *have.values()])
+        have.update(zip(masks, values[len(names) :]))
+        return values[: len(names)]
+
+    mate_tokens = swap(tokens, CORE)
+    have.update(
+        {
+            far: swap(piece, far),
+            near: swap(piece, near),
+            X: swap(piece, X),
+            Y: swap(piece, Y),
+        }
+    )
+    mate_tokens, key_cot, counts, routes = after_round(
+        mate_tokens=mate_tokens, key_cot=key_cot, counts=counts, routes=routes
+    )
+    have.update(
+        {
+            near | X: swap(have[near], X),
+            near | Y: swap(have[near], Y),
+            far | X: swap(have[far], X),
+            far | Y: swap(have[far], Y),
+            both: swap(have[far], near),
+        }
+    )
     bounds = jnp.cumsum(counts[0])
     positions = jnp.arange(rows, dtype=jnp.int32)
     subnet = jnp.sum((positions[:, None] >= bounds[None, : NSUB - 1]).astype(jnp.int32), axis=1)
@@ -287,49 +343,117 @@
     )
     codes = code_rows(routes[:, 0], core, per_peer, half_cols)
     own_cot = jnp.concatenate([mine(upstream), codes], axis=0)
-    mate_cot = swap(jnp.concatenate([theirs(upstream), codes], axis=0), CORE)
-
+
+    late_tokens, own_cot, give_cot = after_round(
+        tokens=tokens,
+        own_cot=own_cot,
+        give_cot=jnp.concatenate([theirs(upstream), codes], axis=0),
+    )
+    columns = [[p + PLANE * z for z in range(levels)] for p in range(PLANE)]
+    own_features = lax.all_to_all(
+        jnp.stack([late_tokens[:, z * wide : (z + 1) * wide] for z in range(levels)]),
+        "dp",
+        split_axis=0,
+        concat_axis=0,
+        axis_index_groups=columns,
+        tiled=True,
+    )
+    have.update(
+        {
+            both | X: swap(have[both], X),
+            both | Y: swap(have[both], Y),
+            X | Y: swap(have[Y], X),
+            far | X | Y: swap(have[far | X], Y),
+        }
+    )
+    mate_cot = swap(give_cot, CORE)
+    mate_cot, own_cot = after_round(mate_cot=mate_cot, own_cot=own_cot)
+    have.update(
+        {
+            near | X | Y: swap(have[near | Y], X),
+            both | X | Y: swap(have[both | X], Y),
+        }
+    )
+    mate_cot, own_cot, own_features = after_round(
+        mate_cot=mate_cot, own_cot=own_cot, own_features=own_features
+    )
+    mate_features = swap(own_features, CORE)
+
+    masks = sorted(have)
+    order = jnp.stack([lax.shift_right_logical(me ^ mask, 1) for mask in masks])
     kept = jax.ShapeDtypeStruct((width_model, half_cols), jnp.bfloat16)
     delta, own_half = pl.pallas_call(
-        functools.partial(delta_kernel, places),
+        delta_kernel,
         out_shape=(jax.ShapeDtypeStruct((2 * rows + CODE_ROWS, half_cols), jnp.bfloat16), kept),
-        in_specs=[SCALAR] * 2 + vmem(4 + len(pieces)),
-        out_specs=tuple(vmem(2)),
-        scratch_shapes=[pltpu.VMEM((2, rows, half_cols), jnp.float32)],
+        in_specs=[SCALAR] * 2 + vmem(2) + anywhere(2 + len(masks)),
+        out_specs=(vmem(1)[0], anywhere(1)[0]),
+        scratch_shapes=[
+            pltpu.VMEM((2, rows, width_model), jnp.bfloat16),
+            pltpu.VMEM(kept.shape, jnp.bfloat16),
+            pltpu.VMEM((2, rows, half_cols), jnp.float32),
+            pltpu.SemaphoreType.DMA((2 + 2 * len(masks),)),
+        ],
         compiler_params=PARAMS,
         name="delta",
-    )(order, me_scalar, tokens, mate_tokens, own_cot, mate_cot, *pieces)
+    )(
+        order,
+        me_scalar,
+        own_cot,
+        mate_cot,
+        tokens,
+        mate_tokens,
+        *[have[mask] for mask in masks],
+    )
 
     deltas = [delta, *(swap(delta, mask) for mask in (near, far, both))]
-    planes = [[z * PLANE + p for p in range(PLANE)] for z in range(levels)]
-
-    def to_plane(value):
-        got = lax.all_to_all(
-            value, "dp", split_axis=0, concat_axis=0, axis_index_groups=planes, tiled=True
-        )
-        return got.reshape(PLANE // 2, 2, *value.shape[1:])
-
+    mate_half = swap(after(own_half, *deltas[1:]), CORE)
+    count = levels * 2 * per_peer
+    delta_room = pltpu.VMEM((levels, *delta.shape), jnp.bfloat16)
     selected = pl.pallas_call(
         select_kernel,
-        out_shape=jax.ShapeDtypeStruct((PLANE * 2 * levels * per_peer, half_cols), jnp.bfloat16),
-        in_specs=[SCALAR] + vmem(levels),
-        out_specs=vmem(1)[0],
+        out_shape=[jax.ShapeDtypeStruct((2 * count, half_cols), jnp.bfloat16)] * 4,
+        in_specs=[SCALAR] + anywhere(levels),
+        out_specs=vmem(4),
+        scratch_shapes=[delta_room, pltpu.SemaphoreType.DMA((levels,))],
         compiler_params=PARAMS,
         name="select",
     )(me_scalar, *deltas)
-    got = to_plane(selected.reshape(PLANE, 2 * levels * per_peer, half_cols))
-
+    got = [
+        swap(value, mask) if mask else value for value, mask in zip(selected, PLANE_MASKS)
+    ]
     shard = width_model // size
     terms = pl.pallas_call(
         weight_grad_kernel,
         out_shape=jax.ShapeDtypeStruct((wide, half_cols), jnp.bfloat16),
-        in_specs=[SCALAR] + vmem(2 + levels),
+        in_specs=[SCALAR] + anywhere(2 + levels),
         out_specs=vmem(1)[0],
-        scratch_shapes=[pltpu.VMEM((wide, half_cols), jnp.float32)],
+        scratch_shapes=[
+            pltpu.VMEM((levels, 2, rows, wide), jnp.bfloat16),
+            delta_room,
+            pltpu.VMEM((wide, half_cols), jnp.float32),
+            pltpu.SemaphoreType.DMA((3 * levels,)),
+        ],
         compiler_params=PARAMS,
         name="weight_grad",
-    )(me_scalar, own_features, mate_features, after(delta, selected), *deltas[1:])
-    parts = to_plane(terms.reshape(PLANE, shard, half_cols))
+    )(me_scalar, own_features, mate_features, after(delta, *selected), *deltas[1:])
+    parts = lax.all_to_all(
+        terms.reshape(PLANE, shard, half_cols),
+        "dp",
+        split_axis=0,
+        concat_axis=0,
+        axis_index_groups=[[z * PLANE + p for p in range(PLANE)] for z in range(levels)],
+        tiled=True,
+    ).reshape(PLANE // 2, 2, shard, half_cols)
+
+    own_got, give_got = pl.pallas_call(
+        share_kernel,
+        out_shape=[jax.ShapeDtypeStruct((4, count, half_cols), jnp.bfloat16)] * 2,
+        in_specs=[SCALAR] + vmem(4),
+        out_specs=vmem(2),
+        compiler_params=PARAMS,
+        name="share",
+    )(me_scalar, after(got[0], terms), *got[1:])
+    mate_got = swap(give_got, CORE)
 
     depth = width_model // 4
     row_grads = pl.pallas_call(
@@ -338,7 +462,7 @@
         grid_spec=pltpu.PrefetchScalarGridSpec(
             num_scalar_prefetch=2,
             grid=(width_model // depth,),
-            in_specs=[pl.BlockSpec(got.shape, lambda i, *_: (0, 0, 0, 0))]
+            in_specs=[pl.BlockSpec(own_got.shape, lambda i, *_: (0, 0, 0))] * 2
             + [pl.BlockSpec((depth, half_cols), lambda i, *_: (i, 0))] * 2,
             out_specs=pl.BlockSpec((receive, width_model), lambda i, *_: (0, 0)),
             scratch_shapes=[
@@ -348,7 +472,7 @@
         ),
         compiler_params=PARAMS,
         name="row_grad",
-    )(order, me_scalar, got, own_half, swap(own_half, CORE))
+    )(order, me_scalar, own_got, mate_got, own_half, mate_half)
 
     key_grad = pl.pallas_call(
         functools.partial(sum_kernel, math.sqrt(rows * size)),

time: 169 us -> 149 us (0.88)
  the two profiles are of different devices: /device:TPU:8 before, /device:TPU:0 now
where the time goes in v11:
time: 149 us
  waiting for transfers between devices  73.5 us (49%)
  starting transfers between devices  34.6 us (23%)
  Pallas kernels  26.1 us (18%)
  local copies, waits for them, and re-layouts  7.51 us (5%)
  other arithmetic  6.15 us (4%)
    ppermute x27, waiting for transfers between devices, swap(): return lax.ppermute(value, 'dp', [(i, i ^ mask) for i in range(size)])  71.1 us
    ppermute x27, starting transfers between devices, swap(): return lax.ppermute(value, 'dp', [(i, i ^ mask) for i in range(size)])  27.6 us
    pallas_call x1, Pallas kernels, per_device_paired(): pl.pallas_call(row_grad_kernel, out_shape=jax.ShapeDtypeStruct((receive,...  8.1 us
    pallas_call x1, Pallas kernels, per_device_paired(): pl.pallas_call(delta_kernel, out_shape=(jax.ShapeDtypeStruct((2 * rows +...  6.52 us
    unnamed x48, local copies, waits for them, and re-layouts  5.75 us
    pallas_call x1, Pallas kernels, per_device_paired(): pl.pallas_call(weight_grad_kernel, out_shape=jax.ShapeDtypeStruct((wide,...  4.76 us
    all_to_all x1, starting transfers between devices, per_device_paired(): lax.all_to_all(terms.reshape(PLANE, shard, half_cols), 'dp', split_axis=0...  3.57 us
    all_to_all x1, starting transfers between devices, per_device_paired(): lax.all_to_all(jnp.stack([late_tokens[:, z * wide:(z + 1) * wide] for z i...  3.51 us
  transfers between devices with their start and end apart: 29, of which 20 were waited for; matrix products, arithmetic and copies ran while one was open for 5% of the time, Pallas kernels for 12%

profile of v11, /device:TPU:0, one launch (start us, length us, event | category | flops | bytes accessed | tf_op | source)
XLA Modules:
  0.0 148.7 jit_solution(9276277000113393359)
XLA Ops:
  1.2 1.0 fusion.11
  2.2 1.8 %collective-permute-done.1 = bf16[128,1024]{1,0:T(8,128)(2,1)S(1)} collective-permute-done((bf16[128,1024]{1,0:T(8,128)(2,1)}, bf16[128,1024]{1,0:T(8,128)(2,1)S(1)}, u32[]{:S(2)}, u32[]{:S(2)}) %collective-permute-start.1) | collective-permute-done | bytes 262176 | tf_op jit(solution)/shard_map/ppermute | solution.py:92
  4.1 3.0 %collective-permute-start.5 = (bf16[256,512]{1,0:T(8,128)(2,1)S(1)}, bf16[256,512]{1,0:T(8,128)(2,1)S(1)}, u32[]{:S(2)}, u32[]{:S(2)}) collective-permute-start(bf16[256,512]{1,0:T(8,128)(2,1)S(1)} %maximum_select_fusion.refs_0_), channel_id=1, source_target_pairs={{0,4},{1,5},{2,6},{3,7},{4,0},{5,1},{6,2},{7,3},{8,12},{9,13},{10,... | collective-permute-start | bytes 786440 | tf_op jit(solution)/shard_map/ppermute | solution.py:92
  7.1 1.5 %collective-permute-start.4 = (bf16[256,512]{1,0:T(8,128)(2,1)S(1)}, bf16[256,512]{1,0:T(8,128)(2,1)S(1)}, u32[]{:S(2)}, u32[]{:S(2)}) collective-permute-start(bf16[256,512]{1,0:T(8,128)(2,1)S(1)} %maximum_select_fusion.refs_0_), channel_id=1, source_target_pairs={{0,2},{1,3},{2,0},{3,1},{4,6},{5,7},{6,4},{7,5},{8,10},{9,11},{10,... | collective-permute-start | bytes 786440 | tf_op jit(solution)/shard_map/ppermute | solution.py:92
  8.6 1.6 %collective-permute-start.3 = (bf16[256,512]{1,0:T(8,128)(2,1)S(1)}, bf16[256,512]{1,0:T(8,128)(2,1)S(1)}, u32[]{:S(2)}, u32[]{:S(2)}) collective-permute-start(bf16[256,512]{1,0:T(8,128)(2,1)S(1)} %maximum_select_fusion.refs_0_), channel_id=1, source_target_pairs={{0,8},{1,9},{2,10},{3,11},{4,12},{5,13},{6,14},{7,15},{8,0},{9,1},... | collective-permute-start | bytes 786440 | tf_op jit(solution)/shard_map/ppermute | solution.py:92
  10.2 2.6 %collective-permute-start.2 = (bf16[256,512]{1,0:T(8,128)(2,1)S(1)}, bf16[256,512]{1,0:T(8,128)(2,1)S(1)}, u32[]{:S(2)}, u32[]{:S(2)}) collective-permute-start(bf16[256,512]{1,0:T(8,128)(2,1)S(1)} %maximum_select_fusion.refs_0_), channel_id=1, source_target_pairs={{0,16},{1,17},{2,18},{3,19},{4,20},{5,21},{6,22},{7,23},{8,24},{9,... | collective-permute-start | bytes 786440 | tf_op jit(solution)/shard_map/ppermute | solution.py:92
  12.8 0.9 collective-permute-done.5.refs_2_
  13.7 1.5 collective-permute-done.4.refs_1_
  15.2 6.7 %collective-permute-done.3.refs_4_ = bf16[256,512]{1,0:T(8,128)(2,1)S(1)} collective-permute-done((bf16[256,512]{1,0:T(8,128)(2,1)S(1)}, bf16[256,512]{1,0:T(8,128)(2,1)S(1)}, u32[]{:S(2)}, u32[]{:S(2)}) %collective-permute-start.3) | collective-permute-done | bytes 262176 | tf_op jit(solution)/shard_map/ppermute | solution.py:92
  21.9 2.4 %collective-permute-done.2.refs_8_ = bf16[256,512]{1,0:T(8,128)(2,1)S(1)} collective-permute-done((bf16[256,512]{1,0:T(8,128)(2,1)S(1)}, bf16[256,512]{1,0:T(8,128)(2,1)S(1)}, u32[]{:S(2)}, u32[]{:S(2)}) %collective-permute-start.2) | collective-permute-done | bytes 262176 | tf_op jit(solution)/shard_map/ppermute | solution.py:92
  25.8 1.5 %collective-permute-start.9 = (bf16[256,512]{1,0:T(8,128)(2,1)S(1)}, bf16[256,512]{1,0:T(8,128)(2,1)}, u32[]{:S(2)}, u32[]{:S(2)}) collective-permute-start(bf16[256,512]{1,0:T(8,128)(2,1)S(1)} %collective-permute-done.2.refs_8_), channel_id=1, source_target_pairs={{0,4},{1,5},{2,6},{3,7},{4,0},{5,1},{6,2},{7,3},{8,12},{9,13},{10,... | collective-permute-start | bytes 786440 | tf_op jit(solution)/shard_map/ppermute | solution.py:92
  27.3 1.5 %collective-permute-start.8 = (bf16[256,512]{1,0:T(8,128)(2,1)S(1)}, bf16[256,512]{1,0:T(8,128)(2,1)}, u32[]{:S(2)}, u32[]{:S(2)}) collective-permute-start(bf16[256,512]{1,0:T(8,128)(2,1)S(1)} %collective-permute-done.2.refs_8_), channel_id=1, source_target_pairs={{0,2},{1,3},{2,0},{3,1},{4,6},{5,7},{6,4},{7,5},{8,10},{9,11},{10,... | collective-permute-start | bytes 786440 | tf_op jit(solution)/shard_map/ppermute | solution.py:92
  28.8 0.8 reduce-window.4
  30.4 0.8 convert_reduce_fusion
  31.2 0.7 select_reduce_fusion
  32.0 1.1 compare_select_fusion
  33.8 0.9 collective-permute-done.9.refs_10_
  34.7 1.2 collective-permute-done.8.refs_9_
  36.0 1.1 pad_maximum_fusion
  37.1 3.5 %all-to-all-start = ((bf16[4,128,1024]{2,1,0:T(8,128)(2,1)}), bf16[4,128,1024]{2,1,0:T(8,128)(2,1)S(1)}, u32[]{:S(2)}, u32[]{:S(2)}) async-start(bf16[4,128,1024]{2,1,0:T(8,128)(2,1)} %pad_maximum_fusion), calls=%async_computation | async-start | bytes 2097152 | tf_op jit(solution)/shard_map/all_to_all | solution.py:353
  40.7 1.6 %collective-permute-start.14 = (bf16[256,512]{1,0:T(8,128)(2,1)S(1)}, bf16[256,512]{1,0:T(8,128)(2,1)S(1)}, u32[]{:S(2)}, u32[]{:S(2)}) collective-permute-start(bf16[256,512]{1,0:T(8,128)(2,1)S(1)} %collective-permute-done.5.refs_2_), channel_id=1, source_target_pairs={{0,2},{1,3},{2,0},{3,1},{4,6},{5,7},{6,4},{7,5},{8,10},{9,11},{10,... | collective-permute-start | bytes 786440 | tf_op jit(solution)/shard_map/ppermute | solution.py:92
  42.7 1.5 %collective-permute-start.13 = (bf16[256,512]{1,0:T(8,128)(2,1)}, bf16[256,512]{1,0:T(8,128)(2,1)S(1)}, u32[]{:S(2)}, u32[]{:S(2)}) collective-permute-start(bf16[256,512]{1,0:T(8,128)(2,1)} %collective-permute-done.10.refs_12_), channel_id=1, source_target_pairs={{0,4},{1,5},{2,6},{3,7},{4,0},{5,1},{6,2},{7,3},{8,12},{9,13},{10,... | collective-permute-start | bytes 786440 | tf_op jit(solution)/shard_map/ppermute | solution.py:92
  44.8 1.6 %collective-permute-done.11.mate_cot_ref = bf16[144,512]{1,0:T(8,128)(2,1)S(1)} collective-permute-done((bf16[144,512]{1,0:T(8,128)(2,1)}, bf16[144,512]{1,0:T(8,128)(2,1)S(1)}, u32[]{:S(2)}, u32[]{:S(2)}) %collective-permute-start.11) | collective-permute-done | bytes 147488 | tf_op jit(solution)/shard_map/ppermute | solution.py:92
  46.4 2.7 %collective-permute-done.14.refs_3_ = bf16[256,512]{1,0:T(8,128)(2,1)S(1)} collective-permute-done((bf16[256,512]{1,0:T(8,128)(2,1)S(1)}, bf16[256,512]{1,0:T(8,128)(2,1)S(1)}, u32[]{:S(2)}, u32[]{:S(2)}) %collective-permute-start.14) | collective-permute-done | bytes 262176 | tf_op jit(solution)/shard_map/ppermute | solution.py:92
  50.5 0.7 copy-done.14
  51.2 2.3 %collective-permute-done.13.refs_14_ = bf16[256,512]{1,0:T(8,128)(2,1)S(1)} collective-permute-done((bf16[256,512]{1,0:T(8,128)(2,1)}, bf16[256,512]{1,0:T(8,128)(2,1)S(1)}, u32[]{:S(2)}, u32[]{:S(2)}) %collective-permute-start.13) | collective-permute-done | bytes 262176 | tf_op jit(solution)/shard_map/ppermute | solution.py:92
  54.3 0.8 collective-permute-start.17
  55.8 5.1 %collective-permute-done.16.refs_7_ = bf16[256,512]{1,0:T(8,128)(2,1)} collective-permute-done((bf16[256,512]{1,0:T(8,128)(2,1)}, bf16[256,512]{1,0:T(8,128)(2,1)}, u32[]{:S(2)}, u32[]{:S(2)}) %collective-permute-start.16) | collective-permute-done | bytes 262176 | tf_op jit(solution)/shard_map/ppermute | solution.py:92
  61.0 2.3 %all-to-all-done.own_ref = bf16[4,128,1024]{2,1,0:T(8,128)(2,1)S(1)} async-done(((bf16[4,128,1024]{2,1,0:T(8,128)(2,1)}), bf16[4,128,1024]{2,1,0:T(8,128)(2,1)S(1)}, u32[]{:S(2)}, u32[]{:S(2)}) %all-to-all-start) | async-done | bytes 1048608 | tf_op jit(solution)/shard_map/all_to_all | solution.py:353
  63.4 6.5 %delta.1 = (bf16[272,512]{1,0:T(8,128)(2,1)}, bf16[4096,512]{1,0:T(8,128)(2,1)}) custom-call(s32[16]{0:T(128)} %stack.87.chips_ref, s32[1]{0:T(128)} %bitcast.16.me_ref, bf16[144,512]{1,0:T(8,128)(2,1)} %get-tuple-element.108.own_cot_ref, bf16[144,512]{1,0:T(8,128)(2,1)} %copy-done.17, bf16[128,4096]{1,0:T(8,128)(2,1)} %own_ref.1, ...), custom_call_target="tpu_custom_call" | custom-call | tf_op jit(solution)/shard_map/delta/pallas_call | solution.py:385
  69.9 2.3 %collective-permute-start.20 = (bf16[272,512]{1,0:T(8,128)(2,1)}, bf16[272,512]{1,0:T(8,128)(2,1)S(1)}, u32[]{:S(2)}, u32[]{:S(2)}) collective-permute-start(bf16[272,512]{1,0:T(8,128)(2,1)} %get-tuple-element.133.refs_0_), channel_id=1, source_target_pairs={{0,24},{1,25},{2,26},{3,27},{4,28},{5,29},{6,30},{7,31},{8,16},{9,... | collective-permute-start | bytes 835592 | tf_op jit(solution)/shard_map/ppermute | solution.py:92
  72.2 2.2 %collective-permute-start.18 = (bf16[272,512]{1,0:T(8,128)(2,1)}, bf16[272,512]{1,0:T(8,128)(2,1)S(1)}, u32[]{:S(2)}, u32[]{:S(2)}) collective-permute-start(bf16[272,512]{1,0:T(8,128)(2,1)} %get-tuple-element.133.refs_0_), channel_id=1, source_target_pairs={{0,8},{1,9},{2,10},{3,11},{4,12},{5,13},{6,14},{7,15},{8,0},{9,1},... | collective-permute-start | bytes 835592 | tf_op jit(solution)/shard_map/ppermute | solution.py:92
  74.4 7.3 %collective-permute-done.20.refs_3_ = bf16[272,512]{1,0:T(8,128)(2,1)S(1)} collective-permute-done((bf16[272,512]{1,0:T(8,128)(2,1)}, bf16[272,512]{1,0:T(8,128)(2,1)S(1)}, u32[]{:S(2)}, u32[]{:S(2)}) %collective-permute-start.20) | collective-permute-done | bytes 278560 | tf_op jit(solution)/shard_map/ppermute | solution.py:92
  81.7 12.0 %collective-permute-done.19.refs_2_ = bf16[272,512]{1,0:T(8,128)(2,1)S(1)} collective-permute-done((bf16[272,512]{1,0:T(8,128)(2,1)}, bf16[272,512]{1,0:T(8,128)(2,1)S(1)}, u32[]{:S(2)}, u32[]{:S(2)}) %collective-permute-start.19) | collective-permute-done | bytes 278560 | tf_op jit(solution)/shard_map/ppermute | solution.py:92
  94.6 2.6 %select.28 = (bf16[128,512]{1,0:T(8,128)(2,1)}, bf16[128,512]{1,0:T(8,128)(2,1)}, bf16[128,512]{1,0:T(8,128)(2,1)}, bf16[128,512]{1,0:T(8,128)(2,1)}) custom-call(s32[1]{0:T(128)} %bitcast.16.me_ref, bf16[272,512]{1,0:T(8,128)(2,1)} %get-tuple-element.133.refs_0_, bf16[272,512]{1,0:T(8,128)(2,1)} %copy-done.5, bf16[272,512]{1,0:T(8,128)(2,1)} %copy-done.4, ...), custom_call_target="tpu_custom_call" | custom-call | tf_op jit(solution)/shard_map/select/pallas_call | solution.py:412
  97.2 4.9 %collective-permute-done.21.mate_ref = bf16[4,128,1024]{2,1,0:T(8,128)(2,1)S(1)} collective-permute-done((bf16[4,128,1024]{2,1,0:T(8,128)(2,1)S(1)}, bf16[4,128,1024]{2,1,0:T(8,128)(2,1)S(1)}, u32[]{:S(2)}, u32[]{:S(2)}) %collective-permute-start.21) | collective-permute-done | bytes 1048608 | tf_op jit(solution)/shard_map/ppermute | solution.py:92
  102.1 1.0 copy-done.6
  103.1 4.8 %weight_grad.1 = bf16[1024,512]{1,0:T(8,128)(2,1)} custom-call(s32[1]{0:T(128)} %bitcast.16.me_ref, bf16[4,128,1024]{2,1,0:T(8,128)(2,1)} %copy-done, bf16[4,128,1024]{2,1,0:T(8,128)(2,1)} %copy-done.6, bf16[272,512]{1,0:T(8,128)(2,1)} %get-tuple-element.133.refs_0_, bf16[272,512]{1,0:T(8,128)(2,1)} %copy-done.5, bf16[272,512]{1,0:T(8,128)(2,1)} %copy-done.4, ...), custom_call_target="tpu_custom_call" | custom-call | tf_op jit(solution)/shard_map/weight_grad/pallas_call | solution.py:425
  107.9 3.6 %all-to-all-start.1 = ((bf16[8,128,512]{2,1,0:T(8,128)(2,1)}), bf16[8,128,512]{2,1,0:T(8,128)(2,1)S(1)}, u32[]{:S(2)}, u32[]{:S(2)}) async-start(bf16[8,128,512]{2,1,0:T(8,128)(2,1)} %bitcast.35), calls=%async_computation.1 | async-start | bytes 2097152 | tf_op jit(solution)/shard_map/all_to_all | solution.py:439
  111.4 2.2 %collective-permute-start.22 = (bf16[128,512]{1,0:T(8,128)(2,1)S(1)}, bf16[128,512]{1,0:T(8,128)(2,1)S(1)}, u32[]{:S(2)}, u32[]{:S(2)}) collective-permute-start(bf16[128,512]{1,0:T(8,128)(2,1)S(1)} %copy-done.23), channel_id=1, source_target_pairs={{0,2},{1,3},{2,0},{3,1},{4,6},{5,7},{6,4},{7,5},{8,10},{9,11},{10,... | collective-permute-start | bytes 393224 | tf_op jit(solution)/shard_map/ppermute | solution.py:92
  113.6 1.2 collective-permute-start.23
  115.2 14.2 %collective-permute-done.22.refs_1_ = bf16[128,512]{1,0:T(8,128)(2,1)S(1)} collective-permute-done((bf16[128,512]{1,0:T(8,128)(2,1)S(1)}, bf16[128,512]{1,0:T(8,128)(2,1)S(1)}, u32[]{:S(2)}, u32[]{:S(2)}) %collective-permute-start.22) | collective-permute-done | bytes 131104 | tf_op jit(solution)/shard_map/ppermute | solution.py:92
  129.4 3.1 %collective-permute-done.24.refs_3_ = bf16[128,512]{1,0:T(8,128)(2,1)S(1)} collective-permute-done((bf16[128,512]{1,0:T(8,128)(2,1)S(1)}, bf16[128,512]{1,0:T(8,128)(2,1)S(1)}, u32[]{:S(2)}, u32[]{:S(2)}) %collective-permute-start.24) | collective-permute-done | bytes 131104 | tf_op jit(solution)/shard_map/ppermute | solution.py:92
  133.1 1.9 %share.1 = (bf16[4,64,512]{2,1,0:T(8,128)(2,1)}, bf16[4,64,512]{2,1,0:T(8,128)(2,1)}) custom-call(s32[1]{0:T(128)} %bitcast.16.me_ref, bf16[128,512]{1,0:T(8,128)(2,1)} %get-tuple-element.134.refs_0_, bf16[128,512]{1,0:T(8,128)(2,1)} %copy-done.18, bf16[128,512]{1,0:T(8,128)(2,1)} %copy-done.19, bf16[128,512]{1,0:T(8,128)(2,1)} %copy-done.20), custom_call_target="tpu_custom_call" | custom-call | tf_op jit(solution)/shard_map/share/pallas_call | solution.py:448
  135.0 1.7 %collective-permute-done.25.mate_got_ref = bf16[4,64,512]{2,1,0:T(8,128)(2,1)S(1)} collective-permute-done((bf16[4,64,512]{2,1,0:T(8,128)(2,1)}, bf16[4,64,512]{2,1,0:T(8,128)(2,1)S(1)}, u32[]{:S(2)}, u32[]{:S(2)}) %collective-permute-start.25) | collective-permute-done | bytes 262176 | tf_op jit(solution)/shard_map/ppermute | solution.py:92
  137.5 8.1 %row_grad.1 = bf16[256,4096]{1,0:T(8,128)(2,1)} custom-call(s32[16]{0:T(128)} %stack.87.chips_ref, s32[1]{0:T(128)} %bitcast.16.me_ref, bf16[4,64,512]{2,1,0:T(8,128)(2,1)} %get-tuple-element.135.own_got_ref, bf16[4,64,512]{2,1,0:T(8,128)(2,1)} %copy-done.16, bf16[4096,512]{1,0:T(8,128)(2,1)} %get-tuple-element.138.refs_0_, ...), custom_call_target="tpu_custom_call" | custom-call | tf_op jit(solution)/shard_map/row_grad/pallas_call | solution.py:459
  145.6 1.0 copy-done.1
  146.6 2.2 %sum.1 = f32[128,1024]{1,0:T(8,128)} custom-call(bf16[4,2,128,512]{3,2,1,0:T(8,128)(2,1)} %bitcast.36), custom_call_target="tpu_custom_call" | custom-call | tf_op jit(solution)/shard_map/sum/pallas_call | solution.py:477
  (82 shorter events, 10.4 us)
Async XLA Ops:
  0.6 35.3 %copy-start.2 = (bf16[128,4096]{1,0:T(8,128)(2,1)S(1)}, bf16[128,4096]{1,0:T(8,128)(2,1)}, u32[]{:S(2)}) copy-start(bf16[128,4096]{1,0:T(8,128)(2,1)} %own_ref.1) | copy-start | bytes 3145732
  0.6 23.6 %collective-permute-start = (bf16[128,4096]{1,0:T(8,128)(2,1)}, bf16[128,4096]{1,0:T(8,128)(2,1)S(1)}, u32[]{:S(2)}, u32[]{:S(2)}) collective-permute-start(bf16[128,4096]{1,0:T(8,128)(2,1)} %own_ref.1), channel_id=1, source_target_pairs={{0,1},{1,0},{2,3},{3,2},{4,5},{5,4},{6,7},{7,6},{8,9},{9,8},{10,11... | collective-permute-start | bytes 3145736 | tf_op jit(solution)/shard_map/ppermute | solution.py:92
  1.2 2.9 %collective-permute-start.1 = (bf16[128,1024]{1,0:T(8,128)(2,1)}, bf16[128,1024]{1,0:T(8,128)(2,1)S(1)}, u32[]{:S(2)}, u32[]{:S(2)}) collective-permute-start(bf16[128,1024]{1,0:T(8,128)(2,1)} %param.11), channel_id=1, source_target_pairs={{0,1},{1,0},{2,3},{3,2},{4,5},{5,4},{6,7},{7,6},{8,9},{9,8},{10,11... | collective-permute-start | bytes 786440 | tf_op jit(solution)/shard_map/ppermute | solution.py:92
  4.1 59.2 %copy-start.7 = (bf16[256,512]{1,0:T(8,128)(2,1)}, bf16[256,512]{1,0:T(8,128)(2,1)S(1)}, u32[]{:S(2)}) copy-start(bf16[256,512]{1,0:T(8,128)(2,1)S(1)} %maximum_select_fusion.refs_0_) | copy-start | bytes 786436
  4.1 9.6 %collective-permute-start.5 = (bf16[256,512]{1,0:T(8,128)(2,1)S(1)}, bf16[256,512]{1,0:T(8,128)(2,1)S(1)}, u32[]{:S(2)}, u32[]{:S(2)}) collective-permute-start(bf16[256,512]{1,0:T(8,128)(2,1)S(1)} %maximum_select_fusion.refs_0_), channel_id=1, source_target_pairs={{0,4},{1,5},{2,6},{3,7},{4,0},{5,1},{6,2},{7,3},{8,12},{9,13},{10,... | collective-permute-start | bytes 786440 | tf_op jit(solution)/shard_map/ppermute | solution.py:92
  7.1 8.1 %collective-permute-start.4 = (bf16[256,512]{1,0:T(8,128)(2,1)S(1)}, bf16[256,512]{1,0:T(8,128)(2,1)S(1)}, u32[]{:S(2)}, u32[]{:S(2)}) collective-permute-start(bf16[256,512]{1,0:T(8,128)(2,1)S(1)} %maximum_select_fusion.refs_0_), channel_id=1, source_target_pairs={{0,2},{1,3},{2,0},{3,1},{4,6},{5,7},{6,4},{7,5},{8,10},{9,11},{10,... | collective-permute-start | bytes 786440 | tf_op jit(solution)/shard_map/ppermute | solution.py:92
  8.6 13.3 %collective-permute-start.3 = (bf16[256,512]{1,0:T(8,128)(2,1)S(1)}, bf16[256,512]{1,0:T(8,128)(2,1)S(1)}, u32[]{:S(2)}, u32[]{:S(2)}) collective-permute-start(bf16[256,512]{1,0:T(8,128)(2,1)S(1)} %maximum_select_fusion.refs_0_), channel_id=1, source_target_pairs={{0,8},{1,9},{2,10},{3,11},{4,12},{5,13},{6,14},{7,15},{8,0},{9,1},... | collective-permute-start | bytes 786440 | tf_op jit(solution)/shard_map/ppermute | solution.py:92
  10.2 14.1 %collective-permute-start.2 = (bf16[256,512]{1,0:T(8,128)(2,1)S(1)}, bf16[256,512]{1,0:T(8,128)(2,1)S(1)}, u32[]{:S(2)}, u32[]{:S(2)}) collective-permute-start(bf16[256,512]{1,0:T(8,128)(2,1)S(1)} %maximum_select_fusion.refs_0_), channel_id=1, source_target_pairs={{0,16},{1,17},{2,18},{3,19},{4,20},{5,21},{6,22},{7,23},{8,24},{9,... | collective-permute-start | bytes 786440 | tf_op jit(solution)/shard_map/ppermute | solution.py:92
  13.7 49.7 %copy-start.9 = (bf16[256,512]{1,0:T(8,128)(2,1)}, bf16[256,512]{1,0:T(8,128)(2,1)S(1)}, u32[]{:S(2)}) copy-start(bf16[256,512]{1,0:T(8,128)(2,1)S(1)} %collective-permute-done.5.refs_2_) | copy-start | bytes 786436
  15.2 48.2 %copy-start.10 = (bf16[256,512]{1,0:T(8,128)(2,1)}, bf16[256,512]{1,0:T(8,128)(2,1)S(1)}, u32[]{:S(2)}) copy-start(bf16[256,512]{1,0:T(8,128)(2,1)S(1)} %collective-permute-done.4.refs_1_) | copy-start | bytes 786436
  21.9 41.5 %copy-start.11 = (bf16[256,512]{1,0:T(8,128)(2,1)}, bf16[256,512]{1,0:T(8,128)(2,1)S(1)}, u32[]{:S(2)}) copy-start(bf16[256,512]{1,0:T(8,128)(2,1)S(1)} %collective-permute-done.3.refs_4_) | copy-start | bytes 786436
  24.2 39.1 %copy-start.12 = (bf16[256,512]{1,0:T(8,128)(2,1)}, bf16[256,512]{1,0:T(8,128)(2,1)S(1)}, u32[]{:S(2)}) copy-start(bf16[256,512]{1,0:T(8,128)(2,1)S(1)} %collective-permute-done.2.refs_8_) | copy-start | bytes 786436
  24.2 39.2 %copy-start.8 = (bf16[128,4096]{1,0:T(8,128)(2,1)}, bf16[128,4096]{1,0:T(8,128)(2,1)S(1)}, u32[]{:S(2)}) copy-start(bf16[128,4096]{1,0:T(8,128)(2,1)S(1)} %collective-permute-done.mate_ref) | copy-start | bytes 3145732
  24.2 9.6 %collective-permute-start.7 = (bf16[256,512]{1,0:T(8,128)(2,1)S(1)}, bf16[256,512]{1,0:T(8,128)(2,1)}, u32[]{:S(2)}, u32[]{:S(2)}) collective-permute-start(bf16[256,512]{1,0:T(8,128)(2,1)S(1)} %collective-permute-done.3.refs_4_), channel_id=1, source_target_pairs={{0,4},{1,5},{2,6},{3,7},{4,0},{5,1},{6,2},{7,3},{8,12},{9,13},{10,... | collective-permute-start | bytes 786440 | tf_op jit(solution)/shard_map/ppermute | solution.py:92
  24.8 9.0 %collective-permute-start.6 = (bf16[256,512]{1,0:T(8,128)(2,1)S(1)}, bf16[256,512]{1,0:T(8,128)(2,1)}, u32[]{:S(2)}, u32[]{:S(2)}) collective-permute-start(bf16[256,512]{1,0:T(8,128)(2,1)S(1)} %collective-permute-done.3.refs_4_), channel_id=1, source_target_pairs={{0,2},{1,3},{2,0},{3,1},{4,6},{5,7},{6,4},{7,5},{8,10},{9,11},{10,... | collective-permute-start | bytes 786440 | tf_op jit(solution)/shard_map/ppermute | solution.py:92
  25.3 8.5 %collective-permute-start.10 = (bf16[256,512]{1,0:T(8,128)(2,1)S(1)}, bf16[256,512]{1,0:T(8,128)(2,1)}, u32[]{:S(2)}, u32[]{:S(2)}) collective-permute-start(bf16[256,512]{1,0:T(8,128)(2,1)S(1)} %collective-permute-done.2.refs_8_), channel_id=1, source_target_pairs={{0,8},{1,9},{2,10},{3,11},{4,12},{5,13},{6,14},{7,15},{8,0},{9,1},... | collective-permute-start | bytes 786440 | tf_op jit(solution)/shard_map/ppermute | solution.py:92
  25.8 8.9 %collective-permute-start.9 = (bf16[256,512]{1,0:T(8,128)(2,1)S(1)}, bf16[256,512]{1,0:T(8,128)(2,1)}, u32[]{:S(2)}, u32[]{:S(2)}) collective-permute-start(bf16[256,512]{1,0:T(8,128)(2,1)S(1)} %collective-permute-done.2.refs_8_), channel_id=1, source_target_pairs={{0,4},{1,5},{2,6},{3,7},{4,0},{5,1},{6,2},{7,3},{8,12},{9,13},{10,... | collective-permute-start | bytes 786440 | tf_op jit(solution)/shard_map/ppermute | solution.py:92
  27.3 8.6 %collective-permute-start.8 = (bf16[256,512]{1,0:T(8,128)(2,1)S(1)}, bf16[256,512]{1,0:T(8,128)(2,1)}, u32[]{:S(2)}, u32[]{:S(2)}) collective-permute-start(bf16[256,512]{1,0:T(8,128)(2,1)S(1)} %collective-permute-done.2.refs_8_), channel_id=1, source_target_pairs={{0,2},{1,3},{2,0},{3,1},{4,6},{5,7},{6,4},{7,5},{8,10},{9,11},{10,... | collective-permute-start | bytes 786440 | tf_op jit(solution)/shard_map/ppermute | solution.py:92
  37.1 26.2 %all-to-all-start = ((bf16[4,128,1024]{2,1,0:T(8,128)(2,1)}), bf16[4,128,1024]{2,1,0:T(8,128)(2,1)S(1)}, u32[]{:S(2)}, u32[]{:S(2)}) async-start(bf16[4,128,1024]{2,1,0:T(8,128)(2,1)} %pad_maximum_fusion), calls=%async_computation | async-start | bytes 2097152 | tf_op jit(solution)/shard_map/all_to_all | solution.py:353
  40.7 8.4 %collective-permute-start.14 = (bf16[256,512]{1,0:T(8,128)(2,1)S(1)}, bf16[256,512]{1,0:T(8,128)(2,1)S(1)}, u32[]{:S(2)}, u32[]{:S(2)}) collective-permute-start(bf16[256,512]{1,0:T(8,128)(2,1)S(1)} %collective-permute-done.5.refs_2_), channel_id=1, source_target_pairs={{0,2},{1,3},{2,0},{3,1},{4,6},{5,7},{6,4},{7,5},{8,10},{9,11},{10,... | collective-permute-start | bytes 786440 | tf_op jit(solution)/shard_map/ppermute | solution.py:92
  42.2 8.2 %collective-permute-start.15 = (bf16[256,512]{1,0:T(8,128)(2,1)}, bf16[256,512]{1,0:T(8,128)(2,1)S(1)}, u32[]{:S(2)}, u32[]{:S(2)}) collective-permute-start(bf16[256,512]{1,0:T(8,128)(2,1)} %collective-permute-done.8.refs_9_), channel_id=1, source_target_pairs={{0,4},{1,5},{2,6},{3,7},{4,0},{5,1},{6,2},{7,3},{8,12},{9,13},{10,... | collective-permute-start | bytes 786440 | tf_op jit(solution)/shard_map/ppermute | solution.py:92
  42.7 10.8 %collective-permute-start.13 = (bf16[256,512]{1,0:T(8,128)(2,1)}, bf16[256,512]{1,0:T(8,128)(2,1)S(1)}, u32[]{:S(2)}, u32[]{:S(2)}) collective-permute-start(bf16[256,512]{1,0:T(8,128)(2,1)} %collective-permute-done.10.refs_12_), channel_id=1, source_target_pairs={{0,4},{1,5},{2,6},{3,7},{4,0},{5,1},{6,2},{7,3},{8,12},{9,13},{10,... | collective-permute-start | bytes 786440 | tf_op jit(solution)/shard_map/ppermute | solution.py:92
  44.2 10.0 %collective-permute-start.12 = (bf16[256,512]{1,0:T(8,128)(2,1)}, bf16[256,512]{1,0:T(8,128)(2,1)}, u32[]{:S(2)}, u32[]{:S(2)}) collective-permute-start(bf16[256,512]{1,0:T(8,128)(2,1)} %collective-permute-done.10.refs_12_), channel_id=1, source_target_pairs={{0,2},{1,3},{2,0},{3,1},{4,6},{5,7},{6,4},{7,5},{8,10},{9,11},{10,... | collective-permute-start | bytes 786440 | tf_op jit(solution)/shard_map/ppermute | solution.py:92
  44.8 1.6 %collective-permute-start.11 = (bf16[144,512]{1,0:T(8,128)(2,1)}, bf16[144,512]{1,0:T(8,128)(2,1)S(1)}, u32[]{:S(2)}, u32[]{:S(2)}) collective-permute-start(bf16[144,512]{1,0:T(8,128)(2,1)} %get-tuple-element.79), channel_id=1, source_target_pairs={{0,1},{1,0},{2,3},{3,2},{4,5},{5,4},{6,7},{7,6},{8,9},{9,8},{10,11... | collective-permute-start | bytes 442376 | tf_op jit(solution)/shard_map/ppermute | solution.py:92
  46.4 17.0 %copy-start.17 = (bf16[144,512]{1,0:T(8,128)(2,1)}, bf16[144,512]{1,0:T(8,128)(2,1)S(1)}, u32[]{:S(2)}) copy-start(bf16[144,512]{1,0:T(8,128)(2,1)S(1)} %collective-permute-done.11.mate_cot_ref) | copy-start | bytes 442372
  50.4 0.7 copy-start.14
  54.2 6.7 %collective-permute-start.16 = (bf16[256,512]{1,0:T(8,128)(2,1)}, bf16[256,512]{1,0:T(8,128)(2,1)}, u32[]{:S(2)}, u32[]{:S(2)}) collective-permute-start(bf16[256,512]{1,0:T(8,128)(2,1)} %collective-permute-done.7.refs_6_), channel_id=1, source_target_pairs={{0,2},{1,3},{2,0},{3,1},{4,6},{5,7},{6,4},{7,5},{8,10},{9,11},{10,... | collective-permute-start | bytes 786440 | tf_op jit(solution)/shard_map/ppermute | solution.py:92
  54.3 6.7 %collective-permute-start.17 = (bf16[256,512]{1,0:T(8,128)(2,1)}, bf16[256,512]{1,0:T(8,128)(2,1)}, u32[]{:S(2)}, u32[]{:S(2)}) collective-permute-start(bf16[256,512]{1,0:T(8,128)(2,1)} %collective-permute-done.12.refs_13_), channel_id=1, source_target_pairs={{0,4},{1,5},{2,6},{3,7},{4,0},{5,1},{6,2},{7,3},{8,12},{9,13},{10,... | collective-permute-start | bytes 786440 | tf_op jit(solution)/shard_map/ppermute | solution.py:92
  63.4 38.8 %copy-start = (bf16[4,128,1024]{2,1,0:T(8,128)(2,1)}, bf16[4,128,1024]{2,1,0:T(8,128)(2,1)S(1)}, u32[]{:S(2)}) copy-start(bf16[4,128,1024]{2,1,0:T(8,128)(2,1)S(1)} %all-to-all-done.own_ref) | copy-start | bytes 3145732
  69.9 11.8 %collective-permute-start.20 = (bf16[272,512]{1,0:T(8,128)(2,1)}, bf16[272,512]{1,0:T(8,128)(2,1)S(1)}, u32[]{:S(2)}, u32[]{:S(2)}) collective-permute-start(bf16[272,512]{1,0:T(8,128)(2,1)} %get-tuple-element.133.refs_0_), channel_id=1, source_target_pairs={{0,24},{1,25},{2,26},{3,27},{4,28},{5,29},{6,30},{7,31},{8,16},{9,... | collective-permute-start | bytes 835592 | tf_op jit(solution)/shard_map/ppermute | solution.py:92
  72.2 21.5 %collective-permute-start.19 = (bf16[272,512]{1,0:T(8,128)(2,1)}, bf16[272,512]{1,0:T(8,128)(2,1)S(1)}, u32[]{:S(2)}, u32[]{:S(2)}) collective-permute-start(bf16[272,512]{1,0:T(8,128)(2,1)} %get-tuple-element.133.refs_0_), channel_id=1, source_target_pairs={{0,16},{1,17},{2,18},{3,19},{4,20},{5,21},{6,22},{7,23},{8,24},{9,... | collective-permute-start | bytes 835592 | tf_op jit(solution)/shard_map/ppermute | solution.py:92
  72.2 21.5 %collective-permute-start.18 = (bf16[272,512]{1,0:T(8,128)(2,1)}, bf16[272,512]{1,0:T(8,128)(2,1)S(1)}, u32[]{:S(2)}, u32[]{:S(2)}) collective-permute-start(bf16[272,512]{1,0:T(8,128)(2,1)} %get-tuple-element.133.refs_0_), channel_id=1, source_target_pairs={{0,8},{1,9},{2,10},{3,11},{4,12},{5,13},{6,14},{7,15},{8,0},{9,1},... | collective-permute-start | bytes 835592 | tf_op jit(solution)/shard_map/ppermute | solution.py:92
  81.7 12.6 %copy-start.3 = (bf16[272,512]{1,0:T(8,128)(2,1)}, bf16[272,512]{1,0:T(8,128)(2,1)S(1)}, u32[]{:S(2)}) copy-start(bf16[272,512]{1,0:T(8,128)(2,1)S(1)} %collective-permute-done.20.refs_3_) | copy-start | bytes 835588
  93.8 0.8 copy-start.5
  93.8 43.0 %collective-permute-start.26 = (bf16[4096,512]{1,0:T(8,128)(2,1)}, bf16[4096,512]{1,0:T(8,128)(2,1)}, u32[]{:S(2)}, u32[]{:S(2)}) collective-permute-start(bf16[4096,512]{1,0:T(8,128)(2,1)} %get-tuple-element.138.refs_0_), channel_id=1, source_target_pairs={{0,1},{1,0},{2,3},{3,2},{4,5},{5,4},{6,7},{7,6},{8,9},{9,8},{10,11... | collective-permute-start | bytes 12582920 | tf_op jit(solution)/shard_map/ppermute | solution.py:92
  93.8 8.3 %collective-permute-start.21 = (bf16[4,128,1024]{2,1,0:T(8,128)(2,1)S(1)}, bf16[4,128,1024]{2,1,0:T(8,128)(2,1)S(1)}, u32[]{:S(2)}, u32[]{:S(2)}) collective-permute-start(bf16[4,128,1024]{2,1,0:T(8,128)(2,1)S(1)} %all-to-all-done.own_ref), channel_id=1, source_target_pairs={{0,1},{1,0},{2,3},{3,2},{4,5},{5,4},{6,7},{7,6},{8,9},{9,8},{10,11... | collective-permute-start | bytes 3145736 | tf_op jit(solution)/shard_map/ppermute | solution.py:92
  97.2 14.3 %copy-start.23 = (bf16[128,512]{1,0:T(8,128)(2,1)S(1)}, bf16[128,512]{1,0:T(8,128)(2,1)}, u32[]{:S(2)}) copy-start(bf16[128,512]{1,0:T(8,128)(2,1)} %get-tuple-element.130) | copy-start | bytes 393220
  97.2 16.4 %copy-start.22 = (bf16[128,512]{1,0:T(8,128)(2,1)S(1)}, bf16[128,512]{1,0:T(8,128)(2,1)}, u32[]{:S(2)}) copy-start(bf16[128,512]{1,0:T(8,128)(2,1)} %get-tuple-element.131) | copy-start | bytes 393220
  97.2 17.7 %copy-start.21 = (bf16[128,512]{1,0:T(8,128)(2,1)S(1)}, bf16[128,512]{1,0:T(8,128)(2,1)}, u32[]{:S(2)}) copy-start(bf16[128,512]{1,0:T(8,128)(2,1)} %get-tuple-element.132) | copy-start | bytes 393220
  102.1 1.0 copy-start.6
  107.9 37.7 %all-to-all-start.1 = ((bf16[8,128,512]{2,1,0:T(8,128)(2,1)}), bf16[8,128,512]{2,1,0:T(8,128)(2,1)S(1)}, u32[]{:S(2)}, u32[]{:S(2)}) async-start(bf16[8,128,512]{2,1,0:T(8,128)(2,1)} %bitcast.35), calls=%async_computation.1 | async-start | bytes 2097152 | tf_op jit(solution)/shard_map/all_to_all | solution.py:439
  111.4 17.9 %collective-permute-start.22 = (bf16[128,512]{1,0:T(8,128)(2,1)S(1)}, bf16[128,512]{1,0:T(8,128)(2,1)S(1)}, u32[]{:S(2)}, u32[]{:S(2)}) collective-permute-start(bf16[128,512]{1,0:T(8,128)(2,1)S(1)} %copy-done.23), channel_id=1, source_target_pairs={{0,2},{1,3},{2,0},{3,1},{4,6},{5,7},{6,4},{7,5},{8,10},{9,11},{10,... | collective-permute-start | bytes 393224 | tf_op jit(solution)/shard_map/ppermute | solution.py:92
  113.6 15.7 %collective-permute-start.23 = (bf16[128,512]{1,0:T(8,128)(2,1)S(1)}, bf16[128,512]{1,0:T(8,128)(2,1)S(1)}, u32[]{:S(2)}, u32[]{:S(2)}) collective-permute-start(bf16[128,512]{1,0:T(8,128)(2,1)S(1)} %copy-done.22), channel_id=1, source_target_pairs={{0,4},{1,5},{2,6},{3,7},{4,0},{5,1},{6,2},{7,3},{8,12},{9,13},{10,... | collective-permute-start | bytes 393224 | tf_op jit(solution)/shard_map/ppermute | solution.py:92
  114.9 17.6 %collective-permute-start.24 = (bf16[128,512]{1,0:T(8,128)(2,1)S(1)}, bf16[128,512]{1,0:T(8,128)(2,1)S(1)}, u32[]{:S(2)}, u32[]{:S(2)}) collective-permute-start(bf16[128,512]{1,0:T(8,128)(2,1)S(1)} %copy-done.21), channel_id=1, source_target_pairs={{0,6},{1,7},{2,4},{3,5},{4,2},{5,3},{6,0},{7,1},{8,14},{9,15},{10,... | collective-permute-start | bytes 393224 | tf_op jit(solution)/shard_map/ppermute | solution.py:92
  129.3 3.1 %copy-start.18 = (bf16[128,512]{1,0:T(8,128)(2,1)}, bf16[128,512]{1,0:T(8,128)(2,1)S(1)}, u32[]{:S(2)}) copy-start(bf16[128,512]{1,0:T(8,128)(2,1)S(1)} %collective-permute-done.22.refs_1_) | copy-start | bytes 393220
  129.4 3.1 %copy-start.19 = (bf16[128,512]{1,0:T(8,128)(2,1)}, bf16[128,512]{1,0:T(8,128)(2,1)S(1)}, u32[]{:S(2)}) copy-start(bf16[128,512]{1,0:T(8,128)(2,1)S(1)} %collective-permute-done.23.refs_2_) | copy-start | bytes 393220
  135.0 1.7 %collective-permute-start.25 = (bf16[4,64,512]{2,1,0:T(8,128)(2,1)}, bf16[4,64,512]{2,1,0:T(8,128)(2,1)S(1)}, u32[]{:S(2)}, u32[]{:S(2)}) collective-permute-start(bf16[4,64,512]{2,1,0:T(8,128)(2,1)} %get-tuple-element.136), channel_id=1, source_target_pairs={{0,1},{1,0},{2,3},{3,2},{4,5},{5,4},{6,7},{7,6},{8,9},{9,8},{10,11... | collective-permute-start | bytes 786440 | tf_op jit(solution)/shard_map/ppermute | solution.py:92
  145.6 1.0 copy-start.1
  (5 other events, 3.5 us)

commit v12 on v11

--- a/solution.py
+++ b/solution.py
@@ -110,37 +110,57 @@
     return copies
 
 
-def delta_kernel(chips_ref, me_ref, own_cot_ref, mate_cot_ref, own_ref, mate_ref, *refs):
-    *pieces, delta_ref, weight_ref, held, weights, acc, sems = refs
-    core = me_ref[0] & 1
-    rows = own_ref.shape[0]
+def project_kernel(begin, chips_ref, own_ref, mate_ref, *refs):
+    begun = None
+    if begin:
+        begun, *refs = refs
+    *pieces, weight_ref, acc, held, weights, sems = refs
     depth = pieces[0].shape[0]
     count = len(pieces)
 
     def rows_of(ref, n):
         return ref.at[n * depth : (n + 1) * depth, :]
 
-    pairs = [(own_ref, held.at[0]), (mate_ref, held.at[1])]
-    pairs += [(ref, rows_of(weights, n)) for n, ref in enumerate(pieces)]
+    pairs = []
+    for n, ref in enumerate(pieces):
+        at = pl.multiple_of(chips_ref[begin + n] * depth, depth)
+        pairs += [
+            (ref, rows_of(weights, n)),
+            (own_ref.at[:, pl.ds(at, depth)], held.at[n, 0]),
+            (mate_ref.at[:, pl.ds(at, depth)], held.at[n, 1]),
+        ]
     copies = fetch(pairs, sems)
-    for copy in copies[:2]:
-        copy.wait()
+    if begin:
+        acc[...] = begun[...]
     kept = []
     for n in range(count):
-        copies[2 + n].wait()
+        for copy in copies[3 * n : 3 * n + 3]:
+            copy.wait()
         out = pltpu.make_async_copy(
-            rows_of(weights, n), rows_of(weight_ref, n), sems.at[2 + count + n]
+            rows_of(weights, n), rows_of(weight_ref, n), sems.at[3 * count + n]
         )
         out.start()
         kept.append(out)
         piece = rows_of(weights, n)[...]
-        at = pl.multiple_of(chips_ref[n] * depth, depth)
         for side in range(2):
-            part = dot(held[side, :, pl.ds(at, depth)], piece, ((1,), (0,)))
-            if n == 0:
+            part = dot(held[n, side], piece, ((1,), (0,)))
+            if begin + n == 0:
                 acc[side] = part
             else:
                 acc[side] += part
+    return kept
+
+
+def first_project_kernel(*refs):
+    for copy in project_kernel(0, *refs):
+        copy.wait()
+
+
+def delta_kernel(begin, chips_ref, me_ref, own_cot_ref, mate_cot_ref, *refs):
+    *refs, delta_ref, weight_ref, acc, held, weights, sems = refs
+    kept = project_kernel(begin, chips_ref, *refs, weight_ref, acc, held, weights, sems)
+    core = me_ref[0] & 1
+    rows = acc.shape[1]
     delta_ref[2 * rows :, :] = jnp.zeros_like(delta_ref[2 * rows :, :])
     for side, cot_ref in enumerate((own_cot_ref, mate_cot_ref)):
         at = pl.multiple_of((core ^ side) * rows, rows)
@@ -195,36 +215,41 @@
     rows = own_ref.shape[1]
     pairs = []
     for n, ref in enumerate(deltas):
+        own = pl.multiple_of((2 * n + core) * rows, rows)
+        mate = pl.multiple_of((2 * n + 1 - core) * rows, rows)
         pairs += [
-            (own_ref.at[plane ^ n], hidden.at[n, 0]),
-            (mate_ref.at[plane ^ n], hidden.at[n, 1]),
-            (ref, held.at[n]),
+            (own_ref.at[plane ^ n], hidden.at[pl.ds(own, rows), :]),
+            (mate_ref.at[plane ^ n], hidden.at[pl.ds(mate, rows), :]),
+            (ref.at[: 2 * rows, :], held.at[2 * n * rows : 2 * (n + 1) * rows, :]),
         ]
     copies = fetch(pairs, sems)
-    for n in range(len(deltas)):
-        for copy in copies[3 * n : 3 * n + 3]:
+    for first in (0, 2):
+        for copy in copies[3 * first : 3 * first + 6]:
             copy.wait()
-        for side in range(2):
-            at = pl.multiple_of((core ^ side) * rows, rows)
-            part = dot(hidden[n, side], held[n, pl.ds(at, rows), :], ((0,), (0,)))
-            if n + side == 0:
-                acc[...] = part
-            else:
-                acc[...] += part
-    part_ref[...] = acc[...].astype(jnp.bfloat16)
-
-
-def sum_kernel(norm, parts_ref, grad_ref):
-    half = parts_ref.shape[3]
+        part = slice(2 * first * rows, 2 * (first + 2) * rows)
+        terms = dot(hidden[part, :], held[part, :], ((0,), (0,)))
+        if first == 0:
+            acc[...] = terms
+        else:
+            part_ref[...] = (acc[...] + terms).astype(jnp.bfloat16)
+
+
+def sum_kernel(norm, parts_ref, grad_ref, held, sems):
+    chips, _, _, half = parts_ref.shape
+    copies = fetch(
+        [(parts_ref.at[n // 2, n % 2], held.at[n]) for n in range(2 * chips)], sems
+    )
+    for copy in copies:
+        copy.wait()
     for side in range(2):
-        total = parts_ref[0, side].astype(jnp.float32)
-        for chip in range(1, parts_ref.shape[0]):
-            total += parts_ref[chip, side].astype(jnp.float32)
+        total = held[side].astype(jnp.float32)
+        for chip in range(1, chips):
+            total += held[2 * chip + side].astype(jnp.float32)
         grad_ref[:, side * half : (side + 1) * half] = total / norm
 
 
 def row_grad_kernel(chips_ref, me_ref, own_got_ref, mate_got_ref, *refs):
-    own_weight_ref, mate_weight_ref, out_ref, rows_ref, held = refs
+    *weights, out_ref, rows_ref, held = refs
     step = pl.program_id(0)
     chips, count, half = own_got_ref.shape
     block = count // 4
@@ -242,12 +267,21 @@
             rows_ref[side] = held[...].T.astype(jnp.bfloat16)
 
     depth = half // 2
-    for n in range(own_weight_ref.shape[0] // depth):
-        part = slice(n * depth, (n + 1) * depth)
-        total = dot(own_weight_ref[part, :], rows_ref[0], ((1,), (0,)))
-        total += dot(mate_weight_ref[part, :], rows_ref[1], ((1,), (0,)))
-        at = chips_ref[own_weight_ref.shape[0] // depth * step + n] * depth
-        out_ref[:, pl.ds(pl.multiple_of(at, depth), depth)] = total.T.astype(jnp.bfloat16)
+
+    def add(own_ref, mate_ref, begin):
+        for n in range(own_ref.shape[0] // depth):
+            part = slice(n * depth, (n + 1) * depth)
+            total = dot(own_ref[part, :], rows_ref[0], ((1,), (0,)))
+            total += dot(mate_ref[part, :], rows_ref[1], ((1,), (0,)))
+            at = pl.multiple_of(chips_ref[begin + n] * depth, depth)
+            out_ref[:, pl.ds(at, depth)] = total.T.astype(jnp.bfloat16)
+
+    per_step = weights[0].shape[0] // depth
+    add(*weights[:2], step * per_step)
+
+    @pl.when(step == pl.num_programs(0) - 1)
+    def _():
+        add(*weights[2:], pl.num_programs(0) * per_step)
 
 
 def code_rows(destination, core, per_peer, width):
@@ -311,13 +345,13 @@
         have.update(zip(masks, values[len(names) :]))
         return values[: len(names)]
 
-    mate_tokens = swap(tokens, CORE)
+    mate_tokens = swap(after(tokens, mate_shard), CORE)
     have.update(
         {
+            Y: swap(piece, Y),
+            X: swap(piece, X),
+            near: swap(piece, near),
             far: swap(piece, far),
-            near: swap(piece, near),
-            X: swap(piece, X),
-            Y: swap(piece, Y),
         }
     )
     mate_tokens, key_cot, counts, routes = after_round(
@@ -368,45 +402,75 @@
     )
     mate_cot = swap(give_cot, CORE)
     mate_cot, own_cot = after_round(mate_cot=mate_cot, own_cot=own_cot)
+    first_masks = list(have)
+    last_masks = [near | X | Y, both | X | Y]
+    order = jnp.stack([lax.shift_right_logical(me ^ mask, 1) for mask in first_masks + last_masks])
+    depth = width_model // chips
+    sums = jax.ShapeDtypeStruct((2, rows, half_cols), jnp.float32)
+
+    def project(kernel, count, results, inputs, specs, name):
+        return pl.pallas_call(
+            kernel,
+            out_shape=(*results, jax.ShapeDtypeStruct((count * depth, half_cols), jnp.bfloat16))
+            + ((sums,) if name == "project" else ()),
+            in_specs=specs + anywhere(count),
+            out_specs=(*vmem(len(results)), anywhere(1)[0])
+            + (tuple(vmem(1)) if name == "project" else ()),
+            scratch_shapes=([] if name == "project" else [pltpu.VMEM(sums.shape, sums.dtype)])
+            + [
+                pltpu.VMEM((count, 2, rows, depth), jnp.bfloat16),
+                pltpu.VMEM((count * depth, half_cols), jnp.bfloat16),
+                pltpu.SemaphoreType.DMA((4 * count,)),
+            ],
+            compiler_params=PARAMS,
+            name=name,
+        )(*inputs)
+
+    first_weight, begun = project(
+        first_project_kernel,
+        len(first_masks),
+        (),
+        (order, tokens, mate_tokens, *[have[mask] for mask in first_masks]),
+        [SCALAR] + anywhere(2),
+        "project",
+    )
     have.update(
         {
             near | X | Y: swap(have[near | Y], X),
             both | X | Y: swap(have[both | X], Y),
         }
     )
-    mate_cot, own_cot, own_features = after_round(
-        mate_cot=mate_cot, own_cot=own_cot, own_features=own_features
+    mate_cot, own_cot, own_features, begun, first_weight = after_round(
+        mate_cot=mate_cot,
+        own_cot=own_cot,
+        own_features=own_features,
+        begun=begun,
+        first_weight=first_weight,
     )
     mate_features = swap(own_features, CORE)
-
-    masks = sorted(have)
-    order = jnp.stack([lax.shift_right_logical(me ^ mask, 1) for mask in masks])
-    kept = jax.ShapeDtypeStruct((width_model, half_cols), jnp.bfloat16)
-    delta, own_half = pl.pallas_call(
-        delta_kernel,
-        out_shape=(jax.ShapeDtypeStruct((2 * rows + CODE_ROWS, half_cols), jnp.bfloat16), kept),
-        in_specs=[SCALAR] * 2 + vmem(2) + anywhere(2 + len(masks)),
-        out_specs=(vmem(1)[0], anywhere(1)[0]),
-        scratch_shapes=[
-            pltpu.VMEM((2, rows, width_model), jnp.bfloat16),
-            pltpu.VMEM(kept.shape, jnp.bfloat16),
-            pltpu.VMEM((2, rows, half_cols), jnp.float32),
-            pltpu.SemaphoreType.DMA((2 + 2 * len(masks),)),
-        ],
-        compiler_params=PARAMS,
-        name="delta",
-    )(
-        order,
-        me_scalar,
-        own_cot,
-        mate_cot,
-        tokens,
-        mate_tokens,
-        *[have[mask] for mask in masks],
+    delta, last_weight = project(
+        functools.partial(delta_kernel, len(first_masks)),
+        len(last_masks),
+        (jax.ShapeDtypeStruct((2 * rows + CODE_ROWS, half_cols), jnp.bfloat16),),
+        (
+            order,
+            me_scalar,
+            own_cot,
+            mate_cot,
+            tokens,
+            mate_tokens,
+            begun,
+            *[have[mask] for mask in last_masks],
+        ),
+        [SCALAR] * 2 + vmem(2) + anywhere(2) + vmem(1),
+        "delta",
     )
 
     deltas = [delta, *(swap(delta, mask) for mask in (near, far, both))]
-    mate_half = swap(after(own_half, *deltas[1:]), CORE)
+    mate_features, first_weight, last_weight, *deltas[1:] = lax.optimization_barrier(
+        (mate_features, first_weight, last_weight, *deltas[1:])
+    )
+    mate_first, mate_last = swap(first_weight, CORE), swap(last_weight, CORE)
     count = levels * 2 * per_peer
     delta_room = pltpu.VMEM((levels, *delta.shape), jnp.bfloat16)
     selected = pl.pallas_call(
@@ -428,8 +492,8 @@
         in_specs=[SCALAR] + anywhere(2 + levels),
         out_specs=vmem(1)[0],
         scratch_shapes=[
-            pltpu.VMEM((levels, 2, rows, wide), jnp.bfloat16),
-            delta_room,
+            pltpu.VMEM((levels * 2 * rows, wide), jnp.bfloat16),
+            pltpu.VMEM((levels * 2 * rows, half_cols), jnp.bfloat16),
             pltpu.VMEM((wide, half_cols), jnp.float32),
             pltpu.SemaphoreType.DMA((3 * levels,)),
         ],
@@ -437,7 +501,7 @@
         name="weight_grad",
     )(me_scalar, own_features, mate_features, after(delta, *selected), *deltas[1:])
     parts = lax.all_to_all(
-        terms.reshape(PLANE, shard, half_cols),
+        after(terms, *got).reshape(PLANE, shard, half_cols),
         "dp",
         split_axis=0,
         concat_axis=0,
@@ -452,18 +516,19 @@
         out_specs=vmem(2),
         compiler_params=PARAMS,
         name="share",
-    )(me_scalar, after(got[0], terms), *got[1:])
+    )(me_scalar, *got)
     mate_got = swap(give_got, CORE)
 
-    depth = width_model // 4
+    block, last_rows = (2 * depth, half_cols), (len(last_masks) * depth, half_cols)
     row_grads = pl.pallas_call(
         row_grad_kernel,
         out_shape=jax.ShapeDtypeStruct((receive, width_model), jnp.bfloat16),
         grid_spec=pltpu.PrefetchScalarGridSpec(
             num_scalar_prefetch=2,
-            grid=(width_model // depth,),
+            grid=(len(first_masks) // 2,),
             in_specs=[pl.BlockSpec(own_got.shape, lambda i, *_: (0, 0, 0))] * 2
-            + [pl.BlockSpec((depth, half_cols), lambda i, *_: (i, 0))] * 2,
+            + [pl.BlockSpec(block, lambda i, *_: (i, 0))] * 2
+            + [pl.BlockSpec(last_rows, lambda i, *_: (0, 0))] * 2,
             out_specs=pl.BlockSpec((receive, width_model), lambda i, *_: (0, 0)),
             scratch_shapes=[
                 pltpu.VMEM((2, half_cols, receive), jnp.bfloat16),
@@ -472,13 +537,17 @@
         ),
         compiler_params=PARAMS,
         name="row_grad",
-    )(order, me_scalar, own_got, mate_got, own_half, mate_half)
+    )(order, me_scalar, own_got, mate_got, first_weight, mate_first, last_weight, mate_last)
 
     key_grad = pl.pallas_call(
         functools.partial(sum_kernel, math.sqrt(rows * size)),
         out_shape=jax.ShapeDtypeStruct((shard, cols), jnp.float32),
-        in_specs=vmem(1),
+        in_specs=anywhere(1),
         out_specs=vmem(1)[0],
+        scratch_shapes=[
+            pltpu.VMEM((PLANE, shard, half_cols), jnp.bfloat16),
+            pltpu.SemaphoreType.DMA((PLANE,)),
+        ],
         compiler_params=PARAMS,
         name="sum",
     )(after(parts, row_grads))

time: 149 us -> 132 us (0.89)
  waiting for transfers between devices: 73.5 us -> 50.8 us
  Pallas kernels: 26.1 us -> 31.3 us
  local copies, waits for them, and re-layouts: 7.51 us -> 4.44 us
  starting transfers between devices: 34.6 us -> 37.6 us
    ppermute x27 -> x28, waiting for transfers between devices: 71.1 us -> 47.9 us  [swap(): return lax.ppermute(value, 'dp', [(i, i ^ mask) for i in range(size)])]
    pallas_call x1 -> x2, Pallas kernels: 6.52 us -> 10.2 us  [project(): pl.pallas_call(kernel, out_shape=(*results, jax.ShapeDtypeStruct((count *...]
    unnamed x48 -> x52, local copies, waits for them, and re-layouts: 5.75 us -> 2.64 us
    pallas_call x1, Pallas kernels: 8.1 us -> 10.3 us  [per_device_paired(): pl.pallas_call(row_grad_kernel, out_shape=jax.ShapeDtypeStruct((receive,...]
    all_to_all x1, starting transfers between devices: 3.51 us -> 5.22 us  [per_device_paired(): lax.all_to_all(jnp.stack([late_tokens[:, z * wide:(z + 1) * wide] for z i...]
    ppermute x27 -> x28, starting transfers between devices: 27.6 us -> 28.8 us  [swap(): return lax.ppermute(value, 'dp', [(i, i ^ mask) for i in range(size)])]
  transfers between devices with their start and end apart: 29 -> 30, of which waited for: 20 -> 15; matrix products, arithmetic and copies ran while one was open for 5% -> 5% of each run, Pallas kernels for 12% -> 22%
where the time goes in v12:
time: 132 us; the launch traced here: 131 us
  waiting for transfers between devices  50.8 us (38%)
  starting transfers between devices  37.6 us (28%)
  Pallas kernels  31.3 us (24%)
  other arithmetic  6.1 us (5%)
  local copies, waits for them, and re-layouts  4.44 us (3%)
    ppermute x28, waiting for transfers between devices, swap(): return lax.ppermute(value, 'dp', [(i, i ^ mask) for i in range(size)])  47.9 us
    ppermute x28, starting transfers between devices, swap(): return lax.ppermute(value, 'dp', [(i, i ^ mask) for i in range(size)])  28.8 us
    pallas_call x1, Pallas kernels, per_device_paired(): pl.pallas_call(row_grad_kernel, out_shape=jax.ShapeDtypeStruct((receive,...  10.3 us
    pallas_call x2, Pallas kernels, project(): pl.pallas_call(kernel, out_shape=(*results, jax.ShapeDtypeStruct((count *...  10.2 us
    all_to_all x1, starting transfers between devices, per_device_paired(): lax.all_to_all(jnp.stack([late_tokens[:, z * wide:(z + 1) * wide] for z i...  5.22 us
    pallas_call x1, Pallas kernels, per_device_paired(): pl.pallas_call(weight_grad_kernel, out_shape=jax.ShapeDtypeStruct((wide,...  3.87 us
    all_to_all x1, starting transfers between devices, per_device_paired(): lax.all_to_all(after(terms, *got).reshape(PLANE, shard, half_cols), 'dp',...  3.56 us
    all_to_all x1, waiting for transfers between devices, per_device_paired(): lax.all_to_all(jnp.stack([late_tokens[:, z * wide:(z + 1) * wide] for z i...  2.87 us
  transfers between devices with their start and end apart: 30, of which 15 were waited for; matrix products, arithmetic and copies ran while one was open for 5% of the time, Pallas kernels for 22%

profile of v12, /device:TPU:0, one launch (start us, length us, event | category | flops | bytes accessed | tf_op | source)
XLA Modules:
  0.0 131.1 jit_solution(9785183564092661609)
XLA Ops:
  1.2 1.4 %collective-permute-done = bf16[128,1024]{1,0:T(8,128)(2,1)S(1)} collective-permute-done((bf16[128,1024]{1,0:T(8,128)(2,1)}, bf16[128,1024]{1,0:T(8,128)(2,1)S(1)}, u32[]{:S(2)}, u32[]{:S(2)}) %collective-permute-start) | collective-permute-done | bytes 262176 | tf_op jit(solution)/shard_map/ppermute | solution.py:92
  2.9 1.0 fusion.11
  4.0 3.8 %collective-permute-start.5 = (bf16[256,512]{1,0:T(8,128)(2,1)S(1)}, bf16[256,512]{1,0:T(8,128)(2,1)S(1)}, u32[]{:S(2)}, u32[]{:S(2)}) collective-permute-start(bf16[256,512]{1,0:T(8,128)(2,1)S(1)} %maximum_select_fusion.refs_3_), channel_id=1, source_target_pairs={{0,16},{1,17},{2,18},{3,19},{4,20},{5,21},{6,22},{7,23},{8,24},{9,... | collective-permute-start | bytes 786440 | tf_op jit(solution)/shard_map/ppermute | solution.py:92
  7.8 1.6 %collective-permute-start.4 = (bf16[256,512]{1,0:T(8,128)(2,1)S(1)}, bf16[256,512]{1,0:T(8,128)(2,1)S(1)}, u32[]{:S(2)}, u32[]{:S(2)}) collective-permute-start(bf16[256,512]{1,0:T(8,128)(2,1)S(1)} %maximum_select_fusion.refs_3_), channel_id=1, source_target_pairs={{0,8},{1,9},{2,10},{3,11},{4,12},{5,13},{6,14},{7,15},{8,0},{9,1},... | collective-permute-start | bytes 786440 | tf_op jit(solution)/shard_map/ppermute | solution.py:92
  9.4 1.5 %collective-permute-start.3 = (bf16[256,512]{1,0:T(8,128)(2,1)S(1)}, bf16[256,512]{1,0:T(8,128)(2,1)S(1)}, u32[]{:S(2)}, u32[]{:S(2)}) collective-permute-start(bf16[256,512]{1,0:T(8,128)(2,1)S(1)} %maximum_select_fusion.refs_3_), channel_id=1, source_target_pairs={{0,2},{1,3},{2,0},{3,1},{4,6},{5,7},{6,4},{7,5},{8,10},{9,11},{10,... | collective-permute-start | bytes 786440 | tf_op jit(solution)/shard_map/ppermute | solution.py:92
  10.9 1.5 %collective-permute-start.2 = (bf16[256,512]{1,0:T(8,128)(2,1)S(1)}, bf16[256,512]{1,0:T(8,128)(2,1)S(1)}, u32[]{:S(2)}, u32[]{:S(2)}) collective-permute-start(bf16[256,512]{1,0:T(8,128)(2,1)S(1)} %maximum_select_fusion.refs_3_), channel_id=1, source_target_pairs={{0,4},{1,5},{2,6},{3,7},{4,0},{5,1},{6,2},{7,3},{8,12},{9,13},{10,... | collective-permute-start | bytes 786440 | tf_op jit(solution)/shard_map/ppermute | solution.py:92
  12.4 8.0 %collective-permute-done.5.refs_7_ = bf16[256,512]{1,0:T(8,128)(2,1)S(1)} collective-permute-done((bf16[256,512]{1,0:T(8,128)(2,1)S(1)}, bf16[256,512]{1,0:T(8,128)(2,1)S(1)}, u32[]{:S(2)}, u32[]{:S(2)}) %collective-permute-start.5) | collective-permute-done | bytes 262176 | tf_op jit(solution)/shard_map/ppermute | solution.py:92
  20.6 1.6 %collective-permute-start.7 = (bf16[256,512]{1,0:T(8,128)(2,1)S(1)}, bf16[256,512]{1,0:T(8,128)(2,1)}, u32[]{:S(2)}, u32[]{:S(2)}) collective-permute-start(bf16[256,512]{1,0:T(8,128)(2,1)S(1)} %collective-permute-done.4.refs_6_), channel_id=1, source_target_pairs={{0,4},{1,5},{2,6},{3,7},{4,0},{5,1},{6,2},{7,3},{8,12},{9,13},{10,... | collective-permute-start | bytes 786440 | tf_op jit(solution)/shard_map/ppermute | solution.py:92
  22.2 1.5 %collective-permute-start.6 = (bf16[256,512]{1,0:T(8,128)(2,1)S(1)}, bf16[256,512]{1,0:T(8,128)(2,1)}, u32[]{:S(2)}, u32[]{:S(2)}) collective-permute-start(bf16[256,512]{1,0:T(8,128)(2,1)S(1)} %collective-permute-done.4.refs_6_), channel_id=1, source_target_pairs={{0,2},{1,3},{2,0},{3,1},{4,6},{5,7},{6,4},{7,5},{8,10},{9,11},{10,... | collective-permute-start | bytes 786440 | tf_op jit(solution)/shard_map/ppermute | solution.py:92
  23.7 1.4 %collective-permute-start.10 = (bf16[256,512]{1,0:T(8,128)(2,1)S(1)}, bf16[256,512]{1,0:T(8,128)(2,1)}, u32[]{:S(2)}, u32[]{:S(2)}) collective-permute-start(bf16[256,512]{1,0:T(8,128)(2,1)S(1)} %collective-permute-done.5.refs_7_), channel_id=1, source_target_pairs={{0,8},{1,9},{2,10},{3,11},{4,12},{5,13},{6,14},{7,15},{8,0},{9,1},... | collective-permute-start | bytes 786440 | tf_op jit(solution)/shard_map/ppermute | solution.py:92
  26.2 0.8 reduce-window.4
  27.1 0.7 convert_bitcast_fusion.1
  27.8 0.8 convert_reduce_fusion
  28.6 0.7 select_reduce_fusion
  29.4 1.1 compare_select_fusion
  30.5 0.7 pad_maximum_fusion.1
  31.6 2.6 %collective-permute-done.9.refs_11_ = bf16[256,512]{1,0:T(8,128)(2,1)} collective-permute-done((bf16[256,512]{1,0:T(8,128)(2,1)S(1)}, bf16[256,512]{1,0:T(8,128)(2,1)}, u32[]{:S(2)}, u32[]{:S(2)}) %collective-permute-start.9) | collective-permute-done | bytes 262176 | tf_op jit(solution)/shard_map/ppermute | solution.py:92
  34.2 1.0 collective-permute-done.8.refs_10_
  35.3 1.1 pad_maximum_fusion
  36.4 5.2 %all-to-all-start = ((bf16[4,128,1024]{2,1,0:T(8,128)(2,1)}), bf16[4,128,1024]{2,1,0:T(8,128)(2,1)S(1)}, u32[]{:S(2)}, u32[]{:S(2)}) async-start(bf16[4,128,1024]{2,1,0:T(8,128)(2,1)} %pad_maximum_fusion), calls=%async_computation | async-start | bytes 2097152 | tf_op jit(solution)/shard_map/all_to_all | solution.py:387
  41.7 1.5 %collective-permute-start.14 = (bf16[256,512]{1,0:T(8,128)(2,1)S(1)}, bf16[256,512]{1,0:T(8,128)(2,1)S(1)}, u32[]{:S(2)}, u32[]{:S(2)}) collective-permute-start(bf16[256,512]{1,0:T(8,128)(2,1)S(1)} %collective-permute-done.2.refs_4_), channel_id=1, source_target_pairs={{0,2},{1,3},{2,0},{3,1},{4,6},{5,7},{6,4},{7,5},{8,10},{9,11},{10,... | collective-permute-start | bytes 786440 | tf_op jit(solution)/shard_map/ppermute | solution.py:92
  43.7 1.5 %collective-permute-start.13 = (bf16[256,512]{1,0:T(8,128)(2,1)}, bf16[256,512]{1,0:T(8,128)(2,1)S(1)}, u32[]{:S(2)}, u32[]{:S(2)}) collective-permute-start(bf16[256,512]{1,0:T(8,128)(2,1)} %collective-permute-done.10.refs_12_), channel_id=1, source_target_pairs={{0,4},{1,5},{2,6},{3,7},{4,0},{5,1},{6,2},{7,3},{8,12},{9,13},{10,... | collective-permute-start | bytes 786440 | tf_op jit(solution)/shard_map/ppermute | solution.py:92
  45.7 1.4 %collective-permute-done.11.mate_cot_ref = bf16[144,512]{1,0:T(8,128)(2,1)S(1)} collective-permute-done((bf16[144,512]{1,0:T(8,128)(2,1)S(1)}, bf16[144,512]{1,0:T(8,128)(2,1)S(1)}, u32[]{:S(2)}, u32[]{:S(2)}) %collective-permute-start.11) | collective-permute-done | bytes 147488 | tf_op jit(solution)/shard_map/ppermute | solution.py:92
  47.1 3.8 %collective-permute-done.14.refs_15_ = bf16[256,512]{1,0:T(8,128)(2,1)S(1)} collective-permute-done((bf16[256,512]{1,0:T(8,128)(2,1)S(1)}, bf16[256,512]{1,0:T(8,128)(2,1)S(1)}, u32[]{:S(2)}, u32[]{:S(2)}) %collective-permute-start.14) | collective-permute-done | bytes 262176 | tf_op jit(solution)/shard_map/ppermute | solution.py:92
  50.9 1.7 %collective-permute-done.15.refs_16_ = bf16[256,512]{1,0:T(8,128)(2,1)S(1)} collective-permute-done((bf16[256,512]{1,0:T(8,128)(2,1)}, bf16[256,512]{1,0:T(8,128)(2,1)S(1)}, u32[]{:S(2)}, u32[]{:S(2)}) %collective-permute-start.15) | collective-permute-done | bytes 262176 | tf_op jit(solution)/shard_map/ppermute | solution.py:92
  52.6 2.9 %collective-permute-done.13.refs_14_ = bf16[256,512]{1,0:T(8,128)(2,1)S(1)} collective-permute-done((bf16[256,512]{1,0:T(8,128)(2,1)}, bf16[256,512]{1,0:T(8,128)(2,1)S(1)}, u32[]{:S(2)}, u32[]{:S(2)}) %collective-permute-start.13) | collective-permute-done | bytes 262176 | tf_op jit(solution)/shard_map/ppermute | solution.py:92
  56.1 0.6 collective-permute-start.17
  56.7 0.7 stack.87.refs_0_.chips_ref
  57.4 6.1 %project.1 = (bf16[3584,512]{1,0:T(8,128)(2,1)}, f32[2,128,512]{2,1,0:T(8,128)}) custom-call(s32[16]{0:T(128)} %stack.87.refs_0_.chips_ref, bf16[128,4096]{1,0:T(8,128)(2,1)} %refs_0_.1, bf16[128,4096]{1,0:T(8,128)(2,1)} %copy-done.3, bf16[256,512]{1,0:T(8,128)(2,1)} %copy-done.8, bf16[256,512]{1,0:T(8,128)(2,1)} %copy-done.14, bf16[256,512]{1,0:T(8,128)(2,1)} %copy-done.13, ...), custom_call_target="tpu_custom_call" | custom-call | tf_op jit(solution)/shard_map/project/pallas_call | solution.py:412
  63.6 2.9 %all-to-all-done.own_ref = bf16[4,128,1024]{2,1,0:T(8,128)(2,1)S(1)} async-done(((bf16[4,128,1024]{2,1,0:T(8,128)(2,1)}), bf16[4,128,1024]{2,1,0:T(8,128)(2,1)S(1)}, u32[]{:S(2)}, u32[]{:S(2)}) %all-to-all-start) | async-done | bytes 1048608 | tf_op jit(solution)/shard_map/all_to_all | solution.py:387
  66.5 4.1 %delta.1 = (bf16[272,512]{1,0:T(8,128)(2,1)}, bf16[512,512]{1,0:T(8,128)(2,1)}) custom-call(s32[16]{0:T(128)} %stack.87.refs_0_.chips_ref, s32[1]{0:T(128)} %bitcast.16.me_ref, bf16[144,512]{1,0:T(8,128)(2,1)} %get-tuple-element.108.own_cot_ref, bf16[144,512]{1,0:T(8,128)(2,1)} %copy-done.22, bf16[128,4096]{1,0:T(8,128)(2,1)} %refs_0_.1, ...), custom_call_target="tpu_custom_call" | custom-call | tf_op jit(solution)/shard_map/delta/pallas_call | solution.py:412
  70.6 1.5 %collective-permute-start.21 = (bf16[272,512]{1,0:T(8,128)(2,1)}, bf16[272,512]{1,0:T(8,128)(2,1)S(1)}, u32[]{:S(2)}, u32[]{:S(2)}) collective-permute-start(bf16[272,512]{1,0:T(8,128)(2,1)} %get-tuple-element.129.refs_0_), channel_id=1, source_target_pairs={{0,24},{1,25},{2,26},{3,27},{4,28},{5,29},{6,30},{7,31},{8,16},{9,... | collective-permute-start | bytes 835592 | tf_op jit(solution)/shard_map/ppermute | solution.py:92
  72.2 2.9 %collective-permute-start.19 = (bf16[272,512]{1,0:T(8,128)(2,1)}, bf16[272,512]{1,0:T(8,128)(2,1)S(1)}, u32[]{:S(2)}, u32[]{:S(2)}) collective-permute-start(bf16[272,512]{1,0:T(8,128)(2,1)} %get-tuple-element.129.refs_0_), channel_id=1, source_target_pairs={{0,8},{1,9},{2,10},{3,11},{4,12},{5,13},{6,14},{7,15},{8,0},{9,1},... | collective-permute-start | bytes 835592 | tf_op jit(solution)/shard_map/ppermute | solution.py:92
  75.1 7.3 %collective-permute-done.21.refs_3_ = bf16[272,512]{1,0:T(8,128)(2,1)S(1)} collective-permute-done((bf16[272,512]{1,0:T(8,128)(2,1)}, bf16[272,512]{1,0:T(8,128)(2,1)S(1)}, u32[]{:S(2)}, u32[]{:S(2)}) %collective-permute-start.21) | collective-permute-done | bytes 278560 | tf_op jit(solution)/shard_map/ppermute | solution.py:92
  82.4 13.5 %collective-permute-done.20.refs_2_ = bf16[272,512]{1,0:T(8,128)(2,1)S(1)} collective-permute-done((bf16[272,512]{1,0:T(8,128)(2,1)}, bf16[272,512]{1,0:T(8,128)(2,1)S(1)}, u32[]{:S(2)}, u32[]{:S(2)}) %collective-permute-start.20) | collective-permute-done | bytes 278560 | tf_op jit(solution)/shard_map/ppermute | solution.py:92
  96.0 0.6 copy-done.5
  96.7 2.6 %select.28 = (bf16[128,512]{1,0:T(8,128)(2,1)}, bf16[128,512]{1,0:T(8,128)(2,1)}, bf16[128,512]{1,0:T(8,128)(2,1)}, bf16[128,512]{1,0:T(8,128)(2,1)}) custom-call(s32[1]{0:T(128)} %bitcast.16.me_ref, bf16[272,512]{1,0:T(8,128)(2,1)} %get-tuple-element.129.refs_0_, bf16[272,512]{1,0:T(8,128)(2,1)} %copy-done.6, bf16[272,512]{1,0:T(8,128)(2,1)} %copy-done.5, ...), custom_call_target="tpu_custom_call" | custom-call | tf_op jit(solution)/shard_map/select/pallas_call | solution.py:476
  99.3 1.6 %collective-permute-start.22 = (bf16[128,512]{1,0:T(8,128)(2,1)}, bf16[128,512]{1,0:T(8,128)(2,1)S(1)}, u32[]{:S(2)}, u32[]{:S(2)}) collective-permute-start(bf16[128,512]{1,0:T(8,128)(2,1)} %get-tuple-element.121), channel_id=1, source_target_pairs={{0,2},{1,3},{2,0},{3,1},{4,6},{5,7},{6,4},{7,5},{8,10},{9,11},{10,... | collective-permute-start | bytes 393224 | tf_op jit(solution)/shard_map/ppermute | solution.py:92
  100.9 1.4 %collective-permute-start.23 = (bf16[128,512]{1,0:T(8,128)(2,1)}, bf16[128,512]{1,0:T(8,128)(2,1)S(1)}, u32[]{:S(2)}, u32[]{:S(2)}) collective-permute-start(bf16[128,512]{1,0:T(8,128)(2,1)} %get-tuple-element.122), channel_id=1, source_target_pairs={{0,4},{1,5},{2,6},{3,7},{4,0},{5,1},{6,2},{7,3},{8,12},{9,13},{10,... | collective-permute-start | bytes 393224 | tf_op jit(solution)/shard_map/ppermute | solution.py:92
  102.9 3.9 %weight_grad.1 = bf16[1024,512]{1,0:T(8,128)(2,1)} custom-call(s32[1]{0:T(128)} %bitcast.16.me_ref, bf16[4,128,1024]{2,1,0:T(8,128)(2,1)} %copy-done.1, bf16[4,128,1024]{2,1,0:T(8,128)(2,1)} %copy-done.7, bf16[272,512]{1,0:T(8,128)(2,1)} %get-tuple-element.129.refs_0_, bf16[272,512]{1,0:T(8,128)(2,1)} %copy-done.6, bf16[272,512]{1,0:T(8,128)(2,1)} %copy-done.5, ...), custom_call_target="tpu_custom_call" | custom-call | tf_op jit(solution)/shard_map/weight_grad/pallas_call | solution.py:489
  106.8 2.1 %collective-permute-done.23.refs_2_ = bf16[128,512]{1,0:T(8,128)(2,1)S(1)} collective-permute-done((bf16[128,512]{1,0:T(8,128)(2,1)}, bf16[128,512]{1,0:T(8,128)(2,1)S(1)}, u32[]{:S(2)}, u32[]{:S(2)}) %collective-permute-start.23) | collective-permute-done | bytes 131104 | tf_op jit(solution)/shard_map/ppermute | solution.py:92
  108.9 3.6 %all-to-all-start.1 = ((bf16[8,128,512]{2,1,0:T(8,128)(2,1)}), bf16[8,128,512]{2,1,0:T(8,128)(2,1)S(1)}, u32[]{:S(2)}, u32[]{:S(2)}) async-start(bf16[8,128,512]{2,1,0:T(8,128)(2,1)} %bitcast.35), calls=%async_computation.1 | async-start | bytes 2097152 | tf_op jit(solution)/shard_map/all_to_all | solution.py:503
  112.9 1.9 %share.1 = (bf16[4,64,512]{2,1,0:T(8,128)(2,1)}, bf16[4,64,512]{2,1,0:T(8,128)(2,1)}) custom-call(s32[1]{0:T(128)} %bitcast.16.me_ref, bf16[128,512]{1,0:T(8,128)(2,1)} %get-tuple-element.120.refs_0_, bf16[128,512]{1,0:T(8,128)(2,1)} %copy-done.23, bf16[128,512]{1,0:T(8,128)(2,1)} %copy-done.24, bf16[128,512]{1,0:T(8,128)(2,1)} %copy-done.25), custom_call_target="tpu_custom_call" | custom-call | tf_op jit(solution)/shard_map/share/pallas_call | solution.py:512
  115.0 1.6 %collective-permute-done.25.mate_got_ref = bf16[4,64,512]{2,1,0:T(8,128)(2,1)S(1)} collective-permute-done((bf16[4,64,512]{2,1,0:T(8,128)(2,1)}, bf16[4,64,512]{2,1,0:T(8,128)(2,1)S(1)}, u32[]{:S(2)}, u32[]{:S(2)}) %collective-permute-start.25) | collective-permute-done | bytes 262176 | tf_op jit(solution)/shard_map/ppermute | solution.py:92
  116.6 0.7 copy-done.21
  117.4 10.3 %row_grad.1 = bf16[256,4096]{1,0:T(8,128)(2,1)} custom-call(s32[16]{0:T(128)} %stack.87.refs_0_.chips_ref, s32[1]{0:T(128)} %bitcast.16.me_ref, bf16[4,64,512]{2,1,0:T(8,128)(2,1)} %get-tuple-element.124.own_got_ref, bf16[4,64,512]{2,1,0:T(8,128)(2,1)} %copy-done.21, bf16[3584,512]{1,0:T(8,128)(2,1)} %get-tuple-element.126.refs_0_, ...), custom_call_target="tpu_custom_call" | custom-call | tf_op jit(solution)/shard_map/row_grad/pallas_call | solution.py:523
  127.8 1.0 copy-done.2
  128.8 2.3 %sum.1 = f32[128,1024]{1,0:T(8,128)} custom-call(bf16[4,2,128,512]{3,2,1,0:T(8,128)(2,1)} %bitcast.36), custom_call_target="tpu_custom_call" | custom-call | tf_op jit(solution)/shard_map/sum/pallas_call | solution.py:542
  (89 shorter events, 6.1 us)
Async XLA Ops:
  0.6 34.6 %copy-start = (bf16[128,4096]{1,0:T(8,128)(2,1)S(1)}, bf16[128,4096]{1,0:T(8,128)(2,1)}, u32[]{:S(2)}) copy-start(bf16[128,4096]{1,0:T(8,128)(2,1)} %refs_0_.1) | copy-start | bytes 3145732
  0.6 1.9 %collective-permute-start = (bf16[128,1024]{1,0:T(8,128)(2,1)}, bf16[128,1024]{1,0:T(8,128)(2,1)S(1)}, u32[]{:S(2)}, u32[]{:S(2)}) collective-permute-start(bf16[128,1024]{1,0:T(8,128)(2,1)} %param.11), channel_id=1, source_target_pairs={{0,1},{1,0},{2,3},{3,2},{4,5},{5,4},{6,7},{7,6},{8,9},{9,8},{10,11... | collective-permute-start | bytes 786440 | tf_op jit(solution)/shard_map/ppermute | solution.py:92
  2.5 18.0 %collective-permute-start.1 = (bf16[128,4096]{1,0:T(8,128)(2,1)}, bf16[128,4096]{1,0:T(8,128)(2,1)S(1)}, u32[]{:S(2)}, u32[]{:S(2)}) collective-permute-start(bf16[128,4096]{1,0:T(8,128)(2,1)} %refs_0_.1), channel_id=1, source_target_pairs={{0,1},{1,0},{2,3},{3,2},{4,5},{5,4},{6,7},{7,6},{8,9},{9,8},{10,11... | collective-permute-start | bytes 3145736 | tf_op jit(solution)/shard_map/ppermute | solution.py:92
  4.0 32.4 %copy-start.8 = (bf16[256,512]{1,0:T(8,128)(2,1)}, bf16[256,512]{1,0:T(8,128)(2,1)S(1)}, u32[]{:S(2)}) copy-start(bf16[256,512]{1,0:T(8,128)(2,1)S(1)} %maximum_select_fusion.refs_3_) | copy-start | bytes 786436
  4.0 16.4 %collective-permute-start.5 = (bf16[256,512]{1,0:T(8,128)(2,1)S(1)}, bf16[256,512]{1,0:T(8,128)(2,1)S(1)}, u32[]{:S(2)}, u32[]{:S(2)}) collective-permute-start(bf16[256,512]{1,0:T(8,128)(2,1)S(1)} %maximum_select_fusion.refs_3_), channel_id=1, source_target_pairs={{0,16},{1,17},{2,18},{3,19},{4,20},{5,21},{6,22},{7,23},{8,24},{9,... | collective-permute-start | bytes 786440 | tf_op jit(solution)/shard_map/ppermute | solution.py:92
  7.8 12.7 %collective-permute-start.4 = (bf16[256,512]{1,0:T(8,128)(2,1)S(1)}, bf16[256,512]{1,0:T(8,128)(2,1)S(1)}, u32[]{:S(2)}, u32[]{:S(2)}) collective-permute-start(bf16[256,512]{1,0:T(8,128)(2,1)S(1)} %maximum_select_fusion.refs_3_), channel_id=1, source_target_pairs={{0,8},{1,9},{2,10},{3,11},{4,12},{5,13},{6,14},{7,15},{8,0},{9,1},... | collective-permute-start | bytes 786440 | tf_op jit(solution)/shard_map/ppermute | solution.py:92
  9.4 11.2 %collective-permute-start.3 = (bf16[256,512]{1,0:T(8,128)(2,1)S(1)}, bf16[256,512]{1,0:T(8,128)(2,1)S(1)}, u32[]{:S(2)}, u32[]{:S(2)}) collective-permute-start(bf16[256,512]{1,0:T(8,128)(2,1)S(1)} %maximum_select_fusion.refs_3_), channel_id=1, source_target_pairs={{0,2},{1,3},{2,0},{3,1},{4,6},{5,7},{6,4},{7,5},{8,10},{9,11},{10,... | collective-permute-start | bytes 786440 | tf_op jit(solution)/shard_map/ppermute | solution.py:92
  10.9 9.7 %collective-permute-start.2 = (bf16[256,512]{1,0:T(8,128)(2,1)S(1)}, bf16[256,512]{1,0:T(8,128)(2,1)S(1)}, u32[]{:S(2)}, u32[]{:S(2)}) collective-permute-start(bf16[256,512]{1,0:T(8,128)(2,1)S(1)} %maximum_select_fusion.refs_3_), channel_id=1, source_target_pairs={{0,4},{1,5},{2,6},{3,7},{4,0},{5,1},{6,2},{7,3},{8,12},{9,13},{10,... | collective-permute-start | bytes 786440 | tf_op jit(solution)/shard_map/ppermute | solution.py:92
  20.4 16.1 %copy-start.11 = (bf16[256,512]{1,0:T(8,128)(2,1)}, bf16[256,512]{1,0:T(8,128)(2,1)S(1)}, u32[]{:S(2)}) copy-start(bf16[256,512]{1,0:T(8,128)(2,1)S(1)} %collective-permute-done.5.refs_7_) | copy-start | bytes 786436
  20.6 15.9 %copy-start.12 = (bf16[256,512]{1,0:T(8,128)(2,1)}, bf16[256,512]{1,0:T(8,128)(2,1)S(1)}, u32[]{:S(2)}) copy-start(bf16[256,512]{1,0:T(8,128)(2,1)S(1)} %collective-permute-done.4.refs_6_) | copy-start | bytes 786436
  20.6 15.9 %copy-start.13 = (bf16[256,512]{1,0:T(8,128)(2,1)}, bf16[256,512]{1,0:T(8,128)(2,1)S(1)}, u32[]{:S(2)}) copy-start(bf16[256,512]{1,0:T(8,128)(2,1)S(1)} %collective-permute-done.3.refs_5_) | copy-start | bytes 786436
  20.6 21.1 %copy-start.14 = (bf16[256,512]{1,0:T(8,128)(2,1)}, bf16[256,512]{1,0:T(8,128)(2,1)S(1)}, u32[]{:S(2)}) copy-start(bf16[256,512]{1,0:T(8,128)(2,1)S(1)} %collective-permute-done.2.refs_4_) | copy-start | bytes 786436
  20.6 15.9 %copy-start.3 = (bf16[128,4096]{1,0:T(8,128)(2,1)}, bf16[128,4096]{1,0:T(8,128)(2,1)S(1)}, u32[]{:S(2)}) copy-start(bf16[128,4096]{1,0:T(8,128)(2,1)S(1)} %collective-permute-done.1.refs_2_.refs_1_) | copy-start | bytes 3145732
  20.6 10.6 %collective-permute-start.7 = (bf16[256,512]{1,0:T(8,128)(2,1)S(1)}, bf16[256,512]{1,0:T(8,128)(2,1)}, u32[]{:S(2)}, u32[]{:S(2)}) collective-permute-start(bf16[256,512]{1,0:T(8,128)(2,1)S(1)} %collective-permute-done.4.refs_6_), channel_id=1, source_target_pairs={{0,4},{1,5},{2,6},{3,7},{4,0},{5,1},{6,2},{7,3},{8,12},{9,13},{10,... | collective-permute-start | bytes 786440 | tf_op jit(solution)/shard_map/ppermute | solution.py:92
  22.2 9.4 %collective-permute-start.6 = (bf16[256,512]{1,0:T(8,128)(2,1)S(1)}, bf16[256,512]{1,0:T(8,128)(2,1)}, u32[]{:S(2)}, u32[]{:S(2)}) collective-permute-start(bf16[256,512]{1,0:T(8,128)(2,1)S(1)} %collective-permute-done.4.refs_6_), channel_id=1, source_target_pairs={{0,2},{1,3},{2,0},{3,1},{4,6},{5,7},{6,4},{7,5},{8,10},{9,11},{10,... | collective-permute-start | bytes 786440 | tf_op jit(solution)/shard_map/ppermute | solution.py:92
  23.7 7.9 %collective-permute-start.10 = (bf16[256,512]{1,0:T(8,128)(2,1)S(1)}, bf16[256,512]{1,0:T(8,128)(2,1)}, u32[]{:S(2)}, u32[]{:S(2)}) collective-permute-start(bf16[256,512]{1,0:T(8,128)(2,1)S(1)} %collective-permute-done.5.refs_7_), channel_id=1, source_target_pairs={{0,8},{1,9},{2,10},{3,11},{4,12},{5,13},{6,14},{7,15},{8,0},{9,1},... | collective-permute-start | bytes 786440 | tf_op jit(solution)/shard_map/ppermute | solution.py:92
  25.2 9.0 %collective-permute-start.9 = (bf16[256,512]{1,0:T(8,128)(2,1)S(1)}, bf16[256,512]{1,0:T(8,128)(2,1)}, u32[]{:S(2)}, u32[]{:S(2)}) collective-permute-start(bf16[256,512]{1,0:T(8,128)(2,1)S(1)} %collective-permute-done.5.refs_7_), channel_id=1, source_target_pairs={{0,4},{1,5},{2,6},{3,7},{4,0},{5,1},{6,2},{7,3},{8,12},{9,13},{10,... | collective-permute-start | bytes 786440 | tf_op jit(solution)/shard_map/ppermute | solution.py:92
  25.7 9.5 %collective-permute-start.8 = (bf16[256,512]{1,0:T(8,128)(2,1)S(1)}, bf16[256,512]{1,0:T(8,128)(2,1)}, u32[]{:S(2)}, u32[]{:S(2)}) collective-permute-start(bf16[256,512]{1,0:T(8,128)(2,1)S(1)} %collective-permute-done.5.refs_7_), channel_id=1, source_target_pairs={{0,2},{1,3},{2,0},{3,1},{4,6},{5,7},{6,4},{7,5},{8,10},{9,11},{10,... | collective-permute-start | bytes 786440 | tf_op jit(solution)/shard_map/ppermute | solution.py:92
  36.4 30.0 %all-to-all-start = ((bf16[4,128,1024]{2,1,0:T(8,128)(2,1)}), bf16[4,128,1024]{2,1,0:T(8,128)(2,1)S(1)}, u32[]{:S(2)}, u32[]{:S(2)}) async-start(bf16[4,128,1024]{2,1,0:T(8,128)(2,1)} %pad_maximum_fusion), calls=%async_computation | async-start | bytes 2097152 | tf_op jit(solution)/shard_map/all_to_all | solution.py:387
  41.7 9.2 %collective-permute-start.14 = (bf16[256,512]{1,0:T(8,128)(2,1)S(1)}, bf16[256,512]{1,0:T(8,128)(2,1)S(1)}, u32[]{:S(2)}, u32[]{:S(2)}) collective-permute-start(bf16[256,512]{1,0:T(8,128)(2,1)S(1)} %collective-permute-done.2.refs_4_), channel_id=1, source_target_pairs={{0,2},{1,3},{2,0},{3,1},{4,6},{5,7},{6,4},{7,5},{8,10},{9,11},{10,... | collective-permute-start | bytes 786440 | tf_op jit(solution)/shard_map/ppermute | solution.py:92
  43.2 9.5 %collective-permute-start.15 = (bf16[256,512]{1,0:T(8,128)(2,1)}, bf16[256,512]{1,0:T(8,128)(2,1)S(1)}, u32[]{:S(2)}, u32[]{:S(2)}) collective-permute-start(bf16[256,512]{1,0:T(8,128)(2,1)} %collective-permute-done.8.refs_10_), channel_id=1, source_target_pairs={{0,4},{1,5},{2,6},{3,7},{4,0},{5,1},{6,2},{7,3},{8,12},{9,13},{10,... | collective-permute-start | bytes 786440 | tf_op jit(solution)/shard_map/ppermute | solution.py:92
  43.7 11.9 %collective-permute-start.13 = (bf16[256,512]{1,0:T(8,128)(2,1)}, bf16[256,512]{1,0:T(8,128)(2,1)S(1)}, u32[]{:S(2)}, u32[]{:S(2)}) collective-permute-start(bf16[256,512]{1,0:T(8,128)(2,1)} %collective-permute-done.10.refs_12_), channel_id=1, source_target_pairs={{0,4},{1,5},{2,6},{3,7},{4,0},{5,1},{6,2},{7,3},{8,12},{9,13},{10,... | collective-permute-start | bytes 786440 | tf_op jit(solution)/shard_map/ppermute | solution.py:92
  45.2 10.3 %collective-permute-start.12 = (bf16[256,512]{1,0:T(8,128)(2,1)}, bf16[256,512]{1,0:T(8,128)(2,1)S(1)}, u32[]{:S(2)}, u32[]{:S(2)}) collective-permute-start(bf16[256,512]{1,0:T(8,128)(2,1)} %collective-permute-done.10.refs_12_), channel_id=1, source_target_pairs={{0,2},{1,3},{2,0},{3,1},{4,6},{5,7},{6,4},{7,5},{8,10},{9,11},{10,... | collective-permute-start | bytes 786440 | tf_op jit(solution)/shard_map/ppermute | solution.py:92
  45.7 1.4 %collective-permute-start.11 = (bf16[144,512]{1,0:T(8,128)(2,1)S(1)}, bf16[144,512]{1,0:T(8,128)(2,1)S(1)}, u32[]{:S(2)}, u32[]{:S(2)}) collective-permute-start(bf16[144,512]{1,0:T(8,128)(2,1)S(1)} %get-tuple-element.76), channel_id=1, source_target_pairs={{0,1},{1,0},{2,3},{3,2},{4,5},{5,4},{6,7},{7,6},{8,9},{9,8},{10,11... | collective-permute-start | bytes 442376 | tf_op jit(solution)/shard_map/ppermute | solution.py:92
  47.1 19.4 %copy-start.22 = (bf16[144,512]{1,0:T(8,128)(2,1)}, bf16[144,512]{1,0:T(8,128)(2,1)S(1)}, u32[]{:S(2)}) copy-start(bf16[144,512]{1,0:T(8,128)(2,1)S(1)} %collective-permute-done.11.mate_cot_ref) | copy-start | bytes 442372
  50.9 6.5 %copy-start.15 = (bf16[256,512]{1,0:T(8,128)(2,1)}, bf16[256,512]{1,0:T(8,128)(2,1)S(1)}, u32[]{:S(2)}) copy-start(bf16[256,512]{1,0:T(8,128)(2,1)S(1)} %collective-permute-done.14.refs_15_) | copy-start | bytes 786436
  52.6 4.8 %copy-start.16 = (bf16[256,512]{1,0:T(8,128)(2,1)}, bf16[256,512]{1,0:T(8,128)(2,1)S(1)}, u32[]{:S(2)}) copy-start(bf16[256,512]{1,0:T(8,128)(2,1)S(1)} %collective-permute-done.15.refs_16_) | copy-start | bytes 786436
  55.5 8.0 %collective-permute-start.16 = (bf16[256,512]{1,0:T(8,128)(2,1)}, bf16[256,512]{1,0:T(8,128)(2,1)S(1)}, u32[]{:S(2)}, u32[]{:S(2)}) collective-permute-start(bf16[256,512]{1,0:T(8,128)(2,1)} %collective-permute-done.7.refs_9_), channel_id=1, source_target_pairs={{0,2},{1,3},{2,0},{3,1},{4,6},{5,7},{6,4},{7,5},{8,10},{9,11},{10,... | collective-permute-start | bytes 786440 | tf_op jit(solution)/shard_map/ppermute | solution.py:92
  56.1 7.4 %collective-permute-start.17 = (bf16[256,512]{1,0:T(8,128)(2,1)S(1)}, bf16[256,512]{1,0:T(8,128)(2,1)S(1)}, u32[]{:S(2)}, u32[]{:S(2)}) collective-permute-start(bf16[256,512]{1,0:T(8,128)(2,1)S(1)} %collective-permute-done.12.refs_13_), channel_id=1, source_target_pairs={{0,4},{1,5},{2,6},{3,7},{4,0},{5,1},{6,2},{7,3},{8,12},{9,13},{10,... | collective-permute-start | bytes 786440 | tf_op jit(solution)/shard_map/ppermute | solution.py:92
  63.6 2.9 %copy-start.19 = (bf16[256,512]{1,0:T(8,128)(2,1)}, bf16[256,512]{1,0:T(8,128)(2,1)S(1)}, u32[]{:S(2)}) copy-start(bf16[256,512]{1,0:T(8,128)(2,1)S(1)} %collective-permute-done.16.refs_3_) | copy-start | bytes 786436
  66.5 36.4 %copy-start.1 = (bf16[4,128,1024]{2,1,0:T(8,128)(2,1)}, bf16[4,128,1024]{2,1,0:T(8,128)(2,1)S(1)}, u32[]{:S(2)}) copy-start(bf16[4,128,1024]{2,1,0:T(8,128)(2,1)S(1)} %all-to-all-done.own_ref) | copy-start | bytes 3145732
  66.5 29.5 %collective-permute-start.18 = (bf16[4,128,1024]{2,1,0:T(8,128)(2,1)S(1)}, bf16[4,128,1024]{2,1,0:T(8,128)(2,1)S(1)}, u32[]{:S(2)}, u32[]{:S(2)}) collective-permute-start(bf16[4,128,1024]{2,1,0:T(8,128)(2,1)S(1)} %all-to-all-done.own_ref), channel_id=1, source_target_pairs={{0,1},{1,0},{2,3},{3,2},{4,5},{5,4},{6,7},{7,6},{8,9},{9,8},{10,11... | collective-permute-start | bytes 3145736 | tf_op jit(solution)/shard_map/ppermute | solution.py:92
  70.6 11.7 %collective-permute-start.21 = (bf16[272,512]{1,0:T(8,128)(2,1)}, bf16[272,512]{1,0:T(8,128)(2,1)S(1)}, u32[]{:S(2)}, u32[]{:S(2)}) collective-permute-start(bf16[272,512]{1,0:T(8,128)(2,1)} %get-tuple-element.129.refs_0_), channel_id=1, source_target_pairs={{0,24},{1,25},{2,26},{3,27},{4,28},{5,29},{6,30},{7,31},{8,16},{9,... | collective-permute-start | bytes 835592 | tf_op jit(solution)/shard_map/ppermute | solution.py:92
  72.2 23.7 %collective-permute-start.20 = (bf16[272,512]{1,0:T(8,128)(2,1)}, bf16[272,512]{1,0:T(8,128)(2,1)S(1)}, u32[]{:S(2)}, u32[]{:S(2)}) collective-permute-start(bf16[272,512]{1,0:T(8,128)(2,1)} %get-tuple-element.129.refs_0_), channel_id=1, source_target_pairs={{0,16},{1,17},{2,18},{3,19},{4,20},{5,21},{6,22},{7,23},{8,24},{9,... | collective-permute-start | bytes 835592 | tf_op jit(solution)/shard_map/ppermute | solution.py:92
  72.2 23.7 %collective-permute-start.19 = (bf16[272,512]{1,0:T(8,128)(2,1)}, bf16[272,512]{1,0:T(8,128)(2,1)S(1)}, u32[]{:S(2)}, u32[]{:S(2)}) collective-permute-start(bf16[272,512]{1,0:T(8,128)(2,1)} %get-tuple-element.129.refs_0_), channel_id=1, source_target_pairs={{0,8},{1,9},{2,10},{3,11},{4,12},{5,13},{6,14},{7,15},{8,0},{9,1},... | collective-permute-start | bytes 835592 | tf_op jit(solution)/shard_map/ppermute | solution.py:92
  82.4 13.7 %copy-start.4 = (bf16[272,512]{1,0:T(8,128)(2,1)}, bf16[272,512]{1,0:T(8,128)(2,1)S(1)}, u32[]{:S(2)}) copy-start(bf16[272,512]{1,0:T(8,128)(2,1)S(1)} %collective-permute-done.21.refs_3_) | copy-start | bytes 835588
  95.9 7.0 %copy-start.7 = (bf16[4,128,1024]{2,1,0:T(8,128)(2,1)}, bf16[4,128,1024]{2,1,0:T(8,128)(2,1)S(1)}, u32[]{:S(2)}) copy-start(bf16[4,128,1024]{2,1,0:T(8,128)(2,1)S(1)} %collective-permute-done.18.mate_ref) | copy-start | bytes 3145732
  95.9 16.5 %copy-start.9 = (bf16[512,512]{1,0:T(8,128)(2,1)S(1)}, bf16[512,512]{1,0:T(8,128)(2,1)}, u32[]{:S(2)}) copy-start(bf16[512,512]{1,0:T(8,128)(2,1)} %get-tuple-element.127.refs_2_) | copy-start | bytes 1572868
  95.9 20.6 %collective-permute-start.26 = (bf16[3584,512]{1,0:T(8,128)(2,1)}, bf16[3584,512]{1,0:T(8,128)(2,1)}, u32[]{:S(2)}, u32[]{:S(2)}) collective-permute-start(bf16[3584,512]{1,0:T(8,128)(2,1)} %get-tuple-element.126.refs_0_), channel_id=1, source_target_pairs={{0,1},{1,0},{2,3},{3,2},{4,5},{5,4},{6,7},{7,6},{8,9},{9,8},{10,11... | collective-permute-start | bytes 11010056 | tf_op jit(solution)/shard_map/ppermute | solution.py:92
  99.3 7.4 %collective-permute-start.22 = (bf16[128,512]{1,0:T(8,128)(2,1)}, bf16[128,512]{1,0:T(8,128)(2,1)S(1)}, u32[]{:S(2)}, u32[]{:S(2)}) collective-permute-start(bf16[128,512]{1,0:T(8,128)(2,1)} %get-tuple-element.121), channel_id=1, source_target_pairs={{0,2},{1,3},{2,0},{3,1},{4,6},{5,7},{6,4},{7,5},{8,10},{9,11},{10,... | collective-permute-start | bytes 393224 | tf_op jit(solution)/shard_map/ppermute | solution.py:92
  100.9 8.0 %collective-permute-start.23 = (bf16[128,512]{1,0:T(8,128)(2,1)}, bf16[128,512]{1,0:T(8,128)(2,1)S(1)}, u32[]{:S(2)}, u32[]{:S(2)}) collective-permute-start(bf16[128,512]{1,0:T(8,128)(2,1)} %get-tuple-element.122), channel_id=1, source_target_pairs={{0,4},{1,5},{2,6},{3,7},{4,0},{5,1},{6,2},{7,3},{8,12},{9,13},{10,... | collective-permute-start | bytes 393224 | tf_op jit(solution)/shard_map/ppermute | solution.py:92
  102.3 6.6 %collective-permute-start.24 = (bf16[128,512]{1,0:T(8,128)(2,1)}, bf16[128,512]{1,0:T(8,128)(2,1)S(1)}, u32[]{:S(2)}, u32[]{:S(2)}) collective-permute-start(bf16[128,512]{1,0:T(8,128)(2,1)} %get-tuple-element.123), channel_id=1, source_target_pairs={{0,6},{1,7},{2,4},{3,5},{4,2},{5,3},{6,0},{7,1},{8,14},{9,15},{10,... | collective-permute-start | bytes 393224 | tf_op jit(solution)/shard_map/ppermute | solution.py:92
  106.8 6.1 %copy-start.23 = (bf16[128,512]{1,0:T(8,128)(2,1)}, bf16[128,512]{1,0:T(8,128)(2,1)S(1)}, u32[]{:S(2)}) copy-start(bf16[128,512]{1,0:T(8,128)(2,1)S(1)} %collective-permute-done.22.refs_1_) | copy-start | bytes 393220
  108.9 4.0 %copy-start.24 = (bf16[128,512]{1,0:T(8,128)(2,1)}, bf16[128,512]{1,0:T(8,128)(2,1)S(1)}, u32[]{:S(2)}) copy-start(bf16[128,512]{1,0:T(8,128)(2,1)S(1)} %collective-permute-done.23.refs_2_) | copy-start | bytes 393220
  108.9 4.0 %copy-start.25 = (bf16[128,512]{1,0:T(8,128)(2,1)}, bf16[128,512]{1,0:T(8,128)(2,1)S(1)}, u32[]{:S(2)}) copy-start(bf16[128,512]{1,0:T(8,128)(2,1)S(1)} %collective-permute-done.24.refs_3_) | copy-start | bytes 393220
  108.9 18.9 %all-to-all-start.1 = ((bf16[8,128,512]{2,1,0:T(8,128)(2,1)}), bf16[8,128,512]{2,1,0:T(8,128)(2,1)S(1)}, u32[]{:S(2)}, u32[]{:S(2)}) async-start(bf16[8,128,512]{2,1,0:T(8,128)(2,1)} %bitcast.35), calls=%async_computation.1 | async-start | bytes 2097152 | tf_op jit(solution)/shard_map/all_to_all | solution.py:503
  112.5 4.1 %collective-permute-start.27 = (bf16[512,512]{1,0:T(8,128)(2,1)S(1)}, bf16[512,512]{1,0:T(8,128)(2,1)S(1)}, u32[]{:S(2)}, u32[]{:S(2)}) collective-permute-start(bf16[512,512]{1,0:T(8,128)(2,1)S(1)} %copy-done.9), channel_id=1, source_target_pairs={{0,1},{1,0},{2,3},{3,2},{4,5},{5,4},{6,7},{7,6},{8,9},{9,8},{10,11... | collective-permute-start | bytes 1572872 | tf_op jit(solution)/shard_map/ppermute | solution.py:92
  114.8 1.7 %collective-permute-start.25 = (bf16[4,64,512]{2,1,0:T(8,128)(2,1)}, bf16[4,64,512]{2,1,0:T(8,128)(2,1)S(1)}, u32[]{:S(2)}, u32[]{:S(2)}) collective-permute-start(bf16[4,64,512]{2,1,0:T(8,128)(2,1)} %get-tuple-element.125), channel_id=1, source_target_pairs={{0,1},{1,0},{2,3},{3,2},{4,5},{5,4},{6,7},{7,6},{8,9},{9,8},{10,11... | collective-permute-start | bytes 786440 | tf_op jit(solution)/shard_map/ppermute | solution.py:92
  (8 other events, 10.8 us)

commit v13 on v12

--- a/solution.py
+++ b/solution.py
@@ -234,54 +234,56 @@
             part_ref[...] = (acc[...] + terms).astype(jnp.bfloat16)
 
 
-def sum_kernel(norm, parts_ref, grad_ref, held, sems):
-    chips, _, _, half = parts_ref.shape
-    copies = fetch(
-        [(parts_ref.at[n // 2, n % 2], held.at[n]) for n in range(2 * chips)], sems
-    )
-    for copy in copies:
-        copy.wait()
+def sum_kernel(norm, parts_ref, grad_ref):
+    half = parts_ref.shape[3]
     for side in range(2):
-        total = held[side].astype(jnp.float32)
-        for chip in range(1, chips):
-            total += held[2 * chip + side].astype(jnp.float32)
+        total = parts_ref[0, side].astype(jnp.float32)
+        for chip in range(1, parts_ref.shape[0]):
+            total += parts_ref[chip, side].astype(jnp.float32)
         grad_ref[:, side * half : (side + 1) * half] = total / norm
 
 
 def row_grad_kernel(chips_ref, me_ref, own_got_ref, mate_got_ref, *refs):
-    *weights, out_ref, rows_ref, held = refs
-    step = pl.program_id(0)
+    weight_refs, (out_ref, weights, out, rows_ref, held, sems) = refs[:4], refs[4:]
     chips, count, half = own_got_ref.shape
     block = count // 4
+    depth = half // 2
+    pieces = weights.shape[1] // depth
     level = lax.shift_right_logical(me_ref[0], 3)
 
-    @pl.when(step == 0)
-    def _():
-        for side, got_ref in enumerate((own_got_ref, mate_got_ref)):
-            for chip, mask in enumerate(PLANE_MASKS):
-                place = lax.shift_right_logical((me_ref[0] ^ mask) & 6, 1)
-                for n in range(4):
-                    at = pl.multiple_of(((level ^ n) * chips + place) * block, block)
-                    rows = got_ref[chip, n * block : (n + 1) * block, :]
-                    held[pl.ds(at, block), :] = rows.astype(jnp.float32)
-            rows_ref[side] = held[...].T.astype(jnp.bfloat16)
-
-    depth = half // 2
-
-    def add(own_ref, mate_ref, begin):
-        for n in range(own_ref.shape[0] // depth):
-            part = slice(n * depth, (n + 1) * depth)
-            total = dot(own_ref[part, :], rows_ref[0], ((1,), (0,)))
-            total += dot(mate_ref[part, :], rows_ref[1], ((1,), (0,)))
-            at = pl.multiple_of(chips_ref[begin + n] * depth, depth)
-            out_ref[:, pl.ds(at, depth)] = total.T.astype(jnp.bfloat16)
-
-    per_step = weights[0].shape[0] // depth
-    add(*weights[:2], step * per_step)
-
-    @pl.when(step == pl.num_programs(0) - 1)
-    def _():
-        add(*weights[2:], pl.num_programs(0) * per_step)
+    def rows_of(ref, n):
+        return ref.at[n * depth : (n + 1) * depth, :]
+
+    pairs = []
+    for n in range(pieces):
+        first = weight_refs[0].shape[0] // depth
+        for side in range(2):
+            ref = weight_refs[side] if n < first else weight_refs[2 + side]
+            pairs.append((rows_of(ref, n % first), rows_of(weights.at[side], n)))
+    copies = fetch(pairs, sems)
+    for side, got_ref in enumerate((own_got_ref, mate_got_ref)):
+        for chip, mask in enumerate(PLANE_MASKS):
+            place = lax.shift_right_logical((me_ref[0] ^ mask) & 6, 1)
+            for n in range(4):
+                at = pl.multiple_of(((level ^ n) * chips + place) * block, block)
+                rows = got_ref[chip, n * block : (n + 1) * block, :]
+                held[pl.ds(at, block), :] = rows.astype(jnp.float32)
+        rows_ref[side] = held[...].T.astype(jnp.bfloat16)
+    written = []
+    for n in range(pieces):
+        for copy in copies[2 * n : 2 * n + 2]:
+            copy.wait()
+        total = dot(rows_of(weights.at[0], n)[...], rows_ref[0], ((1,), (0,)))
+        total += dot(rows_of(weights.at[1], n)[...], rows_ref[1], ((1,), (0,)))
+        out[n] = total.T.astype(jnp.bfloat16)
+        at = pl.multiple_of(chips_ref[n] * depth, depth)
+        copy = pltpu.make_async_copy(
+            out.at[n], out_ref.at[:, pl.ds(at, depth)], sems.at[2 * pieces + n]
+        )
+        copy.start()
+        written.append(copy)
+    for copy in written:
+        copy.wait()
 
 
 def code_rows(destination, core, per_peer, width):
@@ -378,14 +380,15 @@
     codes = code_rows(routes[:, 0], core, per_peer, half_cols)
     own_cot = jnp.concatenate([mine(upstream), codes], axis=0)
 
-    late_tokens, own_cot, give_cot = after_round(
-        tokens=tokens,
+    by_level = jnp.stack([tokens[:, z * wide : (z + 1) * wide] for z in range(levels)])
+    by_level, own_cot, give_cot = after_round(
+        by_level=by_level,
         own_cot=own_cot,
         give_cot=jnp.concatenate([theirs(upstream), codes], axis=0),
     )
     columns = [[p + PLANE * z for z in range(levels)] for p in range(PLANE)]
     own_features = lax.all_to_all(
-        jnp.stack([late_tokens[:, z * wide : (z + 1) * wide] for z in range(levels)]),
+        by_level,
         "dp",
         split_axis=0,
         concat_axis=0,
@@ -466,9 +469,12 @@
         "delta",
     )
 
-    deltas = [delta, *(swap(delta, mask) for mask in (near, far, both))]
-    mate_features, first_weight, last_weight, *deltas[1:] = lax.optimization_barrier(
-        (mate_features, first_weight, last_weight, *deltas[1:])
+    delta_near, delta_far, mate_features = lax.optimization_barrier(
+        (swap(delta, near), swap(delta, far), mate_features)
+    )
+    deltas = [delta, delta_near, delta_far, swap(delta_far, near)]
+    first_weight, last_weight, *deltas[1:] = lax.optimization_barrier(
+        (first_weight, last_weight, *deltas[1:])
     )
     mate_first, mate_last = swap(first_weight, CORE), swap(last_weight, CORE)
     count = levels * 2 * per_peer
@@ -519,22 +525,18 @@
     )(me_scalar, *got)
     mate_got = swap(give_got, CORE)
 
-    block, last_rows = (2 * depth, half_cols), (len(last_masks) * depth, half_cols)
     row_grads = pl.pallas_call(
         row_grad_kernel,
         out_shape=jax.ShapeDtypeStruct((receive, width_model), jnp.bfloat16),
-        grid_spec=pltpu.PrefetchScalarGridSpec(
-            num_scalar_prefetch=2,
-            grid=(len(first_masks) // 2,),
-            in_specs=[pl.BlockSpec(own_got.shape, lambda i, *_: (0, 0, 0))] * 2
-            + [pl.BlockSpec(block, lambda i, *_: (i, 0))] * 2
-            + [pl.BlockSpec(last_rows, lambda i, *_: (0, 0))] * 2,
-            out_specs=pl.BlockSpec((receive, width_model), lambda i, *_: (0, 0)),
-            scratch_shapes=[
-                pltpu.VMEM((2, half_cols, receive), jnp.bfloat16),
-                pltpu.VMEM((receive, half_cols), jnp.float32),
-            ],
-        ),
+        in_specs=[SCALAR] * 2 + vmem(2) + anywhere(4),
+        out_specs=anywhere(1)[0],
+        scratch_shapes=[
+            pltpu.VMEM((2, width_model, half_cols), jnp.bfloat16),
+            pltpu.VMEM((chips, receive, depth), jnp.bfloat16),
+            pltpu.VMEM((2, half_cols, receive), jnp.bfloat16),
+            pltpu.VMEM((receive, half_cols), jnp.float32),
+            pltpu.SemaphoreType.DMA((3 * chips,)),
+        ],
         compiler_params=PARAMS,
         name="row_grad",
     )(order, me_scalar, own_got, mate_got, first_weight, mate_first, last_weight, mate_last)
@@ -542,12 +544,8 @@
     key_grad = pl.pallas_call(
         functools.partial(sum_kernel, math.sqrt(rows * size)),
         out_shape=jax.ShapeDtypeStruct((shard, cols), jnp.float32),
-        in_specs=anywhere(1),
+        in_specs=vmem(1),
         out_specs=vmem(1)[0],
-        scratch_shapes=[
-            pltpu.VMEM((PLANE, shard, half_cols), jnp.bfloat16),
-            pltpu.SemaphoreType.DMA((PLANE,)),
-        ],
         compiler_params=PARAMS,
         name="sum",
     )(after(parts, row_grads))

time: 132 us -> 129 us (0.977)
  other arithmetic: 6.1 us -> 3.48 us
  starting transfers between devices: 37.6 us -> 36.2 us
    ppermute x28, starting transfers between devices: 28.8 us -> 27.4 us  [swap(): return lax.ppermute(value, 'dp', [(i, i ^ mask) for i in range(size)])]
  transfers between devices with their start and end apart: 30 -> 30, of which waited for: 15 -> 17; matrix products, arithmetic and copies ran while one was open for 5% -> 5% of each run, Pallas kernels for 22% -> 23%
where the time goes in v13:
time: 129 us
  waiting for transfers between devices  50.7 us (39%)
  starting transfers between devices  36.2 us (28%)
  Pallas kernels  31.9 us (25%)
  local copies, waits for them, and re-layouts  5.6 us (4%)
  other arithmetic  3.48 us (3%)
    ppermute x28, waiting for transfers between devices, swap(): return lax.ppermute(value, 'dp', [(i, i ^ mask) for i in range(size)])  48.5 us
    ppermute x28, starting transfers between devices, swap(): return lax.ppermute(value, 'dp', [(i, i ^ mask) for i in range(size)])  27.4 us
    pallas_call x1, Pallas kernels, per_device_paired(): pl.pallas_call(row_grad_kernel, out_shape=jax.ShapeDtypeStruct((receive,...  11.1 us
    pallas_call x2, Pallas kernels, project(): pl.pallas_call(kernel, out_shape=(*results, jax.ShapeDtypeStruct((count *...  10.3 us
    all_to_all x1, starting transfers between devices, per_device_paired(): lax.all_to_all(by_level, 'dp', split_axis=0, concat_axis=0, axis_index_gr...  5.22 us
    pallas_call x1, Pallas kernels, per_device_paired(): pl.pallas_call(weight_grad_kernel, out_shape=jax.ShapeDtypeStruct((wide,...  3.88 us
    all_to_all x1, starting transfers between devices, per_device_paired(): lax.all_to_all(after(terms, *got).reshape(PLANE, shard, half_cols), 'dp',...  3.56 us
    unnamed x54, local copies, waits for them, and re-layouts  2.64 us
  transfers between devices with their start and end apart: 30, of which 17 were waited for; matrix products, arithmetic and copies ran while one was open for 5% of the time, Pallas kernels for 23%

profile of v13, /device:TPU:0, one launch (start us, length us, event | category | flops | bytes accessed | tf_op | source)
XLA Modules:
  0.0 128.8 jit_solution(16560320613103852049)
XLA Ops:
  1.2 1.4 %collective-permute-done = bf16[128,1024]{1,0:T(8,128)(2,1)S(1)} collective-permute-done((bf16[128,1024]{1,0:T(8,128)(2,1)}, bf16[128,1024]{1,0:T(8,128)(2,1)S(1)}, u32[]{:S(2)}, u32[]{:S(2)}) %collective-permute-start) | collective-permute-done | bytes 262176 | tf_op jit(solution)/shard_map/ppermute | solution.py:92
  2.9 1.0 fusion.11
  4.0 3.8 %collective-permute-start.5 = (bf16[256,512]{1,0:T(8,128)(2,1)S(1)}, bf16[256,512]{1,0:T(8,128)(2,1)S(1)}, u32[]{:S(2)}, u32[]{:S(2)}) collective-permute-start(bf16[256,512]{1,0:T(8,128)(2,1)S(1)} %maximum_select_fusion.refs_3_), channel_id=1, source_target_pairs={{0,16},{1,17},{2,18},{3,19},{4,20},{5,21},{6,22},{7,23},{8,24},{9,... | collective-permute-start | bytes 786440 | tf_op jit(solution)/shard_map/ppermute | solution.py:92
  7.8 1.6 %collective-permute-start.4 = (bf16[256,512]{1,0:T(8,128)(2,1)S(1)}, bf16[256,512]{1,0:T(8,128)(2,1)S(1)}, u32[]{:S(2)}, u32[]{:S(2)}) collective-permute-start(bf16[256,512]{1,0:T(8,128)(2,1)S(1)} %maximum_select_fusion.refs_3_), channel_id=1, source_target_pairs={{0,8},{1,9},{2,10},{3,11},{4,12},{5,13},{6,14},{7,15},{8,0},{9,1},... | collective-permute-start | bytes 786440 | tf_op jit(solution)/shard_map/ppermute | solution.py:92
  9.4 1.5 %collective-permute-start.3 = (bf16[256,512]{1,0:T(8,128)(2,1)S(1)}, bf16[256,512]{1,0:T(8,128)(2,1)S(1)}, u32[]{:S(2)}, u32[]{:S(2)}) collective-permute-start(bf16[256,512]{1,0:T(8,128)(2,1)S(1)} %maximum_select_fusion.refs_3_), channel_id=1, source_target_pairs={{0,2},{1,3},{2,0},{3,1},{4,6},{5,7},{6,4},{7,5},{8,10},{9,11},{10,... | collective-permute-start | bytes 786440 | tf_op jit(solution)/shard_map/ppermute | solution.py:92
  10.9 1.5 %collective-permute-start.2 = (bf16[256,512]{1,0:T(8,128)(2,1)S(1)}, bf16[256,512]{1,0:T(8,128)(2,1)S(1)}, u32[]{:S(2)}, u32[]{:S(2)}) collective-permute-start(bf16[256,512]{1,0:T(8,128)(2,1)S(1)} %maximum_select_fusion.refs_3_), channel_id=1, source_target_pairs={{0,4},{1,5},{2,6},{3,7},{4,0},{5,1},{6,2},{7,3},{8,12},{9,13},{10,... | collective-permute-start | bytes 786440 | tf_op jit(solution)/shard_map/ppermute | solution.py:92
  12.4 1.3 slice_bitcast_fusion.3
  13.7 1.1 pad_maximum_fusion
  14.8 5.5 %collective-permute-done.5.refs_7_ = bf16[256,512]{1,0:T(8,128)(2,1)S(1)} collective-permute-done((bf16[256,512]{1,0:T(8,128)(2,1)S(1)}, bf16[256,512]{1,0:T(8,128)(2,1)S(1)}, u32[]{:S(2)}, u32[]{:S(2)}) %collective-permute-start.5) | collective-permute-done | bytes 262176 | tf_op jit(solution)/shard_map/ppermute | solution.py:92
  20.6 1.6 %collective-permute-start.7 = (bf16[256,512]{1,0:T(8,128)(2,1)S(1)}, bf16[256,512]{1,0:T(8,128)(2,1)S(1)}, u32[]{:S(2)}, u32[]{:S(2)}) collective-permute-start(bf16[256,512]{1,0:T(8,128)(2,1)S(1)} %collective-permute-done.4.refs_6_), channel_id=1, source_target_pairs={{0,4},{1,5},{2,6},{3,7},{4,0},{5,1},{6,2},{7,3},{8,12},{9,13},{10,... | collective-permute-start | bytes 786440 | tf_op jit(solution)/shard_map/ppermute | solution.py:92
  22.3 1.5 %collective-permute-start.6 = (bf16[256,512]{1,0:T(8,128)(2,1)S(1)}, bf16[256,512]{1,0:T(8,128)(2,1)S(1)}, u32[]{:S(2)}, u32[]{:S(2)}) collective-permute-start(bf16[256,512]{1,0:T(8,128)(2,1)S(1)} %collective-permute-done.4.refs_6_), channel_id=1, source_target_pairs={{0,2},{1,3},{2,0},{3,1},{4,6},{5,7},{6,4},{7,5},{8,10},{9,11},{10,... | collective-permute-start | bytes 786440 | tf_op jit(solution)/shard_map/ppermute | solution.py:92
  23.7 1.4 %collective-permute-start.10 = (bf16[256,512]{1,0:T(8,128)(2,1)S(1)}, bf16[256,512]{1,0:T(8,128)(2,1)S(1)}, u32[]{:S(2)}, u32[]{:S(2)}) collective-permute-start(bf16[256,512]{1,0:T(8,128)(2,1)S(1)} %collective-permute-done.5.refs_7_), channel_id=1, source_target_pairs={{0,8},{1,9},{2,10},{3,11},{4,12},{5,13},{6,14},{7,15},{8,0},{9,1},... | collective-permute-start | bytes 786440 | tf_op jit(solution)/shard_map/ppermute | solution.py:92
  26.7 1.1 compare_select_fusion
  27.8 0.7 pad_maximum_fusion.1
  28.6 1.4 %collective-permute-done.7.refs_9_ = bf16[256,512]{1,0:T(8,128)(2,1)S(1)} collective-permute-done((bf16[256,512]{1,0:T(8,128)(2,1)S(1)}, bf16[256,512]{1,0:T(8,128)(2,1)S(1)}, u32[]{:S(2)}, u32[]{:S(2)}) %collective-permute-start.7) | collective-permute-done | bytes 262176 | tf_op jit(solution)/shard_map/ppermute | solution.py:92
  29.9 1.6 %collective-permute-done.6.refs_8_ = bf16[256,512]{1,0:T(8,128)(2,1)S(1)} collective-permute-done((bf16[256,512]{1,0:T(8,128)(2,1)S(1)}, bf16[256,512]{1,0:T(8,128)(2,1)S(1)}, u32[]{:S(2)}, u32[]{:S(2)}) %collective-permute-start.6) | collective-permute-done | bytes 262176 | tf_op jit(solution)/shard_map/ppermute | solution.py:92
  31.5 2.6 %collective-permute-done.9.refs_11_ = bf16[256,512]{1,0:T(8,128)(2,1)S(1)} collective-permute-done((bf16[256,512]{1,0:T(8,128)(2,1)S(1)}, bf16[256,512]{1,0:T(8,128)(2,1)S(1)}, u32[]{:S(2)}, u32[]{:S(2)}) %collective-permute-start.9) | collective-permute-done | bytes 262176 | tf_op jit(solution)/shard_map/ppermute | solution.py:92
  34.1 1.2 collective-permute-done.8.refs_10_
  35.3 5.2 %all-to-all-start = ((bf16[4,128,1024]{2,1,0:T(8,128)(2,1)}), bf16[4,128,1024]{2,1,0:T(8,128)(2,1)S(1)}, u32[]{:S(2)}, u32[]{:S(2)}) async-start(bf16[4,128,1024]{2,1,0:T(8,128)(2,1)} %pad_maximum_fusion), calls=%async_computation | async-start | bytes 2097152 | tf_op jit(solution)/shard_map/all_to_all | solution.py:390
  40.5 1.5 %collective-permute-start.14 = (bf16[256,512]{1,0:T(8,128)(2,1)S(1)}, bf16[256,512]{1,0:T(8,128)(2,1)S(1)}, u32[]{:S(2)}, u32[]{:S(2)}) collective-permute-start(bf16[256,512]{1,0:T(8,128)(2,1)S(1)} %collective-permute-done.2.refs_4_), channel_id=1, source_target_pairs={{0,2},{1,3},{2,0},{3,1},{4,6},{5,7},{6,4},{7,5},{8,10},{9,11},{10,... | collective-permute-start | bytes 786440 | tf_op jit(solution)/shard_map/ppermute | solution.py:92
  42.0 0.9 collective-permute-start.15
  42.8 1.2 collective-permute-start.13
  44.5 1.6 %collective-permute-done.11.mate_cot_ref = bf16[144,512]{1,0:T(8,128)(2,1)S(1)} collective-permute-done((bf16[144,512]{1,0:T(8,128)(2,1)}, bf16[144,512]{1,0:T(8,128)(2,1)S(1)}, u32[]{:S(2)}, u32[]{:S(2)}) %collective-permute-start.11) | collective-permute-done | bytes 147488 | tf_op jit(solution)/shard_map/ppermute | solution.py:92
  46.1 3.6 %collective-permute-done.14.refs_15_ = bf16[256,512]{1,0:T(8,128)(2,1)S(1)} collective-permute-done((bf16[256,512]{1,0:T(8,128)(2,1)S(1)}, bf16[256,512]{1,0:T(8,128)(2,1)S(1)}, u32[]{:S(2)}, u32[]{:S(2)}) %collective-permute-start.14) | collective-permute-done | bytes 262176 | tf_op jit(solution)/shard_map/ppermute | solution.py:92
  49.7 1.8 %collective-permute-done.15.refs_16_ = bf16[256,512]{1,0:T(8,128)(2,1)} collective-permute-done((bf16[256,512]{1,0:T(8,128)(2,1)}, bf16[256,512]{1,0:T(8,128)(2,1)}, u32[]{:S(2)}, u32[]{:S(2)}) %collective-permute-start.15) | collective-permute-done | bytes 262176 | tf_op jit(solution)/shard_map/ppermute | solution.py:92
  51.5 2.9 %collective-permute-done.13.refs_14_ = bf16[256,512]{1,0:T(8,128)(2,1)} collective-permute-done((bf16[256,512]{1,0:T(8,128)(2,1)}, bf16[256,512]{1,0:T(8,128)(2,1)}, u32[]{:S(2)}, u32[]{:S(2)}) %collective-permute-start.13) | collective-permute-done | bytes 262176 | tf_op jit(solution)/shard_map/ppermute | solution.py:92
  55.0 1.3 collective-permute-start.17
  56.3 0.7 stack.87.refs_0_.chips_ref
  57.0 6.1 %project.1 = (bf16[3584,512]{1,0:T(8,128)(2,1)}, f32[2,128,512]{2,1,0:T(8,128)}) custom-call(s32[16]{0:T(128)} %stack.87.refs_0_.chips_ref, bf16[128,4096]{1,0:T(8,128)(2,1)} %refs_0_.1, bf16[128,4096]{1,0:T(8,128)(2,1)} %copy-done.2, bf16[256,512]{1,0:T(8,128)(2,1)} %copy-done.7, bf16[256,512]{1,0:T(8,128)(2,1)} %copy-done.13, bf16[256,512]{1,0:T(8,128)(2,1)} %copy-done.12, ...), custom_call_target="tpu_custom_call" | custom-call | tf_op jit(solution)/shard_map/project/pallas_call | solution.py:415
  63.1 2.2 %all-to-all-done.own_ref = bf16[4,128,1024]{2,1,0:T(8,128)(2,1)S(1)} async-done(((bf16[4,128,1024]{2,1,0:T(8,128)(2,1)}), bf16[4,128,1024]{2,1,0:T(8,128)(2,1)S(1)}, u32[]{:S(2)}, u32[]{:S(2)}) %all-to-all-start) | async-done | bytes 1048608 | tf_op jit(solution)/shard_map/all_to_all | solution.py:390
  65.3 4.2 %delta.1 = (bf16[272,512]{1,0:T(8,128)(2,1)}, bf16[512,512]{1,0:T(8,128)(2,1)}) custom-call(s32[16]{0:T(128)} %stack.87.refs_0_.chips_ref, s32[1]{0:T(128)} %bitcast.16.me_ref, bf16[144,512]{1,0:T(8,128)(2,1)} %get-tuple-element.110.own_cot_ref, bf16[144,512]{1,0:T(8,128)(2,1)} %copy-done.20, bf16[128,4096]{1,0:T(8,128)(2,1)} %refs_0_.1, ...), custom_call_target="tpu_custom_call" | custom-call | tf_op jit(solution)/shard_map/delta/pallas_call | solution.py:415
  70.0 1.5 %collective-permute-start.18 = (bf16[272,512]{1,0:T(8,128)(2,1)}, bf16[272,512]{1,0:T(8,128)(2,1)S(1)}, u32[]{:S(2)}, u32[]{:S(2)}) collective-permute-start(bf16[272,512]{1,0:T(8,128)(2,1)} %get-tuple-element.133.refs_0_), channel_id=1, source_target_pairs={{0,8},{1,9},{2,10},{3,11},{4,12},{5,13},{6,14},{7,15},{8,0},{9,1},... | collective-permute-start | bytes 835592 | tf_op jit(solution)/shard_map/ppermute | solution.py:92
  71.6 12.9 %collective-permute-done.19.refs_2_ = bf16[272,512]{1,0:T(8,128)(2,1)S(1)} collective-permute-done((bf16[272,512]{1,0:T(8,128)(2,1)}, bf16[272,512]{1,0:T(8,128)(2,1)S(1)}, u32[]{:S(2)}, u32[]{:S(2)}) %collective-permute-start.19) | collective-permute-done | bytes 278560 | tf_op jit(solution)/shard_map/ppermute | solution.py:92
  85.1 8.1 %collective-permute-done.21.refs_3_ = bf16[272,512]{1,0:T(8,128)(2,1)S(1)} collective-permute-done((bf16[272,512]{1,0:T(8,128)(2,1)S(1)}, bf16[272,512]{1,0:T(8,128)(2,1)S(1)}, u32[]{:S(2)}, u32[]{:S(2)}) %collective-permute-start.21) | collective-permute-done | bytes 278560 | tf_op jit(solution)/shard_map/ppermute | solution.py:92
  93.1 0.7 copy-done.5
  93.8 2.6 %select.28 = (bf16[128,512]{1,0:T(8,128)(2,1)}, bf16[128,512]{1,0:T(8,128)(2,1)}, bf16[128,512]{1,0:T(8,128)(2,1)}, bf16[128,512]{1,0:T(8,128)(2,1)}) custom-call(s32[1]{0:T(128)} %bitcast.16.me_ref, bf16[272,512]{1,0:T(8,128)(2,1)} %get-tuple-element.133.refs_0_, bf16[272,512]{1,0:T(8,128)(2,1)} %copy-done.4, bf16[272,512]{1,0:T(8,128)(2,1)} %copy-done.3, ...), custom_call_target="tpu_custom_call" | custom-call | tf_op jit(solution)/shard_map/select/pallas_call | solution.py:482
  96.5 1.5 %collective-permute-start.22 = (bf16[128,512]{1,0:T(8,128)(2,1)}, bf16[128,512]{1,0:T(8,128)(2,1)S(1)}, u32[]{:S(2)}, u32[]{:S(2)}) collective-permute-start(bf16[128,512]{1,0:T(8,128)(2,1)} %get-tuple-element.125), channel_id=1, source_target_pairs={{0,2},{1,3},{2,0},{3,1},{4,6},{5,7},{6,4},{7,5},{8,10},{9,11},{10,... | collective-permute-start | bytes 393224 | tf_op jit(solution)/shard_map/ppermute | solution.py:92
  98.0 1.0 collective-permute-start.23
  99.0 1.0 collective-permute-start.24
  100.0 3.9 %weight_grad.1 = bf16[1024,512]{1,0:T(8,128)(2,1)} custom-call(s32[1]{0:T(128)} %bitcast.16.me_ref, bf16[4,128,1024]{2,1,0:T(8,128)(2,1)} %copy-done, bf16[4,128,1024]{2,1,0:T(8,128)(2,1)} %copy-done.6, bf16[272,512]{1,0:T(8,128)(2,1)} %get-tuple-element.133.refs_0_, bf16[272,512]{1,0:T(8,128)(2,1)} %copy-done.4, bf16[272,512]{1,0:T(8,128)(2,1)} %copy-done.3, ...), custom_call_target="tpu_custom_call" | custom-call | tf_op jit(solution)/shard_map/weight_grad/pallas_call | solution.py:495
  103.9 2.1 %collective-permute-done.23.refs_2_ = bf16[128,512]{1,0:T(8,128)(2,1)S(1)} collective-permute-done((bf16[128,512]{1,0:T(8,128)(2,1)}, bf16[128,512]{1,0:T(8,128)(2,1)S(1)}, u32[]{:S(2)}, u32[]{:S(2)}) %collective-permute-start.23) | collective-permute-done | bytes 131104 | tf_op jit(solution)/shard_map/ppermute | solution.py:92
  106.0 3.6 %all-to-all-start.1 = ((bf16[8,128,512]{2,1,0:T(8,128)(2,1)}), bf16[8,128,512]{2,1,0:T(8,128)(2,1)S(1)}, u32[]{:S(2)}, u32[]{:S(2)}) async-start(bf16[8,128,512]{2,1,0:T(8,128)(2,1)} %bitcast.35), calls=%async_computation.1 | async-start | bytes 2097152 | tf_op jit(solution)/shard_map/all_to_all | solution.py:509
  110.0 1.9 %share.1 = (bf16[4,64,512]{2,1,0:T(8,128)(2,1)}, bf16[4,64,512]{2,1,0:T(8,128)(2,1)}) custom-call(s32[1]{0:T(128)} %bitcast.16.me_ref, bf16[128,512]{1,0:T(8,128)(2,1)} %get-tuple-element.124.refs_0_, bf16[128,512]{1,0:T(8,128)(2,1)} %copy-done.21, bf16[128,512]{1,0:T(8,128)(2,1)} %copy-done.22, bf16[128,512]{1,0:T(8,128)(2,1)} %copy-done.23), custom_call_target="tpu_custom_call" | custom-call | tf_op jit(solution)/shard_map/share/pallas_call | solution.py:518
  112.1 1.6 %collective-permute-done.25.mate_got_ref = bf16[4,64,512]{2,1,0:T(8,128)(2,1)S(1)} collective-permute-done((bf16[4,64,512]{2,1,0:T(8,128)(2,1)}, bf16[4,64,512]{2,1,0:T(8,128)(2,1)S(1)}, u32[]{:S(2)}, u32[]{:S(2)}) %collective-permute-start.25) | collective-permute-done | bytes 262176 | tf_op jit(solution)/shard_map/ppermute | solution.py:92
  113.7 0.7 copy-done.19
  114.5 11.1 %row_grad.1 = bf16[256,4096]{1,0:T(8,128)(2,1)} custom-call(s32[16]{0:T(128)} %stack.87.refs_0_.chips_ref, s32[1]{0:T(128)} %bitcast.16.me_ref, bf16[4,64,512]{2,1,0:T(8,128)(2,1)} %get-tuple-element.128.own_got_ref, bf16[4,64,512]{2,1,0:T(8,128)(2,1)} %copy-done.19, bf16[3584,512]{1,0:T(8,128)(2,1)} %get-tuple-element.130.refs_0_, ...), custom_call_target="tpu_custom_call" | custom-call | tf_op jit(solution)/shard_map/row_grad/pallas_call | solution.py:528
  125.6 1.0 copy-done.1
  126.6 2.2 %sum.1 = f32[128,1024]{1,0:T(8,128)} custom-call(bf16[4,2,128,512]{3,2,1,0:T(8,128)(2,1)} %bitcast.36), custom_call_target="tpu_custom_call" | custom-call | tf_op jit(solution)/shard_map/sum/pallas_call | solution.py:544
  (91 shorter events, 5.8 us)
Async XLA Ops:
  0.6 25.6 %copy-start.24 = (s32[1,4]{1,0:T(1,128)S(1)}, s32[1,4]{1,0:T(1,128)}, u32[]{:S(2)}) copy-start(s32[1,4]{1,0:T(1,128)} %param.9) | copy-start | bytes 52
  0.6 25.9 %copy-start.25 = (s32[128,1]{0,1:T(1,128)S(1)}, s32[128,1]{0,1:T(1,128)}, u32[]{:S(2)}) copy-start(s32[128,1]{0,1:T(1,128)} %param.8) | copy-start | bytes 1540
  0.7 26.0 %copy-start.26 = (s32[4]{0:T(128)S(1)}, s32[4]{0:T(128)}, u32[]{:S(2)}) copy-start(s32[4]{0:T(128)} %param.10) | copy-start | bytes 52
  0.7 1.9 %collective-permute-start = (bf16[128,1024]{1,0:T(8,128)(2,1)}, bf16[128,1024]{1,0:T(8,128)(2,1)S(1)}, u32[]{:S(2)}, u32[]{:S(2)}) collective-permute-start(bf16[128,1024]{1,0:T(8,128)(2,1)} %param.11), channel_id=1, source_target_pairs={{0,1},{1,0},{2,3},{3,2},{4,5},{5,4},{6,7},{7,6},{8,9},{9,8},{10,11... | collective-permute-start | bytes 786440 | tf_op jit(solution)/shard_map/ppermute | solution.py:92
  2.6 18.0 %collective-permute-start.1 = (bf16[128,4096]{1,0:T(8,128)(2,1)}, bf16[128,4096]{1,0:T(8,128)(2,1)S(1)}, u32[]{:S(2)}, u32[]{:S(2)}) collective-permute-start(bf16[128,4096]{1,0:T(8,128)(2,1)} %refs_0_.1), channel_id=1, source_target_pairs={{0,1},{1,0},{2,3},{3,2},{4,5},{5,4},{6,7},{7,6},{8,9},{9,8},{10,11... | collective-permute-start | bytes 3145736 | tf_op jit(solution)/shard_map/ppermute | solution.py:92
  4.0 31.2 %copy-start.7 = (bf16[256,512]{1,0:T(8,128)(2,1)}, bf16[256,512]{1,0:T(8,128)(2,1)S(1)}, u32[]{:S(2)}) copy-start(bf16[256,512]{1,0:T(8,128)(2,1)S(1)} %maximum_select_fusion.refs_3_) | copy-start | bytes 786436
  4.0 16.4 %collective-permute-start.5 = (bf16[256,512]{1,0:T(8,128)(2,1)S(1)}, bf16[256,512]{1,0:T(8,128)(2,1)S(1)}, u32[]{:S(2)}, u32[]{:S(2)}) collective-permute-start(bf16[256,512]{1,0:T(8,128)(2,1)S(1)} %maximum_select_fusion.refs_3_), channel_id=1, source_target_pairs={{0,16},{1,17},{2,18},{3,19},{4,20},{5,21},{6,22},{7,23},{8,24},{9,... | collective-permute-start | bytes 786440 | tf_op jit(solution)/shard_map/ppermute | solution.py:92
  7.8 12.7 %collective-permute-start.4 = (bf16[256,512]{1,0:T(8,128)(2,1)S(1)}, bf16[256,512]{1,0:T(8,128)(2,1)S(1)}, u32[]{:S(2)}, u32[]{:S(2)}) collective-permute-start(bf16[256,512]{1,0:T(8,128)(2,1)S(1)} %maximum_select_fusion.refs_3_), channel_id=1, source_target_pairs={{0,8},{1,9},{2,10},{3,11},{4,12},{5,13},{6,14},{7,15},{8,0},{9,1},... | collective-permute-start | bytes 786440 | tf_op jit(solution)/shard_map/ppermute | solution.py:92
  9.4 11.2 %collective-permute-start.3 = (bf16[256,512]{1,0:T(8,128)(2,1)S(1)}, bf16[256,512]{1,0:T(8,128)(2,1)S(1)}, u32[]{:S(2)}, u32[]{:S(2)}) collective-permute-start(bf16[256,512]{1,0:T(8,128)(2,1)S(1)} %maximum_select_fusion.refs_3_), channel_id=1, source_target_pairs={{0,2},{1,3},{2,0},{3,1},{4,6},{5,7},{6,4},{7,5},{8,10},{9,11},{10,... | collective-permute-start | bytes 786440 | tf_op jit(solution)/shard_map/ppermute | solution.py:92
  10.9 9.7 %collective-permute-start.2 = (bf16[256,512]{1,0:T(8,128)(2,1)S(1)}, bf16[256,512]{1,0:T(8,128)(2,1)S(1)}, u32[]{:S(2)}, u32[]{:S(2)}) collective-permute-start(bf16[256,512]{1,0:T(8,128)(2,1)S(1)} %maximum_select_fusion.refs_3_), channel_id=1, source_target_pairs={{0,4},{1,5},{2,6},{3,7},{4,0},{5,1},{6,2},{7,3},{8,12},{9,13},{10,... | collective-permute-start | bytes 786440 | tf_op jit(solution)/shard_map/ppermute | solution.py:92
  20.4 36.6 %copy-start.10 = (bf16[256,512]{1,0:T(8,128)(2,1)}, bf16[256,512]{1,0:T(8,128)(2,1)S(1)}, u32[]{:S(2)}) copy-start(bf16[256,512]{1,0:T(8,128)(2,1)S(1)} %collective-permute-done.5.refs_7_) | copy-start | bytes 786436
  20.6 36.4 %copy-start.11 = (bf16[256,512]{1,0:T(8,128)(2,1)}, bf16[256,512]{1,0:T(8,128)(2,1)S(1)}, u32[]{:S(2)}) copy-start(bf16[256,512]{1,0:T(8,128)(2,1)S(1)} %collective-permute-done.4.refs_6_) | copy-start | bytes 786436
  20.6 36.4 %copy-start.12 = (bf16[256,512]{1,0:T(8,128)(2,1)}, bf16[256,512]{1,0:T(8,128)(2,1)S(1)}, u32[]{:S(2)}) copy-start(bf16[256,512]{1,0:T(8,128)(2,1)S(1)} %collective-permute-done.3.refs_5_) | copy-start | bytes 786436
  20.6 36.4 %copy-start.13 = (bf16[256,512]{1,0:T(8,128)(2,1)}, bf16[256,512]{1,0:T(8,128)(2,1)S(1)}, u32[]{:S(2)}) copy-start(bf16[256,512]{1,0:T(8,128)(2,1)S(1)} %collective-permute-done.2.refs_4_) | copy-start | bytes 786436
  20.6 36.4 %copy-start.2 = (bf16[128,4096]{1,0:T(8,128)(2,1)}, bf16[128,4096]{1,0:T(8,128)(2,1)S(1)}, u32[]{:S(2)}) copy-start(bf16[128,4096]{1,0:T(8,128)(2,1)S(1)} %collective-permute-done.1.refs_2_.refs_1_) | copy-start | bytes 3145732
  20.6 9.3 %collective-permute-start.7 = (bf16[256,512]{1,0:T(8,128)(2,1)S(1)}, bf16[256,512]{1,0:T(8,128)(2,1)S(1)}, u32[]{:S(2)}, u32[]{:S(2)}) collective-permute-start(bf16[256,512]{1,0:T(8,128)(2,1)S(1)} %collective-permute-done.4.refs_6_), channel_id=1, source_target_pairs={{0,4},{1,5},{2,6},{3,7},{4,0},{5,1},{6,2},{7,3},{8,12},{9,13},{10,... | collective-permute-start | bytes 786440 | tf_op jit(solution)/shard_map/ppermute | solution.py:92
  22.3 9.2 %collective-permute-start.6 = (bf16[256,512]{1,0:T(8,128)(2,1)S(1)}, bf16[256,512]{1,0:T(8,128)(2,1)S(1)}, u32[]{:S(2)}, u32[]{:S(2)}) collective-permute-start(bf16[256,512]{1,0:T(8,128)(2,1)S(1)} %collective-permute-done.4.refs_6_), channel_id=1, source_target_pairs={{0,2},{1,3},{2,0},{3,1},{4,6},{5,7},{6,4},{7,5},{8,10},{9,11},{10,... | collective-permute-start | bytes 786440 | tf_op jit(solution)/shard_map/ppermute | solution.py:92
  23.7 7.8 %collective-permute-start.10 = (bf16[256,512]{1,0:T(8,128)(2,1)S(1)}, bf16[256,512]{1,0:T(8,128)(2,1)S(1)}, u32[]{:S(2)}, u32[]{:S(2)}) collective-permute-start(bf16[256,512]{1,0:T(8,128)(2,1)S(1)} %collective-permute-done.5.refs_7_), channel_id=1, source_target_pairs={{0,8},{1,9},{2,10},{3,11},{4,12},{5,13},{6,14},{7,15},{8,0},{9,1},... | collective-permute-start | bytes 786440 | tf_op jit(solution)/shard_map/ppermute | solution.py:92
  25.2 8.9 %collective-permute-start.9 = (bf16[256,512]{1,0:T(8,128)(2,1)S(1)}, bf16[256,512]{1,0:T(8,128)(2,1)S(1)}, u32[]{:S(2)}, u32[]{:S(2)}) collective-permute-start(bf16[256,512]{1,0:T(8,128)(2,1)S(1)} %collective-permute-done.5.refs_7_), channel_id=1, source_target_pairs={{0,4},{1,5},{2,6},{3,7},{4,0},{5,1},{6,2},{7,3},{8,12},{9,13},{10,... | collective-permute-start | bytes 786440 | tf_op jit(solution)/shard_map/ppermute | solution.py:92
  25.7 9.5 %collective-permute-start.8 = (bf16[256,512]{1,0:T(8,128)(2,1)S(1)}, bf16[256,512]{1,0:T(8,128)(2,1)}, u32[]{:S(2)}, u32[]{:S(2)}) collective-permute-start(bf16[256,512]{1,0:T(8,128)(2,1)S(1)} %collective-permute-done.5.refs_7_), channel_id=1, source_target_pairs={{0,2},{1,3},{2,0},{3,1},{4,6},{5,7},{6,4},{7,5},{8,10},{9,11},{10,... | collective-permute-start | bytes 786440 | tf_op jit(solution)/shard_map/ppermute | solution.py:92
  29.9 5.3 %copy-start.14 = (bf16[256,512]{1,0:T(8,128)(2,1)}, bf16[256,512]{1,0:T(8,128)(2,1)S(1)}, u32[]{:S(2)}) copy-start(bf16[256,512]{1,0:T(8,128)(2,1)S(1)} %collective-permute-done.7.refs_9_) | copy-start | bytes 786436
  35.3 30.0 %all-to-all-start = ((bf16[4,128,1024]{2,1,0:T(8,128)(2,1)}), bf16[4,128,1024]{2,1,0:T(8,128)(2,1)S(1)}, u32[]{:S(2)}, u32[]{:S(2)}) async-start(bf16[4,128,1024]{2,1,0:T(8,128)(2,1)} %pad_maximum_fusion), calls=%async_computation | async-start | bytes 2097152 | tf_op jit(solution)/shard_map/all_to_all | solution.py:390
  40.5 9.2 %collective-permute-start.14 = (bf16[256,512]{1,0:T(8,128)(2,1)S(1)}, bf16[256,512]{1,0:T(8,128)(2,1)S(1)}, u32[]{:S(2)}, u32[]{:S(2)}) collective-permute-start(bf16[256,512]{1,0:T(8,128)(2,1)S(1)} %collective-permute-done.2.refs_4_), channel_id=1, source_target_pairs={{0,2},{1,3},{2,0},{3,1},{4,6},{5,7},{6,4},{7,5},{8,10},{9,11},{10,... | collective-permute-start | bytes 786440 | tf_op jit(solution)/shard_map/ppermute | solution.py:92
  42.0 9.6 %collective-permute-start.15 = (bf16[256,512]{1,0:T(8,128)(2,1)}, bf16[256,512]{1,0:T(8,128)(2,1)}, u32[]{:S(2)}, u32[]{:S(2)}) collective-permute-start(bf16[256,512]{1,0:T(8,128)(2,1)} %collective-permute-done.8.refs_10_), channel_id=1, source_target_pairs={{0,4},{1,5},{2,6},{3,7},{4,0},{5,1},{6,2},{7,3},{8,12},{9,13},{10,... | collective-permute-start | bytes 786440 | tf_op jit(solution)/shard_map/ppermute | solution.py:92
  42.8 11.6 %collective-permute-start.13 = (bf16[256,512]{1,0:T(8,128)(2,1)}, bf16[256,512]{1,0:T(8,128)(2,1)}, u32[]{:S(2)}, u32[]{:S(2)}) collective-permute-start(bf16[256,512]{1,0:T(8,128)(2,1)} %copy-done.16), channel_id=1, source_target_pairs={{0,4},{1,5},{2,6},{3,7},{4,0},{5,1},{6,2},{7,3},{8,12},{9,13},{10,... | collective-permute-start | bytes 786440 | tf_op jit(solution)/shard_map/ppermute | solution.py:92
  44.0 10.5 %collective-permute-start.12 = (bf16[256,512]{1,0:T(8,128)(2,1)}, bf16[256,512]{1,0:T(8,128)(2,1)}, u32[]{:S(2)}, u32[]{:S(2)}) collective-permute-start(bf16[256,512]{1,0:T(8,128)(2,1)} %copy-done.16), channel_id=1, source_target_pairs={{0,2},{1,3},{2,0},{3,1},{4,6},{5,7},{6,4},{7,5},{8,10},{9,11},{10,... | collective-permute-start | bytes 786440 | tf_op jit(solution)/shard_map/ppermute | solution.py:92
  44.5 1.6 %collective-permute-start.11 = (bf16[144,512]{1,0:T(8,128)(2,1)}, bf16[144,512]{1,0:T(8,128)(2,1)S(1)}, u32[]{:S(2)}, u32[]{:S(2)}) collective-permute-start(bf16[144,512]{1,0:T(8,128)(2,1)} %get-tuple-element.78), channel_id=1, source_target_pairs={{0,1},{1,0},{2,3},{3,2},{4,5},{5,4},{6,7},{7,6},{8,9},{9,8},{10,11... | collective-permute-start | bytes 442376 | tf_op jit(solution)/shard_map/ppermute | solution.py:92
  46.1 19.2 %copy-start.20 = (bf16[144,512]{1,0:T(8,128)(2,1)}, bf16[144,512]{1,0:T(8,128)(2,1)S(1)}, u32[]{:S(2)}) copy-start(bf16[144,512]{1,0:T(8,128)(2,1)S(1)} %collective-permute-done.11.mate_cot_ref) | copy-start | bytes 442372
  49.7 7.2 %copy-start.18 = (bf16[256,512]{1,0:T(8,128)(2,1)}, bf16[256,512]{1,0:T(8,128)(2,1)S(1)}, u32[]{:S(2)}) copy-start(bf16[256,512]{1,0:T(8,128)(2,1)S(1)} %collective-permute-done.14.refs_15_) | copy-start | bytes 786436
  54.5 8.6 %collective-permute-start.16 = (bf16[256,512]{1,0:T(8,128)(2,1)}, bf16[256,512]{1,0:T(8,128)(2,1)}, u32[]{:S(2)}, u32[]{:S(2)}) collective-permute-start(bf16[256,512]{1,0:T(8,128)(2,1)} %copy-done.14), channel_id=1, source_target_pairs={{0,2},{1,3},{2,0},{3,1},{4,6},{5,7},{6,4},{7,5},{8,10},{9,11},{10,... | collective-permute-start | bytes 786440 | tf_op jit(solution)/shard_map/ppermute | solution.py:92
  55.0 8.1 %collective-permute-start.17 = (bf16[256,512]{1,0:T(8,128)(2,1)}, bf16[256,512]{1,0:T(8,128)(2,1)}, u32[]{:S(2)}, u32[]{:S(2)}) collective-permute-start(bf16[256,512]{1,0:T(8,128)(2,1)} %collective-permute-done.12.refs_13_), channel_id=1, source_target_pairs={{0,4},{1,5},{2,6},{3,7},{4,0},{5,1},{6,2},{7,3},{8,12},{9,13},{10,... | collective-permute-start | bytes 786440 | tf_op jit(solution)/shard_map/ppermute | solution.py:92
  65.3 34.7 %copy-start = (bf16[4,128,1024]{2,1,0:T(8,128)(2,1)}, bf16[4,128,1024]{2,1,0:T(8,128)(2,1)S(1)}, u32[]{:S(2)}) copy-start(bf16[4,128,1024]{2,1,0:T(8,128)(2,1)S(1)} %all-to-all-done.own_ref) | copy-start | bytes 3145732
  65.3 19.4 %collective-permute-start.20 = (bf16[4,128,1024]{2,1,0:T(8,128)(2,1)S(1)}, bf16[4,128,1024]{2,1,0:T(8,128)(2,1)S(1)}, u32[]{:S(2)}, u32[]{:S(2)}) collective-permute-start(bf16[4,128,1024]{2,1,0:T(8,128)(2,1)S(1)} %all-to-all-done.own_ref), channel_id=1, source_target_pairs={{0,1},{1,0},{2,3},{3,2},{4,5},{5,4},{6,7},{7,6},{8,9},{9,8},{10,11... | collective-permute-start | bytes 3145736 | tf_op jit(solution)/shard_map/ppermute | solution.py:92
  69.5 15.0 %collective-permute-start.19 = (bf16[272,512]{1,0:T(8,128)(2,1)}, bf16[272,512]{1,0:T(8,128)(2,1)S(1)}, u32[]{:S(2)}, u32[]{:S(2)}) collective-permute-start(bf16[272,512]{1,0:T(8,128)(2,1)} %get-tuple-element.133.refs_0_), channel_id=1, source_target_pairs={{0,16},{1,17},{2,18},{3,19},{4,20},{5,21},{6,22},{7,23},{8,24},{9,... | collective-permute-start | bytes 835592 | tf_op jit(solution)/shard_map/ppermute | solution.py:92
  70.0 14.7 %collective-permute-start.18 = (bf16[272,512]{1,0:T(8,128)(2,1)}, bf16[272,512]{1,0:T(8,128)(2,1)S(1)}, u32[]{:S(2)}, u32[]{:S(2)}) collective-permute-start(bf16[272,512]{1,0:T(8,128)(2,1)} %get-tuple-element.133.refs_0_), channel_id=1, source_target_pairs={{0,8},{1,9},{2,10},{3,11},{4,12},{5,13},{6,14},{7,15},{8,0},{9,1},... | collective-permute-start | bytes 835592 | tf_op jit(solution)/shard_map/ppermute | solution.py:92
  84.5 8.6 %copy-start.3 = (bf16[272,512]{1,0:T(8,128)(2,1)}, bf16[272,512]{1,0:T(8,128)(2,1)S(1)}, u32[]{:S(2)}) copy-start(bf16[272,512]{1,0:T(8,128)(2,1)S(1)} %collective-permute-done.19.refs_2_) | copy-start | bytes 835588
  84.7 8.5 %copy-start.4 = (bf16[272,512]{1,0:T(8,128)(2,1)}, bf16[272,512]{1,0:T(8,128)(2,1)S(1)}, u32[]{:S(2)}) copy-start(bf16[272,512]{1,0:T(8,128)(2,1)S(1)} %collective-permute-done.18.refs_1_) | copy-start | bytes 835588
  84.7 15.3 %copy-start.6 = (bf16[4,128,1024]{2,1,0:T(8,128)(2,1)}, bf16[4,128,1024]{2,1,0:T(8,128)(2,1)S(1)}, u32[]{:S(2)}) copy-start(bf16[4,128,1024]{2,1,0:T(8,128)(2,1)S(1)} %collective-permute-done.20.mate_ref) | copy-start | bytes 3145732
  84.7 8.4 %collective-permute-start.21 = (bf16[272,512]{1,0:T(8,128)(2,1)S(1)}, bf16[272,512]{1,0:T(8,128)(2,1)S(1)}, u32[]{:S(2)}, u32[]{:S(2)}) collective-permute-start(bf16[272,512]{1,0:T(8,128)(2,1)S(1)} %collective-permute-done.19.refs_2_), channel_id=1, source_target_pairs={{0,8},{1,9},{2,10},{3,11},{4,12},{5,13},{6,14},{7,15},{8,0},{9,1},... | collective-permute-start | bytes 835592 | tf_op jit(solution)/shard_map/ppermute | solution.py:92
  93.1 16.4 %copy-start.8 = (bf16[512,512]{1,0:T(8,128)(2,1)S(1)}, bf16[512,512]{1,0:T(8,128)(2,1)}, u32[]{:S(2)}) copy-start(bf16[512,512]{1,0:T(8,128)(2,1)} %get-tuple-element.131.refs_2_) | copy-start | bytes 1572868
  93.1 20.5 %collective-permute-start.26 = (bf16[3584,512]{1,0:T(8,128)(2,1)}, bf16[3584,512]{1,0:T(8,128)(2,1)}, u32[]{:S(2)}, u32[]{:S(2)}) collective-permute-start(bf16[3584,512]{1,0:T(8,128)(2,1)} %get-tuple-element.130.refs_0_), channel_id=1, source_target_pairs={{0,1},{1,0},{2,3},{3,2},{4,5},{5,4},{6,7},{7,6},{8,9},{9,8},{10,11... | collective-permute-start | bytes 11010056 | tf_op jit(solution)/shard_map/ppermute | solution.py:92
  96.5 7.5 %collective-permute-start.22 = (bf16[128,512]{1,0:T(8,128)(2,1)}, bf16[128,512]{1,0:T(8,128)(2,1)S(1)}, u32[]{:S(2)}, u32[]{:S(2)}) collective-permute-start(bf16[128,512]{1,0:T(8,128)(2,1)} %get-tuple-element.125), channel_id=1, source_target_pairs={{0,2},{1,3},{2,0},{3,1},{4,6},{5,7},{6,4},{7,5},{8,10},{9,11},{10,... | collective-permute-start | bytes 393224 | tf_op jit(solution)/shard_map/ppermute | solution.py:92
  98.0 8.0 %collective-permute-start.23 = (bf16[128,512]{1,0:T(8,128)(2,1)}, bf16[128,512]{1,0:T(8,128)(2,1)S(1)}, u32[]{:S(2)}, u32[]{:S(2)}) collective-permute-start(bf16[128,512]{1,0:T(8,128)(2,1)} %get-tuple-element.126), channel_id=1, source_target_pairs={{0,4},{1,5},{2,6},{3,7},{4,0},{5,1},{6,2},{7,3},{8,12},{9,13},{10,... | collective-permute-start | bytes 393224 | tf_op jit(solution)/shard_map/ppermute | solution.py:92
  99.0 7.0 %collective-permute-start.24 = (bf16[128,512]{1,0:T(8,128)(2,1)}, bf16[128,512]{1,0:T(8,128)(2,1)S(1)}, u32[]{:S(2)}, u32[]{:S(2)}) collective-permute-start(bf16[128,512]{1,0:T(8,128)(2,1)} %get-tuple-element.127), channel_id=1, source_target_pairs={{0,6},{1,7},{2,4},{3,5},{4,2},{5,3},{6,0},{7,1},{8,14},{9,15},{10,... | collective-permute-start | bytes 393224 | tf_op jit(solution)/shard_map/ppermute | solution.py:92
  103.9 6.1 %copy-start.21 = (bf16[128,512]{1,0:T(8,128)(2,1)}, bf16[128,512]{1,0:T(8,128)(2,1)S(1)}, u32[]{:S(2)}) copy-start(bf16[128,512]{1,0:T(8,128)(2,1)S(1)} %collective-permute-done.22.refs_1_) | copy-start | bytes 393220
  106.0 19.6 %all-to-all-start.1 = ((bf16[8,128,512]{2,1,0:T(8,128)(2,1)}), bf16[8,128,512]{2,1,0:T(8,128)(2,1)S(1)}, u32[]{:S(2)}, u32[]{:S(2)}) async-start(bf16[8,128,512]{2,1,0:T(8,128)(2,1)} %bitcast.35), calls=%async_computation.1 | async-start | bytes 2097152 | tf_op jit(solution)/shard_map/all_to_all | solution.py:509
  109.6 4.1 %collective-permute-start.27 = (bf16[512,512]{1,0:T(8,128)(2,1)S(1)}, bf16[512,512]{1,0:T(8,128)(2,1)S(1)}, u32[]{:S(2)}, u32[]{:S(2)}) collective-permute-start(bf16[512,512]{1,0:T(8,128)(2,1)S(1)} %copy-done.8), channel_id=1, source_target_pairs={{0,1},{1,0},{2,3},{3,2},{4,5},{5,4},{6,7},{7,6},{8,9},{9,8},{10,11... | collective-permute-start | bytes 1572872 | tf_op jit(solution)/shard_map/ppermute | solution.py:92
  111.9 1.7 %collective-permute-start.25 = (bf16[4,64,512]{2,1,0:T(8,128)(2,1)}, bf16[4,64,512]{2,1,0:T(8,128)(2,1)S(1)}, u32[]{:S(2)}, u32[]{:S(2)}) collective-permute-start(bf16[4,64,512]{2,1,0:T(8,128)(2,1)} %get-tuple-element.129), channel_id=1, source_target_pairs={{0,1},{1,0},{2,3},{3,2},{4,5},{5,4},{6,7},{7,6},{8,9},{9,8},{10,11... | collective-permute-start | bytes 786440 | tf_op jit(solution)/shard_map/ppermute | solution.py:92
  (9 other events, 19.9 us)

commit v14 on v13

--- a/solution.py
+++ b/solution.py
@@ -180,23 +180,24 @@
 def select_kernel(me_ref, *refs):
     deltas, sent, (held, sems) = refs[:4], refs[4:8], refs[8:]
     copies = fetch([(ref, held.at[n]) for n, ref in enumerate(deltas)], sems)
-    for copy in copies:
-        copy.wait()
     rows = (held.shape[1] - CODE_ROWS) // 2
     per_core = sent[0].shape[0] // 2
     per_chip = per_core // len(deltas)
-    iota = lax.broadcasted_iota(jnp.int32, (2 * per_core, 2 * rows), 0)
-    core = (iota >= per_core).astype(jnp.int32)
-    slot = iota - core * per_core
-    for out_ref, mask in zip(sent, PLANE_MASKS):
-        total = None
-        for n in range(len(deltas)):
-            code = held[n, 2 * rows :, : 2 * rows].astype(jnp.float32).astype(jnp.int32)
-            want = code[0:1, :] - ((me_ref[0] ^ mask) & -2)
-            hot = (core == want) & (slot == code[1:2, :] + n * per_chip)
-            part = dot(hot.astype(jnp.bfloat16), held[n, : 2 * rows, :], ((1,), (0,)))
-            total = part if total is None else total + part
-        out_ref[...] = total.astype(jnp.bfloat16)
+    iota = lax.broadcasted_iota(jnp.int32, (8 * per_chip, 2 * rows), 0)
+    block = lax.shift_right_logical(iota, per_chip.bit_length() - 1)
+    slot = iota & (per_chip - 1)
+    wanted = ((me_ref[0] & -2) ^ (block & -2)) | (block & 1)
+    for n in range(len(deltas)):
+        copies[n].wait()
+        code = held[n, 2 * rows :, : 2 * rows].astype(jnp.float32).astype(jnp.int32)
+        hot = (wanted == code[0:1, :]) & (slot == code[1:2, :])
+        found = dot(hot.astype(jnp.bfloat16), held[n, : 2 * rows, :], ((1,), (0,)))
+        found = found.astype(jnp.bfloat16)
+        for place in range(8):
+            at = place % 2 * per_core + n * per_chip
+            sent[place // 2][at : at + per_chip, :] = found[
+                place * per_chip : (place + 1) * per_chip, :
+            ]
 
 
 def share_kernel(me_ref, *refs):
@@ -244,7 +245,7 @@
 
 
 def row_grad_kernel(chips_ref, me_ref, own_got_ref, mate_got_ref, *refs):
-    weight_refs, (out_ref, weights, out, rows_ref, held, sems) = refs[:4], refs[4:]
+    weight_refs, (out_ref, weights, out, rows_ref, sems) = refs[:4], refs[4:]
     chips, count, half = own_got_ref.shape
     block = count // 4
     depth = half // 2
@@ -266,16 +267,14 @@
             place = lax.shift_right_logical((me_ref[0] ^ mask) & 6, 1)
             for n in range(4):
                 at = pl.multiple_of(((level ^ n) * chips + place) * block, block)
-                rows = got_ref[chip, n * block : (n + 1) * block, :]
-                held[pl.ds(at, block), :] = rows.astype(jnp.float32)
-        rows_ref[side] = held[...].T.astype(jnp.bfloat16)
+                rows_ref[side, pl.ds(at, block), :] = got_ref[chip, n * block : (n + 1) * block, :]
     written = []
     for n in range(pieces):
         for copy in copies[2 * n : 2 * n + 2]:
             copy.wait()
-        total = dot(rows_of(weights.at[0], n)[...], rows_ref[0], ((1,), (0,)))
-        total += dot(rows_of(weights.at[1], n)[...], rows_ref[1], ((1,), (0,)))
-        out[n] = total.T.astype(jnp.bfloat16)
+        total = dot(rows_ref[0], rows_of(weights.at[0], n)[...], ((1,), (1,)))
+        total += dot(rows_ref[1], rows_of(weights.at[1], n)[...], ((1,), (1,)))
+        out[n] = total.astype(jnp.bfloat16)
         at = pl.multiple_of(chips_ref[n] * depth, depth)
         copy = pltpu.make_async_copy(
             out.at[n], out_ref.at[:, pl.ds(at, depth)], sems.at[2 * pieces + n]
@@ -310,6 +309,11 @@
 
 SCALAR = pl.BlockSpec(memory_space=pltpu.SMEM)
 PARAMS = pltpu.CompilerParams(vmem_limit_bytes=VMEM_LIMIT)
+COST = pl.CostEstimate(flops=1024, bytes_accessed=1024, transcendentals=0)
+
+
+def grant(mebibytes):
+    return pltpu.CompilerParams(vmem_limit_bytes=mebibytes << 20)
 
 
 def per_device_paired(tokens, key_cot, routes, counts, widths, key_weight):
@@ -426,6 +430,7 @@
                 pltpu.SemaphoreType.DMA((4 * count,)),
             ],
             compiler_params=PARAMS,
+            cost_estimate=COST,
             name=name,
         )(*inputs)
 
@@ -443,10 +448,9 @@
             both | X | Y: swap(have[both | X], Y),
         }
     )
-    mate_cot, own_cot, own_features, begun, first_weight = after_round(
+    mate_cot, own_cot, begun, first_weight = after_round(
         mate_cot=mate_cot,
         own_cot=own_cot,
-        own_features=own_features,
         begun=begun,
         first_weight=first_weight,
     )
@@ -533,11 +537,10 @@
         scratch_shapes=[
             pltpu.VMEM((2, width_model, half_cols), jnp.bfloat16),
             pltpu.VMEM((chips, receive, depth), jnp.bfloat16),
-            pltpu.VMEM((2, half_cols, receive), jnp.bfloat16),
-            pltpu.VMEM((receive, half_cols), jnp.float32),
+            pltpu.VMEM((2, receive, half_cols), jnp.bfloat16),
             pltpu.SemaphoreType.DMA((3 * chips,)),
         ],
-        compiler_params=PARAMS,
+        compiler_params=grant(56),
         name="row_grad",
     )(order, me_scalar, own_got, mate_got, first_weight, mate_first, last_weight, mate_last)
 
@@ -546,7 +549,7 @@
         out_shape=jax.ShapeDtypeStruct((shard, cols), jnp.float32),
         in_specs=vmem(1),
         out_specs=vmem(1)[0],
-        compiler_params=PARAMS,
+        compiler_params=grant(16),
         name="sum",
     )(after(parts, row_grads))
     return (row_grads, key_grad)

time: 129 us -> 148 us (1.15)
  blocking collectives: 0 us -> 29.8 us
  starting transfers between devices: 36.2 us -> 30.5 us
  Pallas kernels: 31.9 us -> 29.5 us
    all_to_all x0 -> x1, blocking collectives: none -> 29.8 us  [per_device_paired(): lax.all_to_all(by_level, 'dp', split_axis=0, concat_axis=0, axis_index_gr...]
    all_to_all x1 -> x0, starting transfers between devices: 5.22 us -> none  [per_device_paired(): lax.all_to_all(by_level, 'dp', split_axis=0, concat_axis=0, axis_index_gr...]
    all_to_all x1 -> x0, waiting for transfers between devices: 2.17 us -> none  [per_device_paired(): lax.all_to_all(by_level, 'dp', split_axis=0, concat_axis=0, axis_index_gr...]
    ppermute x28, waiting for transfers between devices: 48.5 us -> 50.4 us  [swap(): return lax.ppermute(value, 'dp', [(i, i ^ mask) for i in range(size)])]
  transfers between devices with their start and end apart: 30 -> 29, of which waited for: 17 -> 14; matrix products, arithmetic and copies ran while one was open for 5% -> 4% of each run, Pallas kernels for 23% -> 19%
where the time goes in v14:
time: 148 us
  waiting for transfers between devices  50.4 us (34%)
  starting transfers between devices  30.5 us (21%)
  blocking collectives  29.8 us (20%)
  Pallas kernels  29.5 us (20%)
  local copies, waits for them, and re-layouts  4.53 us (3%)
  other arithmetic  2.43 us (2%)
    ppermute x28, waiting for transfers between devices, swap(): return lax.ppermute(value, 'dp', [(i, i ^ mask) for i in range(size)])  50.4 us
    all_to_all x1, blocking collectives, per_device_paired(): lax.all_to_all(by_level, 'dp', split_axis=0, concat_axis=0, axis_index_gr...  29.8 us
    ppermute x28, starting transfers between devices, swap(): return lax.ppermute(value, 'dp', [(i, i ^ mask) for i in range(size)])  26.9 us
    pallas_call x1, Pallas kernels, per_device_paired(): pl.pallas_call(row_grad_kernel, out_shape=jax.ShapeDtypeStruct((receive,...  10.4 us
    pallas_call x2, Pallas kernels, project(): pl.pallas_call(kernel, out_shape=(*results, jax.ShapeDtypeStruct((count *...  9.89 us
    pallas_call x1, Pallas kernels, per_device_paired(): pl.pallas_call(weight_grad_kernel, out_shape=jax.ShapeDtypeStruct((wide,...  3.8 us
    all_to_all x1, starting transfers between devices, per_device_paired(): lax.all_to_all(after(terms, *got).reshape(PLANE, shard, half_cols), 'dp',...  3.56 us
  transfers between devices with their start and end apart: 29, of which 14 were waited for; matrix products, arithmetic and copies ran while one was open for 4% of the time, Pallas kernels for 19%

profile of v14, /device:TPU:0, one launch (start us, length us, event | category | flops | bytes accessed | tf_op | source)
XLA Modules:
  0.0 148.0 jit_solution(8985895125511919582)
XLA Ops:
  0.7 0.5 collective-permute-start
  1.2 1.4 collective-permute-done
  2.9 1.0 fusion.11
  4.0 3.8 %collective-permute-start.5 = (bf16[256,512]{1,0:T(8,128)(2,1)S(1)}, bf16[256,512]{1,0:T(8,128)(2,1)}, u32[]{:S(2)}, u32[]{:S(2)}) collective-permute-start(bf16[256,512]{1,0:T(8,128)(2,1)S(1)} %maximum_select_fusion.refs_3_), channel_id=1, source_target_pairs={{0,16},{1,17},{2,18},{3,19},{4,20},{5,21},{6,22},{7,23},{8,24},{9,... | collective-permute-start | bytes 786440 | tf_op jit(solution)/shard_map/ppermute | solution.py:92
  7.8 1.6 %collective-permute-start.4 = (bf16[256,512]{1,0:T(8,128)(2,1)S(1)}, bf16[256,512]{1,0:T(8,128)(2,1)}, u32[]{:S(2)}, u32[]{:S(2)}) collective-permute-start(bf16[256,512]{1,0:T(8,128)(2,1)S(1)} %maximum_select_fusion.refs_3_), channel_id=1, source_target_pairs={{0,8},{1,9},{2,10},{3,11},{4,12},{5,13},{6,14},{7,15},{8,0},{9,1},... | collective-permute-start | bytes 786440 | tf_op jit(solution)/shard_map/ppermute | solution.py:92
  9.4 1.5 %collective-permute-start.3 = (bf16[256,512]{1,0:T(8,128)(2,1)S(1)}, bf16[256,512]{1,0:T(8,128)(2,1)}, u32[]{:S(2)}, u32[]{:S(2)}) collective-permute-start(bf16[256,512]{1,0:T(8,128)(2,1)S(1)} %maximum_select_fusion.refs_3_), channel_id=1, source_target_pairs={{0,2},{1,3},{2,0},{3,1},{4,6},{5,7},{6,4},{7,5},{8,10},{9,11},{10,... | collective-permute-start | bytes 786440 | tf_op jit(solution)/shard_map/ppermute | solution.py:92
  10.9 1.5 %collective-permute-start.2 = (bf16[256,512]{1,0:T(8,128)(2,1)S(1)}, bf16[256,512]{1,0:T(8,128)(2,1)}, u32[]{:S(2)}, u32[]{:S(2)}) collective-permute-start(bf16[256,512]{1,0:T(8,128)(2,1)S(1)} %maximum_select_fusion.refs_3_), channel_id=1, source_target_pairs={{0,4},{1,5},{2,6},{3,7},{4,0},{5,1},{6,2},{7,3},{8,12},{9,13},{10,... | collective-permute-start | bytes 786440 | tf_op jit(solution)/shard_map/ppermute | solution.py:92
  12.4 1.3 slice_bitcast_fusion.3
  13.8 6.6 %collective-permute-done.5.refs_7_ = bf16[256,512]{1,0:T(8,128)(2,1)} collective-permute-done((bf16[256,512]{1,0:T(8,128)(2,1)S(1)}, bf16[256,512]{1,0:T(8,128)(2,1)}, u32[]{:S(2)}, u32[]{:S(2)}) %collective-permute-start.5) | collective-permute-done | bytes 262176 | tf_op jit(solution)/shard_map/ppermute | solution.py:92
  20.7 1.6 %collective-permute-start.7 = (bf16[256,512]{1,0:T(8,128)(2,1)}, bf16[256,512]{1,0:T(8,128)(2,1)S(1)}, u32[]{:S(2)}, u32[]{:S(2)}) collective-permute-start(bf16[256,512]{1,0:T(8,128)(2,1)} %collective-permute-done.4.refs_6_), channel_id=1, source_target_pairs={{0,4},{1,5},{2,6},{3,7},{4,0},{5,1},{6,2},{7,3},{8,12},{9,13},{10,... | collective-permute-start | bytes 786440 | tf_op jit(solution)/shard_map/ppermute | solution.py:92
  22.3 1.5 %collective-permute-start.6 = (bf16[256,512]{1,0:T(8,128)(2,1)}, bf16[256,512]{1,0:T(8,128)(2,1)S(1)}, u32[]{:S(2)}, u32[]{:S(2)}) collective-permute-start(bf16[256,512]{1,0:T(8,128)(2,1)} %collective-permute-done.4.refs_6_), channel_id=1, source_target_pairs={{0,2},{1,3},{2,0},{3,1},{4,6},{5,7},{6,4},{7,5},{8,10},{9,11},{10,... | collective-permute-start | bytes 786440 | tf_op jit(solution)/shard_map/ppermute | solution.py:92
  23.8 1.4 collective-permute-start.10
  25.8 0.5 collective-permute-start.8
  26.8 1.1 compare_select_fusion
  27.9 0.7 pad_maximum_fusion.1
  28.6 1.6 %collective-permute-done.7.refs_9_ = bf16[256,512]{1,0:T(8,128)(2,1)S(1)} collective-permute-done((bf16[256,512]{1,0:T(8,128)(2,1)}, bf16[256,512]{1,0:T(8,128)(2,1)S(1)}, u32[]{:S(2)}, u32[]{:S(2)}) %collective-permute-start.7) | collective-permute-done | bytes 262176 | tf_op jit(solution)/shard_map/ppermute | solution.py:92
  30.2 1.6 %collective-permute-done.6.refs_8_ = bf16[256,512]{1,0:T(8,128)(2,1)S(1)} collective-permute-done((bf16[256,512]{1,0:T(8,128)(2,1)}, bf16[256,512]{1,0:T(8,128)(2,1)S(1)}, u32[]{:S(2)}, u32[]{:S(2)}) %collective-permute-start.6) | collective-permute-done | bytes 262176 | tf_op jit(solution)/shard_map/ppermute | solution.py:92
  31.8 2.7 %collective-permute-done.9.refs_11_ = bf16[256,512]{1,0:T(8,128)(2,1)} collective-permute-done((bf16[256,512]{1,0:T(8,128)(2,1)}, bf16[256,512]{1,0:T(8,128)(2,1)}, u32[]{:S(2)}, u32[]{:S(2)}) %collective-permute-start.9) | collective-permute-done | bytes 262176 | tf_op jit(solution)/shard_map/ppermute | solution.py:92
  34.5 1.0 collective-permute-done.8.refs_10_
  35.5 29.8 %all_to_all.10.own_ref = bf16[4,128,1024]{2,1,0:T(8,128)(2,1)S(1)} all-to-all(bf16[4,128,1024]{2,1,0:T(8,128)(2,1)S(1)} %pad_maximum_fusion), channel_id=1, replica_groups={{0,8,16,24},{1,9,17,25},{2,10,18,26},{3,11,19,27},{4,12,20,28},{5,13,21..., dimensions={0} | all-to-all | bytes 2097152 | tf_op jit(solution)/shard_map/all_to_all | solution.py:394
  65.8 1.5 %collective-permute-start.14 = (bf16[256,512]{1,0:T(8,128)(2,1)}, bf16[256,512]{1,0:T(8,128)(2,1)S(1)}, u32[]{:S(2)}, u32[]{:S(2)}) collective-permute-start(bf16[256,512]{1,0:T(8,128)(2,1)} %collective-permute-done.2.refs_4_), channel_id=1, source_target_pairs={{0,2},{1,3},{2,0},{3,1},{4,6},{5,7},{6,4},{7,5},{8,10},{9,11},{10,... | collective-permute-start | bytes 786440 | tf_op jit(solution)/shard_map/ppermute | solution.py:92
  67.3 0.6 collective-permute-start.15
  67.9 1.4 collective-permute-start.13
  69.3 0.5 collective-permute-start.12
  69.9 5.3 %collective-permute-done.14.refs_15_ = bf16[256,512]{1,0:T(8,128)(2,1)S(1)} collective-permute-done((bf16[256,512]{1,0:T(8,128)(2,1)}, bf16[256,512]{1,0:T(8,128)(2,1)S(1)}, u32[]{:S(2)}, u32[]{:S(2)}) %collective-permute-start.14) | collective-permute-done | bytes 262176 | tf_op jit(solution)/shard_map/ppermute | solution.py:92
  75.2 1.6 %collective-permute-done.15.refs_16_ = bf16[256,512]{1,0:T(8,128)(2,1)} collective-permute-done((bf16[256,512]{1,0:T(8,128)(2,1)}, bf16[256,512]{1,0:T(8,128)(2,1)}, u32[]{:S(2)}, u32[]{:S(2)}) %collective-permute-start.15) | collective-permute-done | bytes 262176 | tf_op jit(solution)/shard_map/ppermute | solution.py:92
  76.8 4.4 %collective-permute-done.13.refs_14_ = bf16[256,512]{1,0:T(8,128)(2,1)} collective-permute-done((bf16[256,512]{1,0:T(8,128)(2,1)}, bf16[256,512]{1,0:T(8,128)(2,1)}, u32[]{:S(2)}, u32[]{:S(2)}) %collective-permute-start.13) | collective-permute-done | bytes 262176 | tf_op jit(solution)/shard_map/ppermute | solution.py:92
  81.3 0.5 collective-permute-start.16
  81.8 0.6 collective-permute-start.17
  82.4 0.6 stack.87.refs_0_.chips_ref
  83.0 6.1 %project.1 = (bf16[3584,512]{1,0:T(8,128)(2,1)}, f32[2,128,512]{2,1,0:T(8,128)}) custom-call(s32[16]{0:T(128)} %stack.87.refs_0_.chips_ref, bf16[128,4096]{1,0:T(8,128)(2,1)} %refs_0_.1, bf16[128,4096]{1,0:T(8,128)(2,1)} %copy-done.1, bf16[256,512]{1,0:T(8,128)(2,1)} %copy-done.6, bf16[256,512]{1,0:T(8,128)(2,1)} %collective-permute-done.2.refs_4_, ...), custom_call_target="tpu_custom_call" | custom-call | flops 1024 | bytes 1024 | tf_op jit(solution)/shard_map/project/pallas_call | solution.py:419
  89.1 3.8 %delta.1 = (bf16[272,512]{1,0:T(8,128)(2,1)}, bf16[512,512]{1,0:T(8,128)(2,1)}) custom-call(s32[16]{0:T(128)} %stack.87.refs_0_.chips_ref, s32[1]{0:T(128)} %bitcast.16.me_ref, bf16[144,512]{1,0:T(8,128)(2,1)} %get-tuple-element.108.own_cot_ref, bf16[144,512]{1,0:T(8,128)(2,1)} %copy-done.13, bf16[128,4096]{1,0:T(8,128)(2,1)} %refs_0_.1, ...), custom_call_target="tpu_custom_call" | custom-call | flops 1024 | bytes 1024 | tf_op jit(solution)/shard_map/delta/pallas_call | solution.py:419
  93.3 1.8 %collective-permute-start.18 = (bf16[272,512]{1,0:T(8,128)(2,1)}, bf16[272,512]{1,0:T(8,128)(2,1)S(1)}, u32[]{:S(2)}, u32[]{:S(2)}) collective-permute-start(bf16[272,512]{1,0:T(8,128)(2,1)} %get-tuple-element.131.refs_0_), channel_id=1, source_target_pairs={{0,8},{1,9},{2,10},{3,11},{4,12},{5,13},{6,14},{7,15},{8,0},{9,1},... | collective-permute-start | bytes 835592 | tf_op jit(solution)/shard_map/ppermute | solution.py:92
  95.1 11.7 %collective-permute-done.19.refs_2_ = bf16[272,512]{1,0:T(8,128)(2,1)S(1)} collective-permute-done((bf16[272,512]{1,0:T(8,128)(2,1)}, bf16[272,512]{1,0:T(8,128)(2,1)S(1)}, u32[]{:S(2)}, u32[]{:S(2)}) %collective-permute-start.19) | collective-permute-done | bytes 278560 | tf_op jit(solution)/shard_map/ppermute | solution.py:92
  106.8 8.6 %collective-permute-done.21.refs_3_ = bf16[272,512]{1,0:T(8,128)(2,1)S(1)} collective-permute-done((bf16[272,512]{1,0:T(8,128)(2,1)S(1)}, bf16[272,512]{1,0:T(8,128)(2,1)S(1)}, u32[]{:S(2)}, u32[]{:S(2)}) %collective-permute-start.21) | collective-permute-done | bytes 278560 | tf_op jit(solution)/shard_map/ppermute | solution.py:92
  115.4 0.7 copy-done.4
  116.1 2.5 %select.28 = (bf16[128,512]{1,0:T(8,128)(2,1)}, bf16[128,512]{1,0:T(8,128)(2,1)}, bf16[128,512]{1,0:T(8,128)(2,1)}, bf16[128,512]{1,0:T(8,128)(2,1)}) custom-call(s32[1]{0:T(128)} %bitcast.16.me_ref, bf16[272,512]{1,0:T(8,128)(2,1)} %get-tuple-element.131.refs_0_, bf16[272,512]{1,0:T(8,128)(2,1)} %copy-done.3, bf16[272,512]{1,0:T(8,128)(2,1)} %copy-done.2, ...), custom_call_target="tpu_custom_call" | custom-call | tf_op jit(solution)/shard_map/select/pallas_call | solution.py:486
  118.6 1.5 %collective-permute-start.22 = (bf16[128,512]{1,0:T(8,128)(2,1)}, bf16[128,512]{1,0:T(8,128)(2,1)S(1)}, u32[]{:S(2)}, u32[]{:S(2)}) collective-permute-start(bf16[128,512]{1,0:T(8,128)(2,1)} %get-tuple-element.123), channel_id=1, source_target_pairs={{0,2},{1,3},{2,0},{3,1},{4,6},{5,7},{6,4},{7,5},{8,10},{9,11},{10,... | collective-permute-start | bytes 393224 | tf_op jit(solution)/shard_map/ppermute | solution.py:92
  120.1 1.4 collective-permute-start.23
  121.5 0.6 collective-permute-start.24
  122.2 3.8 %weight_grad.1 = bf16[1024,512]{1,0:T(8,128)(2,1)} custom-call(s32[1]{0:T(128)} %bitcast.16.me_ref, bf16[4,128,1024]{2,1,0:T(8,128)(2,1)} %copy-done, bf16[4,128,1024]{2,1,0:T(8,128)(2,1)} %copy-done.5, bf16[272,512]{1,0:T(8,128)(2,1)} %get-tuple-element.131.refs_0_, bf16[272,512]{1,0:T(8,128)(2,1)} %copy-done.3, bf16[272,512]{1,0:T(8,128)(2,1)} %copy-done.2, ...), custom_call_target="tpu_custom_call" | custom-call | tf_op jit(solution)/shard_map/weight_grad/pallas_call | solution.py:499
  126.0 2.1 %collective-permute-done.23.refs_2_ = bf16[128,512]{1,0:T(8,128)(2,1)S(1)} collective-permute-done((bf16[128,512]{1,0:T(8,128)(2,1)}, bf16[128,512]{1,0:T(8,128)(2,1)S(1)}, u32[]{:S(2)}, u32[]{:S(2)}) %collective-permute-start.23) | collective-permute-done | bytes 131104 | tf_op jit(solution)/shard_map/ppermute | solution.py:92
  128.1 3.6 %all-to-all-start.1 = ((bf16[8,128,512]{2,1,0:T(8,128)(2,1)}), bf16[8,128,512]{2,1,0:T(8,128)(2,1)S(1)}, u32[]{:S(2)}, u32[]{:S(2)}) async-start(bf16[8,128,512]{2,1,0:T(8,128)(2,1)} %bitcast.36), calls=%async_computation.1 | async-start | bytes 2097152 | tf_op jit(solution)/shard_map/all_to_all | solution.py:513
  132.1 1.9 %share.1 = (bf16[4,64,512]{2,1,0:T(8,128)(2,1)}, bf16[4,64,512]{2,1,0:T(8,128)(2,1)}) custom-call(s32[1]{0:T(128)} %bitcast.16.me_ref, bf16[128,512]{1,0:T(8,128)(2,1)} %get-tuple-element.122.refs_0_, bf16[128,512]{1,0:T(8,128)(2,1)} %copy-done.14, bf16[128,512]{1,0:T(8,128)(2,1)} %copy-done.15, bf16[128,512]{1,0:T(8,128)(2,1)} %copy-done.16), custom_call_target="tpu_custom_call" | custom-call | tf_op jit(solution)/shard_map/share/pallas_call | solution.py:522
  134.2 1.6 %collective-permute-done.25.mate_got_ref = bf16[4,64,512]{2,1,0:T(8,128)(2,1)S(1)} collective-permute-done((bf16[4,64,512]{2,1,0:T(8,128)(2,1)}, bf16[4,64,512]{2,1,0:T(8,128)(2,1)S(1)}, u32[]{:S(2)}, u32[]{:S(2)}) %collective-permute-start.25) | collective-permute-done | bytes 262176 | tf_op jit(solution)/shard_map/ppermute | solution.py:92
  135.8 0.7 copy-done.12
  136.7 10.4 %row_grad.1 = bf16[256,4096]{1,0:T(8,128)(2,1)} custom-call(s32[16]{0:T(128)} %stack.87.refs_0_.chips_ref, s32[1]{0:T(128)} %bitcast.16.me_ref, bf16[4,64,512]{2,1,0:T(8,128)(2,1)} %get-tuple-element.126.own_got_ref, bf16[4,64,512]{2,1,0:T(8,128)(2,1)} %copy-done.12, bf16[3584,512]{1,0:T(8,128)(2,1)} %get-tuple-element.128.refs_0_, ...), custom_call_target="tpu_custom_call" | custom-call | tf_op jit(solution)/shard_map/row_grad/pallas_call | solution.py:532
  147.1 0.9 sum.1
  (76 shorter events, 3.5 us)
Async XLA Ops:
  0.6 25.7 %copy-start.17 = (s32[1,4]{1,0:T(1,128)S(1)}, s32[1,4]{1,0:T(1,128)}, u32[]{:S(2)}) copy-start(s32[1,4]{1,0:T(1,128)} %param.9) | copy-start | bytes 52
  0.6 25.9 %copy-start.18 = (s32[128,1]{0,1:T(1,128)S(1)}, s32[128,1]{0,1:T(1,128)}, u32[]{:S(2)}) copy-start(s32[128,1]{0,1:T(1,128)} %param.8) | copy-start | bytes 1540
  0.7 26.0 %copy-start.19 = (s32[4]{0:T(128)S(1)}, s32[4]{0:T(128)}, u32[]{:S(2)}) copy-start(s32[4]{0:T(128)} %param.10) | copy-start | bytes 52
  0.7 1.9 %collective-permute-start = (bf16[128,1024]{1,0:T(8,128)(2,1)}, bf16[128,1024]{1,0:T(8,128)(2,1)S(1)}, u32[]{:S(2)}, u32[]{:S(2)}) collective-permute-start(bf16[128,1024]{1,0:T(8,128)(2,1)} %param.11), channel_id=1, source_target_pairs={{0,1},{1,0},{2,3},{3,2},{4,5},{5,4},{6,7},{7,6},{8,9},{9,8},{10,11... | collective-permute-start | bytes 786440 | tf_op jit(solution)/shard_map/ppermute | solution.py:92
  2.6 18.1 %collective-permute-start.1 = (bf16[128,4096]{1,0:T(8,128)(2,1)}, bf16[128,4096]{1,0:T(8,128)(2,1)S(1)}, u32[]{:S(2)}, u32[]{:S(2)}) collective-permute-start(bf16[128,4096]{1,0:T(8,128)(2,1)} %refs_0_.1), channel_id=1, source_target_pairs={{0,1},{1,0},{2,3},{3,2},{4,5},{5,4},{6,7},{7,6},{8,9},{9,8},{10,11... | collective-permute-start | bytes 3145736 | tf_op jit(solution)/shard_map/ppermute | solution.py:92
  4.0 61.3 %copy-start.6 = (bf16[256,512]{1,0:T(8,128)(2,1)}, bf16[256,512]{1,0:T(8,128)(2,1)S(1)}, u32[]{:S(2)}) copy-start(bf16[256,512]{1,0:T(8,128)(2,1)S(1)} %maximum_select_fusion.refs_3_) | copy-start | bytes 786436
  4.0 16.5 %collective-permute-start.5 = (bf16[256,512]{1,0:T(8,128)(2,1)S(1)}, bf16[256,512]{1,0:T(8,128)(2,1)}, u32[]{:S(2)}, u32[]{:S(2)}) collective-permute-start(bf16[256,512]{1,0:T(8,128)(2,1)S(1)} %maximum_select_fusion.refs_3_), channel_id=1, source_target_pairs={{0,16},{1,17},{2,18},{3,19},{4,20},{5,21},{6,22},{7,23},{8,24},{9,... | collective-permute-start | bytes 786440 | tf_op jit(solution)/shard_map/ppermute | solution.py:92
  7.8 12.8 %collective-permute-start.4 = (bf16[256,512]{1,0:T(8,128)(2,1)S(1)}, bf16[256,512]{1,0:T(8,128)(2,1)}, u32[]{:S(2)}, u32[]{:S(2)}) collective-permute-start(bf16[256,512]{1,0:T(8,128)(2,1)S(1)} %maximum_select_fusion.refs_3_), channel_id=1, source_target_pairs={{0,8},{1,9},{2,10},{3,11},{4,12},{5,13},{6,14},{7,15},{8,0},{9,1},... | collective-permute-start | bytes 786440 | tf_op jit(solution)/shard_map/ppermute | solution.py:92
  9.4 11.3 %collective-permute-start.3 = (bf16[256,512]{1,0:T(8,128)(2,1)S(1)}, bf16[256,512]{1,0:T(8,128)(2,1)}, u32[]{:S(2)}, u32[]{:S(2)}) collective-permute-start(bf16[256,512]{1,0:T(8,128)(2,1)S(1)} %maximum_select_fusion.refs_3_), channel_id=1, source_target_pairs={{0,2},{1,3},{2,0},{3,1},{4,6},{5,7},{6,4},{7,5},{8,10},{9,11},{10,... | collective-permute-start | bytes 786440 | tf_op jit(solution)/shard_map/ppermute | solution.py:92
  10.9 9.8 %collective-permute-start.2 = (bf16[256,512]{1,0:T(8,128)(2,1)S(1)}, bf16[256,512]{1,0:T(8,128)(2,1)}, u32[]{:S(2)}, u32[]{:S(2)}) collective-permute-start(bf16[256,512]{1,0:T(8,128)(2,1)S(1)} %maximum_select_fusion.refs_3_), channel_id=1, source_target_pairs={{0,4},{1,5},{2,6},{3,7},{4,0},{5,1},{6,2},{7,3},{8,12},{9,13},{10,... | collective-permute-start | bytes 786440 | tf_op jit(solution)/shard_map/ppermute | solution.py:92
  20.7 62.3 %copy-start.1 = (bf16[128,4096]{1,0:T(8,128)(2,1)}, bf16[128,4096]{1,0:T(8,128)(2,1)S(1)}, u32[]{:S(2)}) copy-start(bf16[128,4096]{1,0:T(8,128)(2,1)S(1)} %collective-permute-done.1.refs_2_.refs_1_) | copy-start | bytes 3145732
  20.7 9.5 %collective-permute-start.7 = (bf16[256,512]{1,0:T(8,128)(2,1)}, bf16[256,512]{1,0:T(8,128)(2,1)S(1)}, u32[]{:S(2)}, u32[]{:S(2)}) collective-permute-start(bf16[256,512]{1,0:T(8,128)(2,1)} %collective-permute-done.4.refs_6_), channel_id=1, source_target_pairs={{0,4},{1,5},{2,6},{3,7},{4,0},{5,1},{6,2},{7,3},{8,12},{9,13},{10,... | collective-permute-start | bytes 786440 | tf_op jit(solution)/shard_map/ppermute | solution.py:92
  22.3 9.5 %collective-permute-start.6 = (bf16[256,512]{1,0:T(8,128)(2,1)}, bf16[256,512]{1,0:T(8,128)(2,1)S(1)}, u32[]{:S(2)}, u32[]{:S(2)}) collective-permute-start(bf16[256,512]{1,0:T(8,128)(2,1)} %collective-permute-done.4.refs_6_), channel_id=1, source_target_pairs={{0,2},{1,3},{2,0},{3,1},{4,6},{5,7},{6,4},{7,5},{8,10},{9,11},{10,... | collective-permute-start | bytes 786440 | tf_op jit(solution)/shard_map/ppermute | solution.py:92
  23.8 8.0 %collective-permute-start.10 = (bf16[256,512]{1,0:T(8,128)(2,1)}, bf16[256,512]{1,0:T(8,128)(2,1)}, u32[]{:S(2)}, u32[]{:S(2)}) collective-permute-start(bf16[256,512]{1,0:T(8,128)(2,1)} %collective-permute-done.5.refs_7_), channel_id=1, source_target_pairs={{0,8},{1,9},{2,10},{3,11},{4,12},{5,13},{6,14},{7,15},{8,0},{9,1},... | collective-permute-start | bytes 786440 | tf_op jit(solution)/shard_map/ppermute | solution.py:92
  25.3 9.2 %collective-permute-start.9 = (bf16[256,512]{1,0:T(8,128)(2,1)}, bf16[256,512]{1,0:T(8,128)(2,1)}, u32[]{:S(2)}, u32[]{:S(2)}) collective-permute-start(bf16[256,512]{1,0:T(8,128)(2,1)} %collective-permute-done.5.refs_7_), channel_id=1, source_target_pairs={{0,4},{1,5},{2,6},{3,7},{4,0},{5,1},{6,2},{7,3},{8,12},{9,13},{10,... | collective-permute-start | bytes 786440 | tf_op jit(solution)/shard_map/ppermute | solution.py:92
  25.8 9.7 %collective-permute-start.8 = (bf16[256,512]{1,0:T(8,128)(2,1)}, bf16[256,512]{1,0:T(8,128)(2,1)}, u32[]{:S(2)}, u32[]{:S(2)}) collective-permute-start(bf16[256,512]{1,0:T(8,128)(2,1)} %collective-permute-done.5.refs_7_), channel_id=1, source_target_pairs={{0,2},{1,3},{2,0},{3,1},{4,6},{5,7},{6,4},{7,5},{8,10},{9,11},{10,... | collective-permute-start | bytes 786440 | tf_op jit(solution)/shard_map/ppermute | solution.py:92
  30.2 5.3 %copy-start.9 = (bf16[256,512]{1,0:T(8,128)(2,1)}, bf16[256,512]{1,0:T(8,128)(2,1)S(1)}, u32[]{:S(2)}) copy-start(bf16[256,512]{1,0:T(8,128)(2,1)S(1)} %collective-permute-done.7.refs_9_) | copy-start | bytes 786436
  31.8 3.7 %copy-start.10 = (bf16[256,512]{1,0:T(8,128)(2,1)}, bf16[256,512]{1,0:T(8,128)(2,1)S(1)}, u32[]{:S(2)}) copy-start(bf16[256,512]{1,0:T(8,128)(2,1)S(1)} %collective-permute-done.6.refs_8_) | copy-start | bytes 786436
  65.3 27.7 %copy-start = (bf16[4,128,1024]{2,1,0:T(8,128)(2,1)}, bf16[4,128,1024]{2,1,0:T(8,128)(2,1)S(1)}, u32[]{:S(2)}) copy-start(bf16[4,128,1024]{2,1,0:T(8,128)(2,1)S(1)} %all_to_all.10.own_ref) | copy-start | bytes 3145732
  65.3 41.4 %collective-permute-start.20 = (bf16[4,128,1024]{2,1,0:T(8,128)(2,1)S(1)}, bf16[4,128,1024]{2,1,0:T(8,128)(2,1)S(1)}, u32[]{:S(2)}, u32[]{:S(2)}) collective-permute-start(bf16[4,128,1024]{2,1,0:T(8,128)(2,1)S(1)} %all_to_all.10.own_ref), channel_id=1, source_target_pairs={{0,1},{1,0},{2,3},{3,2},{4,5},{5,4},{6,7},{7,6},{8,9},{9,8},{10,11... | collective-permute-start | bytes 3145736 | tf_op jit(solution)/shard_map/ppermute | solution.py:92
  65.3 4.0 %collective-permute-start.11 = (bf16[144,512]{1,0:T(8,128)(2,1)S(1)}, bf16[144,512]{1,0:T(8,128)(2,1)S(1)}, u32[]{:S(2)}, u32[]{:S(2)}) collective-permute-start(bf16[144,512]{1,0:T(8,128)(2,1)S(1)} %get-tuple-element.77), channel_id=1, source_target_pairs={{0,1},{1,0},{2,3},{3,2},{4,5},{5,4},{6,7},{7,6},{8,9},{9,8},{10,11... | collective-permute-start | bytes 442376 | tf_op jit(solution)/shard_map/ppermute | solution.py:92
  65.8 9.4 %collective-permute-start.14 = (bf16[256,512]{1,0:T(8,128)(2,1)}, bf16[256,512]{1,0:T(8,128)(2,1)S(1)}, u32[]{:S(2)}, u32[]{:S(2)}) collective-permute-start(bf16[256,512]{1,0:T(8,128)(2,1)} %collective-permute-done.2.refs_4_), channel_id=1, source_target_pairs={{0,2},{1,3},{2,0},{3,1},{4,6},{5,7},{6,4},{7,5},{8,10},{9,11},{10,... | collective-permute-start | bytes 786440 | tf_op jit(solution)/shard_map/ppermute | solution.py:92
  67.3 9.5 %collective-permute-start.15 = (bf16[256,512]{1,0:T(8,128)(2,1)}, bf16[256,512]{1,0:T(8,128)(2,1)}, u32[]{:S(2)}, u32[]{:S(2)}) collective-permute-start(bf16[256,512]{1,0:T(8,128)(2,1)} %collective-permute-done.8.refs_10_), channel_id=1, source_target_pairs={{0,4},{1,5},{2,6},{3,7},{4,0},{5,1},{6,2},{7,3},{8,12},{9,13},{10,... | collective-permute-start | bytes 786440 | tf_op jit(solution)/shard_map/ppermute | solution.py:92
  67.9 13.3 %collective-permute-start.13 = (bf16[256,512]{1,0:T(8,128)(2,1)}, bf16[256,512]{1,0:T(8,128)(2,1)}, u32[]{:S(2)}, u32[]{:S(2)}) collective-permute-start(bf16[256,512]{1,0:T(8,128)(2,1)} %collective-permute-done.10.refs_12_), channel_id=1, source_target_pairs={{0,4},{1,5},{2,6},{3,7},{4,0},{5,1},{6,2},{7,3},{8,12},{9,13},{10,... | collective-permute-start | bytes 786440 | tf_op jit(solution)/shard_map/ppermute | solution.py:92
  69.3 19.8 %copy-start.13 = (bf16[144,512]{1,0:T(8,128)(2,1)}, bf16[144,512]{1,0:T(8,128)(2,1)S(1)}, u32[]{:S(2)}) copy-start(bf16[144,512]{1,0:T(8,128)(2,1)S(1)} %collective-permute-done.11.mate_cot_ref) | copy-start | bytes 442372
  69.3 11.9 %collective-permute-start.12 = (bf16[256,512]{1,0:T(8,128)(2,1)}, bf16[256,512]{1,0:T(8,128)(2,1)}, u32[]{:S(2)}, u32[]{:S(2)}) collective-permute-start(bf16[256,512]{1,0:T(8,128)(2,1)} %collective-permute-done.10.refs_12_), channel_id=1, source_target_pairs={{0,2},{1,3},{2,0},{3,1},{4,6},{5,7},{6,4},{7,5},{8,10},{9,11},{10,... | collective-permute-start | bytes 786440 | tf_op jit(solution)/shard_map/ppermute | solution.py:92
  75.2 7.8 %copy-start.11 = (bf16[256,512]{1,0:T(8,128)(2,1)}, bf16[256,512]{1,0:T(8,128)(2,1)S(1)}, u32[]{:S(2)}) copy-start(bf16[256,512]{1,0:T(8,128)(2,1)S(1)} %collective-permute-done.14.refs_15_) | copy-start | bytes 786436
  81.3 7.8 %collective-permute-start.16 = (bf16[256,512]{1,0:T(8,128)(2,1)}, bf16[256,512]{1,0:T(8,128)(2,1)}, u32[]{:S(2)}, u32[]{:S(2)}) collective-permute-start(bf16[256,512]{1,0:T(8,128)(2,1)} %copy-done.9), channel_id=1, source_target_pairs={{0,2},{1,3},{2,0},{3,1},{4,6},{5,7},{6,4},{7,5},{8,10},{9,11},{10,... | collective-permute-start | bytes 786440 | tf_op jit(solution)/shard_map/ppermute | solution.py:92
  81.8 7.3 %collective-permute-start.17 = (bf16[256,512]{1,0:T(8,128)(2,1)}, bf16[256,512]{1,0:T(8,128)(2,1)}, u32[]{:S(2)}, u32[]{:S(2)}) collective-permute-start(bf16[256,512]{1,0:T(8,128)(2,1)} %collective-permute-done.12.refs_13_), channel_id=1, source_target_pairs={{0,4},{1,5},{2,6},{3,7},{4,0},{5,1},{6,2},{7,3},{8,12},{9,13},{10,... | collective-permute-start | bytes 786440 | tf_op jit(solution)/shard_map/ppermute | solution.py:92
  93.0 13.8 %collective-permute-start.19 = (bf16[272,512]{1,0:T(8,128)(2,1)}, bf16[272,512]{1,0:T(8,128)(2,1)S(1)}, u32[]{:S(2)}, u32[]{:S(2)}) collective-permute-start(bf16[272,512]{1,0:T(8,128)(2,1)} %get-tuple-element.131.refs_0_), channel_id=1, source_target_pairs={{0,16},{1,17},{2,18},{3,19},{4,20},{5,21},{6,22},{7,23},{8,24},{9,... | collective-permute-start | bytes 835592 | tf_op jit(solution)/shard_map/ppermute | solution.py:92
  93.3 13.5 %collective-permute-start.18 = (bf16[272,512]{1,0:T(8,128)(2,1)}, bf16[272,512]{1,0:T(8,128)(2,1)S(1)}, u32[]{:S(2)}, u32[]{:S(2)}) collective-permute-start(bf16[272,512]{1,0:T(8,128)(2,1)} %get-tuple-element.131.refs_0_), channel_id=1, source_target_pairs={{0,8},{1,9},{2,10},{3,11},{4,12},{5,13},{6,14},{7,15},{8,0},{9,1},... | collective-permute-start | bytes 835592 | tf_op jit(solution)/shard_map/ppermute | solution.py:92
  106.7 8.7 %copy-start.2 = (bf16[272,512]{1,0:T(8,128)(2,1)}, bf16[272,512]{1,0:T(8,128)(2,1)S(1)}, u32[]{:S(2)}) copy-start(bf16[272,512]{1,0:T(8,128)(2,1)S(1)} %collective-permute-done.19.refs_2_) | copy-start | bytes 835588
  106.7 8.7 %copy-start.3 = (bf16[272,512]{1,0:T(8,128)(2,1)}, bf16[272,512]{1,0:T(8,128)(2,1)S(1)}, u32[]{:S(2)}) copy-start(bf16[272,512]{1,0:T(8,128)(2,1)S(1)} %collective-permute-done.18.refs_1_) | copy-start | bytes 835588
  106.8 15.4 %copy-start.5 = (bf16[4,128,1024]{2,1,0:T(8,128)(2,1)}, bf16[4,128,1024]{2,1,0:T(8,128)(2,1)S(1)}, u32[]{:S(2)}) copy-start(bf16[4,128,1024]{2,1,0:T(8,128)(2,1)S(1)} %collective-permute-done.20.mate_ref) | copy-start | bytes 3145732
  106.8 8.6 %collective-permute-start.21 = (bf16[272,512]{1,0:T(8,128)(2,1)S(1)}, bf16[272,512]{1,0:T(8,128)(2,1)S(1)}, u32[]{:S(2)}, u32[]{:S(2)}) collective-permute-start(bf16[272,512]{1,0:T(8,128)(2,1)S(1)} %collective-permute-done.19.refs_2_), channel_id=1, source_target_pairs={{0,8},{1,9},{2,10},{3,11},{4,12},{5,13},{6,14},{7,15},{8,0},{9,1},... | collective-permute-start | bytes 835592 | tf_op jit(solution)/shard_map/ppermute | solution.py:92
  115.4 16.3 %copy-start.7 = (bf16[512,512]{1,0:T(8,128)(2,1)S(1)}, bf16[512,512]{1,0:T(8,128)(2,1)}, u32[]{:S(2)}) copy-start(bf16[512,512]{1,0:T(8,128)(2,1)} %get-tuple-element.129.refs_2_) | copy-start | bytes 1572868
  115.4 20.4 %collective-permute-start.26 = (bf16[3584,512]{1,0:T(8,128)(2,1)}, bf16[3584,512]{1,0:T(8,128)(2,1)}, u32[]{:S(2)}, u32[]{:S(2)}) collective-permute-start(bf16[3584,512]{1,0:T(8,128)(2,1)} %get-tuple-element.128.refs_0_), channel_id=1, source_target_pairs={{0,1},{1,0},{2,3},{3,2},{4,5},{5,4},{6,7},{7,6},{8,9},{9,8},{10,11... | collective-permute-start | bytes 11010056 | tf_op jit(solution)/shard_map/ppermute | solution.py:92
  118.6 7.4 %collective-permute-start.22 = (bf16[128,512]{1,0:T(8,128)(2,1)}, bf16[128,512]{1,0:T(8,128)(2,1)S(1)}, u32[]{:S(2)}, u32[]{:S(2)}) collective-permute-start(bf16[128,512]{1,0:T(8,128)(2,1)} %get-tuple-element.123), channel_id=1, source_target_pairs={{0,2},{1,3},{2,0},{3,1},{4,6},{5,7},{6,4},{7,5},{8,10},{9,11},{10,... | collective-permute-start | bytes 393224 | tf_op jit(solution)/shard_map/ppermute | solution.py:92
  120.1 8.0 %collective-permute-start.23 = (bf16[128,512]{1,0:T(8,128)(2,1)}, bf16[128,512]{1,0:T(8,128)(2,1)S(1)}, u32[]{:S(2)}, u32[]{:S(2)}) collective-permute-start(bf16[128,512]{1,0:T(8,128)(2,1)} %get-tuple-element.124), channel_id=1, source_target_pairs={{0,4},{1,5},{2,6},{3,7},{4,0},{5,1},{6,2},{7,3},{8,12},{9,13},{10,... | collective-permute-start | bytes 393224 | tf_op jit(solution)/shard_map/ppermute | solution.py:92
  121.5 6.6 %collective-permute-start.24 = (bf16[128,512]{1,0:T(8,128)(2,1)}, bf16[128,512]{1,0:T(8,128)(2,1)S(1)}, u32[]{:S(2)}, u32[]{:S(2)}) collective-permute-start(bf16[128,512]{1,0:T(8,128)(2,1)} %get-tuple-element.125), channel_id=1, source_target_pairs={{0,6},{1,7},{2,4},{3,5},{4,2},{5,3},{6,0},{7,1},{8,14},{9,15},{10,... | collective-permute-start | bytes 393224 | tf_op jit(solution)/shard_map/ppermute | solution.py:92
  126.0 6.1 %copy-start.14 = (bf16[128,512]{1,0:T(8,128)(2,1)}, bf16[128,512]{1,0:T(8,128)(2,1)S(1)}, u32[]{:S(2)}) copy-start(bf16[128,512]{1,0:T(8,128)(2,1)S(1)} %collective-permute-done.22.refs_1_) | copy-start | bytes 393220
  128.1 4.0 %copy-start.15 = (bf16[128,512]{1,0:T(8,128)(2,1)}, bf16[128,512]{1,0:T(8,128)(2,1)S(1)}, u32[]{:S(2)}) copy-start(bf16[128,512]{1,0:T(8,128)(2,1)S(1)} %collective-permute-done.23.refs_2_) | copy-start | bytes 393220
  128.1 4.0 %copy-start.16 = (bf16[128,512]{1,0:T(8,128)(2,1)}, bf16[128,512]{1,0:T(8,128)(2,1)S(1)}, u32[]{:S(2)}) copy-start(bf16[128,512]{1,0:T(8,128)(2,1)S(1)} %collective-permute-done.24.refs_3_) | copy-start | bytes 393220
  128.1 19.0 %all-to-all-start.1 = ((bf16[8,128,512]{2,1,0:T(8,128)(2,1)}), bf16[8,128,512]{2,1,0:T(8,128)(2,1)S(1)}, u32[]{:S(2)}, u32[]{:S(2)}) async-start(bf16[8,128,512]{2,1,0:T(8,128)(2,1)} %bitcast.36), calls=%async_computation.1 | async-start | bytes 2097152 | tf_op jit(solution)/shard_map/all_to_all | solution.py:513
  131.7 4.1 %collective-permute-start.27 = (bf16[512,512]{1,0:T(8,128)(2,1)S(1)}, bf16[512,512]{1,0:T(8,128)(2,1)S(1)}, u32[]{:S(2)}, u32[]{:S(2)}) collective-permute-start(bf16[512,512]{1,0:T(8,128)(2,1)S(1)} %copy-done.7), channel_id=1, source_target_pairs={{0,1},{1,0},{2,3},{3,2},{4,5},{5,4},{6,7},{7,6},{8,9},{9,8},{10,11... | collective-permute-start | bytes 1572872 | tf_op jit(solution)/shard_map/ppermute | solution.py:92
  134.0 1.7 %collective-permute-start.25 = (bf16[4,64,512]{2,1,0:T(8,128)(2,1)}, bf16[4,64,512]{2,1,0:T(8,128)(2,1)S(1)}, u32[]{:S(2)}, u32[]{:S(2)}) collective-permute-start(bf16[4,64,512]{2,1,0:T(8,128)(2,1)} %get-tuple-element.127), channel_id=1, source_target_pairs={{0,1},{1,0},{2,3},{3,2},{4,5},{5,4},{6,7},{7,6},{8,9},{9,8},{10,11... | collective-permute-start | bytes 786440 | tf_op jit(solution)/shard_map/ppermute | solution.py:92
  135.8 0.7 copy-start.12
  135.8 0.9 copy-start.8
  (1 other events, 0.7 us)

commit v15 on v14

--- a/solution.py
+++ b/solution.py
@@ -309,9 +309,6 @@
 
 SCALAR = pl.BlockSpec(memory_space=pltpu.SMEM)
 PARAMS = pltpu.CompilerParams(vmem_limit_bytes=VMEM_LIMIT)
-COST = pl.CostEstimate(flops=1024, bytes_accessed=1024, transcendentals=0)
-
-
 def grant(mebibytes):
     return pltpu.CompilerParams(vmem_limit_bytes=mebibytes << 20)
 
@@ -351,7 +348,6 @@
         have.update(zip(masks, values[len(names) :]))
         return values[: len(names)]
 
-    mate_tokens = swap(after(tokens, mate_shard), CORE)
     have.update(
         {
             Y: swap(piece, Y),
@@ -360,8 +356,14 @@
             far: swap(piece, far),
         }
     )
-    mate_tokens, key_cot, counts, routes = after_round(
-        mate_tokens=mate_tokens, key_cot=key_cot, counts=counts, routes=routes
+    from_both = swap(piece, both)
+    by_level = jnp.stack([tokens[:, z * wide : (z + 1) * wide] for z in range(levels)])
+    by_level, key_cot, counts, routes = after_round(
+        by_level=by_level, key_cot=key_cot, counts=counts, routes=routes
+    )
+    columns = [[p + PLANE * z for z in range(levels)] for p in range(PLANE)]
+    own_features = lax.all_to_all(
+        by_level, "dp", split_axis=0, concat_axis=0, axis_index_groups=columns, tiled=True
     )
     have.update(
         {
@@ -369,9 +371,9 @@
             near | Y: swap(have[near], Y),
             far | X: swap(have[far], X),
             far | Y: swap(have[far], Y),
-            both: swap(have[far], near),
         }
     )
+    have[both] = from_both
     bounds = jnp.cumsum(counts[0])
     positions = jnp.arange(rows, dtype=jnp.int32)
     subnet = jnp.sum((positions[:, None] >= bounds[None, : NSUB - 1]).astype(jnp.int32), axis=1)
@@ -384,21 +386,12 @@
     codes = code_rows(routes[:, 0], core, per_peer, half_cols)
     own_cot = jnp.concatenate([mine(upstream), codes], axis=0)
 
-    by_level = jnp.stack([tokens[:, z * wide : (z + 1) * wide] for z in range(levels)])
-    by_level, own_cot, give_cot = after_round(
-        by_level=by_level,
+    own_cot, give_cot, tokens = after_round(
         own_cot=own_cot,
         give_cot=jnp.concatenate([theirs(upstream), codes], axis=0),
-    )
-    columns = [[p + PLANE * z for z in range(levels)] for p in range(PLANE)]
-    own_features = lax.all_to_all(
-        by_level,
-        "dp",
-        split_axis=0,
-        concat_axis=0,
-        axis_index_groups=columns,
-        tiled=True,
-    )
+        tokens=tokens,
+    )
+    mate_tokens = swap(tokens, CORE)
     have.update(
         {
             both | X: swap(have[both], X),
@@ -407,8 +400,11 @@
             far | X | Y: swap(have[far | X], Y),
         }
     )
+    mate_tokens, give_cot, own_cot = after_round(
+        mate_tokens=mate_tokens, give_cot=give_cot, own_cot=own_cot
+    )
     mate_cot = swap(give_cot, CORE)
-    mate_cot, own_cot = after_round(mate_cot=mate_cot, own_cot=own_cot)
+
     first_masks = list(have)
     last_masks = [near | X | Y, both | X | Y]
     order = jnp.stack([lax.shift_right_logical(me ^ mask, 1) for mask in first_masks + last_masks])
@@ -430,7 +426,6 @@
                 pltpu.SemaphoreType.DMA((4 * count,)),
             ],
             compiler_params=PARAMS,
-            cost_estimate=COST,
             name=name,
         )(*inputs)
 
@@ -448,9 +443,10 @@
             both | X | Y: swap(have[both | X], Y),
         }
     )
-    mate_cot, own_cot, begun, first_weight = after_round(
+    mate_cot, own_cot, own_features, begun, first_weight = after_round(
         mate_cot=mate_cot,
         own_cot=own_cot,
+        own_features=own_features,
         begun=begun,
         first_weight=first_weight,
     )
@@ -489,7 +485,7 @@
         in_specs=[SCALAR] + anywhere(levels),
         out_specs=vmem(4),
         scratch_shapes=[delta_room, pltpu.SemaphoreType.DMA((levels,))],
-        compiler_params=PARAMS,
+        compiler_params=grant(16),
         name="select",
     )(me_scalar, *deltas)
     got = [
@@ -507,7 +503,7 @@
             pltpu.VMEM((wide, half_cols), jnp.float32),
             pltpu.SemaphoreType.DMA((3 * levels,)),
         ],
-        compiler_params=PARAMS,
+        compiler_params=grant(16),
         name="weight_grad",
     )(me_scalar, own_features, mate_features, after(delta, *selected), *deltas[1:])
     parts = lax.all_to_all(
@@ -524,7 +520,7 @@
         out_shape=[jax.ShapeDtypeStruct((4, count, half_cols), jnp.bfloat16)] * 2,
         in_specs=[SCALAR] + vmem(4),
         out_specs=vmem(2),
-        compiler_params=PARAMS,
+        compiler_params=grant(16),
         name="share",
     )(me_scalar, *got)
     mate_got = swap(give_got, CORE)
@@ -540,7 +536,7 @@
             pltpu.VMEM((2, receive, half_cols), jnp.bfloat16),
             pltpu.SemaphoreType.DMA((3 * chips,)),
         ],
-        compiler_params=grant(56),
+        compiler_params=grant(32),
         name="row_grad",
     )(order, me_scalar, own_got, mate_got, first_weight, mate_first, last_weight, mate_last)
 

time: 148 us -> 119 us (0.80)
  blocking collectives: 29.8 us -> 0 us
  starting transfers between devices: 30.5 us -> 37.8 us
  waiting for transfers between devices: 50.4 us -> 44.5 us
  Pallas kernels: 29.5 us -> 24.5 us
  local copies, waits for them, and re-layouts: 4.53 us -> 7.26 us
    all_to_all x1 -> x0, blocking collectives: 29.8 us -> none  [per_device_paired(): lax.all_to_all(by_level, 'dp', split_axis=0, concat_axis=0, axis_index_gr...]
    ppermute x28, waiting for transfers between devices: 50.4 us -> 43.4 us  [swap(): return lax.ppermute(value, 'dp', [(i, i ^ mask) for i in range(size)])]
    all_to_all x0 -> x1, starting transfers between devices: none -> 4.65 us  [per_device_paired(): lax.all_to_all(by_level, 'dp', split_axis=0, concat_axis=0, axis_index_gr...]
    ppermute x28, starting transfers between devices: 26.9 us -> 29.6 us  [swap(): return lax.ppermute(value, 'dp', [(i, i ^ mask) for i in range(size)])]
    unnamed x40 -> x42, local copies, waits for them, and re-layouts: 1.62 us -> 4.27 us
    pallas_call x1, Pallas kernels: 1.92 us -> 0.04 us  [per_device_paired(): pl.pallas_call(share_kernel, out_shape=[jax.ShapeDtypeStruct((4, count, h...]
    pallas_call x1, Pallas kernels: 2.52 us -> 0.98 us  [per_device_paired(): pl.pallas_call(select_kernel, out_shape=[jax.ShapeDtypeStruct((2 * count,...]
  transfers between devices with their start and end apart: 29 -> 30, of which waited for: 14 -> 13; matrix products, arithmetic and copies ran while one was open for 4% -> 5% of each run, Pallas kernels for 19% -> 20%
where the time goes in v15:
time: 119 us; the launch traced here: 118 us
  waiting for transfers between devices  44.5 us (37%)
  starting transfers between devices  37.8 us (32%)
  Pallas kernels  24.5 us (21%)
  local copies, waits for them, and re-layouts  7.26 us (6%)
  other arithmetic  3.48 us (3%)
    ppermute x28, waiting for transfers between devices, swap(): return lax.ppermute(value, 'dp', [(i, i ^ mask) for i in range(size)])  43.4 us
    ppermute x28, starting transfers between devices, swap(): return lax.ppermute(value, 'dp', [(i, i ^ mask) for i in range(size)])  29.6 us
    pallas_call x2, Pallas kernels, project(): pl.pallas_call(kernel, out_shape=(*results, jax.ShapeDtypeStruct((count *...  9.89 us
    pallas_call x1, Pallas kernels, per_device_paired(): pl.pallas_call(row_grad_kernel, out_shape=jax.ShapeDtypeStruct((receive,...  9.87 us
    all_to_all x1, starting transfers between devices, per_device_paired(): lax.all_to_all(by_level, 'dp', split_axis=0, concat_axis=0, axis_index_gr...  4.65 us
    unnamed x42, local copies, waits for them, and re-layouts  4.27 us
    all_to_all x1, starting transfers between devices, per_device_paired(): lax.all_to_all(after(terms, *got).reshape(PLANE, shard, half_cols), 'dp',...  3.56 us
    pallas_call x1, Pallas kernels, per_device_paired(): pl.pallas_call(weight_grad_kernel, out_shape=jax.ShapeDtypeStruct((wide,...  2.76 us
  transfers between devices with their start and end apart: 30, of which 13 were waited for; matrix products, arithmetic and copies ran while one was open for 5% of the time, Pallas kernels for 20%

profile of v15, /device:TPU:0, one launch (start us, length us, event | category | flops | bytes accessed | tf_op | source)
XLA Modules:
  0.0 118.5 jit_solution(5615173647526120988)
XLA Ops:
  0.7 0.5 collective-permute-start
  1.2 1.0 fusion.11
  2.7 4.0 %collective-permute-start.4 = (bf16[256,512]{1,0:T(8,128)(2,1)S(1)}, bf16[256,512]{1,0:T(8,128)(2,1)S(1)}, u32[]{:S(2)}, u32[]{:S(2)}) collective-permute-start(bf16[256,512]{1,0:T(8,128)(2,1)S(1)} %maximum_select_fusion.refs_3_), channel_id=1, source_target_pairs={{0,16},{1,17},{2,18},{3,19},{4,20},{5,21},{6,22},{7,23},{8,24},{9,... | collective-permute-start | bytes 786440 | tf_op jit(solution)/shard_map/ppermute | solution.py:92
  6.7 1.6 %collective-permute-start.3 = (bf16[256,512]{1,0:T(8,128)(2,1)S(1)}, bf16[256,512]{1,0:T(8,128)(2,1)S(1)}, u32[]{:S(2)}, u32[]{:S(2)}) collective-permute-start(bf16[256,512]{1,0:T(8,128)(2,1)S(1)} %maximum_select_fusion.refs_3_), channel_id=1, source_target_pairs={{0,8},{1,9},{2,10},{3,11},{4,12},{5,13},{6,14},{7,15},{8,0},{9,1},... | collective-permute-start | bytes 786440 | tf_op jit(solution)/shard_map/ppermute | solution.py:92
  8.3 1.5 %collective-permute-start.2 = (bf16[256,512]{1,0:T(8,128)(2,1)S(1)}, bf16[256,512]{1,0:T(8,128)(2,1)S(1)}, u32[]{:S(2)}, u32[]{:S(2)}) collective-permute-start(bf16[256,512]{1,0:T(8,128)(2,1)S(1)} %maximum_select_fusion.refs_3_), channel_id=1, source_target_pairs={{0,2},{1,3},{2,0},{3,1},{4,6},{5,7},{6,4},{7,5},{8,10},{9,11},{10,... | collective-permute-start | bytes 786440 | tf_op jit(solution)/shard_map/ppermute | solution.py:92
  9.8 1.5 %collective-permute-start.1 = (bf16[256,512]{1,0:T(8,128)(2,1)S(1)}, bf16[256,512]{1,0:T(8,128)(2,1)S(1)}, u32[]{:S(2)}, u32[]{:S(2)}) collective-permute-start(bf16[256,512]{1,0:T(8,128)(2,1)S(1)} %maximum_select_fusion.refs_3_), channel_id=1, source_target_pairs={{0,4},{1,5},{2,6},{3,7},{4,0},{5,1},{6,2},{7,3},{8,12},{9,13},{10,... | collective-permute-start | bytes 786440 | tf_op jit(solution)/shard_map/ppermute | solution.py:92
  11.3 1.3 %slice_bitcast_fusion.3 = (bf16[1,128,1024]{2,1,0:T(8,128)(2,1)S(1)}, bf16[1,128,1024]{2,1,0:T(8,128)(2,1)S(1)}, bf16[1,128,1024]{2,1,0:T(8,128)(2,1)S(1)}, bf16[1,128,1024]{2,1,0:T(8,128)(2,1)S(1)}) fusion(bf16[128,4096]{1,0:T(8,128)(2,1)} %refs_0_), kind=kLoop, calls=%fused_computation.6 | loop fusion | bytes 2097152 | tf_op jit(solution)/shard_map/stack | solution.py:360
  12.6 1.1 pad_maximum_fusion
  13.9 5.8 %collective-permute-done.4.refs_7_ = bf16[256,512]{1,0:T(8,128)(2,1)S(1)} collective-permute-done((bf16[256,512]{1,0:T(8,128)(2,1)S(1)}, bf16[256,512]{1,0:T(8,128)(2,1)S(1)}, u32[]{:S(2)}, u32[]{:S(2)}) %collective-permute-start.4) | collective-permute-done | bytes 262176 | tf_op jit(solution)/shard_map/ppermute | solution.py:92
  19.7 2.3 %collective-permute-start.6 = (bf16[256,512]{1,0:T(8,128)(2,1)S(1)}, bf16[256,512]{1,0:T(8,128)(2,1)}, u32[]{:S(2)}, u32[]{:S(2)}) collective-permute-start(bf16[256,512]{1,0:T(8,128)(2,1)S(1)} %collective-permute-done.3.refs_6_), channel_id=1, source_target_pairs={{0,4},{1,5},{2,6},{3,7},{4,0},{5,1},{6,2},{7,3},{8,12},{9,13},{10,... | collective-permute-start | bytes 786440 | tf_op jit(solution)/shard_map/ppermute | solution.py:92
  22.0 1.5 %collective-permute-start.5 = (bf16[256,512]{1,0:T(8,128)(2,1)S(1)}, bf16[256,512]{1,0:T(8,128)(2,1)}, u32[]{:S(2)}, u32[]{:S(2)}) collective-permute-start(bf16[256,512]{1,0:T(8,128)(2,1)S(1)} %collective-permute-done.3.refs_6_), channel_id=1, source_target_pairs={{0,2},{1,3},{2,0},{3,1},{4,6},{5,7},{6,4},{7,5},{8,10},{9,11},{10,... | collective-permute-start | bytes 786440 | tf_op jit(solution)/shard_map/ppermute | solution.py:92
  23.5 0.5 collective-permute-start.8
  24.5 4.7 %all-to-all-start = ((bf16[4,128,1024]{2,1,0:T(8,128)(2,1)}), bf16[4,128,1024]{2,1,0:T(8,128)(2,1)S(1)}, u32[]{:S(2)}, u32[]{:S(2)}) async-start(bf16[4,128,1024]{2,1,0:T(8,128)(2,1)} %pad_maximum_fusion), calls=%async_computation | async-start | bytes 2097152 | tf_op jit(solution)/shard_map/all_to_all | solution.py:365
  29.3 1.1 compare_select_fusion
  30.4 0.8 pad_maximum_fusion.1
  31.2 1.4 %collective-permute-done.8.refs_11_ = bf16[256,512]{1,0:T(8,128)(2,1)} collective-permute-done((bf16[256,512]{1,0:T(8,128)(2,1)S(1)}, bf16[256,512]{1,0:T(8,128)(2,1)}, u32[]{:S(2)}, u32[]{:S(2)}) %collective-permute-start.8) | collective-permute-done | bytes 262176 | tf_op jit(solution)/shard_map/ppermute | solution.py:92
  32.6 1.0 collective-permute-done.7.refs_10_
  33.7 1.6 %collective-permute-start.13 = (bf16[256,512]{1,0:T(8,128)(2,1)S(1)}, bf16[256,512]{1,0:T(8,128)(2,1)S(1)}, u32[]{:S(2)}, u32[]{:S(2)}) collective-permute-start(bf16[256,512]{1,0:T(8,128)(2,1)S(1)} %collective-permute-done.1.refs_4_), channel_id=1, source_target_pairs={{0,2},{1,3},{2,0},{3,1},{4,6},{5,7},{6,4},{7,5},{8,10},{9,11},{10,... | collective-permute-start | bytes 786440 | tf_op jit(solution)/shard_map/ppermute | solution.py:92
  35.3 0.5 collective-permute-start.14
  35.8 1.6 %collective-permute-start.12 = (bf16[256,512]{1,0:T(8,128)(2,1)}, bf16[256,512]{1,0:T(8,128)(2,1)S(1)}, u32[]{:S(2)}, u32[]{:S(2)}) collective-permute-start(bf16[256,512]{1,0:T(8,128)(2,1)} %collective-permute-done.9.refs_12_), channel_id=1, source_target_pairs={{0,4},{1,5},{2,6},{3,7},{4,0},{5,1},{6,2},{7,3},{8,12},{9,13},{10,... | collective-permute-start | bytes 786440 | tf_op jit(solution)/shard_map/ppermute | solution.py:92
  37.3 0.5 collective-permute-start.11
  37.8 5.1 %collective-permute-done.13.refs_15_ = bf16[256,512]{1,0:T(8,128)(2,1)S(1)} collective-permute-done((bf16[256,512]{1,0:T(8,128)(2,1)S(1)}, bf16[256,512]{1,0:T(8,128)(2,1)S(1)}, u32[]{:S(2)}, u32[]{:S(2)}) %collective-permute-start.13) | collective-permute-done | bytes 262176 | tf_op jit(solution)/shard_map/ppermute | solution.py:92
  42.9 1.8 %collective-permute-done.14.refs_16_ = bf16[256,512]{1,0:T(8,128)(2,1)S(1)} collective-permute-done((bf16[256,512]{1,0:T(8,128)(2,1)}, bf16[256,512]{1,0:T(8,128)(2,1)S(1)}, u32[]{:S(2)}, u32[]{:S(2)}) %collective-permute-start.14) | collective-permute-done | bytes 262176 | tf_op jit(solution)/shard_map/ppermute | solution.py:92
  44.6 4.8 %collective-permute-done.12.refs_14_ = bf16[256,512]{1,0:T(8,128)(2,1)S(1)} collective-permute-done((bf16[256,512]{1,0:T(8,128)(2,1)}, bf16[256,512]{1,0:T(8,128)(2,1)S(1)}, u32[]{:S(2)}, u32[]{:S(2)}) %collective-permute-start.12) | collective-permute-done | bytes 262176 | tf_op jit(solution)/shard_map/ppermute | solution.py:92
  49.5 0.6 collective-permute-start.16
  50.1 0.8 collective-permute-start.17
  50.9 0.7 stack.87.refs_0_.chips_ref
  51.6 6.1 %project.1 = (bf16[3584,512]{1,0:T(8,128)(2,1)}, f32[2,128,512]{2,1,0:T(8,128)}) custom-call(s32[16]{0:T(128)} %stack.87.refs_0_.chips_ref, bf16[128,4096]{1,0:T(8,128)(2,1)} %refs_0_, bf16[128,4096]{1,0:T(8,128)(2,1)} %copy-done.6, bf16[256,512]{1,0:T(8,128)(2,1)} %copy-done.7, bf16[256,512]{1,0:T(8,128)(2,1)} %copy-done.11, bf16[256,512]{1,0:T(8,128)(2,1)} %copy-done.10, ...), custom_call_target="tpu_custom_call" | custom-call | tf_op jit(solution)/shard_map/project/pallas_call | solution.py:415
  57.7 0.6 collective-permute-start.20
  58.5 3.8 %delta.1 = (bf16[272,512]{1,0:T(8,128)(2,1)}, bf16[512,512]{1,0:T(8,128)(2,1)}) custom-call(s32[16]{0:T(128)} %stack.87.refs_0_.chips_ref, s32[1]{0:T(128)} %bitcast.16.me_ref, bf16[144,512]{1,0:T(8,128)(2,1)} %get-tuple-element.110.own_cot_ref, bf16[144,512]{1,0:T(8,128)(2,1)} %copy-done.17, bf16[128,4096]{1,0:T(8,128)(2,1)} %refs_0_, ...), custom_call_target="tpu_custom_call" | custom-call | tf_op jit(solution)/shard_map/delta/pallas_call | solution.py:415
  62.4 1.4 %collective-permute-start.19 = (bf16[272,512]{1,0:T(8,128)(2,1)}, bf16[272,512]{1,0:T(8,128)(2,1)S(1)}, u32[]{:S(2)}, u32[]{:S(2)}) collective-permute-start(bf16[272,512]{1,0:T(8,128)(2,1)} %get-tuple-element.133.refs_0_), channel_id=1, source_target_pairs={{0,16},{1,17},{2,18},{3,19},{4,20},{5,21},{6,22},{7,23},{8,24},{9,... | collective-permute-start | bytes 835592 | tf_op jit(solution)/shard_map/ppermute | solution.py:92
  63.8 3.8 %collective-permute-start.18 = (bf16[272,512]{1,0:T(8,128)(2,1)}, bf16[272,512]{1,0:T(8,128)(2,1)S(1)}, u32[]{:S(2)}, u32[]{:S(2)}) collective-permute-start(bf16[272,512]{1,0:T(8,128)(2,1)} %get-tuple-element.133.refs_0_), channel_id=1, source_target_pairs={{0,8},{1,9},{2,10},{3,11},{4,12},{5,13},{6,14},{7,15},{8,0},{9,1},... | collective-permute-start | bytes 835592 | tf_op jit(solution)/shard_map/ppermute | solution.py:92
  67.7 11.0 %collective-permute-done.19.refs_2_ = bf16[272,512]{1,0:T(8,128)(2,1)S(1)} collective-permute-done((bf16[272,512]{1,0:T(8,128)(2,1)}, bf16[272,512]{1,0:T(8,128)(2,1)S(1)}, u32[]{:S(2)}, u32[]{:S(2)}) %collective-permute-start.19) | collective-permute-done | bytes 278560 | tf_op jit(solution)/shard_map/ppermute | solution.py:92
  79.0 7.9 %collective-permute-done.21.refs_3_ = bf16[272,512]{1,0:T(8,128)(2,1)S(1)} collective-permute-done((bf16[272,512]{1,0:T(8,128)(2,1)S(1)}, bf16[272,512]{1,0:T(8,128)(2,1)S(1)}, u32[]{:S(2)}, u32[]{:S(2)}) %collective-permute-start.21) | collective-permute-done | bytes 278560 | tf_op jit(solution)/shard_map/ppermute | solution.py:92
  86.9 1.0 copy-done.1
  87.9 1.0 select.28
  88.9 1.3 %collective-permute-start.22 = (bf16[128,512]{1,0:T(8,128)(2,1)S(1)}, bf16[128,512]{1,0:T(8,128)(2,1)S(1)}, u32[]{:S(2)}, u32[]{:S(2)}) collective-permute-start(bf16[128,512]{1,0:T(8,128)(2,1)S(1)} %get-tuple-element.125), channel_id=1, source_target_pairs={{0,2},{1,3},{2,0},{3,1},{4,6},{5,7},{6,4},{7,5},{8,10},{9,11},{10,... | collective-permute-start | bytes 393224 | tf_op jit(solution)/shard_map/ppermute | solution.py:92
  90.2 1.5 %collective-permute-start.23 = (bf16[128,512]{1,0:T(8,128)(2,1)S(1)}, bf16[128,512]{1,0:T(8,128)(2,1)S(1)}, u32[]{:S(2)}, u32[]{:S(2)}) collective-permute-start(bf16[128,512]{1,0:T(8,128)(2,1)S(1)} %get-tuple-element.126), channel_id=1, source_target_pairs={{0,4},{1,5},{2,6},{3,7},{4,0},{5,1},{6,2},{7,3},{8,12},{9,13},{10,... | collective-permute-start | bytes 393224 | tf_op jit(solution)/shard_map/ppermute | solution.py:92
  91.7 0.7 collective-permute-start.24
  92.4 1.0 copy-done.2
  93.4 2.8 %weight_grad.1 = bf16[1024,512]{1,0:T(8,128)(2,1)} custom-call(s32[1]{0:T(128)} %bitcast.16.me_ref, bf16[4,128,1024]{2,1,0:T(8,128)(2,1)S(1)} %all-to-all-done.own_ref, bf16[4,128,1024]{2,1,0:T(8,128)(2,1)S(1)} %collective-permute-done.20.mate_ref, bf16[272,512]{1,0:T(8,128)(2,1)S(1)} %copy-done.2, bf16[272,512]{1,0:T(8,128)(2,1)S(1)} %collective-permute-done.18.refs_1_, ...), custom_call_target="tpu_custom_call" | custom-call | tf_op jit(solution)/shard_map/weight_grad/pallas_call | solution.py:495
  96.2 2.4 %collective-permute-done.23.refs_2_ = bf16[128,512]{1,0:T(8,128)(2,1)S(1)} collective-permute-done((bf16[128,512]{1,0:T(8,128)(2,1)S(1)}, bf16[128,512]{1,0:T(8,128)(2,1)S(1)}, u32[]{:S(2)}, u32[]{:S(2)}) %collective-permute-start.23) | collective-permute-done | bytes 131104 | tf_op jit(solution)/shard_map/ppermute | solution.py:92
  98.6 3.6 %all-to-all-start.1 = ((bf16[8,128,512]{2,1,0:T(8,128)(2,1)}), bf16[8,128,512]{2,1,0:T(8,128)(2,1)S(1)}, u32[]{:S(2)}, u32[]{:S(2)}) async-start(bf16[8,128,512]{2,1,0:T(8,128)(2,1)} %bitcast.26), calls=%async_computation.1 | async-start | bytes 2097152 | tf_op jit(solution)/shard_map/all_to_all | solution.py:509
  102.9 1.7 %collective-permute-done.25.mate_got_ref = bf16[4,64,512]{2,1,0:T(8,128)(2,1)S(1)} collective-permute-done((bf16[4,64,512]{2,1,0:T(8,128)(2,1)S(1)}, bf16[4,64,512]{2,1,0:T(8,128)(2,1)S(1)}, u32[]{:S(2)}, u32[]{:S(2)}) %collective-permute-start.25) | collective-permute-done | bytes 262176 | tf_op jit(solution)/shard_map/ppermute | solution.py:92
  104.6 2.0 %copy-done = bf16[3584,512]{1,0:T(8,128)(2,1)S(1)} copy-done((bf16[3584,512]{1,0:T(8,128)(2,1)S(1)}, bf16[3584,512]{1,0:T(8,128)(2,1)}, u32[]{:S(2)}) %copy-start) | copy-done | bytes 3670040
  106.6 9.9 %row_grad.1 = bf16[256,4096]{1,0:T(8,128)(2,1)} custom-call(s32[16]{0:T(128)S(1)} %copy-done.4, s32[1]{0:T(128)} %bitcast.16.me_ref, bf16[4,64,512]{2,1,0:T(8,128)(2,1)S(1)} %get-tuple-element.128.own_got_ref, bf16[4,64,512]{2,1,0:T(8,128)(2,1)S(1)} %collective-permute-done.25.mate_got_ref, bf16[3584,512]{1,0:T(8,128)(2,1)S(1)} %copy-done, ...), custom_call_target="tpu_custom_call" | custom-call | tf_op jit(solution)/shard_map/row_grad/pallas_call | solution.py:528
  116.5 1.0 all-to-all-done.1
  117.5 0.9 sum.1
  (79 shorter events, 2.8 us)
Async XLA Ops:
  0.6 23.5 %copy-start.18 = (s32[1,4]{1,0:T(1,128)S(1)}, s32[1,4]{1,0:T(1,128)}, u32[]{:S(2)}) copy-start(s32[1,4]{1,0:T(1,128)} %param.9) | copy-start | bytes 52
  0.6 23.8 %copy-start.19 = (s32[128,1]{0,1:T(1,128)S(1)}, s32[128,1]{0,1:T(1,128)}, u32[]{:S(2)}) copy-start(s32[128,1]{0,1:T(1,128)} %param.8) | copy-start | bytes 1540
  0.7 1.9 %collective-permute-start = (bf16[128,1024]{1,0:T(8,128)(2,1)}, bf16[128,1024]{1,0:T(8,128)(2,1)S(1)}, u32[]{:S(2)}, u32[]{:S(2)}) collective-permute-start(bf16[128,1024]{1,0:T(8,128)(2,1)} %param.11), channel_id=1, source_target_pairs={{0,1},{1,0},{2,3},{3,2},{4,5},{5,4},{6,7},{7,6},{8,9},{9,8},{10,11... | collective-permute-start | bytes 786440 | tf_op jit(solution)/shard_map/ppermute | solution.py:92
  2.6 26.6 %copy-start.20 = (s32[4]{0:T(128)S(1)}, s32[4]{0:T(128)}, u32[]{:S(2)}) copy-start(s32[4]{0:T(128)} %param.10) | copy-start | bytes 52
  2.6 27.8 %copy-start.7 = (bf16[256,512]{1,0:T(8,128)(2,1)}, bf16[256,512]{1,0:T(8,128)(2,1)S(1)}, u32[]{:S(2)}) copy-start(bf16[256,512]{1,0:T(8,128)(2,1)S(1)} %maximum_select_fusion.refs_3_) | copy-start | bytes 786436
  2.7 31.0 %copy-start.5 = (bf16[128,4096]{1,0:T(8,128)(2,1)S(1)}, bf16[128,4096]{1,0:T(8,128)(2,1)}, u32[]{:S(2)}) copy-start(bf16[128,4096]{1,0:T(8,128)(2,1)} %refs_0_) | copy-start | bytes 3145732
  2.7 17.0 %collective-permute-start.4 = (bf16[256,512]{1,0:T(8,128)(2,1)S(1)}, bf16[256,512]{1,0:T(8,128)(2,1)S(1)}, u32[]{:S(2)}, u32[]{:S(2)}) collective-permute-start(bf16[256,512]{1,0:T(8,128)(2,1)S(1)} %maximum_select_fusion.refs_3_), channel_id=1, source_target_pairs={{0,16},{1,17},{2,18},{3,19},{4,20},{5,21},{6,22},{7,23},{8,24},{9,... | collective-permute-start | bytes 786440 | tf_op jit(solution)/shard_map/ppermute | solution.py:92
  6.7 13.0 %collective-permute-start.3 = (bf16[256,512]{1,0:T(8,128)(2,1)S(1)}, bf16[256,512]{1,0:T(8,128)(2,1)S(1)}, u32[]{:S(2)}, u32[]{:S(2)}) collective-permute-start(bf16[256,512]{1,0:T(8,128)(2,1)S(1)} %maximum_select_fusion.refs_3_), channel_id=1, source_target_pairs={{0,8},{1,9},{2,10},{3,11},{4,12},{5,13},{6,14},{7,15},{8,0},{9,1},... | collective-permute-start | bytes 786440 | tf_op jit(solution)/shard_map/ppermute | solution.py:92
  8.3 11.4 %collective-permute-start.2 = (bf16[256,512]{1,0:T(8,128)(2,1)S(1)}, bf16[256,512]{1,0:T(8,128)(2,1)S(1)}, u32[]{:S(2)}, u32[]{:S(2)}) collective-permute-start(bf16[256,512]{1,0:T(8,128)(2,1)S(1)} %maximum_select_fusion.refs_3_), channel_id=1, source_target_pairs={{0,2},{1,3},{2,0},{3,1},{4,6},{5,7},{6,4},{7,5},{8,10},{9,11},{10,... | collective-permute-start | bytes 786440 | tf_op jit(solution)/shard_map/ppermute | solution.py:92
  9.8 9.9 %collective-permute-start.1 = (bf16[256,512]{1,0:T(8,128)(2,1)S(1)}, bf16[256,512]{1,0:T(8,128)(2,1)S(1)}, u32[]{:S(2)}, u32[]{:S(2)}) collective-permute-start(bf16[256,512]{1,0:T(8,128)(2,1)S(1)} %maximum_select_fusion.refs_3_), channel_id=1, source_target_pairs={{0,4},{1,5},{2,6},{3,7},{4,0},{5,1},{6,2},{7,3},{8,12},{9,13},{10,... | collective-permute-start | bytes 786440 | tf_op jit(solution)/shard_map/ppermute | solution.py:92
  13.7 17.5 %collective-permute-start.9 = (bf16[256,512]{1,0:T(8,128)(2,1)S(1)}, bf16[256,512]{1,0:T(8,128)(2,1)}, u32[]{:S(2)}, u32[]{:S(2)}) collective-permute-start(bf16[256,512]{1,0:T(8,128)(2,1)S(1)} %maximum_select_fusion.refs_3_), channel_id=1, source_target_pairs={{0,24},{1,25},{2,26},{3,27},{4,28},{5,29},{6,30},{7,31},{8,16},{9,... | collective-permute-start | bytes 786440 | tf_op jit(solution)/shard_map/ppermute | solution.py:92
  19.7 13.9 %copy-start.8 = (bf16[256,512]{1,0:T(8,128)(2,1)}, bf16[256,512]{1,0:T(8,128)(2,1)S(1)}, u32[]{:S(2)}) copy-start(bf16[256,512]{1,0:T(8,128)(2,1)S(1)} %collective-permute-done.4.refs_7_) | copy-start | bytes 786436
  19.7 13.9 %copy-start.9 = (bf16[256,512]{1,0:T(8,128)(2,1)}, bf16[256,512]{1,0:T(8,128)(2,1)S(1)}, u32[]{:S(2)}) copy-start(bf16[256,512]{1,0:T(8,128)(2,1)S(1)} %collective-permute-done.3.refs_6_) | copy-start | bytes 786436
  19.7 9.6 %copy-start.10 = (bf16[256,512]{1,0:T(8,128)(2,1)}, bf16[256,512]{1,0:T(8,128)(2,1)S(1)}, u32[]{:S(2)}) copy-start(bf16[256,512]{1,0:T(8,128)(2,1)S(1)} %collective-permute-done.2.refs_5_) | copy-start | bytes 786436
  19.7 31.9 %copy-start.11 = (bf16[256,512]{1,0:T(8,128)(2,1)}, bf16[256,512]{1,0:T(8,128)(2,1)S(1)}, u32[]{:S(2)}) copy-start(bf16[256,512]{1,0:T(8,128)(2,1)S(1)} %collective-permute-done.1.refs_4_) | copy-start | bytes 786436
  19.7 11.5 %collective-permute-start.6 = (bf16[256,512]{1,0:T(8,128)(2,1)S(1)}, bf16[256,512]{1,0:T(8,128)(2,1)}, u32[]{:S(2)}, u32[]{:S(2)}) collective-permute-start(bf16[256,512]{1,0:T(8,128)(2,1)S(1)} %collective-permute-done.3.refs_6_), channel_id=1, source_target_pairs={{0,4},{1,5},{2,6},{3,7},{4,0},{5,1},{6,2},{7,3},{8,12},{9,13},{10,... | collective-permute-start | bytes 786440 | tf_op jit(solution)/shard_map/ppermute | solution.py:92
  22.0 9.2 %collective-permute-start.5 = (bf16[256,512]{1,0:T(8,128)(2,1)S(1)}, bf16[256,512]{1,0:T(8,128)(2,1)}, u32[]{:S(2)}, u32[]{:S(2)}) collective-permute-start(bf16[256,512]{1,0:T(8,128)(2,1)S(1)} %collective-permute-done.3.refs_6_), channel_id=1, source_target_pairs={{0,2},{1,3},{2,0},{3,1},{4,6},{5,7},{6,4},{7,5},{8,10},{9,11},{10,... | collective-permute-start | bytes 786440 | tf_op jit(solution)/shard_map/ppermute | solution.py:92
  23.5 9.1 %collective-permute-start.8 = (bf16[256,512]{1,0:T(8,128)(2,1)S(1)}, bf16[256,512]{1,0:T(8,128)(2,1)}, u32[]{:S(2)}, u32[]{:S(2)}) collective-permute-start(bf16[256,512]{1,0:T(8,128)(2,1)S(1)} %collective-permute-done.4.refs_7_), channel_id=1, source_target_pairs={{0,4},{1,5},{2,6},{3,7},{4,0},{5,1},{6,2},{7,3},{8,12},{9,13},{10,... | collective-permute-start | bytes 786440 | tf_op jit(solution)/shard_map/ppermute | solution.py:92
  24.0 9.6 %collective-permute-start.7 = (bf16[256,512]{1,0:T(8,128)(2,1)S(1)}, bf16[256,512]{1,0:T(8,128)(2,1)}, u32[]{:S(2)}, u32[]{:S(2)}) collective-permute-start(bf16[256,512]{1,0:T(8,128)(2,1)S(1)} %collective-permute-done.4.refs_7_), channel_id=1, source_target_pairs={{0,2},{1,3},{2,0},{3,1},{4,6},{5,7},{6,4},{7,5},{8,10},{9,11},{10,... | collective-permute-start | bytes 786440 | tf_op jit(solution)/shard_map/ppermute | solution.py:92
  24.5 33.2 %all-to-all-start = ((bf16[4,128,1024]{2,1,0:T(8,128)(2,1)}), bf16[4,128,1024]{2,1,0:T(8,128)(2,1)S(1)}, u32[]{:S(2)}, u32[]{:S(2)}) async-start(bf16[4,128,1024]{2,1,0:T(8,128)(2,1)} %pad_maximum_fusion), calls=%async_computation | async-start | bytes 2097152 | tf_op jit(solution)/shard_map/all_to_all | solution.py:365
  33.6 15.8 %collective-permute-start.10 = (bf16[128,4096]{1,0:T(8,128)(2,1)S(1)}, bf16[128,4096]{1,0:T(8,128)(2,1)S(1)}, u32[]{:S(2)}, u32[]{:S(2)}) collective-permute-start(bf16[128,4096]{1,0:T(8,128)(2,1)S(1)} %copy-done.5), channel_id=1, source_target_pairs={{0,1},{1,0},{2,3},{3,2},{4,5},{5,4},{6,7},{7,6},{8,9},{9,8},{10,11... | collective-permute-start | bytes 3145736 | tf_op jit(solution)/shard_map/ppermute | solution.py:92
  33.7 9.2 %collective-permute-start.13 = (bf16[256,512]{1,0:T(8,128)(2,1)S(1)}, bf16[256,512]{1,0:T(8,128)(2,1)S(1)}, u32[]{:S(2)}, u32[]{:S(2)}) collective-permute-start(bf16[256,512]{1,0:T(8,128)(2,1)S(1)} %collective-permute-done.1.refs_4_), channel_id=1, source_target_pairs={{0,2},{1,3},{2,0},{3,1},{4,6},{5,7},{6,4},{7,5},{8,10},{9,11},{10,... | collective-permute-start | bytes 786440 | tf_op jit(solution)/shard_map/ppermute | solution.py:92
  35.3 9.4 %collective-permute-start.14 = (bf16[256,512]{1,0:T(8,128)(2,1)}, bf16[256,512]{1,0:T(8,128)(2,1)S(1)}, u32[]{:S(2)}, u32[]{:S(2)}) collective-permute-start(bf16[256,512]{1,0:T(8,128)(2,1)} %collective-permute-done.7.refs_10_), channel_id=1, source_target_pairs={{0,4},{1,5},{2,6},{3,7},{4,0},{5,1},{6,2},{7,3},{8,12},{9,13},{10,... | collective-permute-start | bytes 786440 | tf_op jit(solution)/shard_map/ppermute | solution.py:92
  35.8 13.7 %collective-permute-start.12 = (bf16[256,512]{1,0:T(8,128)(2,1)}, bf16[256,512]{1,0:T(8,128)(2,1)S(1)}, u32[]{:S(2)}, u32[]{:S(2)}) collective-permute-start(bf16[256,512]{1,0:T(8,128)(2,1)} %collective-permute-done.9.refs_12_), channel_id=1, source_target_pairs={{0,4},{1,5},{2,6},{3,7},{4,0},{5,1},{6,2},{7,3},{8,12},{9,13},{10,... | collective-permute-start | bytes 786440 | tf_op jit(solution)/shard_map/ppermute | solution.py:92
  37.3 12.2 %collective-permute-start.11 = (bf16[256,512]{1,0:T(8,128)(2,1)}, bf16[256,512]{1,0:T(8,128)(2,1)}, u32[]{:S(2)}, u32[]{:S(2)}) collective-permute-start(bf16[256,512]{1,0:T(8,128)(2,1)} %collective-permute-done.9.refs_12_), channel_id=1, source_target_pairs={{0,2},{1,3},{2,0},{3,1},{4,6},{5,7},{6,4},{7,5},{8,10},{9,11},{10,... | collective-permute-start | bytes 786440 | tf_op jit(solution)/shard_map/ppermute | solution.py:92
  42.9 6.6 %copy-start.12 = (bf16[256,512]{1,0:T(8,128)(2,1)}, bf16[256,512]{1,0:T(8,128)(2,1)S(1)}, u32[]{:S(2)}) copy-start(bf16[256,512]{1,0:T(8,128)(2,1)S(1)} %collective-permute-done.13.refs_15_) | copy-start | bytes 786436
  44.6 5.4 %copy-start.14 = (bf16[256,512]{1,0:T(8,128)(2,1)}, bf16[256,512]{1,0:T(8,128)(2,1)S(1)}, u32[]{:S(2)}) copy-start(bf16[256,512]{1,0:T(8,128)(2,1)S(1)} %collective-permute-done.14.refs_16_) | copy-start | bytes 786436
  49.5 1.4 %copy-start.16 = (bf16[256,512]{1,0:T(8,128)(2,1)}, bf16[256,512]{1,0:T(8,128)(2,1)S(1)}, u32[]{:S(2)}) copy-start(bf16[256,512]{1,0:T(8,128)(2,1)S(1)} %collective-permute-done.12.refs_14_) | copy-start | bytes 786436
  49.5 2.1 %copy-start.6 = (bf16[128,4096]{1,0:T(8,128)(2,1)}, bf16[128,4096]{1,0:T(8,128)(2,1)S(1)}, u32[]{:S(2)}) copy-start(bf16[128,4096]{1,0:T(8,128)(2,1)S(1)} %collective-permute-done.10.refs_2_.refs_1_) | copy-start | bytes 3145732
  49.5 8.2 %collective-permute-start.16 = (bf16[256,512]{1,0:T(8,128)(2,1)}, bf16[256,512]{1,0:T(8,128)(2,1)S(1)}, u32[]{:S(2)}, u32[]{:S(2)}) collective-permute-start(bf16[256,512]{1,0:T(8,128)(2,1)} %collective-permute-done.6.refs_9_), channel_id=1, source_target_pairs={{0,2},{1,3},{2,0},{3,1},{4,6},{5,7},{6,4},{7,5},{8,10},{9,11},{10,... | collective-permute-start | bytes 786440 | tf_op jit(solution)/shard_map/ppermute | solution.py:92
  50.1 7.6 %collective-permute-start.17 = (bf16[256,512]{1,0:T(8,128)(2,1)}, bf16[256,512]{1,0:T(8,128)(2,1)S(1)}, u32[]{:S(2)}, u32[]{:S(2)}) collective-permute-start(bf16[256,512]{1,0:T(8,128)(2,1)} %collective-permute-done.11.refs_13_), channel_id=1, source_target_pairs={{0,4},{1,5},{2,6},{3,7},{4,0},{5,1},{6,2},{7,3},{8,12},{9,13},{10,... | collective-permute-start | bytes 786440 | tf_op jit(solution)/shard_map/ppermute | solution.py:92
  50.9 6.8 %collective-permute-start.15 = (bf16[144,512]{1,0:T(8,128)(2,1)}, bf16[144,512]{1,0:T(8,128)(2,1)S(1)}, u32[]{:S(2)}, u32[]{:S(2)}) collective-permute-start(bf16[144,512]{1,0:T(8,128)(2,1)} %get-tuple-element.90), channel_id=1, source_target_pairs={{0,1},{1,0},{2,3},{3,2},{4,5},{5,4},{6,7},{7,6},{8,9},{9,8},{10,11... | collective-permute-start | bytes 442376 | tf_op jit(solution)/shard_map/ppermute | solution.py:92
  57.7 21.1 %collective-permute-start.20 = (bf16[4,128,1024]{2,1,0:T(8,128)(2,1)S(1)}, bf16[4,128,1024]{2,1,0:T(8,128)(2,1)S(1)}, u32[]{:S(2)}, u32[]{:S(2)}) collective-permute-start(bf16[4,128,1024]{2,1,0:T(8,128)(2,1)S(1)} %all-to-all-done.own_ref), channel_id=1, source_target_pairs={{0,1},{1,0},{2,3},{3,2},{4,5},{5,4},{6,7},{7,6},{8,9},{9,8},{10,11... | collective-permute-start | bytes 3145736 | tf_op jit(solution)/shard_map/ppermute | solution.py:92
  62.4 16.3 %collective-permute-start.19 = (bf16[272,512]{1,0:T(8,128)(2,1)}, bf16[272,512]{1,0:T(8,128)(2,1)S(1)}, u32[]{:S(2)}, u32[]{:S(2)}) collective-permute-start(bf16[272,512]{1,0:T(8,128)(2,1)} %get-tuple-element.133.refs_0_), channel_id=1, source_target_pairs={{0,16},{1,17},{2,18},{3,19},{4,20},{5,21},{6,22},{7,23},{8,24},{9,... | collective-permute-start | bytes 835592 | tf_op jit(solution)/shard_map/ppermute | solution.py:92
  63.8 15.0 %collective-permute-start.18 = (bf16[272,512]{1,0:T(8,128)(2,1)}, bf16[272,512]{1,0:T(8,128)(2,1)S(1)}, u32[]{:S(2)}, u32[]{:S(2)}) collective-permute-start(bf16[272,512]{1,0:T(8,128)(2,1)} %get-tuple-element.133.refs_0_), channel_id=1, source_target_pairs={{0,8},{1,9},{2,10},{3,11},{4,12},{5,13},{6,14},{7,15},{8,0},{9,1},... | collective-permute-start | bytes 835592 | tf_op jit(solution)/shard_map/ppermute | solution.py:92
  78.8 8.1 %collective-permute-start.21 = (bf16[272,512]{1,0:T(8,128)(2,1)S(1)}, bf16[272,512]{1,0:T(8,128)(2,1)S(1)}, u32[]{:S(2)}, u32[]{:S(2)}) collective-permute-start(bf16[272,512]{1,0:T(8,128)(2,1)S(1)} %collective-permute-done.19.refs_2_), channel_id=1, source_target_pairs={{0,8},{1,9},{2,10},{3,11},{4,12},{5,13},{6,14},{7,15},{8,0},{9,1},... | collective-permute-start | bytes 835592 | tf_op jit(solution)/shard_map/ppermute | solution.py:92
  86.9 17.6 %collective-permute-start.26 = (bf16[3584,512]{1,0:T(8,128)(2,1)}, bf16[3584,512]{1,0:T(8,128)(2,1)}, u32[]{:S(2)}, u32[]{:S(2)}) collective-permute-start(bf16[3584,512]{1,0:T(8,128)(2,1)} %get-tuple-element.130.refs_0_), channel_id=1, source_target_pairs={{0,1},{1,0},{2,3},{3,2},{4,5},{5,4},{6,7},{7,6},{8,9},{9,8},{10,11... | collective-permute-start | bytes 11010056 | tf_op jit(solution)/shard_map/ppermute | solution.py:92
  86.9 1.0 copy-start.1
  87.9 14.3 %copy-start.3 = (bf16[512,512]{1,0:T(8,128)(2,1)S(1)}, bf16[512,512]{1,0:T(8,128)(2,1)}, u32[]{:S(2)}) copy-start(bf16[512,512]{1,0:T(8,128)(2,1)} %get-tuple-element.131.refs_2_) | copy-start | bytes 1572868
  88.9 15.7 %copy-start.4 = (s32[16]{0:T(128)S(1)}, s32[16]{0:T(128)}, u32[]{:S(2)}) copy-start(s32[16]{0:T(128)} %stack.87.refs_0_.chips_ref) | copy-start | bytes 196
  88.9 7.3 %collective-permute-start.22 = (bf16[128,512]{1,0:T(8,128)(2,1)S(1)}, bf16[128,512]{1,0:T(8,128)(2,1)S(1)}, u32[]{:S(2)}, u32[]{:S(2)}) collective-permute-start(bf16[128,512]{1,0:T(8,128)(2,1)S(1)} %get-tuple-element.125), channel_id=1, source_target_pairs={{0,2},{1,3},{2,0},{3,1},{4,6},{5,7},{6,4},{7,5},{8,10},{9,11},{10,... | collective-permute-start | bytes 393224 | tf_op jit(solution)/shard_map/ppermute | solution.py:92
  90.2 8.4 %collective-permute-start.23 = (bf16[128,512]{1,0:T(8,128)(2,1)S(1)}, bf16[128,512]{1,0:T(8,128)(2,1)S(1)}, u32[]{:S(2)}, u32[]{:S(2)}) collective-permute-start(bf16[128,512]{1,0:T(8,128)(2,1)S(1)} %get-tuple-element.126), channel_id=1, source_target_pairs={{0,4},{1,5},{2,6},{3,7},{4,0},{5,1},{6,2},{7,3},{8,12},{9,13},{10,... | collective-permute-start | bytes 393224 | tf_op jit(solution)/shard_map/ppermute | solution.py:92
  91.7 6.9 %collective-permute-start.24 = (bf16[128,512]{1,0:T(8,128)(2,1)S(1)}, bf16[128,512]{1,0:T(8,128)(2,1)S(1)}, u32[]{:S(2)}, u32[]{:S(2)}) collective-permute-start(bf16[128,512]{1,0:T(8,128)(2,1)S(1)} %get-tuple-element.127), channel_id=1, source_target_pairs={{0,6},{1,7},{2,4},{3,5},{4,2},{5,3},{6,0},{7,1},{8,14},{9,15},{10,... | collective-permute-start | bytes 393224 | tf_op jit(solution)/shard_map/ppermute | solution.py:92
  92.4 1.0 copy-start.2
  98.6 18.9 %all-to-all-start.1 = ((bf16[8,128,512]{2,1,0:T(8,128)(2,1)}), bf16[8,128,512]{2,1,0:T(8,128)(2,1)S(1)}, u32[]{:S(2)}, u32[]{:S(2)}) async-start(bf16[8,128,512]{2,1,0:T(8,128)(2,1)} %bitcast.26), calls=%async_computation.1 | async-start | bytes 2097152 | tf_op jit(solution)/shard_map/all_to_all | solution.py:509
  102.2 2.4 %collective-permute-start.27 = (bf16[512,512]{1,0:T(8,128)(2,1)S(1)}, bf16[512,512]{1,0:T(8,128)(2,1)S(1)}, u32[]{:S(2)}, u32[]{:S(2)}) collective-permute-start(bf16[512,512]{1,0:T(8,128)(2,1)S(1)} %copy-done.3), channel_id=1, source_target_pairs={{0,1},{1,0},{2,3},{3,2},{4,5},{5,4},{6,7},{7,6},{8,9},{9,8},{10,11... | collective-permute-start | bytes 1572872 | tf_op jit(solution)/shard_map/ppermute | solution.py:92
  102.6 1.9 %collective-permute-start.25 = (bf16[4,64,512]{2,1,0:T(8,128)(2,1)S(1)}, bf16[4,64,512]{2,1,0:T(8,128)(2,1)S(1)}, u32[]{:S(2)}, u32[]{:S(2)}) collective-permute-start(bf16[4,64,512]{2,1,0:T(8,128)(2,1)S(1)} %get-tuple-element.129), channel_id=1, source_target_pairs={{0,1},{1,0},{2,3},{3,2},{4,5},{5,4},{6,7},{7,6},{8,9},{9,8},{10,11... | collective-permute-start | bytes 786440 | tf_op jit(solution)/shard_map/ppermute | solution.py:92
  104.6 2.0 %copy-start = (bf16[3584,512]{1,0:T(8,128)(2,1)S(1)}, bf16[3584,512]{1,0:T(8,128)(2,1)}, u32[]{:S(2)}) copy-start(bf16[3584,512]{1,0:T(8,128)(2,1)} %get-tuple-element.130.refs_0_) | copy-start | bytes 11010052
  (3 other events, 2.3 us)

commit v16 on v15

--- a/solution.py
+++ b/solution.py
@@ -178,39 +178,28 @@
 
 
 def select_kernel(me_ref, *refs):
-    deltas, sent, (held, sems) = refs[:4], refs[4:8], refs[8:]
+    *deltas, sent_ref, held, sems = refs
     copies = fetch([(ref, held.at[n]) for n, ref in enumerate(deltas)], sems)
     rows = (held.shape[1] - CODE_ROWS) // 2
-    per_core = sent[0].shape[0] // 2
-    per_chip = per_core // len(deltas)
-    iota = lax.broadcasted_iota(jnp.int32, (8 * per_chip, 2 * rows), 0)
-    block = lax.shift_right_logical(iota, per_chip.bit_length() - 1)
+    per_chip = sent_ref.shape[1] // len(deltas)
+    iota = lax.broadcasted_iota(jnp.int32, (PLANE * per_chip, 2 * rows), 0)
+    wanted = (me_ref[0] & -PLANE) + lax.shift_right_logical(iota, per_chip.bit_length() - 1)
     slot = iota & (per_chip - 1)
-    wanted = ((me_ref[0] & -2) ^ (block & -2)) | (block & 1)
     for n in range(len(deltas)):
         copies[n].wait()
         code = held[n, 2 * rows :, : 2 * rows].astype(jnp.float32).astype(jnp.int32)
         hot = (wanted == code[0:1, :]) & (slot == code[1:2, :])
         found = dot(hot.astype(jnp.bfloat16), held[n, : 2 * rows, :], ((1,), (0,)))
         found = found.astype(jnp.bfloat16)
-        for place in range(8):
-            at = place % 2 * per_core + n * per_chip
-            sent[place // 2][at : at + per_chip, :] = found[
+        for place in range(PLANE):
+            sent_ref[place, n * per_chip : (n + 1) * per_chip, :] = found[
                 place * per_chip : (place + 1) * per_chip, :
             ]
 
 
-def share_kernel(me_ref, *refs):
-    got, (keep_ref, give_ref) = refs[:4], refs[4:]
-    count = keep_ref.shape[1]
-    core = me_ref[0] & 1
-    for n, ref in enumerate(got):
-        keep_ref[n] = ref[pl.ds(pl.multiple_of(core * count, count), count), :]
-        give_ref[n] = ref[pl.ds(pl.multiple_of((1 - core) * count, count), count), :]
-
-
 def weight_grad_kernel(me_ref, own_ref, mate_ref, *refs):
-    *deltas, part_ref, hidden, held, acc, sems = refs
+    *deltas, own_part_ref, part_x, part_y, part_both, hidden, held, acc, sems = refs
+    part_refs = (part_x, part_y, part_both)
     plane = lax.shift_right_logical(me_ref[0], 3)
     core = me_ref[0] & 1
     rows = own_ref.shape[1]
@@ -232,21 +221,34 @@
         if first == 0:
             acc[...] = terms
         else:
-            part_ref[...] = (acc[...] + terms).astype(jnp.bfloat16)
-
-
-def sum_kernel(norm, parts_ref, grad_ref):
-    half = parts_ref.shape[3]
-    for side in range(2):
-        total = parts_ref[0, side].astype(jnp.float32)
-        for chip in range(1, parts_ref.shape[0]):
-            total += parts_ref[chip, side].astype(jnp.float32)
-        grad_ref[:, side * half : (side + 1) * half] = total / norm
-
-
-def row_grad_kernel(chips_ref, me_ref, own_got_ref, mate_got_ref, *refs):
+            acc[...] += terms
+    count = own_part_ref.shape[0]
+    for ref, mask in zip((own_part_ref, *part_refs), PLANE_MASKS):
+        place = lax.shift_right_logical((me_ref[0] ^ mask) & 6, 1)
+        at = pl.multiple_of(place * count, count)
+        ref[...] = acc[pl.ds(at, count), :].astype(ref.dtype)
+
+
+def sum_kernel(me_ref, own_ref, *refs):
+    *part_refs, keep_ref, give_ref = refs
+    count = keep_ref.shape[0]
+    for ref, core in ((keep_ref, me_ref[0] & 1), (give_ref, 1 - (me_ref[0] & 1))):
+        here = pl.ds(pl.multiple_of(core * count, count), count)
+        total = own_ref[here, :]
+        for part_ref in part_refs:
+            total += part_ref[here, :].astype(jnp.float32)
+        ref[...] = total
+
+
+def join_kernel(norm, me_ref, own_ref, mate_ref, grad_ref):
+    half = own_ref.shape[1]
+    for ref, core in ((own_ref, me_ref[0] & 1), (mate_ref, 1 - (me_ref[0] & 1))):
+        grad_ref[:, pl.ds(pl.multiple_of(core * half, half), half)] = ref[...] / norm
+
+
+def row_grad_kernel(chips_ref, me_ref, got_ref, *refs):
     weight_refs, (out_ref, weights, out, rows_ref, sems) = refs[:4], refs[4:]
-    chips, count, half = own_got_ref.shape
+    chips, _, count, half = got_ref.shape
     block = count // 4
     depth = half // 2
     pieces = weights.shape[1] // depth
@@ -262,12 +264,13 @@
             ref = weight_refs[side] if n < first else weight_refs[2 + side]
             pairs.append((rows_of(ref, n % first), rows_of(weights.at[side], n)))
     copies = fetch(pairs, sems)
-    for side, got_ref in enumerate((own_got_ref, mate_got_ref)):
-        for chip, mask in enumerate(PLANE_MASKS):
-            place = lax.shift_right_logical((me_ref[0] ^ mask) & 6, 1)
-            for n in range(4):
-                at = pl.multiple_of(((level ^ n) * chips + place) * block, block)
-                rows_ref[side, pl.ds(at, block), :] = got_ref[chip, n * block : (n + 1) * block, :]
+    core = me_ref[0] & 1
+    for chip in range(chips):
+        for n in range(4):
+            at = pl.multiple_of(((level ^ n) * chips + chip) * block, block)
+            for side in range(2):
+                rows = got_ref[chip, pl.ds(core ^ side, 1), n * block : (n + 1) * block, :]
+                rows_ref[side, pl.ds(at, block), :] = rows[0]
     written = []
     for n in range(pieces):
         for copy in copies[2 * n : 2 * n + 2]:
@@ -481,22 +484,30 @@
     delta_room = pltpu.VMEM((levels, *delta.shape), jnp.bfloat16)
     selected = pl.pallas_call(
         select_kernel,
-        out_shape=[jax.ShapeDtypeStruct((2 * count, half_cols), jnp.bfloat16)] * 4,
+        out_shape=jax.ShapeDtypeStruct((PLANE, count, half_cols), jnp.bfloat16),
         in_specs=[SCALAR] + anywhere(levels),
-        out_specs=vmem(4),
+        out_specs=vmem(1)[0],
         scratch_shapes=[delta_room, pltpu.SemaphoreType.DMA((levels,))],
         compiler_params=grant(16),
         name="select",
     )(me_scalar, *deltas)
-    got = [
-        swap(value, mask) if mask else value for value, mask in zip(selected, PLANE_MASKS)
-    ]
+    got = lax.all_to_all(
+        selected,
+        "dp",
+        split_axis=0,
+        concat_axis=0,
+        axis_index_groups=[[z * PLANE + p for p in range(PLANE)] for z in range(levels)],
+        tiled=True,
+    ).reshape(PLANE // 2, 2, count, half_cols)
+
     shard = width_model // size
-    terms = pl.pallas_call(
+    mine_terms = jax.ShapeDtypeStruct((wide // 4, half_cols), jnp.float32)
+    sent_terms = jax.ShapeDtypeStruct(mine_terms.shape, jnp.bfloat16)
+    own_part, *parts = pl.pallas_call(
         weight_grad_kernel,
-        out_shape=jax.ShapeDtypeStruct((wide, half_cols), jnp.bfloat16),
+        out_shape=(mine_terms, *[sent_terms] * 3),
         in_specs=[SCALAR] + anywhere(2 + levels),
-        out_specs=vmem(1)[0],
+        out_specs=tuple(vmem(4)),
         scratch_shapes=[
             pltpu.VMEM((levels * 2 * rows, wide), jnp.bfloat16),
             pltpu.VMEM((levels * 2 * rows, half_cols), jnp.bfloat16),
@@ -505,30 +516,13 @@
         ],
         compiler_params=grant(16),
         name="weight_grad",
-    )(me_scalar, own_features, mate_features, after(delta, *selected), *deltas[1:])
-    parts = lax.all_to_all(
-        after(terms, *got).reshape(PLANE, shard, half_cols),
-        "dp",
-        split_axis=0,
-        concat_axis=0,
-        axis_index_groups=[[z * PLANE + p for p in range(PLANE)] for z in range(levels)],
-        tiled=True,
-    ).reshape(PLANE // 2, 2, shard, half_cols)
-
-    own_got, give_got = pl.pallas_call(
-        share_kernel,
-        out_shape=[jax.ShapeDtypeStruct((4, count, half_cols), jnp.bfloat16)] * 2,
-        in_specs=[SCALAR] + vmem(4),
-        out_specs=vmem(2),
-        compiler_params=grant(16),
-        name="share",
-    )(me_scalar, *got)
-    mate_got = swap(give_got, CORE)
+    )(me_scalar, own_features, mate_features, after(delta, selected), *deltas[1:])
+    parts = [swap(part, mask) for part, mask in zip(parts, PLANE_MASKS[1:])]
 
     row_grads = pl.pallas_call(
         row_grad_kernel,
         out_shape=jax.ShapeDtypeStruct((receive, width_model), jnp.bfloat16),
-        in_specs=[SCALAR] * 2 + vmem(2) + anywhere(4),
+        in_specs=[SCALAR] * 2 + vmem(1) + anywhere(4),
         out_specs=anywhere(1)[0],
         scratch_shapes=[
             pltpu.VMEM((2, width_model, half_cols), jnp.bfloat16),
@@ -538,16 +532,25 @@
         ],
         compiler_params=grant(32),
         name="row_grad",
-    )(order, me_scalar, own_got, mate_got, first_weight, mate_first, last_weight, mate_last)
-
+    )(order, me_scalar, got, first_weight, mate_first, last_weight, mate_last)
+
+    half_grad = jax.ShapeDtypeStruct((shard, half_cols), jnp.float32)
+    keep_grad, give_grad = pl.pallas_call(
+        sum_kernel,
+        out_shape=(half_grad, half_grad),
+        in_specs=[SCALAR] + vmem(4),
+        out_specs=tuple(vmem(2)),
+        compiler_params=grant(16),
+        name="sum",
+    )(me_scalar, after(own_part, row_grads), *parts)
     key_grad = pl.pallas_call(
-        functools.partial(sum_kernel, math.sqrt(rows * size)),
+        functools.partial(join_kernel, math.sqrt(rows * size)),
         out_shape=jax.ShapeDtypeStruct((shard, cols), jnp.float32),
-        in_specs=vmem(1),
+        in_specs=[SCALAR] + vmem(2),
         out_specs=vmem(1)[0],
         compiler_params=grant(16),
-        name="sum",
-    )(after(parts, row_grads))
+        name="join",
+    )(me_scalar, keep_grad, swap(give_grad, CORE))
     return (row_grads, key_grad)
 
 

time: 119 us -> 119 us (level)
  waiting for transfers between devices: 44.5 us -> 41.9 us
  local copies, waits for them, and re-layouts: 7.26 us -> 9.6 us
    ppermute x28, waiting for transfers between devices: 43.4 us -> 39.7 us  [swap(): return lax.ppermute(value, 'dp', [(i, i ^ mask) for i in range(size)])]
    unnamed x42 -> x46, local copies, waits for them, and re-layouts: 4.27 us -> 6.68 us
  transfers between devices with their start and end apart: 30 -> 30, of which waited for: 13 -> 12; matrix products, arithmetic and copies ran while one was open for 5% -> 5% of each run, Pallas kernels for 20% -> 20%
where the time goes in v16:
time: 119 us
  waiting for transfers between devices  41.9 us (35%)
  starting transfers between devices  37.6 us (32%)
  Pallas kernels  25.2 us (21%)
  local copies, waits for them, and re-layouts  9.6 us (8%)
  other arithmetic  3.47 us (3%)
    ppermute x28, waiting for transfers between devices, swap(): return lax.ppermute(value, 'dp', [(i, i ^ mask) for i in range(size)])  39.7 us
    ppermute x28, starting transfers between devices, swap(): return lax.ppermute(value, 'dp', [(i, i ^ mask) for i in range(size)])  29.5 us
    pallas_call x2, Pallas kernels, project(): pl.pallas_call(kernel, out_shape=(*results, jax.ShapeDtypeStruct((count *...  9.9 us
    pallas_call x1, Pallas kernels, per_device_paired(): pl.pallas_call(row_grad_kernel, out_shape=jax.ShapeDtypeStruct((receive,...  9.87 us
    unnamed x46, local copies, waits for them, and re-layouts  6.68 us
    all_to_all x1, starting transfers between devices, per_device_paired(): lax.all_to_all(by_level, 'dp', split_axis=0, concat_axis=0, axis_index_gr...  4.65 us
    all_to_all x1, starting transfers between devices, per_device_paired(): lax.all_to_all(selected, 'dp', split_axis=0, concat_axis=0, axis_index_gr...  3.51 us
    pallas_call x1, Pallas kernels, per_device_paired(): pl.pallas_call(weight_grad_kernel, out_shape=(mine_terms, *[sent_terms] *...  2.75 us
  transfers between devices with their start and end apart: 30, of which 12 were waited for; matrix products, arithmetic and copies ran while one was open for 5% of the time, Pallas kernels for 20%

profile of v16, /device:TPU:0, one launch (start us, length us, event | category | flops | bytes accessed | tf_op | source)
XLA Modules:
  0.0 118.8 jit_solution(10372097700968985345)
XLA Ops:
  0.7 0.5 collective-permute-start
  1.2 1.0 fusion.11
  2.7 4.0 %collective-permute-start.4 = (bf16[256,512]{1,0:T(8,128)(2,1)S(1)}, bf16[256,512]{1,0:T(8,128)(2,1)S(1)}, u32[]{:S(2)}, u32[]{:S(2)}) collective-permute-start(bf16[256,512]{1,0:T(8,128)(2,1)S(1)} %maximum_select_fusion.refs_3_), channel_id=1, source_target_pairs={{0,16},{1,17},{2,18},{3,19},{4,20},{5,21},{6,22},{7,23},{8,24},{9,... | collective-permute-start | bytes 786440 | tf_op jit(solution)/shard_map/ppermute | solution.py:92
  6.7 1.6 %collective-permute-start.3 = (bf16[256,512]{1,0:T(8,128)(2,1)S(1)}, bf16[256,512]{1,0:T(8,128)(2,1)S(1)}, u32[]{:S(2)}, u32[]{:S(2)}) collective-permute-start(bf16[256,512]{1,0:T(8,128)(2,1)S(1)} %maximum_select_fusion.refs_3_), channel_id=1, source_target_pairs={{0,8},{1,9},{2,10},{3,11},{4,12},{5,13},{6,14},{7,15},{8,0},{9,1},... | collective-permute-start | bytes 786440 | tf_op jit(solution)/shard_map/ppermute | solution.py:92
  8.3 1.5 %collective-permute-start.2 = (bf16[256,512]{1,0:T(8,128)(2,1)S(1)}, bf16[256,512]{1,0:T(8,128)(2,1)S(1)}, u32[]{:S(2)}, u32[]{:S(2)}) collective-permute-start(bf16[256,512]{1,0:T(8,128)(2,1)S(1)} %maximum_select_fusion.refs_3_), channel_id=1, source_target_pairs={{0,2},{1,3},{2,0},{3,1},{4,6},{5,7},{6,4},{7,5},{8,10},{9,11},{10,... | collective-permute-start | bytes 786440 | tf_op jit(solution)/shard_map/ppermute | solution.py:92
  9.8 1.5 %collective-permute-start.1 = (bf16[256,512]{1,0:T(8,128)(2,1)S(1)}, bf16[256,512]{1,0:T(8,128)(2,1)S(1)}, u32[]{:S(2)}, u32[]{:S(2)}) collective-permute-start(bf16[256,512]{1,0:T(8,128)(2,1)S(1)} %maximum_select_fusion.refs_3_), channel_id=1, source_target_pairs={{0,4},{1,5},{2,6},{3,7},{4,0},{5,1},{6,2},{7,3},{8,12},{9,13},{10,... | collective-permute-start | bytes 786440 | tf_op jit(solution)/shard_map/ppermute | solution.py:92
  11.3 1.3 %slice_bitcast_fusion.3 = (bf16[1,128,1024]{2,1,0:T(8,128)(2,1)S(1)}, bf16[1,128,1024]{2,1,0:T(8,128)(2,1)S(1)}, bf16[1,128,1024]{2,1,0:T(8,128)(2,1)S(1)}, bf16[1,128,1024]{2,1,0:T(8,128)(2,1)S(1)}) fusion(bf16[128,4096]{1,0:T(8,128)(2,1)} %refs_0_), kind=kLoop, calls=%fused_computation.6 | loop fusion | bytes 2097152 | tf_op jit(solution)/shard_map/stack | solution.py:363
  12.6 1.1 pad_maximum_fusion
  13.9 5.8 %collective-permute-done.4.refs_7_ = bf16[256,512]{1,0:T(8,128)(2,1)S(1)} collective-permute-done((bf16[256,512]{1,0:T(8,128)(2,1)S(1)}, bf16[256,512]{1,0:T(8,128)(2,1)S(1)}, u32[]{:S(2)}, u32[]{:S(2)}) %collective-permute-start.4) | collective-permute-done | bytes 262176 | tf_op jit(solution)/shard_map/ppermute | solution.py:92
  19.7 2.3 %collective-permute-start.6 = (bf16[256,512]{1,0:T(8,128)(2,1)S(1)}, bf16[256,512]{1,0:T(8,128)(2,1)}, u32[]{:S(2)}, u32[]{:S(2)}) collective-permute-start(bf16[256,512]{1,0:T(8,128)(2,1)S(1)} %collective-permute-done.3.refs_6_), channel_id=1, source_target_pairs={{0,4},{1,5},{2,6},{3,7},{4,0},{5,1},{6,2},{7,3},{8,12},{9,13},{10,... | collective-permute-start | bytes 786440 | tf_op jit(solution)/shard_map/ppermute | solution.py:92
  22.0 1.5 %collective-permute-start.5 = (bf16[256,512]{1,0:T(8,128)(2,1)S(1)}, bf16[256,512]{1,0:T(8,128)(2,1)}, u32[]{:S(2)}, u32[]{:S(2)}) collective-permute-start(bf16[256,512]{1,0:T(8,128)(2,1)S(1)} %collective-permute-done.3.refs_6_), channel_id=1, source_target_pairs={{0,2},{1,3},{2,0},{3,1},{4,6},{5,7},{6,4},{7,5},{8,10},{9,11},{10,... | collective-permute-start | bytes 786440 | tf_op jit(solution)/shard_map/ppermute | solution.py:92
  23.5 0.5 collective-permute-start.8
  24.5 4.7 %all-to-all-start = ((bf16[4,128,1024]{2,1,0:T(8,128)(2,1)}), bf16[4,128,1024]{2,1,0:T(8,128)(2,1)S(1)}, u32[]{:S(2)}, u32[]{:S(2)}) async-start(bf16[4,128,1024]{2,1,0:T(8,128)(2,1)} %pad_maximum_fusion), calls=%async_computation | async-start | bytes 2097152 | tf_op jit(solution)/shard_map/all_to_all | solution.py:368
  29.3 1.1 compare_select_fusion
  30.4 0.7 pad_maximum_fusion.1
  31.2 1.5 %collective-permute-done.8.refs_11_ = bf16[256,512]{1,0:T(8,128)(2,1)} collective-permute-done((bf16[256,512]{1,0:T(8,128)(2,1)S(1)}, bf16[256,512]{1,0:T(8,128)(2,1)}, u32[]{:S(2)}, u32[]{:S(2)}) %collective-permute-start.8) | collective-permute-done | bytes 262176 | tf_op jit(solution)/shard_map/ppermute | solution.py:92
  32.6 1.0 collective-permute-done.7.refs_10_
  33.7 1.6 %collective-permute-start.13 = (bf16[256,512]{1,0:T(8,128)(2,1)S(1)}, bf16[256,512]{1,0:T(8,128)(2,1)S(1)}, u32[]{:S(2)}, u32[]{:S(2)}) collective-permute-start(bf16[256,512]{1,0:T(8,128)(2,1)S(1)} %collective-permute-done.1.refs_4_), channel_id=1, source_target_pairs={{0,2},{1,3},{2,0},{3,1},{4,6},{5,7},{6,4},{7,5},{8,10},{9,11},{10,... | collective-permute-start | bytes 786440 | tf_op jit(solution)/shard_map/ppermute | solution.py:92
  35.3 0.5 collective-permute-start.14
  35.8 1.6 %collective-permute-start.12 = (bf16[256,512]{1,0:T(8,128)(2,1)}, bf16[256,512]{1,0:T(8,128)(2,1)S(1)}, u32[]{:S(2)}, u32[]{:S(2)}) collective-permute-start(bf16[256,512]{1,0:T(8,128)(2,1)} %collective-permute-done.9.refs_12_), channel_id=1, source_target_pairs={{0,4},{1,5},{2,6},{3,7},{4,0},{5,1},{6,2},{7,3},{8,12},{9,13},{10,... | collective-permute-start | bytes 786440 | tf_op jit(solution)/shard_map/ppermute | solution.py:92
  37.8 5.1 %collective-permute-done.13.refs_15_ = bf16[256,512]{1,0:T(8,128)(2,1)S(1)} collective-permute-done((bf16[256,512]{1,0:T(8,128)(2,1)S(1)}, bf16[256,512]{1,0:T(8,128)(2,1)S(1)}, u32[]{:S(2)}, u32[]{:S(2)}) %collective-permute-start.13) | collective-permute-done | bytes 262176 | tf_op jit(solution)/shard_map/ppermute | solution.py:92
  42.9 1.8 %collective-permute-done.14.refs_16_ = bf16[256,512]{1,0:T(8,128)(2,1)S(1)} collective-permute-done((bf16[256,512]{1,0:T(8,128)(2,1)}, bf16[256,512]{1,0:T(8,128)(2,1)S(1)}, u32[]{:S(2)}, u32[]{:S(2)}) %collective-permute-start.14) | collective-permute-done | bytes 262176 | tf_op jit(solution)/shard_map/ppermute | solution.py:92
  44.6 4.8 %collective-permute-done.12.refs_14_ = bf16[256,512]{1,0:T(8,128)(2,1)S(1)} collective-permute-done((bf16[256,512]{1,0:T(8,128)(2,1)}, bf16[256,512]{1,0:T(8,128)(2,1)S(1)}, u32[]{:S(2)}, u32[]{:S(2)}) %collective-permute-start.12) | collective-permute-done | bytes 262176 | tf_op jit(solution)/shard_map/ppermute | solution.py:92
  49.5 0.6 collective-permute-start.16
  50.1 0.8 collective-permute-start.17
  50.9 0.6 stack.87.refs_0_.chips_ref
  51.5 6.1 %project.1 = (bf16[3584,512]{1,0:T(8,128)(2,1)}, f32[2,128,512]{2,1,0:T(8,128)}) custom-call(s32[16]{0:T(128)} %stack.87.refs_0_.chips_ref, bf16[128,4096]{1,0:T(8,128)(2,1)} %refs_0_, bf16[128,4096]{1,0:T(8,128)(2,1)} %copy-done.8, bf16[256,512]{1,0:T(8,128)(2,1)} %copy-done.9, bf16[256,512]{1,0:T(8,128)(2,1)} %copy-done.13, bf16[256,512]{1,0:T(8,128)(2,1)} %copy-done.12, ...), custom_call_target="tpu_custom_call" | custom-call | tf_op jit(solution)/shard_map/project/pallas_call | solution.py:418
  57.7 0.7 copy-done.15
  59.0 3.8 %delta.1 = (bf16[272,512]{1,0:T(8,128)(2,1)}, bf16[512,512]{1,0:T(8,128)(2,1)}) custom-call(s32[16]{0:T(128)} %stack.87.refs_0_.chips_ref, s32[1]{0:T(128)} %bitcast.16.me_ref, bf16[144,512]{1,0:T(8,128)(2,1)} %get-tuple-element.109.own_cot_ref, bf16[144,512]{1,0:T(8,128)(2,1)} %copy-done.19, bf16[128,4096]{1,0:T(8,128)(2,1)} %refs_0_, ...), custom_call_target="tpu_custom_call" | custom-call | tf_op jit(solution)/shard_map/delta/pallas_call | solution.py:418
  62.9 1.4 %collective-permute-start.19 = (bf16[272,512]{1,0:T(8,128)(2,1)}, bf16[272,512]{1,0:T(8,128)(2,1)S(1)}, u32[]{:S(2)}, u32[]{:S(2)}) collective-permute-start(bf16[272,512]{1,0:T(8,128)(2,1)} %get-tuple-element.126.refs_0_), channel_id=1, source_target_pairs={{0,16},{1,17},{2,18},{3,19},{4,20},{5,21},{6,22},{7,23},{8,24},{9,... | collective-permute-start | bytes 835592 | tf_op jit(solution)/shard_map/ppermute | solution.py:92
  64.2 3.8 %collective-permute-start.18 = (bf16[272,512]{1,0:T(8,128)(2,1)}, bf16[272,512]{1,0:T(8,128)(2,1)S(1)}, u32[]{:S(2)}, u32[]{:S(2)}) collective-permute-start(bf16[272,512]{1,0:T(8,128)(2,1)} %get-tuple-element.126.refs_0_), channel_id=1, source_target_pairs={{0,8},{1,9},{2,10},{3,11},{4,12},{5,13},{6,14},{7,15},{8,0},{9,1},... | collective-permute-start | bytes 835592 | tf_op jit(solution)/shard_map/ppermute | solution.py:92
  68.1 10.6 %collective-permute-done.19.refs_2_ = bf16[272,512]{1,0:T(8,128)(2,1)S(1)} collective-permute-done((bf16[272,512]{1,0:T(8,128)(2,1)}, bf16[272,512]{1,0:T(8,128)(2,1)S(1)}, u32[]{:S(2)}, u32[]{:S(2)}) %collective-permute-start.19) | collective-permute-done | bytes 278560 | tf_op jit(solution)/shard_map/ppermute | solution.py:92
  79.1 7.2 %collective-permute-done.21.refs_3_ = bf16[272,512]{1,0:T(8,128)(2,1)S(1)} collective-permute-done((bf16[272,512]{1,0:T(8,128)(2,1)S(1)}, bf16[272,512]{1,0:T(8,128)(2,1)S(1)}, u32[]{:S(2)}, u32[]{:S(2)}) %collective-permute-start.21) | collective-permute-done | bytes 278560 | tf_op jit(solution)/shard_map/ppermute | solution.py:92
  86.3 0.5 collective-permute-start.23
  86.8 1.0 copy-done.1
  87.8 1.8 %select.28 = bf16[8,64,512]{2,1,0:T(8,128)(2,1)} custom-call(s32[1]{0:T(128)} %bitcast.16.me_ref, bf16[272,512]{1,0:T(8,128)(2,1)S(1)} %copy-done.1, bf16[272,512]{1,0:T(8,128)(2,1)S(1)} %collective-permute-done.18.refs_1_, bf16[272,512]{1,0:T(8,128)(2,1)S(1)} %collective-permute-done.19.refs_2_, bf16[272,512]{1,0:T(8,128)(2,1)S(1)} %collective-permute-done.21.refs_3_), custom_call_target="tpu_custom_call" | custom-call | tf_op jit(solution)/shard_map/select/pallas_call | solution.py:485
  89.6 3.5 %all-to-all-start.1 = ((bf16[8,64,512]{2,1,0:T(8,128)(2,1)}), bf16[8,64,512]{2,1,0:T(8,128)(2,1)S(1)}, u32[]{:S(2)}, u32[]{:S(2)}) async-start(bf16[8,64,512]{2,1,0:T(8,128)(2,1)} %select.28), calls=%async_computation.1 | async-start | bytes 1048576 | tf_op jit(solution)/shard_map/all_to_all | solution.py:494
  93.1 0.9 copy-done.2
  94.0 2.7 %weight_grad.1 = (f32[256,512]{1,0:T(8,128)S(1)}, bf16[256,512]{1,0:T(8,128)(2,1)}, bf16[256,512]{1,0:T(8,128)(2,1)}, bf16[256,512]{1,0:T(8,128)(2,1)}) custom-call(s32[1]{0:T(128)} %bitcast.16.me_ref, bf16[4,128,1024]{2,1,0:T(8,128)(2,1)S(1)} %all-to-all-done.own_ref, bf16[4,128,1024]{2,1,0:T(8,128)(2,1)S(1)} %collective-permute-done.20.mate_ref, ...), custom_call_target="tpu_custom_call" | custom-call | tf_op jit(solution)/shard_map/weight_grad/pallas_call | solution.py:506
  96.8 0.8 copy-done.4
  97.6 2.0 %collective-permute-start.24 = (bf16[256,512]{1,0:T(8,128)(2,1)}, bf16[256,512]{1,0:T(8,128)(2,1)S(1)}, u32[]{:S(2)}, u32[]{:S(2)}) collective-permute-start(bf16[256,512]{1,0:T(8,128)(2,1)} %get-tuple-element.129), channel_id=1, source_target_pairs={{0,2},{1,3},{2,0},{3,1},{4,6},{5,7},{6,4},{7,5},{8,10},{9,11},{10,... | collective-permute-start | bytes 786440 | tf_op jit(solution)/shard_map/ppermute | solution.py:92
  99.6 1.5 %collective-permute-start.25 = (bf16[256,512]{1,0:T(8,128)(2,1)}, bf16[256,512]{1,0:T(8,128)(2,1)S(1)}, u32[]{:S(2)}, u32[]{:S(2)}) collective-permute-start(bf16[256,512]{1,0:T(8,128)(2,1)} %get-tuple-element.130), channel_id=1, source_target_pairs={{0,4},{1,5},{2,6},{3,7},{4,0},{5,1},{6,2},{7,3},{8,12},{9,13},{10,... | collective-permute-start | bytes 786440 | tf_op jit(solution)/shard_map/ppermute | solution.py:92
  101.1 2.1 %all-to-all-done.1 = bf16[8,64,512]{2,1,0:T(8,128)(2,1)S(1)} async-done(((bf16[8,64,512]{2,1,0:T(8,128)(2,1)}), bf16[8,64,512]{2,1,0:T(8,128)(2,1)S(1)}, u32[]{:S(2)}, u32[]{:S(2)}) %all-to-all-start.1) | async-done | bytes 524320 | tf_op jit(solution)/shard_map/all_to_all | solution.py:494
  103.3 2.0 %copy-done = bf16[3584,512]{1,0:T(8,128)(2,1)S(1)} copy-done((bf16[3584,512]{1,0:T(8,128)(2,1)S(1)}, bf16[3584,512]{1,0:T(8,128)(2,1)}, u32[]{:S(2)}) %copy-start) | copy-done | bytes 3670040
  105.3 1.0 copy-done.3
  106.4 9.9 %row_grad.1 = bf16[256,4096]{1,0:T(8,128)(2,1)} custom-call(s32[16]{0:T(128)S(1)} %copy-done.6, s32[1]{0:T(128)} %bitcast.16.me_ref, bf16[4,2,64,512]{3,2,1,0:T(8,128)(2,1)S(1)} %bitcast.34, bf16[3584,512]{1,0:T(8,128)(2,1)S(1)} %copy-done, bf16[3584,512]{1,0:T(8,128)(2,1)} %collective-permute-done.22.refs_1_, bf16[512,512]{1,0:T(8,128)(2,1)S(1)} %copy-done.3, ...), custom_call_target="tpu_custom_call" | custom-call | tf_op jit(solution)/shard_map/row_grad/pallas_call | solution.py:522
  116.5 1.5 %collective-permute-done.27.mate_ref = f32[128,512]{1,0:T(8,128)S(1)} collective-permute-done((f32[128,512]{1,0:T(8,128)S(1)}, f32[128,512]{1,0:T(8,128)S(1)}, u32[]{:S(2)}, u32[]{:S(2)}) %collective-permute-start.27) | collective-permute-done | bytes 262176 | tf_op jit(solution)/shard_map/ppermute | solution.py:92
  118.0 0.8 join.1
  (83 shorter events, 3.4 us)
Async XLA Ops:
  0.6 23.5 %copy-start.20 = (s32[1,4]{1,0:T(1,128)S(1)}, s32[1,4]{1,0:T(1,128)}, u32[]{:S(2)}) copy-start(s32[1,4]{1,0:T(1,128)} %param.9) | copy-start | bytes 52
  0.6 23.8 %copy-start.21 = (s32[128,1]{0,1:T(1,128)S(1)}, s32[128,1]{0,1:T(1,128)}, u32[]{:S(2)}) copy-start(s32[128,1]{0,1:T(1,128)} %param.8) | copy-start | bytes 1540
  0.7 1.9 %collective-permute-start = (bf16[128,1024]{1,0:T(8,128)(2,1)}, bf16[128,1024]{1,0:T(8,128)(2,1)S(1)}, u32[]{:S(2)}, u32[]{:S(2)}) collective-permute-start(bf16[128,1024]{1,0:T(8,128)(2,1)} %param.11), channel_id=1, source_target_pairs={{0,1},{1,0},{2,3},{3,2},{4,5},{5,4},{6,7},{7,6},{8,9},{9,8},{10,11... | collective-permute-start | bytes 786440 | tf_op jit(solution)/shard_map/ppermute | solution.py:92
  2.6 26.6 %copy-start.22 = (s32[4]{0:T(128)S(1)}, s32[4]{0:T(128)}, u32[]{:S(2)}) copy-start(s32[4]{0:T(128)} %param.10) | copy-start | bytes 52
  2.6 27.8 %copy-start.9 = (bf16[256,512]{1,0:T(8,128)(2,1)}, bf16[256,512]{1,0:T(8,128)(2,1)S(1)}, u32[]{:S(2)}) copy-start(bf16[256,512]{1,0:T(8,128)(2,1)S(1)} %maximum_select_fusion.refs_3_) | copy-start | bytes 786436
  2.7 31.0 %copy-start.7 = (bf16[128,4096]{1,0:T(8,128)(2,1)S(1)}, bf16[128,4096]{1,0:T(8,128)(2,1)}, u32[]{:S(2)}) copy-start(bf16[128,4096]{1,0:T(8,128)(2,1)} %refs_0_) | copy-start | bytes 3145732
  2.7 17.0 %collective-permute-start.4 = (bf16[256,512]{1,0:T(8,128)(2,1)S(1)}, bf16[256,512]{1,0:T(8,128)(2,1)S(1)}, u32[]{:S(2)}, u32[]{:S(2)}) collective-permute-start(bf16[256,512]{1,0:T(8,128)(2,1)S(1)} %maximum_select_fusion.refs_3_), channel_id=1, source_target_pairs={{0,16},{1,17},{2,18},{3,19},{4,20},{5,21},{6,22},{7,23},{8,24},{9,... | collective-permute-start | bytes 786440 | tf_op jit(solution)/shard_map/ppermute | solution.py:92
  6.7 13.0 %collective-permute-start.3 = (bf16[256,512]{1,0:T(8,128)(2,1)S(1)}, bf16[256,512]{1,0:T(8,128)(2,1)S(1)}, u32[]{:S(2)}, u32[]{:S(2)}) collective-permute-start(bf16[256,512]{1,0:T(8,128)(2,1)S(1)} %maximum_select_fusion.refs_3_), channel_id=1, source_target_pairs={{0,8},{1,9},{2,10},{3,11},{4,12},{5,13},{6,14},{7,15},{8,0},{9,1},... | collective-permute-start | bytes 786440 | tf_op jit(solution)/shard_map/ppermute | solution.py:92
  8.3 11.4 %collective-permute-start.2 = (bf16[256,512]{1,0:T(8,128)(2,1)S(1)}, bf16[256,512]{1,0:T(8,128)(2,1)S(1)}, u32[]{:S(2)}, u32[]{:S(2)}) collective-permute-start(bf16[256,512]{1,0:T(8,128)(2,1)S(1)} %maximum_select_fusion.refs_3_), channel_id=1, source_target_pairs={{0,2},{1,3},{2,0},{3,1},{4,6},{5,7},{6,4},{7,5},{8,10},{9,11},{10,... | collective-permute-start | bytes 786440 | tf_op jit(solution)/shard_map/ppermute | solution.py:92
  9.8 9.9 %collective-permute-start.1 = (bf16[256,512]{1,0:T(8,128)(2,1)S(1)}, bf16[256,512]{1,0:T(8,128)(2,1)S(1)}, u32[]{:S(2)}, u32[]{:S(2)}) collective-permute-start(bf16[256,512]{1,0:T(8,128)(2,1)S(1)} %maximum_select_fusion.refs_3_), channel_id=1, source_target_pairs={{0,4},{1,5},{2,6},{3,7},{4,0},{5,1},{6,2},{7,3},{8,12},{9,13},{10,... | collective-permute-start | bytes 786440 | tf_op jit(solution)/shard_map/ppermute | solution.py:92
  13.7 17.5 %collective-permute-start.9 = (bf16[256,512]{1,0:T(8,128)(2,1)S(1)}, bf16[256,512]{1,0:T(8,128)(2,1)}, u32[]{:S(2)}, u32[]{:S(2)}) collective-permute-start(bf16[256,512]{1,0:T(8,128)(2,1)S(1)} %maximum_select_fusion.refs_3_), channel_id=1, source_target_pairs={{0,24},{1,25},{2,26},{3,27},{4,28},{5,29},{6,30},{7,31},{8,16},{9,... | collective-permute-start | bytes 786440 | tf_op jit(solution)/shard_map/ppermute | solution.py:92
  19.7 13.9 %copy-start.10 = (bf16[256,512]{1,0:T(8,128)(2,1)}, bf16[256,512]{1,0:T(8,128)(2,1)S(1)}, u32[]{:S(2)}) copy-start(bf16[256,512]{1,0:T(8,128)(2,1)S(1)} %collective-permute-done.4.refs_7_) | copy-start | bytes 786436
  19.7 13.9 %copy-start.11 = (bf16[256,512]{1,0:T(8,128)(2,1)}, bf16[256,512]{1,0:T(8,128)(2,1)S(1)}, u32[]{:S(2)}) copy-start(bf16[256,512]{1,0:T(8,128)(2,1)S(1)} %collective-permute-done.3.refs_6_) | copy-start | bytes 786436
  19.7 10.7 %copy-start.12 = (bf16[256,512]{1,0:T(8,128)(2,1)}, bf16[256,512]{1,0:T(8,128)(2,1)S(1)}, u32[]{:S(2)}) copy-start(bf16[256,512]{1,0:T(8,128)(2,1)S(1)} %collective-permute-done.2.refs_5_) | copy-start | bytes 786436
  19.7 31.8 %copy-start.13 = (bf16[256,512]{1,0:T(8,128)(2,1)}, bf16[256,512]{1,0:T(8,128)(2,1)S(1)}, u32[]{:S(2)}) copy-start(bf16[256,512]{1,0:T(8,128)(2,1)S(1)} %collective-permute-done.1.refs_4_) | copy-start | bytes 786436
  19.7 11.5 %collective-permute-start.6 = (bf16[256,512]{1,0:T(8,128)(2,1)S(1)}, bf16[256,512]{1,0:T(8,128)(2,1)}, u32[]{:S(2)}, u32[]{:S(2)}) collective-permute-start(bf16[256,512]{1,0:T(8,128)(2,1)S(1)} %collective-permute-done.3.refs_6_), channel_id=1, source_target_pairs={{0,4},{1,5},{2,6},{3,7},{4,0},{5,1},{6,2},{7,3},{8,12},{9,13},{10,... | collective-permute-start | bytes 786440 | tf_op jit(solution)/shard_map/ppermute | solution.py:92
  22.0 9.1 %collective-permute-start.5 = (bf16[256,512]{1,0:T(8,128)(2,1)S(1)}, bf16[256,512]{1,0:T(8,128)(2,1)}, u32[]{:S(2)}, u32[]{:S(2)}) collective-permute-start(bf16[256,512]{1,0:T(8,128)(2,1)S(1)} %collective-permute-done.3.refs_6_), channel_id=1, source_target_pairs={{0,2},{1,3},{2,0},{3,1},{4,6},{5,7},{6,4},{7,5},{8,10},{9,11},{10,... | collective-permute-start | bytes 786440 | tf_op jit(solution)/shard_map/ppermute | solution.py:92
  23.5 9.1 %collective-permute-start.8 = (bf16[256,512]{1,0:T(8,128)(2,1)S(1)}, bf16[256,512]{1,0:T(8,128)(2,1)}, u32[]{:S(2)}, u32[]{:S(2)}) collective-permute-start(bf16[256,512]{1,0:T(8,128)(2,1)S(1)} %collective-permute-done.4.refs_7_), channel_id=1, source_target_pairs={{0,4},{1,5},{2,6},{3,7},{4,0},{5,1},{6,2},{7,3},{8,12},{9,13},{10,... | collective-permute-start | bytes 786440 | tf_op jit(solution)/shard_map/ppermute | solution.py:92
  24.0 9.6 %collective-permute-start.7 = (bf16[256,512]{1,0:T(8,128)(2,1)S(1)}, bf16[256,512]{1,0:T(8,128)(2,1)}, u32[]{:S(2)}, u32[]{:S(2)}) collective-permute-start(bf16[256,512]{1,0:T(8,128)(2,1)S(1)} %collective-permute-done.4.refs_7_), channel_id=1, source_target_pairs={{0,2},{1,3},{2,0},{3,1},{4,6},{5,7},{6,4},{7,5},{8,10},{9,11},{10,... | collective-permute-start | bytes 786440 | tf_op jit(solution)/shard_map/ppermute | solution.py:92
  24.5 33.1 %all-to-all-start = ((bf16[4,128,1024]{2,1,0:T(8,128)(2,1)}), bf16[4,128,1024]{2,1,0:T(8,128)(2,1)S(1)}, u32[]{:S(2)}, u32[]{:S(2)}) async-start(bf16[4,128,1024]{2,1,0:T(8,128)(2,1)} %pad_maximum_fusion), calls=%async_computation | async-start | bytes 2097152 | tf_op jit(solution)/shard_map/all_to_all | solution.py:368
  33.6 15.8 %collective-permute-start.10 = (bf16[128,4096]{1,0:T(8,128)(2,1)S(1)}, bf16[128,4096]{1,0:T(8,128)(2,1)S(1)}, u32[]{:S(2)}, u32[]{:S(2)}) collective-permute-start(bf16[128,4096]{1,0:T(8,128)(2,1)S(1)} %copy-done.7), channel_id=1, source_target_pairs={{0,1},{1,0},{2,3},{3,2},{4,5},{5,4},{6,7},{7,6},{8,9},{9,8},{10,11... | collective-permute-start | bytes 3145736 | tf_op jit(solution)/shard_map/ppermute | solution.py:92
  33.7 9.2 %collective-permute-start.13 = (bf16[256,512]{1,0:T(8,128)(2,1)S(1)}, bf16[256,512]{1,0:T(8,128)(2,1)S(1)}, u32[]{:S(2)}, u32[]{:S(2)}) collective-permute-start(bf16[256,512]{1,0:T(8,128)(2,1)S(1)} %collective-permute-done.1.refs_4_), channel_id=1, source_target_pairs={{0,2},{1,3},{2,0},{3,1},{4,6},{5,7},{6,4},{7,5},{8,10},{9,11},{10,... | collective-permute-start | bytes 786440 | tf_op jit(solution)/shard_map/ppermute | solution.py:92
  35.3 9.4 %collective-permute-start.14 = (bf16[256,512]{1,0:T(8,128)(2,1)}, bf16[256,512]{1,0:T(8,128)(2,1)S(1)}, u32[]{:S(2)}, u32[]{:S(2)}) collective-permute-start(bf16[256,512]{1,0:T(8,128)(2,1)} %collective-permute-done.7.refs_10_), channel_id=1, source_target_pairs={{0,4},{1,5},{2,6},{3,7},{4,0},{5,1},{6,2},{7,3},{8,12},{9,13},{10,... | collective-permute-start | bytes 786440 | tf_op jit(solution)/shard_map/ppermute | solution.py:92
  35.8 13.7 %collective-permute-start.12 = (bf16[256,512]{1,0:T(8,128)(2,1)}, bf16[256,512]{1,0:T(8,128)(2,1)S(1)}, u32[]{:S(2)}, u32[]{:S(2)}) collective-permute-start(bf16[256,512]{1,0:T(8,128)(2,1)} %collective-permute-done.9.refs_12_), channel_id=1, source_target_pairs={{0,4},{1,5},{2,6},{3,7},{4,0},{5,1},{6,2},{7,3},{8,12},{9,13},{10,... | collective-permute-start | bytes 786440 | tf_op jit(solution)/shard_map/ppermute | solution.py:92
  37.3 12.2 %collective-permute-start.11 = (bf16[256,512]{1,0:T(8,128)(2,1)}, bf16[256,512]{1,0:T(8,128)(2,1)}, u32[]{:S(2)}, u32[]{:S(2)}) collective-permute-start(bf16[256,512]{1,0:T(8,128)(2,1)} %collective-permute-done.9.refs_12_), channel_id=1, source_target_pairs={{0,2},{1,3},{2,0},{3,1},{4,6},{5,7},{6,4},{7,5},{8,10},{9,11},{10,... | collective-permute-start | bytes 786440 | tf_op jit(solution)/shard_map/ppermute | solution.py:92
  42.9 6.6 %copy-start.14 = (bf16[256,512]{1,0:T(8,128)(2,1)}, bf16[256,512]{1,0:T(8,128)(2,1)S(1)}, u32[]{:S(2)}) copy-start(bf16[256,512]{1,0:T(8,128)(2,1)S(1)} %collective-permute-done.13.refs_15_) | copy-start | bytes 786436
  44.6 5.4 %copy-start.16 = (bf16[256,512]{1,0:T(8,128)(2,1)}, bf16[256,512]{1,0:T(8,128)(2,1)S(1)}, u32[]{:S(2)}) copy-start(bf16[256,512]{1,0:T(8,128)(2,1)S(1)} %collective-permute-done.14.refs_16_) | copy-start | bytes 786436
  49.5 1.4 %copy-start.18 = (bf16[256,512]{1,0:T(8,128)(2,1)}, bf16[256,512]{1,0:T(8,128)(2,1)S(1)}, u32[]{:S(2)}) copy-start(bf16[256,512]{1,0:T(8,128)(2,1)S(1)} %collective-permute-done.12.refs_14_) | copy-start | bytes 786436
  49.5 2.0 %copy-start.8 = (bf16[128,4096]{1,0:T(8,128)(2,1)}, bf16[128,4096]{1,0:T(8,128)(2,1)S(1)}, u32[]{:S(2)}) copy-start(bf16[128,4096]{1,0:T(8,128)(2,1)S(1)} %collective-permute-done.10.refs_2_.refs_1_) | copy-start | bytes 3145732
  49.5 8.1 %collective-permute-start.16 = (bf16[256,512]{1,0:T(8,128)(2,1)}, bf16[256,512]{1,0:T(8,128)(2,1)S(1)}, u32[]{:S(2)}, u32[]{:S(2)}) collective-permute-start(bf16[256,512]{1,0:T(8,128)(2,1)} %collective-permute-done.6.refs_9_), channel_id=1, source_target_pairs={{0,2},{1,3},{2,0},{3,1},{4,6},{5,7},{6,4},{7,5},{8,10},{9,11},{10,... | collective-permute-start | bytes 786440 | tf_op jit(solution)/shard_map/ppermute | solution.py:92
  50.1 7.6 %collective-permute-start.17 = (bf16[256,512]{1,0:T(8,128)(2,1)}, bf16[256,512]{1,0:T(8,128)(2,1)S(1)}, u32[]{:S(2)}, u32[]{:S(2)}) collective-permute-start(bf16[256,512]{1,0:T(8,128)(2,1)} %collective-permute-done.11.refs_13_), channel_id=1, source_target_pairs={{0,4},{1,5},{2,6},{3,7},{4,0},{5,1},{6,2},{7,3},{8,12},{9,13},{10,... | collective-permute-start | bytes 786440 | tf_op jit(solution)/shard_map/ppermute | solution.py:92
  50.9 6.7 %collective-permute-start.15 = (bf16[144,512]{1,0:T(8,128)(2,1)}, bf16[144,512]{1,0:T(8,128)(2,1)S(1)}, u32[]{:S(2)}, u32[]{:S(2)}) collective-permute-start(bf16[144,512]{1,0:T(8,128)(2,1)} %get-tuple-element.89), channel_id=1, source_target_pairs={{0,1},{1,0},{2,3},{3,2},{4,5},{5,4},{6,7},{7,6},{8,9},{9,8},{10,11... | collective-permute-start | bytes 442376 | tf_op jit(solution)/shard_map/ppermute | solution.py:92
  57.6 1.4 %copy-start.19 = (bf16[144,512]{1,0:T(8,128)(2,1)}, bf16[144,512]{1,0:T(8,128)(2,1)S(1)}, u32[]{:S(2)}) copy-start(bf16[144,512]{1,0:T(8,128)(2,1)S(1)} %collective-permute-done.15.mate_cot_ref) | copy-start | bytes 442372
  58.5 20.3 %collective-permute-start.20 = (bf16[4,128,1024]{2,1,0:T(8,128)(2,1)S(1)}, bf16[4,128,1024]{2,1,0:T(8,128)(2,1)S(1)}, u32[]{:S(2)}, u32[]{:S(2)}) collective-permute-start(bf16[4,128,1024]{2,1,0:T(8,128)(2,1)S(1)} %all-to-all-done.own_ref), channel_id=1, source_target_pairs={{0,1},{1,0},{2,3},{3,2},{4,5},{5,4},{6,7},{7,6},{8,9},{9,8},{10,11... | collective-permute-start | bytes 3145736 | tf_op jit(solution)/shard_map/ppermute | solution.py:92
  62.8 40.4 %copy-start.6 = (s32[16]{0:T(128)S(1)}, s32[16]{0:T(128)}, u32[]{:S(2)}) copy-start(s32[16]{0:T(128)} %stack.87.refs_0_.chips_ref) | copy-start | bytes 196
  62.9 15.8 %collective-permute-start.19 = (bf16[272,512]{1,0:T(8,128)(2,1)}, bf16[272,512]{1,0:T(8,128)(2,1)S(1)}, u32[]{:S(2)}, u32[]{:S(2)}) collective-permute-start(bf16[272,512]{1,0:T(8,128)(2,1)} %get-tuple-element.126.refs_0_), channel_id=1, source_target_pairs={{0,16},{1,17},{2,18},{3,19},{4,20},{5,21},{6,22},{7,23},{8,24},{9,... | collective-permute-start | bytes 835592 | tf_op jit(solution)/shard_map/ppermute | solution.py:92
  64.2 14.6 %collective-permute-start.18 = (bf16[272,512]{1,0:T(8,128)(2,1)}, bf16[272,512]{1,0:T(8,128)(2,1)S(1)}, u32[]{:S(2)}, u32[]{:S(2)}) collective-permute-start(bf16[272,512]{1,0:T(8,128)(2,1)} %get-tuple-element.126.refs_0_), channel_id=1, source_target_pairs={{0,8},{1,9},{2,10},{3,11},{4,12},{5,13},{6,14},{7,15},{8,0},{9,1},... | collective-permute-start | bytes 835592 | tf_op jit(solution)/shard_map/ppermute | solution.py:92
  78.8 7.6 %collective-permute-start.21 = (bf16[272,512]{1,0:T(8,128)(2,1)S(1)}, bf16[272,512]{1,0:T(8,128)(2,1)S(1)}, u32[]{:S(2)}, u32[]{:S(2)}) collective-permute-start(bf16[272,512]{1,0:T(8,128)(2,1)S(1)} %collective-permute-done.19.refs_2_), channel_id=1, source_target_pairs={{0,8},{1,9},{2,10},{3,11},{4,12},{5,13},{6,14},{7,15},{8,0},{9,1},... | collective-permute-start | bytes 835592 | tf_op jit(solution)/shard_map/ppermute | solution.py:92
  86.3 16.9 %collective-permute-start.22 = (bf16[3584,512]{1,0:T(8,128)(2,1)}, bf16[3584,512]{1,0:T(8,128)(2,1)}, u32[]{:S(2)}, u32[]{:S(2)}) collective-permute-start(bf16[3584,512]{1,0:T(8,128)(2,1)} %get-tuple-element.123.refs_0_), channel_id=1, source_target_pairs={{0,1},{1,0},{2,3},{3,2},{4,5},{5,4},{6,7},{7,6},{8,9},{9,8},{10,11... | collective-permute-start | bytes 11010056 | tf_op jit(solution)/shard_map/ppermute | solution.py:92
  86.3 16.9 %collective-permute-start.23 = (bf16[512,512]{1,0:T(8,128)(2,1)}, bf16[512,512]{1,0:T(8,128)(2,1)}, u32[]{:S(2)}, u32[]{:S(2)}) collective-permute-start(bf16[512,512]{1,0:T(8,128)(2,1)} %get-tuple-element.124.refs_2_), channel_id=1, source_target_pairs={{0,1},{1,0},{2,3},{3,2},{4,5},{5,4},{6,7},{7,6},{8,9},{9,8},{10,11... | collective-permute-start | bytes 1572872 | tf_op jit(solution)/shard_map/ppermute | solution.py:92
  89.6 13.7 %all-to-all-start.1 = ((bf16[8,64,512]{2,1,0:T(8,128)(2,1)}), bf16[8,64,512]{2,1,0:T(8,128)(2,1)S(1)}, u32[]{:S(2)}, u32[]{:S(2)}) async-start(bf16[8,64,512]{2,1,0:T(8,128)(2,1)} %select.28), calls=%async_computation.1 | async-start | bytes 1048576 | tf_op jit(solution)/shard_map/all_to_all | solution.py:494
  97.6 18.6 %collective-permute-start.24 = (bf16[256,512]{1,0:T(8,128)(2,1)}, bf16[256,512]{1,0:T(8,128)(2,1)S(1)}, u32[]{:S(2)}, u32[]{:S(2)}) collective-permute-start(bf16[256,512]{1,0:T(8,128)(2,1)} %get-tuple-element.129), channel_id=1, source_target_pairs={{0,2},{1,3},{2,0},{3,1},{4,6},{5,7},{6,4},{7,5},{8,10},{9,11},{10,... | collective-permute-start | bytes 786440 | tf_op jit(solution)/shard_map/ppermute | solution.py:92
  99.6 16.7 %collective-permute-start.25 = (bf16[256,512]{1,0:T(8,128)(2,1)}, bf16[256,512]{1,0:T(8,128)(2,1)S(1)}, u32[]{:S(2)}, u32[]{:S(2)}) collective-permute-start(bf16[256,512]{1,0:T(8,128)(2,1)} %get-tuple-element.130), channel_id=1, source_target_pairs={{0,4},{1,5},{2,6},{3,7},{4,0},{5,1},{6,2},{7,3},{8,12},{9,13},{10,... | collective-permute-start | bytes 786440 | tf_op jit(solution)/shard_map/ppermute | solution.py:92
  101.1 15.2 %collective-permute-start.26 = (bf16[256,512]{1,0:T(8,128)(2,1)}, bf16[256,512]{1,0:T(8,128)(2,1)S(1)}, u32[]{:S(2)}, u32[]{:S(2)}) collective-permute-start(bf16[256,512]{1,0:T(8,128)(2,1)} %get-tuple-element.131), channel_id=1, source_target_pairs={{0,6},{1,7},{2,4},{3,5},{4,2},{5,3},{6,0},{7,1},{8,14},{9,15},{10,... | collective-permute-start | bytes 786440 | tf_op jit(solution)/shard_map/ppermute | solution.py:92
  103.3 2.0 %copy-start = (bf16[3584,512]{1,0:T(8,128)(2,1)S(1)}, bf16[3584,512]{1,0:T(8,128)(2,1)}, u32[]{:S(2)}) copy-start(bf16[3584,512]{1,0:T(8,128)(2,1)} %get-tuple-element.123.refs_0_) | copy-start | bytes 11010052
  105.3 1.0 copy-start.3
  106.4 9.9 %copy-start.5 = (f32[256,512]{1,0:T(8,128)S(1)}, f32[256,512]{1,0:T(8,128)}, u32[]{:S(2)}) copy-start(f32[256,512]{1,0:T(8,128)} %copy-done.4) | copy-start | bytes 1572868
  116.4 1.6 %collective-permute-start.27 = (f32[128,512]{1,0:T(8,128)S(1)}, f32[128,512]{1,0:T(8,128)S(1)}, u32[]{:S(2)}, u32[]{:S(2)}) collective-permute-start(f32[128,512]{1,0:T(8,128)S(1)} %get-tuple-element.133), channel_id=1, source_target_pairs={{0,1},{1,0},{2,3},{3,2},{4,5},{5,4},{6,7},{7,6},{8,9},{9,8},{10,11... | collective-permute-start | bytes 786440 | tf_op jit(solution)/shard_map/ppermute | solution.py:92
  (5 other events, 4.3 us)

commit v17 on v16

--- a/solution.py
+++ b/solution.py
@@ -223,10 +223,16 @@
         else:
             acc[...] += terms
     count = own_part_ref.shape[0]
-    for ref, mask in zip((own_part_ref, *part_refs), PLANE_MASKS):
+
+    def block(mask):
         place = lax.shift_right_logical((me_ref[0] ^ mask) & 6, 1)
-        at = pl.multiple_of(place * count, count)
-        ref[...] = acc[pl.ds(at, count), :].astype(ref.dtype)
+        return acc.at[pl.ds(pl.multiple_of(place * count, count), count), :]
+
+    own = pltpu.make_async_copy(block(0), own_part_ref, sems.at[3 * len(deltas)])
+    own.start()
+    for ref, mask in zip(part_refs, PLANE_MASKS[1:]):
+        ref[...] = block(mask)[...].astype(ref.dtype)
+    own.wait()
 
 
 def sum_kernel(me_ref, own_ref, *refs):
@@ -251,7 +257,7 @@
     chips, _, count, half = got_ref.shape
     block = count // 4
     depth = half // 2
-    pieces = weights.shape[1] // depth
+    pieces = weights.shape[0] // depth
     level = lax.shift_right_logical(me_ref[0], 3)
 
     def rows_of(ref, n):
@@ -262,7 +268,8 @@
         first = weight_refs[0].shape[0] // depth
         for side in range(2):
             ref = weight_refs[side] if n < first else weight_refs[2 + side]
-            pairs.append((rows_of(ref, n % first), rows_of(weights.at[side], n)))
+            target = weights.at[n * depth : (n + 1) * depth, side * half : (side + 1) * half]
+            pairs.append((rows_of(ref, n % first), target))
     copies = fetch(pairs, sems)
     core = me_ref[0] & 1
     for chip in range(chips):
@@ -270,20 +277,20 @@
             at = pl.multiple_of(((level ^ n) * chips + chip) * block, block)
             for side in range(2):
                 rows = got_ref[chip, pl.ds(core ^ side, 1), n * block : (n + 1) * block, :]
-                rows_ref[side, pl.ds(at, block), :] = rows[0]
+                rows_ref[pl.ds(at, block), side * half : (side + 1) * half] = rows[0]
     written = []
-    for n in range(pieces):
-        for copy in copies[2 * n : 2 * n + 2]:
+    for first in range(0, pieces, 2):
+        for copy in copies[2 * first : 2 * first + 4]:
             copy.wait()
-        total = dot(rows_ref[0], rows_of(weights.at[0], n)[...], ((1,), (1,)))
-        total += dot(rows_ref[1], rows_of(weights.at[1], n)[...], ((1,), (1,)))
-        out[n] = total.astype(jnp.bfloat16)
-        at = pl.multiple_of(chips_ref[n] * depth, depth)
-        copy = pltpu.make_async_copy(
-            out.at[n], out_ref.at[:, pl.ds(at, depth)], sems.at[2 * pieces + n]
-        )
-        copy.start()
-        written.append(copy)
+        total = dot(rows_ref[...], weights[first * depth : (first + 2) * depth, :], ((1,), (1,)))
+        for n in (first, first + 1):
+            out[n] = total[:, (n - first) * depth : (n - first + 1) * depth].astype(jnp.bfloat16)
+            at = pl.multiple_of(chips_ref[n] * depth, depth)
+            copy = pltpu.make_async_copy(
+                out.at[n], out_ref.at[:, pl.ds(at, depth)], sems.at[2 * pieces + n]
+            )
+            copy.start()
+            written.append(copy)
     for copy in written:
         copy.wait()
 
@@ -300,6 +307,10 @@
 
 def anywhere(count):
     return [pl.BlockSpec(memory_space=pl.ANY)] * count
+
+
+def hbm(count):
+    return [pl.BlockSpec(memory_space=pltpu.HBM)] * count
 
 
 def vmem(count):
@@ -428,7 +439,7 @@
                 pltpu.VMEM((count * depth, half_cols), jnp.bfloat16),
                 pltpu.SemaphoreType.DMA((4 * count,)),
             ],
-            compiler_params=PARAMS,
+            compiler_params=PARAMS if name == "project" else grant(24),
             name=name,
         )(*inputs)
 
@@ -468,7 +479,7 @@
             begun,
             *[have[mask] for mask in last_masks],
         ),
-        [SCALAR] * 2 + vmem(2) + anywhere(2) + vmem(1),
+        [SCALAR] * 2 + vmem(2) + hbm(2) + vmem(1),
         "delta",
     )
 
@@ -485,7 +496,7 @@
     selected = pl.pallas_call(
         select_kernel,
         out_shape=jax.ShapeDtypeStruct((PLANE, count, half_cols), jnp.bfloat16),
-        in_specs=[SCALAR] + anywhere(levels),
+        in_specs=[SCALAR] + hbm(1) + anywhere(levels - 1),
         out_specs=vmem(1)[0],
         scratch_shapes=[delta_room, pltpu.SemaphoreType.DMA((levels,))],
         compiler_params=grant(16),
@@ -506,13 +517,13 @@
     own_part, *parts = pl.pallas_call(
         weight_grad_kernel,
         out_shape=(mine_terms, *[sent_terms] * 3),
-        in_specs=[SCALAR] + anywhere(2 + levels),
-        out_specs=tuple(vmem(4)),
+        in_specs=[SCALAR] + anywhere(2) + hbm(1) + anywhere(levels - 1),
+        out_specs=tuple(hbm(1) + vmem(3)),
         scratch_shapes=[
             pltpu.VMEM((levels * 2 * rows, wide), jnp.bfloat16),
             pltpu.VMEM((levels * 2 * rows, half_cols), jnp.bfloat16),
             pltpu.VMEM((wide, half_cols), jnp.float32),
-            pltpu.SemaphoreType.DMA((3 * levels,)),
+            pltpu.SemaphoreType.DMA((3 * levels + 1,)),
         ],
         compiler_params=grant(16),
         name="weight_grad",
@@ -522,12 +533,12 @@
     row_grads = pl.pallas_call(
         row_grad_kernel,
         out_shape=jax.ShapeDtypeStruct((receive, width_model), jnp.bfloat16),
-        in_specs=[SCALAR] * 2 + vmem(1) + anywhere(4),
+        in_specs=[SCALAR] * 2 + vmem(1) + hbm(4),
         out_specs=anywhere(1)[0],
         scratch_shapes=[
-            pltpu.VMEM((2, width_model, half_cols), jnp.bfloat16),
+            pltpu.VMEM((width_model, cols), jnp.bfloat16),
             pltpu.VMEM((chips, receive, depth), jnp.bfloat16),
-            pltpu.VMEM((2, receive, half_cols), jnp.bfloat16),
+            pltpu.VMEM((receive, cols), jnp.bfloat16),
             pltpu.SemaphoreType.DMA((3 * chips,)),
         ],
         compiler_params=grant(32),

time: 119 us -> 122 us (1.025)
  Pallas kernels: 25.2 us -> 20.5 us
  local copies, waits for them, and re-layouts: 9.6 us -> 14 us
  waiting for transfers between devices: 41.9 us -> 44.6 us
    unnamed x46 -> x48, local copies, waits for them, and re-layouts: 6.68 us -> 11.1 us
    pallas_call x1, Pallas kernels: 9.87 us -> 6.6 us  [per_device_paired(): pl.pallas_call(row_grad_kernel, out_shape=jax.ShapeDtypeStruct((receive,...]
    ppermute x28, waiting for transfers between devices: 39.7 us -> 42 us  [swap(): return lax.ppermute(value, 'dp', [(i, i ^ mask) for i in range(size)])]
    pallas_call x2, Pallas kernels: 9.9 us -> 8.39 us  [project(): pl.pallas_call(kernel, out_shape=(*results, jax.ShapeDtypeStruct((count *...]
  transfers between devices with their start and end apart: 30 -> 30, of which waited for: 12 -> 13; matrix products, arithmetic and copies ran while one was open for 5% -> 5% of each run, Pallas kernels for 20% -> 16%
where the time goes in v17:
time: 122 us; the launch traced here: 121 us
  waiting for transfers between devices  44.6 us (37%)
  starting transfers between devices  37.4 us (31%)
  Pallas kernels  20.5 us (17%)
  local copies, waits for them, and re-layouts  14 us (11%)
  other arithmetic  3.56 us (3%)
    ppermute x28, waiting for transfers between devices, swap(): return lax.ppermute(value, 'dp', [(i, i ^ mask) for i in range(size)])  42 us
    ppermute x28, starting transfers between devices, swap(): return lax.ppermute(value, 'dp', [(i, i ^ mask) for i in range(size)])  29.2 us
    unnamed x48, local copies, waits for them, and re-layouts  11.1 us
    pallas_call x2, Pallas kernels, project(): pl.pallas_call(kernel, out_shape=(*results, jax.ShapeDtypeStruct((count *...  8.39 us
    pallas_call x1, Pallas kernels, per_device_paired(): pl.pallas_call(row_grad_kernel, out_shape=jax.ShapeDtypeStruct((receive,...  6.6 us
    all_to_all x1, starting transfers between devices, per_device_paired(): lax.all_to_all(by_level, 'dp', split_axis=0, concat_axis=0, axis_index_gr...  4.65 us
    all_to_all x1, starting transfers between devices, per_device_paired(): lax.all_to_all(selected, 'dp', split_axis=0, concat_axis=0, axis_index_gr...  3.5 us
    pallas_call x1, Pallas kernels, per_device_paired(): pl.pallas_call(weight_grad_kernel, out_shape=(mine_terms, *[sent_terms] *...  2.74 us
  transfers between devices with their start and end apart: 30, of which 13 were waited for; matrix products, arithmetic and copies ran while one was open for 5% of the time, Pallas kernels for 16%

profile of v17, /device:TPU:0, one launch (start us, length us, event | category | flops | bytes accessed | tf_op | source)
XLA Modules:
  0.0 121.1 jit_solution(1645611164308103748)
XLA Ops:
  1.2 1.0 fusion.11
  2.7 4.0 %collective-permute-start.4 = (bf16[256,512]{1,0:T(8,128)(2,1)S(1)}, bf16[256,512]{1,0:T(8,128)(2,1)}, u32[]{:S(2)}, u32[]{:S(2)}) collective-permute-start(bf16[256,512]{1,0:T(8,128)(2,1)S(1)} %maximum_select_fusion.refs_3_), channel_id=1, source_target_pairs={{0,16},{1,17},{2,18},{3,19},{4,20},{5,21},{6,22},{7,23},{8,24},{9,... | collective-permute-start | bytes 786440 | tf_op jit(solution)/shard_map/ppermute | solution.py:92
  6.7 1.6 %collective-permute-start.3 = (bf16[256,512]{1,0:T(8,128)(2,1)S(1)}, bf16[256,512]{1,0:T(8,128)(2,1)}, u32[]{:S(2)}, u32[]{:S(2)}) collective-permute-start(bf16[256,512]{1,0:T(8,128)(2,1)S(1)} %maximum_select_fusion.refs_3_), channel_id=1, source_target_pairs={{0,8},{1,9},{2,10},{3,11},{4,12},{5,13},{6,14},{7,15},{8,0},{9,1},... | collective-permute-start | bytes 786440 | tf_op jit(solution)/shard_map/ppermute | solution.py:92
  8.3 1.5 %collective-permute-start.2 = (bf16[256,512]{1,0:T(8,128)(2,1)S(1)}, bf16[256,512]{1,0:T(8,128)(2,1)S(1)}, u32[]{:S(2)}, u32[]{:S(2)}) collective-permute-start(bf16[256,512]{1,0:T(8,128)(2,1)S(1)} %maximum_select_fusion.refs_3_), channel_id=1, source_target_pairs={{0,2},{1,3},{2,0},{3,1},{4,6},{5,7},{6,4},{7,5},{8,10},{9,11},{10,... | collective-permute-start | bytes 786440 | tf_op jit(solution)/shard_map/ppermute | solution.py:92
  9.8 1.5 %collective-permute-start.1 = (bf16[256,512]{1,0:T(8,128)(2,1)S(1)}, bf16[256,512]{1,0:T(8,128)(2,1)S(1)}, u32[]{:S(2)}, u32[]{:S(2)}) collective-permute-start(bf16[256,512]{1,0:T(8,128)(2,1)S(1)} %maximum_select_fusion.refs_3_), channel_id=1, source_target_pairs={{0,4},{1,5},{2,6},{3,7},{4,0},{5,1},{6,2},{7,3},{8,12},{9,13},{10,... | collective-permute-start | bytes 786440 | tf_op jit(solution)/shard_map/ppermute | solution.py:92
  11.3 1.3 %slice_bitcast_fusion.3 = (bf16[1,128,1024]{2,1,0:T(8,128)(2,1)S(1)}, bf16[1,128,1024]{2,1,0:T(8,128)(2,1)S(1)}, bf16[1,128,1024]{2,1,0:T(8,128)(2,1)S(1)}, bf16[1,128,1024]{2,1,0:T(8,128)(2,1)S(1)}) fusion(bf16[128,4096]{1,0:T(8,128)(2,1)} %refs_0_), kind=kLoop, calls=%fused_computation.6 | loop fusion | bytes 2097152 | tf_op jit(solution)/shard_map/stack | solution.py:374
  12.6 1.1 pad_maximum_fusion
  13.9 5.9 %collective-permute-done.4.refs_7_ = bf16[256,512]{1,0:T(8,128)(2,1)} collective-permute-done((bf16[256,512]{1,0:T(8,128)(2,1)S(1)}, bf16[256,512]{1,0:T(8,128)(2,1)}, u32[]{:S(2)}, u32[]{:S(2)}) %collective-permute-start.4) | collective-permute-done | bytes 262176 | tf_op jit(solution)/shard_map/ppermute | solution.py:92
  19.8 2.3 %collective-permute-start.6 = (bf16[256,512]{1,0:T(8,128)(2,1)}, bf16[256,512]{1,0:T(8,128)(2,1)}, u32[]{:S(2)}, u32[]{:S(2)}) collective-permute-start(bf16[256,512]{1,0:T(8,128)(2,1)} %collective-permute-done.3.refs_6_), channel_id=1, source_target_pairs={{0,4},{1,5},{2,6},{3,7},{4,0},{5,1},{6,2},{7,3},{8,12},{9,13},{10,... | collective-permute-start | bytes 786440 | tf_op jit(solution)/shard_map/ppermute | solution.py:92
  22.1 1.5 %collective-permute-start.5 = (bf16[256,512]{1,0:T(8,128)(2,1)}, bf16[256,512]{1,0:T(8,128)(2,1)}, u32[]{:S(2)}, u32[]{:S(2)}) collective-permute-start(bf16[256,512]{1,0:T(8,128)(2,1)} %collective-permute-done.3.refs_6_), channel_id=1, source_target_pairs={{0,2},{1,3},{2,0},{3,1},{4,6},{5,7},{6,4},{7,5},{8,10},{9,11},{10,... | collective-permute-start | bytes 786440 | tf_op jit(solution)/shard_map/ppermute | solution.py:92
  24.6 4.7 %all-to-all-start = ((bf16[4,128,1024]{2,1,0:T(8,128)(2,1)}), bf16[4,128,1024]{2,1,0:T(8,128)(2,1)S(1)}, u32[]{:S(2)}, u32[]{:S(2)}) async-start(bf16[4,128,1024]{2,1,0:T(8,128)(2,1)} %pad_maximum_fusion), calls=%async_computation | async-start | bytes 2097152 | tf_op jit(solution)/shard_map/all_to_all | solution.py:379
  29.4 1.2 compare_select_fusion
  30.6 0.7 pad_maximum_fusion.1
  31.4 1.6 %collective-permute-done.8.refs_11_ = bf16[256,512]{1,0:T(8,128)(2,1)} collective-permute-done((bf16[256,512]{1,0:T(8,128)(2,1)}, bf16[256,512]{1,0:T(8,128)(2,1)}, u32[]{:S(2)}, u32[]{:S(2)}) %collective-permute-start.8) | collective-permute-done | bytes 262176 | tf_op jit(solution)/shard_map/ppermute | solution.py:92
  32.9 1.0 collective-permute-done.7.refs_10_
  33.9 1.5 %collective-permute-start.13 = (bf16[256,512]{1,0:T(8,128)(2,1)}, bf16[256,512]{1,0:T(8,128)(2,1)S(1)}, u32[]{:S(2)}, u32[]{:S(2)}) collective-permute-start(bf16[256,512]{1,0:T(8,128)(2,1)} %copy-done.17), channel_id=1, source_target_pairs={{0,2},{1,3},{2,0},{3,1},{4,6},{5,7},{6,4},{7,5},{8,10},{9,11},{10,... | collective-permute-start | bytes 786440 | tf_op jit(solution)/shard_map/ppermute | solution.py:92
  35.9 1.5 %collective-permute-start.12 = (bf16[256,512]{1,0:T(8,128)(2,1)}, bf16[256,512]{1,0:T(8,128)(2,1)S(1)}, u32[]{:S(2)}, u32[]{:S(2)}) collective-permute-start(bf16[256,512]{1,0:T(8,128)(2,1)} %collective-permute-done.9.refs_12_), channel_id=1, source_target_pairs={{0,4},{1,5},{2,6},{3,7},{4,0},{5,1},{6,2},{7,3},{8,12},{9,13},{10,... | collective-permute-start | bytes 786440 | tf_op jit(solution)/shard_map/ppermute | solution.py:92
  38.0 5.3 %collective-permute-done.13.refs_15_ = bf16[256,512]{1,0:T(8,128)(2,1)S(1)} collective-permute-done((bf16[256,512]{1,0:T(8,128)(2,1)}, bf16[256,512]{1,0:T(8,128)(2,1)S(1)}, u32[]{:S(2)}, u32[]{:S(2)}) %collective-permute-start.13) | collective-permute-done | bytes 262176 | tf_op jit(solution)/shard_map/ppermute | solution.py:92
  43.2 1.5 %collective-permute-done.14.refs_16_ = bf16[256,512]{1,0:T(8,128)(2,1)S(1)} collective-permute-done((bf16[256,512]{1,0:T(8,128)(2,1)}, bf16[256,512]{1,0:T(8,128)(2,1)S(1)}, u32[]{:S(2)}, u32[]{:S(2)}) %collective-permute-start.14) | collective-permute-done | bytes 262176 | tf_op jit(solution)/shard_map/ppermute | solution.py:92
  44.8 4.9 %collective-permute-done.12.refs_14_ = bf16[256,512]{1,0:T(8,128)(2,1)S(1)} collective-permute-done((bf16[256,512]{1,0:T(8,128)(2,1)}, bf16[256,512]{1,0:T(8,128)(2,1)S(1)}, u32[]{:S(2)}, u32[]{:S(2)}) %collective-permute-start.12) | collective-permute-done | bytes 262176 | tf_op jit(solution)/shard_map/ppermute | solution.py:92
  49.7 1.0 copy-done.2
  51.2 0.8 collective-permute-start.17
  52.0 0.6 stack.87.refs_0_.chips_ref
  52.7 6.1 %project.1 = (bf16[3584,512]{1,0:T(8,128)(2,1)}, f32[2,128,512]{2,1,0:T(8,128)}) custom-call(s32[16]{0:T(128)} %stack.87.refs_0_.chips_ref, bf16[128,4096]{1,0:T(8,128)(2,1)} %refs_0_, bf16[128,4096]{1,0:T(8,128)(2,1)} %copy-done.2, bf16[256,512]{1,0:T(8,128)(2,1)} %copy-done.15, bf16[256,512]{1,0:T(8,128)(2,1)} %copy-done.17, bf16[256,512]{1,0:T(8,128)(2,1)} %copy-done.16, ...), custom_call_target="tpu_custom_call" | custom-call | tf_op jit(solution)/shard_map/project/pallas_call | solution.py:429
  58.8 0.7 copy-done.11
  59.4 0.7 copy-done.9
  60.7 0.9 copy-done.7
  61.6 1.0 copy-done.8
  62.6 0.9 copy-done.10
  63.6 0.9 copy-done.12
  65.1 2.3 %delta.1 = (bf16[272,512]{1,0:T(8,128)(2,1)S(1)}, bf16[512,512]{1,0:T(8,128)(2,1)}) custom-call(s32[16]{0:T(128)S(1)} %copy-done.13, s32[1]{0:T(128)} %bitcast.16.me_ref, bf16[144,512]{1,0:T(8,128)(2,1)S(1)} %copy-done.7, bf16[144,512]{1,0:T(8,128)(2,1)S(1)} %copy-done.12, bf16[128,4096]{1,0:T(8,128)(2,1)S(1)} %copy-done.1, bf16[128,4096]{1,0:T(8,128)(2,1)S(1)} %copy-done.3, ...), custom_call_target="tpu_custom_call" | custom-call | tf_op jit(solution)/shard_map/delta/pallas_call | solution.py:429
  67.4 1.4 %collective-permute-start.19 = (bf16[272,512]{1,0:T(8,128)(2,1)S(1)}, bf16[272,512]{1,0:T(8,128)(2,1)S(1)}, u32[]{:S(2)}, u32[]{:S(2)}) collective-permute-start(bf16[272,512]{1,0:T(8,128)(2,1)S(1)} %get-tuple-element.126.refs_0_), channel_id=1, source_target_pairs={{0,16},{1,17},{2,18},{3,19},{4,20},{5,21},{6,22},{7,23},{8,24},{9,... | collective-permute-start | bytes 835592 | tf_op jit(solution)/shard_map/ppermute | solution.py:92
  68.8 3.8 %collective-permute-start.18 = (bf16[272,512]{1,0:T(8,128)(2,1)S(1)}, bf16[272,512]{1,0:T(8,128)(2,1)S(1)}, u32[]{:S(2)}, u32[]{:S(2)}) collective-permute-start(bf16[272,512]{1,0:T(8,128)(2,1)S(1)} %get-tuple-element.126.refs_0_), channel_id=1, source_target_pairs={{0,8},{1,9},{2,10},{3,11},{4,12},{5,13},{6,14},{7,15},{8,0},{9,1},... | collective-permute-start | bytes 835592 | tf_op jit(solution)/shard_map/ppermute | solution.py:92
  72.6 10.4 %collective-permute-done.19.refs_2_ = bf16[272,512]{1,0:T(8,128)(2,1)S(1)} collective-permute-done((bf16[272,512]{1,0:T(8,128)(2,1)S(1)}, bf16[272,512]{1,0:T(8,128)(2,1)S(1)}, u32[]{:S(2)}, u32[]{:S(2)}) %collective-permute-start.19) | collective-permute-done | bytes 278560 | tf_op jit(solution)/shard_map/ppermute | solution.py:92
  83.2 1.0 copy-done.5
  84.4 7.4 %collective-permute-done.21.refs_3_ = bf16[272,512]{1,0:T(8,128)(2,1)S(1)} collective-permute-done((bf16[272,512]{1,0:T(8,128)(2,1)S(1)}, bf16[272,512]{1,0:T(8,128)(2,1)S(1)}, u32[]{:S(2)}, u32[]{:S(2)}) %collective-permute-start.21) | collective-permute-done | bytes 278560 | tf_op jit(solution)/shard_map/ppermute | solution.py:92
  92.3 1.8 %select.28 = bf16[8,64,512]{2,1,0:T(8,128)(2,1)} custom-call(s32[1]{0:T(128)} %bitcast.16.me_ref, bf16[272,512]{1,0:T(8,128)(2,1)S(1)} %get-tuple-element.126.refs_0_, bf16[272,512]{1,0:T(8,128)(2,1)S(1)} %collective-permute-done.18.refs_1_, bf16[272,512]{1,0:T(8,128)(2,1)S(1)} %collective-permute-done.19.refs_2_, ...), custom_call_target="tpu_custom_call" | custom-call | tf_op jit(solution)/shard_map/select/pallas_call | solution.py:496
  94.1 3.5 %all-to-all-start.1 = ((bf16[8,64,512]{2,1,0:T(8,128)(2,1)}), bf16[8,64,512]{2,1,0:T(8,128)(2,1)S(1)}, u32[]{:S(2)}, u32[]{:S(2)}) async-start(bf16[8,64,512]{2,1,0:T(8,128)(2,1)} %select.28), calls=%async_computation.1 | async-start | bytes 1048576 | tf_op jit(solution)/shard_map/all_to_all | solution.py:505
  97.6 1.2 %copy-done.6 = bf16[4,128,1024]{2,1,0:T(8,128)(2,1)S(1)} copy-done((bf16[4,128,1024]{2,1,0:T(8,128)(2,1)S(1)}, bf16[4,128,1024]{2,1,0:T(8,128)(2,1)}, u32[]{:S(2)}) %copy-start.6) | copy-done | bytes 1048600
  98.8 2.7 %weight_grad.1 = (f32[256,512]{1,0:T(8,128)S(1)}, bf16[256,512]{1,0:T(8,128)(2,1)}, bf16[256,512]{1,0:T(8,128)(2,1)}, bf16[256,512]{1,0:T(8,128)(2,1)}) custom-call(s32[1]{0:T(128)} %bitcast.16.me_ref, bf16[4,128,1024]{2,1,0:T(8,128)(2,1)S(1)} %all-to-all-done.own_ref, bf16[4,128,1024]{2,1,0:T(8,128)(2,1)S(1)} %copy-done.6, ...), custom_call_target="tpu_custom_call" | custom-call | tf_op jit(solution)/shard_map/weight_grad/pallas_call | solution.py:517
  101.6 2.0 %collective-permute-start.24 = (bf16[256,512]{1,0:T(8,128)(2,1)}, bf16[256,512]{1,0:T(8,128)(2,1)S(1)}, u32[]{:S(2)}, u32[]{:S(2)}) collective-permute-start(bf16[256,512]{1,0:T(8,128)(2,1)} %get-tuple-element.129), channel_id=1, source_target_pairs={{0,2},{1,3},{2,0},{3,1},{4,6},{5,7},{6,4},{7,5},{8,10},{9,11},{10,... | collective-permute-start | bytes 786440 | tf_op jit(solution)/shard_map/ppermute | solution.py:92
  103.6 1.5 %collective-permute-start.25 = (bf16[256,512]{1,0:T(8,128)(2,1)}, bf16[256,512]{1,0:T(8,128)(2,1)S(1)}, u32[]{:S(2)}, u32[]{:S(2)}) collective-permute-start(bf16[256,512]{1,0:T(8,128)(2,1)} %get-tuple-element.130), channel_id=1, source_target_pairs={{0,4},{1,5},{2,6},{3,7},{4,0},{5,1},{6,2},{7,3},{8,12},{9,13},{10,... | collective-permute-start | bytes 786440 | tf_op jit(solution)/shard_map/ppermute | solution.py:92
  105.1 2.6 %all-to-all-done.1 = bf16[8,64,512]{2,1,0:T(8,128)(2,1)S(1)} async-done(((bf16[8,64,512]{2,1,0:T(8,128)(2,1)}), bf16[8,64,512]{2,1,0:T(8,128)(2,1)S(1)}, u32[]{:S(2)}, u32[]{:S(2)}) %all-to-all-start.1) | async-done | bytes 524320 | tf_op jit(solution)/shard_map/all_to_all | solution.py:505
  107.8 2.0 %copy-done.4 = bf16[3584,512]{1,0:T(8,128)(2,1)S(1)} copy-done((bf16[3584,512]{1,0:T(8,128)(2,1)S(1)}, bf16[3584,512]{1,0:T(8,128)(2,1)}, u32[]{:S(2)}) %copy-start.4) | copy-done | bytes 3670040
  109.8 6.6 %row_grad.1 = bf16[256,4096]{1,0:T(8,128)(2,1)} custom-call(s32[16]{0:T(128)S(1)} %copy-done.14, s32[1]{0:T(128)} %bitcast.16.me_ref, bf16[4,2,64,512]{3,2,1,0:T(8,128)(2,1)S(1)} %bitcast.34, bf16[3584,512]{1,0:T(8,128)(2,1)S(1)} %copy-done.4, bf16[3584,512]{1,0:T(8,128)(2,1)} %collective-permute-done.22.refs_1_, ...), custom_call_target="tpu_custom_call" | custom-call | tf_op jit(solution)/shard_map/row_grad/pallas_call | solution.py:533
  116.4 2.1 %collective-permute-done.26.refs_2_ = bf16[256,512]{1,0:T(8,128)(2,1)S(1)} collective-permute-done((bf16[256,512]{1,0:T(8,128)(2,1)}, bf16[256,512]{1,0:T(8,128)(2,1)S(1)}, u32[]{:S(2)}, u32[]{:S(2)}) %collective-permute-start.26) | collective-permute-done | bytes 262176 | tf_op jit(solution)/shard_map/ppermute | solution.py:92
  118.7 1.5 %collective-permute-done.27.mate_ref = f32[128,512]{1,0:T(8,128)S(1)} collective-permute-done((f32[128,512]{1,0:T(8,128)S(1)}, f32[128,512]{1,0:T(8,128)S(1)}, u32[]{:S(2)}, u32[]{:S(2)}) %collective-permute-start.27) | collective-permute-done | bytes 262176 | tf_op jit(solution)/shard_map/ppermute | solution.py:92
  120.2 0.8 join.1
  (85 shorter events, 6.2 us)
Async XLA Ops:
  0.6 23.6 %copy-start.21 = (s32[1,4]{1,0:T(1,128)S(1)}, s32[1,4]{1,0:T(1,128)}, u32[]{:S(2)}) copy-start(s32[1,4]{1,0:T(1,128)} %param.9) | copy-start | bytes 52
  0.6 23.9 %copy-start.22 = (s32[128,1]{0,1:T(1,128)S(1)}, s32[128,1]{0,1:T(1,128)}, u32[]{:S(2)}) copy-start(s32[128,1]{0,1:T(1,128)} %param.8) | copy-start | bytes 1540
  0.7 1.9 %collective-permute-start = (bf16[128,1024]{1,0:T(8,128)(2,1)}, bf16[128,1024]{1,0:T(8,128)(2,1)S(1)}, u32[]{:S(2)}, u32[]{:S(2)}) collective-permute-start(bf16[128,1024]{1,0:T(8,128)(2,1)} %param.11), channel_id=1, source_target_pairs={{0,1},{1,0},{2,3},{3,2},{4,5},{5,4},{6,7},{7,6},{8,9},{9,8},{10,11... | collective-permute-start | bytes 786440 | tf_op jit(solution)/shard_map/ppermute | solution.py:92
  2.6 26.7 %copy-start.23 = (s32[4]{0:T(128)S(1)}, s32[4]{0:T(128)}, u32[]{:S(2)}) copy-start(s32[4]{0:T(128)} %param.10) | copy-start | bytes 52
  2.6 28.0 %copy-start.15 = (bf16[256,512]{1,0:T(8,128)(2,1)}, bf16[256,512]{1,0:T(8,128)(2,1)S(1)}, u32[]{:S(2)}) copy-start(bf16[256,512]{1,0:T(8,128)(2,1)S(1)} %maximum_select_fusion.refs_3_) | copy-start | bytes 786436
  2.7 31.3 %copy-start = (bf16[128,4096]{1,0:T(8,128)(2,1)S(1)}, bf16[128,4096]{1,0:T(8,128)(2,1)}, u32[]{:S(2)}) copy-start(bf16[128,4096]{1,0:T(8,128)(2,1)} %refs_0_) | copy-start | bytes 3145732
  2.7 17.1 %collective-permute-start.4 = (bf16[256,512]{1,0:T(8,128)(2,1)S(1)}, bf16[256,512]{1,0:T(8,128)(2,1)}, u32[]{:S(2)}, u32[]{:S(2)}) collective-permute-start(bf16[256,512]{1,0:T(8,128)(2,1)S(1)} %maximum_select_fusion.refs_3_), channel_id=1, source_target_pairs={{0,16},{1,17},{2,18},{3,19},{4,20},{5,21},{6,22},{7,23},{8,24},{9,... | collective-permute-start | bytes 786440 | tf_op jit(solution)/shard_map/ppermute | solution.py:92
  6.7 13.1 %collective-permute-start.3 = (bf16[256,512]{1,0:T(8,128)(2,1)S(1)}, bf16[256,512]{1,0:T(8,128)(2,1)}, u32[]{:S(2)}, u32[]{:S(2)}) collective-permute-start(bf16[256,512]{1,0:T(8,128)(2,1)S(1)} %maximum_select_fusion.refs_3_), channel_id=1, source_target_pairs={{0,8},{1,9},{2,10},{3,11},{4,12},{5,13},{6,14},{7,15},{8,0},{9,1},... | collective-permute-start | bytes 786440 | tf_op jit(solution)/shard_map/ppermute | solution.py:92
  8.3 11.5 %collective-permute-start.2 = (bf16[256,512]{1,0:T(8,128)(2,1)S(1)}, bf16[256,512]{1,0:T(8,128)(2,1)S(1)}, u32[]{:S(2)}, u32[]{:S(2)}) collective-permute-start(bf16[256,512]{1,0:T(8,128)(2,1)S(1)} %maximum_select_fusion.refs_3_), channel_id=1, source_target_pairs={{0,2},{1,3},{2,0},{3,1},{4,6},{5,7},{6,4},{7,5},{8,10},{9,11},{10,... | collective-permute-start | bytes 786440 | tf_op jit(solution)/shard_map/ppermute | solution.py:92
  9.8 10.0 %collective-permute-start.1 = (bf16[256,512]{1,0:T(8,128)(2,1)S(1)}, bf16[256,512]{1,0:T(8,128)(2,1)S(1)}, u32[]{:S(2)}, u32[]{:S(2)}) collective-permute-start(bf16[256,512]{1,0:T(8,128)(2,1)S(1)} %maximum_select_fusion.refs_3_), channel_id=1, source_target_pairs={{0,4},{1,5},{2,6},{3,7},{4,0},{5,1},{6,2},{7,3},{8,12},{9,13},{10,... | collective-permute-start | bytes 786440 | tf_op jit(solution)/shard_map/ppermute | solution.py:92
  13.7 17.7 %collective-permute-start.9 = (bf16[256,512]{1,0:T(8,128)(2,1)S(1)}, bf16[256,512]{1,0:T(8,128)(2,1)}, u32[]{:S(2)}, u32[]{:S(2)}) collective-permute-start(bf16[256,512]{1,0:T(8,128)(2,1)S(1)} %maximum_select_fusion.refs_3_), channel_id=1, source_target_pairs={{0,24},{1,25},{2,26},{3,27},{4,28},{5,29},{6,30},{7,31},{8,16},{9,... | collective-permute-start | bytes 786440 | tf_op jit(solution)/shard_map/ppermute | solution.py:92
  19.8 9.6 %copy-start.16 = (bf16[256,512]{1,0:T(8,128)(2,1)}, bf16[256,512]{1,0:T(8,128)(2,1)S(1)}, u32[]{:S(2)}) copy-start(bf16[256,512]{1,0:T(8,128)(2,1)S(1)} %collective-permute-done.2.refs_5_) | copy-start | bytes 786436
  19.8 4.8 %copy-start.17 = (bf16[256,512]{1,0:T(8,128)(2,1)}, bf16[256,512]{1,0:T(8,128)(2,1)S(1)}, u32[]{:S(2)}) copy-start(bf16[256,512]{1,0:T(8,128)(2,1)S(1)} %collective-permute-done.1.refs_4_) | copy-start | bytes 786436
  19.8 11.6 %collective-permute-start.6 = (bf16[256,512]{1,0:T(8,128)(2,1)}, bf16[256,512]{1,0:T(8,128)(2,1)}, u32[]{:S(2)}, u32[]{:S(2)}) collective-permute-start(bf16[256,512]{1,0:T(8,128)(2,1)} %collective-permute-done.3.refs_6_), channel_id=1, source_target_pairs={{0,4},{1,5},{2,6},{3,7},{4,0},{5,1},{6,2},{7,3},{8,12},{9,13},{10,... | collective-permute-start | bytes 786440 | tf_op jit(solution)/shard_map/ppermute | solution.py:92
  22.1 9.2 %collective-permute-start.5 = (bf16[256,512]{1,0:T(8,128)(2,1)}, bf16[256,512]{1,0:T(8,128)(2,1)}, u32[]{:S(2)}, u32[]{:S(2)}) collective-permute-start(bf16[256,512]{1,0:T(8,128)(2,1)} %collective-permute-done.3.refs_6_), channel_id=1, source_target_pairs={{0,2},{1,3},{2,0},{3,1},{4,6},{5,7},{6,4},{7,5},{8,10},{9,11},{10,... | collective-permute-start | bytes 786440 | tf_op jit(solution)/shard_map/ppermute | solution.py:92
  23.6 9.3 %collective-permute-start.8 = (bf16[256,512]{1,0:T(8,128)(2,1)}, bf16[256,512]{1,0:T(8,128)(2,1)}, u32[]{:S(2)}, u32[]{:S(2)}) collective-permute-start(bf16[256,512]{1,0:T(8,128)(2,1)} %collective-permute-done.4.refs_7_), channel_id=1, source_target_pairs={{0,4},{1,5},{2,6},{3,7},{4,0},{5,1},{6,2},{7,3},{8,12},{9,13},{10,... | collective-permute-start | bytes 786440 | tf_op jit(solution)/shard_map/ppermute | solution.py:92
  24.1 9.8 %collective-permute-start.7 = (bf16[256,512]{1,0:T(8,128)(2,1)}, bf16[256,512]{1,0:T(8,128)(2,1)}, u32[]{:S(2)}, u32[]{:S(2)}) collective-permute-start(bf16[256,512]{1,0:T(8,128)(2,1)} %collective-permute-done.4.refs_7_), channel_id=1, source_target_pairs={{0,2},{1,3},{2,0},{3,1},{4,6},{5,7},{6,4},{7,5},{8,10},{9,11},{10,... | collective-permute-start | bytes 786440 | tf_op jit(solution)/shard_map/ppermute | solution.py:92
  24.6 34.8 %all-to-all-start = ((bf16[4,128,1024]{2,1,0:T(8,128)(2,1)}), bf16[4,128,1024]{2,1,0:T(8,128)(2,1)S(1)}, u32[]{:S(2)}, u32[]{:S(2)}) async-start(bf16[4,128,1024]{2,1,0:T(8,128)(2,1)} %pad_maximum_fusion), calls=%async_computation | async-start | bytes 2097152 | tf_op jit(solution)/shard_map/all_to_all | solution.py:379
  29.4 31.3 %copy-start.1 = (bf16[128,4096]{1,0:T(8,128)(2,1)S(1)}, bf16[128,4096]{1,0:T(8,128)(2,1)}, u32[]{:S(2)}) copy-start(bf16[128,4096]{1,0:T(8,128)(2,1)} %refs_0_) | copy-start | bytes 3145732
  33.9 15.8 %collective-permute-start.10 = (bf16[128,4096]{1,0:T(8,128)(2,1)S(1)}, bf16[128,4096]{1,0:T(8,128)(2,1)S(1)}, u32[]{:S(2)}, u32[]{:S(2)}) collective-permute-start(bf16[128,4096]{1,0:T(8,128)(2,1)S(1)} %copy-done), channel_id=1, source_target_pairs={{0,1},{1,0},{2,3},{3,2},{4,5},{5,4},{6,7},{7,6},{8,9},{9,8},{10,11... | collective-permute-start | bytes 3145736 | tf_op jit(solution)/shard_map/ppermute | solution.py:92
  33.9 9.3 %collective-permute-start.13 = (bf16[256,512]{1,0:T(8,128)(2,1)}, bf16[256,512]{1,0:T(8,128)(2,1)S(1)}, u32[]{:S(2)}, u32[]{:S(2)}) collective-permute-start(bf16[256,512]{1,0:T(8,128)(2,1)} %copy-done.17), channel_id=1, source_target_pairs={{0,2},{1,3},{2,0},{3,1},{4,6},{5,7},{6,4},{7,5},{8,10},{9,11},{10,... | collective-permute-start | bytes 786440 | tf_op jit(solution)/shard_map/ppermute | solution.py:92
  35.4 9.4 %collective-permute-start.14 = (bf16[256,512]{1,0:T(8,128)(2,1)}, bf16[256,512]{1,0:T(8,128)(2,1)S(1)}, u32[]{:S(2)}, u32[]{:S(2)}) collective-permute-start(bf16[256,512]{1,0:T(8,128)(2,1)} %collective-permute-done.7.refs_10_), channel_id=1, source_target_pairs={{0,4},{1,5},{2,6},{3,7},{4,0},{5,1},{6,2},{7,3},{8,12},{9,13},{10,... | collective-permute-start | bytes 786440 | tf_op jit(solution)/shard_map/ppermute | solution.py:92
  35.9 13.8 %collective-permute-start.12 = (bf16[256,512]{1,0:T(8,128)(2,1)}, bf16[256,512]{1,0:T(8,128)(2,1)S(1)}, u32[]{:S(2)}, u32[]{:S(2)}) collective-permute-start(bf16[256,512]{1,0:T(8,128)(2,1)} %collective-permute-done.9.refs_12_), channel_id=1, source_target_pairs={{0,4},{1,5},{2,6},{3,7},{4,0},{5,1},{6,2},{7,3},{8,12},{9,13},{10,... | collective-permute-start | bytes 786440 | tf_op jit(solution)/shard_map/ppermute | solution.py:92
  37.4 12.2 %collective-permute-start.11 = (bf16[256,512]{1,0:T(8,128)(2,1)}, bf16[256,512]{1,0:T(8,128)(2,1)}, u32[]{:S(2)}, u32[]{:S(2)}) collective-permute-start(bf16[256,512]{1,0:T(8,128)(2,1)} %collective-permute-done.9.refs_12_), channel_id=1, source_target_pairs={{0,2},{1,3},{2,0},{3,1},{4,6},{5,7},{6,4},{7,5},{8,10},{9,11},{10,... | collective-permute-start | bytes 786440 | tf_op jit(solution)/shard_map/ppermute | solution.py:92
  43.2 8.0 %copy-start.18 = (bf16[256,512]{1,0:T(8,128)(2,1)}, bf16[256,512]{1,0:T(8,128)(2,1)S(1)}, u32[]{:S(2)}) copy-start(bf16[256,512]{1,0:T(8,128)(2,1)S(1)} %collective-permute-done.13.refs_15_) | copy-start | bytes 786436
  44.8 7.2 %copy-start.19 = (bf16[256,512]{1,0:T(8,128)(2,1)}, bf16[256,512]{1,0:T(8,128)(2,1)S(1)}, u32[]{:S(2)}) copy-start(bf16[256,512]{1,0:T(8,128)(2,1)S(1)} %collective-permute-done.14.refs_16_) | copy-start | bytes 786436
  49.7 2.3 %copy-start.20 = (bf16[256,512]{1,0:T(8,128)(2,1)}, bf16[256,512]{1,0:T(8,128)(2,1)S(1)}, u32[]{:S(2)}) copy-start(bf16[256,512]{1,0:T(8,128)(2,1)S(1)} %collective-permute-done.12.refs_14_) | copy-start | bytes 786436
  49.7 1.0 copy-start.2
  50.7 8.8 %collective-permute-start.16 = (bf16[256,512]{1,0:T(8,128)(2,1)}, bf16[256,512]{1,0:T(8,128)(2,1)S(1)}, u32[]{:S(2)}, u32[]{:S(2)}) collective-permute-start(bf16[256,512]{1,0:T(8,128)(2,1)} %collective-permute-done.6.refs_9_), channel_id=1, source_target_pairs={{0,2},{1,3},{2,0},{3,1},{4,6},{5,7},{6,4},{7,5},{8,10},{9,11},{10,... | collective-permute-start | bytes 786440 | tf_op jit(solution)/shard_map/ppermute | solution.py:92
  51.2 9.4 %copy-start.3 = (bf16[128,4096]{1,0:T(8,128)(2,1)S(1)}, bf16[128,4096]{1,0:T(8,128)(2,1)}, u32[]{:S(2)}) copy-start(bf16[128,4096]{1,0:T(8,128)(2,1)} %copy-done.2) | copy-start | bytes 3145732
  51.2 8.9 %collective-permute-start.17 = (bf16[256,512]{1,0:T(8,128)(2,1)}, bf16[256,512]{1,0:T(8,128)(2,1)}, u32[]{:S(2)}, u32[]{:S(2)}) collective-permute-start(bf16[256,512]{1,0:T(8,128)(2,1)} %collective-permute-done.11.refs_13_), channel_id=1, source_target_pairs={{0,4},{1,5},{2,6},{3,7},{4,0},{5,1},{6,2},{7,3},{8,12},{9,13},{10,... | collective-permute-start | bytes 786440 | tf_op jit(solution)/shard_map/ppermute | solution.py:92
  52.0 6.8 %collective-permute-start.15 = (bf16[144,512]{1,0:T(8,128)(2,1)}, bf16[144,512]{1,0:T(8,128)(2,1)S(1)}, u32[]{:S(2)}, u32[]{:S(2)}) collective-permute-start(bf16[144,512]{1,0:T(8,128)(2,1)} %get-tuple-element.89), channel_id=1, source_target_pairs={{0,1},{1,0},{2,3},{3,2},{4,5},{5,4},{6,7},{7,6},{8,9},{9,8},{10,11... | collective-permute-start | bytes 442376 | tf_op jit(solution)/shard_map/ppermute | solution.py:92
  60.2 23.0 %collective-permute-start.20 = (bf16[4,128,1024]{2,1,0:T(8,128)(2,1)S(1)}, bf16[4,128,1024]{2,1,0:T(8,128)(2,1)S(1)}, u32[]{:S(2)}, u32[]{:S(2)}) collective-permute-start(bf16[4,128,1024]{2,1,0:T(8,128)(2,1)S(1)} %all-to-all-done.own_ref), channel_id=1, source_target_pairs={{0,1},{1,0},{2,3},{3,2},{4,5},{5,4},{6,7},{7,6},{8,9},{9,8},{10,11... | collective-permute-start | bytes 3145736 | tf_op jit(solution)/shard_map/ppermute | solution.py:92
  61.6 1.0 copy-start.8
  67.4 40.3 %copy-start.14 = (s32[16]{0:T(128)S(1)}, s32[16]{0:T(128)}, u32[]{:S(2)}) copy-start(s32[16]{0:T(128)} %stack.87.refs_0_.chips_ref) | copy-start | bytes 196
  67.4 15.6 %collective-permute-start.19 = (bf16[272,512]{1,0:T(8,128)(2,1)S(1)}, bf16[272,512]{1,0:T(8,128)(2,1)S(1)}, u32[]{:S(2)}, u32[]{:S(2)}) collective-permute-start(bf16[272,512]{1,0:T(8,128)(2,1)S(1)} %get-tuple-element.126.refs_0_), channel_id=1, source_target_pairs={{0,16},{1,17},{2,18},{3,19},{4,20},{5,21},{6,22},{7,23},{8,24},{9,... | collective-permute-start | bytes 835592 | tf_op jit(solution)/shard_map/ppermute | solution.py:92
  68.8 14.3 %collective-permute-start.18 = (bf16[272,512]{1,0:T(8,128)(2,1)S(1)}, bf16[272,512]{1,0:T(8,128)(2,1)S(1)}, u32[]{:S(2)}, u32[]{:S(2)}) collective-permute-start(bf16[272,512]{1,0:T(8,128)(2,1)S(1)} %get-tuple-element.126.refs_0_), channel_id=1, source_target_pairs={{0,8},{1,9},{2,10},{3,11},{4,12},{5,13},{6,14},{7,15},{8,0},{9,1},... | collective-permute-start | bytes 835592 | tf_op jit(solution)/shard_map/ppermute | solution.py:92
  83.1 1.0 copy-start.5
  84.1 7.6 %collective-permute-start.21 = (bf16[272,512]{1,0:T(8,128)(2,1)S(1)}, bf16[272,512]{1,0:T(8,128)(2,1)S(1)}, u32[]{:S(2)}, u32[]{:S(2)}) collective-permute-start(bf16[272,512]{1,0:T(8,128)(2,1)S(1)} %collective-permute-done.19.refs_2_), channel_id=1, source_target_pairs={{0,8},{1,9},{2,10},{3,11},{4,12},{5,13},{6,14},{7,15},{8,0},{9,1},... | collective-permute-start | bytes 835592 | tf_op jit(solution)/shard_map/ppermute | solution.py:92
  91.7 16.0 %collective-permute-start.22 = (bf16[3584,512]{1,0:T(8,128)(2,1)}, bf16[3584,512]{1,0:T(8,128)(2,1)}, u32[]{:S(2)}, u32[]{:S(2)}) collective-permute-start(bf16[3584,512]{1,0:T(8,128)(2,1)} %get-tuple-element.123.refs_0_), channel_id=1, source_target_pairs={{0,1},{1,0},{2,3},{3,2},{4,5},{5,4},{6,7},{7,6},{8,9},{9,8},{10,11... | collective-permute-start | bytes 11010056 | tf_op jit(solution)/shard_map/ppermute | solution.py:92
  91.7 16.0 %collective-permute-start.23 = (bf16[512,512]{1,0:T(8,128)(2,1)}, bf16[512,512]{1,0:T(8,128)(2,1)}, u32[]{:S(2)}, u32[]{:S(2)}) collective-permute-start(bf16[512,512]{1,0:T(8,128)(2,1)} %get-tuple-element.124.refs_2_), channel_id=1, source_target_pairs={{0,1},{1,0},{2,3},{3,2},{4,5},{5,4},{6,7},{7,6},{8,9},{9,8},{10,11... | collective-permute-start | bytes 1572872 | tf_op jit(solution)/shard_map/ppermute | solution.py:92
  94.1 13.7 %all-to-all-start.1 = ((bf16[8,64,512]{2,1,0:T(8,128)(2,1)}), bf16[8,64,512]{2,1,0:T(8,128)(2,1)S(1)}, u32[]{:S(2)}, u32[]{:S(2)}) async-start(bf16[8,64,512]{2,1,0:T(8,128)(2,1)} %select.28), calls=%async_computation.1 | async-start | bytes 1048576 | tf_op jit(solution)/shard_map/all_to_all | solution.py:505
  97.6 1.2 %copy-start.6 = (bf16[4,128,1024]{2,1,0:T(8,128)(2,1)S(1)}, bf16[4,128,1024]{2,1,0:T(8,128)(2,1)}, u32[]{:S(2)}) copy-start(bf16[4,128,1024]{2,1,0:T(8,128)(2,1)} %copy-done.5) | copy-start | bytes 3145732
  101.6 14.9 %collective-permute-start.24 = (bf16[256,512]{1,0:T(8,128)(2,1)}, bf16[256,512]{1,0:T(8,128)(2,1)S(1)}, u32[]{:S(2)}, u32[]{:S(2)}) collective-permute-start(bf16[256,512]{1,0:T(8,128)(2,1)} %get-tuple-element.129), channel_id=1, source_target_pairs={{0,2},{1,3},{2,0},{3,1},{4,6},{5,7},{6,4},{7,5},{8,10},{9,11},{10,... | collective-permute-start | bytes 786440 | tf_op jit(solution)/shard_map/ppermute | solution.py:92
  103.6 12.8 %collective-permute-start.25 = (bf16[256,512]{1,0:T(8,128)(2,1)}, bf16[256,512]{1,0:T(8,128)(2,1)S(1)}, u32[]{:S(2)}, u32[]{:S(2)}) collective-permute-start(bf16[256,512]{1,0:T(8,128)(2,1)} %get-tuple-element.130), channel_id=1, source_target_pairs={{0,4},{1,5},{2,6},{3,7},{4,0},{5,1},{6,2},{7,3},{8,12},{9,13},{10,... | collective-permute-start | bytes 786440 | tf_op jit(solution)/shard_map/ppermute | solution.py:92
  105.1 13.5 %collective-permute-start.26 = (bf16[256,512]{1,0:T(8,128)(2,1)}, bf16[256,512]{1,0:T(8,128)(2,1)S(1)}, u32[]{:S(2)}, u32[]{:S(2)}) collective-permute-start(bf16[256,512]{1,0:T(8,128)(2,1)} %get-tuple-element.131), channel_id=1, source_target_pairs={{0,6},{1,7},{2,4},{3,5},{4,2},{5,3},{6,0},{7,1},{8,14},{9,15},{10,... | collective-permute-start | bytes 786440 | tf_op jit(solution)/shard_map/ppermute | solution.py:92
  107.8 2.0 %copy-start.4 = (bf16[3584,512]{1,0:T(8,128)(2,1)S(1)}, bf16[3584,512]{1,0:T(8,128)(2,1)}, u32[]{:S(2)}) copy-start(bf16[3584,512]{1,0:T(8,128)(2,1)} %get-tuple-element.123.refs_0_) | copy-start | bytes 11010052
  118.6 1.6 %collective-permute-start.27 = (f32[128,512]{1,0:T(8,128)S(1)}, f32[128,512]{1,0:T(8,128)S(1)}, u32[]{:S(2)}, u32[]{:S(2)}) collective-permute-start(f32[128,512]{1,0:T(8,128)S(1)} %get-tuple-element.133), channel_id=1, source_target_pairs={{0,1},{1,0},{2,3},{3,2},{4,5},{5,4},{6,7},{7,6},{8,9},{9,8},{10,11... | collective-permute-start | bytes 786440 | tf_op jit(solution)/shard_map/ppermute | solution.py:92
  (6 other events, 4.8 us)

commit v18 on v17

--- a/solution.py
+++ b/solution.py
@@ -439,7 +439,7 @@
                 pltpu.VMEM((count * depth, half_cols), jnp.bfloat16),
                 pltpu.SemaphoreType.DMA((4 * count,)),
             ],
-            compiler_params=PARAMS if name == "project" else grant(24),
+            compiler_params=PARAMS,
             name=name,
         )(*inputs)
 
@@ -479,7 +479,7 @@
             begun,
             *[have[mask] for mask in last_masks],
         ),
-        [SCALAR] * 2 + vmem(2) + hbm(2) + vmem(1),
+        [SCALAR] * 2 + vmem(2) + anywhere(2) + vmem(1),
         "delta",
     )
 
@@ -496,7 +496,7 @@
     selected = pl.pallas_call(
         select_kernel,
         out_shape=jax.ShapeDtypeStruct((PLANE, count, half_cols), jnp.bfloat16),
-        in_specs=[SCALAR] + hbm(1) + anywhere(levels - 1),
+        in_specs=[SCALAR] + anywhere(levels),
         out_specs=vmem(1)[0],
         scratch_shapes=[delta_room, pltpu.SemaphoreType.DMA((levels,))],
         compiler_params=grant(16),
@@ -517,7 +517,7 @@
     own_part, *parts = pl.pallas_call(
         weight_grad_kernel,
         out_shape=(mine_terms, *[sent_terms] * 3),
-        in_specs=[SCALAR] + anywhere(2) + hbm(1) + anywhere(levels - 1),
+        in_specs=[SCALAR] + anywhere(2 + levels),
         out_specs=tuple(hbm(1) + vmem(3)),
         scratch_shapes=[
             pltpu.VMEM((levels * 2 * rows, wide), jnp.bfloat16),
@@ -533,7 +533,7 @@
     row_grads = pl.pallas_call(
         row_grad_kernel,
         out_shape=jax.ShapeDtypeStruct((receive, width_model), jnp.bfloat16),
-        in_specs=[SCALAR] * 2 + vmem(1) + hbm(4),
+        in_specs=[SCALAR] * 2 + vmem(1) + anywhere(4),
         out_specs=anywhere(1)[0],
         scratch_shapes=[
             pltpu.VMEM((width_model, cols), jnp.bfloat16),
@@ -541,7 +541,7 @@
             pltpu.VMEM((receive, cols), jnp.bfloat16),
             pltpu.SemaphoreType.DMA((3 * chips,)),
         ],
-        compiler_params=grant(32),
+        compiler_params=grant(62),
         name="row_grad",
     )(order, me_scalar, got, first_weight, mate_first, last_weight, mate_last)
 

time: 122 us -> 118 us (0.967)
  local copies, waits for them, and re-layouts: 14 us -> 5.59 us
  Pallas kernels: 20.5 us -> 22.6 us
  waiting for transfers between devices: 44.6 us -> 46 us
    unnamed x48 -> x36, local copies, waits for them, and re-layouts: 11.1 us -> 2.72 us
    pallas_call x2, Pallas kernels: 8.39 us -> 9.86 us  [project(): pl.pallas_call(kernel, out_shape=(*results, jax.ShapeDtypeStruct((count *...]
  transfers between devices with their start and end apart: 30 -> 30, of which waited for: 13 -> 14; matrix products, arithmetic and copies ran while one was open for 5% -> 5% of each run, Pallas kernels for 16% -> 18%
where the time goes in v18:
time: 118 us; the launch traced here: 117 us
  waiting for transfers between devices  46 us (39%)
  starting transfers between devices  38.4 us (33%)
  Pallas kernels  22.6 us (19%)
  local copies, waits for them, and re-layouts  5.59 us (5%)
  other arithmetic  3.47 us (3%)
    ppermute x28, waiting for transfers between devices, swap(): return lax.ppermute(value, 'dp', [(i, i ^ mask) for i in range(size)])  43.1 us
    ppermute x28, starting transfers between devices, swap(): return lax.ppermute(value, 'dp', [(i, i ^ mask) for i in range(size)])  29.6 us
    pallas_call x2, Pallas kernels, project(): pl.pallas_call(kernel, out_shape=(*results, jax.ShapeDtypeStruct((count *...  9.86 us
    pallas_call x1, Pallas kernels, per_device_paired(): pl.pallas_call(row_grad_kernel, out_shape=jax.ShapeDtypeStruct((receive,...  7.25 us
    all_to_all x1, starting transfers between devices, per_device_paired(): lax.all_to_all(by_level, 'dp', split_axis=0, concat_axis=0, axis_index_gr...  4.65 us
    all_to_all x1, starting transfers between devices, per_device_paired(): lax.all_to_all(selected, 'dp', split_axis=0, concat_axis=0, axis_index_gr...  4.15 us
    all_to_all x1, waiting for transfers between devices, per_device_paired(): lax.all_to_all(selected, 'dp', split_axis=0, concat_axis=0, axis_index_gr...  2.93 us
    pallas_call x1, Pallas kernels, per_device_paired(): pl.pallas_call(weight_grad_kernel, out_shape=(mine_terms, *[sent_terms] *...  2.76 us
  transfers between devices with their start and end apart: 30, of which 14 were waited for; matrix products, arithmetic and copies ran while one was open for 5% of the time, Pallas kernels for 18%

profile of v18, /device:TPU:0, one launch (start us, length us, event | category | flops | bytes accessed | tf_op | source)
XLA Modules:
  0.0 117.0 jit_solution(14776930775051893270)
XLA Ops:
  0.7 0.5 collective-permute-start
  1.2 1.0 fusion.11
  2.7 4.0 %collective-permute-start.4 = (bf16[256,512]{1,0:T(8,128)(2,1)S(1)}, bf16[256,512]{1,0:T(8,128)(2,1)S(1)}, u32[]{:S(2)}, u32[]{:S(2)}) collective-permute-start(bf16[256,512]{1,0:T(8,128)(2,1)S(1)} %maximum_select_fusion.refs_3_), channel_id=1, source_target_pairs={{0,16},{1,17},{2,18},{3,19},{4,20},{5,21},{6,22},{7,23},{8,24},{9,... | collective-permute-start | bytes 786440 | tf_op jit(solution)/shard_map/ppermute | solution.py:92
  6.7 1.6 %collective-permute-start.3 = (bf16[256,512]{1,0:T(8,128)(2,1)S(1)}, bf16[256,512]{1,0:T(8,128)(2,1)S(1)}, u32[]{:S(2)}, u32[]{:S(2)}) collective-permute-start(bf16[256,512]{1,0:T(8,128)(2,1)S(1)} %maximum_select_fusion.refs_3_), channel_id=1, source_target_pairs={{0,8},{1,9},{2,10},{3,11},{4,12},{5,13},{6,14},{7,15},{8,0},{9,1},... | collective-permute-start | bytes 786440 | tf_op jit(solution)/shard_map/ppermute | solution.py:92
  8.3 1.5 %collective-permute-start.2 = (bf16[256,512]{1,0:T(8,128)(2,1)S(1)}, bf16[256,512]{1,0:T(8,128)(2,1)S(1)}, u32[]{:S(2)}, u32[]{:S(2)}) collective-permute-start(bf16[256,512]{1,0:T(8,128)(2,1)S(1)} %maximum_select_fusion.refs_3_), channel_id=1, source_target_pairs={{0,2},{1,3},{2,0},{3,1},{4,6},{5,7},{6,4},{7,5},{8,10},{9,11},{10,... | collective-permute-start | bytes 786440 | tf_op jit(solution)/shard_map/ppermute | solution.py:92
  9.8 1.5 %collective-permute-start.1 = (bf16[256,512]{1,0:T(8,128)(2,1)S(1)}, bf16[256,512]{1,0:T(8,128)(2,1)S(1)}, u32[]{:S(2)}, u32[]{:S(2)}) collective-permute-start(bf16[256,512]{1,0:T(8,128)(2,1)S(1)} %maximum_select_fusion.refs_3_), channel_id=1, source_target_pairs={{0,4},{1,5},{2,6},{3,7},{4,0},{5,1},{6,2},{7,3},{8,12},{9,13},{10,... | collective-permute-start | bytes 786440 | tf_op jit(solution)/shard_map/ppermute | solution.py:92
  11.3 1.3 %slice_bitcast_fusion.3 = (bf16[1,128,1024]{2,1,0:T(8,128)(2,1)S(1)}, bf16[1,128,1024]{2,1,0:T(8,128)(2,1)S(1)}, bf16[1,128,1024]{2,1,0:T(8,128)(2,1)S(1)}, bf16[1,128,1024]{2,1,0:T(8,128)(2,1)S(1)}) fusion(bf16[128,4096]{1,0:T(8,128)(2,1)} %refs_0_), kind=kLoop, calls=%fused_computation.6 | loop fusion | bytes 2097152 | tf_op jit(solution)/shard_map/stack | solution.py:374
  12.6 1.1 pad_maximum_fusion
  13.9 5.8 %collective-permute-done.4.refs_7_ = bf16[256,512]{1,0:T(8,128)(2,1)S(1)} collective-permute-done((bf16[256,512]{1,0:T(8,128)(2,1)S(1)}, bf16[256,512]{1,0:T(8,128)(2,1)S(1)}, u32[]{:S(2)}, u32[]{:S(2)}) %collective-permute-start.4) | collective-permute-done | bytes 262176 | tf_op jit(solution)/shard_map/ppermute | solution.py:92
  19.7 2.3 %collective-permute-start.6 = (bf16[256,512]{1,0:T(8,128)(2,1)S(1)}, bf16[256,512]{1,0:T(8,128)(2,1)}, u32[]{:S(2)}, u32[]{:S(2)}) collective-permute-start(bf16[256,512]{1,0:T(8,128)(2,1)S(1)} %collective-permute-done.3.refs_6_), channel_id=1, source_target_pairs={{0,4},{1,5},{2,6},{3,7},{4,0},{5,1},{6,2},{7,3},{8,12},{9,13},{10,... | collective-permute-start | bytes 786440 | tf_op jit(solution)/shard_map/ppermute | solution.py:92
  22.0 1.5 %collective-permute-start.5 = (bf16[256,512]{1,0:T(8,128)(2,1)S(1)}, bf16[256,512]{1,0:T(8,128)(2,1)}, u32[]{:S(2)}, u32[]{:S(2)}) collective-permute-start(bf16[256,512]{1,0:T(8,128)(2,1)S(1)} %collective-permute-done.3.refs_6_), channel_id=1, source_target_pairs={{0,2},{1,3},{2,0},{3,1},{4,6},{5,7},{6,4},{7,5},{8,10},{9,11},{10,... | collective-permute-start | bytes 786440 | tf_op jit(solution)/shard_map/ppermute | solution.py:92
  23.5 0.5 collective-permute-start.8
  24.5 4.7 %all-to-all-start = ((bf16[4,128,1024]{2,1,0:T(8,128)(2,1)}), bf16[4,128,1024]{2,1,0:T(8,128)(2,1)S(1)}, u32[]{:S(2)}, u32[]{:S(2)}) async-start(bf16[4,128,1024]{2,1,0:T(8,128)(2,1)} %pad_maximum_fusion), calls=%async_computation | async-start | bytes 2097152 | tf_op jit(solution)/shard_map/all_to_all | solution.py:379
  29.3 1.1 compare_select_fusion
  30.4 0.8 pad_maximum_fusion.1
  31.2 1.4 %collective-permute-done.8.refs_11_ = bf16[256,512]{1,0:T(8,128)(2,1)} collective-permute-done((bf16[256,512]{1,0:T(8,128)(2,1)S(1)}, bf16[256,512]{1,0:T(8,128)(2,1)}, u32[]{:S(2)}, u32[]{:S(2)}) %collective-permute-start.8) | collective-permute-done | bytes 262176 | tf_op jit(solution)/shard_map/ppermute | solution.py:92
  32.6 1.0 collective-permute-done.7.refs_10_
  33.7 1.6 %collective-permute-start.13 = (bf16[256,512]{1,0:T(8,128)(2,1)S(1)}, bf16[256,512]{1,0:T(8,128)(2,1)S(1)}, u32[]{:S(2)}, u32[]{:S(2)}) collective-permute-start(bf16[256,512]{1,0:T(8,128)(2,1)S(1)} %collective-permute-done.1.refs_4_), channel_id=1, source_target_pairs={{0,2},{1,3},{2,0},{3,1},{4,6},{5,7},{6,4},{7,5},{8,10},{9,11},{10,... | collective-permute-start | bytes 786440 | tf_op jit(solution)/shard_map/ppermute | solution.py:92
  35.3 0.5 collective-permute-start.14
  35.8 1.6 %collective-permute-start.12 = (bf16[256,512]{1,0:T(8,128)(2,1)}, bf16[256,512]{1,0:T(8,128)(2,1)S(1)}, u32[]{:S(2)}, u32[]{:S(2)}) collective-permute-start(bf16[256,512]{1,0:T(8,128)(2,1)} %collective-permute-done.9.refs_12_), channel_id=1, source_target_pairs={{0,4},{1,5},{2,6},{3,7},{4,0},{5,1},{6,2},{7,3},{8,12},{9,13},{10,... | collective-permute-start | bytes 786440 | tf_op jit(solution)/shard_map/ppermute | solution.py:92
  37.3 0.5 collective-permute-start.11
  37.8 5.1 %collective-permute-done.13.refs_15_ = bf16[256,512]{1,0:T(8,128)(2,1)S(1)} collective-permute-done((bf16[256,512]{1,0:T(8,128)(2,1)S(1)}, bf16[256,512]{1,0:T(8,128)(2,1)S(1)}, u32[]{:S(2)}, u32[]{:S(2)}) %collective-permute-start.13) | collective-permute-done | bytes 262176 | tf_op jit(solution)/shard_map/ppermute | solution.py:92
  42.9 1.8 %collective-permute-done.14.refs_16_ = bf16[256,512]{1,0:T(8,128)(2,1)S(1)} collective-permute-done((bf16[256,512]{1,0:T(8,128)(2,1)}, bf16[256,512]{1,0:T(8,128)(2,1)S(1)}, u32[]{:S(2)}, u32[]{:S(2)}) %collective-permute-start.14) | collective-permute-done | bytes 262176 | tf_op jit(solution)/shard_map/ppermute | solution.py:92
  44.6 4.8 %collective-permute-done.12.refs_14_ = bf16[256,512]{1,0:T(8,128)(2,1)S(1)} collective-permute-done((bf16[256,512]{1,0:T(8,128)(2,1)}, bf16[256,512]{1,0:T(8,128)(2,1)S(1)}, u32[]{:S(2)}, u32[]{:S(2)}) %collective-permute-start.12) | collective-permute-done | bytes 262176 | tf_op jit(solution)/shard_map/ppermute | solution.py:92
  49.5 0.6 collective-permute-start.16
  50.1 0.8 collective-permute-start.17
  50.9 0.6 stack.87.refs_0_.chips_ref
  51.5 6.1 %project.1 = (bf16[3584,512]{1,0:T(8,128)(2,1)}, f32[2,128,512]{2,1,0:T(8,128)}) custom-call(s32[16]{0:T(128)} %stack.87.refs_0_.chips_ref, bf16[128,4096]{1,0:T(8,128)(2,1)} %refs_0_, bf16[128,4096]{1,0:T(8,128)(2,1)} %copy-done.3, bf16[256,512]{1,0:T(8,128)(2,1)} %copy-done.4, bf16[256,512]{1,0:T(8,128)(2,1)} %copy-done.8, bf16[256,512]{1,0:T(8,128)(2,1)} %copy-done.7, ...), custom_call_target="tpu_custom_call" | custom-call | tf_op jit(solution)/shard_map/project/pallas_call | solution.py:429
  57.7 0.6 copy-done.10
  58.4 0.5 collective-permute-start.20
  58.9 3.8 %delta.1 = (bf16[272,512]{1,0:T(8,128)(2,1)}, bf16[512,512]{1,0:T(8,128)(2,1)}) custom-call(s32[16]{0:T(128)} %stack.87.refs_0_.chips_ref, s32[1]{0:T(128)} %bitcast.16.me_ref, bf16[144,512]{1,0:T(8,128)(2,1)} %get-tuple-element.109.own_cot_ref, bf16[144,512]{1,0:T(8,128)(2,1)} %copy-done.14, bf16[128,4096]{1,0:T(8,128)(2,1)} %refs_0_, ...), custom_call_target="tpu_custom_call" | custom-call | tf_op jit(solution)/shard_map/delta/pallas_call | solution.py:429
  62.7 1.4 %collective-permute-start.19 = (bf16[272,512]{1,0:T(8,128)(2,1)}, bf16[272,512]{1,0:T(8,128)(2,1)S(1)}, u32[]{:S(2)}, u32[]{:S(2)}) collective-permute-start(bf16[272,512]{1,0:T(8,128)(2,1)} %get-tuple-element.126.refs_0_), channel_id=1, source_target_pairs={{0,16},{1,17},{2,18},{3,19},{4,20},{5,21},{6,22},{7,23},{8,24},{9,... | collective-permute-start | bytes 835592 | tf_op jit(solution)/shard_map/ppermute | solution.py:92
  64.1 3.8 %collective-permute-start.18 = (bf16[272,512]{1,0:T(8,128)(2,1)}, bf16[272,512]{1,0:T(8,128)(2,1)S(1)}, u32[]{:S(2)}, u32[]{:S(2)}) collective-permute-start(bf16[272,512]{1,0:T(8,128)(2,1)} %get-tuple-element.126.refs_0_), channel_id=1, source_target_pairs={{0,8},{1,9},{2,10},{3,11},{4,12},{5,13},{6,14},{7,15},{8,0},{9,1},... | collective-permute-start | bytes 835592 | tf_op jit(solution)/shard_map/ppermute | solution.py:92
  68.0 10.6 %collective-permute-done.19.refs_2_ = bf16[272,512]{1,0:T(8,128)(2,1)S(1)} collective-permute-done((bf16[272,512]{1,0:T(8,128)(2,1)}, bf16[272,512]{1,0:T(8,128)(2,1)S(1)}, u32[]{:S(2)}, u32[]{:S(2)}) %collective-permute-start.19) | collective-permute-done | bytes 278560 | tf_op jit(solution)/shard_map/ppermute | solution.py:92
  79.1 7.1 %collective-permute-done.21.refs_3_ = bf16[272,512]{1,0:T(8,128)(2,1)S(1)} collective-permute-done((bf16[272,512]{1,0:T(8,128)(2,1)S(1)}, bf16[272,512]{1,0:T(8,128)(2,1)S(1)}, u32[]{:S(2)}, u32[]{:S(2)}) %collective-permute-start.21) | collective-permute-done | bytes 278560 | tf_op jit(solution)/shard_map/ppermute | solution.py:92
  86.2 0.5 collective-permute-start.23
  86.7 1.0 copy-done
  87.7 1.8 %select.28 = bf16[8,64,512]{2,1,0:T(8,128)(2,1)} custom-call(s32[1]{0:T(128)} %bitcast.16.me_ref, bf16[272,512]{1,0:T(8,128)(2,1)S(1)} %copy-done, bf16[272,512]{1,0:T(8,128)(2,1)S(1)} %collective-permute-done.18.refs_1_, bf16[272,512]{1,0:T(8,128)(2,1)S(1)} %collective-permute-done.19.refs_2_, bf16[272,512]{1,0:T(8,128)(2,1)S(1)} %collective-permute-done.21.refs_3_), custom_call_target="tpu_custom_call" | custom-call | tf_op jit(solution)/shard_map/select/pallas_call | solution.py:496
  89.5 4.2 %all-to-all-start.1 = ((bf16[8,64,512]{2,1,0:T(8,128)(2,1)}), bf16[8,64,512]{2,1,0:T(8,128)(2,1)}, u32[]{:S(2)}, u32[]{:S(2)}) async-start(bf16[8,64,512]{2,1,0:T(8,128)(2,1)} %select.28), calls=%async_computation.1 | async-start | bytes 1048576 | tf_op jit(solution)/shard_map/all_to_all | solution.py:505
  93.6 0.9 copy-done.1
  94.6 2.8 %weight_grad.1 = (f32[256,512]{1,0:T(8,128)S(1)}, bf16[256,512]{1,0:T(8,128)(2,1)}, bf16[256,512]{1,0:T(8,128)(2,1)}, bf16[256,512]{1,0:T(8,128)(2,1)}) custom-call(s32[1]{0:T(128)} %bitcast.16.me_ref, bf16[4,128,1024]{2,1,0:T(8,128)(2,1)S(1)} %all-to-all-done.own_ref, bf16[4,128,1024]{2,1,0:T(8,128)(2,1)S(1)} %collective-permute-done.20.mate_ref, ...), custom_call_target="tpu_custom_call" | custom-call | tf_op jit(solution)/shard_map/weight_grad/pallas_call | solution.py:517
  97.3 2.0 %collective-permute-start.24 = (bf16[256,512]{1,0:T(8,128)(2,1)}, bf16[256,512]{1,0:T(8,128)(2,1)S(1)}, u32[]{:S(2)}, u32[]{:S(2)}) collective-permute-start(bf16[256,512]{1,0:T(8,128)(2,1)} %get-tuple-element.129), channel_id=1, source_target_pairs={{0,2},{1,3},{2,0},{3,1},{4,6},{5,7},{6,4},{7,5},{8,10},{9,11},{10,... | collective-permute-start | bytes 786440 | tf_op jit(solution)/shard_map/ppermute | solution.py:92
  99.3 1.5 %collective-permute-start.25 = (bf16[256,512]{1,0:T(8,128)(2,1)}, bf16[256,512]{1,0:T(8,128)(2,1)S(1)}, u32[]{:S(2)}, u32[]{:S(2)}) collective-permute-start(bf16[256,512]{1,0:T(8,128)(2,1)} %get-tuple-element.130), channel_id=1, source_target_pairs={{0,4},{1,5},{2,6},{3,7},{4,0},{5,1},{6,2},{7,3},{8,12},{9,13},{10,... | collective-permute-start | bytes 786440 | tf_op jit(solution)/shard_map/ppermute | solution.py:92
  100.9 2.9 %all-to-all-done.1 = bf16[8,64,512]{2,1,0:T(8,128)(2,1)} async-done(((bf16[8,64,512]{2,1,0:T(8,128)(2,1)}), bf16[8,64,512]{2,1,0:T(8,128)(2,1)}, u32[]{:S(2)}, u32[]{:S(2)}) %all-to-all-start.1) | async-done | bytes 524320 | tf_op jit(solution)/shard_map/all_to_all | solution.py:505
  103.9 7.2 %row_grad.1 = bf16[256,4096]{1,0:T(8,128)(2,1)} custom-call(s32[16]{0:T(128)} %stack.87.refs_0_.chips_ref, s32[1]{0:T(128)} %bitcast.16.me_ref, bf16[4,2,64,512]{3,2,1,0:T(8,128)(2,1)} %bitcast.26.got_ref, bf16[3584,512]{1,0:T(8,128)(2,1)} %get-tuple-element.123.refs_0_, bf16[3584,512]{1,0:T(8,128)(2,1)} %collective-permute-done.22.refs_1_, ...), custom_call_target="tpu_custom_call" | custom-call | tf_op jit(solution)/shard_map/row_grad/pallas_call | solution.py:533
  111.1 3.4 %collective-permute-done.26.refs_2_ = bf16[256,512]{1,0:T(8,128)(2,1)S(1)} collective-permute-done((bf16[256,512]{1,0:T(8,128)(2,1)}, bf16[256,512]{1,0:T(8,128)(2,1)S(1)}, u32[]{:S(2)}, u32[]{:S(2)}) %collective-permute-start.26) | collective-permute-done | bytes 262176 | tf_op jit(solution)/shard_map/ppermute | solution.py:92
  114.7 1.5 %collective-permute-done.27.mate_ref = f32[128,512]{1,0:T(8,128)S(1)} collective-permute-done((f32[128,512]{1,0:T(8,128)S(1)}, f32[128,512]{1,0:T(8,128)S(1)}, u32[]{:S(2)}, u32[]{:S(2)}) %collective-permute-start.27) | collective-permute-done | bytes 262176 | tf_op jit(solution)/shard_map/ppermute | solution.py:92
  116.2 0.8 join.1
  (73 shorter events, 2.5 us)
Async XLA Ops:
  0.6 23.5 %copy-start.15 = (s32[1,4]{1,0:T(1,128)S(1)}, s32[1,4]{1,0:T(1,128)}, u32[]{:S(2)}) copy-start(s32[1,4]{1,0:T(1,128)} %param.9) | copy-start | bytes 52
  0.6 23.8 %copy-start.16 = (s32[128,1]{0,1:T(1,128)S(1)}, s32[128,1]{0,1:T(1,128)}, u32[]{:S(2)}) copy-start(s32[128,1]{0,1:T(1,128)} %param.8) | copy-start | bytes 1540
  0.7 1.9 %collective-permute-start = (bf16[128,1024]{1,0:T(8,128)(2,1)}, bf16[128,1024]{1,0:T(8,128)(2,1)S(1)}, u32[]{:S(2)}, u32[]{:S(2)}) collective-permute-start(bf16[128,1024]{1,0:T(8,128)(2,1)} %param.11), channel_id=1, source_target_pairs={{0,1},{1,0},{2,3},{3,2},{4,5},{5,4},{6,7},{7,6},{8,9},{9,8},{10,11... | collective-permute-start | bytes 786440 | tf_op jit(solution)/shard_map/ppermute | solution.py:92
  2.6 26.6 %copy-start.17 = (s32[4]{0:T(128)S(1)}, s32[4]{0:T(128)}, u32[]{:S(2)}) copy-start(s32[4]{0:T(128)} %param.10) | copy-start | bytes 52
  2.6 27.8 %copy-start.4 = (bf16[256,512]{1,0:T(8,128)(2,1)}, bf16[256,512]{1,0:T(8,128)(2,1)S(1)}, u32[]{:S(2)}) copy-start(bf16[256,512]{1,0:T(8,128)(2,1)S(1)} %maximum_select_fusion.refs_3_) | copy-start | bytes 786436
  2.7 31.0 %copy-start.2 = (bf16[128,4096]{1,0:T(8,128)(2,1)S(1)}, bf16[128,4096]{1,0:T(8,128)(2,1)}, u32[]{:S(2)}) copy-start(bf16[128,4096]{1,0:T(8,128)(2,1)} %refs_0_) | copy-start | bytes 3145732
  2.7 17.0 %collective-permute-start.4 = (bf16[256,512]{1,0:T(8,128)(2,1)S(1)}, bf16[256,512]{1,0:T(8,128)(2,1)S(1)}, u32[]{:S(2)}, u32[]{:S(2)}) collective-permute-start(bf16[256,512]{1,0:T(8,128)(2,1)S(1)} %maximum_select_fusion.refs_3_), channel_id=1, source_target_pairs={{0,16},{1,17},{2,18},{3,19},{4,20},{5,21},{6,22},{7,23},{8,24},{9,... | collective-permute-start | bytes 786440 | tf_op jit(solution)/shard_map/ppermute | solution.py:92
  6.7 13.0 %collective-permute-start.3 = (bf16[256,512]{1,0:T(8,128)(2,1)S(1)}, bf16[256,512]{1,0:T(8,128)(2,1)S(1)}, u32[]{:S(2)}, u32[]{:S(2)}) collective-permute-start(bf16[256,512]{1,0:T(8,128)(2,1)S(1)} %maximum_select_fusion.refs_3_), channel_id=1, source_target_pairs={{0,8},{1,9},{2,10},{3,11},{4,12},{5,13},{6,14},{7,15},{8,0},{9,1},... | collective-permute-start | bytes 786440 | tf_op jit(solution)/shard_map/ppermute | solution.py:92
  8.3 11.4 %collective-permute-start.2 = (bf16[256,512]{1,0:T(8,128)(2,1)S(1)}, bf16[256,512]{1,0:T(8,128)(2,1)S(1)}, u32[]{:S(2)}, u32[]{:S(2)}) collective-permute-start(bf16[256,512]{1,0:T(8,128)(2,1)S(1)} %maximum_select_fusion.refs_3_), channel_id=1, source_target_pairs={{0,2},{1,3},{2,0},{3,1},{4,6},{5,7},{6,4},{7,5},{8,10},{9,11},{10,... | collective-permute-start | bytes 786440 | tf_op jit(solution)/shard_map/ppermute | solution.py:92
  9.8 9.9 %collective-permute-start.1 = (bf16[256,512]{1,0:T(8,128)(2,1)S(1)}, bf16[256,512]{1,0:T(8,128)(2,1)S(1)}, u32[]{:S(2)}, u32[]{:S(2)}) collective-permute-start(bf16[256,512]{1,0:T(8,128)(2,1)S(1)} %maximum_select_fusion.refs_3_), channel_id=1, source_target_pairs={{0,4},{1,5},{2,6},{3,7},{4,0},{5,1},{6,2},{7,3},{8,12},{9,13},{10,... | collective-permute-start | bytes 786440 | tf_op jit(solution)/shard_map/ppermute | solution.py:92
  13.7 17.5 %collective-permute-start.9 = (bf16[256,512]{1,0:T(8,128)(2,1)S(1)}, bf16[256,512]{1,0:T(8,128)(2,1)}, u32[]{:S(2)}, u32[]{:S(2)}) collective-permute-start(bf16[256,512]{1,0:T(8,128)(2,1)S(1)} %maximum_select_fusion.refs_3_), channel_id=1, source_target_pairs={{0,24},{1,25},{2,26},{3,27},{4,28},{5,29},{6,30},{7,31},{8,16},{9,... | collective-permute-start | bytes 786440 | tf_op jit(solution)/shard_map/ppermute | solution.py:92
  19.7 13.9 %copy-start.5 = (bf16[256,512]{1,0:T(8,128)(2,1)}, bf16[256,512]{1,0:T(8,128)(2,1)S(1)}, u32[]{:S(2)}) copy-start(bf16[256,512]{1,0:T(8,128)(2,1)S(1)} %collective-permute-done.4.refs_7_) | copy-start | bytes 786436
  19.7 13.9 %copy-start.6 = (bf16[256,512]{1,0:T(8,128)(2,1)}, bf16[256,512]{1,0:T(8,128)(2,1)S(1)}, u32[]{:S(2)}) copy-start(bf16[256,512]{1,0:T(8,128)(2,1)S(1)} %collective-permute-done.3.refs_6_) | copy-start | bytes 786436
  19.7 10.7 %copy-start.7 = (bf16[256,512]{1,0:T(8,128)(2,1)}, bf16[256,512]{1,0:T(8,128)(2,1)S(1)}, u32[]{:S(2)}) copy-start(bf16[256,512]{1,0:T(8,128)(2,1)S(1)} %collective-permute-done.2.refs_5_) | copy-start | bytes 786436
  19.7 31.8 %copy-start.8 = (bf16[256,512]{1,0:T(8,128)(2,1)}, bf16[256,512]{1,0:T(8,128)(2,1)S(1)}, u32[]{:S(2)}) copy-start(bf16[256,512]{1,0:T(8,128)(2,1)S(1)} %collective-permute-done.1.refs_4_) | copy-start | bytes 786436
  19.7 11.5 %collective-permute-start.6 = (bf16[256,512]{1,0:T(8,128)(2,1)S(1)}, bf16[256,512]{1,0:T(8,128)(2,1)}, u32[]{:S(2)}, u32[]{:S(2)}) collective-permute-start(bf16[256,512]{1,0:T(8,128)(2,1)S(1)} %collective-permute-done.3.refs_6_), channel_id=1, source_target_pairs={{0,4},{1,5},{2,6},{3,7},{4,0},{5,1},{6,2},{7,3},{8,12},{9,13},{10,... | collective-permute-start | bytes 786440 | tf_op jit(solution)/shard_map/ppermute | solution.py:92
  22.0 9.2 %collective-permute-start.5 = (bf16[256,512]{1,0:T(8,128)(2,1)S(1)}, bf16[256,512]{1,0:T(8,128)(2,1)}, u32[]{:S(2)}, u32[]{:S(2)}) collective-permute-start(bf16[256,512]{1,0:T(8,128)(2,1)S(1)} %collective-permute-done.3.refs_6_), channel_id=1, source_target_pairs={{0,2},{1,3},{2,0},{3,1},{4,6},{5,7},{6,4},{7,5},{8,10},{9,11},{10,... | collective-permute-start | bytes 786440 | tf_op jit(solution)/shard_map/ppermute | solution.py:92
  23.5 9.1 %collective-permute-start.8 = (bf16[256,512]{1,0:T(8,128)(2,1)S(1)}, bf16[256,512]{1,0:T(8,128)(2,1)}, u32[]{:S(2)}, u32[]{:S(2)}) collective-permute-start(bf16[256,512]{1,0:T(8,128)(2,1)S(1)} %collective-permute-done.4.refs_7_), channel_id=1, source_target_pairs={{0,4},{1,5},{2,6},{3,7},{4,0},{5,1},{6,2},{7,3},{8,12},{9,13},{10,... | collective-permute-start | bytes 786440 | tf_op jit(solution)/shard_map/ppermute | solution.py:92
  24.0 9.6 %collective-permute-start.7 = (bf16[256,512]{1,0:T(8,128)(2,1)S(1)}, bf16[256,512]{1,0:T(8,128)(2,1)}, u32[]{:S(2)}, u32[]{:S(2)}) collective-permute-start(bf16[256,512]{1,0:T(8,128)(2,1)S(1)} %collective-permute-done.4.refs_7_), channel_id=1, source_target_pairs={{0,2},{1,3},{2,0},{3,1},{4,6},{5,7},{6,4},{7,5},{8,10},{9,11},{10,... | collective-permute-start | bytes 786440 | tf_op jit(solution)/shard_map/ppermute | solution.py:92
  24.5 33.0 %all-to-all-start = ((bf16[4,128,1024]{2,1,0:T(8,128)(2,1)}), bf16[4,128,1024]{2,1,0:T(8,128)(2,1)S(1)}, u32[]{:S(2)}, u32[]{:S(2)}) async-start(bf16[4,128,1024]{2,1,0:T(8,128)(2,1)} %pad_maximum_fusion), calls=%async_computation | async-start | bytes 2097152 | tf_op jit(solution)/shard_map/all_to_all | solution.py:379
  33.6 15.8 %collective-permute-start.10 = (bf16[128,4096]{1,0:T(8,128)(2,1)S(1)}, bf16[128,4096]{1,0:T(8,128)(2,1)S(1)}, u32[]{:S(2)}, u32[]{:S(2)}) collective-permute-start(bf16[128,4096]{1,0:T(8,128)(2,1)S(1)} %copy-done.2), channel_id=1, source_target_pairs={{0,1},{1,0},{2,3},{3,2},{4,5},{5,4},{6,7},{7,6},{8,9},{9,8},{10,11... | collective-permute-start | bytes 3145736 | tf_op jit(solution)/shard_map/ppermute | solution.py:92
  33.7 9.2 %collective-permute-start.13 = (bf16[256,512]{1,0:T(8,128)(2,1)S(1)}, bf16[256,512]{1,0:T(8,128)(2,1)S(1)}, u32[]{:S(2)}, u32[]{:S(2)}) collective-permute-start(bf16[256,512]{1,0:T(8,128)(2,1)S(1)} %collective-permute-done.1.refs_4_), channel_id=1, source_target_pairs={{0,2},{1,3},{2,0},{3,1},{4,6},{5,7},{6,4},{7,5},{8,10},{9,11},{10,... | collective-permute-start | bytes 786440 | tf_op jit(solution)/shard_map/ppermute | solution.py:92
  35.3 9.4 %collective-permute-start.14 = (bf16[256,512]{1,0:T(8,128)(2,1)}, bf16[256,512]{1,0:T(8,128)(2,1)S(1)}, u32[]{:S(2)}, u32[]{:S(2)}) collective-permute-start(bf16[256,512]{1,0:T(8,128)(2,1)} %collective-permute-done.7.refs_10_), channel_id=1, source_target_pairs={{0,4},{1,5},{2,6},{3,7},{4,0},{5,1},{6,2},{7,3},{8,12},{9,13},{10,... | collective-permute-start | bytes 786440 | tf_op jit(solution)/shard_map/ppermute | solution.py:92
  35.8 13.7 %collective-permute-start.12 = (bf16[256,512]{1,0:T(8,128)(2,1)}, bf16[256,512]{1,0:T(8,128)(2,1)S(1)}, u32[]{:S(2)}, u32[]{:S(2)}) collective-permute-start(bf16[256,512]{1,0:T(8,128)(2,1)} %collective-permute-done.9.refs_12_), channel_id=1, source_target_pairs={{0,4},{1,5},{2,6},{3,7},{4,0},{5,1},{6,2},{7,3},{8,12},{9,13},{10,... | collective-permute-start | bytes 786440 | tf_op jit(solution)/shard_map/ppermute | solution.py:92
  37.3 12.2 %collective-permute-start.11 = (bf16[256,512]{1,0:T(8,128)(2,1)}, bf16[256,512]{1,0:T(8,128)(2,1)}, u32[]{:S(2)}, u32[]{:S(2)}) collective-permute-start(bf16[256,512]{1,0:T(8,128)(2,1)} %collective-permute-done.9.refs_12_), channel_id=1, source_target_pairs={{0,2},{1,3},{2,0},{3,1},{4,6},{5,7},{6,4},{7,5},{8,10},{9,11},{10,... | collective-permute-start | bytes 786440 | tf_op jit(solution)/shard_map/ppermute | solution.py:92
  42.9 6.6 %copy-start.9 = (bf16[256,512]{1,0:T(8,128)(2,1)}, bf16[256,512]{1,0:T(8,128)(2,1)S(1)}, u32[]{:S(2)}) copy-start(bf16[256,512]{1,0:T(8,128)(2,1)S(1)} %collective-permute-done.13.refs_15_) | copy-start | bytes 786436
  44.6 5.4 %copy-start.11 = (bf16[256,512]{1,0:T(8,128)(2,1)}, bf16[256,512]{1,0:T(8,128)(2,1)S(1)}, u32[]{:S(2)}) copy-start(bf16[256,512]{1,0:T(8,128)(2,1)S(1)} %collective-permute-done.14.refs_16_) | copy-start | bytes 786436
  49.5 1.4 %copy-start.13 = (bf16[256,512]{1,0:T(8,128)(2,1)}, bf16[256,512]{1,0:T(8,128)(2,1)S(1)}, u32[]{:S(2)}) copy-start(bf16[256,512]{1,0:T(8,128)(2,1)S(1)} %collective-permute-done.12.refs_14_) | copy-start | bytes 786436
  49.5 2.0 %copy-start.3 = (bf16[128,4096]{1,0:T(8,128)(2,1)}, bf16[128,4096]{1,0:T(8,128)(2,1)S(1)}, u32[]{:S(2)}) copy-start(bf16[128,4096]{1,0:T(8,128)(2,1)S(1)} %collective-permute-done.10.refs_2_.refs_1_) | copy-start | bytes 3145732
  49.5 8.1 %collective-permute-start.16 = (bf16[256,512]{1,0:T(8,128)(2,1)}, bf16[256,512]{1,0:T(8,128)(2,1)S(1)}, u32[]{:S(2)}, u32[]{:S(2)}) collective-permute-start(bf16[256,512]{1,0:T(8,128)(2,1)} %collective-permute-done.6.refs_9_), channel_id=1, source_target_pairs={{0,2},{1,3},{2,0},{3,1},{4,6},{5,7},{6,4},{7,5},{8,10},{9,11},{10,... | collective-permute-start | bytes 786440 | tf_op jit(solution)/shard_map/ppermute | solution.py:92
  50.1 7.6 %collective-permute-start.17 = (bf16[256,512]{1,0:T(8,128)(2,1)}, bf16[256,512]{1,0:T(8,128)(2,1)S(1)}, u32[]{:S(2)}, u32[]{:S(2)}) collective-permute-start(bf16[256,512]{1,0:T(8,128)(2,1)} %collective-permute-done.11.refs_13_), channel_id=1, source_target_pairs={{0,4},{1,5},{2,6},{3,7},{4,0},{5,1},{6,2},{7,3},{8,12},{9,13},{10,... | collective-permute-start | bytes 786440 | tf_op jit(solution)/shard_map/ppermute | solution.py:92
  50.9 6.7 %collective-permute-start.15 = (bf16[144,512]{1,0:T(8,128)(2,1)}, bf16[144,512]{1,0:T(8,128)(2,1)S(1)}, u32[]{:S(2)}, u32[]{:S(2)}) collective-permute-start(bf16[144,512]{1,0:T(8,128)(2,1)} %get-tuple-element.89), channel_id=1, source_target_pairs={{0,1},{1,0},{2,3},{3,2},{4,5},{5,4},{6,7},{7,6},{8,9},{9,8},{10,11... | collective-permute-start | bytes 442376 | tf_op jit(solution)/shard_map/ppermute | solution.py:92
  57.5 1.4 %copy-start.14 = (bf16[144,512]{1,0:T(8,128)(2,1)}, bf16[144,512]{1,0:T(8,128)(2,1)S(1)}, u32[]{:S(2)}) copy-start(bf16[144,512]{1,0:T(8,128)(2,1)S(1)} %collective-permute-done.15.mate_cot_ref) | copy-start | bytes 442372
  57.6 0.7 copy-start.10
  57.7 0.7 copy-start.12
  58.4 20.2 %collective-permute-start.20 = (bf16[4,128,1024]{2,1,0:T(8,128)(2,1)S(1)}, bf16[4,128,1024]{2,1,0:T(8,128)(2,1)S(1)}, u32[]{:S(2)}, u32[]{:S(2)}) collective-permute-start(bf16[4,128,1024]{2,1,0:T(8,128)(2,1)S(1)} %all-to-all-done.own_ref), channel_id=1, source_target_pairs={{0,1},{1,0},{2,3},{3,2},{4,5},{5,4},{6,7},{7,6},{8,9},{9,8},{10,11... | collective-permute-start | bytes 3145736 | tf_op jit(solution)/shard_map/ppermute | solution.py:92
  62.7 15.8 %collective-permute-start.19 = (bf16[272,512]{1,0:T(8,128)(2,1)}, bf16[272,512]{1,0:T(8,128)(2,1)S(1)}, u32[]{:S(2)}, u32[]{:S(2)}) collective-permute-start(bf16[272,512]{1,0:T(8,128)(2,1)} %get-tuple-element.126.refs_0_), channel_id=1, source_target_pairs={{0,16},{1,17},{2,18},{3,19},{4,20},{5,21},{6,22},{7,23},{8,24},{9,... | collective-permute-start | bytes 835592 | tf_op jit(solution)/shard_map/ppermute | solution.py:92
  64.1 14.6 %collective-permute-start.18 = (bf16[272,512]{1,0:T(8,128)(2,1)}, bf16[272,512]{1,0:T(8,128)(2,1)S(1)}, u32[]{:S(2)}, u32[]{:S(2)}) collective-permute-start(bf16[272,512]{1,0:T(8,128)(2,1)} %get-tuple-element.126.refs_0_), channel_id=1, source_target_pairs={{0,8},{1,9},{2,10},{3,11},{4,12},{5,13},{6,14},{7,15},{8,0},{9,1},... | collective-permute-start | bytes 835592 | tf_op jit(solution)/shard_map/ppermute | solution.py:92
  78.7 7.6 %collective-permute-start.21 = (bf16[272,512]{1,0:T(8,128)(2,1)S(1)}, bf16[272,512]{1,0:T(8,128)(2,1)S(1)}, u32[]{:S(2)}, u32[]{:S(2)}) collective-permute-start(bf16[272,512]{1,0:T(8,128)(2,1)S(1)} %collective-permute-done.19.refs_2_), channel_id=1, source_target_pairs={{0,8},{1,9},{2,10},{3,11},{4,12},{5,13},{6,14},{7,15},{8,0},{9,1},... | collective-permute-start | bytes 835592 | tf_op jit(solution)/shard_map/ppermute | solution.py:92
  86.2 17.6 %collective-permute-start.22 = (bf16[3584,512]{1,0:T(8,128)(2,1)}, bf16[3584,512]{1,0:T(8,128)(2,1)}, u32[]{:S(2)}, u32[]{:S(2)}) collective-permute-start(bf16[3584,512]{1,0:T(8,128)(2,1)} %get-tuple-element.123.refs_0_), channel_id=1, source_target_pairs={{0,1},{1,0},{2,3},{3,2},{4,5},{5,4},{6,7},{7,6},{8,9},{9,8},{10,11... | collective-permute-start | bytes 11010056 | tf_op jit(solution)/shard_map/ppermute | solution.py:92
  86.2 17.6 %collective-permute-start.23 = (bf16[512,512]{1,0:T(8,128)(2,1)}, bf16[512,512]{1,0:T(8,128)(2,1)}, u32[]{:S(2)}, u32[]{:S(2)}) collective-permute-start(bf16[512,512]{1,0:T(8,128)(2,1)} %get-tuple-element.124.refs_2_), channel_id=1, source_target_pairs={{0,1},{1,0},{2,3},{3,2},{4,5},{5,4},{6,7},{7,6},{8,9},{9,8},{10,11... | collective-permute-start | bytes 1572872 | tf_op jit(solution)/shard_map/ppermute | solution.py:92
  86.7 1.0 copy-start
  89.5 14.4 %all-to-all-start.1 = ((bf16[8,64,512]{2,1,0:T(8,128)(2,1)}), bf16[8,64,512]{2,1,0:T(8,128)(2,1)}, u32[]{:S(2)}, u32[]{:S(2)}) async-start(bf16[8,64,512]{2,1,0:T(8,128)(2,1)} %select.28), calls=%async_computation.1 | async-start | bytes 1048576 | tf_op jit(solution)/shard_map/all_to_all | solution.py:505
  93.6 1.0 copy-start.1
  97.3 13.8 %collective-permute-start.24 = (bf16[256,512]{1,0:T(8,128)(2,1)}, bf16[256,512]{1,0:T(8,128)(2,1)S(1)}, u32[]{:S(2)}, u32[]{:S(2)}) collective-permute-start(bf16[256,512]{1,0:T(8,128)(2,1)} %get-tuple-element.129), channel_id=1, source_target_pairs={{0,2},{1,3},{2,0},{3,1},{4,6},{5,7},{6,4},{7,5},{8,10},{9,11},{10,... | collective-permute-start | bytes 786440 | tf_op jit(solution)/shard_map/ppermute | solution.py:92
  99.3 11.8 %collective-permute-start.25 = (bf16[256,512]{1,0:T(8,128)(2,1)}, bf16[256,512]{1,0:T(8,128)(2,1)S(1)}, u32[]{:S(2)}, u32[]{:S(2)}) collective-permute-start(bf16[256,512]{1,0:T(8,128)(2,1)} %get-tuple-element.130), channel_id=1, source_target_pairs={{0,4},{1,5},{2,6},{3,7},{4,0},{5,1},{6,2},{7,3},{8,12},{9,13},{10,... | collective-permute-start | bytes 786440 | tf_op jit(solution)/shard_map/ppermute | solution.py:92
  100.8 13.7 %collective-permute-start.26 = (bf16[256,512]{1,0:T(8,128)(2,1)}, bf16[256,512]{1,0:T(8,128)(2,1)S(1)}, u32[]{:S(2)}, u32[]{:S(2)}) collective-permute-start(bf16[256,512]{1,0:T(8,128)(2,1)} %get-tuple-element.131), channel_id=1, source_target_pairs={{0,6},{1,7},{2,4},{3,5},{4,2},{5,3},{6,0},{7,1},{8,14},{9,15},{10,... | collective-permute-start | bytes 786440 | tf_op jit(solution)/shard_map/ppermute | solution.py:92
  114.6 1.6 %collective-permute-start.27 = (f32[128,512]{1,0:T(8,128)S(1)}, f32[128,512]{1,0:T(8,128)S(1)}, u32[]{:S(2)}, u32[]{:S(2)}) collective-permute-start(f32[128,512]{1,0:T(8,128)S(1)} %get-tuple-element.133), channel_id=1, source_target_pairs={{0,1},{1,0},{2,3},{3,2},{4,5},{5,4},{6,7},{7,6},{8,9},{9,8},{10,11... | collective-permute-start | bytes 786440 | tf_op jit(solution)/shard_map/ppermute | solution.py:92

commit v19 on v18

--- a/solution.py
+++ b/solution.py
@@ -177,29 +177,30 @@
         copy.wait()
 
 
-def select_kernel(me_ref, *refs):
+def select_kernel(begin, me_ref, *refs):
     *deltas, sent_ref, held, sems = refs
-    copies = fetch([(ref, held.at[n]) for n, ref in enumerate(deltas)], sems)
+    copies = fetch([(ref, held.at[n]) for n, ref in enumerate(deltas[-held.shape[0] :])], sems)
     rows = (held.shape[1] - CODE_ROWS) // 2
-    per_chip = sent_ref.shape[1] // len(deltas)
+    per_chip = sent_ref.shape[1] // (begin + held.shape[0])
+    if begin:
+        sent_ref[:, : begin * per_chip, :] = deltas[0][...]
     iota = lax.broadcasted_iota(jnp.int32, (PLANE * per_chip, 2 * rows), 0)
     wanted = (me_ref[0] & -PLANE) + lax.shift_right_logical(iota, per_chip.bit_length() - 1)
     slot = iota & (per_chip - 1)
-    for n in range(len(deltas)):
+    for n in range(held.shape[0]):
         copies[n].wait()
         code = held[n, 2 * rows :, : 2 * rows].astype(jnp.float32).astype(jnp.int32)
         hot = (wanted == code[0:1, :]) & (slot == code[1:2, :])
         found = dot(hot.astype(jnp.bfloat16), held[n, : 2 * rows, :], ((1,), (0,)))
         found = found.astype(jnp.bfloat16)
+        at = (begin + n) * per_chip
         for place in range(PLANE):
-            sent_ref[place, n * per_chip : (n + 1) * per_chip, :] = found[
+            sent_ref[place, at : at + per_chip, :] = found[
                 place * per_chip : (place + 1) * per_chip, :
             ]
 
 
-def weight_grad_kernel(me_ref, own_ref, mate_ref, *refs):
-    *deltas, own_part_ref, part_x, part_y, part_both, hidden, held, acc, sems = refs
-    part_refs = (part_x, part_y, part_both)
+def plane_terms(begin, me_ref, own_ref, mate_ref, deltas, hidden, held, sems):
     plane = lax.shift_right_logical(me_ref[0], 3)
     core = me_ref[0] & 1
     rows = own_ref.shape[1]
@@ -208,20 +209,26 @@
         own = pl.multiple_of((2 * n + core) * rows, rows)
         mate = pl.multiple_of((2 * n + 1 - core) * rows, rows)
         pairs += [
-            (own_ref.at[plane ^ n], hidden.at[pl.ds(own, rows), :]),
-            (mate_ref.at[plane ^ n], hidden.at[pl.ds(mate, rows), :]),
+            (own_ref.at[plane ^ (begin + n)], hidden.at[pl.ds(own, rows), :]),
+            (mate_ref.at[plane ^ (begin + n)], hidden.at[pl.ds(mate, rows), :]),
             (ref.at[: 2 * rows, :], held.at[2 * n * rows : 2 * (n + 1) * rows, :]),
         ]
-    copies = fetch(pairs, sems)
-    for first in (0, 2):
-        for copy in copies[3 * first : 3 * first + 6]:
-            copy.wait()
-        part = slice(2 * first * rows, 2 * (first + 2) * rows)
-        terms = dot(hidden[part, :], held[part, :], ((0,), (0,)))
-        if first == 0:
-            acc[...] = terms
-        else:
-            acc[...] += terms
+    for copy in fetch(pairs, sems):
+        copy.wait()
+    return dot(hidden[...], held[...], ((0,), (0,)))
+
+
+def first_terms_kernel(me_ref, own_ref, mate_ref, *refs):
+    *deltas, terms_ref, hidden, held, sems = refs
+    terms_ref[...] = plane_terms(0, me_ref, own_ref, mate_ref, deltas, hidden, held, sems)
+
+
+def weight_grad_kernel(begin, me_ref, own_ref, mate_ref, begun_ref, *refs):
+    *deltas, own_part_ref, part_x, part_y, part_both, hidden, held, acc, sems = refs
+    part_refs = (part_x, part_y, part_both)
+    acc[...] = begun_ref[...] + plane_terms(
+        begin, me_ref, own_ref, mate_ref, deltas, hidden, held, sems
+    )
     count = own_part_ref.shape[0]
 
     def block(mask):
@@ -492,16 +499,25 @@
     )
     mate_first, mate_last = swap(first_weight, CORE), swap(last_weight, CORE)
     count = levels * 2 * per_peer
-    delta_room = pltpu.VMEM((levels, *delta.shape), jnp.bfloat16)
-    selected = pl.pallas_call(
-        select_kernel,
-        out_shape=jax.ShapeDtypeStruct((PLANE, count, half_cols), jnp.bfloat16),
-        in_specs=[SCALAR] + anywhere(levels),
-        out_specs=vmem(1)[0],
-        scratch_shapes=[delta_room, pltpu.SemaphoreType.DMA((levels,))],
-        compiler_params=grant(16),
-        name="select",
-    )(me_scalar, *deltas)
+    def select(begin, before, deltas, name):
+        return pl.pallas_call(
+            functools.partial(select_kernel, begin),
+            out_shape=jax.ShapeDtypeStruct(
+                (PLANE, count // levels * (begin + len(deltas)), half_cols), jnp.bfloat16
+            ),
+            in_specs=[SCALAR] + vmem(len(before)) + anywhere(len(deltas)),
+            out_specs=vmem(1)[0],
+            scratch_shapes=[
+                pltpu.VMEM((len(deltas), *delta.shape), jnp.bfloat16),
+                pltpu.SemaphoreType.DMA((len(deltas),)),
+            ],
+            compiler_params=grant(16),
+            name=name,
+        )(me_scalar, *before, *deltas)
+
+    there = [delta, delta_near, delta_far]
+    selected = select(0, [], there, "first_select")
+    selected = select(3, [selected], deltas[3:], "select")
     got = lax.all_to_all(
         selected,
         "dp",
@@ -514,20 +530,33 @@
     shard = width_model // size
     mine_terms = jax.ShapeDtypeStruct((wide // 4, half_cols), jnp.float32)
     sent_terms = jax.ShapeDtypeStruct(mine_terms.shape, jnp.bfloat16)
+    all_terms = jax.ShapeDtypeStruct((wide, half_cols), jnp.float32)
+
+    def room(chips):
+        return [
+            pltpu.VMEM((chips * 2 * rows, wide), jnp.bfloat16),
+            pltpu.VMEM((chips * 2 * rows, half_cols), jnp.bfloat16),
+        ]
+
+    begun_terms = pl.pallas_call(
+        first_terms_kernel,
+        out_shape=all_terms,
+        in_specs=[SCALAR] + anywhere(5),
+        out_specs=vmem(1)[0],
+        scratch_shapes=room(3) + [pltpu.SemaphoreType.DMA((9,))],
+        compiler_params=grant(16),
+        name="first_terms",
+    )(me_scalar, own_features, mate_features, *there)
     own_part, *parts = pl.pallas_call(
-        weight_grad_kernel,
+        functools.partial(weight_grad_kernel, 3),
         out_shape=(mine_terms, *[sent_terms] * 3),
-        in_specs=[SCALAR] + anywhere(2 + levels),
+        in_specs=[SCALAR] + anywhere(2) + vmem(1) + anywhere(1),
         out_specs=tuple(hbm(1) + vmem(3)),
-        scratch_shapes=[
-            pltpu.VMEM((levels * 2 * rows, wide), jnp.bfloat16),
-            pltpu.VMEM((levels * 2 * rows, half_cols), jnp.bfloat16),
-            pltpu.VMEM((wide, half_cols), jnp.float32),
-            pltpu.SemaphoreType.DMA((3 * levels + 1,)),
-        ],
+        scratch_shapes=room(1)
+        + [pltpu.VMEM(all_terms.shape, all_terms.dtype), pltpu.SemaphoreType.DMA((4,))],
         compiler_params=grant(16),
         name="weight_grad",
-    )(me_scalar, own_features, mate_features, after(delta, selected), *deltas[1:])
+    )(me_scalar, own_features, mate_features, begun_terms, after(deltas[3], selected))
     parts = [swap(part, mask) for part, mask in zip(parts, PLANE_MASKS[1:])]
 
     row_grads = pl.pallas_call(

time: 118 us -> 118 us (level)
    pallas_call x2 -> x4, Pallas kernels: 4.52 us -> 4.61 us  [the longest x2 1.79 us: select(): pl.pallas_call(functools.partial(select_kernel, begin), out_shape=jax.Sha...]
  transfers between devices with their start and end apart: 30 -> 30, of which waited for: 14 -> 13; matrix products, arithmetic and copies ran while one was open for 5% -> 5% of each run, Pallas kernels for 18% -> 19%
where the time goes in v19:
time: 118 us; the launch traced here: 117 us
  waiting for transfers between devices  46 us (39%)
  starting transfers between devices  38.3 us (32%)
  Pallas kernels  22.7 us (19%)
  local copies, waits for them, and re-layouts  5.77 us (5%)
  other arithmetic  3.47 us (3%)
    ppermute x28, waiting for transfers between devices, swap(): return lax.ppermute(value, 'dp', [(i, i ^ mask) for i in range(size)])  43.1 us
    ppermute x28, starting transfers between devices, swap(): return lax.ppermute(value, 'dp', [(i, i ^ mask) for i in range(size)])  29.5 us
    pallas_call x2, Pallas kernels, project(): pl.pallas_call(kernel, out_shape=(*results, jax.ShapeDtypeStruct((count *...  9.86 us
    pallas_call x1, Pallas kernels, per_device_paired(): pl.pallas_call(row_grad_kernel, out_shape=jax.ShapeDtypeStruct((receive,...  7.24 us
    all_to_all x1, starting transfers between devices, per_device_paired(): lax.all_to_all(by_level, 'dp', split_axis=0, concat_axis=0, axis_index_gr...  4.65 us
    all_to_all x1, starting transfers between devices, per_device_paired(): lax.all_to_all(selected, 'dp', split_axis=0, concat_axis=0, axis_index_gr...  4.15 us
    all_to_all x1, waiting for transfers between devices, per_device_paired(): lax.all_to_all(selected, 'dp', split_axis=0, concat_axis=0, axis_index_gr...  2.86 us
    unnamed x36, local copies, waits for them, and re-layouts  2.79 us
  transfers between devices with their start and end apart: 30, of which 13 were waited for; matrix products, arithmetic and copies ran while one was open for 5% of the time, Pallas kernels for 19%

profile of v19, /device:TPU:0, one launch (start us, length us, event | category | flops | bytes accessed | tf_op | source)
XLA Modules:
  0.0 117.2 jit_solution(14866743265059754356)
XLA Ops:
  0.7 0.5 collective-permute-start
  1.2 1.0 fusion.11
  2.7 4.0 %collective-permute-start.4 = (bf16[256,512]{1,0:T(8,128)(2,1)S(1)}, bf16[256,512]{1,0:T(8,128)(2,1)S(1)}, u32[]{:S(2)}, u32[]{:S(2)}) collective-permute-start(bf16[256,512]{1,0:T(8,128)(2,1)S(1)} %maximum_select_fusion.refs_3_), channel_id=1, source_target_pairs={{0,16},{1,17},{2,18},{3,19},{4,20},{5,21},{6,22},{7,23},{8,24},{9,... | collective-permute-start | bytes 786440 | tf_op jit(solution)/shard_map/ppermute | solution.py:92
  6.7 1.6 %collective-permute-start.3 = (bf16[256,512]{1,0:T(8,128)(2,1)S(1)}, bf16[256,512]{1,0:T(8,128)(2,1)S(1)}, u32[]{:S(2)}, u32[]{:S(2)}) collective-permute-start(bf16[256,512]{1,0:T(8,128)(2,1)S(1)} %maximum_select_fusion.refs_3_), channel_id=1, source_target_pairs={{0,8},{1,9},{2,10},{3,11},{4,12},{5,13},{6,14},{7,15},{8,0},{9,1},... | collective-permute-start | bytes 786440 | tf_op jit(solution)/shard_map/ppermute | solution.py:92
  8.3 1.5 %collective-permute-start.2 = (bf16[256,512]{1,0:T(8,128)(2,1)S(1)}, bf16[256,512]{1,0:T(8,128)(2,1)S(1)}, u32[]{:S(2)}, u32[]{:S(2)}) collective-permute-start(bf16[256,512]{1,0:T(8,128)(2,1)S(1)} %maximum_select_fusion.refs_3_), channel_id=1, source_target_pairs={{0,2},{1,3},{2,0},{3,1},{4,6},{5,7},{6,4},{7,5},{8,10},{9,11},{10,... | collective-permute-start | bytes 786440 | tf_op jit(solution)/shard_map/ppermute | solution.py:92
  9.8 1.5 %collective-permute-start.1 = (bf16[256,512]{1,0:T(8,128)(2,1)S(1)}, bf16[256,512]{1,0:T(8,128)(2,1)S(1)}, u32[]{:S(2)}, u32[]{:S(2)}) collective-permute-start(bf16[256,512]{1,0:T(8,128)(2,1)S(1)} %maximum_select_fusion.refs_3_), channel_id=1, source_target_pairs={{0,4},{1,5},{2,6},{3,7},{4,0},{5,1},{6,2},{7,3},{8,12},{9,13},{10,... | collective-permute-start | bytes 786440 | tf_op jit(solution)/shard_map/ppermute | solution.py:92
  11.3 1.3 %slice_bitcast_fusion.3 = (bf16[1,128,1024]{2,1,0:T(8,128)(2,1)S(1)}, bf16[1,128,1024]{2,1,0:T(8,128)(2,1)S(1)}, bf16[1,128,1024]{2,1,0:T(8,128)(2,1)S(1)}, bf16[1,128,1024]{2,1,0:T(8,128)(2,1)S(1)}) fusion(bf16[128,4096]{1,0:T(8,128)(2,1)} %refs_0_), kind=kLoop, calls=%fused_computation.6 | loop fusion | bytes 2097152 | tf_op jit(solution)/shard_map/stack | solution.py:381
  12.6 1.1 pad_maximum_fusion
  13.9 5.8 %collective-permute-done.4.refs_7_ = bf16[256,512]{1,0:T(8,128)(2,1)S(1)} collective-permute-done((bf16[256,512]{1,0:T(8,128)(2,1)S(1)}, bf16[256,512]{1,0:T(8,128)(2,1)S(1)}, u32[]{:S(2)}, u32[]{:S(2)}) %collective-permute-start.4) | collective-permute-done | bytes 262176 | tf_op jit(solution)/shard_map/ppermute | solution.py:92
  19.7 2.3 %collective-permute-start.6 = (bf16[256,512]{1,0:T(8,128)(2,1)S(1)}, bf16[256,512]{1,0:T(8,128)(2,1)}, u32[]{:S(2)}, u32[]{:S(2)}) collective-permute-start(bf16[256,512]{1,0:T(8,128)(2,1)S(1)} %collective-permute-done.3.refs_6_), channel_id=1, source_target_pairs={{0,4},{1,5},{2,6},{3,7},{4,0},{5,1},{6,2},{7,3},{8,12},{9,13},{10,... | collective-permute-start | bytes 786440 | tf_op jit(solution)/shard_map/ppermute | solution.py:92
  22.0 1.5 %collective-permute-start.5 = (bf16[256,512]{1,0:T(8,128)(2,1)S(1)}, bf16[256,512]{1,0:T(8,128)(2,1)}, u32[]{:S(2)}, u32[]{:S(2)}) collective-permute-start(bf16[256,512]{1,0:T(8,128)(2,1)S(1)} %collective-permute-done.3.refs_6_), channel_id=1, source_target_pairs={{0,2},{1,3},{2,0},{3,1},{4,6},{5,7},{6,4},{7,5},{8,10},{9,11},{10,... | collective-permute-start | bytes 786440 | tf_op jit(solution)/shard_map/ppermute | solution.py:92
  23.5 0.5 collective-permute-start.8
  24.5 4.7 %all-to-all-start = ((bf16[4,128,1024]{2,1,0:T(8,128)(2,1)}), bf16[4,128,1024]{2,1,0:T(8,128)(2,1)S(1)}, u32[]{:S(2)}, u32[]{:S(2)}) async-start(bf16[4,128,1024]{2,1,0:T(8,128)(2,1)} %pad_maximum_fusion), calls=%async_computation | async-start | bytes 2097152 | tf_op jit(solution)/shard_map/all_to_all | solution.py:386
  29.3 1.1 compare_select_fusion
  30.4 0.8 pad_maximum_fusion.1
  31.2 1.4 %collective-permute-done.8.refs_11_ = bf16[256,512]{1,0:T(8,128)(2,1)} collective-permute-done((bf16[256,512]{1,0:T(8,128)(2,1)S(1)}, bf16[256,512]{1,0:T(8,128)(2,1)}, u32[]{:S(2)}, u32[]{:S(2)}) %collective-permute-start.8) | collective-permute-done | bytes 262176 | tf_op jit(solution)/shard_map/ppermute | solution.py:92
  32.6 1.0 collective-permute-done.7.refs_10_
  33.7 1.6 %collective-permute-start.13 = (bf16[256,512]{1,0:T(8,128)(2,1)S(1)}, bf16[256,512]{1,0:T(8,128)(2,1)S(1)}, u32[]{:S(2)}, u32[]{:S(2)}) collective-permute-start(bf16[256,512]{1,0:T(8,128)(2,1)S(1)} %collective-permute-done.1.refs_4_), channel_id=1, source_target_pairs={{0,2},{1,3},{2,0},{3,1},{4,6},{5,7},{6,4},{7,5},{8,10},{9,11},{10,... | collective-permute-start | bytes 786440 | tf_op jit(solution)/shard_map/ppermute | solution.py:92
  35.3 0.5 collective-permute-start.14
  35.8 1.6 %collective-permute-start.12 = (bf16[256,512]{1,0:T(8,128)(2,1)}, bf16[256,512]{1,0:T(8,128)(2,1)S(1)}, u32[]{:S(2)}, u32[]{:S(2)}) collective-permute-start(bf16[256,512]{1,0:T(8,128)(2,1)} %collective-permute-done.9.refs_12_), channel_id=1, source_target_pairs={{0,4},{1,5},{2,6},{3,7},{4,0},{5,1},{6,2},{7,3},{8,12},{9,13},{10,... | collective-permute-start | bytes 786440 | tf_op jit(solution)/shard_map/ppermute | solution.py:92
  37.8 5.1 %collective-permute-done.13.refs_15_ = bf16[256,512]{1,0:T(8,128)(2,1)S(1)} collective-permute-done((bf16[256,512]{1,0:T(8,128)(2,1)S(1)}, bf16[256,512]{1,0:T(8,128)(2,1)S(1)}, u32[]{:S(2)}, u32[]{:S(2)}) %collective-permute-start.13) | collective-permute-done | bytes 262176 | tf_op jit(solution)/shard_map/ppermute | solution.py:92
  42.9 1.8 %collective-permute-done.14.refs_16_ = bf16[256,512]{1,0:T(8,128)(2,1)S(1)} collective-permute-done((bf16[256,512]{1,0:T(8,128)(2,1)}, bf16[256,512]{1,0:T(8,128)(2,1)S(1)}, u32[]{:S(2)}, u32[]{:S(2)}) %collective-permute-start.14) | collective-permute-done | bytes 262176 | tf_op jit(solution)/shard_map/ppermute | solution.py:92
  44.6 4.8 %collective-permute-done.12.refs_14_ = bf16[256,512]{1,0:T(8,128)(2,1)S(1)} collective-permute-done((bf16[256,512]{1,0:T(8,128)(2,1)}, bf16[256,512]{1,0:T(8,128)(2,1)S(1)}, u32[]{:S(2)}, u32[]{:S(2)}) %collective-permute-start.12) | collective-permute-done | bytes 262176 | tf_op jit(solution)/shard_map/ppermute | solution.py:92
  49.5 0.6 collective-permute-start.16
  50.1 0.8 collective-permute-start.17
  50.9 0.7 stack.87.refs_0_.chips_ref
  51.6 6.1 %project.1 = (bf16[3584,512]{1,0:T(8,128)(2,1)}, f32[2,128,512]{2,1,0:T(8,128)}) custom-call(s32[16]{0:T(128)} %stack.87.refs_0_.chips_ref, bf16[128,4096]{1,0:T(8,128)(2,1)} %refs_0_, bf16[128,4096]{1,0:T(8,128)(2,1)} %copy-done.3, bf16[256,512]{1,0:T(8,128)(2,1)} %copy-done.4, bf16[256,512]{1,0:T(8,128)(2,1)} %copy-done.8, bf16[256,512]{1,0:T(8,128)(2,1)} %copy-done.7, ...), custom_call_target="tpu_custom_call" | custom-call | tf_op jit(solution)/shard_map/project/pallas_call | solution.py:436
  57.7 0.7 copy-done.10
  59.0 3.8 %delta.1 = (bf16[272,512]{1,0:T(8,128)(2,1)}, bf16[512,512]{1,0:T(8,128)(2,1)}) custom-call(s32[16]{0:T(128)} %stack.87.refs_0_.chips_ref, s32[1]{0:T(128)} %bitcast.16.me_ref, bf16[144,512]{1,0:T(8,128)(2,1)} %get-tuple-element.107.own_cot_ref, bf16[144,512]{1,0:T(8,128)(2,1)} %copy-done.14, bf16[128,4096]{1,0:T(8,128)(2,1)} %refs_0_, ...), custom_call_target="tpu_custom_call" | custom-call | tf_op jit(solution)/shard_map/delta/pallas_call | solution.py:436
  62.9 1.4 %collective-permute-start.19 = (bf16[272,512]{1,0:T(8,128)(2,1)}, bf16[272,512]{1,0:T(8,128)(2,1)S(1)}, u32[]{:S(2)}, u32[]{:S(2)}) collective-permute-start(bf16[272,512]{1,0:T(8,128)(2,1)} %get-tuple-element.112.refs_0_), channel_id=1, source_target_pairs={{0,16},{1,17},{2,18},{3,19},{4,20},{5,21},{6,22},{7,23},{8,24},{9,... | collective-permute-start | bytes 835592 | tf_op jit(solution)/shard_map/ppermute | solution.py:92
  64.2 3.8 %collective-permute-start.18 = (bf16[272,512]{1,0:T(8,128)(2,1)}, bf16[272,512]{1,0:T(8,128)(2,1)S(1)}, u32[]{:S(2)}, u32[]{:S(2)}) collective-permute-start(bf16[272,512]{1,0:T(8,128)(2,1)} %get-tuple-element.112.refs_0_), channel_id=1, source_target_pairs={{0,8},{1,9},{2,10},{3,11},{4,12},{5,13},{6,14},{7,15},{8,0},{9,1},... | collective-permute-start | bytes 835592 | tf_op jit(solution)/shard_map/ppermute | solution.py:92
  68.1 10.6 %collective-permute-done.19.refs_2_ = bf16[272,512]{1,0:T(8,128)(2,1)S(1)} collective-permute-done((bf16[272,512]{1,0:T(8,128)(2,1)}, bf16[272,512]{1,0:T(8,128)(2,1)S(1)}, u32[]{:S(2)}, u32[]{:S(2)}) %collective-permute-start.19) | collective-permute-done | bytes 278560 | tf_op jit(solution)/shard_map/ppermute | solution.py:92
  79.1 7.2 %collective-permute-done.21.refs_1_.refs_0_ = bf16[272,512]{1,0:T(8,128)(2,1)S(1)} collective-permute-done((bf16[272,512]{1,0:T(8,128)(2,1)S(1)}, bf16[272,512]{1,0:T(8,128)(2,1)S(1)}, u32[]{:S(2)}, u32[]{:S(2)}) %collective-permute-start.21) | collective-permute-done | bytes 278560 | tf_op jit(solution)/shard_map/ppermute | solution.py:92
  86.3 0.5 collective-permute-start.23
  86.9 1.0 copy-done
  87.8 0.7 first_select.1.refs_0_
  88.5 1.1 select.28
  89.6 4.2 %all-to-all-start.1 = ((bf16[8,64,512]{2,1,0:T(8,128)(2,1)}), bf16[8,64,512]{2,1,0:T(8,128)(2,1)}, u32[]{:S(2)}, u32[]{:S(2)}) async-start(bf16[8,64,512]{2,1,0:T(8,128)(2,1)} %select.28), calls=%async_computation.1 | async-start | bytes 1048576 | tf_op jit(solution)/shard_map/all_to_all | solution.py:521
  93.8 0.9 copy-done.1
  94.7 1.3 %first_terms.1.begun_ref = f32[1024,512]{1,0:T(8,128)S(1)} custom-call(s32[1]{0:T(128)} %bitcast.16.me_ref, bf16[4,128,1024]{2,1,0:T(8,128)(2,1)S(1)} %all-to-all-done.own_ref, bf16[4,128,1024]{2,1,0:T(8,128)(2,1)S(1)} %collective-permute-done.20.mate_ref, bf16[272,512]{1,0:T(8,128)(2,1)S(1)} %copy-done.1, ...), custom_call_target="tpu_custom_call" | custom-call | tf_op jit(solution)/shard_map/first_terms/pallas_call | solution.py:541
  96.0 1.5 %weight_grad.1 = (f32[256,512]{1,0:T(8,128)S(1)}, bf16[256,512]{1,0:T(8,128)(2,1)}, bf16[256,512]{1,0:T(8,128)(2,1)S(1)}, bf16[256,512]{1,0:T(8,128)(2,1)S(1)}) custom-call(s32[1]{0:T(128)} %bitcast.16.me_ref, bf16[4,128,1024]{2,1,0:T(8,128)(2,1)S(1)} %all-to-all-done.own_ref, bf16[4,128,1024]{2,1,0:T(8,128)(2,1)S(1)} %collective-permute-done.20.mate_ref, ...), custom_call_target="tpu_custom_call" | custom-call | tf_op jit(solution)/shard_map/weight_grad/pallas_call | solution.py:550
  97.6 2.0 %collective-permute-start.24 = (bf16[256,512]{1,0:T(8,128)(2,1)}, bf16[256,512]{1,0:T(8,128)(2,1)S(1)}, u32[]{:S(2)}, u32[]{:S(2)}) collective-permute-start(bf16[256,512]{1,0:T(8,128)(2,1)} %get-tuple-element.125), channel_id=1, source_target_pairs={{0,2},{1,3},{2,0},{3,1},{4,6},{5,7},{6,4},{7,5},{8,10},{9,11},{10,... | collective-permute-start | bytes 786440 | tf_op jit(solution)/shard_map/ppermute | solution.py:92
  99.5 1.5 %collective-permute-start.25 = (bf16[256,512]{1,0:T(8,128)(2,1)S(1)}, bf16[256,512]{1,0:T(8,128)(2,1)S(1)}, u32[]{:S(2)}, u32[]{:S(2)}) collective-permute-start(bf16[256,512]{1,0:T(8,128)(2,1)S(1)} %get-tuple-element.126), channel_id=1, source_target_pairs={{0,4},{1,5},{2,6},{3,7},{4,0},{5,1},{6,2},{7,3},{8,12},{9,13},{10,... | collective-permute-start | bytes 786440 | tf_op jit(solution)/shard_map/ppermute | solution.py:92
  101.1 2.9 %all-to-all-done.1 = bf16[8,64,512]{2,1,0:T(8,128)(2,1)} async-done(((bf16[8,64,512]{2,1,0:T(8,128)(2,1)}), bf16[8,64,512]{2,1,0:T(8,128)(2,1)}, u32[]{:S(2)}, u32[]{:S(2)}) %all-to-all-start.1) | async-done | bytes 524320 | tf_op jit(solution)/shard_map/all_to_all | solution.py:521
  104.0 7.2 %row_grad.1 = bf16[256,4096]{1,0:T(8,128)(2,1)} custom-call(s32[16]{0:T(128)} %stack.87.refs_0_.chips_ref, s32[1]{0:T(128)} %bitcast.16.me_ref, bf16[4,2,64,512]{3,2,1,0:T(8,128)(2,1)} %bitcast.26.got_ref, bf16[3584,512]{1,0:T(8,128)(2,1)} %get-tuple-element.119.refs_0_, bf16[3584,512]{1,0:T(8,128)(2,1)} %collective-permute-done.22.refs_1_, ...), custom_call_target="tpu_custom_call" | custom-call | tf_op jit(solution)/shard_map/row_grad/pallas_call | solution.py:562
  111.3 3.4 %collective-permute-done.26.refs_2_ = bf16[256,512]{1,0:T(8,128)(2,1)S(1)} collective-permute-done((bf16[256,512]{1,0:T(8,128)(2,1)S(1)}, bf16[256,512]{1,0:T(8,128)(2,1)S(1)}, u32[]{:S(2)}, u32[]{:S(2)}) %collective-permute-start.26) | collective-permute-done | bytes 262176 | tf_op jit(solution)/shard_map/ppermute | solution.py:92
  114.8 1.5 %collective-permute-done.27.mate_ref = f32[128,512]{1,0:T(8,128)S(1)} collective-permute-done((f32[128,512]{1,0:T(8,128)S(1)}, f32[128,512]{1,0:T(8,128)S(1)}, u32[]{:S(2)}, u32[]{:S(2)}) %collective-permute-start.27) | collective-permute-done | bytes 262176 | tf_op jit(solution)/shard_map/ppermute | solution.py:92
  116.4 0.8 join.1
  (75 shorter events, 3.4 us)
Async XLA Ops:
  0.6 23.5 %copy-start.15 = (s32[1,4]{1,0:T(1,128)S(1)}, s32[1,4]{1,0:T(1,128)}, u32[]{:S(2)}) copy-start(s32[1,4]{1,0:T(1,128)} %param.9) | copy-start | bytes 52
  0.6 23.8 %copy-start.16 = (s32[128,1]{0,1:T(1,128)S(1)}, s32[128,1]{0,1:T(1,128)}, u32[]{:S(2)}) copy-start(s32[128,1]{0,1:T(1,128)} %param.8) | copy-start | bytes 1540
  0.7 1.9 %collective-permute-start = (bf16[128,1024]{1,0:T(8,128)(2,1)}, bf16[128,1024]{1,0:T(8,128)(2,1)S(1)}, u32[]{:S(2)}, u32[]{:S(2)}) collective-permute-start(bf16[128,1024]{1,0:T(8,128)(2,1)} %param.11), channel_id=1, source_target_pairs={{0,1},{1,0},{2,3},{3,2},{4,5},{5,4},{6,7},{7,6},{8,9},{9,8},{10,11... | collective-permute-start | bytes 786440 | tf_op jit(solution)/shard_map/ppermute | solution.py:92
  2.6 26.6 %copy-start.17 = (s32[4]{0:T(128)S(1)}, s32[4]{0:T(128)}, u32[]{:S(2)}) copy-start(s32[4]{0:T(128)} %param.10) | copy-start | bytes 52
  2.6 27.8 %copy-start.4 = (bf16[256,512]{1,0:T(8,128)(2,1)}, bf16[256,512]{1,0:T(8,128)(2,1)S(1)}, u32[]{:S(2)}) copy-start(bf16[256,512]{1,0:T(8,128)(2,1)S(1)} %maximum_select_fusion.refs_3_) | copy-start | bytes 786436
  2.7 31.0 %copy-start.2 = (bf16[128,4096]{1,0:T(8,128)(2,1)S(1)}, bf16[128,4096]{1,0:T(8,128)(2,1)}, u32[]{:S(2)}) copy-start(bf16[128,4096]{1,0:T(8,128)(2,1)} %refs_0_) | copy-start | bytes 3145732
  2.7 17.0 %collective-permute-start.4 = (bf16[256,512]{1,0:T(8,128)(2,1)S(1)}, bf16[256,512]{1,0:T(8,128)(2,1)S(1)}, u32[]{:S(2)}, u32[]{:S(2)}) collective-permute-start(bf16[256,512]{1,0:T(8,128)(2,1)S(1)} %maximum_select_fusion.refs_3_), channel_id=1, source_target_pairs={{0,16},{1,17},{2,18},{3,19},{4,20},{5,21},{6,22},{7,23},{8,24},{9,... | collective-permute-start | bytes 786440 | tf_op jit(solution)/shard_map/ppermute | solution.py:92
  6.7 13.0 %collective-permute-start.3 = (bf16[256,512]{1,0:T(8,128)(2,1)S(1)}, bf16[256,512]{1,0:T(8,128)(2,1)S(1)}, u32[]{:S(2)}, u32[]{:S(2)}) collective-permute-start(bf16[256,512]{1,0:T(8,128)(2,1)S(1)} %maximum_select_fusion.refs_3_), channel_id=1, source_target_pairs={{0,8},{1,9},{2,10},{3,11},{4,12},{5,13},{6,14},{7,15},{8,0},{9,1},... | collective-permute-start | bytes 786440 | tf_op jit(solution)/shard_map/ppermute | solution.py:92
  8.3 11.4 %collective-permute-start.2 = (bf16[256,512]{1,0:T(8,128)(2,1)S(1)}, bf16[256,512]{1,0:T(8,128)(2,1)S(1)}, u32[]{:S(2)}, u32[]{:S(2)}) collective-permute-start(bf16[256,512]{1,0:T(8,128)(2,1)S(1)} %maximum_select_fusion.refs_3_), channel_id=1, source_target_pairs={{0,2},{1,3},{2,0},{3,1},{4,6},{5,7},{6,4},{7,5},{8,10},{9,11},{10,... | collective-permute-start | bytes 786440 | tf_op jit(solution)/shard_map/ppermute | solution.py:92
  9.8 9.9 %collective-permute-start.1 = (bf16[256,512]{1,0:T(8,128)(2,1)S(1)}, bf16[256,512]{1,0:T(8,128)(2,1)S(1)}, u32[]{:S(2)}, u32[]{:S(2)}) collective-permute-start(bf16[256,512]{1,0:T(8,128)(2,1)S(1)} %maximum_select_fusion.refs_3_), channel_id=1, source_target_pairs={{0,4},{1,5},{2,6},{3,7},{4,0},{5,1},{6,2},{7,3},{8,12},{9,13},{10,... | collective-permute-start | bytes 786440 | tf_op jit(solution)/shard_map/ppermute | solution.py:92
  13.7 17.5 %collective-permute-start.9 = (bf16[256,512]{1,0:T(8,128)(2,1)S(1)}, bf16[256,512]{1,0:T(8,128)(2,1)}, u32[]{:S(2)}, u32[]{:S(2)}) collective-permute-start(bf16[256,512]{1,0:T(8,128)(2,1)S(1)} %maximum_select_fusion.refs_3_), channel_id=1, source_target_pairs={{0,24},{1,25},{2,26},{3,27},{4,28},{5,29},{6,30},{7,31},{8,16},{9,... | collective-permute-start | bytes 786440 | tf_op jit(solution)/shard_map/ppermute | solution.py:92
  19.7 13.9 %copy-start.5 = (bf16[256,512]{1,0:T(8,128)(2,1)}, bf16[256,512]{1,0:T(8,128)(2,1)S(1)}, u32[]{:S(2)}) copy-start(bf16[256,512]{1,0:T(8,128)(2,1)S(1)} %collective-permute-done.4.refs_7_) | copy-start | bytes 786436
  19.7 13.9 %copy-start.6 = (bf16[256,512]{1,0:T(8,128)(2,1)}, bf16[256,512]{1,0:T(8,128)(2,1)S(1)}, u32[]{:S(2)}) copy-start(bf16[256,512]{1,0:T(8,128)(2,1)S(1)} %collective-permute-done.3.refs_6_) | copy-start | bytes 786436
  19.7 10.7 %copy-start.7 = (bf16[256,512]{1,0:T(8,128)(2,1)}, bf16[256,512]{1,0:T(8,128)(2,1)S(1)}, u32[]{:S(2)}) copy-start(bf16[256,512]{1,0:T(8,128)(2,1)S(1)} %collective-permute-done.2.refs_5_) | copy-start | bytes 786436
  19.7 31.9 %copy-start.8 = (bf16[256,512]{1,0:T(8,128)(2,1)}, bf16[256,512]{1,0:T(8,128)(2,1)S(1)}, u32[]{:S(2)}) copy-start(bf16[256,512]{1,0:T(8,128)(2,1)S(1)} %collective-permute-done.1.refs_4_) | copy-start | bytes 786436
  19.7 11.5 %collective-permute-start.6 = (bf16[256,512]{1,0:T(8,128)(2,1)S(1)}, bf16[256,512]{1,0:T(8,128)(2,1)}, u32[]{:S(2)}, u32[]{:S(2)}) collective-permute-start(bf16[256,512]{1,0:T(8,128)(2,1)S(1)} %collective-permute-done.3.refs_6_), channel_id=1, source_target_pairs={{0,4},{1,5},{2,6},{3,7},{4,0},{5,1},{6,2},{7,3},{8,12},{9,13},{10,... | collective-permute-start | bytes 786440 | tf_op jit(solution)/shard_map/ppermute | solution.py:92
  22.0 9.2 %collective-permute-start.5 = (bf16[256,512]{1,0:T(8,128)(2,1)S(1)}, bf16[256,512]{1,0:T(8,128)(2,1)}, u32[]{:S(2)}, u32[]{:S(2)}) collective-permute-start(bf16[256,512]{1,0:T(8,128)(2,1)S(1)} %collective-permute-done.3.refs_6_), channel_id=1, source_target_pairs={{0,2},{1,3},{2,0},{3,1},{4,6},{5,7},{6,4},{7,5},{8,10},{9,11},{10,... | collective-permute-start | bytes 786440 | tf_op jit(solution)/shard_map/ppermute | solution.py:92
  23.5 9.1 %collective-permute-start.8 = (bf16[256,512]{1,0:T(8,128)(2,1)S(1)}, bf16[256,512]{1,0:T(8,128)(2,1)}, u32[]{:S(2)}, u32[]{:S(2)}) collective-permute-start(bf16[256,512]{1,0:T(8,128)(2,1)S(1)} %collective-permute-done.4.refs_7_), channel_id=1, source_target_pairs={{0,4},{1,5},{2,6},{3,7},{4,0},{5,1},{6,2},{7,3},{8,12},{9,13},{10,... | collective-permute-start | bytes 786440 | tf_op jit(solution)/shard_map/ppermute | solution.py:92
  24.0 9.6 %collective-permute-start.7 = (bf16[256,512]{1,0:T(8,128)(2,1)S(1)}, bf16[256,512]{1,0:T(8,128)(2,1)}, u32[]{:S(2)}, u32[]{:S(2)}) collective-permute-start(bf16[256,512]{1,0:T(8,128)(2,1)S(1)} %collective-permute-done.4.refs_7_), channel_id=1, source_target_pairs={{0,2},{1,3},{2,0},{3,1},{4,6},{5,7},{6,4},{7,5},{8,10},{9,11},{10,... | collective-permute-start | bytes 786440 | tf_op jit(solution)/shard_map/ppermute | solution.py:92
  24.5 33.1 %all-to-all-start = ((bf16[4,128,1024]{2,1,0:T(8,128)(2,1)}), bf16[4,128,1024]{2,1,0:T(8,128)(2,1)S(1)}, u32[]{:S(2)}, u32[]{:S(2)}) async-start(bf16[4,128,1024]{2,1,0:T(8,128)(2,1)} %pad_maximum_fusion), calls=%async_computation | async-start | bytes 2097152 | tf_op jit(solution)/shard_map/all_to_all | solution.py:386
  33.6 15.8 %collective-permute-start.10 = (bf16[128,4096]{1,0:T(8,128)(2,1)S(1)}, bf16[128,4096]{1,0:T(8,128)(2,1)S(1)}, u32[]{:S(2)}, u32[]{:S(2)}) collective-permute-start(bf16[128,4096]{1,0:T(8,128)(2,1)S(1)} %copy-done.2), channel_id=1, source_target_pairs={{0,1},{1,0},{2,3},{3,2},{4,5},{5,4},{6,7},{7,6},{8,9},{9,8},{10,11... | collective-permute-start | bytes 3145736 | tf_op jit(solution)/shard_map/ppermute | solution.py:92
  33.7 9.2 %collective-permute-start.13 = (bf16[256,512]{1,0:T(8,128)(2,1)S(1)}, bf16[256,512]{1,0:T(8,128)(2,1)S(1)}, u32[]{:S(2)}, u32[]{:S(2)}) collective-permute-start(bf16[256,512]{1,0:T(8,128)(2,1)S(1)} %collective-permute-done.1.refs_4_), channel_id=1, source_target_pairs={{0,2},{1,3},{2,0},{3,1},{4,6},{5,7},{6,4},{7,5},{8,10},{9,11},{10,... | collective-permute-start | bytes 786440 | tf_op jit(solution)/shard_map/ppermute | solution.py:92
  35.3 9.4 %collective-permute-start.14 = (bf16[256,512]{1,0:T(8,128)(2,1)}, bf16[256,512]{1,0:T(8,128)(2,1)S(1)}, u32[]{:S(2)}, u32[]{:S(2)}) collective-permute-start(bf16[256,512]{1,0:T(8,128)(2,1)} %collective-permute-done.7.refs_10_), channel_id=1, source_target_pairs={{0,4},{1,5},{2,6},{3,7},{4,0},{5,1},{6,2},{7,3},{8,12},{9,13},{10,... | collective-permute-start | bytes 786440 | tf_op jit(solution)/shard_map/ppermute | solution.py:92
  35.8 13.7 %collective-permute-start.12 = (bf16[256,512]{1,0:T(8,128)(2,1)}, bf16[256,512]{1,0:T(8,128)(2,1)S(1)}, u32[]{:S(2)}, u32[]{:S(2)}) collective-permute-start(bf16[256,512]{1,0:T(8,128)(2,1)} %collective-permute-done.9.refs_12_), channel_id=1, source_target_pairs={{0,4},{1,5},{2,6},{3,7},{4,0},{5,1},{6,2},{7,3},{8,12},{9,13},{10,... | collective-permute-start | bytes 786440 | tf_op jit(solution)/shard_map/ppermute | solution.py:92
  37.3 12.2 %collective-permute-start.11 = (bf16[256,512]{1,0:T(8,128)(2,1)}, bf16[256,512]{1,0:T(8,128)(2,1)}, u32[]{:S(2)}, u32[]{:S(2)}) collective-permute-start(bf16[256,512]{1,0:T(8,128)(2,1)} %collective-permute-done.9.refs_12_), channel_id=1, source_target_pairs={{0,2},{1,3},{2,0},{3,1},{4,6},{5,7},{6,4},{7,5},{8,10},{9,11},{10,... | collective-permute-start | bytes 786440 | tf_op jit(solution)/shard_map/ppermute | solution.py:92
  42.9 6.6 %copy-start.9 = (bf16[256,512]{1,0:T(8,128)(2,1)}, bf16[256,512]{1,0:T(8,128)(2,1)S(1)}, u32[]{:S(2)}) copy-start(bf16[256,512]{1,0:T(8,128)(2,1)S(1)} %collective-permute-done.13.refs_15_) | copy-start | bytes 786436
  44.6 5.4 %copy-start.11 = (bf16[256,512]{1,0:T(8,128)(2,1)}, bf16[256,512]{1,0:T(8,128)(2,1)S(1)}, u32[]{:S(2)}) copy-start(bf16[256,512]{1,0:T(8,128)(2,1)S(1)} %collective-permute-done.14.refs_16_) | copy-start | bytes 786436
  49.5 1.4 %copy-start.13 = (bf16[256,512]{1,0:T(8,128)(2,1)}, bf16[256,512]{1,0:T(8,128)(2,1)S(1)}, u32[]{:S(2)}) copy-start(bf16[256,512]{1,0:T(8,128)(2,1)S(1)} %collective-permute-done.12.refs_14_) | copy-start | bytes 786436
  49.5 2.1 %copy-start.3 = (bf16[128,4096]{1,0:T(8,128)(2,1)}, bf16[128,4096]{1,0:T(8,128)(2,1)S(1)}, u32[]{:S(2)}) copy-start(bf16[128,4096]{1,0:T(8,128)(2,1)S(1)} %collective-permute-done.10.refs_2_.refs_1_) | copy-start | bytes 3145732
  49.5 8.2 %collective-permute-start.16 = (bf16[256,512]{1,0:T(8,128)(2,1)}, bf16[256,512]{1,0:T(8,128)(2,1)S(1)}, u32[]{:S(2)}, u32[]{:S(2)}) collective-permute-start(bf16[256,512]{1,0:T(8,128)(2,1)} %collective-permute-done.6.refs_9_), channel_id=1, source_target_pairs={{0,2},{1,3},{2,0},{3,1},{4,6},{5,7},{6,4},{7,5},{8,10},{9,11},{10,... | collective-permute-start | bytes 786440 | tf_op jit(solution)/shard_map/ppermute | solution.py:92
  50.1 7.6 %collective-permute-start.17 = (bf16[256,512]{1,0:T(8,128)(2,1)}, bf16[256,512]{1,0:T(8,128)(2,1)S(1)}, u32[]{:S(2)}, u32[]{:S(2)}) collective-permute-start(bf16[256,512]{1,0:T(8,128)(2,1)} %collective-permute-done.11.refs_13_), channel_id=1, source_target_pairs={{0,4},{1,5},{2,6},{3,7},{4,0},{5,1},{6,2},{7,3},{8,12},{9,13},{10,... | collective-permute-start | bytes 786440 | tf_op jit(solution)/shard_map/ppermute | solution.py:92
  50.9 6.8 %collective-permute-start.15 = (bf16[144,512]{1,0:T(8,128)(2,1)}, bf16[144,512]{1,0:T(8,128)(2,1)S(1)}, u32[]{:S(2)}, u32[]{:S(2)}) collective-permute-start(bf16[144,512]{1,0:T(8,128)(2,1)} %get-tuple-element.87), channel_id=1, source_target_pairs={{0,1},{1,0},{2,3},{3,2},{4,5},{5,4},{6,7},{7,6},{8,9},{9,8},{10,11... | collective-permute-start | bytes 442376 | tf_op jit(solution)/shard_map/ppermute | solution.py:92
  57.7 1.4 %copy-start.14 = (bf16[144,512]{1,0:T(8,128)(2,1)}, bf16[144,512]{1,0:T(8,128)(2,1)S(1)}, u32[]{:S(2)}) copy-start(bf16[144,512]{1,0:T(8,128)(2,1)S(1)} %collective-permute-done.15.mate_cot_ref) | copy-start | bytes 442372
  57.7 0.7 copy-start.10
  57.7 0.8 copy-start.12
  58.5 20.2 %collective-permute-start.20 = (bf16[4,128,1024]{2,1,0:T(8,128)(2,1)S(1)}, bf16[4,128,1024]{2,1,0:T(8,128)(2,1)S(1)}, u32[]{:S(2)}, u32[]{:S(2)}) collective-permute-start(bf16[4,128,1024]{2,1,0:T(8,128)(2,1)S(1)} %all-to-all-done.own_ref), channel_id=1, source_target_pairs={{0,1},{1,0},{2,3},{3,2},{4,5},{5,4},{6,7},{7,6},{8,9},{9,8},{10,11... | collective-permute-start | bytes 3145736 | tf_op jit(solution)/shard_map/ppermute | solution.py:92
  62.9 15.8 %collective-permute-start.19 = (bf16[272,512]{1,0:T(8,128)(2,1)}, bf16[272,512]{1,0:T(8,128)(2,1)S(1)}, u32[]{:S(2)}, u32[]{:S(2)}) collective-permute-start(bf16[272,512]{1,0:T(8,128)(2,1)} %get-tuple-element.112.refs_0_), channel_id=1, source_target_pairs={{0,16},{1,17},{2,18},{3,19},{4,20},{5,21},{6,22},{7,23},{8,24},{9,... | collective-permute-start | bytes 835592 | tf_op jit(solution)/shard_map/ppermute | solution.py:92
  64.2 14.6 %collective-permute-start.18 = (bf16[272,512]{1,0:T(8,128)(2,1)}, bf16[272,512]{1,0:T(8,128)(2,1)S(1)}, u32[]{:S(2)}, u32[]{:S(2)}) collective-permute-start(bf16[272,512]{1,0:T(8,128)(2,1)} %get-tuple-element.112.refs_0_), channel_id=1, source_target_pairs={{0,8},{1,9},{2,10},{3,11},{4,12},{5,13},{6,14},{7,15},{8,0},{9,1},... | collective-permute-start | bytes 835592 | tf_op jit(solution)/shard_map/ppermute | solution.py:92
  78.8 7.6 %collective-permute-start.21 = (bf16[272,512]{1,0:T(8,128)(2,1)S(1)}, bf16[272,512]{1,0:T(8,128)(2,1)S(1)}, u32[]{:S(2)}, u32[]{:S(2)}) collective-permute-start(bf16[272,512]{1,0:T(8,128)(2,1)S(1)} %collective-permute-done.19.refs_2_), channel_id=1, source_target_pairs={{0,8},{1,9},{2,10},{3,11},{4,12},{5,13},{6,14},{7,15},{8,0},{9,1},... | collective-permute-start | bytes 835592 | tf_op jit(solution)/shard_map/ppermute | solution.py:92
  86.3 17.7 %collective-permute-start.22 = (bf16[3584,512]{1,0:T(8,128)(2,1)}, bf16[3584,512]{1,0:T(8,128)(2,1)}, u32[]{:S(2)}, u32[]{:S(2)}) collective-permute-start(bf16[3584,512]{1,0:T(8,128)(2,1)} %get-tuple-element.119.refs_0_), channel_id=1, source_target_pairs={{0,1},{1,0},{2,3},{3,2},{4,5},{5,4},{6,7},{7,6},{8,9},{9,8},{10,11... | collective-permute-start | bytes 11010056 | tf_op jit(solution)/shard_map/ppermute | solution.py:92
  86.3 17.7 %collective-permute-start.23 = (bf16[512,512]{1,0:T(8,128)(2,1)}, bf16[512,512]{1,0:T(8,128)(2,1)}, u32[]{:S(2)}, u32[]{:S(2)}) collective-permute-start(bf16[512,512]{1,0:T(8,128)(2,1)} %get-tuple-element.120.refs_2_), channel_id=1, source_target_pairs={{0,1},{1,0},{2,3},{3,2},{4,5},{5,4},{6,7},{7,6},{8,9},{9,8},{10,11... | collective-permute-start | bytes 1572872 | tf_op jit(solution)/shard_map/ppermute | solution.py:92
  86.8 1.0 copy-start
  89.6 14.4 %all-to-all-start.1 = ((bf16[8,64,512]{2,1,0:T(8,128)(2,1)}), bf16[8,64,512]{2,1,0:T(8,128)(2,1)}, u32[]{:S(2)}, u32[]{:S(2)}) async-start(bf16[8,64,512]{2,1,0:T(8,128)(2,1)} %select.28), calls=%async_computation.1 | async-start | bytes 1048576 | tf_op jit(solution)/shard_map/all_to_all | solution.py:521
  93.8 1.0 copy-start.1
  97.6 13.7 %collective-permute-start.24 = (bf16[256,512]{1,0:T(8,128)(2,1)}, bf16[256,512]{1,0:T(8,128)(2,1)S(1)}, u32[]{:S(2)}, u32[]{:S(2)}) collective-permute-start(bf16[256,512]{1,0:T(8,128)(2,1)} %get-tuple-element.125), channel_id=1, source_target_pairs={{0,2},{1,3},{2,0},{3,1},{4,6},{5,7},{6,4},{7,5},{8,10},{9,11},{10,... | collective-permute-start | bytes 786440 | tf_op jit(solution)/shard_map/ppermute | solution.py:92
  99.5 11.7 %collective-permute-start.25 = (bf16[256,512]{1,0:T(8,128)(2,1)S(1)}, bf16[256,512]{1,0:T(8,128)(2,1)S(1)}, u32[]{:S(2)}, u32[]{:S(2)}) collective-permute-start(bf16[256,512]{1,0:T(8,128)(2,1)S(1)} %get-tuple-element.126), channel_id=1, source_target_pairs={{0,4},{1,5},{2,6},{3,7},{4,0},{5,1},{6,2},{7,3},{8,12},{9,13},{10,... | collective-permute-start | bytes 786440 | tf_op jit(solution)/shard_map/ppermute | solution.py:92
  101.0 13.6 %collective-permute-start.26 = (bf16[256,512]{1,0:T(8,128)(2,1)S(1)}, bf16[256,512]{1,0:T(8,128)(2,1)S(1)}, u32[]{:S(2)}, u32[]{:S(2)}) collective-permute-start(bf16[256,512]{1,0:T(8,128)(2,1)S(1)} %get-tuple-element.127), channel_id=1, source_target_pairs={{0,6},{1,7},{2,4},{3,5},{4,2},{5,3},{6,0},{7,1},{8,14},{9,15},{10,... | collective-permute-start | bytes 786440 | tf_op jit(solution)/shard_map/ppermute | solution.py:92
  114.8 1.6 %collective-permute-start.27 = (f32[128,512]{1,0:T(8,128)S(1)}, f32[128,512]{1,0:T(8,128)S(1)}, u32[]{:S(2)}, u32[]{:S(2)}) collective-permute-start(f32[128,512]{1,0:T(8,128)S(1)} %get-tuple-element.129), channel_id=1, source_target_pairs={{0,1},{1,0},{2,3},{3,2},{4,5},{5,4},{6,7},{7,6},{8,9},{9,8},{10,11... | collective-permute-start | bytes 786440 | tf_op jit(solution)/shard_map/ppermute | solution.py:92

commit v20 on v19

--- a/solution.py
+++ b/solution.py
@@ -494,10 +494,6 @@
         (swap(delta, near), swap(delta, far), mate_features)
     )
     deltas = [delta, delta_near, delta_far, swap(delta_far, near)]
-    first_weight, last_weight, *deltas[1:] = lax.optimization_barrier(
-        (first_weight, last_weight, *deltas[1:])
-    )
-    mate_first, mate_last = swap(first_weight, CORE), swap(last_weight, CORE)
     count = levels * 2 * per_peer
     def select(begin, before, deltas, name):
         return pl.pallas_call(
@@ -517,6 +513,30 @@
 
     there = [delta, delta_near, delta_far]
     selected = select(0, [], there, "first_select")
+    shard = width_model // size
+    mine_terms = jax.ShapeDtypeStruct((wide // 4, half_cols), jnp.float32)
+    sent_terms = jax.ShapeDtypeStruct(mine_terms.shape, jnp.bfloat16)
+    all_terms = jax.ShapeDtypeStruct((wide, half_cols), jnp.float32)
+
+    def room(chips):
+        return [
+            pltpu.VMEM((chips * 2 * rows, wide), jnp.bfloat16),
+            pltpu.VMEM((chips * 2 * rows, half_cols), jnp.bfloat16),
+        ]
+
+    begun_terms = pl.pallas_call(
+        first_terms_kernel,
+        out_shape=all_terms,
+        in_specs=[SCALAR] + anywhere(5),
+        out_specs=vmem(1)[0],
+        scratch_shapes=room(3) + [pltpu.SemaphoreType.DMA((9,))],
+        compiler_params=grant(16),
+        name="first_terms",
+    )(me_scalar, own_features, mate_features, *there)
+    first_weight, last_weight, selected, begun_terms, *deltas[1:] = lax.optimization_barrier(
+        (first_weight, last_weight, selected, begun_terms, *deltas[1:])
+    )
+    mate_first, mate_last = swap(first_weight, CORE), swap(last_weight, CORE)
     selected = select(3, [selected], deltas[3:], "select")
     got = lax.all_to_all(
         selected,
@@ -526,27 +546,6 @@
         axis_index_groups=[[z * PLANE + p for p in range(PLANE)] for z in range(levels)],
         tiled=True,
     ).reshape(PLANE // 2, 2, count, half_cols)
-
-    shard = width_model // size
-    mine_terms = jax.ShapeDtypeStruct((wide // 4, half_cols), jnp.float32)
-    sent_terms = jax.ShapeDtypeStruct(mine_terms.shape, jnp.bfloat16)
-    all_terms = jax.ShapeDtypeStruct((wide, half_cols), jnp.float32)
-
-    def room(chips):
-        return [
-            pltpu.VMEM((chips * 2 * rows, wide), jnp.bfloat16),
-            pltpu.VMEM((chips * 2 * rows, half_cols), jnp.bfloat16),
-        ]
-
-    begun_terms = pl.pallas_call(
-        first_terms_kernel,
-        out_shape=all_terms,
-        in_specs=[SCALAR] + anywhere(5),
-        out_specs=vmem(1)[0],
-        scratch_shapes=room(3) + [pltpu.SemaphoreType.DMA((9,))],
-        compiler_params=grant(16),
-        name="first_terms",
-    )(me_scalar, own_features, mate_features, *there)
     own_part, *parts = pl.pallas_call(
         functools.partial(weight_grad_kernel, 3),
         out_shape=(mine_terms, *[sent_terms] * 3),

time: 118 us -> 117 us (level)
  waiting for transfers between devices: 46 us -> 40.7 us
  local copies, waits for them, and re-layouts: 5.77 us -> 10.7 us
    ppermute x28, waiting for transfers between devices: 43.1 us -> 37.8 us  [swap(): return lax.ppermute(value, 'dp', [(i, i ^ mask) for i in range(size)])]
    unnamed x36 -> x48, local copies, waits for them, and re-layouts: 2.79 us -> 7.73 us
  transfers between devices with their start and end apart: 30 -> 30, of which waited for: 13 -> 13; matrix products, arithmetic and copies ran while one was open for 5% -> 5% of each run, Pallas kernels for 19% -> 18%
where the time goes in v20:
time: 117 us; the launch traced here: 116 us
  waiting for transfers between devices  40.7 us (35%)
  starting transfers between devices  38.4 us (33%)
  Pallas kernels  22.1 us (19%)
  local copies, waits for them, and re-layouts  10.7 us (9%)
  other arithmetic  3.49 us (3%)
    ppermute x28, waiting for transfers between devices, swap(): return lax.ppermute(value, 'dp', [(i, i ^ mask) for i in range(size)])  37.8 us
    ppermute x28, starting transfers between devices, swap(): return lax.ppermute(value, 'dp', [(i, i ^ mask) for i in range(size)])  29.6 us
    pallas_call x2, Pallas kernels, project(): pl.pallas_call(kernel, out_shape=(*results, jax.ShapeDtypeStruct((count *...  9.89 us
    unnamed x48, local copies, waits for them, and re-layouts  7.73 us
    pallas_call x1, Pallas kernels, per_device_paired(): pl.pallas_call(row_grad_kernel, out_shape=jax.ShapeDtypeStruct((receive,...  7.31 us
    all_to_all x1, starting transfers between devices, per_device_paired(): lax.all_to_all(by_level, 'dp', split_axis=0, concat_axis=0, axis_index_gr...  4.65 us
    all_to_all x1, starting transfers between devices, per_device_paired(): lax.all_to_all(selected, 'dp', split_axis=0, concat_axis=0, axis_index_gr...  4.15 us
    all_to_all x1, waiting for transfers between devices, per_device_paired(): lax.all_to_all(selected, 'dp', split_axis=0, concat_axis=0, axis_index_gr...  2.95 us
  transfers between devices with their start and end apart: 30, of which 13 were waited for; matrix products, arithmetic and copies ran while one was open for 5% of the time, Pallas kernels for 18%

profile of v20, /device:TPU:0, one launch (start us, length us, event | category | flops | bytes accessed | tf_op | source)
XLA Modules:
  0.0 116.4 jit_solution(18134671087142512681)
XLA Ops:
  1.2 1.0 fusion.11
  2.7 4.0 %collective-permute-start.4 = (bf16[256,512]{1,0:T(8,128)(2,1)S(1)}, bf16[256,512]{1,0:T(8,128)(2,1)S(1)}, u32[]{:S(2)}, u32[]{:S(2)}) collective-permute-start(bf16[256,512]{1,0:T(8,128)(2,1)S(1)} %maximum_select_fusion.refs_3_), channel_id=1, source_target_pairs={{0,16},{1,17},{2,18},{3,19},{4,20},{5,21},{6,22},{7,23},{8,24},{9,... | collective-permute-start | bytes 786440 | tf_op jit(solution)/shard_map/ppermute | solution.py:92
  6.7 1.6 %collective-permute-start.3 = (bf16[256,512]{1,0:T(8,128)(2,1)S(1)}, bf16[256,512]{1,0:T(8,128)(2,1)S(1)}, u32[]{:S(2)}, u32[]{:S(2)}) collective-permute-start(bf16[256,512]{1,0:T(8,128)(2,1)S(1)} %maximum_select_fusion.refs_3_), channel_id=1, source_target_pairs={{0,8},{1,9},{2,10},{3,11},{4,12},{5,13},{6,14},{7,15},{8,0},{9,1},... | collective-permute-start | bytes 786440 | tf_op jit(solution)/shard_map/ppermute | solution.py:92
  8.3 1.5 %collective-permute-start.2 = (bf16[256,512]{1,0:T(8,128)(2,1)S(1)}, bf16[256,512]{1,0:T(8,128)(2,1)S(1)}, u32[]{:S(2)}, u32[]{:S(2)}) collective-permute-start(bf16[256,512]{1,0:T(8,128)(2,1)S(1)} %maximum_select_fusion.refs_3_), channel_id=1, source_target_pairs={{0,2},{1,3},{2,0},{3,1},{4,6},{5,7},{6,4},{7,5},{8,10},{9,11},{10,... | collective-permute-start | bytes 786440 | tf_op jit(solution)/shard_map/ppermute | solution.py:92
  9.8 1.5 %collective-permute-start.1 = (bf16[256,512]{1,0:T(8,128)(2,1)S(1)}, bf16[256,512]{1,0:T(8,128)(2,1)S(1)}, u32[]{:S(2)}, u32[]{:S(2)}) collective-permute-start(bf16[256,512]{1,0:T(8,128)(2,1)S(1)} %maximum_select_fusion.refs_3_), channel_id=1, source_target_pairs={{0,4},{1,5},{2,6},{3,7},{4,0},{5,1},{6,2},{7,3},{8,12},{9,13},{10,... | collective-permute-start | bytes 786440 | tf_op jit(solution)/shard_map/ppermute | solution.py:92
  11.3 1.3 %slice_bitcast_fusion.3 = (bf16[1,128,1024]{2,1,0:T(8,128)(2,1)S(1)}, bf16[1,128,1024]{2,1,0:T(8,128)(2,1)S(1)}, bf16[1,128,1024]{2,1,0:T(8,128)(2,1)S(1)}, bf16[1,128,1024]{2,1,0:T(8,128)(2,1)S(1)}) fusion(bf16[128,4096]{1,0:T(8,128)(2,1)} %refs_0_), kind=kLoop, calls=%fused_computation.6 | loop fusion | bytes 2097152 | tf_op jit(solution)/shard_map/stack | solution.py:381
  12.6 1.1 pad_maximum_fusion
  13.9 5.8 %collective-permute-done.4.refs_7_ = bf16[256,512]{1,0:T(8,128)(2,1)S(1)} collective-permute-done((bf16[256,512]{1,0:T(8,128)(2,1)S(1)}, bf16[256,512]{1,0:T(8,128)(2,1)S(1)}, u32[]{:S(2)}, u32[]{:S(2)}) %collective-permute-start.4) | collective-permute-done | bytes 262176 | tf_op jit(solution)/shard_map/ppermute | solution.py:92
  19.7 2.3 %collective-permute-start.6 = (bf16[256,512]{1,0:T(8,128)(2,1)S(1)}, bf16[256,512]{1,0:T(8,128)(2,1)}, u32[]{:S(2)}, u32[]{:S(2)}) collective-permute-start(bf16[256,512]{1,0:T(8,128)(2,1)S(1)} %collective-permute-done.3.refs_6_), channel_id=1, source_target_pairs={{0,4},{1,5},{2,6},{3,7},{4,0},{5,1},{6,2},{7,3},{8,12},{9,13},{10,... | collective-permute-start | bytes 786440 | tf_op jit(solution)/shard_map/ppermute | solution.py:92
  22.0 1.5 %collective-permute-start.5 = (bf16[256,512]{1,0:T(8,128)(2,1)S(1)}, bf16[256,512]{1,0:T(8,128)(2,1)}, u32[]{:S(2)}, u32[]{:S(2)}) collective-permute-start(bf16[256,512]{1,0:T(8,128)(2,1)S(1)} %collective-permute-done.3.refs_6_), channel_id=1, source_target_pairs={{0,2},{1,3},{2,0},{3,1},{4,6},{5,7},{6,4},{7,5},{8,10},{9,11},{10,... | collective-permute-start | bytes 786440 | tf_op jit(solution)/shard_map/ppermute | solution.py:92
  24.5 4.7 %all-to-all-start = ((bf16[4,128,1024]{2,1,0:T(8,128)(2,1)}), bf16[4,128,1024]{2,1,0:T(8,128)(2,1)S(1)}, u32[]{:S(2)}, u32[]{:S(2)}) async-start(bf16[4,128,1024]{2,1,0:T(8,128)(2,1)} %pad_maximum_fusion), calls=%async_computation | async-start | bytes 2097152 | tf_op jit(solution)/shard_map/all_to_all | solution.py:386
  29.3 1.1 compare_select_fusion
  30.4 0.8 pad_maximum_fusion.1
  31.2 1.4 %collective-permute-done.8.refs_11_ = bf16[256,512]{1,0:T(8,128)(2,1)} collective-permute-done((bf16[256,512]{1,0:T(8,128)(2,1)S(1)}, bf16[256,512]{1,0:T(8,128)(2,1)}, u32[]{:S(2)}, u32[]{:S(2)}) %collective-permute-start.8) | collective-permute-done | bytes 262176 | tf_op jit(solution)/shard_map/ppermute | solution.py:92
  32.6 1.0 collective-permute-done.7.refs_10_
  33.7 1.6 %collective-permute-start.13 = (bf16[256,512]{1,0:T(8,128)(2,1)S(1)}, bf16[256,512]{1,0:T(8,128)(2,1)S(1)}, u32[]{:S(2)}, u32[]{:S(2)}) collective-permute-start(bf16[256,512]{1,0:T(8,128)(2,1)S(1)} %collective-permute-done.1.refs_4_), channel_id=1, source_target_pairs={{0,2},{1,3},{2,0},{3,1},{4,6},{5,7},{6,4},{7,5},{8,10},{9,11},{10,... | collective-permute-start | bytes 786440 | tf_op jit(solution)/shard_map/ppermute | solution.py:92
  35.8 1.6 %collective-permute-start.12 = (bf16[256,512]{1,0:T(8,128)(2,1)}, bf16[256,512]{1,0:T(8,128)(2,1)S(1)}, u32[]{:S(2)}, u32[]{:S(2)}) collective-permute-start(bf16[256,512]{1,0:T(8,128)(2,1)} %collective-permute-done.9.refs_12_), channel_id=1, source_target_pairs={{0,4},{1,5},{2,6},{3,7},{4,0},{5,1},{6,2},{7,3},{8,12},{9,13},{10,... | collective-permute-start | bytes 786440 | tf_op jit(solution)/shard_map/ppermute | solution.py:92
  37.8 5.1 %collective-permute-done.13.refs_15_ = bf16[256,512]{1,0:T(8,128)(2,1)S(1)} collective-permute-done((bf16[256,512]{1,0:T(8,128)(2,1)S(1)}, bf16[256,512]{1,0:T(8,128)(2,1)S(1)}, u32[]{:S(2)}, u32[]{:S(2)}) %collective-permute-start.13) | collective-permute-done | bytes 262176 | tf_op jit(solution)/shard_map/ppermute | solution.py:92
  42.9 1.8 %collective-permute-done.14.refs_16_ = bf16[256,512]{1,0:T(8,128)(2,1)S(1)} collective-permute-done((bf16[256,512]{1,0:T(8,128)(2,1)}, bf16[256,512]{1,0:T(8,128)(2,1)S(1)}, u32[]{:S(2)}, u32[]{:S(2)}) %collective-permute-start.14) | collective-permute-done | bytes 262176 | tf_op jit(solution)/shard_map/ppermute | solution.py:92
  44.6 4.8 %collective-permute-done.12.refs_14_ = bf16[256,512]{1,0:T(8,128)(2,1)S(1)} collective-permute-done((bf16[256,512]{1,0:T(8,128)(2,1)}, bf16[256,512]{1,0:T(8,128)(2,1)S(1)}, u32[]{:S(2)}, u32[]{:S(2)}) %collective-permute-start.12) | collective-permute-done | bytes 262176 | tf_op jit(solution)/shard_map/ppermute | solution.py:92
  49.5 0.6 collective-permute-start.16
  50.1 0.8 collective-permute-start.17
  50.9 0.6 stack.87.refs_0_.chips_ref
  51.5 6.1 %project.1 = (bf16[3584,512]{1,0:T(8,128)(2,1)}, f32[2,128,512]{2,1,0:T(8,128)}) custom-call(s32[16]{0:T(128)} %stack.87.refs_0_.chips_ref, bf16[128,4096]{1,0:T(8,128)(2,1)} %refs_0_, bf16[128,4096]{1,0:T(8,128)(2,1)} %copy-done.9, bf16[256,512]{1,0:T(8,128)(2,1)} %copy-done.10, bf16[256,512]{1,0:T(8,128)(2,1)} %copy-done.14, bf16[256,512]{1,0:T(8,128)(2,1)} %copy-done.13, ...), custom_call_target="tpu_custom_call" | custom-call | tf_op jit(solution)/shard_map/project/pallas_call | solution.py:436
  57.7 0.7 copy-done.16
  59.0 3.8 %delta.1 = (bf16[272,512]{1,0:T(8,128)(2,1)}, bf16[512,512]{1,0:T(8,128)(2,1)}) custom-call(s32[16]{0:T(128)} %stack.87.refs_0_.chips_ref, s32[1]{0:T(128)} %bitcast.16.me_ref, bf16[144,512]{1,0:T(8,128)(2,1)} %get-tuple-element.110.own_cot_ref, bf16[144,512]{1,0:T(8,128)(2,1)} %copy-done.20, bf16[128,4096]{1,0:T(8,128)(2,1)} %refs_0_, ...), custom_call_target="tpu_custom_call" | custom-call | tf_op jit(solution)/shard_map/delta/pallas_call | solution.py:436
  62.8 1.4 %collective-permute-start.19 = (bf16[272,512]{1,0:T(8,128)(2,1)}, bf16[272,512]{1,0:T(8,128)(2,1)S(1)}, u32[]{:S(2)}, u32[]{:S(2)}) collective-permute-start(bf16[272,512]{1,0:T(8,128)(2,1)} %get-tuple-element.116.refs_0_), channel_id=1, source_target_pairs={{0,16},{1,17},{2,18},{3,19},{4,20},{5,21},{6,22},{7,23},{8,24},{9,... | collective-permute-start | bytes 835592 | tf_op jit(solution)/shard_map/ppermute | solution.py:92
  64.2 3.8 %collective-permute-start.18 = (bf16[272,512]{1,0:T(8,128)(2,1)}, bf16[272,512]{1,0:T(8,128)(2,1)S(1)}, u32[]{:S(2)}, u32[]{:S(2)}) collective-permute-start(bf16[272,512]{1,0:T(8,128)(2,1)} %get-tuple-element.116.refs_0_), channel_id=1, source_target_pairs={{0,8},{1,9},{2,10},{3,11},{4,12},{5,13},{6,14},{7,15},{8,0},{9,1},... | collective-permute-start | bytes 835592 | tf_op jit(solution)/shard_map/ppermute | solution.py:92
  68.0 10.6 %collective-permute-done.19.refs_2_ = bf16[272,512]{1,0:T(8,128)(2,1)S(1)} collective-permute-done((bf16[272,512]{1,0:T(8,128)(2,1)}, bf16[272,512]{1,0:T(8,128)(2,1)S(1)}, u32[]{:S(2)}, u32[]{:S(2)}) %collective-permute-start.19) | collective-permute-done | bytes 278560 | tf_op jit(solution)/shard_map/ppermute | solution.py:92
  78.7 1.0 copy-done
  80.1 1.0 copy-done.4
  81.1 0.7 first_select.1.refs_0_
  81.8 1.2 %copy-done.1 = bf16[4,128,1024]{2,1,0:T(8,128)(2,1)S(1)} copy-done((bf16[4,128,1024]{2,1,0:T(8,128)(2,1)S(1)}, bf16[4,128,1024]{2,1,0:T(8,128)(2,1)}, u32[]{:S(2)}) %copy-start.1) | copy-done | bytes 1048600
  83.0 1.0 copy-done.5
  84.0 1.3 %first_terms.1.begun_ref = f32[1024,512]{1,0:T(8,128)S(1)} custom-call(s32[1]{0:T(128)} %bitcast.16.me_ref, bf16[4,128,1024]{2,1,0:T(8,128)(2,1)S(1)} %all-to-all-done.own_ref, bf16[4,128,1024]{2,1,0:T(8,128)(2,1)S(1)} %copy-done.1, bf16[272,512]{1,0:T(8,128)(2,1)S(1)} %copy-done.5, bf16[272,512]{1,0:T(8,128)(2,1)S(1)} %collective-permute-done.18.refs_1_, ...), custom_call_target="tpu_custom_call" | custom-call | tf_op jit(solution)/shard_map/first_terms/pallas_call | solution.py:527
  85.3 2.0 %collective-permute-done.21.refs_1_.refs_0_ = bf16[272,512]{1,0:T(8,128)(2,1)S(1)} collective-permute-done((bf16[272,512]{1,0:T(8,128)(2,1)S(1)}, bf16[272,512]{1,0:T(8,128)(2,1)S(1)}, u32[]{:S(2)}, u32[]{:S(2)}) %collective-permute-start.21) | collective-permute-done | bytes 278560 | tf_op jit(solution)/shard_map/ppermute | solution.py:92
  88.0 0.8 copy-done.3
  88.8 4.1 %all-to-all-start.1 = ((bf16[8,64,512]{2,1,0:T(8,128)(2,1)}), bf16[8,64,512]{2,1,0:T(8,128)(2,1)}, u32[]{:S(2)}, u32[]{:S(2)}) async-start(bf16[8,64,512]{2,1,0:T(8,128)(2,1)} %copy-done.3), calls=%async_computation.1 | async-start | bytes 1048576 | tf_op jit(solution)/shard_map/all_to_all | solution.py:541
  93.0 1.2 %copy-done.2 = bf16[4,128,1024]{2,1,0:T(8,128)(2,1)S(1)} copy-done((bf16[4,128,1024]{2,1,0:T(8,128)(2,1)S(1)}, bf16[4,128,1024]{2,1,0:T(8,128)(2,1)}, u32[]{:S(2)}) %copy-start.2) | copy-done | bytes 1048600
  94.2 1.7 %weight_grad.1 = (f32[256,512]{1,0:T(8,128)S(1)}, bf16[256,512]{1,0:T(8,128)(2,1)}, bf16[256,512]{1,0:T(8,128)(2,1)}, bf16[256,512]{1,0:T(8,128)(2,1)}) custom-call(s32[1]{0:T(128)} %bitcast.16.me_ref, bf16[4,128,1024]{2,1,0:T(8,128)(2,1)S(1)} %all-to-all-done.own_ref, bf16[4,128,1024]{2,1,0:T(8,128)(2,1)S(1)} %copy-done.2, ...), custom_call_target="tpu_custom_call" | custom-call | tf_op jit(solution)/shard_map/weight_grad/pallas_call | solution.py:549
  96.0 0.8 copy-done.6
  96.7 1.9 %collective-permute-start.24 = (bf16[256,512]{1,0:T(8,128)(2,1)}, bf16[256,512]{1,0:T(8,128)(2,1)S(1)}, u32[]{:S(2)}, u32[]{:S(2)}) collective-permute-start(bf16[256,512]{1,0:T(8,128)(2,1)} %get-tuple-element.129), channel_id=1, source_target_pairs={{0,2},{1,3},{2,0},{3,1},{4,6},{5,7},{6,4},{7,5},{8,10},{9,11},{10,... | collective-permute-start | bytes 786440 | tf_op jit(solution)/shard_map/ppermute | solution.py:92
  98.6 1.5 %collective-permute-start.25 = (bf16[256,512]{1,0:T(8,128)(2,1)}, bf16[256,512]{1,0:T(8,128)(2,1)S(1)}, u32[]{:S(2)}, u32[]{:S(2)}) collective-permute-start(bf16[256,512]{1,0:T(8,128)(2,1)} %get-tuple-element.130), channel_id=1, source_target_pairs={{0,4},{1,5},{2,6},{3,7},{4,0},{5,1},{6,2},{7,3},{8,12},{9,13},{10,... | collective-permute-start | bytes 786440 | tf_op jit(solution)/shard_map/ppermute | solution.py:92
  100.2 3.0 %all-to-all-done.1 = bf16[8,64,512]{2,1,0:T(8,128)(2,1)} async-done(((bf16[8,64,512]{2,1,0:T(8,128)(2,1)}), bf16[8,64,512]{2,1,0:T(8,128)(2,1)}, u32[]{:S(2)}, u32[]{:S(2)}) %all-to-all-start.1) | async-done | bytes 524320 | tf_op jit(solution)/shard_map/all_to_all | solution.py:541
  103.2 7.3 %row_grad.1 = bf16[256,4096]{1,0:T(8,128)(2,1)} custom-call(s32[16]{0:T(128)} %stack.87.refs_0_.chips_ref, s32[1]{0:T(128)} %bitcast.16.me_ref, bf16[4,2,64,512]{3,2,1,0:T(8,128)(2,1)} %bitcast.26.got_ref, bf16[3584,512]{1,0:T(8,128)(2,1)} %get-tuple-element.123.refs_0_, bf16[3584,512]{1,0:T(8,128)(2,1)} %collective-permute-done.22.refs_1_, ...), custom_call_target="tpu_custom_call" | custom-call | tf_op jit(solution)/shard_map/row_grad/pallas_call | solution.py:561
  110.5 3.3 %collective-permute-done.26.refs_2_ = bf16[256,512]{1,0:T(8,128)(2,1)S(1)} collective-permute-done((bf16[256,512]{1,0:T(8,128)(2,1)}, bf16[256,512]{1,0:T(8,128)(2,1)S(1)}, u32[]{:S(2)}, u32[]{:S(2)}) %collective-permute-start.26) | collective-permute-done | bytes 262176 | tf_op jit(solution)/shard_map/ppermute | solution.py:92
  114.0 1.5 %collective-permute-done.27.mate_ref = f32[128,512]{1,0:T(8,128)S(1)} collective-permute-done((f32[128,512]{1,0:T(8,128)S(1)}, f32[128,512]{1,0:T(8,128)S(1)}, u32[]{:S(2)}, u32[]{:S(2)}) %collective-permute-start.27) | collective-permute-done | bytes 262176 | tf_op jit(solution)/shard_map/ppermute | solution.py:92
  115.6 0.8 join.1
  (87 shorter events, 5.8 us)
Async XLA Ops:
  0.6 23.5 %copy-start.21 = (s32[1,4]{1,0:T(1,128)S(1)}, s32[1,4]{1,0:T(1,128)}, u32[]{:S(2)}) copy-start(s32[1,4]{1,0:T(1,128)} %param.9) | copy-start | bytes 52
  0.6 23.8 %copy-start.22 = (s32[128,1]{0,1:T(1,128)S(1)}, s32[128,1]{0,1:T(1,128)}, u32[]{:S(2)}) copy-start(s32[128,1]{0,1:T(1,128)} %param.8) | copy-start | bytes 1540
  0.7 1.9 %collective-permute-start = (bf16[128,1024]{1,0:T(8,128)(2,1)}, bf16[128,1024]{1,0:T(8,128)(2,1)S(1)}, u32[]{:S(2)}, u32[]{:S(2)}) collective-permute-start(bf16[128,1024]{1,0:T(8,128)(2,1)} %param.11), channel_id=1, source_target_pairs={{0,1},{1,0},{2,3},{3,2},{4,5},{5,4},{6,7},{7,6},{8,9},{9,8},{10,11... | collective-permute-start | bytes 786440 | tf_op jit(solution)/shard_map/ppermute | solution.py:92
  2.6 26.6 %copy-start.23 = (s32[4]{0:T(128)S(1)}, s32[4]{0:T(128)}, u32[]{:S(2)}) copy-start(s32[4]{0:T(128)} %param.10) | copy-start | bytes 52
  2.6 27.8 %copy-start.10 = (bf16[256,512]{1,0:T(8,128)(2,1)}, bf16[256,512]{1,0:T(8,128)(2,1)S(1)}, u32[]{:S(2)}) copy-start(bf16[256,512]{1,0:T(8,128)(2,1)S(1)} %maximum_select_fusion.refs_3_) | copy-start | bytes 786436
  2.7 31.0 %copy-start.8 = (bf16[128,4096]{1,0:T(8,128)(2,1)S(1)}, bf16[128,4096]{1,0:T(8,128)(2,1)}, u32[]{:S(2)}) copy-start(bf16[128,4096]{1,0:T(8,128)(2,1)} %refs_0_) | copy-start | bytes 3145732
  2.7 17.0 %collective-permute-start.4 = (bf16[256,512]{1,0:T(8,128)(2,1)S(1)}, bf16[256,512]{1,0:T(8,128)(2,1)S(1)}, u32[]{:S(2)}, u32[]{:S(2)}) collective-permute-start(bf16[256,512]{1,0:T(8,128)(2,1)S(1)} %maximum_select_fusion.refs_3_), channel_id=1, source_target_pairs={{0,16},{1,17},{2,18},{3,19},{4,20},{5,21},{6,22},{7,23},{8,24},{9,... | collective-permute-start | bytes 786440 | tf_op jit(solution)/shard_map/ppermute | solution.py:92
  6.7 13.0 %collective-permute-start.3 = (bf16[256,512]{1,0:T(8,128)(2,1)S(1)}, bf16[256,512]{1,0:T(8,128)(2,1)S(1)}, u32[]{:S(2)}, u32[]{:S(2)}) collective-permute-start(bf16[256,512]{1,0:T(8,128)(2,1)S(1)} %maximum_select_fusion.refs_3_), channel_id=1, source_target_pairs={{0,8},{1,9},{2,10},{3,11},{4,12},{5,13},{6,14},{7,15},{8,0},{9,1},... | collective-permute-start | bytes 786440 | tf_op jit(solution)/shard_map/ppermute | solution.py:92
  8.3 11.4 %collective-permute-start.2 = (bf16[256,512]{1,0:T(8,128)(2,1)S(1)}, bf16[256,512]{1,0:T(8,128)(2,1)S(1)}, u32[]{:S(2)}, u32[]{:S(2)}) collective-permute-start(bf16[256,512]{1,0:T(8,128)(2,1)S(1)} %maximum_select_fusion.refs_3_), channel_id=1, source_target_pairs={{0,2},{1,3},{2,0},{3,1},{4,6},{5,7},{6,4},{7,5},{8,10},{9,11},{10,... | collective-permute-start | bytes 786440 | tf_op jit(solution)/shard_map/ppermute | solution.py:92
  9.8 9.9 %collective-permute-start.1 = (bf16[256,512]{1,0:T(8,128)(2,1)S(1)}, bf16[256,512]{1,0:T(8,128)(2,1)S(1)}, u32[]{:S(2)}, u32[]{:S(2)}) collective-permute-start(bf16[256,512]{1,0:T(8,128)(2,1)S(1)} %maximum_select_fusion.refs_3_), channel_id=1, source_target_pairs={{0,4},{1,5},{2,6},{3,7},{4,0},{5,1},{6,2},{7,3},{8,12},{9,13},{10,... | collective-permute-start | bytes 786440 | tf_op jit(solution)/shard_map/ppermute | solution.py:92
  13.7 17.5 %collective-permute-start.9 = (bf16[256,512]{1,0:T(8,128)(2,1)S(1)}, bf16[256,512]{1,0:T(8,128)(2,1)}, u32[]{:S(2)}, u32[]{:S(2)}) collective-permute-start(bf16[256,512]{1,0:T(8,128)(2,1)S(1)} %maximum_select_fusion.refs_3_), channel_id=1, source_target_pairs={{0,24},{1,25},{2,26},{3,27},{4,28},{5,29},{6,30},{7,31},{8,16},{9,... | collective-permute-start | bytes 786440 | tf_op jit(solution)/shard_map/ppermute | solution.py:92
  19.7 13.9 %copy-start.11 = (bf16[256,512]{1,0:T(8,128)(2,1)}, bf16[256,512]{1,0:T(8,128)(2,1)S(1)}, u32[]{:S(2)}) copy-start(bf16[256,512]{1,0:T(8,128)(2,1)S(1)} %collective-permute-done.4.refs_7_) | copy-start | bytes 786436
  19.7 13.9 %copy-start.12 = (bf16[256,512]{1,0:T(8,128)(2,1)}, bf16[256,512]{1,0:T(8,128)(2,1)S(1)}, u32[]{:S(2)}) copy-start(bf16[256,512]{1,0:T(8,128)(2,1)S(1)} %collective-permute-done.3.refs_6_) | copy-start | bytes 786436
  19.7 9.6 %copy-start.13 = (bf16[256,512]{1,0:T(8,128)(2,1)}, bf16[256,512]{1,0:T(8,128)(2,1)S(1)}, u32[]{:S(2)}) copy-start(bf16[256,512]{1,0:T(8,128)(2,1)S(1)} %collective-permute-done.2.refs_5_) | copy-start | bytes 786436
  19.7 31.8 %copy-start.14 = (bf16[256,512]{1,0:T(8,128)(2,1)}, bf16[256,512]{1,0:T(8,128)(2,1)S(1)}, u32[]{:S(2)}) copy-start(bf16[256,512]{1,0:T(8,128)(2,1)S(1)} %collective-permute-done.1.refs_4_) | copy-start | bytes 786436
  19.7 11.5 %collective-permute-start.6 = (bf16[256,512]{1,0:T(8,128)(2,1)S(1)}, bf16[256,512]{1,0:T(8,128)(2,1)}, u32[]{:S(2)}, u32[]{:S(2)}) collective-permute-start(bf16[256,512]{1,0:T(8,128)(2,1)S(1)} %collective-permute-done.3.refs_6_), channel_id=1, source_target_pairs={{0,4},{1,5},{2,6},{3,7},{4,0},{5,1},{6,2},{7,3},{8,12},{9,13},{10,... | collective-permute-start | bytes 786440 | tf_op jit(solution)/shard_map/ppermute | solution.py:92
  22.0 9.2 %collective-permute-start.5 = (bf16[256,512]{1,0:T(8,128)(2,1)S(1)}, bf16[256,512]{1,0:T(8,128)(2,1)}, u32[]{:S(2)}, u32[]{:S(2)}) collective-permute-start(bf16[256,512]{1,0:T(8,128)(2,1)S(1)} %collective-permute-done.3.refs_6_), channel_id=1, source_target_pairs={{0,2},{1,3},{2,0},{3,1},{4,6},{5,7},{6,4},{7,5},{8,10},{9,11},{10,... | collective-permute-start | bytes 786440 | tf_op jit(solution)/shard_map/ppermute | solution.py:92
  23.5 9.1 %collective-permute-start.8 = (bf16[256,512]{1,0:T(8,128)(2,1)S(1)}, bf16[256,512]{1,0:T(8,128)(2,1)}, u32[]{:S(2)}, u32[]{:S(2)}) collective-permute-start(bf16[256,512]{1,0:T(8,128)(2,1)S(1)} %collective-permute-done.4.refs_7_), channel_id=1, source_target_pairs={{0,4},{1,5},{2,6},{3,7},{4,0},{5,1},{6,2},{7,3},{8,12},{9,13},{10,... | collective-permute-start | bytes 786440 | tf_op jit(solution)/shard_map/ppermute | solution.py:92
  24.0 9.6 %collective-permute-start.7 = (bf16[256,512]{1,0:T(8,128)(2,1)S(1)}, bf16[256,512]{1,0:T(8,128)(2,1)}, u32[]{:S(2)}, u32[]{:S(2)}) collective-permute-start(bf16[256,512]{1,0:T(8,128)(2,1)S(1)} %collective-permute-done.4.refs_7_), channel_id=1, source_target_pairs={{0,2},{1,3},{2,0},{3,1},{4,6},{5,7},{6,4},{7,5},{8,10},{9,11},{10,... | collective-permute-start | bytes 786440 | tf_op jit(solution)/shard_map/ppermute | solution.py:92
  24.5 33.1 %all-to-all-start = ((bf16[4,128,1024]{2,1,0:T(8,128)(2,1)}), bf16[4,128,1024]{2,1,0:T(8,128)(2,1)S(1)}, u32[]{:S(2)}, u32[]{:S(2)}) async-start(bf16[4,128,1024]{2,1,0:T(8,128)(2,1)} %pad_maximum_fusion), calls=%async_computation | async-start | bytes 2097152 | tf_op jit(solution)/shard_map/all_to_all | solution.py:386
  33.6 15.8 %collective-permute-start.10 = (bf16[128,4096]{1,0:T(8,128)(2,1)S(1)}, bf16[128,4096]{1,0:T(8,128)(2,1)S(1)}, u32[]{:S(2)}, u32[]{:S(2)}) collective-permute-start(bf16[128,4096]{1,0:T(8,128)(2,1)S(1)} %copy-done.8), channel_id=1, source_target_pairs={{0,1},{1,0},{2,3},{3,2},{4,5},{5,4},{6,7},{7,6},{8,9},{9,8},{10,11... | collective-permute-start | bytes 3145736 | tf_op jit(solution)/shard_map/ppermute | solution.py:92
  33.7 9.2 %collective-permute-start.13 = (bf16[256,512]{1,0:T(8,128)(2,1)S(1)}, bf16[256,512]{1,0:T(8,128)(2,1)S(1)}, u32[]{:S(2)}, u32[]{:S(2)}) collective-permute-start(bf16[256,512]{1,0:T(8,128)(2,1)S(1)} %collective-permute-done.1.refs_4_), channel_id=1, source_target_pairs={{0,2},{1,3},{2,0},{3,1},{4,6},{5,7},{6,4},{7,5},{8,10},{9,11},{10,... | collective-permute-start | bytes 786440 | tf_op jit(solution)/shard_map/ppermute | solution.py:92
  35.3 9.4 %collective-permute-start.14 = (bf16[256,512]{1,0:T(8,128)(2,1)}, bf16[256,512]{1,0:T(8,128)(2,1)S(1)}, u32[]{:S(2)}, u32[]{:S(2)}) collective-permute-start(bf16[256,512]{1,0:T(8,128)(2,1)} %collective-permute-done.7.refs_10_), channel_id=1, source_target_pairs={{0,4},{1,5},{2,6},{3,7},{4,0},{5,1},{6,2},{7,3},{8,12},{9,13},{10,... | collective-permute-start | bytes 786440 | tf_op jit(solution)/shard_map/ppermute | solution.py:92
  35.8 13.7 %collective-permute-start.12 = (bf16[256,512]{1,0:T(8,128)(2,1)}, bf16[256,512]{1,0:T(8,128)(2,1)S(1)}, u32[]{:S(2)}, u32[]{:S(2)}) collective-permute-start(bf16[256,512]{1,0:T(8,128)(2,1)} %collective-permute-done.9.refs_12_), channel_id=1, source_target_pairs={{0,4},{1,5},{2,6},{3,7},{4,0},{5,1},{6,2},{7,3},{8,12},{9,13},{10,... | collective-permute-start | bytes 786440 | tf_op jit(solution)/shard_map/ppermute | solution.py:92
  37.3 12.2 %collective-permute-start.11 = (bf16[256,512]{1,0:T(8,128)(2,1)}, bf16[256,512]{1,0:T(8,128)(2,1)}, u32[]{:S(2)}, u32[]{:S(2)}) collective-permute-start(bf16[256,512]{1,0:T(8,128)(2,1)} %collective-permute-done.9.refs_12_), channel_id=1, source_target_pairs={{0,2},{1,3},{2,0},{3,1},{4,6},{5,7},{6,4},{7,5},{8,10},{9,11},{10,... | collective-permute-start | bytes 786440 | tf_op jit(solution)/shard_map/ppermute | solution.py:92
  42.9 6.6 %copy-start.15 = (bf16[256,512]{1,0:T(8,128)(2,1)}, bf16[256,512]{1,0:T(8,128)(2,1)S(1)}, u32[]{:S(2)}) copy-start(bf16[256,512]{1,0:T(8,128)(2,1)S(1)} %collective-permute-done.13.refs_15_) | copy-start | bytes 786436
  44.6 5.4 %copy-start.17 = (bf16[256,512]{1,0:T(8,128)(2,1)}, bf16[256,512]{1,0:T(8,128)(2,1)S(1)}, u32[]{:S(2)}) copy-start(bf16[256,512]{1,0:T(8,128)(2,1)S(1)} %collective-permute-done.14.refs_16_) | copy-start | bytes 786436
  49.5 1.4 %copy-start.19 = (bf16[256,512]{1,0:T(8,128)(2,1)}, bf16[256,512]{1,0:T(8,128)(2,1)S(1)}, u32[]{:S(2)}) copy-start(bf16[256,512]{1,0:T(8,128)(2,1)S(1)} %collective-permute-done.12.refs_14_) | copy-start | bytes 786436
  49.5 2.0 %copy-start.9 = (bf16[128,4096]{1,0:T(8,128)(2,1)}, bf16[128,4096]{1,0:T(8,128)(2,1)S(1)}, u32[]{:S(2)}) copy-start(bf16[128,4096]{1,0:T(8,128)(2,1)S(1)} %collective-permute-done.10.refs_2_.refs_1_) | copy-start | bytes 3145732
  49.5 8.1 %collective-permute-start.16 = (bf16[256,512]{1,0:T(8,128)(2,1)}, bf16[256,512]{1,0:T(8,128)(2,1)S(1)}, u32[]{:S(2)}, u32[]{:S(2)}) collective-permute-start(bf16[256,512]{1,0:T(8,128)(2,1)} %collective-permute-done.6.refs_9_), channel_id=1, source_target_pairs={{0,2},{1,3},{2,0},{3,1},{4,6},{5,7},{6,4},{7,5},{8,10},{9,11},{10,... | collective-permute-start | bytes 786440 | tf_op jit(solution)/shard_map/ppermute | solution.py:92
  50.1 7.6 %collective-permute-start.17 = (bf16[256,512]{1,0:T(8,128)(2,1)}, bf16[256,512]{1,0:T(8,128)(2,1)S(1)}, u32[]{:S(2)}, u32[]{:S(2)}) collective-permute-start(bf16[256,512]{1,0:T(8,128)(2,1)} %collective-permute-done.11.refs_13_), channel_id=1, source_target_pairs={{0,4},{1,5},{2,6},{3,7},{4,0},{5,1},{6,2},{7,3},{8,12},{9,13},{10,... | collective-permute-start | bytes 786440 | tf_op jit(solution)/shard_map/ppermute | solution.py:92
  50.9 6.7 %collective-permute-start.15 = (bf16[144,512]{1,0:T(8,128)(2,1)}, bf16[144,512]{1,0:T(8,128)(2,1)S(1)}, u32[]{:S(2)}, u32[]{:S(2)}) collective-permute-start(bf16[144,512]{1,0:T(8,128)(2,1)} %get-tuple-element.89), channel_id=1, source_target_pairs={{0,1},{1,0},{2,3},{3,2},{4,5},{5,4},{6,7},{7,6},{8,9},{9,8},{10,11... | collective-permute-start | bytes 442376 | tf_op jit(solution)/shard_map/ppermute | solution.py:92
  57.6 1.4 %copy-start.20 = (bf16[144,512]{1,0:T(8,128)(2,1)}, bf16[144,512]{1,0:T(8,128)(2,1)S(1)}, u32[]{:S(2)}) copy-start(bf16[144,512]{1,0:T(8,128)(2,1)S(1)} %collective-permute-done.15.mate_cot_ref) | copy-start | bytes 442372
  58.5 20.3 %collective-permute-start.20 = (bf16[4,128,1024]{2,1,0:T(8,128)(2,1)S(1)}, bf16[4,128,1024]{2,1,0:T(8,128)(2,1)S(1)}, u32[]{:S(2)}, u32[]{:S(2)}) collective-permute-start(bf16[4,128,1024]{2,1,0:T(8,128)(2,1)S(1)} %all-to-all-done.own_ref), channel_id=1, source_target_pairs={{0,1},{1,0},{2,3},{3,2},{4,5},{5,4},{6,7},{7,6},{8,9},{9,8},{10,11... | collective-permute-start | bytes 3145736 | tf_op jit(solution)/shard_map/ppermute | solution.py:92
  62.8 15.8 %collective-permute-start.19 = (bf16[272,512]{1,0:T(8,128)(2,1)}, bf16[272,512]{1,0:T(8,128)(2,1)S(1)}, u32[]{:S(2)}, u32[]{:S(2)}) collective-permute-start(bf16[272,512]{1,0:T(8,128)(2,1)} %get-tuple-element.116.refs_0_), channel_id=1, source_target_pairs={{0,16},{1,17},{2,18},{3,19},{4,20},{5,21},{6,22},{7,23},{8,24},{9,... | collective-permute-start | bytes 835592 | tf_op jit(solution)/shard_map/ppermute | solution.py:92
  64.2 14.6 %collective-permute-start.18 = (bf16[272,512]{1,0:T(8,128)(2,1)}, bf16[272,512]{1,0:T(8,128)(2,1)S(1)}, u32[]{:S(2)}, u32[]{:S(2)}) collective-permute-start(bf16[272,512]{1,0:T(8,128)(2,1)} %get-tuple-element.116.refs_0_), channel_id=1, source_target_pairs={{0,8},{1,9},{2,10},{3,11},{4,12},{5,13},{6,14},{7,15},{8,0},{9,1},... | collective-permute-start | bytes 835592 | tf_op jit(solution)/shard_map/ppermute | solution.py:92
  78.7 1.0 copy-start
  79.7 7.6 %collective-permute-start.21 = (bf16[272,512]{1,0:T(8,128)(2,1)S(1)}, bf16[272,512]{1,0:T(8,128)(2,1)S(1)}, u32[]{:S(2)}, u32[]{:S(2)}) collective-permute-start(bf16[272,512]{1,0:T(8,128)(2,1)S(1)} %collective-permute-done.19.refs_2_), channel_id=1, source_target_pairs={{0,8},{1,9},{2,10},{3,11},{4,12},{5,13},{6,14},{7,15},{8,0},{9,1},... | collective-permute-start | bytes 835592 | tf_op jit(solution)/shard_map/ppermute | solution.py:92
  81.8 1.2 %copy-start.1 = (bf16[4,128,1024]{2,1,0:T(8,128)(2,1)S(1)}, bf16[4,128,1024]{2,1,0:T(8,128)(2,1)}, u32[]{:S(2)}) copy-start(bf16[4,128,1024]{2,1,0:T(8,128)(2,1)} %copy-done) | copy-start | bytes 3145732
  87.2 16.0 %collective-permute-start.22 = (bf16[3584,512]{1,0:T(8,128)(2,1)}, bf16[3584,512]{1,0:T(8,128)(2,1)}, u32[]{:S(2)}, u32[]{:S(2)}) collective-permute-start(bf16[3584,512]{1,0:T(8,128)(2,1)} %get-tuple-element.123.refs_0_), channel_id=1, source_target_pairs={{0,1},{1,0},{2,3},{3,2},{4,5},{5,4},{6,7},{7,6},{8,9},{9,8},{10,11... | collective-permute-start | bytes 11010056 | tf_op jit(solution)/shard_map/ppermute | solution.py:92
  87.2 16.0 %collective-permute-start.23 = (bf16[512,512]{1,0:T(8,128)(2,1)}, bf16[512,512]{1,0:T(8,128)(2,1)}, u32[]{:S(2)}, u32[]{:S(2)}) collective-permute-start(bf16[512,512]{1,0:T(8,128)(2,1)} %get-tuple-element.124.refs_2_), channel_id=1, source_target_pairs={{0,1},{1,0},{2,3},{3,2},{4,5},{5,4},{6,7},{7,6},{8,9},{9,8},{10,11... | collective-permute-start | bytes 1572872 | tf_op jit(solution)/shard_map/ppermute | solution.py:92
  88.8 14.4 %all-to-all-start.1 = ((bf16[8,64,512]{2,1,0:T(8,128)(2,1)}), bf16[8,64,512]{2,1,0:T(8,128)(2,1)}, u32[]{:S(2)}, u32[]{:S(2)}) async-start(bf16[8,64,512]{2,1,0:T(8,128)(2,1)} %copy-done.3), calls=%async_computation.1 | async-start | bytes 1048576 | tf_op jit(solution)/shard_map/all_to_all | solution.py:541
  93.0 1.2 %copy-start.2 = (bf16[4,128,1024]{2,1,0:T(8,128)(2,1)S(1)}, bf16[4,128,1024]{2,1,0:T(8,128)(2,1)}, u32[]{:S(2)}) copy-start(bf16[4,128,1024]{2,1,0:T(8,128)(2,1)} %copy-done) | copy-start | bytes 3145732
  96.7 13.8 %collective-permute-start.24 = (bf16[256,512]{1,0:T(8,128)(2,1)}, bf16[256,512]{1,0:T(8,128)(2,1)S(1)}, u32[]{:S(2)}, u32[]{:S(2)}) collective-permute-start(bf16[256,512]{1,0:T(8,128)(2,1)} %get-tuple-element.129), channel_id=1, source_target_pairs={{0,2},{1,3},{2,0},{3,1},{4,6},{5,7},{6,4},{7,5},{8,10},{9,11},{10,... | collective-permute-start | bytes 786440 | tf_op jit(solution)/shard_map/ppermute | solution.py:92
  98.6 11.9 %collective-permute-start.25 = (bf16[256,512]{1,0:T(8,128)(2,1)}, bf16[256,512]{1,0:T(8,128)(2,1)S(1)}, u32[]{:S(2)}, u32[]{:S(2)}) collective-permute-start(bf16[256,512]{1,0:T(8,128)(2,1)} %get-tuple-element.130), channel_id=1, source_target_pairs={{0,4},{1,5},{2,6},{3,7},{4,0},{5,1},{6,2},{7,3},{8,12},{9,13},{10,... | collective-permute-start | bytes 786440 | tf_op jit(solution)/shard_map/ppermute | solution.py:92
  100.1 13.7 %collective-permute-start.26 = (bf16[256,512]{1,0:T(8,128)(2,1)}, bf16[256,512]{1,0:T(8,128)(2,1)S(1)}, u32[]{:S(2)}, u32[]{:S(2)}) collective-permute-start(bf16[256,512]{1,0:T(8,128)(2,1)} %get-tuple-element.131), channel_id=1, source_target_pairs={{0,6},{1,7},{2,4},{3,5},{4,2},{5,3},{6,0},{7,1},{8,14},{9,15},{10,... | collective-permute-start | bytes 786440 | tf_op jit(solution)/shard_map/ppermute | solution.py:92
  103.2 10.7 %copy-start.7 = (f32[256,512]{1,0:T(8,128)S(1)}, f32[256,512]{1,0:T(8,128)}, u32[]{:S(2)}) copy-start(f32[256,512]{1,0:T(8,128)} %copy-done.6) | copy-start | bytes 1572868
  114.0 1.6 %collective-permute-start.27 = (f32[128,512]{1,0:T(8,128)S(1)}, f32[128,512]{1,0:T(8,128)S(1)}, u32[]{:S(2)}, u32[]{:S(2)}) collective-permute-start(f32[128,512]{1,0:T(8,128)S(1)} %get-tuple-element.133), channel_id=1, source_target_pairs={{0,1},{1,0},{2,3},{3,2},{4,5},{5,4},{6,7},{7,6},{8,9},{9,8},{10,11... | collective-permute-start | bytes 786440 | tf_op jit(solution)/shard_map/ppermute | solution.py:92
  (6 other events, 5.0 us)

commit v21 on v20

--- a/solution.py
+++ b/solution.py
@@ -507,7 +507,7 @@
                 pltpu.VMEM((len(deltas), *delta.shape), jnp.bfloat16),
                 pltpu.SemaphoreType.DMA((len(deltas),)),
             ],
-            compiler_params=grant(16),
+            compiler_params=grant(62),
             name=name,
         )(me_scalar, *before, *deltas)
 
@@ -530,7 +530,7 @@
         in_specs=[SCALAR] + anywhere(5),
         out_specs=vmem(1)[0],
         scratch_shapes=room(3) + [pltpu.SemaphoreType.DMA((9,))],
-        compiler_params=grant(16),
+        compiler_params=grant(62),
         name="first_terms",
     )(me_scalar, own_features, mate_features, *there)
     first_weight, last_weight, selected, begun_terms, *deltas[1:] = lax.optimization_barrier(
@@ -553,7 +553,7 @@
         out_specs=tuple(hbm(1) + vmem(3)),
         scratch_shapes=room(1)
         + [pltpu.VMEM(all_terms.shape, all_terms.dtype), pltpu.SemaphoreType.DMA((4,))],
-        compiler_params=grant(16),
+        compiler_params=grant(62),
         name="weight_grad",
     )(me_scalar, own_features, mate_features, begun_terms, after(deltas[3], selected))
     parts = [swap(part, mask) for part, mask in zip(parts, PLANE_MASKS[1:])]

time: 117 us -> 120 us (1.026)
  Pallas kernels: 22.1 us -> 32.4 us
  local copies, waits for them, and re-layouts: 10.7 us -> 6.27 us
  waiting for transfers between devices: 40.7 us -> 38.9 us
    unnamed x48 -> x46, local copies, waits for them, and re-layouts: 7.73 us -> 3.34 us
    pallas_call x2, Pallas kernels: 0.98 us -> 5.25 us  [select(): pl.pallas_call(functools.partial(select_kernel, begin), out_shape=jax.Sha...]
    pallas_call x1, Pallas kernels: 1.74 us -> 5.01 us  [per_device_paired(): pl.pallas_call(functools.partial(weight_grad_kernel, 3), out_shape=(mine_...]
    pallas_call x1, Pallas kernels: 1.28 us -> 4 us  [per_device_paired(): pl.pallas_call(first_terms_kernel, out_shape=all_terms, in_specs=[SCALAR]...]
    all_to_all x1, waiting for transfers between devices: 2.95 us -> 1.26 us  [per_device_paired(): lax.all_to_all(selected, 'dp', split_axis=0, concat_axis=0, axis_index_gr...]
  transfers between devices with their start and end apart: 30 -> 30, of which waited for: 13 -> 13; matrix products, arithmetic and copies ran while one was open for 5% -> 5% of each run, Pallas kernels for 18% -> 26%
where the time goes in v21:
time: 120 us; the launch traced here: 119 us
  waiting for transfers between devices  38.9 us (32%)
  starting transfers between devices  37.5 us (31%)
  Pallas kernels  32.4 us (27%)
  local copies, waits for them, and re-layouts  6.27 us (5%)
  other arithmetic  3.4 us (3%)
    ppermute x28, waiting for transfers between devices, swap(): return lax.ppermute(value, 'dp', [(i, i ^ mask) for i in range(size)])  37.6 us
    ppermute x28, starting transfers between devices, swap(): return lax.ppermute(value, 'dp', [(i, i ^ mask) for i in range(size)])  29.3 us
    pallas_call x2, Pallas kernels, project(): pl.pallas_call(kernel, out_shape=(*results, jax.ShapeDtypeStruct((count *...  9.88 us
    pallas_call x1, Pallas kernels, per_device_paired(): pl.pallas_call(row_grad_kernel, out_shape=jax.ShapeDtypeStruct((receive,...  7.3 us
    pallas_call x2, Pallas kernels, select(): pl.pallas_call(functools.partial(select_kernel, begin), out_shape=jax.Sha...  5.25 us
    pallas_call x1, Pallas kernels, per_device_paired(): pl.pallas_call(functools.partial(weight_grad_kernel, 3), out_shape=(mine_...  5.01 us
    all_to_all x1, starting transfers between devices, per_device_paired(): lax.all_to_all(by_level, 'dp', split_axis=0, concat_axis=0, axis_index_gr...  4.65 us
    pallas_call x1, Pallas kernels, per_device_paired(): pl.pallas_call(first_terms_kernel, out_shape=all_terms, in_specs=[SCALAR]...  4 us
  transfers between devices with their start and end apart: 30, of which 13 were waited for; matrix products, arithmetic and copies ran while one was open for 5% of the time, Pallas kernels for 26%

profile of v21, /device:TPU:0, one launch (start us, length us, event | category | flops | bytes accessed | tf_op | source)
XLA Modules:
  0.0 119.4 jit_solution(8691932382592341456)
XLA Ops:
  0.7 0.5 collective-permute-start
  1.2 1.0 fusion.11
  2.7 4.0 %collective-permute-start.4 = (bf16[256,512]{1,0:T(8,128)(2,1)S(1)}, bf16[256,512]{1,0:T(8,128)(2,1)S(1)}, u32[]{:S(2)}, u32[]{:S(2)}) collective-permute-start(bf16[256,512]{1,0:T(8,128)(2,1)S(1)} %maximum_select_fusion.refs_3_), channel_id=1, source_target_pairs={{0,16},{1,17},{2,18},{3,19},{4,20},{5,21},{6,22},{7,23},{8,24},{9,... | collective-permute-start | bytes 786440 | tf_op jit(solution)/shard_map/ppermute | solution.py:92
  6.7 1.6 %collective-permute-start.3 = (bf16[256,512]{1,0:T(8,128)(2,1)S(1)}, bf16[256,512]{1,0:T(8,128)(2,1)S(1)}, u32[]{:S(2)}, u32[]{:S(2)}) collective-permute-start(bf16[256,512]{1,0:T(8,128)(2,1)S(1)} %maximum_select_fusion.refs_3_), channel_id=1, source_target_pairs={{0,8},{1,9},{2,10},{3,11},{4,12},{5,13},{6,14},{7,15},{8,0},{9,1},... | collective-permute-start | bytes 786440 | tf_op jit(solution)/shard_map/ppermute | solution.py:92
  8.3 1.5 %collective-permute-start.2 = (bf16[256,512]{1,0:T(8,128)(2,1)S(1)}, bf16[256,512]{1,0:T(8,128)(2,1)S(1)}, u32[]{:S(2)}, u32[]{:S(2)}) collective-permute-start(bf16[256,512]{1,0:T(8,128)(2,1)S(1)} %maximum_select_fusion.refs_3_), channel_id=1, source_target_pairs={{0,2},{1,3},{2,0},{3,1},{4,6},{5,7},{6,4},{7,5},{8,10},{9,11},{10,... | collective-permute-start | bytes 786440 | tf_op jit(solution)/shard_map/ppermute | solution.py:92
  9.8 1.5 %collective-permute-start.1 = (bf16[256,512]{1,0:T(8,128)(2,1)S(1)}, bf16[256,512]{1,0:T(8,128)(2,1)}, u32[]{:S(2)}, u32[]{:S(2)}) collective-permute-start(bf16[256,512]{1,0:T(8,128)(2,1)S(1)} %maximum_select_fusion.refs_3_), channel_id=1, source_target_pairs={{0,4},{1,5},{2,6},{3,7},{4,0},{5,1},{6,2},{7,3},{8,12},{9,13},{10,... | collective-permute-start | bytes 786440 | tf_op jit(solution)/shard_map/ppermute | solution.py:92
  11.3 1.3 %slice_bitcast_fusion.3 = (bf16[1,128,1024]{2,1,0:T(8,128)(2,1)S(1)}, bf16[1,128,1024]{2,1,0:T(8,128)(2,1)S(1)}, bf16[1,128,1024]{2,1,0:T(8,128)(2,1)S(1)}, bf16[1,128,1024]{2,1,0:T(8,128)(2,1)S(1)}) fusion(bf16[128,4096]{1,0:T(8,128)(2,1)} %refs_0_), kind=kLoop, calls=%fused_computation.6 | loop fusion | bytes 2097152 | tf_op jit(solution)/shard_map/stack | solution.py:381
  12.6 1.1 pad_maximum_fusion
  13.9 5.8 %collective-permute-done.4.refs_7_ = bf16[256,512]{1,0:T(8,128)(2,1)S(1)} collective-permute-done((bf16[256,512]{1,0:T(8,128)(2,1)S(1)}, bf16[256,512]{1,0:T(8,128)(2,1)S(1)}, u32[]{:S(2)}, u32[]{:S(2)}) %collective-permute-start.4) | collective-permute-done | bytes 262176 | tf_op jit(solution)/shard_map/ppermute | solution.py:92
  19.7 2.3 %collective-permute-start.6 = (bf16[256,512]{1,0:T(8,128)(2,1)S(1)}, bf16[256,512]{1,0:T(8,128)(2,1)}, u32[]{:S(2)}, u32[]{:S(2)}) collective-permute-start(bf16[256,512]{1,0:T(8,128)(2,1)S(1)} %collective-permute-done.3.refs_6_), channel_id=1, source_target_pairs={{0,4},{1,5},{2,6},{3,7},{4,0},{5,1},{6,2},{7,3},{8,12},{9,13},{10,... | collective-permute-start | bytes 786440 | tf_op jit(solution)/shard_map/ppermute | solution.py:92
  22.0 1.5 %collective-permute-start.5 = (bf16[256,512]{1,0:T(8,128)(2,1)S(1)}, bf16[256,512]{1,0:T(8,128)(2,1)}, u32[]{:S(2)}, u32[]{:S(2)}) collective-permute-start(bf16[256,512]{1,0:T(8,128)(2,1)S(1)} %collective-permute-done.3.refs_6_), channel_id=1, source_target_pairs={{0,2},{1,3},{2,0},{3,1},{4,6},{5,7},{6,4},{7,5},{8,10},{9,11},{10,... | collective-permute-start | bytes 786440 | tf_op jit(solution)/shard_map/ppermute | solution.py:92
  24.5 4.7 %all-to-all-start = ((bf16[4,128,1024]{2,1,0:T(8,128)(2,1)}), bf16[4,128,1024]{2,1,0:T(8,128)(2,1)S(1)}, u32[]{:S(2)}, u32[]{:S(2)}) async-start(bf16[4,128,1024]{2,1,0:T(8,128)(2,1)} %pad_maximum_fusion), calls=%async_computation | async-start | bytes 2097152 | tf_op jit(solution)/shard_map/all_to_all | solution.py:386
  29.3 1.1 compare_select_fusion
  30.4 0.7 pad_maximum_fusion.1
  31.1 1.5 %collective-permute-done.8.refs_11_ = bf16[256,512]{1,0:T(8,128)(2,1)} collective-permute-done((bf16[256,512]{1,0:T(8,128)(2,1)S(1)}, bf16[256,512]{1,0:T(8,128)(2,1)}, u32[]{:S(2)}, u32[]{:S(2)}) %collective-permute-start.8) | collective-permute-done | bytes 262176 | tf_op jit(solution)/shard_map/ppermute | solution.py:92
  32.6 1.0 collective-permute-done.7.refs_10_
  33.6 1.5 %collective-permute-start.13 = (bf16[256,512]{1,0:T(8,128)(2,1)}, bf16[256,512]{1,0:T(8,128)(2,1)S(1)}, u32[]{:S(2)}, u32[]{:S(2)}) collective-permute-start(bf16[256,512]{1,0:T(8,128)(2,1)} %collective-permute-done.1.refs_4_), channel_id=1, source_target_pairs={{0,2},{1,3},{2,0},{3,1},{4,6},{5,7},{6,4},{7,5},{8,10},{9,11},{10,... | collective-permute-start | bytes 786440 | tf_op jit(solution)/shard_map/ppermute | solution.py:92
  35.6 1.5 %collective-permute-start.12 = (bf16[256,512]{1,0:T(8,128)(2,1)}, bf16[256,512]{1,0:T(8,128)(2,1)S(1)}, u32[]{:S(2)}, u32[]{:S(2)}) collective-permute-start(bf16[256,512]{1,0:T(8,128)(2,1)} %collective-permute-done.9.refs_12_), channel_id=1, source_target_pairs={{0,4},{1,5},{2,6},{3,7},{4,0},{5,1},{6,2},{7,3},{8,12},{9,13},{10,... | collective-permute-start | bytes 786440 | tf_op jit(solution)/shard_map/ppermute | solution.py:92
  37.1 0.5 collective-permute-start.11
  37.7 5.3 %collective-permute-done.13.refs_15_ = bf16[256,512]{1,0:T(8,128)(2,1)S(1)} collective-permute-done((bf16[256,512]{1,0:T(8,128)(2,1)}, bf16[256,512]{1,0:T(8,128)(2,1)S(1)}, u32[]{:S(2)}, u32[]{:S(2)}) %collective-permute-start.13) | collective-permute-done | bytes 262176 | tf_op jit(solution)/shard_map/ppermute | solution.py:92
  42.9 1.5 %collective-permute-done.14.refs_16_ = bf16[256,512]{1,0:T(8,128)(2,1)S(1)} collective-permute-done((bf16[256,512]{1,0:T(8,128)(2,1)}, bf16[256,512]{1,0:T(8,128)(2,1)S(1)}, u32[]{:S(2)}, u32[]{:S(2)}) %collective-permute-start.14) | collective-permute-done | bytes 262176 | tf_op jit(solution)/shard_map/ppermute | solution.py:92
  44.4 4.9 %collective-permute-done.12.refs_14_ = bf16[256,512]{1,0:T(8,128)(2,1)S(1)} collective-permute-done((bf16[256,512]{1,0:T(8,128)(2,1)}, bf16[256,512]{1,0:T(8,128)(2,1)S(1)}, u32[]{:S(2)}, u32[]{:S(2)}) %collective-permute-start.12) | collective-permute-done | bytes 262176 | tf_op jit(solution)/shard_map/ppermute | solution.py:92
  49.4 1.0 copy-done.4
  50.4 0.5 collective-permute-start.16
  50.9 0.8 collective-permute-start.17
  51.7 0.6 stack.87.refs_0_.chips_ref
  52.4 6.1 %project.1 = (bf16[3584,512]{1,0:T(8,128)(2,1)}, f32[2,128,512]{2,1,0:T(8,128)}) custom-call(s32[16]{0:T(128)} %stack.87.refs_0_.chips_ref, bf16[128,4096]{1,0:T(8,128)(2,1)} %refs_0_, bf16[128,4096]{1,0:T(8,128)(2,1)} %copy-done.4, bf16[256,512]{1,0:T(8,128)(2,1)} %copy-done.9, bf16[256,512]{1,0:T(8,128)(2,1)} %collective-permute-done.1.refs_4_, ...), custom_call_target="tpu_custom_call" | custom-call | tf_op jit(solution)/shard_map/project/pallas_call | solution.py:436
  58.6 0.5 collective-permute-start.20
  59.4 3.8 %delta.1 = (bf16[272,512]{1,0:T(8,128)(2,1)}, bf16[512,512]{1,0:T(8,128)(2,1)}) custom-call(s32[16]{0:T(128)} %stack.87.refs_0_.chips_ref, s32[1]{0:T(128)} %bitcast.16.me_ref, bf16[144,512]{1,0:T(8,128)(2,1)} %get-tuple-element.110.own_cot_ref, bf16[144,512]{1,0:T(8,128)(2,1)} %copy-done.19, bf16[128,4096]{1,0:T(8,128)(2,1)} %refs_0_, ...), custom_call_target="tpu_custom_call" | custom-call | tf_op jit(solution)/shard_map/delta/pallas_call | solution.py:436
  63.2 1.4 %collective-permute-start.19 = (bf16[272,512]{1,0:T(8,128)(2,1)}, bf16[272,512]{1,0:T(8,128)(2,1)S(1)}, u32[]{:S(2)}, u32[]{:S(2)}) collective-permute-start(bf16[272,512]{1,0:T(8,128)(2,1)} %get-tuple-element.116.refs_0_), channel_id=1, source_target_pairs={{0,16},{1,17},{2,18},{3,19},{4,20},{5,21},{6,22},{7,23},{8,24},{9,... | collective-permute-start | bytes 835592 | tf_op jit(solution)/shard_map/ppermute | solution.py:92
  64.6 3.9 %collective-permute-start.18 = (bf16[272,512]{1,0:T(8,128)(2,1)}, bf16[272,512]{1,0:T(8,128)(2,1)S(1)}, u32[]{:S(2)}, u32[]{:S(2)}) collective-permute-start(bf16[272,512]{1,0:T(8,128)(2,1)} %get-tuple-element.116.refs_0_), channel_id=1, source_target_pairs={{0,8},{1,9},{2,10},{3,11},{4,12},{5,13},{6,14},{7,15},{8,0},{9,1},... | collective-permute-start | bytes 835592 | tf_op jit(solution)/shard_map/ppermute | solution.py:92
  68.4 11.0 %collective-permute-done.19.refs_2_ = bf16[272,512]{1,0:T(8,128)(2,1)S(1)} collective-permute-done((bf16[272,512]{1,0:T(8,128)(2,1)}, bf16[272,512]{1,0:T(8,128)(2,1)S(1)}, u32[]{:S(2)}, u32[]{:S(2)}) %collective-permute-start.19) | collective-permute-done | bytes 278560 | tf_op jit(solution)/shard_map/ppermute | solution.py:92
  79.6 1.0 copy-done.3
  80.8 2.3 %first_select.1.refs_0_ = bf16[8,48,512]{2,1,0:T(8,128)(2,1)} custom-call(s32[1]{0:T(128)} %bitcast.16.me_ref, bf16[272,512]{1,0:T(8,128)(2,1)} %get-tuple-element.116.refs_0_, bf16[272,512]{1,0:T(8,128)(2,1)} %copy-done.8, bf16[272,512]{1,0:T(8,128)(2,1)} %copy-done.7), custom_call_target="tpu_custom_call" | custom-call | tf_op jit(solution)/shard_map/first_select/pallas_call | solution.py:499
  83.2 4.0 %first_terms.1.begun_ref = f32[1024,512]{1,0:T(8,128)} custom-call(s32[1]{0:T(128)} %bitcast.16.me_ref, bf16[4,128,1024]{2,1,0:T(8,128)(2,1)} %copy-done.1, bf16[4,128,1024]{2,1,0:T(8,128)(2,1)} %copy-done.3, bf16[272,512]{1,0:T(8,128)(2,1)} %get-tuple-element.116.refs_0_, bf16[272,512]{1,0:T(8,128)(2,1)} %copy-done.8, bf16[272,512]{1,0:T(8,128)(2,1)} %copy-done.7), custom_call_target="tpu_custom_call" | custom-call | tf_op jit(solution)/shard_map/first_terms/pallas_call | solution.py:527
  87.2 1.5 %collective-permute-done.21.refs_1_.refs_0_ = bf16[272,512]{1,0:T(8,128)(2,1)S(1)} collective-permute-done((bf16[272,512]{1,0:T(8,128)(2,1)S(1)}, bf16[272,512]{1,0:T(8,128)(2,1)S(1)}, u32[]{:S(2)}, u32[]{:S(2)}) %collective-permute-start.21) | collective-permute-done | bytes 278560 | tf_op jit(solution)/shard_map/ppermute | solution.py:92
  88.7 0.5 collective-permute-start.23
  89.4 2.9 %select.28 = bf16[8,64,512]{2,1,0:T(8,128)(2,1)} custom-call(s32[1]{0:T(128)} %bitcast.16.me_ref, bf16[8,48,512]{2,1,0:T(8,128)(2,1)} %first_select.1.refs_0_, bf16[272,512]{1,0:T(8,128)(2,1)} %copy-done.6), custom_call_target="tpu_custom_call" | custom-call | tf_op jit(solution)/shard_map/select/pallas_call | solution.py:499
  92.3 3.5 %all-to-all-start.1 = ((bf16[8,64,512]{2,1,0:T(8,128)(2,1)}), bf16[8,64,512]{2,1,0:T(8,128)(2,1)S(1)}, u32[]{:S(2)}, u32[]{:S(2)}) async-start(bf16[8,64,512]{2,1,0:T(8,128)(2,1)} %select.28), calls=%async_computation.1 | async-start | bytes 1048576 | tf_op jit(solution)/shard_map/all_to_all | solution.py:541
  95.8 5.0 %weight_grad.1 = (f32[256,512]{1,0:T(8,128)}, bf16[256,512]{1,0:T(8,128)(2,1)}, bf16[256,512]{1,0:T(8,128)(2,1)}, bf16[256,512]{1,0:T(8,128)(2,1)}) custom-call(s32[1]{0:T(128)} %bitcast.16.me_ref, bf16[4,128,1024]{2,1,0:T(8,128)(2,1)} %copy-done.1, bf16[4,128,1024]{2,1,0:T(8,128)(2,1)} %copy-done.3, f32[1024,512]{1,0:T(8,128)} %first_terms.1.begun_ref, ...), custom_call_target="tpu_custom_call" | custom-call | tf_op jit(solution)/shard_map/weight_grad/pallas_call | solution.py:549
  100.9 2.0 %collective-permute-start.24 = (bf16[256,512]{1,0:T(8,128)(2,1)}, bf16[256,512]{1,0:T(8,128)(2,1)S(1)}, u32[]{:S(2)}, u32[]{:S(2)}) collective-permute-start(bf16[256,512]{1,0:T(8,128)(2,1)} %get-tuple-element.129), channel_id=1, source_target_pairs={{0,2},{1,3},{2,0},{3,1},{4,6},{5,7},{6,4},{7,5},{8,10},{9,11},{10,... | collective-permute-start | bytes 786440 | tf_op jit(solution)/shard_map/ppermute | solution.py:92
  102.9 1.5 %collective-permute-start.25 = (bf16[256,512]{1,0:T(8,128)(2,1)}, bf16[256,512]{1,0:T(8,128)(2,1)S(1)}, u32[]{:S(2)}, u32[]{:S(2)}) collective-permute-start(bf16[256,512]{1,0:T(8,128)(2,1)} %get-tuple-element.130), channel_id=1, source_target_pairs={{0,4},{1,5},{2,6},{3,7},{4,0},{5,1},{6,2},{7,3},{8,12},{9,13},{10,... | collective-permute-start | bytes 786440 | tf_op jit(solution)/shard_map/ppermute | solution.py:92
  104.4 1.3 %all-to-all-done.1 = bf16[8,64,512]{2,1,0:T(8,128)(2,1)S(1)} async-done(((bf16[8,64,512]{2,1,0:T(8,128)(2,1)}), bf16[8,64,512]{2,1,0:T(8,128)(2,1)S(1)}, u32[]{:S(2)}, u32[]{:S(2)}) %all-to-all-start.1) | async-done | bytes 524320 | tf_op jit(solution)/shard_map/all_to_all | solution.py:541
  105.7 0.8 copy-done.5
  106.5 7.3 %row_grad.1 = bf16[256,4096]{1,0:T(8,128)(2,1)} custom-call(s32[16]{0:T(128)} %stack.87.refs_0_.chips_ref, s32[1]{0:T(128)} %bitcast.16.me_ref, bf16[4,2,64,512]{3,2,1,0:T(8,128)(2,1)} %bitcast.34, bf16[3584,512]{1,0:T(8,128)(2,1)} %get-tuple-element.123.refs_0_, bf16[3584,512]{1,0:T(8,128)(2,1)} %collective-permute-done.22.refs_1_, ...), custom_call_target="tpu_custom_call" | custom-call | tf_op jit(solution)/shard_map/row_grad/pallas_call | solution.py:561
  113.8 3.1 %collective-permute-done.25.refs_1_ = bf16[256,512]{1,0:T(8,128)(2,1)S(1)} collective-permute-done((bf16[256,512]{1,0:T(8,128)(2,1)}, bf16[256,512]{1,0:T(8,128)(2,1)S(1)}, u32[]{:S(2)}, u32[]{:S(2)}) %collective-permute-start.25) | collective-permute-done | bytes 262176 | tf_op jit(solution)/shard_map/ppermute | solution.py:92
  117.1 1.5 %collective-permute-done.27.mate_ref = f32[128,512]{1,0:T(8,128)S(1)} collective-permute-done((f32[128,512]{1,0:T(8,128)S(1)}, f32[128,512]{1,0:T(8,128)S(1)}, u32[]{:S(2)}, u32[]{:S(2)}) %collective-permute-start.27) | collective-permute-done | bytes 262176 | tf_op jit(solution)/shard_map/ppermute | solution.py:92
  118.6 0.8 join.1
  (85 shorter events, 3.5 us)
Async XLA Ops:
  0.6 23.5 %copy-start.20 = (s32[1,4]{1,0:T(1,128)S(1)}, s32[1,4]{1,0:T(1,128)}, u32[]{:S(2)}) copy-start(s32[1,4]{1,0:T(1,128)} %param.9) | copy-start | bytes 52
  0.6 23.8 %copy-start.21 = (s32[128,1]{0,1:T(1,128)S(1)}, s32[128,1]{0,1:T(1,128)}, u32[]{:S(2)}) copy-start(s32[128,1]{0,1:T(1,128)} %param.8) | copy-start | bytes 1540
  0.7 1.9 %collective-permute-start = (bf16[128,1024]{1,0:T(8,128)(2,1)}, bf16[128,1024]{1,0:T(8,128)(2,1)S(1)}, u32[]{:S(2)}, u32[]{:S(2)}) collective-permute-start(bf16[128,1024]{1,0:T(8,128)(2,1)} %param.11), channel_id=1, source_target_pairs={{0,1},{1,0},{2,3},{3,2},{4,5},{5,4},{6,7},{7,6},{8,9},{9,8},{10,11... | collective-permute-start | bytes 786440 | tf_op jit(solution)/shard_map/ppermute | solution.py:92
  2.6 26.6 %copy-start.22 = (s32[4]{0:T(128)S(1)}, s32[4]{0:T(128)}, u32[]{:S(2)}) copy-start(s32[4]{0:T(128)} %param.10) | copy-start | bytes 52
  2.6 27.7 %copy-start.9 = (bf16[256,512]{1,0:T(8,128)(2,1)}, bf16[256,512]{1,0:T(8,128)(2,1)S(1)}, u32[]{:S(2)}) copy-start(bf16[256,512]{1,0:T(8,128)(2,1)S(1)} %maximum_select_fusion.refs_3_) | copy-start | bytes 786436
  2.7 30.9 %copy-start.2 = (bf16[128,4096]{1,0:T(8,128)(2,1)S(1)}, bf16[128,4096]{1,0:T(8,128)(2,1)}, u32[]{:S(2)}) copy-start(bf16[128,4096]{1,0:T(8,128)(2,1)} %refs_0_) | copy-start | bytes 3145732
  2.7 17.0 %collective-permute-start.4 = (bf16[256,512]{1,0:T(8,128)(2,1)S(1)}, bf16[256,512]{1,0:T(8,128)(2,1)S(1)}, u32[]{:S(2)}, u32[]{:S(2)}) collective-permute-start(bf16[256,512]{1,0:T(8,128)(2,1)S(1)} %maximum_select_fusion.refs_3_), channel_id=1, source_target_pairs={{0,16},{1,17},{2,18},{3,19},{4,20},{5,21},{6,22},{7,23},{8,24},{9,... | collective-permute-start | bytes 786440 | tf_op jit(solution)/shard_map/ppermute | solution.py:92
  6.7 13.0 %collective-permute-start.3 = (bf16[256,512]{1,0:T(8,128)(2,1)S(1)}, bf16[256,512]{1,0:T(8,128)(2,1)S(1)}, u32[]{:S(2)}, u32[]{:S(2)}) collective-permute-start(bf16[256,512]{1,0:T(8,128)(2,1)S(1)} %maximum_select_fusion.refs_3_), channel_id=1, source_target_pairs={{0,8},{1,9},{2,10},{3,11},{4,12},{5,13},{6,14},{7,15},{8,0},{9,1},... | collective-permute-start | bytes 786440 | tf_op jit(solution)/shard_map/ppermute | solution.py:92
  8.3 11.4 %collective-permute-start.2 = (bf16[256,512]{1,0:T(8,128)(2,1)S(1)}, bf16[256,512]{1,0:T(8,128)(2,1)S(1)}, u32[]{:S(2)}, u32[]{:S(2)}) collective-permute-start(bf16[256,512]{1,0:T(8,128)(2,1)S(1)} %maximum_select_fusion.refs_3_), channel_id=1, source_target_pairs={{0,2},{1,3},{2,0},{3,1},{4,6},{5,7},{6,4},{7,5},{8,10},{9,11},{10,... | collective-permute-start | bytes 786440 | tf_op jit(solution)/shard_map/ppermute | solution.py:92
  9.8 9.9 %collective-permute-start.1 = (bf16[256,512]{1,0:T(8,128)(2,1)S(1)}, bf16[256,512]{1,0:T(8,128)(2,1)}, u32[]{:S(2)}, u32[]{:S(2)}) collective-permute-start(bf16[256,512]{1,0:T(8,128)(2,1)S(1)} %maximum_select_fusion.refs_3_), channel_id=1, source_target_pairs={{0,4},{1,5},{2,6},{3,7},{4,0},{5,1},{6,2},{7,3},{8,12},{9,13},{10,... | collective-permute-start | bytes 786440 | tf_op jit(solution)/shard_map/ppermute | solution.py:92
  13.7 17.4 %collective-permute-start.9 = (bf16[256,512]{1,0:T(8,128)(2,1)S(1)}, bf16[256,512]{1,0:T(8,128)(2,1)}, u32[]{:S(2)}, u32[]{:S(2)}) collective-permute-start(bf16[256,512]{1,0:T(8,128)(2,1)S(1)} %maximum_select_fusion.refs_3_), channel_id=1, source_target_pairs={{0,24},{1,25},{2,26},{3,27},{4,28},{5,29},{6,30},{7,31},{8,16},{9,... | collective-permute-start | bytes 786440 | tf_op jit(solution)/shard_map/ppermute | solution.py:92
  19.7 32.7 %copy-start.10 = (bf16[256,512]{1,0:T(8,128)(2,1)}, bf16[256,512]{1,0:T(8,128)(2,1)S(1)}, u32[]{:S(2)}) copy-start(bf16[256,512]{1,0:T(8,128)(2,1)S(1)} %collective-permute-done.4.refs_7_) | copy-start | bytes 786436
  19.7 32.7 %copy-start.11 = (bf16[256,512]{1,0:T(8,128)(2,1)}, bf16[256,512]{1,0:T(8,128)(2,1)S(1)}, u32[]{:S(2)}) copy-start(bf16[256,512]{1,0:T(8,128)(2,1)S(1)} %collective-permute-done.3.refs_6_) | copy-start | bytes 786436
  19.7 32.7 %copy-start.12 = (bf16[256,512]{1,0:T(8,128)(2,1)}, bf16[256,512]{1,0:T(8,128)(2,1)S(1)}, u32[]{:S(2)}) copy-start(bf16[256,512]{1,0:T(8,128)(2,1)S(1)} %collective-permute-done.2.refs_5_) | copy-start | bytes 786436
  19.7 11.4 %collective-permute-start.6 = (bf16[256,512]{1,0:T(8,128)(2,1)S(1)}, bf16[256,512]{1,0:T(8,128)(2,1)}, u32[]{:S(2)}, u32[]{:S(2)}) collective-permute-start(bf16[256,512]{1,0:T(8,128)(2,1)S(1)} %collective-permute-done.3.refs_6_), channel_id=1, source_target_pairs={{0,4},{1,5},{2,6},{3,7},{4,0},{5,1},{6,2},{7,3},{8,12},{9,13},{10,... | collective-permute-start | bytes 786440 | tf_op jit(solution)/shard_map/ppermute | solution.py:92
  22.0 9.1 %collective-permute-start.5 = (bf16[256,512]{1,0:T(8,128)(2,1)S(1)}, bf16[256,512]{1,0:T(8,128)(2,1)}, u32[]{:S(2)}, u32[]{:S(2)}) collective-permute-start(bf16[256,512]{1,0:T(8,128)(2,1)S(1)} %collective-permute-done.3.refs_6_), channel_id=1, source_target_pairs={{0,2},{1,3},{2,0},{3,1},{4,6},{5,7},{6,4},{7,5},{8,10},{9,11},{10,... | collective-permute-start | bytes 786440 | tf_op jit(solution)/shard_map/ppermute | solution.py:92
  23.5 9.1 %collective-permute-start.8 = (bf16[256,512]{1,0:T(8,128)(2,1)S(1)}, bf16[256,512]{1,0:T(8,128)(2,1)}, u32[]{:S(2)}, u32[]{:S(2)}) collective-permute-start(bf16[256,512]{1,0:T(8,128)(2,1)S(1)} %collective-permute-done.4.refs_7_), channel_id=1, source_target_pairs={{0,4},{1,5},{2,6},{3,7},{4,0},{5,1},{6,2},{7,3},{8,12},{9,13},{10,... | collective-permute-start | bytes 786440 | tf_op jit(solution)/shard_map/ppermute | solution.py:92
  24.0 9.6 %collective-permute-start.7 = (bf16[256,512]{1,0:T(8,128)(2,1)S(1)}, bf16[256,512]{1,0:T(8,128)(2,1)}, u32[]{:S(2)}, u32[]{:S(2)}) collective-permute-start(bf16[256,512]{1,0:T(8,128)(2,1)S(1)} %collective-permute-done.4.refs_7_), channel_id=1, source_target_pairs={{0,2},{1,3},{2,0},{3,1},{4,6},{5,7},{6,4},{7,5},{8,10},{9,11},{10,... | collective-permute-start | bytes 786440 | tf_op jit(solution)/shard_map/ppermute | solution.py:92
  24.5 34.0 %all-to-all-start = ((bf16[4,128,1024]{2,1,0:T(8,128)(2,1)}), bf16[4,128,1024]{2,1,0:T(8,128)(2,1)S(1)}, u32[]{:S(2)}, u32[]{:S(2)}) async-start(bf16[4,128,1024]{2,1,0:T(8,128)(2,1)} %pad_maximum_fusion), calls=%async_computation | async-start | bytes 2097152 | tf_op jit(solution)/shard_map/all_to_all | solution.py:386
  33.6 15.8 %collective-permute-start.10 = (bf16[128,4096]{1,0:T(8,128)(2,1)S(1)}, bf16[128,4096]{1,0:T(8,128)(2,1)S(1)}, u32[]{:S(2)}, u32[]{:S(2)}) collective-permute-start(bf16[128,4096]{1,0:T(8,128)(2,1)S(1)} %copy-done.2), channel_id=1, source_target_pairs={{0,1},{1,0},{2,3},{3,2},{4,5},{5,4},{6,7},{7,6},{8,9},{9,8},{10,11... | collective-permute-start | bytes 3145736 | tf_op jit(solution)/shard_map/ppermute | solution.py:92
  33.6 9.3 %collective-permute-start.13 = (bf16[256,512]{1,0:T(8,128)(2,1)}, bf16[256,512]{1,0:T(8,128)(2,1)S(1)}, u32[]{:S(2)}, u32[]{:S(2)}) collective-permute-start(bf16[256,512]{1,0:T(8,128)(2,1)} %collective-permute-done.1.refs_4_), channel_id=1, source_target_pairs={{0,2},{1,3},{2,0},{3,1},{4,6},{5,7},{6,4},{7,5},{8,10},{9,11},{10,... | collective-permute-start | bytes 786440 | tf_op jit(solution)/shard_map/ppermute | solution.py:92
  35.1 9.4 %collective-permute-start.14 = (bf16[256,512]{1,0:T(8,128)(2,1)}, bf16[256,512]{1,0:T(8,128)(2,1)S(1)}, u32[]{:S(2)}, u32[]{:S(2)}) collective-permute-start(bf16[256,512]{1,0:T(8,128)(2,1)} %collective-permute-done.7.refs_10_), channel_id=1, source_target_pairs={{0,4},{1,5},{2,6},{3,7},{4,0},{5,1},{6,2},{7,3},{8,12},{9,13},{10,... | collective-permute-start | bytes 786440 | tf_op jit(solution)/shard_map/ppermute | solution.py:92
  35.6 13.8 %collective-permute-start.12 = (bf16[256,512]{1,0:T(8,128)(2,1)}, bf16[256,512]{1,0:T(8,128)(2,1)S(1)}, u32[]{:S(2)}, u32[]{:S(2)}) collective-permute-start(bf16[256,512]{1,0:T(8,128)(2,1)} %collective-permute-done.9.refs_12_), channel_id=1, source_target_pairs={{0,4},{1,5},{2,6},{3,7},{4,0},{5,1},{6,2},{7,3},{8,12},{9,13},{10,... | collective-permute-start | bytes 786440 | tf_op jit(solution)/shard_map/ppermute | solution.py:92
  37.1 12.2 %collective-permute-start.11 = (bf16[256,512]{1,0:T(8,128)(2,1)}, bf16[256,512]{1,0:T(8,128)(2,1)S(1)}, u32[]{:S(2)}, u32[]{:S(2)}) collective-permute-start(bf16[256,512]{1,0:T(8,128)(2,1)} %collective-permute-done.9.refs_12_), channel_id=1, source_target_pairs={{0,2},{1,3},{2,0},{3,1},{4,6},{5,7},{6,4},{7,5},{8,10},{9,11},{10,... | collective-permute-start | bytes 786440 | tf_op jit(solution)/shard_map/ppermute | solution.py:92
  42.9 8.0 %copy-start.14 = (bf16[256,512]{1,0:T(8,128)(2,1)}, bf16[256,512]{1,0:T(8,128)(2,1)S(1)}, u32[]{:S(2)}) copy-start(bf16[256,512]{1,0:T(8,128)(2,1)S(1)} %collective-permute-done.13.refs_15_) | copy-start | bytes 786436
  44.4 7.2 %copy-start.16 = (bf16[256,512]{1,0:T(8,128)(2,1)}, bf16[256,512]{1,0:T(8,128)(2,1)S(1)}, u32[]{:S(2)}) copy-start(bf16[256,512]{1,0:T(8,128)(2,1)S(1)} %collective-permute-done.14.refs_16_) | copy-start | bytes 786436
  49.4 2.3 %copy-start.18 = (bf16[256,512]{1,0:T(8,128)(2,1)}, bf16[256,512]{1,0:T(8,128)(2,1)S(1)}, u32[]{:S(2)}) copy-start(bf16[256,512]{1,0:T(8,128)(2,1)S(1)} %collective-permute-done.12.refs_14_) | copy-start | bytes 786436
  49.4 3.0 %copy-start.13 = (bf16[256,512]{1,0:T(8,128)(2,1)}, bf16[256,512]{1,0:T(8,128)(2,1)S(1)}, u32[]{:S(2)}) copy-start(bf16[256,512]{1,0:T(8,128)(2,1)S(1)} %collective-permute-done.11.refs_13_) | copy-start | bytes 786436
  49.4 1.0 copy-start.4
  50.4 8.1 %collective-permute-start.16 = (bf16[256,512]{1,0:T(8,128)(2,1)}, bf16[256,512]{1,0:T(8,128)(2,1)S(1)}, u32[]{:S(2)}, u32[]{:S(2)}) collective-permute-start(bf16[256,512]{1,0:T(8,128)(2,1)} %collective-permute-done.6.refs_9_), channel_id=1, source_target_pairs={{0,2},{1,3},{2,0},{3,1},{4,6},{5,7},{6,4},{7,5},{8,10},{9,11},{10,... | collective-permute-start | bytes 786440 | tf_op jit(solution)/shard_map/ppermute | solution.py:92
  50.9 7.6 %collective-permute-start.17 = (bf16[256,512]{1,0:T(8,128)(2,1)S(1)}, bf16[256,512]{1,0:T(8,128)(2,1)S(1)}, u32[]{:S(2)}, u32[]{:S(2)}) collective-permute-start(bf16[256,512]{1,0:T(8,128)(2,1)S(1)} %collective-permute-done.11.refs_13_), channel_id=1, source_target_pairs={{0,4},{1,5},{2,6},{3,7},{4,0},{5,1},{6,2},{7,3},{8,12},{9,13},{10,... | collective-permute-start | bytes 786440 | tf_op jit(solution)/shard_map/ppermute | solution.py:92
  51.7 6.8 %collective-permute-start.15 = (bf16[144,512]{1,0:T(8,128)(2,1)S(1)}, bf16[144,512]{1,0:T(8,128)(2,1)S(1)}, u32[]{:S(2)}, u32[]{:S(2)}) collective-permute-start(bf16[144,512]{1,0:T(8,128)(2,1)S(1)} %get-tuple-element.89), channel_id=1, source_target_pairs={{0,1},{1,0},{2,3},{3,2},{4,5},{5,4},{6,7},{7,6},{8,9},{9,8},{10,11... | collective-permute-start | bytes 442376 | tf_op jit(solution)/shard_map/ppermute | solution.py:92
  58.5 24.6 %copy-start.1 = (bf16[4,128,1024]{2,1,0:T(8,128)(2,1)}, bf16[4,128,1024]{2,1,0:T(8,128)(2,1)S(1)}, u32[]{:S(2)}) copy-start(bf16[4,128,1024]{2,1,0:T(8,128)(2,1)S(1)} %all-to-all-done.own_ref) | copy-start | bytes 3145732
  58.6 21.0 %collective-permute-start.20 = (bf16[4,128,1024]{2,1,0:T(8,128)(2,1)S(1)}, bf16[4,128,1024]{2,1,0:T(8,128)(2,1)S(1)}, u32[]{:S(2)}, u32[]{:S(2)}) collective-permute-start(bf16[4,128,1024]{2,1,0:T(8,128)(2,1)S(1)} %all-to-all-done.own_ref), channel_id=1, source_target_pairs={{0,1},{1,0},{2,3},{3,2},{4,5},{5,4},{6,7},{7,6},{8,9},{9,8},{10,11... | collective-permute-start | bytes 3145736 | tf_op jit(solution)/shard_map/ppermute | solution.py:92
  63.2 16.3 %collective-permute-start.19 = (bf16[272,512]{1,0:T(8,128)(2,1)}, bf16[272,512]{1,0:T(8,128)(2,1)S(1)}, u32[]{:S(2)}, u32[]{:S(2)}) collective-permute-start(bf16[272,512]{1,0:T(8,128)(2,1)} %get-tuple-element.116.refs_0_), channel_id=1, source_target_pairs={{0,16},{1,17},{2,18},{3,19},{4,20},{5,21},{6,22},{7,23},{8,24},{9,... | collective-permute-start | bytes 835592 | tf_op jit(solution)/shard_map/ppermute | solution.py:92
  64.6 15.0 %collective-permute-start.18 = (bf16[272,512]{1,0:T(8,128)(2,1)}, bf16[272,512]{1,0:T(8,128)(2,1)S(1)}, u32[]{:S(2)}, u32[]{:S(2)}) collective-permute-start(bf16[272,512]{1,0:T(8,128)(2,1)} %get-tuple-element.116.refs_0_), channel_id=1, source_target_pairs={{0,8},{1,9},{2,10},{3,11},{4,12},{5,13},{6,14},{7,15},{8,0},{9,1},... | collective-permute-start | bytes 835592 | tf_op jit(solution)/shard_map/ppermute | solution.py:92
  79.5 1.3 %copy-start.7 = (bf16[272,512]{1,0:T(8,128)(2,1)}, bf16[272,512]{1,0:T(8,128)(2,1)S(1)}, u32[]{:S(2)}) copy-start(bf16[272,512]{1,0:T(8,128)(2,1)S(1)} %collective-permute-done.19.refs_2_) | copy-start | bytes 835588
  79.6 1.2 %copy-start.8 = (bf16[272,512]{1,0:T(8,128)(2,1)}, bf16[272,512]{1,0:T(8,128)(2,1)S(1)}, u32[]{:S(2)}) copy-start(bf16[272,512]{1,0:T(8,128)(2,1)S(1)} %collective-permute-done.18.refs_1_) | copy-start | bytes 835588
  79.6 1.0 copy-start.3
  80.6 8.1 %collective-permute-start.21 = (bf16[272,512]{1,0:T(8,128)(2,1)S(1)}, bf16[272,512]{1,0:T(8,128)(2,1)S(1)}, u32[]{:S(2)}, u32[]{:S(2)}) collective-permute-start(bf16[272,512]{1,0:T(8,128)(2,1)S(1)} %collective-permute-done.19.refs_2_), channel_id=1, source_target_pairs={{0,8},{1,9},{2,10},{3,11},{4,12},{5,13},{6,14},{7,15},{8,0},{9,1},... | collective-permute-start | bytes 835592 | tf_op jit(solution)/shard_map/ppermute | solution.py:92
  88.7 17.0 %collective-permute-start.22 = (bf16[3584,512]{1,0:T(8,128)(2,1)}, bf16[3584,512]{1,0:T(8,128)(2,1)}, u32[]{:S(2)}, u32[]{:S(2)}) collective-permute-start(bf16[3584,512]{1,0:T(8,128)(2,1)} %get-tuple-element.123.refs_0_), channel_id=1, source_target_pairs={{0,1},{1,0},{2,3},{3,2},{4,5},{5,4},{6,7},{7,6},{8,9},{9,8},{10,11... | collective-permute-start | bytes 11010056 | tf_op jit(solution)/shard_map/ppermute | solution.py:92
  88.7 17.0 %collective-permute-start.23 = (bf16[512,512]{1,0:T(8,128)(2,1)}, bf16[512,512]{1,0:T(8,128)(2,1)}, u32[]{:S(2)}, u32[]{:S(2)}) collective-permute-start(bf16[512,512]{1,0:T(8,128)(2,1)} %get-tuple-element.124.refs_2_), channel_id=1, source_target_pairs={{0,1},{1,0},{2,3},{3,2},{4,5},{5,4},{6,7},{7,6},{8,9},{9,8},{10,11... | collective-permute-start | bytes 1572872 | tf_op jit(solution)/shard_map/ppermute | solution.py:92
  92.3 13.4 %all-to-all-start.1 = ((bf16[8,64,512]{2,1,0:T(8,128)(2,1)}), bf16[8,64,512]{2,1,0:T(8,128)(2,1)S(1)}, u32[]{:S(2)}, u32[]{:S(2)}) async-start(bf16[8,64,512]{2,1,0:T(8,128)(2,1)} %select.28), calls=%async_computation.1 | async-start | bytes 1048576 | tf_op jit(solution)/shard_map/all_to_all | solution.py:541
  100.9 13.0 %collective-permute-start.24 = (bf16[256,512]{1,0:T(8,128)(2,1)}, bf16[256,512]{1,0:T(8,128)(2,1)S(1)}, u32[]{:S(2)}, u32[]{:S(2)}) collective-permute-start(bf16[256,512]{1,0:T(8,128)(2,1)} %get-tuple-element.129), channel_id=1, source_target_pairs={{0,2},{1,3},{2,0},{3,1},{4,6},{5,7},{6,4},{7,5},{8,10},{9,11},{10,... | collective-permute-start | bytes 786440 | tf_op jit(solution)/shard_map/ppermute | solution.py:92
  102.9 14.0 %collective-permute-start.25 = (bf16[256,512]{1,0:T(8,128)(2,1)}, bf16[256,512]{1,0:T(8,128)(2,1)S(1)}, u32[]{:S(2)}, u32[]{:S(2)}) collective-permute-start(bf16[256,512]{1,0:T(8,128)(2,1)} %get-tuple-element.130), channel_id=1, source_target_pairs={{0,4},{1,5},{2,6},{3,7},{4,0},{5,1},{6,2},{7,3},{8,12},{9,13},{10,... | collective-permute-start | bytes 786440 | tf_op jit(solution)/shard_map/ppermute | solution.py:92
  104.4 12.5 %collective-permute-start.26 = (bf16[256,512]{1,0:T(8,128)(2,1)}, bf16[256,512]{1,0:T(8,128)(2,1)S(1)}, u32[]{:S(2)}, u32[]{:S(2)}) collective-permute-start(bf16[256,512]{1,0:T(8,128)(2,1)} %get-tuple-element.131), channel_id=1, source_target_pairs={{0,6},{1,7},{2,4},{3,5},{4,2},{5,3},{6,0},{7,1},{8,14},{9,15},{10,... | collective-permute-start | bytes 786440 | tf_op jit(solution)/shard_map/ppermute | solution.py:92
  106.5 10.4 %copy-start = (f32[256,512]{1,0:T(8,128)S(1)}, f32[256,512]{1,0:T(8,128)}, u32[]{:S(2)}) copy-start(f32[256,512]{1,0:T(8,128)} %get-tuple-element.128.own_ref) | copy-start | bytes 1572868
  117.0 1.6 %collective-permute-start.27 = (f32[128,512]{1,0:T(8,128)S(1)}, f32[128,512]{1,0:T(8,128)S(1)}, u32[]{:S(2)}, u32[]{:S(2)}) collective-permute-start(f32[128,512]{1,0:T(8,128)S(1)} %get-tuple-element.133), channel_id=1, source_target_pairs={{0,1},{1,0},{2,3},{3,2},{4,5},{5,4},{6,7},{7,6},{8,9},{9,8},{10,11... | collective-permute-start | bytes 786440 | tf_op jit(solution)/shard_map/ppermute | solution.py:92
  (5 other events, 3.8 us)
